TPU v7x, 32 devices: a whole 2x2x4 slice. The times are simulated.
32 devices in a mesh: groups: 2 (over x), seq: 16 (over z, y, core).
Axes of the slice: x: 2, y: 2, z: 4, core: 2. Of those that a mesh axis runs over, the one named last changes fastest.
Arguments:
- queries: bfloat16 [256, 2560], P(('groups', 'seq')), parts along dimension 0, may hold values from -160 to 160
- new_keys: bfloat16 [256, 2560], P(('groups', 'seq')), parts along dimension 0, may hold values from -7 to 7
- new_values: bfloat16 [256, 2560], P(('groups', 'seq')), parts along dimension 0, may hold values from -6 to 6
- cache_keys: bfloat16 [16384, 2560], P(('groups', 'seq')), parts along dimension 0, may hold values from -6 to 6
- cache_values: bfloat16 [16384, 2560], P(('groups', 'seq')), parts along dimension 0, may hold values from -6 to 6
- victims: int32 [32], P('groups'), parts along dimension 0, may hold values from 0 to 63, as said below
Outputs:
- attended: bfloat16 [256, 2560], P(('groups', 'seq')), parts along dimension 0
There are 2 independent parts, one for each index of `groups`. A program takes and returns all parts, laid end to end along the dimension named above; each array names one. Nothing has to cross between parts.
Inputs may be any that keep to these rules, and one draw needn't show every extreme that they name: `victims`: 16 distinct block ids of the cache; the first and the last block are always among them.
All inputs are finite; a program needn't handle non-finite values.
Results may differ from a plain program's by a relative error of at most 0.01.
Values may be sent and summed in bfloat16 or wider, within the bound.
No kernel may reach another device: no remote copies, remote signals or barrier semaphores. Data moves between devices by JAX's collectives and lax.ppermute only.
A program may use at most 128 MiB of HBM per device.

v0:
```python
import math

import jax
import jax.numpy as jnp
from jax import lax
from jax.sharding import PartitionSpec as P

HD = 128
BLK = 128


def similarity(query_cols, other):
    return lax.dot_general(
        query_cols, other, (((1,), (1,)), ((), ())), preferred_element_type=jnp.float32
    )


def per_device(queries, new_keys, new_values, cache_keys, cache_values, victims):
    members = lax.axis_size("seq")
    tok_dev = queries.shape[0]
    columns = queries.shape[1]
    head_count = columns // HD
    cache_rows = cache_keys.shape[0]
    block_count = cache_rows // BLK
    block_ids = lax.axis_index("seq") * block_count + jnp.arange(block_count, dtype=jnp.int32)
    evicted = jnp.any(victims[:, None] == block_ids[None, :], axis=0)
    cache_live = jnp.repeat(jnp.logical_not(evicted), BLK)[None, :]
    everyone = lax.all_gather(queries, "seq", axis=0, tiled=True)
    total = everyone.shape[0]
    scaling = 1.0 / math.sqrt(HD)

    def scores(head):
        first_col = head * HD
        query_cols = lax.dynamic_slice_in_dim(everyone, first_col, HD, 1)
        cached = (
            similarity(query_cols, lax.dynamic_slice_in_dim(cache_keys, first_col, HD, 1)) * scaling
        )
        cached = jnp.where(cache_live, cached, -1e30)
        fresh_scores = (
            similarity(query_cols, lax.dynamic_slice_in_dim(new_keys, first_col, HD, 1)) * scaling
        )
        return (cached, fresh_scores)

    def weigh(head, cached, fresh_scores, row_top):
        first_col = head * HD
        cached_exp = jnp.where(cache_live, jnp.exp(cached - row_top[:, None]), 0.0)
        fresh_exp = jnp.exp(fresh_scores - row_top[:, None])
        row_mass = jnp.sum(cached_exp, axis=1) + jnp.sum(fresh_exp, axis=1)
        head_out = jnp.dot(
            cached_exp.astype(jnp.bfloat16),
            lax.dynamic_slice_in_dim(cache_values, first_col, HD, 1),
            preferred_element_type=jnp.float32,
        )
        head_out = head_out + jnp.dot(
            fresh_exp.astype(jnp.bfloat16),
            lax.dynamic_slice_in_dim(new_values, first_col, HD, 1),
            preferred_element_type=jnp.float32,
        )
        return (head_out, row_mass)

    empty_out = jnp.zeros((total, columns), jnp.float32)
    empty_stat = jnp.zeros((total, head_count), jnp.float32)

    def head_pass(head, carry):
        outputs, maxima, masses = carry
        cached, fresh_scores = scores(head)
        row_top = jnp.maximum(jnp.max(cached, axis=1), jnp.max(fresh_scores, axis=1))
        head_out, row_mass = weigh(head, cached, fresh_scores, row_top)
        outputs = lax.dynamic_update_slice_in_dim(outputs, head_out, head * HD, 1)
        maxima = lax.dynamic_update_slice_in_dim(maxima, row_top[:, None], head, 1)
        masses = lax.dynamic_update_slice_in_dim(masses, row_mass[:, None], head, 1)
        return (outputs, maxima, masses)

    outputs, maxima, masses = lax.fori_loop(
        0, head_count, head_pass, (empty_out, empty_stat, empty_stat)
    )
    got_out, got_max, got_mass = (
        lax.all_to_all(
            outputs.reshape(members, tok_dev, columns),
            "seq",
            split_axis=0,
            concat_axis=0,
            tiled=True,
        ),
        lax.all_to_all(
            maxima.reshape(members, tok_dev, head_count),
            "seq",
            split_axis=0,
            concat_axis=0,
            tiled=True,
        ),
        lax.all_to_all(
            masses.reshape(members, tok_dev, head_count),
            "seq",
            split_axis=0,
            concat_axis=0,
            tiled=True,
        ),
    )
    peak_max = jnp.max(got_max, axis=0)
    factor = jnp.exp(got_max - peak_max[None])
    factor = factor / jnp.sum(factor * got_mass, axis=0)[None]
    merged = jnp.einsum("pthd,pth->thd", got_out.reshape(members, tok_dev, head_count, HD), factor)
    return merged.reshape(tok_dev, columns).astype(jnp.bfloat16)


def solution(mesh):
    in_specs = (
        P(("groups", "seq"), None),
        P(("groups", "seq"), None),
        P(("groups", "seq"), None),
        P(("groups", "seq"), None),
        P(("groups", "seq"), None),
        P("groups"),
    )
    out_specs = P(("groups", "seq"), None)
    return jax.shard_map(
        per_device, mesh=mesh, in_specs=in_specs, out_specs=out_specs, check_vma=False
    )
```

profile of v0, /device:TPU:0, one launch (start us, length us, event | category | flops | bytes accessed | tf_op | source)
XLA Modules:
  0.0 170.1 jit_solution(4086784012809041473)
XLA Ops:
  0.9 25.3 %all_gather.3 = bf16[128,2560]{1,0:T(8,128)(2,1)S(1)} all-gather(bf16[8,2560]{1,0:T(8,128)(2,1)} %param.8), channel_id=1, replica_groups=mesh['groups'=2,'seq'=16] {'seq'}, dimensions={0}, use_global_device_ids=true | all-gather | bytes 696320 | tf_op jit(solution)/shard_map/all_gather | solution.py:28
  27.1 102.0 %while.18 = (s32[]{:T(128)}, bf16[128,2560]{1,0:T(8,128)(2,1)}, f32[128,20]{0,1:T(8,128)S(1)}, f32[128,20]{0,1:T(8,128)S(1)}, bf16[128,2560]{1,0:T(8,128)(2,1)S(...) while((s32[]{:T(128)}, bf16[128,2560]{1,0:T(8,128)(2,1)}, ...), condition=%wide.region_6.7_spmd.clone, body=%wide.region_1.6_spmd.clone.sunk | while | flops 34690820 | bytes 1341643 | solution.py:74
  30.6 1.5 fusion.49
  35.7 1.5 fusion.49
  40.8 1.5 fusion.49
  45.9 1.5 fusion.49
  51.0 1.6 fusion.49
  56.1 1.5 fusion.49
  58.6 1.2 fusion.46
  61.2 1.5 fusion.49
  63.7 1.2 fusion.46
  66.3 1.5 fusion.49
  71.4 1.5 fusion.49
  76.5 1.5 fusion.49
  78.9 1.2 fusion.46
  81.6 1.5 fusion.49
  84.0 1.2 fusion.46
  86.7 1.5 fusion.49
  91.8 1.5 fusion.49
  96.9 1.5 fusion.49
  99.3 1.2 fusion.46
  102.0 1.6 fusion.49
  107.1 1.5 fusion.49
  112.2 1.5 fusion.49
  117.3 1.5 fusion.49
  122.4 1.5 fusion.49
  127.5 1.5 fusion.49
  129.9 3.5 %all-to-all-start.2 = ((f32[16,1,160]{2,1,0:T(1,128)}), f32[16,1,160]{2,1,0:T(1,128)S(1)}, u32[]{:S(2)}, u32[]{:S(2)}) async-start(f32[16,1,160]{2,1,0:T(1,128)} %reshape.62), calls=%async_computation.2 | async-start | bytes 32768 | tf_op jit(solution)/shard_map/all_to_all | solution.py:92
  133.6 6.2 %all-to-all-done.2 = f32[16,1,160]{2,1,0:T(1,128)S(1)} async-done(((f32[16,1,160]{2,1,0:T(1,128)}), f32[16,1,160]{2,1,0:T(1,128)S(1)}, u32[]{:S(2)}, u32[]{:S(2)}) %all-to-all-start.2) | async-done | bytes 10272 | tf_op jit(solution)/shard_map/all_to_all | solution.py:92
  139.8 9.1 %all_to_all.15 = f32[16,1,160]{2,1,0:T(1,128)S(1)} all-to-all(f32[16,1,160]{2,1,0:T(1,128)S(1)} %reshape.60), channel_id=1, replica_groups=mesh['groups'=2,'seq'=16] {'seq'}, dimensions={0} | all-to-all | bytes 20480 | tf_op jit(solution)/shard_map/all_to_all | solution.py:85
  148.9 3.6 %all-to-all-start = ((bf16[16,8,2560]{2,1,0:T(8,128)(2,1)}), bf16[16,8,2560]{2,1,0:T(8,128)(2,1)S(1)}, u32[]{:S(2)}, u32[]{:S(2)}) async-start(bf16[16,8,2560]{2,1,0:T(8,128)(2,1)} %bitcast), calls=%async_computation | async-start | bytes 1310720 | tf_op jit(solution)/shard_map/all_to_all | solution.py:78
  154.8 14.2 %all-to-all-done = bf16[16,8,2560]{2,1,0:T(8,128)(2,1)S(1)} async-done(((bf16[16,8,2560]{2,1,0:T(8,128)(2,1)}), bf16[16,8,2560]{2,1,0:T(8,128)(2,1)S(1)}, u32[]{:S(2)}, u32[]{:S(2)}) %all-to-all-start) | async-done | bytes 655392 | tf_op jit(solution)/shard_map/all_to_all | solution.py:78
  (216 shorter events, 71.0 us)
Async XLA Ops:
  129.9 10.0 %all-to-all-start.2 = ((f32[16,1,160]{2,1,0:T(1,128)}), f32[16,1,160]{2,1,0:T(1,128)S(1)}, u32[]{:S(2)}, u32[]{:S(2)}) async-start(f32[16,1,160]{2,1,0:T(1,128)} %reshape.62), calls=%async_computation.2 | async-start | bytes 32768 | tf_op jit(solution)/shard_map/all_to_all | solution.py:92
  148.9 20.2 %all-to-all-start = ((bf16[16,8,2560]{2,1,0:T(8,128)(2,1)}), bf16[16,8,2560]{2,1,0:T(8,128)(2,1)S(1)}, u32[]{:S(2)}, u32[]{:S(2)}) async-start(bf16[16,8,2560]{2,1,0:T(8,128)(2,1)} %bitcast), calls=%async_computation | async-start | bytes 1310720 | tf_op jit(solution)/shard_map/all_to_all | solution.py:78
where the time goes:
time: 172 us; the launch traced here: 170 us
  matrix products  94.4 us (55%)
  blocking collectives  34.4 us (20%)
  waiting for transfers between devices  20.5 us (12%)
  starting transfers between devices  7.09 us (4%)
  other arithmetic  6.91 us (4%)
  local copies, waits for them, and re-layouts  6.33 us (4%)
    dot_general x40, matrix products, similarity(): lax.dot_general(query_cols, other, (((1,), (1,)), ((), ())), preferred_el...  40.3 us
    dot_general x20, matrix products, weigh(): jnp.dot(fresh_exp.astype(jnp.bfloat16), lax.dynamic_slice_in_dim(new_valu...  30.6 us
    all_gather x1, blocking collectives, per_device(): everyone = lax.all_gather(queries, 'seq', axis=0, tiled=True)  25.3 us
    dot_general x20, matrix products, weigh(): jnp.dot(cached_exp.astype(jnp.bfloat16), lax.dynamic_slice_in_dim(cache_v...  23 us
    all_to_all x1, waiting for transfers between devices, per_device(): lax.all_to_all(outputs.reshape(members, tok_dev, columns), 'seq', split_a...  14.2 us
    all_to_all x1, blocking collectives, per_device(): lax.all_to_all(maxima.reshape(members, tok_dev, head_count), 'seq', split...  9.06 us
    all_to_all x1, waiting for transfers between devices, per_device(): lax.all_to_all(masses.reshape(members, tok_dev, head_count), 'seq', split...  6.24 us
    reduce_sum x40, other arithmetic, weigh(): row_mass = jnp.sum(cached_exp, axis=1) + jnp.sum(fresh_exp, axis=1)  4.38 us
  transfers between devices with their start and end apart: 2, of which 2 were waited for; matrix products, arithmetic and copies ran while one was open for 1% of the time, Pallas kernels for 0%

commit v1 on v0

v1 whole, which is shorter than its diff:
```python
import functools
import math

import jax
import jax.numpy as jnp
from jax import lax
from jax.experimental import pallas as pl
from jax.experimental.pallas import tpu as pltpu
from jax.sharding import PartitionSpec as P

HD = 128
BLK = 128
STAT = 128
LANE = STAT // 3
NEG = -1e30
F32 = jnp.float32
BF16 = jnp.bfloat16


def factors(members):
    cores = 2 if members % 2 == 0 else 1
    chips = members // cores
    far = next(a for a in range(1, chips + 1) if chips % a == 0 and a * a >= chips)
    return far, chips // far, cores


def shift_perm(shape, axis, by):
    a_n, b_n, c_n = shape
    pairs = []
    for a in range(a_n):
        for b in range(b_n):
            for c in range(c_n):
                at = [a, b, c]
                src = list(at)
                src[axis] = (src[axis] + by) % shape[axis]
                flat = lambda p: (p[0] * b_n + p[1]) * c_n + p[2]
                pairs.append((flat(src), flat(at)))
    return pairs


def lanes(rows):
    return lax.broadcasted_iota(jnp.int32, (rows, STAT), 1)


def pack_stats(top, mass):
    high = mass.astype(BF16).astype(F32)
    return top + pltpu.roll(high, LANE, 1) + pltpu.roll(mass - high, 2 * LANE, 1)


def unpack_stats(packed, heads):
    used = lanes(packed.shape[0]) < heads
    mass = pltpu.roll(packed, STAT - LANE, 1) + pltpu.roll(packed, STAT - 2 * LANE, 1)
    return jnp.where(used, packed, 0.0), jnp.where(used, mass, 0.0)


def attend_kernel(group, scale, bias_ref, qs_refs, k_ref, v_ref, nk_ref, nv_ref, outs, top_acc, mass_acc):
    step = pl.program_id(1)
    rows = qs_refs[0].shape[0] * len(qs_refs)
    per = qs_refs[0].shape[0]
    lane = lanes(rows)

    @pl.when(step == 0)
    def _():
        top_acc[...] = jnp.zeros_like(top_acc)
        mass_acc[...] = jnp.zeros_like(mass_acc)

    contract_last = (((1,), (1,)), ((), ()))
    tops = top_acc[...]
    masses = mass_acc[...]
    bias = bias_ref[...]
    for i in range(group):
        cols = slice(i * HD, (i + 1) * HD)
        q = jnp.concatenate([r[:, cols] for r in qs_refs], axis=0)
        cached = lax.dot_general(q, k_ref[:, cols], contract_last, preferred_element_type=F32)
        fresh = lax.dot_general(q, nk_ref[:, cols], contract_last, preferred_element_type=F32)
        cached = cached * scale + bias
        fresh = fresh * scale
        top = jnp.maximum(
            jnp.max(cached, axis=1, keepdims=True), jnp.max(fresh, axis=1, keepdims=True)
        )
        top = top.astype(BF16).astype(F32)
        cached = jnp.exp2(cached - top)
        fresh = jnp.exp2(fresh - top)
        mass = jnp.sum(cached, axis=1, keepdims=True) + jnp.sum(fresh, axis=1, keepdims=True)
        out = jnp.dot(cached.astype(BF16), v_ref[:, cols], preferred_element_type=F32)
        out = out + jnp.dot(fresh.astype(BF16), nv_ref[:, cols], preferred_element_type=F32)
        head = step * group + i
        at = pl.multiple_of(head * HD, HD)
        for j, o_ref in enumerate(outs):
            o_ref[:, pl.ds(at, HD)] = out[j * per : (j + 1) * per].astype(o_ref.dtype)
        tops = jnp.where(lane == head, top, tops)
        masses = jnp.where(lane == head, mass, masses)
    top_acc[...] = tops
    mass_acc[...] = masses

    @pl.when(step == pl.num_programs(1) - 1)
    def _():
        packed = pack_stats(top_acc[...], mass_acc[...])
        for j, o_ref in enumerate(outs):
            width = o_ref.shape[1]
            o_ref[:, width - STAT :] = packed[j * per : (j + 1) * per].astype(o_ref.dtype)


def attend(parts, keys, values, new_keys, new_values, bias, first_head, heads):
    rows = parts[0].shape[0]
    group = next(g for g in (5, 4, 2, 1) if heads % g == 0 and first_head % g == 0)
    tile = min(rows, max(16, 128 // len(parts)))
    cache_rows = keys.shape[0]
    tok = new_keys.shape[0]
    width = heads * HD + STAT
    offset = first_head // group
    scale = math.log2(math.e) / math.sqrt(HD)
    n = len(parts)

    def body(*refs):
        attend_kernel(
            group, scale, refs[0], refs[1 : 1 + n], *refs[1 + n : 5 + n], refs[5 + n : 5 + 2 * n],
            *refs[5 + 2 * n :],
        )

    kv_spec = pl.BlockSpec((cache_rows, group * HD), lambda r, g: (0, g + offset))
    fresh_spec = pl.BlockSpec((tok, group * HD), lambda r, g: (0, g + offset))
    return pl.pallas_call(
        body,
        grid=(rows // tile, heads // group),
        in_specs=[pl.BlockSpec((1, cache_rows), lambda r, g: (0, 0))]
        + [pl.BlockSpec((tile, group * HD), lambda r, g: (r, g))] * n
        + [kv_spec, kv_spec, fresh_spec, fresh_spec],
        out_specs=[pl.BlockSpec((tile, width), lambda r, g: (r, 0))] * n,
        out_shape=[jax.ShapeDtypeStruct((rows, width), F32 if j == 0 else BF16) for j in range(n)],
        scratch_shapes=[pltpu.VMEM((tile * n, STAT), F32)] * 2,
        compiler_params=pltpu.CompilerParams(
            dimension_semantics=("arbitrary", "arbitrary"), vmem_limit_bytes=32 * 1024 * 1024
        ),
        cost_estimate=pl.CostEstimate(
            flops=4 * n * rows * cache_rows * heads * HD,
            bytes_accessed=4 * cache_rows * heads * HD,
            transcendentals=n * rows * cache_rows * heads,
        ),
        name="attend",
    )(bias, *parts, keys, values, new_keys, new_values)


def merge_kernel(heads, count, last, *refs):
    ins, outs = refs[:count], refs[count:]
    width = ins[0].shape[1]
    stats = [unpack_stats(r[:, width - STAT :].astype(F32), heads) for r in ins]
    top = functools.reduce(jnp.maximum, [t for t, _ in stats])
    weights = [jnp.exp2(t - top) for t, _ in stats]
    mass = functools.reduce(jnp.add, [w * m for w, (_, m) in zip(weights, stats)])
    if last:
        used = lanes(mass.shape[0]) < heads
        inverse = 1.0 / jnp.where(used, mass, 1.0)
        weights = [w * inverse for w in weights]
    per = outs[0].shape[0]
    for head in range(heads):
        cols = slice(head * HD, (head + 1) * HD)
        total = functools.reduce(
            jnp.add,
            [r[:, cols].astype(F32) * w[:, head : head + 1] for r, w in zip(ins, weights)],
        )
        for j, o_ref in enumerate(outs):
            o_ref[:, cols] = total[j * per : (j + 1) * per].astype(o_ref.dtype)
    if not last:
        packed = pack_stats(top, mass)
        for j, o_ref in enumerate(outs):
            o_ref[:, width - STAT :] = packed[j * per : (j + 1) * per].astype(o_ref.dtype)


def merge(partials, heads, pieces, last=False):
    rows, width = partials[0].shape
    per = rows // pieces
    if last:
        shapes = [jax.ShapeDtypeStruct((rows, heads * HD), BF16)]
    else:
        shapes = [
            jax.ShapeDtypeStruct((per, width), F32 if j == 0 else BF16) for j in range(pieces)
        ]
    return pl.pallas_call(
        functools.partial(merge_kernel, heads, len(partials), last),
        in_specs=[pl.BlockSpec(memory_space=pltpu.VMEM)] * len(partials),
        out_specs=[pl.BlockSpec(memory_space=pltpu.VMEM)] * len(shapes),
        out_shape=shapes,
        compiler_params=pltpu.CompilerParams(vmem_limit_bytes=48 * 1024 * 1024),
        cost_estimate=pl.CostEstimate(
            flops=4 * len(partials) * rows * width,
            bytes_accessed=4 * (len(partials) + 1) * rows * width,
            transcendentals=0,
        ),
        name="merge",
    )(*partials)


def per_device(queries, new_keys, new_values, cache_keys, cache_values, victims):
    members = lax.axis_size("seq")
    shape = factors(members)
    a_n, b_n, c_n = shape
    heads = queries.shape[1] // HD
    cache_rows = cache_keys.shape[0]
    block_count = cache_rows // BLK
    block_ids = lax.axis_index("seq") * block_count + jnp.arange(block_count, dtype=jnp.int32)
    evicted = jnp.any(victims[:, None] == block_ids[None, :], axis=0)
    bias = jnp.repeat(jnp.where(evicted, NEG, 0.0), BLK)[None, :]

    def fetch(x, axis, by):
        return lax.ppermute(x, "seq", shift_perm(shape, axis, by))

    def give(x, axis, by):
        return lax.ppermute(x, "seq", shift_perm(shape, axis, -by))

    plane = jnp.concatenate([queries] + [fetch(queries, 0, d) for d in range(1, a_n)], axis=0)
    plane = jnp.concatenate([plane] + [fetch(plane, 1, d) for d in range(1, b_n)], axis=0)
    parts = [plane] + [fetch(plane, 2, d) for d in range(1, c_n)]

    sums = attend(parts, cache_keys, cache_values, new_keys, new_values, bias, 0, heads)
    sums = [sums[0]] + [give(s, 2, d + 1) for d, s in enumerate(sums[1:])]
    sums = merge(sums, heads, b_n)
    sums = [sums[0]] + [give(s, 1, d + 1) for d, s in enumerate(sums[1:])]
    sums = merge(sums, heads, a_n)
    sums = [sums[0]] + [give(s, 0, d + 1) for d, s in enumerate(sums[1:])]
    return merge(sums, heads, 1, last=True)[0]


def solution(mesh):
    rows = P(("groups", "seq"), None)
    return jax.shard_map(
        per_device,
        mesh=mesh,
        in_specs=(rows, rows, rows, rows, rows, P("groups")),
        out_specs=rows,
        check_vma=False,
    )
```

time: 172 us -> 48.3 us (0.28)
  matrix products: 94.4 us -> 0 us
  blocking collectives: 34.4 us -> 0 us
  Pallas kernels: 0 us -> 9.08 us
  starting transfers between devices: 7.09 us -> 14.4 us
  other arithmetic: 6.91 us -> 1.64 us
  waiting for transfers between devices: 20.5 us -> 16.8 us
    dot_general x81 -> x0, matrix products: 94.4 us -> none  [the longest x40 40.3 us: similarity(): lax.dot_general(query_cols, other, (((1,), (1,)), ((), ())), preferred_el...]
    all_gather x1 -> x0, blocking collectives: 25.3 us -> none  [per_device(): everyone = lax.all_gather(queries, 'seq', axis=0, tiled=True)]
    all_to_all x2 -> x0, waiting for transfers between devices: 20.5 us -> none  [the longest x1 14.2 us: per_device(): lax.all_to_all(outputs.reshape(members, tok_dev, columns), 'seq', split_a...]
    ppermute x0 -> x10, waiting for transfers between devices: none -> 16.8 us  [the longest x5 10.2 us: give(): return lax.ppermute(x, 'seq', shift_perm(shape, axis, -by))]
    ppermute x0 -> x10, starting transfers between devices: none -> 14.4 us  [the longest x5 8.62 us: fetch(): return lax.ppermute(x, 'seq', shift_perm(shape, axis, by))]
    pallas_call x0 -> x4, Pallas kernels: none -> 9.08 us  [the longest x1 7.43 us: attend(): pl.pallas_call(body, grid=(rows // tile, heads // group), in_specs=[pl.Bl...]
    all_to_all x1 -> x0, blocking collectives: 9.06 us -> none  [per_device(): lax.all_to_all(maxima.reshape(members, tok_dev, head_count), 'seq', split...]
    all_to_all x2 -> x0, starting transfers between devices: 7.09 us -> none  [the longest x1 3.59 us: per_device(): lax.all_to_all(outputs.reshape(members, tok_dev, columns), 'seq', split_a...]
  transfers between devices with their start and end apart: 2 -> 10, of which waited for: 2 -> 9; matrix products, arithmetic and copies ran while one was open for 1% -> 4% of each run, Pallas kernels for 0% -> 0%
where the time goes in v1:
time: 48.3 us; the launch traced here: 47.9 us
  waiting for transfers between devices  16.8 us (35%)
  starting transfers between devices  14.4 us (30%)
  Pallas kernels  9.08 us (19%)
  local copies, waits for them, and re-layouts  5.94 us (12%)
  other arithmetic  1.64 us (3%)
    ppermute x5, waiting for transfers between devices, give(): return lax.ppermute(x, 'seq', shift_perm(shape, axis, -by))  10.2 us
    ppermute x5, starting transfers between devices, fetch(): return lax.ppermute(x, 'seq', shift_perm(shape, axis, by))  8.62 us
    pallas_call x1, Pallas kernels, attend(): pl.pallas_call(body, grid=(rows // tile, heads // group), in_specs=[pl.Bl...  7.43 us
    ppermute x5, waiting for transfers between devices, fetch(): return lax.ppermute(x, 'seq', shift_perm(shape, axis, by))  6.58 us
    unnamed x12, local copies, waits for them, and re-layouts  5.86 us
    ppermute x5, starting transfers between devices, give(): return lax.ppermute(x, 'seq', shift_perm(shape, axis, -by))  5.76 us
    pallas_call x3, Pallas kernels, merge(): pl.pallas_call(functools.partial(merge_kernel, heads, len(partials), last...  1.65 us
  transfers between devices with their start and end apart: 10, of which 9 were waited for; matrix products, arithmetic and copies ran while one was open for 4% of the time, Pallas kernels for 0%

profile of v1, /device:TPU:0, one launch (start us, length us, event | category | flops | bytes accessed | tf_op | source)
XLA Modules:
  0.0 47.9 jit_solution(11682194968880898238)
XLA Ops:
  0.0 3.0 %collective-permute-start.2 = (bf16[8,2560]{1,0:T(8,128)(2,1)}, bf16[8,2560]{1,0:T(8,128)(2,1)S(1)}, u32[]{:S(2)}, u32[]{:S(2)}) collective-permute-start(bf16[8,2560]{1,0:T(8,128)(2,1)} %param.6), channel_id=1, source_target_pairs={{12,0},{13,1},{14,2},{15,3},{0,4},{1,5},{2,6},{3,7},{4,8},{5,9},{6... | collective-permute-start | bytes 122888 | tf_op jit(solution)/shard_map/ppermute | solution.py:206
  3.0 2.6 %collective-permute-start.1 = (bf16[8,2560]{1,0:T(8,128)(2,1)}, bf16[8,2560]{1,0:T(8,128)(2,1)S(1)}, u32[]{:S(2)}, u32[]{:S(2)}) collective-permute-start(bf16[8,2560]{1,0:T(8,128)(2,1)} %param.6), channel_id=1, source_target_pairs={{8,0},{9,1},{10,2},{11,3},{12,4},{13,5},{14,6},{15,7},{0,8},{1,9},... | collective-permute-start | bytes 122888 | tf_op jit(solution)/shard_map/ppermute | solution.py:206
  5.6 1.3 %collective-permute-start = (bf16[8,2560]{1,0:T(8,128)(2,1)}, bf16[8,2560]{1,0:T(8,128)(2,1)S(1)}, u32[]{:S(2)}, u32[]{:S(2)}) collective-permute-start(bf16[8,2560]{1,0:T(8,128)(2,1)} %param.6), channel_id=1, source_target_pairs={{4,0},{5,1},{6,2},{7,3},{8,4},{9,5},{10,6},{11,7},{12,8},{13,9},{1... | collective-permute-start | bytes 122888 | tf_op jit(solution)/shard_map/ppermute | solution.py:206
  7.0 0.8 %constant_dynamic-update-slice_fusion.4 = bf16[64,2560]{1,0:T(8,128)(2,1)S(1)} fusion(bf16[8,2560]{1,0:T(8,128)(2,1)} %param.6), kind=kLoop, calls=%fused_computation.5 | loop fusion | bytes 81920
  7.8 0.0 collective-permute-done.2
  7.8 0.8 %collective-permute-done.1 = bf16[8,2560]{1,0:T(8,128)(2,1)S(1)} collective-permute-done((bf16[8,2560]{1,0:T(8,128)(2,1)}, bf16[8,2560]{1,0:T(8,128)(2,1)S(1)}, u32[]{:S(2)}, u32[]{:S(2)}) %collective-permute-start.1) | collective-permute-done | bytes 40992 | tf_op jit(solution)/shard_map/ppermute | solution.py:206
  8.6 1.2 %collective-permute-done = bf16[8,2560]{1,0:T(8,128)(2,1)S(1)} collective-permute-done((bf16[8,2560]{1,0:T(8,128)(2,1)}, bf16[8,2560]{1,0:T(8,128)(2,1)S(1)}, u32[]{:S(2)}, u32[]{:S(2)}) %collective-permute-start) | collective-permute-done | bytes 40992 | tf_op jit(solution)/shard_map/ppermute | solution.py:206
  9.8 0.8 %pad_maximum_fusion = bf16[32,2560]{1,0:T(8,128)(2,1)S(1)} fusion(bf16[8,2560]{1,0:T(8,128)(2,1)S(1)} %collective-permute-done.2, bf16[8,2560]{1,0:T(8,128)(2,1)S(1)} %collective-permute-done.1, bf16[8,2560]{1,0:T(8,128)(2,1)S(1)} %collective-permute-done, bf16[8,2560]{1,0:T(8,128)(2,1)} %param.6), kind=kLoop, calls=%fused_computation | loop fusion | flops 655360 | bytes 327680 | tf_op jit(solution)/shard_map/concatenate | solution.py:211
  10.6 1.6 %collective-permute-start.3 = (bf16[32,2560]{1,0:T(8,128)(2,1)S(1)}, bf16[32,2560]{1,0:T(8,128)(2,1)S(1)}, u32[]{:S(2)}, u32[]{:S(2)}) collective-permute-start(bf16[32,2560]{1,0:T(8,128)(2,1)S(1)} %pad_maximum_fusion), channel_id=1, source_target_pairs={{2,0},{3,1},{0,2},{1,3},{6,4},{7,5},{4,6},{5,7},{10,8},{11,9},{8,1... | collective-permute-start | bytes 491528 | tf_op jit(solution)/shard_map/ppermute | solution.py:206
  12.2 3.8 %collective-permute-done.3 = bf16[32,2560]{1,0:T(8,128)(2,1)S(1)} collective-permute-done((bf16[32,2560]{1,0:T(8,128)(2,1)S(1)}, bf16[32,2560]{1,0:T(8,128)(2,1)S(1)}, u32[]{:S(2)}, u32[]{:S(2)}) %collective-permute-start.3) | collective-permute-done | bytes 163872 | tf_op jit(solution)/shard_map/ppermute | solution.py:206
  16.0 0.1 collective-permute-start.4
  16.1 0.8 %compare_reduce_fusion = pred[4]{0:T(512)(128)(4,1)S(1)} fusion(s32[16]{0:T(128)} %param.11, s32[4]{0:T(128)S(1)} %iota_add_fusion), kind=kLoop, calls=%fused_computation.6 | loop fusion | flops 124 | bytes 84 | tf_op jit(solution)/shard_map/reduce_or | solution.py:202
  16.9 0.8 %collective-permute-done.4.refs_2_ = bf16[64,2560]{1,0:T(8,128)(2,1)S(1)} collective-permute-done((bf16[64,2560]{1,0:T(8,128)(2,1)S(1)}, bf16[64,2560]{1,0:T(8,128)(2,1)S(1)}, u32[]{:S(2)}, u32[]{:S(2)}) %collective-permute-start.4) | collective-permute-done | bytes 327712 | tf_op jit(solution)/shard_map/ppermute | solution.py:206
  17.7 0.1 broadcast_in_dim.15
  17.8 1.7 %copy-done = bf16[512,2560]{1,0:T(8,128)(2,1)S(1)} copy-done((bf16[512,2560]{1,0:T(8,128)(2,1)S(1)}, bf16[512,2560]{1,0:T(8,128)(2,1)}, u32[]{:S(2)}) %copy-start) | copy-done | bytes 2621464
  19.5 1.7 %copy-done.1 = bf16[512,2560]{1,0:T(8,128)(2,1)S(1)} copy-done((bf16[512,2560]{1,0:T(8,128)(2,1)S(1)}, bf16[512,2560]{1,0:T(8,128)(2,1)}, u32[]{:S(2)}) %copy-start.1) | copy-done | bytes 2621464
  21.3 0.8 %copy-done.2 = bf16[8,2560]{1,0:T(8,128)(2,1)S(1)} copy-done((bf16[8,2560]{1,0:T(8,128)(2,1)S(1)}, bf16[8,2560]{1,0:T(8,128)(2,1)}, u32[]{:S(2)}) %copy-start.2) | copy-done | bytes 40984
  22.0 0.8 %copy-done.3 = bf16[8,2560]{1,0:T(8,128)(2,1)S(1)} copy-done((bf16[8,2560]{1,0:T(8,128)(2,1)S(1)}, bf16[8,2560]{1,0:T(8,128)(2,1)}, u32[]{:S(2)}) %copy-start.3) | copy-done | bytes 40984
  22.8 7.4 %attend.1 = (f32[64,2688]{1,0:T(8,128)S(1)}, bf16[64,2688]{1,0:T(8,128)(2,1)S(1)}) custom-call(f32[1,512]{1,0:T(1,128)S(1)} %bitcast.1, bf16[64,2560]{1,0:T(8,128)(2,1)S(1)} %constant_dynamic-update-slice_fusion.refs_1_, bf16[64,2560]{1,0:T(8,128)(2,1)S(1)} %collective-permute-done.4.refs_2_, bf16[512,2560]{1,0:T(8,128)(2,1)S(1)} %copy-done, ...), custom_call_target="tpu_custom_call" | custom-call | flops 671088640 | bytes 5242880 | tf_op jit(solution)/shard_map/attend/pallas_call | solution.py:123
  30.3 0.2 collective-permute-start.5
  30.5 1.5 %collective-permute-done.5.refs_1_ = bf16[64,2688]{1,0:T(8,128)(2,1)S(1)} collective-permute-done((bf16[64,2688]{1,0:T(8,128)(2,1)S(1)}, bf16[64,2688]{1,0:T(8,128)(2,1)S(1)}, u32[]{:S(2)}, u32[]{:S(2)}) %collective-permute-start.5) | collective-permute-done | bytes 344096 | tf_op jit(solution)/shard_map/ppermute | solution.py:209
  32.0 0.5 merge.3
  32.5 1.6 %collective-permute-start.6 = (bf16[32,2688]{1,0:T(8,128)(2,1)S(1)}, bf16[32,2688]{1,0:T(8,128)(2,1)S(1)}, u32[]{:S(2)}, u32[]{:S(2)}) collective-permute-start(bf16[32,2688]{1,0:T(8,128)(2,1)S(1)} %get-tuple-element.16), channel_id=1, source_target_pairs={{2,0},{3,1},{0,2},{1,3},{6,4},{7,5},{4,6},{5,7},{10,8},{11,9},{8,1... | collective-permute-start | bytes 516104 | tf_op jit(solution)/shard_map/ppermute | solution.py:209
  34.0 4.9 %collective-permute-done.6.refs_1_ = bf16[32,2688]{1,0:T(8,128)(2,1)S(1)} collective-permute-done((bf16[32,2688]{1,0:T(8,128)(2,1)S(1)}, bf16[32,2688]{1,0:T(8,128)(2,1)S(1)}, u32[]{:S(2)}, u32[]{:S(2)}) %collective-permute-start.6) | collective-permute-done | bytes 172064 | tf_op jit(solution)/shard_map/ppermute | solution.py:209
  38.9 0.3 merge.4
  39.2 0.4 collective-permute-start.7
  39.6 3.4 %collective-permute-start.8 = (bf16[8,2688]{1,0:T(8,128)(2,1)S(1)}, bf16[8,2688]{1,0:T(8,128)(2,1)S(1)}, u32[]{:S(2)}, u32[]{:S(2)}) collective-permute-start(bf16[8,2688]{1,0:T(8,128)(2,1)S(1)} %get-tuple-element.19), channel_id=1, source_target_pairs={{8,0},{9,1},{10,2},{11,3},{12,4},{13,5},{14,6},{15,7},{0,8},{1,9},... | collective-permute-start | bytes 129032 | tf_op jit(solution)/shard_map/ppermute | solution.py:209
  43.0 0.2 collective-permute-start.9
  43.2 2.1 %collective-permute-done.7.refs_1_ = bf16[8,2688]{1,0:T(8,128)(2,1)S(1)} collective-permute-done((bf16[8,2688]{1,0:T(8,128)(2,1)S(1)}, bf16[8,2688]{1,0:T(8,128)(2,1)S(1)}, u32[]{:S(2)}, u32[]{:S(2)}) %collective-permute-start.7) | collective-permute-done | bytes 43040 | tf_op jit(solution)/shard_map/ppermute | solution.py:209
  45.3 1.0 %collective-permute-done.8.refs_2_ = bf16[8,2688]{1,0:T(8,128)(2,1)S(1)} collective-permute-done((bf16[8,2688]{1,0:T(8,128)(2,1)S(1)}, bf16[8,2688]{1,0:T(8,128)(2,1)S(1)}, u32[]{:S(2)}, u32[]{:S(2)}) %collective-permute-start.8) | collective-permute-done | bytes 43040 | tf_op jit(solution)/shard_map/ppermute | solution.py:209
  46.3 0.7 %collective-permute-done.9.refs_3_ = bf16[8,2688]{1,0:T(8,128)(2,1)S(1)} collective-permute-done((bf16[8,2688]{1,0:T(8,128)(2,1)S(1)}, bf16[8,2688]{1,0:T(8,128)(2,1)S(1)}, u32[]{:S(2)}, u32[]{:S(2)}) %collective-permute-start.9) | collective-permute-done | bytes 43040 | tf_op jit(solution)/shard_map/ppermute | solution.py:209
  47.0 0.9 %merge.5 = bf16[8,2560]{1,0:T(8,128)(2,1)} custom-call(f32[8,2688]{1,0:T(8,128)S(1)} %get-tuple-element.17.refs_0_, bf16[8,2688]{1,0:T(8,128)(2,1)S(1)} %collective-permute-done.7.refs_1_, bf16[8,2688]{1,0:T(8,128)(2,1)S(1)} %collective-permute-done.8.refs_2_, bf16[8,2688]{1,0:T(8,128)(2,1)S(1)} %collective-permute-done.9.refs_3_), custom_call_target="tpu_custom_call" | custom-call | flops 344064 | bytes 430080 | tf_op jit(solution)/shard_map/merge/pallas_call | solution.py:179
  (10 shorter events, 0.0 us)
Async XLA Ops:
  0.0 7.8 %collective-permute-start.2 = (bf16[8,2560]{1,0:T(8,128)(2,1)}, bf16[8,2560]{1,0:T(8,128)(2,1)S(1)}, u32[]{:S(2)}, u32[]{:S(2)}) collective-permute-start(bf16[8,2560]{1,0:T(8,128)(2,1)} %param.6), channel_id=1, source_target_pairs={{12,0},{13,1},{14,2},{15,3},{0,4},{1,5},{2,6},{3,7},{4,8},{5,9},{6... | collective-permute-start | bytes 122888 | tf_op jit(solution)/shard_map/ppermute | solution.py:206
  3.0 5.6 %collective-permute-start.1 = (bf16[8,2560]{1,0:T(8,128)(2,1)}, bf16[8,2560]{1,0:T(8,128)(2,1)S(1)}, u32[]{:S(2)}, u32[]{:S(2)}) collective-permute-start(bf16[8,2560]{1,0:T(8,128)(2,1)} %param.6), channel_id=1, source_target_pairs={{8,0},{9,1},{10,2},{11,3},{12,4},{13,5},{14,6},{15,7},{0,8},{1,9},... | collective-permute-start | bytes 122888 | tf_op jit(solution)/shard_map/ppermute | solution.py:206
  5.6 4.2 %collective-permute-start = (bf16[8,2560]{1,0:T(8,128)(2,1)}, bf16[8,2560]{1,0:T(8,128)(2,1)S(1)}, u32[]{:S(2)}, u32[]{:S(2)}) collective-permute-start(bf16[8,2560]{1,0:T(8,128)(2,1)} %param.6), channel_id=1, source_target_pairs={{4,0},{5,1},{6,2},{7,3},{8,4},{9,5},{10,6},{11,7},{12,8},{13,9},{1... | collective-permute-start | bytes 122888 | tf_op jit(solution)/shard_map/ppermute | solution.py:206
  10.6 5.4 %collective-permute-start.3 = (bf16[32,2560]{1,0:T(8,128)(2,1)S(1)}, bf16[32,2560]{1,0:T(8,128)(2,1)S(1)}, u32[]{:S(2)}, u32[]{:S(2)}) collective-permute-start(bf16[32,2560]{1,0:T(8,128)(2,1)S(1)} %pad_maximum_fusion), channel_id=1, source_target_pairs={{2,0},{3,1},{0,2},{1,3},{6,4},{7,5},{4,6},{5,7},{10,8},{11,9},{8,1... | collective-permute-start | bytes 491528 | tf_op jit(solution)/shard_map/ppermute | solution.py:206
  16.0 1.7 %collective-permute-start.4 = (bf16[64,2560]{1,0:T(8,128)(2,1)S(1)}, bf16[64,2560]{1,0:T(8,128)(2,1)S(1)}, u32[]{:S(2)}, u32[]{:S(2)}) collective-permute-start(bf16[64,2560]{1,0:T(8,128)(2,1)S(1)} %constant_dynamic-update-slice_fusion.refs_1_), channel_id=1, source_target_pairs={{1,0},{0,1},{3,2},{2,3},{5,4},{4,5},{7,6},{6,7},{9,8},{8,9},{11,10... | collective-permute-start | bytes 983048 | tf_op jit(solution)/shard_map/ppermute | solution.py:206
  17.8 1.7 %copy-start = (bf16[512,2560]{1,0:T(8,128)(2,1)S(1)}, bf16[512,2560]{1,0:T(8,128)(2,1)}, u32[]{:S(2)}) copy-start(bf16[512,2560]{1,0:T(8,128)(2,1)} %refs_3_.1) | copy-start | bytes 7864324
  19.5 1.7 %copy-start.1 = (bf16[512,2560]{1,0:T(8,128)(2,1)S(1)}, bf16[512,2560]{1,0:T(8,128)(2,1)}, u32[]{:S(2)}) copy-start(bf16[512,2560]{1,0:T(8,128)(2,1)} %refs_4_.1) | copy-start | bytes 7864324
  21.3 0.8 %copy-start.2 = (bf16[8,2560]{1,0:T(8,128)(2,1)S(1)}, bf16[8,2560]{1,0:T(8,128)(2,1)}, u32[]{:S(2)}) copy-start(bf16[8,2560]{1,0:T(8,128)(2,1)} %refs_5_.1) | copy-start | bytes 122884
  22.0 0.8 %copy-start.3 = (bf16[8,2560]{1,0:T(8,128)(2,1)S(1)}, bf16[8,2560]{1,0:T(8,128)(2,1)}, u32[]{:S(2)}) copy-start(bf16[8,2560]{1,0:T(8,128)(2,1)} %refs_6_.1) | copy-start | bytes 122884
  30.3 1.7 %collective-permute-start.5 = (bf16[64,2688]{1,0:T(8,128)(2,1)S(1)}, bf16[64,2688]{1,0:T(8,128)(2,1)S(1)}, u32[]{:S(2)}, u32[]{:S(2)}) collective-permute-start(bf16[64,2688]{1,0:T(8,128)(2,1)S(1)} %get-tuple-element.14), channel_id=1, source_target_pairs={{1,0},{0,1},{3,2},{2,3},{5,4},{4,5},{7,6},{6,7},{9,8},{8,9},{11,10... | collective-permute-start | bytes 1032200 | tf_op jit(solution)/shard_map/ppermute | solution.py:209
  32.5 6.5 %collective-permute-start.6 = (bf16[32,2688]{1,0:T(8,128)(2,1)S(1)}, bf16[32,2688]{1,0:T(8,128)(2,1)S(1)}, u32[]{:S(2)}, u32[]{:S(2)}) collective-permute-start(bf16[32,2688]{1,0:T(8,128)(2,1)S(1)} %get-tuple-element.16), channel_id=1, source_target_pairs={{2,0},{3,1},{0,2},{1,3},{6,4},{7,5},{4,6},{5,7},{10,8},{11,9},{8,1... | collective-permute-start | bytes 516104 | tf_op jit(solution)/shard_map/ppermute | solution.py:209
  39.2 6.0 %collective-permute-start.7 = (bf16[8,2688]{1,0:T(8,128)(2,1)S(1)}, bf16[8,2688]{1,0:T(8,128)(2,1)S(1)}, u32[]{:S(2)}, u32[]{:S(2)}) collective-permute-start(bf16[8,2688]{1,0:T(8,128)(2,1)S(1)} %get-tuple-element.18), channel_id=1, source_target_pairs={{12,0},{13,1},{14,2},{15,3},{0,4},{1,5},{2,6},{3,7},{4,8},{5,9},{6... | collective-permute-start | bytes 129032 | tf_op jit(solution)/shard_map/ppermute | solution.py:209
  39.6 6.7 %collective-permute-start.8 = (bf16[8,2688]{1,0:T(8,128)(2,1)S(1)}, bf16[8,2688]{1,0:T(8,128)(2,1)S(1)}, u32[]{:S(2)}, u32[]{:S(2)}) collective-permute-start(bf16[8,2688]{1,0:T(8,128)(2,1)S(1)} %get-tuple-element.19), channel_id=1, source_target_pairs={{8,0},{9,1},{10,2},{11,3},{12,4},{13,5},{14,6},{15,7},{0,8},{1,9},... | collective-permute-start | bytes 129032 | tf_op jit(solution)/shard_map/ppermute | solution.py:209
  43.0 4.0 %collective-permute-start.9 = (bf16[8,2688]{1,0:T(8,128)(2,1)S(1)}, bf16[8,2688]{1,0:T(8,128)(2,1)S(1)}, u32[]{:S(2)}, u32[]{:S(2)}) collective-permute-start(bf16[8,2688]{1,0:T(8,128)(2,1)S(1)} %get-tuple-element.20), channel_id=1, source_target_pairs={{4,0},{5,1},{6,2},{7,3},{8,4},{9,5},{10,6},{11,7},{12,8},{13,9},{1... | collective-permute-start | bytes 129032 | tf_op jit(solution)/shard_map/ppermute | solution.py:209

commit v2 on v1

v2 whole, which is shorter than its diff:
```python
import functools
import math

import jax
import jax.numpy as jnp
from jax import lax
from jax.experimental import pallas as pl
from jax.experimental.pallas import tpu as pltpu
from jax.sharding import PartitionSpec as P

HD = 128
BLK = 128
STAT = 128
LANE = STAT // 3
NEG = -1e30
F32 = jnp.float32
BF16 = jnp.bfloat16


def factors(members):
    cores = 2 if members % 2 == 0 else 1
    chips = members // cores
    far = next(a for a in range(1, chips + 1) if chips % a == 0 and a * a >= chips)
    return far, chips // far, cores


def shift_perm(shape, axis, by):
    a_n, b_n, c_n = shape
    pairs = []
    for a in range(a_n):
        for b in range(b_n):
            for c in range(c_n):
                at = [a, b, c]
                src = list(at)
                src[axis] = (src[axis] + by) % shape[axis]
                flat = lambda p: (p[0] * b_n + p[1]) * c_n + p[2]
                pairs.append((flat(src), flat(at)))
    return pairs


def lanes(rows):
    return lax.broadcasted_iota(jnp.int32, (rows, STAT), 1)


def pack_stats(top, mass):
    high = mass.astype(BF16).astype(F32)
    return top + pltpu.roll(high, LANE, 1) + pltpu.roll(mass - high, 2 * LANE, 1)


def unpack_stats(packed, heads):
    used = lanes(packed.shape[0]) < heads
    mass = pltpu.roll(packed, STAT - LANE, 1) + pltpu.roll(packed, STAT - 2 * LANE, 1)
    return jnp.where(used, packed, 0.0), jnp.where(used, mass, 0.0)


def attend_kernel(sizes, scale, refs):
    parts, loads, group = sizes
    bias_ref, refs = refs[0], refs[1:]
    q_refs, refs = refs[:parts], refs[parts:]
    sources, refs = refs[:4], refs[4:]
    home_ref, away_refs, refs = refs[0], refs[1 : len(refs) - 7], refs[len(refs) - 7 :]
    buffers, sems, top_acc, mass_acc = refs[:4], refs[4], refs[5], refs[6]
    k_buf, v_buf, nk_buf, nv_buf = buffers
    outs = [(o, j) for o in (home_ref, *away_refs) for j in range(o.shape[0])]
    per = q_refs[0].shape[0]
    rows = per * parts
    wide = group * HD
    lane = lanes(rows)
    contract_last = (((1,), (1,)), ((), ()))

    def copies(load):
        cols = pl.ds(pl.multiple_of(load * wide, HD), wide)
        return [
            pltpu.make_async_copy(src.at[:, cols], dst.at[:, cols], sems.at[i, load])
            for i, (src, dst) in enumerate(zip(sources[:2], buffers[:2]))
        ]

    fresh_copies = [
        pltpu.make_async_copy(src, dst, sems.at[2 + i, 0])
        for i, (src, dst) in enumerate(zip(sources[2:], buffers[2:]))
    ]

    @pl.when(pl.program_id(0) == 0)
    def _():
        for copy in copies(0) + fresh_copies:
            copy.start()
        for load in range(1, loads):
            for copy in copies(load):
                copy.start()
        for copy in fresh_copies:
            copy.wait()

    top_acc[...] = jnp.zeros_like(top_acc)
    mass_acc[...] = jnp.zeros_like(mass_acc)
    bias = bias_ref[...]

    def heads_of(load, carry):
        @pl.when(pl.program_id(0) == 0)
        def _():
            for copy in copies(load):
                copy.wait()

        def columns(i):
            return pl.ds(pl.multiple_of((load * group + i) * HD, HD), HD)

        def scores(i):
            cols = columns(i)
            q = jnp.concatenate([r[:, cols] for r in q_refs], axis=0)
            cached = lax.dot_general(q, k_buf[:, cols], contract_last, preferred_element_type=F32)
            fresh = lax.dot_general(q, nk_buf[:, cols], contract_last, preferred_element_type=F32)
            return cached, fresh

        tops = top_acc[...]
        masses = mass_acc[...]
        ahead = scores(0)
        for i in range(group):
            cached, fresh = ahead
            if i + 1 < group:
                ahead = scores(i + 1)
            cached = cached * scale + bias
            fresh = fresh * scale
            top = jnp.maximum(
                jnp.max(cached, axis=1, keepdims=True), jnp.max(fresh, axis=1, keepdims=True)
            )
            top = top.astype(BF16).astype(F32)
            cached = jnp.exp2(cached - top)
            fresh = jnp.exp2(fresh - top)
            mass = jnp.sum(cached, axis=1, keepdims=True) + jnp.sum(fresh, axis=1, keepdims=True)
            cols = columns(i)
            out = jnp.dot(cached.astype(BF16), v_buf[:, cols], preferred_element_type=F32)
            out = out + jnp.dot(fresh.astype(BF16), nv_buf[:, cols], preferred_element_type=F32)
            for p, (o_ref, j) in enumerate(outs):
                o_ref[j, :, cols] = out[p * per : (p + 1) * per].astype(o_ref.dtype)
            head = load * group + i
            tops = jnp.where(lane == head, top, tops)
            masses = jnp.where(lane == head, mass, masses)
        top_acc[...] = tops
        mass_acc[...] = masses
        return carry

    lax.fori_loop(0, loads, heads_of, 0)
    packed = pack_stats(top_acc[...], mass_acc[...])
    for p, (o_ref, j) in enumerate(outs):
        width = o_ref.shape[2]
        o_ref[j, :, width - STAT :] = packed[p * per : (p + 1) * per].astype(o_ref.dtype)


def attend(parts, keys, values, new_keys, new_values, bias):
    flat = [p for core in parts for p in core]
    n = len(flat)
    rows, columns = flat[0].shape
    heads = columns // HD
    group = next(g for g in (5, 4, 2, 1) if heads % g == 0)
    loads = heads // group
    tile = min(rows, max(16, 128 // n))
    cache_rows = keys.shape[0]
    width = columns + STAT
    scale = math.log2(math.e) / math.sqrt(HD)
    stack = len(parts[0])

    def body(*refs):
        attend_kernel((n, loads, group), scale, refs)

    in_hbm = pl.BlockSpec(memory_space=pltpu.HBM)
    return pl.pallas_call(
        body,
        grid=(rows // tile,),
        in_specs=[pl.BlockSpec((1, cache_rows), lambda r: (0, 0))]
        + [pl.BlockSpec((tile, columns), lambda r: (r, 0))] * n
        + [in_hbm] * 4,
        out_specs=[pl.BlockSpec((stack, tile, width), lambda r: (0, r, 0))] * len(parts),
        out_shape=[
            jax.ShapeDtypeStruct((stack, rows, width), F32 if c == 0 else BF16)
            for c in range(len(parts))
        ],
        scratch_shapes=[pltpu.VMEM(x.shape, x.dtype) for x in (keys, values, new_keys, new_values)]
        + [pltpu.SemaphoreType.DMA((4, loads))]
        + [pltpu.VMEM((tile * n, STAT), F32)] * 2,
        compiler_params=pltpu.CompilerParams(
            dimension_semantics=("arbitrary",), vmem_limit_bytes=40 * 1024 * 1024
        ),
        cost_estimate=pl.CostEstimate(
            flops=4 * n * rows * cache_rows * columns,
            bytes_accessed=4 * cache_rows * columns,
            transcendentals=n * rows * cache_rows * heads,
        ),
        name="attend",
    )(bias, *flat, keys, values, new_keys, new_values)


def merged(arrays, heads, last):
    columns = heads * HD
    stats = [unpack_stats(get(slice(columns, columns + STAT)), heads) for get in arrays]
    top = functools.reduce(jnp.maximum, [t for t, _ in stats])
    weights = [jnp.exp2(t - top) for t, _ in stats]
    mass = functools.reduce(jnp.add, [w * m for w, (_, m) in zip(weights, stats)])
    if last:
        inverse = 1.0 / jnp.where(lanes(mass.shape[0]) < heads, mass, 1.0)
        weights = [w * inverse for w in weights]
    for head in range(heads):
        cols = slice(head * HD, (head + 1) * HD)
        yield cols, functools.reduce(
            jnp.add, [get(cols) * w[:, head : head + 1] for get, w in zip(arrays, weights)]
        )
    if not last:
        yield slice(columns, columns + STAT), pack_stats(top, mass)


def getter(ref, *index):
    return lambda cols: ref[(*index, slice(None), cols)].astype(F32)


def merge_stacks(ins, heads):
    layers, rows, width = ins[0].shape

    def body(*refs):
        for j in range(layers):
            out = refs[len(ins) + j]
            for cols, total in merged([getter(r, j) for r in refs[: len(ins)]], heads, False):
                out[:, cols] = total.astype(out.dtype)

    return call_merge(
        body, ins, [jax.ShapeDtypeStruct((rows, width), F32 if j == 0 else BF16) for j in range(layers)]
    )


def merge_rows(ins, heads, pieces):
    rows, width = ins[0].shape
    per = rows // pieces

    def body(*refs):
        out = refs[len(ins)]
        for cols, total in merged([getter(r) for r in refs[: len(ins)]], heads, False):
            for j in range(pieces):
                out[j, :, cols] = total[j * per : (j + 1) * per].astype(out.dtype)

    return call_merge(body, ins, [jax.ShapeDtypeStruct((pieces, per, width), BF16)])[0]


def finish(stack, heads):
    pieces, rows, width = stack.shape

    def body(ref, out):
        for cols, total in merged([getter(ref, j) for j in range(pieces)], heads, True):
            out[:, cols] = total.astype(out.dtype)

    return call_merge(body, [stack], [jax.ShapeDtypeStruct((rows, heads * HD), BF16)])[0]


def call_merge(body, ins, shapes):
    size = sum(math.prod(x.shape) for x in ins)
    return pl.pallas_call(
        body,
        in_specs=[pl.BlockSpec(memory_space=pltpu.VMEM)] * len(ins),
        out_specs=[pl.BlockSpec(memory_space=pltpu.VMEM)] * len(shapes),
        out_shape=shapes,
        compiler_params=pltpu.CompilerParams(vmem_limit_bytes=48 * 1024 * 1024),
        cost_estimate=pl.CostEstimate(flops=4 * size, bytes_accessed=4 * size, transcendentals=0),
        name="merge",
    )(*ins)


def per_device(queries, new_keys, new_values, cache_keys, cache_values, victims):
    members = lax.axis_size("seq")
    shape = factors(members)
    a_n, b_n, c_n = shape
    heads = queries.shape[1] // HD
    block_count = cache_keys.shape[0] // BLK
    block_ids = lax.axis_index("seq") * block_count + jnp.arange(block_count, dtype=jnp.int32)
    evicted = jnp.any(victims[:, None] == block_ids[None, :], axis=0)
    bias = jnp.repeat(jnp.where(evicted, NEG, 0.0), BLK)[None, :]

    def fetch(x, axis, by):
        return lax.ppermute(x, "seq", shift_perm(shape, axis, by))

    def give(x, axis, by):
        return lax.ppermute(x, "seq", shift_perm(shape, axis, -by))

    lines = [[(a * b_n * c_n) + rest for a in range(a_n)] for rest in range(b_n * c_n)]

    def exchange(stack):
        return lax.all_to_all(
            stack, "seq", split_axis=0, concat_axis=0, axis_index_groups=lines, tiled=True
        )

    tok = queries.shape[0]
    line = exchange(jnp.broadcast_to(queries[None], (a_n, *queries.shape)))
    line = line.reshape(a_n * tok, -1)
    plane = [line] + [fetch(line, 1, d) for d in range(1, b_n)]
    parts = [plane] + [[fetch(x, 2, d) for x in plane] for d in range(1, c_n)]

    sums = attend(parts, cache_keys, cache_values, new_keys, new_values, bias)
    sums = [sums[0]] + [give(s, 2, d + 1) for d, s in enumerate(sums[1:])]
    sums = merge_stacks(sums, heads)
    sums = [sums[0]] + [give(s, 1, d + 1) for d, s in enumerate(sums[1:])]
    return finish(exchange(merge_rows(sums, heads, a_n)), heads)


def solution(mesh):
    rows = P(("groups", "seq"), None)
    return jax.shard_map(
        per_device,
        mesh=mesh,
        in_specs=(rows, rows, rows, rows, rows, P("groups")),
        out_specs=rows,
        check_vma=False,
    )
```

time: 48.3 us -> 51.3 us (1.062)
  blocking collectives: 0 us -> 9.61 us
  starting transfers between devices: 14.4 us -> 9.7 us
  Pallas kernels: 9.08 us -> 6.91 us
  other arithmetic: 1.64 us -> 0.85 us
  local copies, waits for them, and re-layouts: 5.94 us -> 6.55 us
    all_to_all x0 -> x1, blocking collectives: none -> 9.61 us  [exchange(): lax.all_to_all(stack, 'seq', split_axis=0, concat_axis=0, axis_index_grou...]
    ppermute x5 -> x3, starting transfers between devices: 8.62 us -> 1.59 us  [fetch(): return lax.ppermute(x, 'seq', shift_perm(shape, axis, by))]
    all_to_all x0 -> x1, waiting for transfers between devices: none -> 6.43 us  [exchange(): lax.all_to_all(stack, 'seq', split_axis=0, concat_axis=0, axis_index_grou...]
    all_to_all x0 -> x1, starting transfers between devices: none -> 6.32 us  [exchange(): lax.all_to_all(stack, 'seq', split_axis=0, concat_axis=0, axis_index_grou...]
    ppermute x5 -> x2, starting transfers between devices: 5.76 us -> 1.8 us  [give(): return lax.ppermute(x, 'seq', shift_perm(shape, axis, -by))]
    ppermute x5 -> x2, waiting for transfers between devices: 10.2 us -> 6.41 us  [give(): return lax.ppermute(x, 'seq', shift_perm(shape, axis, -by))]
    ppermute x5 -> x3, waiting for transfers between devices: 6.58 us -> 4.27 us  [fetch(): return lax.ppermute(x, 'seq', shift_perm(shape, axis, by))]
    pallas_call x4, Pallas kernels: 9.08 us -> 6.91 us  [the longest x1 5.22 us: attend(): pl.pallas_call(body, grid=(rows // tile,), in_specs=[pl.BlockSpec((1, cac...]
  transfers between devices with their start and end apart: 10 -> 6, of which waited for: 9 -> 5; matrix products, arithmetic and copies ran while one was open for 4% -> 2% of each run, Pallas kernels for 0% -> 0%
where the time goes in v2:
time: 51.3 us; the launch traced here: 50.8 us
  waiting for transfers between devices  17.1 us (33%)
  starting transfers between devices  9.7 us (19%)
  blocking collectives  9.61 us (19%)
  Pallas kernels  6.91 us (13%)
  local copies, waits for them, and re-layouts  6.55 us (13%)
  other arithmetic  0.85 us (2%)
    all_to_all x1, blocking collectives, exchange(): lax.all_to_all(stack, 'seq', split_axis=0, concat_axis=0, axis_index_grou...  9.61 us
    all_to_all x1, waiting for transfers between devices, exchange(): lax.all_to_all(stack, 'seq', split_axis=0, concat_axis=0, axis_index_grou...  6.43 us
    ppermute x2, waiting for transfers between devices, give(): return lax.ppermute(x, 'seq', shift_perm(shape, axis, -by))  6.41 us
    all_to_all x1, starting transfers between devices, exchange(): lax.all_to_all(stack, 'seq', split_axis=0, concat_axis=0, axis_index_grou...  6.32 us
    pallas_call x1, Pallas kernels, attend(): pl.pallas_call(body, grid=(rows // tile,), in_specs=[pl.BlockSpec((1, cac...  5.22 us
    unnamed x8, local copies, waits for them, and re-layouts  5.04 us
    ppermute x3, waiting for transfers between devices, fetch(): return lax.ppermute(x, 'seq', shift_perm(shape, axis, by))  4.27 us
    ppermute x2, starting transfers between devices, give(): return lax.ppermute(x, 'seq', shift_perm(shape, axis, -by))  1.8 us
  transfers between devices with their start and end apart: 6, of which 5 were waited for; matrix products, arithmetic and copies ran while one was open for 2% of the time, Pallas kernels for 0%

profile of v2, /device:TPU:0, one launch (start us, length us, event | category | flops | bytes accessed | tf_op | source)
XLA Modules:
  0.0 50.8 jit_solution(7736144101234811258)
XLA Ops:
  0.0 1.4 %broadcast_in_dim.22 = bf16[4,8,2560]{2,1,0:T(8,128)(2,1)} broadcast(bf16[8,2560]{1,0:T(8,128)(2,1)} %param.6), dimensions={1,2} | broadcast | bytes 204800 | tf_op jit(solution)/shard_map/broadcast_in_dim | solution.py:287
  1.4 6.3 %all-to-all-start = ((bf16[4,8,2560]{2,1,0:T(8,128)(2,1)}), bf16[4,8,2560]{2,1,0:T(8,128)(2,1)S(1)}, u32[]{:S(2)}, u32[]{:S(2)}) async-start(bf16[4,8,2560]{2,1,0:T(8,128)(2,1)} %broadcast_in_dim.22), calls=%async_computation | async-start | bytes 327680 | tf_op jit(solution)/shard_map/all_to_all | solution.py:282
  7.8 6.4 %all-to-all-done = bf16[4,8,2560]{2,1,0:T(8,128)(2,1)S(1)} async-done(((bf16[4,8,2560]{2,1,0:T(8,128)(2,1)}), bf16[4,8,2560]{2,1,0:T(8,128)(2,1)S(1)}, u32[]{:S(2)}, u32[]{:S(2)}) %all-to-all-start) | async-done | bytes 163872 | tf_op jit(solution)/shard_map/all_to_all | solution.py:282
  14.2 1.5 %collective-permute-start = (bf16[32,2560]{1,0:T(8,128)(2,1)S(1)}, bf16[32,2560]{1,0:T(8,128)(2,1)S(1)}, u32[]{:S(2)}, u32[]{:S(2)}) collective-permute-start(bf16[32,2560]{1,0:T(8,128)(2,1)S(1)} %bitcast.2), channel_id=1, source_target_pairs={{2,0},{3,1},{0,2},{1,3},{6,4},{7,5},{4,6},{5,7},{10,8},{11,9},{8,1... | collective-permute-start | bytes 491528 | tf_op jit(solution)/shard_map/ppermute | solution.py:274
  15.7 0.8 %compare_reduce_fusion = pred[4]{0:T(512)(128)(4,1)S(1)} fusion(s32[16]{0:T(128)} %param.11, s32[4]{0:T(128)S(1)} %iota_add_fusion), kind=kLoop, calls=%fused_computation | loop fusion | flops 124 | bytes 84 | tf_op jit(solution)/shard_map/reduce_or | solution.py:270
  16.6 0.1 collective-permute-start.1
  16.6 2.9 %collective-permute-done.refs_2_ = bf16[32,2560]{1,0:T(8,128)(2,1)S(1)} collective-permute-done((bf16[32,2560]{1,0:T(8,128)(2,1)S(1)}, bf16[32,2560]{1,0:T(8,128)(2,1)S(1)}, u32[]{:S(2)}, u32[]{:S(2)}) %collective-permute-start) | collective-permute-done | bytes 163872 | tf_op jit(solution)/shard_map/ppermute | solution.py:274
  19.5 0.0 collective-permute-start.2
  19.5 0.0 collective-permute-done.1.refs_3_
  19.5 1.4 %collective-permute-done.2.refs_4_ = bf16[32,2560]{1,0:T(8,128)(2,1)S(1)} collective-permute-done((bf16[32,2560]{1,0:T(8,128)(2,1)S(1)}, bf16[32,2560]{1,0:T(8,128)(2,1)S(1)}, u32[]{:S(2)}, u32[]{:S(2)}) %collective-permute-start.2) | collective-permute-done | bytes 163872 | tf_op jit(solution)/shard_map/ppermute | solution.py:274
  20.9 0.1 broadcast_in_dim.21
  21.0 0.0 copy-start
  21.0 1.7 %copy-done = bf16[512,2560]{1,0:T(8,128)(2,1)S(1)} copy-done((bf16[512,2560]{1,0:T(8,128)(2,1)S(1)}, bf16[512,2560]{1,0:T(8,128)(2,1)}, u32[]{:S(2)}) %copy-start) | copy-done | bytes 2621464
  22.7 0.0 copy-start.1
  22.7 1.7 %copy-done.1 = bf16[512,2560]{1,0:T(8,128)(2,1)S(1)} copy-done((bf16[512,2560]{1,0:T(8,128)(2,1)S(1)}, bf16[512,2560]{1,0:T(8,128)(2,1)}, u32[]{:S(2)}) %copy-start.1) | copy-done | bytes 2621464
  24.5 0.0 copy-start.2
  24.5 0.8 %copy-done.2 = bf16[8,2560]{1,0:T(8,128)(2,1)S(1)} copy-done((bf16[8,2560]{1,0:T(8,128)(2,1)S(1)}, bf16[8,2560]{1,0:T(8,128)(2,1)}, u32[]{:S(2)}) %copy-start.2) | copy-done | bytes 40984
  25.2 0.0 copy-start.3
  25.2 0.8 %copy-done.3 = bf16[8,2560]{1,0:T(8,128)(2,1)S(1)} copy-done((bf16[8,2560]{1,0:T(8,128)(2,1)S(1)}, bf16[8,2560]{1,0:T(8,128)(2,1)}, u32[]{:S(2)}) %copy-start.3) | copy-done | bytes 40984
  26.0 5.2 %attend.1 = (f32[2,32,2688]{2,1,0:T(8,128)S(1)}, bf16[2,32,2688]{2,1,0:T(8,128)(2,1)S(1)}) custom-call(f32[1,512]{1,0:T(1,128)S(1)} %bitcast.5, bf16[32,2560]{1,0:T(8,128)(2,1)S(1)} %bitcast.4, bf16[32,2560]{1,0:T(8,128)(2,1)S(1)} %collective-permute-done.refs_2_, bf16[32,2560]{1,0:T(8,128)(2,1)S(1)} %collective-permute-done.1.refs_3_, ...), custom_call_target="tpu_custom_call" | custom-call | flops 671088640 | bytes 5242880 | tf_op jit(solution)/shard_map/attend/pallas_call | solution.py:165
  31.2 0.2 collective-permute-start.3
  31.5 1.5 %collective-permute-done.3.refs_1_ = bf16[2,32,2688]{2,1,0:T(8,128)(2,1)S(1)} collective-permute-done((bf16[2,32,2688]{2,1,0:T(8,128)(2,1)S(1)}, bf16[2,32,2688]{2,1,0:T(8,128)(2,1)S(1)}, u32[]{:S(2)}, u32[]{:S(2)}) %collective-permute-start.3) | collective-permute-done | bytes 344096 | tf_op jit(solution)/shard_map/ppermute | solution.py:277
  33.0 0.5 %merge.3 = (f32[32,2688]{1,0:T(8,128)S(1)}, bf16[32,2688]{1,0:T(8,128)(2,1)S(1)}) custom-call(f32[2,32,2688]{2,1,0:T(8,128)S(1)} %get-tuple-element.9.refs_0_, bf16[2,32,2688]{2,1,0:T(8,128)(2,1)S(1)} %collective-permute-done.3.refs_1_), custom_call_target="tpu_custom_call" | custom-call | flops 1376256 | bytes 1376256 | tf_op jit(solution)/shard_map/merge/pallas_call | solution.py:252
  33.5 1.6 %collective-permute-start.4 = (bf16[32,2688]{1,0:T(8,128)(2,1)S(1)}, bf16[32,2688]{1,0:T(8,128)(2,1)S(1)}, u32[]{:S(2)}, u32[]{:S(2)}) collective-permute-start(bf16[32,2688]{1,0:T(8,128)(2,1)S(1)} %get-tuple-element.12), channel_id=1, source_target_pairs={{2,0},{3,1},{0,2},{1,3},{6,4},{7,5},{4,6},{5,7},{10,8},{11,9},{8,1... | collective-permute-start | bytes 516104 | tf_op jit(solution)/shard_map/ppermute | solution.py:277
  35.1 4.9 %collective-permute-done.4.refs_1_ = bf16[32,2688]{1,0:T(8,128)(2,1)S(1)} collective-permute-done((bf16[32,2688]{1,0:T(8,128)(2,1)S(1)}, bf16[32,2688]{1,0:T(8,128)(2,1)S(1)}, u32[]{:S(2)}, u32[]{:S(2)}) %collective-permute-start.4) | collective-permute-done | bytes 172064 | tf_op jit(solution)/shard_map/ppermute | solution.py:277
  40.0 0.3 merge.4
  40.3 9.6 %all_to_all.10.ref = bf16[4,8,2688]{2,1,0:T(8,128)(2,1)S(1)} all-to-all(bf16[4,8,2688]{2,1,0:T(8,128)(2,1)S(1)} %merge.4), channel_id=1, replica_groups={{0,4,8,12},{1,5,9,13},{2,6,10,14},{3,7,11,15},{16,20,24,28},{17,21,25,2..., dimensions={0} | all-to-all | bytes 344064 | tf_op jit(solution)/shard_map/all_to_all | solution.py:282
  49.9 0.9 %merge.5 = bf16[8,2560]{1,0:T(8,128)(2,1)} custom-call(bf16[4,8,2688]{2,1,0:T(8,128)(2,1)S(1)} %all_to_all.10.ref), custom_call_target="tpu_custom_call" | custom-call | flops 344064 | bytes 344064 | tf_op jit(solution)/shard_map/merge/pallas_call | solution.py:252
  (2 shorter events, 0.0 us)
Async XLA Ops:
  1.4 12.7 %all-to-all-start = ((bf16[4,8,2560]{2,1,0:T(8,128)(2,1)}), bf16[4,8,2560]{2,1,0:T(8,128)(2,1)S(1)}, u32[]{:S(2)}, u32[]{:S(2)}) async-start(bf16[4,8,2560]{2,1,0:T(8,128)(2,1)} %broadcast_in_dim.22), calls=%async_computation | async-start | bytes 327680 | tf_op jit(solution)/shard_map/all_to_all | solution.py:282
  14.2 5.3 %collective-permute-start = (bf16[32,2560]{1,0:T(8,128)(2,1)S(1)}, bf16[32,2560]{1,0:T(8,128)(2,1)S(1)}, u32[]{:S(2)}, u32[]{:S(2)}) collective-permute-start(bf16[32,2560]{1,0:T(8,128)(2,1)S(1)} %bitcast.2), channel_id=1, source_target_pairs={{2,0},{3,1},{0,2},{1,3},{6,4},{7,5},{4,6},{5,7},{10,8},{11,9},{8,1... | collective-permute-start | bytes 491528 | tf_op jit(solution)/shard_map/ppermute | solution.py:274
  16.6 3.0 %collective-permute-start.1 = (bf16[32,2560]{1,0:T(8,128)(2,1)S(1)}, bf16[32,2560]{1,0:T(8,128)(2,1)S(1)}, u32[]{:S(2)}, u32[]{:S(2)}) collective-permute-start(bf16[32,2560]{1,0:T(8,128)(2,1)S(1)} %bitcast.3), channel_id=1, source_target_pairs={{1,0},{0,1},{3,2},{2,3},{5,4},{4,5},{7,6},{6,7},{9,8},{8,9},{11,10... | collective-permute-start | bytes 491528 | tf_op jit(solution)/shard_map/ppermute | solution.py:274
  19.5 1.4 %collective-permute-start.2 = (bf16[32,2560]{1,0:T(8,128)(2,1)S(1)}, bf16[32,2560]{1,0:T(8,128)(2,1)S(1)}, u32[]{:S(2)}, u32[]{:S(2)}) collective-permute-start(bf16[32,2560]{1,0:T(8,128)(2,1)S(1)} %collective-permute-done.refs_2_), channel_id=1, source_target_pairs={{1,0},{0,1},{3,2},{2,3},{5,4},{4,5},{7,6},{6,7},{9,8},{8,9},{11,10... | collective-permute-start | bytes 491528 | tf_op jit(solution)/shard_map/ppermute | solution.py:274
  21.0 1.7 %copy-start = (bf16[512,2560]{1,0:T(8,128)(2,1)S(1)}, bf16[512,2560]{1,0:T(8,128)(2,1)}, u32[]{:S(2)}) copy-start(bf16[512,2560]{1,0:T(8,128)(2,1)} %refs_5_.1) | copy-start | bytes 7864324
  22.7 1.7 %copy-start.1 = (bf16[512,2560]{1,0:T(8,128)(2,1)S(1)}, bf16[512,2560]{1,0:T(8,128)(2,1)}, u32[]{:S(2)}) copy-start(bf16[512,2560]{1,0:T(8,128)(2,1)} %refs_6_.1) | copy-start | bytes 7864324
  24.5 0.8 %copy-start.2 = (bf16[8,2560]{1,0:T(8,128)(2,1)S(1)}, bf16[8,2560]{1,0:T(8,128)(2,1)}, u32[]{:S(2)}) copy-start(bf16[8,2560]{1,0:T(8,128)(2,1)} %refs_7_.1) | copy-start | bytes 122884
  25.2 0.8 %copy-start.3 = (bf16[8,2560]{1,0:T(8,128)(2,1)S(1)}, bf16[8,2560]{1,0:T(8,128)(2,1)}, u32[]{:S(2)}) copy-start(bf16[8,2560]{1,0:T(8,128)(2,1)} %refs_8_.1) | copy-start | bytes 122884
  31.2 1.7 %collective-permute-start.3 = (bf16[2,32,2688]{2,1,0:T(8,128)(2,1)S(1)}, bf16[2,32,2688]{2,1,0:T(8,128)(2,1)S(1)}, u32[]{:S(2)}, u32[]{:S(2)}) collective-permute-start(bf16[2,32,2688]{2,1,0:T(8,128)(2,1)S(1)} %get-tuple-element.10), channel_id=1, source_target_pairs={{1,0},{0,1},{3,2},{2,3},{5,4},{4,5},{7,6},{6,7},{9,8},{8,9},{11,10... | collective-permute-start | bytes 1032200 | tf_op jit(solution)/shard_map/ppermute | solution.py:277
  33.5 6.5 %collective-permute-start.4 = (bf16[32,2688]{1,0:T(8,128)(2,1)S(1)}, bf16[32,2688]{1,0:T(8,128)(2,1)S(1)}, u32[]{:S(2)}, u32[]{:S(2)}) collective-permute-start(bf16[32,2688]{1,0:T(8,128)(2,1)S(1)} %get-tuple-element.12), channel_id=1, source_target_pairs={{2,0},{3,1},{0,2},{1,3},{6,4},{7,5},{4,6},{5,7},{10,8},{11,9},{8,1... | collective-permute-start | bytes 516104 | tf_op jit(solution)/shard_map/ppermute | solution.py:277

commit v3 on v2

--- a/solution.py
+++ b/solution.py
@@ -162,6 +162,7 @@
         attend_kernel((n, loads, group), scale, refs)
 
     in_hbm = pl.BlockSpec(memory_space=pltpu.HBM)
+    held = (keys, values, new_keys, new_values)
     return pl.pallas_call(
         body,
         grid=(rows // tile,),
@@ -173,7 +174,7 @@
             jax.ShapeDtypeStruct((stack, rows, width), F32 if c == 0 else BF16)
             for c in range(len(parts))
         ],
-        scratch_shapes=[pltpu.VMEM(x.shape, x.dtype) for x in (keys, values, new_keys, new_values)]
+        scratch_shapes=[pltpu.VMEM(x.shape, x.dtype) for x in held]
         + [pltpu.SemaphoreType.DMA((4, loads))]
         + [pltpu.VMEM((tile * n, STAT), F32)] * 2,
         compiler_params=pltpu.CompilerParams(
@@ -185,7 +186,7 @@
             transcendentals=n * rows * cache_rows * heads,
         ),
         name="attend",
-    )(bias, *flat, keys, values, new_keys, new_values)
+    )(bias, *flat, *[pltpu.with_memory_space_constraint(x, pltpu.HBM) for x in held])
 
 
 def merged(arrays, heads, last):
@@ -210,41 +211,39 @@
     return lambda cols: ref[(*index, slice(None), cols)].astype(F32)
 
 
-def merge_stacks(ins, heads):
-    layers, rows, width = ins[0].shape
-
-    def body(*refs):
-        for j in range(layers):
-            out = refs[len(ins) + j]
-            for cols, total in merged([getter(r, j) for r in refs[: len(ins)]], heads, False):
-                out[:, cols] = total.astype(out.dtype)
-
-    return call_merge(
-        body, ins, [jax.ShapeDtypeStruct((rows, width), F32 if j == 0 else BF16) for j in range(layers)]
-    )
-
-
-def merge_rows(ins, heads, pieces):
+def merge_rows(ins, heads, pieces, kinds):
     rows, width = ins[0].shape
     per = rows // pieces
 
     def body(*refs):
+        outs = refs[len(ins) :]
+        for cols, total in merged([getter(r) for r in refs[: len(ins)]], heads, False):
+            for j, out in enumerate(outs):
+                out[:, cols] = total[j * per : (j + 1) * per].astype(out.dtype)
+
+    return call_merge(body, ins, [jax.ShapeDtypeStruct((per, width), kind) for kind in kinds])
+
+
+def finish(ins, heads):
+    rows = ins[0].shape[0]
+
+    def body(*refs):
         out = refs[len(ins)]
-        for cols, total in merged([getter(r) for r in refs[: len(ins)]], heads, False):
-            for j in range(pieces):
-                out[j, :, cols] = total[j * per : (j + 1) * per].astype(out.dtype)
-
-    return call_merge(body, ins, [jax.ShapeDtypeStruct((pieces, per, width), BF16)])[0]
-
-
-def finish(stack, heads):
-    pieces, rows, width = stack.shape
-
-    def body(ref, out):
-        for cols, total in merged([getter(ref, j) for j in range(pieces)], heads, True):
+        for cols, total in merged([getter(r) for r in refs[: len(ins)]], heads, True):
             out[:, cols] = total.astype(out.dtype)
 
-    return call_merge(body, [stack], [jax.ShapeDtypeStruct((rows, heads * HD), BF16)])[0]
+    return call_merge(body, ins, [jax.ShapeDtypeStruct((rows, heads * HD), BF16)])[0]
+
+
+def join(pieces):
+    rows = sum(p.shape[0] for p in pieces)
+
+    def body(*refs):
+        out = refs[-1]
+        out[...] = jnp.concatenate([r[...].astype(F32) for r in refs[:-1]], axis=0).astype(out.dtype)
+
+    shape = jax.ShapeDtypeStruct((rows, pieces[0].shape[1]), pieces[0].dtype)
+    return call_merge(body, pieces, [shape])[0]
 
 
 def call_merge(body, ins, shapes):
@@ -276,24 +275,36 @@
     def give(x, axis, by):
         return lax.ppermute(x, "seq", shift_perm(shape, axis, -by))
 
-    lines = [[(a * b_n * c_n) + rest for a in range(a_n)] for rest in range(b_n * c_n)]
-
-    def exchange(stack):
-        return lax.all_to_all(
-            stack, "seq", split_axis=0, concat_axis=0, axis_index_groups=lines, tiled=True
-        )
-
-    tok = queries.shape[0]
-    line = exchange(jnp.broadcast_to(queries[None], (a_n, *queries.shape)))
-    line = line.reshape(a_n * tok, -1)
-    plane = [line] + [fetch(line, 1, d) for d in range(1, b_n)]
-    parts = [plane] + [[fetch(x, 2, d) for x in plane] for d in range(1, c_n)]
-
-    sums = attend(parts, cache_keys, cache_values, new_keys, new_values, bias)
-    sums = [sums[0]] + [give(s, 2, d + 1) for d, s in enumerate(sums[1:])]
-    sums = merge_stacks(sums, heads)
-    sums = [sums[0]] + [give(s, 1, d + 1) for d, s in enumerate(sums[1:])]
-    return finish(exchange(merge_rows(sums, heads, a_n)), heads)
+    far_first = sorted(range(1, a_n), key=lambda d: -min(d, a_n - d))
+    line = [queries] + [None] * (a_n - 1)
+    for d in far_first:
+        line[d] = fetch(queries, 0, d)
+    others = [[fetch(x, 1, d) for x in line] for d in range(1, b_n)]
+
+    def both_cores(pieces):
+        joined = join(pieces)
+        return [joined] + [fetch(joined, 2, d) for d in range(1, c_n)]
+
+    held = (cache_keys, cache_values, new_keys, new_values)
+
+    def partials(blocks, kinds):
+        cores = [both_cores(pieces) for pieces in blocks]
+        stacks = attend([[c[d] for c in cores] for d in range(c_n)], *held, bias)
+        back = [give(x, 2, d + 1) for d, x in enumerate(stacks[1:])]
+        return [
+            merge_rows([stacks[0][j]] + [x[j] for x in back], heads, a_n, kinds)
+            for j in range(len(blocks))
+        ]
+
+    own = partials([line], [F32] * a_n)[0]
+    got = [
+        [give(x, 1, d + 1) for x in pieces]
+        for d, pieces in enumerate(partials(others, [BF16] * a_n))
+    ]
+    sums = [[own[d]] + [pieces[d] for pieces in got] for d in range(a_n)]
+    for d in far_first:
+        sums[d] = [give(merge_rows(sums[d], heads, 1, [BF16])[0], 0, d)]
+    return finish([x for pieces in sums for x in pieces], heads)
 
 
 def solution(mesh):

time: 51.3 us -> 43.1 us (0.84)
  blocking collectives: 9.61 us -> 0 us
  starting transfers between devices: 9.7 us -> 19.2 us
  waiting for transfers between devices: 17.1 us -> 8.95 us
  Pallas kernels: 6.91 us -> 12.9 us
  local copies, waits for them, and re-layouts: 6.55 us -> 0.85 us
    all_to_all x1 -> x0, blocking collectives: 9.61 us -> none  [exchange(): lax.all_to_all(stack, 'seq', split_axis=0, concat_axis=0, axis_index_grou...]
    ppermute x3 -> x9, starting transfers between devices: 1.59 us -> 11.1 us  [fetch(): return lax.ppermute(x, 'seq', shift_perm(shape, axis, by))]
    all_to_all x1 -> x0, waiting for transfers between devices: 6.43 us -> none  [exchange(): lax.all_to_all(stack, 'seq', split_axis=0, concat_axis=0, axis_index_grou...]
    all_to_all x1 -> x0, starting transfers between devices: 6.32 us -> none  [exchange(): lax.all_to_all(stack, 'seq', split_axis=0, concat_axis=0, axis_index_grou...]
    ppermute x2 -> x9, starting transfers between devices: 1.8 us -> 8.08 us  [give(): return lax.ppermute(x, 'seq', shift_perm(shape, axis, -by))]
    pallas_call x1 -> x2, Pallas kernels: 5.22 us -> 11 us  [attend(): pl.pallas_call(body, grid=(rows // tile,), in_specs=[pl.BlockSpec((1, cac...]
    unnamed x8 -> x2, local copies, waits for them, and re-layouts: 5.04 us -> 0.78 us
    ppermute x2 -> x9, waiting for transfers between devices: 6.41 us -> 4.63 us  [give(): return lax.ppermute(x, 'seq', shift_perm(shape, axis, -by))]
  transfers between devices with their start and end apart: 6 -> 18, of which waited for: 5 -> 6; matrix products, arithmetic and copies ran while one was open for 2% -> 2% of each run, Pallas kernels for 0% -> 28%
where the time goes in v3:
time: 43.1 us; the launch traced here: 42.9 us
  starting transfers between devices  19.2 us (45%)
  Pallas kernels  12.9 us (30%)
  waiting for transfers between devices  8.95 us (21%)
  other arithmetic  0.85 us (2%)
  local copies, waits for them, and re-layouts  0.85 us (2%)
    ppermute x9, starting transfers between devices, fetch(): return lax.ppermute(x, 'seq', shift_perm(shape, axis, by))  11.1 us
    pallas_call x2, Pallas kernels, attend(): pl.pallas_call(body, grid=(rows // tile,), in_specs=[pl.BlockSpec((1, cac...  11 us
    ppermute x9, starting transfers between devices, give(): return lax.ppermute(x, 'seq', shift_perm(shape, axis, -by))  8.08 us
    ppermute x9, waiting for transfers between devices, give(): return lax.ppermute(x, 'seq', shift_perm(shape, axis, -by))  4.63 us
    ppermute x9, waiting for transfers between devices, fetch(): return lax.ppermute(x, 'seq', shift_perm(shape, axis, by))  4.32 us
    pallas_call x8, Pallas kernels, call_merge(): pl.pallas_call(body, in_specs=[pl.BlockSpec(memory_space=pltpu.VMEM)] * l...  1.95 us
  transfers between devices with their start and end apart: 18, of which 6 were waited for; matrix products, arithmetic and copies ran while one was open for 2% of the time, Pallas kernels for 28%

profile of v3, /device:TPU:0, one launch (start us, length us, event | category | flops | bytes accessed | tf_op | source)
XLA Modules:
  0.0 42.9 jit_solution(17002371165122935858)
XLA Ops:
  0.0 5.0 %collective-permute-start = (bf16[8,2560]{1,0:T(8,128)(2,1)}, bf16[8,2560]{1,0:T(8,128)(2,1)S(1)}, u32[]{:S(2)}, u32[]{:S(2)}) collective-permute-start(bf16[8,2560]{1,0:T(8,128)(2,1)} %refs_0_.1), channel_id=1, source_target_pairs={{4,0},{5,1},{6,2},{7,3},{8,4},{9,5},{10,6},{11,7},{12,8},{13,9},{1... | collective-permute-start | bytes 122888 | tf_op jit(solution)/shard_map/ppermute | solution.py:273
  5.1 1.0 %collective-permute-start.2 = (bf16[8,2560]{1,0:T(8,128)(2,1)}, bf16[8,2560]{1,0:T(8,128)(2,1)S(1)}, u32[]{:S(2)}, u32[]{:S(2)}) collective-permute-start(bf16[8,2560]{1,0:T(8,128)(2,1)} %refs_0_.1), channel_id=1, source_target_pairs={{12,0},{13,1},{14,2},{15,3},{0,4},{1,5},{2,6},{3,7},{4,8},{5,9},{6... | collective-permute-start | bytes 122888 | tf_op jit(solution)/shard_map/ppermute | solution.py:273
  6.1 1.5 %collective-permute-start.5 = (bf16[8,2560]{1,0:T(8,128)(2,1)}, bf16[8,2560]{1,0:T(8,128)(2,1)S(1)}, u32[]{:S(2)}, u32[]{:S(2)}) collective-permute-start(bf16[8,2560]{1,0:T(8,128)(2,1)} %refs_0_.1), channel_id=1, source_target_pairs={{2,0},{3,1},{0,2},{1,3},{6,4},{7,5},{4,6},{5,7},{10,8},{11,9},{8,1... | collective-permute-start | bytes 122888 | tf_op jit(solution)/shard_map/ppermute | solution.py:273
  7.6 1.0 %collective-permute-start.6 = (bf16[8,2560]{1,0:T(8,128)(2,1)S(1)}, bf16[8,2560]{1,0:T(8,128)(2,1)S(1)}, u32[]{:S(2)}, u32[]{:S(2)}) collective-permute-start(bf16[8,2560]{1,0:T(8,128)(2,1)S(1)} %collective-permute-done.refs_1_), channel_id=1, source_target_pairs={{2,0},{3,1},{0,2},{1,3},{6,4},{7,5},{4,6},{5,7},{10,8},{11,9},{8,1... | collective-permute-start | bytes 122888 | tf_op jit(solution)/shard_map/ppermute | solution.py:273
  8.6 1.6 %collective-permute-done.1.refs_2_ = bf16[8,2560]{1,0:T(8,128)(2,1)S(1)} collective-permute-done((bf16[8,2560]{1,0:T(8,128)(2,1)}, bf16[8,2560]{1,0:T(8,128)(2,1)S(1)}, u32[]{:S(2)}, u32[]{:S(2)}) %collective-permute-start.1) | collective-permute-done | bytes 40992 | tf_op jit(solution)/shard_map/ppermute | solution.py:273
  10.2 1.5 %collective-permute-start.7 = (bf16[8,2560]{1,0:T(8,128)(2,1)S(1)}, bf16[8,2560]{1,0:T(8,128)(2,1)S(1)}, u32[]{:S(2)}, u32[]{:S(2)}) collective-permute-start(bf16[8,2560]{1,0:T(8,128)(2,1)S(1)} %collective-permute-done.1.refs_2_), channel_id=1, source_target_pairs={{2,0},{3,1},{0,2},{1,3},{6,4},{7,5},{4,6},{5,7},{10,8},{11,9},{8,1... | collective-permute-start | bytes 122888 | tf_op jit(solution)/shard_map/ppermute | solution.py:273
  11.7 0.9 %collective-permute-start.8 = (bf16[8,2560]{1,0:T(8,128)(2,1)S(1)}, bf16[8,2560]{1,0:T(8,128)(2,1)S(1)}, u32[]{:S(2)}, u32[]{:S(2)}) collective-permute-start(bf16[8,2560]{1,0:T(8,128)(2,1)S(1)} %collective-permute-done.2.refs_3_), channel_id=1, source_target_pairs={{2,0},{3,1},{0,2},{1,3},{6,4},{7,5},{4,6},{5,7},{10,8},{11,9},{8,1... | collective-permute-start | bytes 122888 | tf_op jit(solution)/shard_map/ppermute | solution.py:273
  12.6 0.8 %compare_reduce_fusion = pred[4]{0:T(512)(128)(4,1)S(1)} fusion(s32[16]{0:T(128)} %param.11, s32[4]{0:T(128)S(1)} %iota_add_fusion), kind=kLoop, calls=%fused_computation | loop fusion | flops 124 | bytes 84 | tf_op jit(solution)/shard_map/reduce_or | solution.py:269
  13.4 0.8 %copy-done = bf16[8,2560]{1,0:T(8,128)(2,1)S(1)} copy-done((bf16[8,2560]{1,0:T(8,128)(2,1)S(1)}, bf16[8,2560]{1,0:T(8,128)(2,1)}, u32[]{:S(2)}) %copy-start) | copy-done | bytes 40984
  14.2 0.1 collective-permute-start.3
  14.3 1.4 %collective-permute-done.8.refs_3_ = bf16[8,2560]{1,0:T(8,128)(2,1)S(1)} collective-permute-done((bf16[8,2560]{1,0:T(8,128)(2,1)S(1)}, bf16[8,2560]{1,0:T(8,128)(2,1)S(1)}, u32[]{:S(2)}, u32[]{:S(2)}) %collective-permute-start.8) | collective-permute-done | bytes 40992 | tf_op jit(solution)/shard_map/ppermute | solution.py:273
  15.8 1.4 %collective-permute-done.9.refs_2_ = bf16[32,2560]{1,0:T(8,128)(2,1)S(1)} collective-permute-done((bf16[32,2560]{1,0:T(8,128)(2,1)S(1)}, bf16[32,2560]{1,0:T(8,128)(2,1)S(1)}, u32[]{:S(2)}, u32[]{:S(2)}) %collective-permute-start.9) | collective-permute-done | bytes 163872 | tf_op jit(solution)/shard_map/ppermute | solution.py:273
  17.2 5.5 %attend.3 = (f32[1,32,2688]{2,1,0:T(8,128)S(1)}, bf16[1,32,2688]{2,1,0:T(8,128)(2,1)S(1)}) custom-call(f32[1,512]{1,0:T(1,128)S(1)} %bitcast.9, bf16[32,2560]{1,0:T(8,128)(2,1)S(1)} %merge.10.refs_1_, bf16[32,2560]{1,0:T(8,128)(2,1)S(1)} %collective-permute-done.9.refs_2_, bf16[512,2560]{1,0:T(8,128)(2,1)} %refs_3_.3, bf16[512,2560]{1,0:T(8,128)(2,1)} %refs_4_.3, ...), custom_call_target="tpu_custom_call" | custom-call | flops 335544320 | bytes 5242880 | tf_op jit(solution)/shard_map/attend/pallas_call | solution.py:166
  22.7 0.2 collective-permute-start.10
  22.9 5.5 %attend.2 = (f32[1,32,2688]{2,1,0:T(8,128)S(1)}, bf16[1,32,2688]{2,1,0:T(8,128)(2,1)S(1)}) custom-call(f32[1,512]{1,0:T(1,128)S(1)} %bitcast.10, bf16[32,2560]{1,0:T(8,128)(2,1)S(1)} %merge.8.refs_1_, bf16[32,2560]{1,0:T(8,128)(2,1)S(1)} %collective-permute-done.3.refs_2_, bf16[512,2560]{1,0:T(8,128)(2,1)} %refs_3_.3, bf16[512,2560]{1,0:T(8,128)(2,1)} %refs_4_.3, ...), custom_call_target="tpu_custom_call" | custom-call | flops 335544320 | bytes 5242880 | tf_op jit(solution)/shard_map/attend/pallas_call | solution.py:166
  28.4 0.4 %collective-permute-start.4 = (bf16[1,32,2688]{2,1,0:T(8,128)(2,1)S(1)}, bf16[1,32,2688]{2,1,0:T(8,128)(2,1)S(1)}, u32[]{:S(2)}, u32[]{:S(2)}) collective-permute-start(bf16[1,32,2688]{2,1,0:T(8,128)(2,1)S(1)} %get-tuple-element.18), channel_id=1, source_target_pairs={{1,0},{0,1},{3,2},{2,3},{5,4},{4,5},{7,6},{6,7},{9,8},{8,9},{11,10... | collective-permute-start | bytes 516104 | tf_op jit(solution)/shard_map/ppermute | solution.py:276
  28.9 0.3 merge.11
  29.1 1.0 %collective-permute-start.16 = (bf16[8,2688]{1,0:T(8,128)(2,1)S(1)}, bf16[8,2688]{1,0:T(8,128)(2,1)S(1)}, u32[]{:S(2)}, u32[]{:S(2)}) collective-permute-start(bf16[8,2688]{1,0:T(8,128)(2,1)S(1)} %get-tuple-element.28), channel_id=1, source_target_pairs={{2,0},{3,1},{0,2},{1,3},{6,4},{7,5},{4,6},{5,7},{10,8},{11,9},{8,1... | collective-permute-start | bytes 129032 | tf_op jit(solution)/shard_map/ppermute | solution.py:276
  30.1 1.1 %collective-permute-start.14 = (bf16[8,2688]{1,0:T(8,128)(2,1)S(1)}, bf16[8,2688]{1,0:T(8,128)(2,1)S(1)}, u32[]{:S(2)}, u32[]{:S(2)}) collective-permute-start(bf16[8,2688]{1,0:T(8,128)(2,1)S(1)} %get-tuple-element.26), channel_id=1, source_target_pairs={{2,0},{3,1},{0,2},{1,3},{6,4},{7,5},{4,6},{5,7},{10,8},{11,9},{8,1... | collective-permute-start | bytes 129032 | tf_op jit(solution)/shard_map/ppermute | solution.py:276
  31.2 0.9 %collective-permute-start.12 = (bf16[8,2688]{1,0:T(8,128)(2,1)S(1)}, bf16[8,2688]{1,0:T(8,128)(2,1)S(1)}, u32[]{:S(2)}, u32[]{:S(2)}) collective-permute-start(bf16[8,2688]{1,0:T(8,128)(2,1)S(1)} %get-tuple-element.24), channel_id=1, source_target_pairs={{2,0},{3,1},{0,2},{1,3},{6,4},{7,5},{4,6},{5,7},{10,8},{11,9},{8,1... | collective-permute-start | bytes 129032 | tf_op jit(solution)/shard_map/ppermute | solution.py:276
  32.1 0.3 merge.9
  32.4 1.2 %collective-permute-start.11 = (bf16[8,2688]{1,0:T(8,128)(2,1)S(1)}, bf16[8,2688]{1,0:T(8,128)(2,1)S(1)}, u32[]{:S(2)}, u32[]{:S(2)}) collective-permute-start(bf16[8,2688]{1,0:T(8,128)(2,1)S(1)} %get-tuple-element.22), channel_id=1, source_target_pairs={{2,0},{3,1},{0,2},{1,3},{6,4},{7,5},{4,6},{5,7},{10,8},{11,9},{8,1... | collective-permute-start | bytes 129032 | tf_op jit(solution)/shard_map/ppermute | solution.py:276
  33.6 0.1 merge.14
  33.8 1.6 %collective-permute-start.17 = (bf16[8,2688]{1,0:T(8,128)(2,1)S(1)}, bf16[8,2688]{1,0:T(8,128)(2,1)S(1)}, u32[]{:S(2)}, u32[]{:S(2)}) collective-permute-start(bf16[8,2688]{1,0:T(8,128)(2,1)S(1)} %merge.14), channel_id=1, source_target_pairs={{4,0},{5,1},{6,2},{7,3},{8,4},{9,5},{10,6},{11,7},{12,8},{13,9},{1... | collective-permute-start | bytes 129032 | tf_op jit(solution)/shard_map/ppermute | solution.py:276
  35.4 0.1 merge.13
  35.6 0.4 collective-permute-start.15
  35.9 0.1 merge.12
  36.1 1.3 %collective-permute-start.13 = (bf16[8,2688]{1,0:T(8,128)(2,1)S(1)}, bf16[8,2688]{1,0:T(8,128)(2,1)S(1)}, u32[]{:S(2)}, u32[]{:S(2)}) collective-permute-start(bf16[8,2688]{1,0:T(8,128)(2,1)S(1)} %merge.12), channel_id=1, source_target_pairs={{12,0},{13,1},{14,2},{15,3},{0,4},{1,5},{2,6},{3,7},{4,8},{5,9},{6... | collective-permute-start | bytes 129032 | tf_op jit(solution)/shard_map/ppermute | solution.py:276
  37.4 0.5 %collective-permute-done.17.refs_4_ = bf16[8,2688]{1,0:T(8,128)(2,1)S(1)} collective-permute-done((bf16[8,2688]{1,0:T(8,128)(2,1)S(1)}, bf16[8,2688]{1,0:T(8,128)(2,1)S(1)}, u32[]{:S(2)}, u32[]{:S(2)}) %collective-permute-start.17) | collective-permute-done | bytes 43040 | tf_op jit(solution)/shard_map/ppermute | solution.py:276
  37.9 3.0 %collective-permute-done.15.refs_3_ = bf16[8,2688]{1,0:T(8,128)(2,1)S(1)} collective-permute-done((bf16[8,2688]{1,0:T(8,128)(2,1)S(1)}, bf16[8,2688]{1,0:T(8,128)(2,1)S(1)}, u32[]{:S(2)}, u32[]{:S(2)}) %collective-permute-start.15) | collective-permute-done | bytes 43040 | tf_op jit(solution)/shard_map/ppermute | solution.py:276
  40.9 1.1 %collective-permute-done.13.refs_2_ = bf16[8,2688]{1,0:T(8,128)(2,1)S(1)} collective-permute-done((bf16[8,2688]{1,0:T(8,128)(2,1)S(1)}, bf16[8,2688]{1,0:T(8,128)(2,1)S(1)}, u32[]{:S(2)}, u32[]{:S(2)}) %collective-permute-start.13) | collective-permute-done | bytes 43040 | tf_op jit(solution)/shard_map/ppermute | solution.py:276
  42.0 0.9 %merge.15 = bf16[8,2560]{1,0:T(8,128)(2,1)} custom-call(f32[8,2688]{1,0:T(8,128)S(1)} %get-tuple-element.19.refs_0_, bf16[8,2688]{1,0:T(8,128)(2,1)S(1)} %collective-permute-done.11.refs_1_, bf16[8,2688]{1,0:T(8,128)(2,1)S(1)} %collective-permute-done.13.refs_2_, bf16[8,2688]{1,0:T(8,128)(2,1)S(1)} %collective-permute-done.15.refs_3_, ...), custom_call_target="tpu_custom_call" | custom-call | flops 430080 | bytes 430080 | tf_op jit(solution)/shard_map/merge/pallas_call | solution.py:251
  (20 shorter events, 0.2 us)
Async XLA Ops:
  0.0 7.6 %collective-permute-start = (bf16[8,2560]{1,0:T(8,128)(2,1)}, bf16[8,2560]{1,0:T(8,128)(2,1)S(1)}, u32[]{:S(2)}, u32[]{:S(2)}) collective-permute-start(bf16[8,2560]{1,0:T(8,128)(2,1)} %refs_0_.1), channel_id=1, source_target_pairs={{4,0},{5,1},{6,2},{7,3},{8,4},{9,5},{10,6},{11,7},{12,8},{13,9},{1... | collective-permute-start | bytes 122888 | tf_op jit(solution)/shard_map/ppermute | solution.py:273
  5.0 5.1 %collective-permute-start.1 = (bf16[8,2560]{1,0:T(8,128)(2,1)}, bf16[8,2560]{1,0:T(8,128)(2,1)S(1)}, u32[]{:S(2)}, u32[]{:S(2)}) collective-permute-start(bf16[8,2560]{1,0:T(8,128)(2,1)} %refs_0_.1), channel_id=1, source_target_pairs={{8,0},{9,1},{10,2},{11,3},{12,4},{13,5},{14,6},{15,7},{0,8},{1,9},... | collective-permute-start | bytes 122888 | tf_op jit(solution)/shard_map/ppermute | solution.py:273
  5.1 6.6 %collective-permute-start.2 = (bf16[8,2560]{1,0:T(8,128)(2,1)}, bf16[8,2560]{1,0:T(8,128)(2,1)S(1)}, u32[]{:S(2)}, u32[]{:S(2)}) collective-permute-start(bf16[8,2560]{1,0:T(8,128)(2,1)} %refs_0_.1), channel_id=1, source_target_pairs={{12,0},{13,1},{14,2},{15,3},{0,4},{1,5},{2,6},{3,7},{4,8},{5,9},{6... | collective-permute-start | bytes 122888 | tf_op jit(solution)/shard_map/ppermute | solution.py:273
  6.1 8.2 %collective-permute-start.5 = (bf16[8,2560]{1,0:T(8,128)(2,1)}, bf16[8,2560]{1,0:T(8,128)(2,1)S(1)}, u32[]{:S(2)}, u32[]{:S(2)}) collective-permute-start(bf16[8,2560]{1,0:T(8,128)(2,1)} %refs_0_.1), channel_id=1, source_target_pairs={{2,0},{3,1},{0,2},{1,3},{6,4},{7,5},{4,6},{5,7},{10,8},{11,9},{8,1... | collective-permute-start | bytes 122888 | tf_op jit(solution)/shard_map/ppermute | solution.py:273
  7.6 6.7 %collective-permute-start.6 = (bf16[8,2560]{1,0:T(8,128)(2,1)S(1)}, bf16[8,2560]{1,0:T(8,128)(2,1)S(1)}, u32[]{:S(2)}, u32[]{:S(2)}) collective-permute-start(bf16[8,2560]{1,0:T(8,128)(2,1)S(1)} %collective-permute-done.refs_1_), channel_id=1, source_target_pairs={{2,0},{3,1},{0,2},{1,3},{6,4},{7,5},{4,6},{5,7},{10,8},{11,9},{8,1... | collective-permute-start | bytes 122888 | tf_op jit(solution)/shard_map/ppermute | solution.py:273
  10.2 4.2 %collective-permute-start.7 = (bf16[8,2560]{1,0:T(8,128)(2,1)S(1)}, bf16[8,2560]{1,0:T(8,128)(2,1)S(1)}, u32[]{:S(2)}, u32[]{:S(2)}) collective-permute-start(bf16[8,2560]{1,0:T(8,128)(2,1)S(1)} %collective-permute-done.1.refs_2_), channel_id=1, source_target_pairs={{2,0},{3,1},{0,2},{1,3},{6,4},{7,5},{4,6},{5,7},{10,8},{11,9},{8,1... | collective-permute-start | bytes 122888 | tf_op jit(solution)/shard_map/ppermute | solution.py:273
  11.7 4.0 %collective-permute-start.8 = (bf16[8,2560]{1,0:T(8,128)(2,1)S(1)}, bf16[8,2560]{1,0:T(8,128)(2,1)S(1)}, u32[]{:S(2)}, u32[]{:S(2)}) collective-permute-start(bf16[8,2560]{1,0:T(8,128)(2,1)S(1)} %collective-permute-done.2.refs_3_), channel_id=1, source_target_pairs={{2,0},{3,1},{0,2},{1,3},{6,4},{7,5},{4,6},{5,7},{10,8},{11,9},{8,1... | collective-permute-start | bytes 122888 | tf_op jit(solution)/shard_map/ppermute | solution.py:273
  13.4 0.8 %copy-start = (bf16[8,2560]{1,0:T(8,128)(2,1)S(1)}, bf16[8,2560]{1,0:T(8,128)(2,1)}, u32[]{:S(2)}) copy-start(bf16[8,2560]{1,0:T(8,128)(2,1)} %refs_0_.1) | copy-start | bytes 122884
  14.2 8.7 %collective-permute-start.3 = (bf16[32,2560]{1,0:T(8,128)(2,1)S(1)}, bf16[32,2560]{1,0:T(8,128)(2,1)S(1)}, u32[]{:S(2)}, u32[]{:S(2)}) collective-permute-start(bf16[32,2560]{1,0:T(8,128)(2,1)S(1)} %merge.8.refs_1_), channel_id=1, source_target_pairs={{1,0},{0,1},{3,2},{2,3},{5,4},{4,5},{7,6},{6,7},{9,8},{8,9},{11,10... | collective-permute-start | bytes 491528 | tf_op jit(solution)/shard_map/ppermute | solution.py:273
  15.7 1.5 %collective-permute-start.9 = (bf16[32,2560]{1,0:T(8,128)(2,1)S(1)}, bf16[32,2560]{1,0:T(8,128)(2,1)S(1)}, u32[]{:S(2)}, u32[]{:S(2)}) collective-permute-start(bf16[32,2560]{1,0:T(8,128)(2,1)S(1)} %merge.10.refs_1_), channel_id=1, source_target_pairs={{1,0},{0,1},{3,2},{2,3},{5,4},{4,5},{7,6},{6,7},{9,8},{8,9},{11,10... | collective-permute-start | bytes 491528 | tf_op jit(solution)/shard_map/ppermute | solution.py:273
  22.7 6.1 %collective-permute-start.10 = (bf16[1,32,2688]{2,1,0:T(8,128)(2,1)S(1)}, bf16[1,32,2688]{2,1,0:T(8,128)(2,1)S(1)}, u32[]{:S(2)}, u32[]{:S(2)}) collective-permute-start(bf16[1,32,2688]{2,1,0:T(8,128)(2,1)S(1)} %get-tuple-element.21), channel_id=1, source_target_pairs={{1,0},{0,1},{3,2},{2,3},{5,4},{4,5},{7,6},{6,7},{9,8},{8,9},{11,10... | collective-permute-start | bytes 516104 | tf_op jit(solution)/shard_map/ppermute | solution.py:276
  28.4 3.7 %collective-permute-start.4 = (bf16[1,32,2688]{2,1,0:T(8,128)(2,1)S(1)}, bf16[1,32,2688]{2,1,0:T(8,128)(2,1)S(1)}, u32[]{:S(2)}, u32[]{:S(2)}) collective-permute-start(bf16[1,32,2688]{2,1,0:T(8,128)(2,1)S(1)} %get-tuple-element.18), channel_id=1, source_target_pairs={{1,0},{0,1},{3,2},{2,3},{5,4},{4,5},{7,6},{6,7},{9,8},{8,9},{11,10... | collective-permute-start | bytes 516104 | tf_op jit(solution)/shard_map/ppermute | solution.py:276
  29.1 4.5 %collective-permute-start.16 = (bf16[8,2688]{1,0:T(8,128)(2,1)S(1)}, bf16[8,2688]{1,0:T(8,128)(2,1)S(1)}, u32[]{:S(2)}, u32[]{:S(2)}) collective-permute-start(bf16[8,2688]{1,0:T(8,128)(2,1)S(1)} %get-tuple-element.28), channel_id=1, source_target_pairs={{2,0},{3,1},{0,2},{1,3},{6,4},{7,5},{4,6},{5,7},{10,8},{11,9},{8,1... | collective-permute-start | bytes 129032 | tf_op jit(solution)/shard_map/ppermute | solution.py:276
  30.1 5.3 %collective-permute-start.14 = (bf16[8,2688]{1,0:T(8,128)(2,1)S(1)}, bf16[8,2688]{1,0:T(8,128)(2,1)S(1)}, u32[]{:S(2)}, u32[]{:S(2)}) collective-permute-start(bf16[8,2688]{1,0:T(8,128)(2,1)S(1)} %get-tuple-element.26), channel_id=1, source_target_pairs={{2,0},{3,1},{0,2},{1,3},{6,4},{7,5},{4,6},{5,7},{10,8},{11,9},{8,1... | collective-permute-start | bytes 129032 | tf_op jit(solution)/shard_map/ppermute | solution.py:276
  31.2 4.7 %collective-permute-start.12 = (bf16[8,2688]{1,0:T(8,128)(2,1)S(1)}, bf16[8,2688]{1,0:T(8,128)(2,1)S(1)}, u32[]{:S(2)}, u32[]{:S(2)}) collective-permute-start(bf16[8,2688]{1,0:T(8,128)(2,1)S(1)} %get-tuple-element.24), channel_id=1, source_target_pairs={{2,0},{3,1},{0,2},{1,3},{6,4},{7,5},{4,6},{5,7},{10,8},{11,9},{8,1... | collective-permute-start | bytes 129032 | tf_op jit(solution)/shard_map/ppermute | solution.py:276
  32.4 4.9 %collective-permute-start.11 = (bf16[8,2688]{1,0:T(8,128)(2,1)S(1)}, bf16[8,2688]{1,0:T(8,128)(2,1)S(1)}, u32[]{:S(2)}, u32[]{:S(2)}) collective-permute-start(bf16[8,2688]{1,0:T(8,128)(2,1)S(1)} %get-tuple-element.22), channel_id=1, source_target_pairs={{2,0},{3,1},{0,2},{1,3},{6,4},{7,5},{4,6},{5,7},{10,8},{11,9},{8,1... | collective-permute-start | bytes 129032 | tf_op jit(solution)/shard_map/ppermute | solution.py:276
  33.8 4.1 %collective-permute-start.17 = (bf16[8,2688]{1,0:T(8,128)(2,1)S(1)}, bf16[8,2688]{1,0:T(8,128)(2,1)S(1)}, u32[]{:S(2)}, u32[]{:S(2)}) collective-permute-start(bf16[8,2688]{1,0:T(8,128)(2,1)S(1)} %merge.14), channel_id=1, source_target_pairs={{4,0},{5,1},{6,2},{7,3},{8,4},{9,5},{10,6},{11,7},{12,8},{13,9},{1... | collective-permute-start | bytes 129032 | tf_op jit(solution)/shard_map/ppermute | solution.py:276
  35.6 5.3 %collective-permute-start.15 = (bf16[8,2688]{1,0:T(8,128)(2,1)S(1)}, bf16[8,2688]{1,0:T(8,128)(2,1)S(1)}, u32[]{:S(2)}, u32[]{:S(2)}) collective-permute-start(bf16[8,2688]{1,0:T(8,128)(2,1)S(1)} %merge.13), channel_id=1, source_target_pairs={{8,0},{9,1},{10,2},{11,3},{12,4},{13,5},{14,6},{15,7},{0,8},{1,9},... | collective-permute-start | bytes 129032 | tf_op jit(solution)/shard_map/ppermute | solution.py:276
  36.1 5.9 %collective-permute-start.13 = (bf16[8,2688]{1,0:T(8,128)(2,1)S(1)}, bf16[8,2688]{1,0:T(8,128)(2,1)S(1)}, u32[]{:S(2)}, u32[]{:S(2)}) collective-permute-start(bf16[8,2688]{1,0:T(8,128)(2,1)S(1)} %merge.12), channel_id=1, source_target_pairs={{12,0},{13,1},{14,2},{15,3},{0,4},{1,5},{2,6},{3,7},{4,8},{5,9},{6... | collective-permute-start | bytes 129032 | tf_op jit(solution)/shard_map/ppermute | solution.py:276

commit v4 on v3

v4 whole, which is shorter than its diff:
```python
import functools
import itertools
import math

import jax
import jax.numpy as jnp
from jax import lax
from jax.experimental import pallas as pl
from jax.experimental.pallas import tpu as pltpu
from jax.sharding import PartitionSpec as P

HD = 128
BLK = 128
STAT = 128
LANE = STAT // 3
NEG = -1e30
F32 = jnp.float32
BF16 = jnp.bfloat16


def factors(members):
    cores = 2 if members % 2 == 0 else 1
    chips = members // cores
    far = next(a for a in range(1, chips + 1) if chips % a == 0 and a * a >= chips)
    return far, chips // far, cores


def shift_perm(shape, by):
    def flat(place):
        return functools.reduce(lambda at, kn: at * kn[1] + kn[0] % kn[1], zip(place, shape), 0)

    places = itertools.product(*map(range, shape))
    return [(flat([p + d for p, d in zip(at, by)]), flat(at)) for at in places]


def lanes(rows):
    return lax.broadcasted_iota(jnp.int32, (rows, STAT), 1)


def pack_stats(top, mass):
    high = mass.astype(BF16).astype(F32)
    return top + pltpu.roll(high, LANE, 1) + pltpu.roll(mass - high, 2 * LANE, 1)


def unpack_stats(packed, heads):
    used = lanes(packed.shape[0]) < heads
    mass = pltpu.roll(packed, STAT - LANE, 1) + pltpu.roll(packed, STAT - 2 * LANE, 1)
    return jnp.where(used, packed, 0.0), jnp.where(used, mass, 0.0)


def attend_kernel(sizes, scale, refs):
    parts, loads, group, pack = sizes
    bias_ref, refs = refs[0], refs[1:]
    q_refs, refs = refs[:parts], refs[parts:]
    sources, refs = refs[:4], refs[4:]
    outs, refs = refs[: len(refs) - 7], refs[len(refs) - 7 :]
    k_buf, v_buf, nk_buf, nv_buf, sems, top_acc, mass_acc = refs
    per = q_refs[0].shape[0]
    rows = per * parts
    wide = pack * HD
    cache_rows = sources[0].shape[0]
    lane = lanes(rows)
    contract_last = (((1,), (1,)), ((), ()))

    def copies(load):
        cols = pl.ds(pl.multiple_of(load * group * wide, HD), group * wide)
        return [
            pltpu.make_async_copy(
                src.at[:, cols], dst.at[pl.ds(0, cache_rows), cols], sems.at[i, load]
            )
            for i, (src, dst) in enumerate(zip(sources[:2], (k_buf, v_buf)))
        ]

    fresh_copies = [
        pltpu.make_async_copy(src, dst, sems.at[2 + i, 0])
        for i, (src, dst) in enumerate(zip(sources[2:], (nk_buf, nv_buf)))
    ]

    @pl.when(pl.program_id(0) == 0)
    def _():
        for copy in copies(0) + fresh_copies:
            copy.start()
        for load in range(1, loads):
            for copy in copies(load):
                copy.start()
        for copy, src, dst in zip(fresh_copies, (nk_buf, nv_buf), (k_buf, v_buf)):
            copy.wait()
            rest = dst.shape[0] - cache_rows - src.shape[0]
            tail = jnp.concatenate(
                [src[...].astype(F32), jnp.zeros((rest, src.shape[1]), F32)], axis=0
            )
            dst[cache_rows:, :] = tail.astype(BF16)

    top_acc[...] = jnp.zeros_like(top_acc)
    mass_acc[...] = jnp.zeros_like(mass_acc)
    bias = bias_ref[...]
    mine = [
        lax.broadcasted_iota(jnp.int32, (rows, wide), 1) // HD == k for k in range(pack)
    ]

    def heads_of(load, carry):
        @pl.when(pl.program_id(0) == 0)
        def _():
            for copy in copies(load):
                copy.wait()

        def columns(i):
            return pl.ds(pl.multiple_of((load * group + i) * wide, HD), wide)

        def scores(i):
            cols = columns(i)
            q = jnp.concatenate([r[:, cols] for r in q_refs], axis=0)
            if pack > 1:
                zero = jnp.zeros_like(q)
                q = jnp.concatenate([jnp.where(m, q, zero) for m in mine], axis=0)
            return lax.dot_general(q, k_buf[:, cols], contract_last, preferred_element_type=F32)

        tops = top_acc[...]
        masses = mass_acc[...]
        ahead = scores(0)
        for i in range(group):
            score = ahead
            if i + 1 < group:
                ahead = scores(i + 1)
            score = score * scale + bias
            top = jnp.max(score, axis=1, keepdims=True).astype(BF16).astype(F32)
            score = jnp.exp2(score - top)
            mass = jnp.sum(score, axis=1, keepdims=True)
            out = jnp.dot(score.astype(BF16), v_buf[:, columns(i)], preferred_element_type=F32)
            for k in range(pack):
                head = (load * group + i) * pack + k
                cols = pl.ds(pl.multiple_of(head * HD, HD), HD)
                one = out[k * rows : (k + 1) * rows, k * HD : (k + 1) * HD]
                for p in range(parts):
                    o_ref = outs[p]
                    o_ref[:, cols] = one[p * per : (p + 1) * per].astype(o_ref.dtype)
                tops = jnp.where(lane == head, top[k * rows : (k + 1) * rows], tops)
                masses = jnp.where(lane == head, mass[k * rows : (k + 1) * rows], masses)
        top_acc[...] = tops
        mass_acc[...] = masses
        return carry

    lax.fori_loop(0, loads, heads_of, 0)
    packed = pack_stats(top_acc[...], mass_acc[...])
    for p, o_ref in enumerate(outs):
        width = o_ref.shape[1]
        o_ref[:, width - STAT :] = packed[p * per : (p + 1) * per].astype(o_ref.dtype)


def attend(parts, keys, values, new_keys, new_values, bias):
    n = len(parts)
    rows, columns = parts[0].shape
    heads = columns // HD
    pack = 2 if heads % 2 == 0 else 1
    group = next(g for g in (2, 1) if heads % (g * pack) == 0)
    loads = heads // (group * pack)
    tile = next(t for t in (64, 32, 16, rows) if rows % t == 0)
    cache_rows = keys.shape[0]
    padded = cache_rows + -(-new_keys.shape[0] // BLK) * BLK
    width = columns + STAT
    scale = math.log2(math.e) / math.sqrt(HD)
    held = (keys, values, new_keys, new_values)

    def body(*refs):
        attend_kernel((n, loads, group, pack), scale, refs)

    return pl.pallas_call(
        body,
        grid=(rows // tile,),
        in_specs=[pl.BlockSpec((1, padded), lambda r: (0, 0))]
        + [pl.BlockSpec((tile, columns), lambda r: (r, 0))] * n
        + [pl.BlockSpec(memory_space=pltpu.HBM)] * 4,
        out_specs=[pl.BlockSpec((tile, width), lambda r: (r, 0))] * n,
        out_shape=[jax.ShapeDtypeStruct((rows, width), F32 if c == 0 else BF16) for c in range(n)],
        scratch_shapes=[pltpu.VMEM((padded, columns), BF16)] * 2
        + [pltpu.VMEM(new_keys.shape, BF16)] * 2
        + [pltpu.SemaphoreType.DMA((4, loads))]
        + [pltpu.VMEM((tile * n, STAT), F32)] * 2,
        compiler_params=pltpu.CompilerParams(
            dimension_semantics=("arbitrary",), vmem_limit_bytes=40 * 1024 * 1024
        ),
        cost_estimate=pl.CostEstimate(
            flops=4 * n * rows * cache_rows * columns,
            bytes_accessed=4 * cache_rows * columns,
            transcendentals=n * rows * cache_rows * heads,
        ),
        name="attend",
    )(bias, *parts, *[pltpu.with_memory_space_constraint(x, pltpu.HBM) for x in held])


def merged(arrays, heads, last):
    columns = heads * HD
    stats = [unpack_stats(get(slice(columns, columns + STAT)), heads) for get in arrays]
    top = functools.reduce(jnp.maximum, [t for t, _ in stats])
    weights = [jnp.exp2(t - top) for t, _ in stats]
    mass = functools.reduce(jnp.add, [w * m for w, (_, m) in zip(weights, stats)])
    if last:
        inverse = 1.0 / jnp.where(lanes(mass.shape[0]) < heads, mass, 1.0)
        weights = [w * inverse for w in weights]
    for head in range(heads):
        cols = slice(head * HD, (head + 1) * HD)
        yield cols, functools.reduce(
            jnp.add, [get(cols) * w[:, head : head + 1] for get, w in zip(arrays, weights)]
        )
    if not last:
        yield slice(columns, columns + STAT), pack_stats(top, mass)


def getter(ref, *index):
    return lambda cols: ref[(*index, slice(None), cols)].astype(F32)


def merge_rows(ins, heads, pieces, kinds):
    rows, width = ins[0].shape
    per = rows // pieces

    def body(*refs):
        outs = refs[len(ins) :]
        for cols, total in merged([getter(r) for r in refs[: len(ins)]], heads, False):
            for j, out in enumerate(outs):
                out[:, cols] = total[j * per : (j + 1) * per].astype(out.dtype)

    return call_merge(body, ins, [jax.ShapeDtypeStruct((per, width), kind) for kind in kinds])


def finish(ins, heads):
    rows = ins[0].shape[0]

    def body(*refs):
        out = refs[len(ins)]
        for cols, total in merged([getter(r) for r in refs[: len(ins)]], heads, True):
            out[:, cols] = total.astype(out.dtype)

    return call_merge(body, ins, [jax.ShapeDtypeStruct((rows, heads * HD), BF16)])[0]


def join(pieces):
    rows = sum(p.shape[0] for p in pieces)

    def body(*refs):
        out = refs[-1]
        out[...] = jnp.concatenate([r[...].astype(F32) for r in refs[:-1]], axis=0).astype(out.dtype)

    shape = jax.ShapeDtypeStruct((rows, pieces[0].shape[1]), pieces[0].dtype)
    return call_merge(body, pieces, [shape])[0]


def call_merge(body, ins, shapes):
    size = sum(math.prod(x.shape) for x in ins)
    return pl.pallas_call(
        body,
        in_specs=[pl.BlockSpec(memory_space=pltpu.VMEM)] * len(ins),
        out_specs=[pl.BlockSpec(memory_space=pltpu.VMEM)] * len(shapes),
        out_shape=shapes,
        compiler_params=pltpu.CompilerParams(vmem_limit_bytes=48 * 1024 * 1024),
        cost_estimate=pl.CostEstimate(flops=4 * size, bytes_accessed=4 * size, transcendentals=0),
        name="merge",
    )(*ins)


def per_device(queries, new_keys, new_values, cache_keys, cache_values, victims):
    members = lax.axis_size("seq")
    shape = factors(members)
    a_n, b_n, c_n = shape
    heads = queries.shape[1] // HD
    block_count = cache_keys.shape[0] // BLK
    block_ids = lax.axis_index("seq") * block_count + jnp.arange(block_count, dtype=jnp.int32)
    evicted = jnp.any(victims[:, None] == block_ids[None, :], axis=0)
    bias = jnp.repeat(jnp.where(evicted, NEG, 0.0), BLK)[None, :]
    tok = new_keys.shape[0]
    fresh_bias = jnp.where(jnp.arange(-(-tok // BLK) * BLK) < tok, 0.0, NEG)[None, :]
    bias = jnp.concatenate([bias, fresh_bias], axis=1)

    def fetch(x, by):
        return lax.ppermute(x, "seq", shift_perm(shape, by))

    def give(x, by):
        return lax.ppermute(x, "seq", shift_perm(shape, [-d for d in by]))

    chips = [(a, b, 0) for a in range(a_n) for b in range(b_n)]
    far_first = sorted(chips[1:], key=lambda at: (-min(at[0], a_n - at[0]), -at[1]))

    blocks = {at: fetch(queries, at) for at in far_first}
    blocks[chips[0]] = join([queries])
    plane = join([blocks[at] for at in chips])
    parts = [plane] + [fetch(plane, (0, 0, c)) for c in range(1, c_n)]
    parts = attend(parts, cache_keys, cache_values, new_keys, new_values, bias)
    parts = [parts[0]] + [give(x, (0, 0, c + 1)) for c, x in enumerate(parts[1:])]
    kinds = [F32] + [BF16] * (len(chips) - 1)
    pieces = dict(zip(chips, merge_rows(parts, heads, len(chips), kinds)))
    for at in far_first:
        pieces[at] = give(pieces[at], at)
    return finish([pieces[at] for at in chips], heads)


def solution(mesh):
    rows = P(("groups", "seq"), None)
    return jax.shard_map(
        per_device,
        mesh=mesh,
        in_specs=(rows, rows, rows, rows, rows, P("groups")),
        out_specs=rows,
        check_vma=False,
    )
```

time: 43.1 us -> 44.3 us (1.028)
  Pallas kernels: 12.9 us -> 7.24 us
  starting transfers between devices: 19.2 us -> 24 us
  waiting for transfers between devices: 8.95 us -> 11.1 us
    pallas_call x2 -> x1, Pallas kernels: 11 us -> 5.75 us  [attend(): pl.pallas_call(body, grid=(rows // tile,), in_specs=[pl.BlockSpec((1, pad...]
    ppermute x18 -> x16, starting transfers between devices: 19.2 us -> 24 us  [the longest x8 12.6 us: fetch(): return lax.ppermute(x, 'seq', shift_perm(shape, by))]
    ppermute x18 -> x16, waiting for transfers between devices: 8.95 us -> 11.1 us  [the longest x8 6.58 us: fetch(): return lax.ppermute(x, 'seq', shift_perm(shape, by))]
    pallas_call x8 -> x4, Pallas kernels: 1.95 us -> 1.49 us  [call_merge(): pl.pallas_call(body, in_specs=[pl.BlockSpec(memory_space=pltpu.VMEM)] * l...]
  transfers between devices with their start and end apart: 18 -> 16, of which waited for: 6 -> 6; matrix products, arithmetic and copies ran while one was open for 2% -> 2% of each run, Pallas kernels for 28% -> 0%
where the time goes in v4:
time: 44.3 us; the launch traced here: 44.1 us
  starting transfers between devices  24 us (54%)
  waiting for transfers between devices  11.1 us (25%)
  Pallas kernels  7.24 us (16%)
  local copies, waits for them, and re-layouts  0.88 us (2%)
  other arithmetic  0.86 us (2%)
    ppermute x8, starting transfers between devices, fetch(): return lax.ppermute(x, 'seq', shift_perm(shape, by))  12.6 us
    ppermute x8, starting transfers between devices, give(): return lax.ppermute(x, 'seq', shift_perm(shape, [-d for d in by]))  11.4 us
    ppermute x8, waiting for transfers between devices, fetch(): return lax.ppermute(x, 'seq', shift_perm(shape, by))  6.58 us
    pallas_call x1, Pallas kernels, attend(): pl.pallas_call(body, grid=(rows // tile,), in_specs=[pl.BlockSpec((1, pad...  5.75 us
    ppermute x8, waiting for transfers between devices, give(): return lax.ppermute(x, 'seq', shift_perm(shape, [-d for d in by]))  4.47 us
    pallas_call x4, Pallas kernels, call_merge(): pl.pallas_call(body, in_specs=[pl.BlockSpec(memory_space=pltpu.VMEM)] * l...  1.49 us
  transfers between devices with their start and end apart: 16, of which 6 were waited for; matrix products, arithmetic and copies ran while one was open for 2% of the time, Pallas kernels for 0%

profile of v4, /device:TPU:0, one launch (start us, length us, event | category | flops | bytes accessed | tf_op | source)
XLA Modules:
  0.0 44.1 jit_solution(6296011829364736564)
XLA Ops:
  0.0 5.0 %collective-permute-start.4 = (bf16[8,2560]{1,0:T(8,128)(2,1)}, bf16[8,2560]{1,0:T(8,128)(2,1)S(1)}, u32[]{:S(2)}, u32[]{:S(2)}) collective-permute-start(bf16[8,2560]{1,0:T(8,128)(2,1)} %refs_0_.1), channel_id=1, source_target_pairs={{10,0},{11,1},{8,2},{9,3},{14,4},{15,5},{12,6},{13,7},{2,8},{3,9},... | collective-permute-start | bytes 122888 | tf_op jit(solution)/shard_map/ppermute | solution.py:275
  5.0 0.3 collective-permute-start.3
  5.3 3.5 %collective-permute-start.2 = (bf16[8,2560]{1,0:T(8,128)(2,1)}, bf16[8,2560]{1,0:T(8,128)(2,1)S(1)}, u32[]{:S(2)}, u32[]{:S(2)}) collective-permute-start(bf16[8,2560]{1,0:T(8,128)(2,1)} %refs_0_.1), channel_id=1, source_target_pairs={{6,0},{7,1},{4,2},{5,3},{10,4},{11,5},{8,6},{9,7},{14,8},{15,9},{1... | collective-permute-start | bytes 122888 | tf_op jit(solution)/shard_map/ppermute | solution.py:275
  8.9 0.4 %collective-permute-start.1 = (bf16[8,2560]{1,0:T(8,128)(2,1)}, bf16[8,2560]{1,0:T(8,128)(2,1)S(1)}, u32[]{:S(2)}, u32[]{:S(2)}) collective-permute-start(bf16[8,2560]{1,0:T(8,128)(2,1)} %refs_0_.1), channel_id=1, source_target_pairs={{4,0},{5,1},{6,2},{7,3},{8,4},{9,5},{10,6},{11,7},{12,8},{13,9},{1... | collective-permute-start | bytes 122888 | tf_op jit(solution)/shard_map/ppermute | solution.py:275
  9.3 1.5 %collective-permute-start = (bf16[8,2560]{1,0:T(8,128)(2,1)}, bf16[8,2560]{1,0:T(8,128)(2,1)S(1)}, u32[]{:S(2)}, u32[]{:S(2)}) collective-permute-start(bf16[8,2560]{1,0:T(8,128)(2,1)} %refs_0_.1), channel_id=1, source_target_pairs={{2,0},{3,1},{0,2},{1,3},{6,4},{7,5},{4,6},{5,7},{10,8},{11,9},{8,1... | collective-permute-start | bytes 122888 | tf_op jit(solution)/shard_map/ppermute | solution.py:275
  10.8 0.8 %compare_reduce_fusion = pred[4]{0:T(512)(128)(4,1)S(1)} fusion(s32[16]{0:T(128)} %param.11, s32[4]{0:T(128)S(1)} %iota_add_fusion), kind=kLoop, calls=%fused_computation.2 | loop fusion | flops 124 | bytes 84 | tf_op jit(solution)/shard_map/reduce_or | solution.py:268
  11.7 0.0 collective-permute-done.4.refs_5_
  11.7 1.6 %collective-permute-start.6 = (bf16[8,2560]{1,0:T(8,128)(2,1)}, bf16[8,2560]{1,0:T(8,128)(2,1)S(1)}, u32[]{:S(2)}, u32[]{:S(2)}) collective-permute-start(bf16[8,2560]{1,0:T(8,128)(2,1)} %refs_0_.1), channel_id=1, source_target_pairs={{14,0},{15,1},{12,2},{13,3},{2,4},{3,5},{0,6},{1,7},{6,8},{7,9},{4... | collective-permute-start | bytes 122888 | tf_op jit(solution)/shard_map/ppermute | solution.py:275
  13.3 0.0 collective-permute-done.3.refs_4_
  13.3 0.1 collective-permute-start.5
  13.4 0.8 %copy-done = bf16[8,2560]{1,0:T(8,128)(2,1)S(1)} copy-done((bf16[8,2560]{1,0:T(8,128)(2,1)S(1)}, bf16[8,2560]{1,0:T(8,128)(2,1)}, u32[]{:S(2)}) %copy-start) | copy-done | bytes 40984
  14.2 0.0 collective-permute-done.2.refs_3_
  14.2 0.0 collective-permute-done.1.refs_2_
  14.2 0.0 collective-permute-done.refs_1_
  14.2 4.4 %collective-permute-done.6.refs_7_ = bf16[8,2560]{1,0:T(8,128)(2,1)S(1)} collective-permute-done((bf16[8,2560]{1,0:T(8,128)(2,1)}, bf16[8,2560]{1,0:T(8,128)(2,1)S(1)}, u32[]{:S(2)}, u32[]{:S(2)}) %collective-permute-start.6) | collective-permute-done | bytes 40992 | tf_op jit(solution)/shard_map/ppermute | solution.py:275
  18.7 0.6 %collective-permute-done.5.refs_6_ = bf16[8,2560]{1,0:T(8,128)(2,1)S(1)} collective-permute-done((bf16[8,2560]{1,0:T(8,128)(2,1)}, bf16[8,2560]{1,0:T(8,128)(2,1)S(1)}, u32[]{:S(2)}, u32[]{:S(2)}) %collective-permute-start.5) | collective-permute-done | bytes 40992 | tf_op jit(solution)/shard_map/ppermute | solution.py:275
  19.3 0.1 collective-permute-start.7
  19.4 0.1 broadcast_in_dim.24
  19.5 1.5 %collective-permute-done.7.refs_2_ = bf16[64,2560]{1,0:T(8,128)(2,1)S(1)} collective-permute-done((bf16[64,2560]{1,0:T(8,128)(2,1)S(1)}, bf16[64,2560]{1,0:T(8,128)(2,1)S(1)}, u32[]{:S(2)}, u32[]{:S(2)}) %collective-permute-start.7) | collective-permute-done | bytes 327712 | tf_op jit(solution)/shard_map/ppermute | solution.py:275
  21.0 5.8 %attend.1 = (f32[64,2688]{1,0:T(8,128)S(1)}, bf16[64,2688]{1,0:T(8,128)(2,1)S(1)}) custom-call(f32[1,640]{1,0:T(1,128)S(1)} %pad_maximum_fusion.refs_0_, bf16[64,2560]{1,0:T(8,128)(2,1)S(1)} %merge.5.refs_1_, bf16[64,2560]{1,0:T(8,128)(2,1)S(1)} %collective-permute-done.7.refs_2_, bf16[512,2560]{1,0:T(8,128)(2,1)} %refs_3_.1, bf16[512,2560]{1,0:T(8,128)(2,1)} %refs_4_.1, ...), custom_call_target="tpu_custom_call" | custom-call | flops 671088640 | bytes 5242880 | tf_op jit(solution)/shard_map/attend/pallas_call | solution.py:167
  26.8 0.2 collective-permute-start.8
  27.0 1.5 %collective-permute-done.8.refs_1_ = bf16[64,2688]{1,0:T(8,128)(2,1)S(1)} collective-permute-done((bf16[64,2688]{1,0:T(8,128)(2,1)S(1)}, bf16[64,2688]{1,0:T(8,128)(2,1)S(1)}, u32[]{:S(2)}, u32[]{:S(2)}) %collective-permute-start.8) | collective-permute-done | bytes 344096 | tf_op jit(solution)/shard_map/ppermute | solution.py:278
  28.5 0.5 %merge.6 = (f32[8,2688]{1,0:T(8,128)S(1)}, bf16[8,2688]{1,0:T(8,128)(2,1)S(1)}, bf16[8,2688]{1,0:T(8,128)(2,1)S(1)}, bf16[8,2688]{1,0:T(8,128)(2,1)S(1)}, bf16[8...) custom-call(f32[64,2688]{1,0:T(8,128)S(1)} %get-tuple-element.15.ref, ...), custom_call_target="tpu_custom_call" | custom-call | flops 1376256 | bytes 1376256 | tf_op jit(solution)/shard_map/merge/pallas_call | solution.py:250
  29.0 1.6 %collective-permute-start.9 = (bf16[8,2688]{1,0:T(8,128)(2,1)S(1)}, bf16[8,2688]{1,0:T(8,128)(2,1)S(1)}, u32[]{:S(2)}, u32[]{:S(2)}) collective-permute-start(bf16[8,2688]{1,0:T(8,128)(2,1)S(1)} %get-tuple-element.18), channel_id=1, source_target_pairs={{2,0},{3,1},{0,2},{1,3},{6,4},{7,5},{4,6},{5,7},{10,8},{11,9},{8,1... | collective-permute-start | bytes 129032 | tf_op jit(solution)/shard_map/ppermute | solution.py:278
  30.5 0.0 collective-permute-start.10
  30.5 4.3 %collective-permute-start.12 = (bf16[8,2688]{1,0:T(8,128)(2,1)S(1)}, bf16[8,2688]{1,0:T(8,128)(2,1)S(1)}, u32[]{:S(2)}, u32[]{:S(2)}) collective-permute-start(bf16[8,2688]{1,0:T(8,128)(2,1)S(1)} %get-tuple-element.21), channel_id=1, source_target_pairs={{8,0},{9,1},{10,2},{11,3},{12,4},{13,5},{14,6},{15,7},{0,8},{1,9},... | collective-permute-start | bytes 129032 | tf_op jit(solution)/shard_map/ppermute | solution.py:278
  34.9 1.0 %collective-permute-start.13 = (bf16[8,2688]{1,0:T(8,128)(2,1)S(1)}, bf16[8,2688]{1,0:T(8,128)(2,1)S(1)}, u32[]{:S(2)}, u32[]{:S(2)}) collective-permute-start(bf16[8,2688]{1,0:T(8,128)(2,1)S(1)} %get-tuple-element.22), channel_id=1, source_target_pairs={{10,0},{11,1},{8,2},{9,3},{14,4},{15,5},{12,6},{13,7},{2,8},{3,9},... | collective-permute-start | bytes 129032 | tf_op jit(solution)/shard_map/ppermute | solution.py:278
  35.8 2.4 %collective-permute-start.14 = (bf16[8,2688]{1,0:T(8,128)(2,1)S(1)}, bf16[8,2688]{1,0:T(8,128)(2,1)S(1)}, u32[]{:S(2)}, u32[]{:S(2)}) collective-permute-start(bf16[8,2688]{1,0:T(8,128)(2,1)S(1)} %get-tuple-element.23), channel_id=1, source_target_pairs={{4,0},{5,1},{6,2},{7,3},{8,4},{9,5},{10,6},{11,7},{12,8},{13,9},{1... | collective-permute-start | bytes 129032 | tf_op jit(solution)/shard_map/ppermute | solution.py:278
  38.2 2.0 %collective-permute-start.15 = (bf16[8,2688]{1,0:T(8,128)(2,1)S(1)}, bf16[8,2688]{1,0:T(8,128)(2,1)S(1)}, u32[]{:S(2)}, u32[]{:S(2)}) collective-permute-start(bf16[8,2688]{1,0:T(8,128)(2,1)S(1)} %get-tuple-element.24), channel_id=1, source_target_pairs={{6,0},{7,1},{4,2},{5,3},{10,4},{11,5},{8,6},{9,7},{14,8},{15,9},{1... | collective-permute-start | bytes 129032 | tf_op jit(solution)/shard_map/ppermute | solution.py:278
  40.2 1.3 %collective-permute-done.13.refs_5_ = bf16[8,2688]{1,0:T(8,128)(2,1)S(1)} collective-permute-done((bf16[8,2688]{1,0:T(8,128)(2,1)S(1)}, bf16[8,2688]{1,0:T(8,128)(2,1)S(1)}, u32[]{:S(2)}, u32[]{:S(2)}) %collective-permute-start.13) | collective-permute-done | bytes 43040 | tf_op jit(solution)/shard_map/ppermute | solution.py:278
  41.5 1.6 %collective-permute-done.15.refs_7_ = bf16[8,2688]{1,0:T(8,128)(2,1)S(1)} collective-permute-done((bf16[8,2688]{1,0:T(8,128)(2,1)S(1)}, bf16[8,2688]{1,0:T(8,128)(2,1)S(1)}, u32[]{:S(2)}, u32[]{:S(2)}) %collective-permute-start.15) | collective-permute-done | bytes 43040 | tf_op jit(solution)/shard_map/ppermute | solution.py:278
  43.1 1.0 %merge.7 = bf16[8,2560]{1,0:T(8,128)(2,1)} custom-call(f32[8,2688]{1,0:T(8,128)S(1)} %get-tuple-element.17.refs_0_, bf16[8,2688]{1,0:T(8,128)(2,1)S(1)} %collective-permute-done.9.refs_1_, bf16[8,2688]{1,0:T(8,128)(2,1)S(1)} %collective-permute-done.10.refs_2_, bf16[8,2688]{1,0:T(8,128)(2,1)S(1)} %collective-permute-done.11.refs_3_, ...), custom_call_target="tpu_custom_call" | custom-call | flops 688128 | bytes 688128 | tf_op jit(solution)/shard_map/merge/pallas_call | solution.py:250
  (13 shorter events, 0.1 us)
Async XLA Ops:
  0.0 11.7 %collective-permute-start.4 = (bf16[8,2560]{1,0:T(8,128)(2,1)}, bf16[8,2560]{1,0:T(8,128)(2,1)S(1)}, u32[]{:S(2)}, u32[]{:S(2)}) collective-permute-start(bf16[8,2560]{1,0:T(8,128)(2,1)} %refs_0_.1), channel_id=1, source_target_pairs={{10,0},{11,1},{8,2},{9,3},{14,4},{15,5},{12,6},{13,7},{2,8},{3,9},... | collective-permute-start | bytes 122888 | tf_op jit(solution)/shard_map/ppermute | solution.py:275
  5.0 8.3 %collective-permute-start.3 = (bf16[8,2560]{1,0:T(8,128)(2,1)}, bf16[8,2560]{1,0:T(8,128)(2,1)S(1)}, u32[]{:S(2)}, u32[]{:S(2)}) collective-permute-start(bf16[8,2560]{1,0:T(8,128)(2,1)} %refs_0_.1), channel_id=1, source_target_pairs={{8,0},{9,1},{10,2},{11,3},{12,4},{13,5},{14,6},{15,7},{0,8},{1,9},... | collective-permute-start | bytes 122888 | tf_op jit(solution)/shard_map/ppermute | solution.py:275
  5.3 8.9 %collective-permute-start.2 = (bf16[8,2560]{1,0:T(8,128)(2,1)}, bf16[8,2560]{1,0:T(8,128)(2,1)S(1)}, u32[]{:S(2)}, u32[]{:S(2)}) collective-permute-start(bf16[8,2560]{1,0:T(8,128)(2,1)} %refs_0_.1), channel_id=1, source_target_pairs={{6,0},{7,1},{4,2},{5,3},{10,4},{11,5},{8,6},{9,7},{14,8},{15,9},{1... | collective-permute-start | bytes 122888 | tf_op jit(solution)/shard_map/ppermute | solution.py:275
  8.9 5.3 %collective-permute-start.1 = (bf16[8,2560]{1,0:T(8,128)(2,1)}, bf16[8,2560]{1,0:T(8,128)(2,1)S(1)}, u32[]{:S(2)}, u32[]{:S(2)}) collective-permute-start(bf16[8,2560]{1,0:T(8,128)(2,1)} %refs_0_.1), channel_id=1, source_target_pairs={{4,0},{5,1},{6,2},{7,3},{8,4},{9,5},{10,6},{11,7},{12,8},{13,9},{1... | collective-permute-start | bytes 122888 | tf_op jit(solution)/shard_map/ppermute | solution.py:275
  9.3 4.9 %collective-permute-start = (bf16[8,2560]{1,0:T(8,128)(2,1)}, bf16[8,2560]{1,0:T(8,128)(2,1)S(1)}, u32[]{:S(2)}, u32[]{:S(2)}) collective-permute-start(bf16[8,2560]{1,0:T(8,128)(2,1)} %refs_0_.1), channel_id=1, source_target_pairs={{2,0},{3,1},{0,2},{1,3},{6,4},{7,5},{4,6},{5,7},{10,8},{11,9},{8,1... | collective-permute-start | bytes 122888 | tf_op jit(solution)/shard_map/ppermute | solution.py:275
  11.7 7.0 %collective-permute-start.6 = (bf16[8,2560]{1,0:T(8,128)(2,1)}, bf16[8,2560]{1,0:T(8,128)(2,1)S(1)}, u32[]{:S(2)}, u32[]{:S(2)}) collective-permute-start(bf16[8,2560]{1,0:T(8,128)(2,1)} %refs_0_.1), channel_id=1, source_target_pairs={{14,0},{15,1},{12,2},{13,3},{2,4},{3,5},{0,6},{1,7},{6,8},{7,9},{4... | collective-permute-start | bytes 122888 | tf_op jit(solution)/shard_map/ppermute | solution.py:275
  13.3 6.0 %collective-permute-start.5 = (bf16[8,2560]{1,0:T(8,128)(2,1)}, bf16[8,2560]{1,0:T(8,128)(2,1)S(1)}, u32[]{:S(2)}, u32[]{:S(2)}) collective-permute-start(bf16[8,2560]{1,0:T(8,128)(2,1)} %refs_0_.1), channel_id=1, source_target_pairs={{12,0},{13,1},{14,2},{15,3},{0,4},{1,5},{2,6},{3,7},{4,8},{5,9},{6... | collective-permute-start | bytes 122888 | tf_op jit(solution)/shard_map/ppermute | solution.py:275
  13.4 0.8 %copy-start = (bf16[8,2560]{1,0:T(8,128)(2,1)S(1)}, bf16[8,2560]{1,0:T(8,128)(2,1)}, u32[]{:S(2)}) copy-start(bf16[8,2560]{1,0:T(8,128)(2,1)} %refs_0_.1) | copy-start | bytes 122884
  19.3 1.7 %collective-permute-start.7 = (bf16[64,2560]{1,0:T(8,128)(2,1)S(1)}, bf16[64,2560]{1,0:T(8,128)(2,1)S(1)}, u32[]{:S(2)}, u32[]{:S(2)}) collective-permute-start(bf16[64,2560]{1,0:T(8,128)(2,1)S(1)} %merge.5.refs_1_), channel_id=1, source_target_pairs={{1,0},{0,1},{3,2},{2,3},{5,4},{4,5},{7,6},{6,7},{9,8},{8,9},{11,10... | collective-permute-start | bytes 983048 | tf_op jit(solution)/shard_map/ppermute | solution.py:275
  26.8 1.7 %collective-permute-start.8 = (bf16[64,2688]{1,0:T(8,128)(2,1)S(1)}, bf16[64,2688]{1,0:T(8,128)(2,1)S(1)}, u32[]{:S(2)}, u32[]{:S(2)}) collective-permute-start(bf16[64,2688]{1,0:T(8,128)(2,1)S(1)} %get-tuple-element.16), channel_id=1, source_target_pairs={{1,0},{0,1},{3,2},{2,3},{5,4},{4,5},{7,6},{6,7},{9,8},{8,9},{11,10... | collective-permute-start | bytes 1032200 | tf_op jit(solution)/shard_map/ppermute | solution.py:278
  29.0 6.9 %collective-permute-start.9 = (bf16[8,2688]{1,0:T(8,128)(2,1)S(1)}, bf16[8,2688]{1,0:T(8,128)(2,1)S(1)}, u32[]{:S(2)}, u32[]{:S(2)}) collective-permute-start(bf16[8,2688]{1,0:T(8,128)(2,1)S(1)} %get-tuple-element.18), channel_id=1, source_target_pairs={{2,0},{3,1},{0,2},{1,3},{6,4},{7,5},{4,6},{5,7},{10,8},{11,9},{8,1... | collective-permute-start | bytes 129032 | tf_op jit(solution)/shard_map/ppermute | solution.py:278
  30.5 7.7 %collective-permute-start.10 = (bf16[8,2688]{1,0:T(8,128)(2,1)S(1)}, bf16[8,2688]{1,0:T(8,128)(2,1)S(1)}, u32[]{:S(2)}, u32[]{:S(2)}) collective-permute-start(bf16[8,2688]{1,0:T(8,128)(2,1)S(1)} %get-tuple-element.19), channel_id=1, source_target_pairs={{12,0},{13,1},{14,2},{15,3},{0,4},{1,5},{2,6},{3,7},{4,8},{5,9},{6... | collective-permute-start | bytes 129032 | tf_op jit(solution)/shard_map/ppermute | solution.py:278
  30.5 9.6 %collective-permute-start.11 = (bf16[8,2688]{1,0:T(8,128)(2,1)S(1)}, bf16[8,2688]{1,0:T(8,128)(2,1)S(1)}, u32[]{:S(2)}, u32[]{:S(2)}) collective-permute-start(bf16[8,2688]{1,0:T(8,128)(2,1)S(1)} %get-tuple-element.20), channel_id=1, source_target_pairs={{14,0},{15,1},{12,2},{13,3},{2,4},{3,5},{0,6},{1,7},{6,8},{7,9},{4... | collective-permute-start | bytes 129032 | tf_op jit(solution)/shard_map/ppermute | solution.py:278
  30.5 9.6 %collective-permute-start.12 = (bf16[8,2688]{1,0:T(8,128)(2,1)S(1)}, bf16[8,2688]{1,0:T(8,128)(2,1)S(1)}, u32[]{:S(2)}, u32[]{:S(2)}) collective-permute-start(bf16[8,2688]{1,0:T(8,128)(2,1)S(1)} %get-tuple-element.21), channel_id=1, source_target_pairs={{8,0},{9,1},{10,2},{11,3},{12,4},{13,5},{14,6},{15,7},{0,8},{1,9},... | collective-permute-start | bytes 129032 | tf_op jit(solution)/shard_map/ppermute | solution.py:278
  34.9 6.6 %collective-permute-start.13 = (bf16[8,2688]{1,0:T(8,128)(2,1)S(1)}, bf16[8,2688]{1,0:T(8,128)(2,1)S(1)}, u32[]{:S(2)}, u32[]{:S(2)}) collective-permute-start(bf16[8,2688]{1,0:T(8,128)(2,1)S(1)} %get-tuple-element.22), channel_id=1, source_target_pairs={{10,0},{11,1},{8,2},{9,3},{14,4},{15,5},{12,6},{13,7},{2,8},{3,9},... | collective-permute-start | bytes 129032 | tf_op jit(solution)/shard_map/ppermute | solution.py:278
  35.8 5.6 %collective-permute-start.14 = (bf16[8,2688]{1,0:T(8,128)(2,1)S(1)}, bf16[8,2688]{1,0:T(8,128)(2,1)S(1)}, u32[]{:S(2)}, u32[]{:S(2)}) collective-permute-start(bf16[8,2688]{1,0:T(8,128)(2,1)S(1)} %get-tuple-element.23), channel_id=1, source_target_pairs={{4,0},{5,1},{6,2},{7,3},{8,4},{9,5},{10,6},{11,7},{12,8},{13,9},{1... | collective-permute-start | bytes 129032 | tf_op jit(solution)/shard_map/ppermute | solution.py:278
  38.2 4.9 %collective-permute-start.15 = (bf16[8,2688]{1,0:T(8,128)(2,1)S(1)}, bf16[8,2688]{1,0:T(8,128)(2,1)S(1)}, u32[]{:S(2)}, u32[]{:S(2)}) collective-permute-start(bf16[8,2688]{1,0:T(8,128)(2,1)S(1)} %get-tuple-element.24), channel_id=1, source_target_pairs={{6,0},{7,1},{4,2},{5,3},{10,4},{11,5},{8,6},{9,7},{14,8},{15,9},{1... | collective-permute-start | bytes 129032 | tf_op jit(solution)/shard_map/ppermute | solution.py:278

commit v5 on v4

v5 whole, which is shorter than its diff:
```python
import functools
import itertools
import math

import jax
import jax.numpy as jnp
from jax import lax
from jax.experimental import pallas as pl
from jax.experimental.pallas import tpu as pltpu
from jax.sharding import PartitionSpec as P

HD = 128
BLK = 128
STAT = 128
LANE = STAT // 3
NEG = -1e30
F32 = jnp.float32
BF16 = jnp.bfloat16


def factors(members):
    cores = 2 if members % 2 == 0 else 1
    chips = members // cores
    far = next(a for a in range(1, chips + 1) if chips % a == 0 and a * a >= chips)
    return far, chips // far, cores


def shift_perm(shape, by):
    def flat(place):
        return functools.reduce(lambda at, kn: at * kn[1] + kn[0] % kn[1], zip(place, shape), 0)

    places = itertools.product(*map(range, shape))
    return [(flat([p + d for p, d in zip(at, by)]), flat(at)) for at in places]


def lanes(rows):
    return lax.broadcasted_iota(jnp.int32, (rows, STAT), 1)


def pack_stats(top, mass):
    high = mass.astype(BF16).astype(F32)
    return top + pltpu.roll(high, LANE, 1) + pltpu.roll(mass - high, 2 * LANE, 1)


def unpack_stats(packed, heads):
    used = lanes(packed.shape[0]) < heads
    mass = pltpu.roll(packed, STAT - LANE, 1) + pltpu.roll(packed, STAT - 2 * LANE, 1)
    return jnp.where(used, packed, 0.0), jnp.where(used, mass, 0.0)


def attend_kernel(sizes, scale, bias_ref, q_refs, k_ref, v_ref, outs, top_acc, mass_acc):
    tile, steps, group, pack = sizes
    parts = len(q_refs)
    rows = tile * parts
    wide = pack * HD
    lane = lanes(rows)
    contract_last = (((1,), (1,)), ((), ()))
    bias = bias_ref[...]
    mine = [lax.broadcasted_iota(jnp.int32, (rows, wide), 1) // HD == k for k in range(pack)]

    def row_tile(r, carry):
        at = pl.ds(pl.multiple_of(r * tile, tile), tile)
        top_acc[...] = jnp.zeros_like(top_acc)
        mass_acc[...] = jnp.zeros_like(mass_acc)

        def heads_of(step, carry):
            def columns(i):
                return pl.ds(pl.multiple_of((step * group + i) * wide, HD), wide)

            def scores(i):
                cols = columns(i)
                q = jnp.concatenate([ref[at, cols] for ref in q_refs], axis=0)
                if pack > 1:
                    zero = jnp.zeros_like(q)
                    q = jnp.concatenate([jnp.where(m, q, zero) for m in mine], axis=0)
                return lax.dot_general(q, k_ref[:, cols], contract_last, preferred_element_type=F32)

            tops = top_acc[...]
            masses = mass_acc[...]
            ahead = scores(0)
            for i in range(group):
                score = ahead
                if i + 1 < group:
                    ahead = scores(i + 1)
                score = score * scale + bias
                top = jnp.max(score, axis=1, keepdims=True).astype(BF16).astype(F32)
                score = jnp.exp2(score - top)
                mass = jnp.sum(score, axis=1, keepdims=True)
                out = jnp.dot(score.astype(BF16), v_ref[:, columns(i)], preferred_element_type=F32)
                for k in range(pack):
                    head = (step * group + i) * pack + k
                    cols = pl.ds(pl.multiple_of(head * HD, HD), HD)
                    one = out[k * rows : (k + 1) * rows, k * HD : (k + 1) * HD]
                    for p, o_ref in enumerate(outs):
                        o_ref[at, cols] = one[p * tile : (p + 1) * tile].astype(o_ref.dtype)
                    tops = jnp.where(lane == head, top[k * rows : (k + 1) * rows], tops)
                    masses = jnp.where(lane == head, mass[k * rows : (k + 1) * rows], masses)
            top_acc[...] = tops
            mass_acc[...] = masses
            return carry

        lax.fori_loop(0, steps, heads_of, 0)
        packed = pack_stats(top_acc[...], mass_acc[...])
        for p, o_ref in enumerate(outs):
            width = o_ref.shape[1]
            o_ref[at, width - STAT :] = packed[p * tile : (p + 1) * tile].astype(o_ref.dtype)
        return carry

    lax.fori_loop(0, q_refs[0].shape[0] // tile, row_tile, 0)


def attend(blocks, kinds, keys, values, bias):
    n = len(blocks)
    rows, columns = blocks[0].shape
    heads = columns // HD
    pack = 2 if heads % 2 == 0 else 1
    group = next(g for g in (2, 1) if heads % (g * pack) == 0)
    tile = next(t for t in (32, 16, rows) if rows % t == 0)
    width = columns + STAT
    scale = math.log2(math.e) / math.sqrt(HD)

    def body(*refs):
        attend_kernel(
            (tile, heads // (group * pack), group, pack), scale, refs[0], refs[1 : 1 + n],
            *refs[1 + n : 3 + n], refs[3 + n : 3 + 2 * n], *refs[3 + 2 * n :],
        )

    return pl.pallas_call(
        body,
        in_specs=[pl.BlockSpec(memory_space=pltpu.VMEM)] * (n + 3),
        out_specs=[pl.BlockSpec(memory_space=pltpu.VMEM)] * n,
        out_shape=[jax.ShapeDtypeStruct((rows, width), kind) for kind in kinds],
        scratch_shapes=[pltpu.VMEM((tile * n, STAT), F32)] * 2,
        compiler_params=pltpu.CompilerParams(vmem_limit_bytes=40 * 1024 * 1024),
        cost_estimate=pl.CostEstimate(
            flops=4 * n * rows * keys.shape[0] * columns,
            bytes_accessed=4 * keys.shape[0] * columns,
            transcendentals=n * rows * keys.shape[0] * heads,
        ),
        name="attend",
    )(bias, *blocks, keys, values)


def load(cached, fresh, after):
    cache_rows, columns = cached[0].shape
    tok = fresh[0].shape[0]
    padded = cache_rows + -(-tok // BLK) * BLK
    n = len(cached)

    def body(*refs):
        cached_refs, fresh_refs, outs = refs[:n], refs[n : 2 * n], refs[2 * n + 1 : 3 * n + 1]
        tails, sems = refs[3 * n + 1 : 4 * n + 1], refs[4 * n + 1]
        small = [
            pltpu.make_async_copy(src, dst, sems.at[1, i])
            for i, (src, dst) in enumerate(zip(fresh_refs, tails))
        ]
        large = [
            pltpu.make_async_copy(src, dst.at[pl.ds(0, cache_rows), :], sems.at[0, i])
            for i, (src, dst) in enumerate(zip(cached_refs, outs))
        ]
        for copy in small + large:
            copy.start()
        for copy, tail, out in zip(small, tails, outs):
            copy.wait()
            rest = jnp.zeros((padded - cache_rows - tok, columns), F32)
            rows = jnp.concatenate([tail[...].astype(F32), rest], axis=0)
            out[cache_rows:, :] = rows.astype(out.dtype)
        for copy in large:
            copy.wait()

    in_hbm = pl.BlockSpec(memory_space=pltpu.HBM)
    return pl.pallas_call(
        body,
        in_specs=[in_hbm] * (2 * n) + [pl.BlockSpec(memory_space=pl.ANY)],
        out_specs=[pl.BlockSpec(memory_space=pltpu.VMEM)] * n,
        out_shape=[jax.ShapeDtypeStruct((padded, columns), BF16)] * n,
        scratch_shapes=[pltpu.VMEM(x.shape, BF16) for x in fresh]
        + [pltpu.SemaphoreType.DMA((2, n))],
        compiler_params=pltpu.CompilerParams(vmem_limit_bytes=24 * 1024 * 1024),
        cost_estimate=pl.CostEstimate(
            flops=0, bytes_accessed=4 * n * cache_rows * columns, transcendentals=0
        ),
        name="load",
    )(*[pltpu.with_memory_space_constraint(x, pltpu.HBM) for x in (*cached, *fresh)], after)


def merged(arrays, heads, last):
    columns = heads * HD
    stats = [unpack_stats(get(slice(columns, columns + STAT)), heads) for get in arrays]
    top = functools.reduce(jnp.maximum, [t for t, _ in stats])
    weights = [jnp.exp2(t - top) for t, _ in stats]
    mass = functools.reduce(jnp.add, [w * m for w, (_, m) in zip(weights, stats)])
    if last:
        inverse = 1.0 / jnp.where(lanes(mass.shape[0]) < heads, mass, 1.0)
        weights = [w * inverse for w in weights]
    for head in range(heads):
        cols = slice(head * HD, (head + 1) * HD)
        yield cols, functools.reduce(
            jnp.add, [get(cols) * w[:, head : head + 1] for get, w in zip(arrays, weights)]
        )
    if not last:
        yield slice(columns, columns + STAT), pack_stats(top, mass)


def getter(ref, *index):
    return lambda cols: ref[(*index, slice(None), cols)].astype(F32)


def merge_rows(ins, heads, pieces, kinds):
    rows, width = ins[0].shape
    per = rows // pieces

    def body(*refs):
        outs = refs[len(ins) :]
        for cols, total in merged([getter(r) for r in refs[: len(ins)]], heads, False):
            for j, out in enumerate(outs):
                out[:, cols] = total[j * per : (j + 1) * per].astype(out.dtype)

    return call_merge(body, ins, [jax.ShapeDtypeStruct((per, width), kind) for kind in kinds])


def finish(ins, heads):
    rows = ins[0].shape[0]

    def body(*refs):
        out = refs[len(ins)]
        for cols, total in merged([getter(r) for r in refs[: len(ins)]], heads, True):
            out[:, cols] = total.astype(out.dtype)

    return call_merge(body, ins, [jax.ShapeDtypeStruct((rows, heads * HD), BF16)])[0]


def join(pieces, after=()):
    rows = sum(p.shape[0] for p in pieces)

    def body(*refs):
        out = refs[-1]
        ins = [r[...].astype(F32) for r in refs[: len(pieces)]]
        out[...] = jnp.concatenate(ins, axis=0).astype(out.dtype)

    shape = jax.ShapeDtypeStruct((rows, pieces[0].shape[1]), pieces[0].dtype)
    return call_merge(body, pieces, [shape], after)[0]


def call_merge(body, ins, shapes, after=()):
    size = sum(math.prod(x.shape) for x in ins)
    return pl.pallas_call(
        body,
        in_specs=[pl.BlockSpec(memory_space=pltpu.VMEM)] * len(ins)
        + [pl.BlockSpec(memory_space=pl.ANY)] * len(after),
        out_specs=[pl.BlockSpec(memory_space=pltpu.VMEM)] * len(shapes),
        out_shape=shapes,
        compiler_params=pltpu.CompilerParams(vmem_limit_bytes=48 * 1024 * 1024),
        cost_estimate=pl.CostEstimate(flops=4 * size, bytes_accessed=4 * size, transcendentals=0),
        name="merge",
    )(*ins, *after)


def per_device(queries, new_keys, new_values, cache_keys, cache_values, victims):
    members = lax.axis_size("seq")
    shape = factors(members)
    a_n, b_n, c_n = shape
    heads = queries.shape[1] // HD
    block_count = cache_keys.shape[0] // BLK
    block_ids = lax.axis_index("seq") * block_count + jnp.arange(block_count, dtype=jnp.int32)
    evicted = jnp.any(victims[:, None] == block_ids[None, :], axis=0)
    bias = jnp.repeat(jnp.where(evicted, NEG, 0.0), BLK)[None, :]
    tok = new_keys.shape[0]
    fresh_bias = jnp.where(jnp.arange(-(-tok // BLK) * BLK) < tok, 0.0, NEG)[None, :]
    bias = jnp.concatenate([bias, fresh_bias], axis=1)

    def fetch(x, by):
        return lax.ppermute(x, "seq", shift_perm(shape, by))

    def give(x, by):
        return lax.ppermute(x, "seq", shift_perm(shape, [-d for d in by]))

    far_first = sorted(range(1, a_n), key=lambda d: -min(d, a_n - d))
    line = [queries] + [None] * (a_n - 1)
    for d in far_first:
        line[d] = fetch(queries, (d, 0, 0))
    lines = [line] + [[fetch(x, (0, d, 0)) for x in line] for d in range(1, b_n)]
    last = line[far_first[-1]] if far_first else queries
    keys, values = load((cache_keys, cache_values), (new_keys, new_values), last)

    home = [join([join([queries])] + line[1:])] + [join(x, (keys,)) for x in lines[1:]]
    away = [[fetch(x, (0, 0, c)) for x in home] for c in range(1, c_n)]
    blocks = home + [x for core in away for x in core]
    kinds = [F32] * b_n + [BF16] * (b_n * (c_n - 1))
    blocks = attend(blocks, kinds, keys, values, bias)
    home, away = blocks[:b_n], blocks[b_n:]

    def over_cores(b, kind):
        got = [give(away[c * b_n + b], (0, 0, c + 1)) for c in range(c_n - 1)]
        return merge_rows([home[b]] + got, heads, a_n, [kind] * a_n)

    got = [[give(x, (0, d, 0)) for x in over_cores(d, BF16)] for d in range(1, b_n)]
    own = over_cores(0, F32)
    sums = [[own[d]] + [pieces[d] for pieces in got] for d in range(a_n)]
    for d in far_first:
        sums[d] = [give(merge_rows(sums[d], heads, 1, [BF16])[0], (d, 0, 0))]
    return finish([x for pieces in sums for x in pieces], heads)


def solution(mesh):
    rows = P(("groups", "seq"), None)
    return jax.shard_map(
        per_device,
        mesh=mesh,
        in_specs=(rows, rows, rows, rows, rows, P("groups")),
        out_specs=rows,
        check_vma=False,
    )
```

time: 44.3 us -> 37.6 us (0.85)
  starting transfers between devices: 24 us -> 18.2 us
  waiting for transfers between devices: 11.1 us -> 8.44 us
  Pallas kernels: 7.24 us -> 8.9 us
    ppermute x8 -> x9, starting transfers between devices: 11.4 us -> 7.97 us  [give(): return lax.ppermute(x, 'seq', shift_perm(shape, [-d for d in by]))]
    ppermute x8 -> x9, waiting for transfers between devices: 6.58 us -> 3.72 us  [fetch(): return lax.ppermute(x, 'seq', shift_perm(shape, by))]
    ppermute x8 -> x9, starting transfers between devices: 12.6 us -> 10.3 us  [fetch(): return lax.ppermute(x, 'seq', shift_perm(shape, by))]
    pallas_call x1 -> x2, Pallas kernels: 5.75 us -> 6.95 us  [the longest x1 4.33 us: attend(): pl.pallas_call(body, in_specs=[pl.BlockSpec(memory_space=pltpu.VMEM)] * (...]
    pallas_call x4 -> x9, Pallas kernels: 1.49 us -> 1.95 us  [call_merge(): pl.pallas_call(body, in_specs=[pl.BlockSpec(memory_space=pltpu.VMEM)] * l...]
    ppermute x8 -> x9, waiting for transfers between devices: 4.47 us -> 4.72 us  [give(): return lax.ppermute(x, 'seq', shift_perm(shape, [-d for d in by]))]
  transfers between devices with their start and end apart: 16 -> 18, of which waited for: 6 -> 9; matrix products, arithmetic and copies ran while one was open for 2% -> 2% of each run, Pallas kernels for 0% -> 10%
where the time goes in v5:
time: 37.6 us; the launch traced here: 37.4 us
  starting transfers between devices  18.2 us (48%)
  Pallas kernels  8.9 us (24%)
  waiting for transfers between devices  8.44 us (22%)
  other arithmetic  0.86 us (2%)
  local copies, waits for them, and re-layouts  0.85 us (2%)
    ppermute x9, starting transfers between devices, fetch(): return lax.ppermute(x, 'seq', shift_perm(shape, by))  10.3 us
    ppermute x9, starting transfers between devices, give(): return lax.ppermute(x, 'seq', shift_perm(shape, [-d for d in by]))  7.97 us
    ppermute x9, waiting for transfers between devices, give(): return lax.ppermute(x, 'seq', shift_perm(shape, [-d for d in by]))  4.72 us
    pallas_call x1, Pallas kernels, attend(): pl.pallas_call(body, in_specs=[pl.BlockSpec(memory_space=pltpu.VMEM)] * (...  4.33 us
    ppermute x9, waiting for transfers between devices, fetch(): return lax.ppermute(x, 'seq', shift_perm(shape, by))  3.72 us
    pallas_call x1, Pallas kernels, load(): pl.pallas_call(body, in_specs=[in_hbm] * (2 * n) + [pl.BlockSpec(memory_s...  2.62 us
    pallas_call x9, Pallas kernels, call_merge(): pl.pallas_call(body, in_specs=[pl.BlockSpec(memory_space=pltpu.VMEM)] * l...  1.95 us
    reduce_or x1, other arithmetic, per_device(): evicted = jnp.any(victims[:, None] == block_ids[None, :], axis=0)  0.84 us
  transfers between devices with their start and end apart: 18, of which 9 were waited for; matrix products, arithmetic and copies ran while one was open for 2% of the time, Pallas kernels for 10%

profile of v5, /device:TPU:0, one launch (start us, length us, event | category | flops | bytes accessed | tf_op | source)
XLA Modules:
  0.0 37.4 jit_solution(563681477187907754)
XLA Ops:
  0.0 4.0 %collective-permute-start.1 = (bf16[8,2560]{1,0:T(8,128)(2,1)}, bf16[8,2560]{1,0:T(8,128)(2,1)S(1)}, u32[]{:S(2)}, u32[]{:S(2)}) collective-permute-start(bf16[8,2560]{1,0:T(8,128)(2,1)} %refs_0_.2), channel_id=1, source_target_pairs={{8,0},{9,1},{10,2},{11,3},{12,4},{13,5},{14,6},{15,7},{0,8},{1,9},... | collective-permute-start | bytes 122888 | tf_op jit(solution)/shard_map/ppermute | solution.py:273
  4.0 1.3 %collective-permute-start = (bf16[8,2560]{1,0:T(8,128)(2,1)}, bf16[8,2560]{1,0:T(8,128)(2,1)S(1)}, u32[]{:S(2)}, u32[]{:S(2)}) collective-permute-start(bf16[8,2560]{1,0:T(8,128)(2,1)} %refs_0_.2), channel_id=1, source_target_pairs={{4,0},{5,1},{6,2},{7,3},{8,4},{9,5},{10,6},{11,7},{12,8},{13,9},{1... | collective-permute-start | bytes 122888 | tf_op jit(solution)/shard_map/ppermute | solution.py:273
  5.4 1.5 %collective-permute-start.3 = (bf16[8,2560]{1,0:T(8,128)(2,1)}, bf16[8,2560]{1,0:T(8,128)(2,1)S(1)}, u32[]{:S(2)}, u32[]{:S(2)}) collective-permute-start(bf16[8,2560]{1,0:T(8,128)(2,1)} %refs_0_.2), channel_id=1, source_target_pairs={{2,0},{3,1},{0,2},{1,3},{6,4},{7,5},{4,6},{5,7},{10,8},{11,9},{8,1... | collective-permute-start | bytes 122888 | tf_op jit(solution)/shard_map/ppermute | solution.py:273
  6.9 0.7 %collective-permute-start.2 = (bf16[8,2560]{1,0:T(8,128)(2,1)}, bf16[8,2560]{1,0:T(8,128)(2,1)S(1)}, u32[]{:S(2)}, u32[]{:S(2)}) collective-permute-start(bf16[8,2560]{1,0:T(8,128)(2,1)} %refs_0_.2), channel_id=1, source_target_pairs={{12,0},{13,1},{14,2},{15,3},{0,4},{1,5},{2,6},{3,7},{4,8},{5,9},{6... | collective-permute-start | bytes 122888 | tf_op jit(solution)/shard_map/ppermute | solution.py:273
  7.6 0.8 %compare_reduce_fusion = pred[4]{0:T(512)(128)(4,1)S(1)} fusion(s32[16]{0:T(128)} %param.11, s32[4]{0:T(128)S(1)} %iota_add_fusion), kind=kLoop, calls=%fused_computation.2 | loop fusion | flops 124 | bytes 84 | tf_op jit(solution)/shard_map/reduce_or | solution.py:266
  8.4 0.8 %copy-done = bf16[8,2560]{1,0:T(8,128)(2,1)S(1)} copy-done((bf16[8,2560]{1,0:T(8,128)(2,1)S(1)}, bf16[8,2560]{1,0:T(8,128)(2,1)}, u32[]{:S(2)}) %copy-start) | copy-done | bytes 40984
  9.2 0.5 %collective-permute-start.5 = (bf16[8,2560]{1,0:T(8,128)(2,1)S(1)}, bf16[8,2560]{1,0:T(8,128)(2,1)S(1)}, u32[]{:S(2)}, u32[]{:S(2)}) collective-permute-start(bf16[8,2560]{1,0:T(8,128)(2,1)S(1)} %collective-permute-done.1.refs_2_), channel_id=1, source_target_pairs={{2,0},{3,1},{0,2},{1,3},{6,4},{7,5},{4,6},{5,7},{10,8},{11,9},{8,1... | collective-permute-start | bytes 122888 | tf_op jit(solution)/shard_map/ppermute | solution.py:273
  9.7 1.5 %collective-permute-start.4 = (bf16[8,2560]{1,0:T(8,128)(2,1)S(1)}, bf16[8,2560]{1,0:T(8,128)(2,1)S(1)}, u32[]{:S(2)}, u32[]{:S(2)}) collective-permute-start(bf16[8,2560]{1,0:T(8,128)(2,1)S(1)} %collective-permute-done.refs_1_), channel_id=1, source_target_pairs={{2,0},{3,1},{0,2},{1,3},{6,4},{7,5},{4,6},{5,7},{10,8},{11,9},{8,1... | collective-permute-start | bytes 122888 | tf_op jit(solution)/shard_map/ppermute | solution.py:273
  11.2 1.7 %collective-permute-done.2.refs_3_.refs_4_ = bf16[8,2560]{1,0:T(8,128)(2,1)S(1)} collective-permute-done((bf16[8,2560]{1,0:T(8,128)(2,1)}, bf16[8,2560]{1,0:T(8,128)(2,1)S(1)}, u32[]{:S(2)}, u32[]{:S(2)}) %collective-permute-start.2) | collective-permute-done | bytes 40992 | tf_op jit(solution)/shard_map/ppermute | solution.py:273
  12.9 0.5 %collective-permute-start.6 = (bf16[8,2560]{1,0:T(8,128)(2,1)S(1)}, bf16[8,2560]{1,0:T(8,128)(2,1)S(1)}, u32[]{:S(2)}, u32[]{:S(2)}) collective-permute-start(bf16[8,2560]{1,0:T(8,128)(2,1)S(1)} %collective-permute-done.2.refs_3_.refs_4_), channel_id=1, source_target_pairs={{2,0},{3,1},{0,2},{1,3},{6,4},{7,5},{4,6},{5,7},{10,8},{11,9},{8,1... | collective-permute-start | bytes 122888 | tf_op jit(solution)/shard_map/ppermute | solution.py:273
  13.5 2.6 %load.1 = (bf16[640,2560]{1,0:T(8,128)(2,1)S(1)}, bf16[640,2560]{1,0:T(8,128)(2,1)S(1)}) custom-call(bf16[512,2560]{1,0:T(8,128)(2,1)} %refs_0_.3, bf16[512,2560]{1,0:T(8,128)(2,1)} %refs_1_.1, bf16[8,2560]{1,0:T(8,128)(2,1)} %refs_2_.1, bf16[8,2560]{1,0:T(8,128)(2,1)} %refs_3_.1, bf16[8,2560]{1,0:T(8,128)(2,1)S(1)} %collective-permute-done.2.refs_3_.refs_4_), custom_call_target="tpu_custom_call" | custom-call | bytes 10485760 | tf_op jit(solution)/shard_map/load/pallas_call | solution.py:172
  16.2 0.7 %collective-permute-done.6.refs_3_ = bf16[8,2560]{1,0:T(8,128)(2,1)S(1)} collective-permute-done((bf16[8,2560]{1,0:T(8,128)(2,1)S(1)}, bf16[8,2560]{1,0:T(8,128)(2,1)S(1)}, u32[]{:S(2)}, u32[]{:S(2)}) %collective-permute-start.6) | collective-permute-done | bytes 40992 | tf_op jit(solution)/shard_map/ppermute | solution.py:273
  17.1 1.3 %collective-permute-done.8.refs_4_ = bf16[32,2560]{1,0:T(8,128)(2,1)S(1)} collective-permute-done((bf16[32,2560]{1,0:T(8,128)(2,1)S(1)}, bf16[32,2560]{1,0:T(8,128)(2,1)S(1)}, u32[]{:S(2)}, u32[]{:S(2)}) %collective-permute-start.8) | collective-permute-done | bytes 163872 | tf_op jit(solution)/shard_map/ppermute | solution.py:273
  18.4 4.3 %attend.1 = (f32[32,2688]{1,0:T(8,128)S(1)}, f32[32,2688]{1,0:T(8,128)S(1)}, bf16[32,2688]{1,0:T(8,128)(2,1)S(1)}, bf16[32,2688]{1,0:T(8,128)(2,1)S(1)}) custom-call(f32[1,640]{1,0:T(1,128)S(1)} %pad_maximum_fusion.refs_0_, bf16[32,2560]{1,0:T(8,128)(2,1)S(1)} %merge.10.refs_1_, bf16[32,2560]{1,0:T(8,128)(2,1)S(1)} %merge.11.refs_2_, ...), custom_call_target="tpu_custom_call" | custom-call | flops 838860800 | bytes 6553600 | tf_op jit(solution)/shard_map/attend/pallas_call | solution.py:128
  22.7 0.2 collective-permute-start.10
  22.9 0.4 collective-permute-start.9
  23.3 0.9 %collective-permute-done.10.refs_1_ = bf16[32,2688]{1,0:T(8,128)(2,1)S(1)} collective-permute-done((bf16[32,2688]{1,0:T(8,128)(2,1)S(1)}, bf16[32,2688]{1,0:T(8,128)(2,1)S(1)}, u32[]{:S(2)}, u32[]{:S(2)}) %collective-permute-start.10) | collective-permute-done | bytes 172064 | tf_op jit(solution)/shard_map/ppermute | solution.py:276
  24.2 0.3 merge.13
  24.5 1.0 %collective-permute-start.12 = (bf16[8,2688]{1,0:T(8,128)(2,1)S(1)}, bf16[8,2688]{1,0:T(8,128)(2,1)S(1)}, u32[]{:S(2)}, u32[]{:S(2)}) collective-permute-start(bf16[8,2688]{1,0:T(8,128)(2,1)S(1)} %get-tuple-element.28), channel_id=1, source_target_pairs={{2,0},{3,1},{0,2},{1,3},{6,4},{7,5},{4,6},{5,7},{10,8},{11,9},{8,1... | collective-permute-start | bytes 129032 | tf_op jit(solution)/shard_map/ppermute | solution.py:276
  25.5 1.1 %collective-permute-start.14 = (bf16[8,2688]{1,0:T(8,128)(2,1)S(1)}, bf16[8,2688]{1,0:T(8,128)(2,1)S(1)}, u32[]{:S(2)}, u32[]{:S(2)}) collective-permute-start(bf16[8,2688]{1,0:T(8,128)(2,1)S(1)} %get-tuple-element.30), channel_id=1, source_target_pairs={{2,0},{3,1},{0,2},{1,3},{6,4},{7,5},{4,6},{5,7},{10,8},{11,9},{8,1... | collective-permute-start | bytes 129032 | tf_op jit(solution)/shard_map/ppermute | solution.py:276
  26.6 0.9 %collective-permute-start.16 = (bf16[8,2688]{1,0:T(8,128)(2,1)S(1)}, bf16[8,2688]{1,0:T(8,128)(2,1)S(1)}, u32[]{:S(2)}, u32[]{:S(2)}) collective-permute-start(bf16[8,2688]{1,0:T(8,128)(2,1)S(1)} %get-tuple-element.32), channel_id=1, source_target_pairs={{2,0},{3,1},{0,2},{1,3},{6,4},{7,5},{4,6},{5,7},{10,8},{11,9},{8,1... | collective-permute-start | bytes 129032 | tf_op jit(solution)/shard_map/ppermute | solution.py:276
  27.5 1.1 %collective-permute-start.11 = (bf16[8,2688]{1,0:T(8,128)(2,1)S(1)}, bf16[8,2688]{1,0:T(8,128)(2,1)S(1)}, u32[]{:S(2)}, u32[]{:S(2)}) collective-permute-start(bf16[8,2688]{1,0:T(8,128)(2,1)S(1)} %get-tuple-element.26), channel_id=1, source_target_pairs={{2,0},{3,1},{0,2},{1,3},{6,4},{7,5},{4,6},{5,7},{10,8},{11,9},{8,1... | collective-permute-start | bytes 129032 | tf_op jit(solution)/shard_map/ppermute | solution.py:276
  28.6 0.3 merge.12
  29.0 0.1 merge.14
  29.2 0.7 %collective-permute-done.14.refs_1_ = bf16[8,2688]{1,0:T(8,128)(2,1)S(1)} collective-permute-done((bf16[8,2688]{1,0:T(8,128)(2,1)S(1)}, bf16[8,2688]{1,0:T(8,128)(2,1)S(1)}, u32[]{:S(2)}, u32[]{:S(2)}) %collective-permute-start.14) | collective-permute-done | bytes 43040 | tf_op jit(solution)/shard_map/ppermute | solution.py:276
  30.0 0.1 merge.15
  30.1 1.4 %collective-permute-start.15 = (bf16[8,2688]{1,0:T(8,128)(2,1)S(1)}, bf16[8,2688]{1,0:T(8,128)(2,1)S(1)}, u32[]{:S(2)}, u32[]{:S(2)}) collective-permute-start(bf16[8,2688]{1,0:T(8,128)(2,1)S(1)} %merge.15), channel_id=1, source_target_pairs={{8,0},{9,1},{10,2},{11,3},{12,4},{13,5},{14,6},{15,7},{0,8},{1,9},... | collective-permute-start | bytes 129032 | tf_op jit(solution)/shard_map/ppermute | solution.py:276
  31.5 0.1 merge.16
  31.6 1.9 %collective-permute-start.17 = (bf16[8,2688]{1,0:T(8,128)(2,1)S(1)}, bf16[8,2688]{1,0:T(8,128)(2,1)S(1)}, u32[]{:S(2)}, u32[]{:S(2)}) collective-permute-start(bf16[8,2688]{1,0:T(8,128)(2,1)S(1)} %merge.16), channel_id=1, source_target_pairs={{4,0},{5,1},{6,2},{7,3},{8,4},{9,5},{10,6},{11,7},{12,8},{13,9},{1... | collective-permute-start | bytes 129032 | tf_op jit(solution)/shard_map/ppermute | solution.py:276
  33.5 1.7 %collective-permute-done.13.refs_2_ = bf16[8,2688]{1,0:T(8,128)(2,1)S(1)} collective-permute-done((bf16[8,2688]{1,0:T(8,128)(2,1)S(1)}, bf16[8,2688]{1,0:T(8,128)(2,1)S(1)}, u32[]{:S(2)}, u32[]{:S(2)}) %collective-permute-start.13) | collective-permute-done | bytes 43040 | tf_op jit(solution)/shard_map/ppermute | solution.py:276
  35.1 1.3 %collective-permute-done.15.refs_3_ = bf16[8,2688]{1,0:T(8,128)(2,1)S(1)} collective-permute-done((bf16[8,2688]{1,0:T(8,128)(2,1)S(1)}, bf16[8,2688]{1,0:T(8,128)(2,1)S(1)}, u32[]{:S(2)}, u32[]{:S(2)}) %collective-permute-start.15) | collective-permute-done | bytes 43040 | tf_op jit(solution)/shard_map/ppermute | solution.py:276
  36.5 0.9 %merge.17 = bf16[8,2560]{1,0:T(8,128)(2,1)} custom-call(f32[8,2688]{1,0:T(8,128)S(1)} %get-tuple-element.23.refs_0_, bf16[8,2688]{1,0:T(8,128)(2,1)S(1)} %collective-permute-done.11.refs_1_, bf16[8,2688]{1,0:T(8,128)(2,1)S(1)} %collective-permute-done.13.refs_2_, bf16[8,2688]{1,0:T(8,128)(2,1)S(1)} %collective-permute-done.15.refs_3_, ...), custom_call_target="tpu_custom_call" | custom-call | flops 430080 | bytes 430080 | tf_op jit(solution)/shard_map/merge/pallas_call | solution.py:247
  (23 shorter events, 0.5 us)
Async XLA Ops:
  0.0 9.2 %collective-permute-start.1 = (bf16[8,2560]{1,0:T(8,128)(2,1)}, bf16[8,2560]{1,0:T(8,128)(2,1)S(1)}, u32[]{:S(2)}, u32[]{:S(2)}) collective-permute-start(bf16[8,2560]{1,0:T(8,128)(2,1)} %refs_0_.2), channel_id=1, source_target_pairs={{8,0},{9,1},{10,2},{11,3},{12,4},{13,5},{14,6},{15,7},{0,8},{1,9},... | collective-permute-start | bytes 122888 | tf_op jit(solution)/shard_map/ppermute | solution.py:273
  4.0 5.7 %collective-permute-start = (bf16[8,2560]{1,0:T(8,128)(2,1)}, bf16[8,2560]{1,0:T(8,128)(2,1)S(1)}, u32[]{:S(2)}, u32[]{:S(2)}) collective-permute-start(bf16[8,2560]{1,0:T(8,128)(2,1)} %refs_0_.2), channel_id=1, source_target_pairs={{4,0},{5,1},{6,2},{7,3},{8,4},{9,5},{10,6},{11,7},{12,8},{13,9},{1... | collective-permute-start | bytes 122888 | tf_op jit(solution)/shard_map/ppermute | solution.py:273
  5.4 10.8 %collective-permute-start.3 = (bf16[8,2560]{1,0:T(8,128)(2,1)}, bf16[8,2560]{1,0:T(8,128)(2,1)S(1)}, u32[]{:S(2)}, u32[]{:S(2)}) collective-permute-start(bf16[8,2560]{1,0:T(8,128)(2,1)} %refs_0_.2), channel_id=1, source_target_pairs={{2,0},{3,1},{0,2},{1,3},{6,4},{7,5},{4,6},{5,7},{10,8},{11,9},{8,1... | collective-permute-start | bytes 122888 | tf_op jit(solution)/shard_map/ppermute | solution.py:273
  6.9 6.0 %collective-permute-start.2 = (bf16[8,2560]{1,0:T(8,128)(2,1)}, bf16[8,2560]{1,0:T(8,128)(2,1)S(1)}, u32[]{:S(2)}, u32[]{:S(2)}) collective-permute-start(bf16[8,2560]{1,0:T(8,128)(2,1)} %refs_0_.2), channel_id=1, source_target_pairs={{12,0},{13,1},{14,2},{15,3},{0,4},{1,5},{2,6},{3,7},{4,8},{5,9},{6... | collective-permute-start | bytes 122888 | tf_op jit(solution)/shard_map/ppermute | solution.py:273
  8.4 0.8 %copy-start = (bf16[8,2560]{1,0:T(8,128)(2,1)S(1)}, bf16[8,2560]{1,0:T(8,128)(2,1)}, u32[]{:S(2)}) copy-start(bf16[8,2560]{1,0:T(8,128)(2,1)} %refs_0_.2) | copy-start | bytes 122884
  9.2 6.9 %collective-permute-start.5 = (bf16[8,2560]{1,0:T(8,128)(2,1)S(1)}, bf16[8,2560]{1,0:T(8,128)(2,1)S(1)}, u32[]{:S(2)}, u32[]{:S(2)}) collective-permute-start(bf16[8,2560]{1,0:T(8,128)(2,1)S(1)} %collective-permute-done.1.refs_2_), channel_id=1, source_target_pairs={{2,0},{3,1},{0,2},{1,3},{6,4},{7,5},{4,6},{5,7},{10,8},{11,9},{8,1... | collective-permute-start | bytes 122888 | tf_op jit(solution)/shard_map/ppermute | solution.py:273
  9.7 6.4 %collective-permute-start.4 = (bf16[8,2560]{1,0:T(8,128)(2,1)S(1)}, bf16[8,2560]{1,0:T(8,128)(2,1)S(1)}, u32[]{:S(2)}, u32[]{:S(2)}) collective-permute-start(bf16[8,2560]{1,0:T(8,128)(2,1)S(1)} %collective-permute-done.refs_1_), channel_id=1, source_target_pairs={{2,0},{3,1},{0,2},{1,3},{6,4},{7,5},{4,6},{5,7},{10,8},{11,9},{8,1... | collective-permute-start | bytes 122888 | tf_op jit(solution)/shard_map/ppermute | solution.py:273
  12.9 4.0 %collective-permute-start.6 = (bf16[8,2560]{1,0:T(8,128)(2,1)S(1)}, bf16[8,2560]{1,0:T(8,128)(2,1)S(1)}, u32[]{:S(2)}, u32[]{:S(2)}) collective-permute-start(bf16[8,2560]{1,0:T(8,128)(2,1)S(1)} %collective-permute-done.2.refs_3_.refs_4_), channel_id=1, source_target_pairs={{2,0},{3,1},{0,2},{1,3},{6,4},{7,5},{4,6},{5,7},{10,8},{11,9},{8,1... | collective-permute-start | bytes 122888 | tf_op jit(solution)/shard_map/ppermute | solution.py:273
  13.4 3.7 %collective-permute-start.7 = (bf16[32,2560]{1,0:T(8,128)(2,1)S(1)}, bf16[32,2560]{1,0:T(8,128)(2,1)S(1)}, u32[]{:S(2)}, u32[]{:S(2)}) collective-permute-start(bf16[32,2560]{1,0:T(8,128)(2,1)S(1)} %merge.10.refs_1_), channel_id=1, source_target_pairs={{1,0},{0,1},{3,2},{2,3},{5,4},{4,5},{7,6},{6,7},{9,8},{8,9},{11,10... | collective-permute-start | bytes 491528 | tf_op jit(solution)/shard_map/ppermute | solution.py:273
  16.9 1.5 %collective-permute-start.8 = (bf16[32,2560]{1,0:T(8,128)(2,1)S(1)}, bf16[32,2560]{1,0:T(8,128)(2,1)S(1)}, u32[]{:S(2)}, u32[]{:S(2)}) collective-permute-start(bf16[32,2560]{1,0:T(8,128)(2,1)S(1)} %merge.11.refs_2_), channel_id=1, source_target_pairs={{1,0},{0,1},{3,2},{2,3},{5,4},{4,5},{7,6},{6,7},{9,8},{8,9},{11,10... | collective-permute-start | bytes 491528 | tf_op jit(solution)/shard_map/ppermute | solution.py:273
  22.7 1.5 %collective-permute-start.10 = (bf16[32,2688]{1,0:T(8,128)(2,1)S(1)}, bf16[32,2688]{1,0:T(8,128)(2,1)S(1)}, u32[]{:S(2)}, u32[]{:S(2)}) collective-permute-start(bf16[32,2688]{1,0:T(8,128)(2,1)S(1)} %get-tuple-element.25), channel_id=1, source_target_pairs={{1,0},{0,1},{3,2},{2,3},{5,4},{4,5},{7,6},{6,7},{9,8},{8,9},{11,10... | collective-permute-start | bytes 516104 | tf_op jit(solution)/shard_map/ppermute | solution.py:276
  22.9 5.7 %collective-permute-start.9 = (bf16[32,2688]{1,0:T(8,128)(2,1)S(1)}, bf16[32,2688]{1,0:T(8,128)(2,1)S(1)}, u32[]{:S(2)}, u32[]{:S(2)}) collective-permute-start(bf16[32,2688]{1,0:T(8,128)(2,1)S(1)} %get-tuple-element.22), channel_id=1, source_target_pairs={{1,0},{0,1},{3,2},{2,3},{5,4},{4,5},{7,6},{6,7},{9,8},{8,9},{11,10... | collective-permute-start | bytes 516104 | tf_op jit(solution)/shard_map/ppermute | solution.py:276
  24.5 4.5 %collective-permute-start.12 = (bf16[8,2688]{1,0:T(8,128)(2,1)S(1)}, bf16[8,2688]{1,0:T(8,128)(2,1)S(1)}, u32[]{:S(2)}, u32[]{:S(2)}) collective-permute-start(bf16[8,2688]{1,0:T(8,128)(2,1)S(1)} %get-tuple-element.28), channel_id=1, source_target_pairs={{2,0},{3,1},{0,2},{1,3},{6,4},{7,5},{4,6},{5,7},{10,8},{11,9},{8,1... | collective-permute-start | bytes 129032 | tf_op jit(solution)/shard_map/ppermute | solution.py:276
  25.5 4.5 %collective-permute-start.14 = (bf16[8,2688]{1,0:T(8,128)(2,1)S(1)}, bf16[8,2688]{1,0:T(8,128)(2,1)S(1)}, u32[]{:S(2)}, u32[]{:S(2)}) collective-permute-start(bf16[8,2688]{1,0:T(8,128)(2,1)S(1)} %get-tuple-element.30), channel_id=1, source_target_pairs={{2,0},{3,1},{0,2},{1,3},{6,4},{7,5},{4,6},{5,7},{10,8},{11,9},{8,1... | collective-permute-start | bytes 129032 | tf_op jit(solution)/shard_map/ppermute | solution.py:276
  26.6 4.9 %collective-permute-start.16 = (bf16[8,2688]{1,0:T(8,128)(2,1)S(1)}, bf16[8,2688]{1,0:T(8,128)(2,1)S(1)}, u32[]{:S(2)}, u32[]{:S(2)}) collective-permute-start(bf16[8,2688]{1,0:T(8,128)(2,1)S(1)} %get-tuple-element.32), channel_id=1, source_target_pairs={{2,0},{3,1},{0,2},{1,3},{6,4},{7,5},{4,6},{5,7},{10,8},{11,9},{8,1... | collective-permute-start | bytes 129032 | tf_op jit(solution)/shard_map/ppermute | solution.py:276
  27.5 6.0 %collective-permute-start.11 = (bf16[8,2688]{1,0:T(8,128)(2,1)S(1)}, bf16[8,2688]{1,0:T(8,128)(2,1)S(1)}, u32[]{:S(2)}, u32[]{:S(2)}) collective-permute-start(bf16[8,2688]{1,0:T(8,128)(2,1)S(1)} %get-tuple-element.26), channel_id=1, source_target_pairs={{2,0},{3,1},{0,2},{1,3},{6,4},{7,5},{4,6},{5,7},{10,8},{11,9},{8,1... | collective-permute-start | bytes 129032 | tf_op jit(solution)/shard_map/ppermute | solution.py:276
  29.2 6.0 %collective-permute-start.13 = (bf16[8,2688]{1,0:T(8,128)(2,1)S(1)}, bf16[8,2688]{1,0:T(8,128)(2,1)S(1)}, u32[]{:S(2)}, u32[]{:S(2)}) collective-permute-start(bf16[8,2688]{1,0:T(8,128)(2,1)S(1)} %merge.14), channel_id=1, source_target_pairs={{12,0},{13,1},{14,2},{15,3},{0,4},{1,5},{2,6},{3,7},{4,8},{5,9},{6... | collective-permute-start | bytes 129032 | tf_op jit(solution)/shard_map/ppermute | solution.py:276
  30.1 6.3 %collective-permute-start.15 = (bf16[8,2688]{1,0:T(8,128)(2,1)S(1)}, bf16[8,2688]{1,0:T(8,128)(2,1)S(1)}, u32[]{:S(2)}, u32[]{:S(2)}) collective-permute-start(bf16[8,2688]{1,0:T(8,128)(2,1)S(1)} %merge.15), channel_id=1, source_target_pairs={{8,0},{9,1},{10,2},{11,3},{12,4},{13,5},{14,6},{15,7},{0,8},{1,9},... | collective-permute-start | bytes 129032 | tf_op jit(solution)/shard_map/ppermute | solution.py:276
  31.6 4.8 %collective-permute-start.17 = (bf16[8,2688]{1,0:T(8,128)(2,1)S(1)}, bf16[8,2688]{1,0:T(8,128)(2,1)S(1)}, u32[]{:S(2)}, u32[]{:S(2)}) collective-permute-start(bf16[8,2688]{1,0:T(8,128)(2,1)S(1)} %merge.16), channel_id=1, source_target_pairs={{4,0},{5,1},{6,2},{7,3},{8,4},{9,5},{10,6},{11,7},{12,8},{13,9},{1... | collective-permute-start | bytes 129032 | tf_op jit(solution)/shard_map/ppermute | solution.py:276

commit v6 on v5

--- a/solution.py
+++ b/solution.py
@@ -25,12 +25,17 @@
     return far, chips // far, cores
 
 
-def shift_perm(shape, by):
+def partner(at, by, size):
+    return at ^ by if size & (size - 1) == 0 else (at + by) % size
+
+
+def partner_perm(shape, by, back):
     def flat(place):
-        return functools.reduce(lambda at, kn: at * kn[1] + kn[0] % kn[1], zip(place, shape), 0)
+        return functools.reduce(lambda at, kn: at * kn[1] + kn[0], zip(place, shape), 0)
 
     places = itertools.product(*map(range, shape))
-    return [(flat([p + d for p, d in zip(at, by)]), flat(at)) for at in places]
+    pairs = [(flat([partner(*x) for x in zip(at, by, shape)]), flat(at)) for at in places]
+    return [pair[::-1] for pair in pairs] if back else pairs
 
 
 def lanes(rows):
@@ -49,9 +54,9 @@
 
 
 def attend_kernel(sizes, scale, bias_ref, q_refs, k_ref, v_ref, outs, top_acc, mass_acc):
-    tile, steps, group, pack = sizes
-    parts = len(q_refs)
-    rows = tile * parts
+    tile, steps, group, pack, lines = sizes
+    rows = tile * len(outs)
+    line_rows = outs[0].shape[0]
     wide = pack * HD
     lane = lanes(rows)
     contract_last = (((1,), (1,)), ((), ()))
@@ -60,6 +65,7 @@
 
     def row_tile(r, carry):
         at = pl.ds(pl.multiple_of(r * tile, tile), tile)
+        in_plane = [pl.ds(pl.multiple_of(b * line_rows + r * tile, tile), tile) for b in range(lines)]
         top_acc[...] = jnp.zeros_like(top_acc)
         mass_acc[...] = jnp.zeros_like(mass_acc)
 
@@ -69,7 +75,7 @@
 
             def scores(i):
                 cols = columns(i)
-                q = jnp.concatenate([ref[at, cols] for ref in q_refs], axis=0)
+                q = jnp.concatenate([ref[rs, cols] for ref in q_refs for rs in in_plane], axis=0)
                 if pack > 1:
                     zero = jnp.zeros_like(q)
                     q = jnp.concatenate([jnp.where(m, q, zero) for m in mine], axis=0)
@@ -106,12 +112,12 @@
             o_ref[at, width - STAT :] = packed[p * tile : (p + 1) * tile].astype(o_ref.dtype)
         return carry
 
-    lax.fori_loop(0, q_refs[0].shape[0] // tile, row_tile, 0)
-
-
-def attend(blocks, kinds, keys, values, bias):
-    n = len(blocks)
-    rows, columns = blocks[0].shape
+    lax.fori_loop(0, line_rows // tile, row_tile, 0)
+
+
+def attend(planes, lines, kinds, keys, values, bias):
+    n, m = len(planes), len(kinds)
+    rows, columns = planes[0].shape[0] // lines, planes[0].shape[1]
     heads = columns // HD
     pack = 2 if heads % 2 == 0 else 1
     group = next(g for g in (2, 1) if heads % (g * pack) == 0)
@@ -121,35 +127,40 @@
 
     def body(*refs):
         attend_kernel(
-            (tile, heads // (group * pack), group, pack), scale, refs[0], refs[1 : 1 + n],
-            *refs[1 + n : 3 + n], refs[3 + n : 3 + 2 * n], *refs[3 + 2 * n :],
+            (tile, heads // (group * pack), group, pack, lines), scale, refs[0], refs[1 : 1 + n],
+            *refs[1 + n : 3 + n], refs[3 + n : 3 + n + m], *refs[3 + n + m :],
         )
 
     return pl.pallas_call(
         body,
         in_specs=[pl.BlockSpec(memory_space=pltpu.VMEM)] * (n + 3),
-        out_specs=[pl.BlockSpec(memory_space=pltpu.VMEM)] * n,
+        out_specs=[pl.BlockSpec(memory_space=pltpu.VMEM)] * m,
         out_shape=[jax.ShapeDtypeStruct((rows, width), kind) for kind in kinds],
-        scratch_shapes=[pltpu.VMEM((tile * n, STAT), F32)] * 2,
+        scratch_shapes=[pltpu.VMEM((tile * m, STAT), F32)] * 2,
         compiler_params=pltpu.CompilerParams(vmem_limit_bytes=40 * 1024 * 1024),
         cost_estimate=pl.CostEstimate(
-            flops=4 * n * rows * keys.shape[0] * columns,
+            flops=4 * m * rows * keys.shape[0] * columns,
             bytes_accessed=4 * keys.shape[0] * columns,
-            transcendentals=n * rows * keys.shape[0] * heads,
+            transcendentals=m * rows * keys.shape[0] * heads,
         ),
         name="attend",
-    )(bias, *blocks, keys, values)
-
-
-def load(cached, fresh, after):
+    )(bias, *planes, keys, values)
+
+
+def load(cached, fresh, victims, queries, after):
     cache_rows, columns = cached[0].shape
     tok = fresh[0].shape[0]
     padded = cache_rows + -(-tok // BLK) * BLK
     n = len(cached)
 
     def body(*refs):
-        cached_refs, fresh_refs, outs = refs[:n], refs[n : 2 * n], refs[2 * n + 1 : 3 * n + 1]
-        tails, sems = refs[3 * n + 1 : 4 * n + 1], refs[4 * n + 1]
+        cached_refs, fresh_refs, victims_ref, queries_ref = refs[:n], refs[n : 2 * n], *refs[2 * n : 2 * n + 2]
+        refs = refs[2 * n + 3 :]
+        outs, bias_ref, q_ref, tails, ids_ref, sems = (
+            refs[:n], refs[n], refs[n + 1], refs[n + 2 : 2 * n + 2], *refs[2 * n + 2 :]
+        )
+        ids = pltpu.make_async_copy(victims_ref, ids_ref, sems.at[1, n])
+        rest = pltpu.make_async_copy(queries_ref, q_ref, sems.at[0, n])
         small = [
             pltpu.make_async_copy(src, dst, sems.at[1, i])
             for i, (src, dst) in enumerate(zip(fresh_refs, tails))
@@ -158,30 +169,42 @@
             pltpu.make_async_copy(src, dst.at[pl.ds(0, cache_rows), :], sems.at[0, i])
             for i, (src, dst) in enumerate(zip(cached_refs, outs))
         ]
-        for copy in small + large:
+        for copy in [ids] + small + large + [rest]:
             copy.start()
+        ids.wait()
+        blocks = cache_rows // BLK
+        first = lax.axis_index("seq") * blocks
+        for block in range(blocks):
+            hits = jnp.where(ids_ref[...] == first + block, 1.0, 0.0)
+            hit = jnp.max(hits, axis=1, keepdims=True)
+            gone = jnp.where(hit > 0.0, NEG, 0.0)
+            bias_ref[:, block * BLK : (block + 1) * BLK] = jnp.broadcast_to(gone, (1, BLK))
+        token = lax.broadcasted_iota(jnp.int32, (1, padded - cache_rows), 1)
+        bias_ref[:, cache_rows:] = jnp.where(token < tok, 0.0, NEG)
         for copy, tail, out in zip(small, tails, outs):
             copy.wait()
-            rest = jnp.zeros((padded - cache_rows - tok, columns), F32)
-            rows = jnp.concatenate([tail[...].astype(F32), rest], axis=0)
+            zeros = jnp.zeros((padded - cache_rows - tok, columns), F32)
+            rows = jnp.concatenate([tail[...].astype(F32), zeros], axis=0)
             out[cache_rows:, :] = rows.astype(out.dtype)
-        for copy in large:
+        for copy in large + [rest]:
             copy.wait()
 
     in_hbm = pl.BlockSpec(memory_space=pltpu.HBM)
+    held = (*cached, *fresh, victims, queries)
     return pl.pallas_call(
         body,
-        in_specs=[in_hbm] * (2 * n) + [pl.BlockSpec(memory_space=pl.ANY)],
-        out_specs=[pl.BlockSpec(memory_space=pltpu.VMEM)] * n,
-        out_shape=[jax.ShapeDtypeStruct((padded, columns), BF16)] * n,
+        in_specs=[in_hbm] * len(held) + [pl.BlockSpec(memory_space=pl.ANY)],
+        out_specs=[pl.BlockSpec(memory_space=pltpu.VMEM)] * (n + 2),
+        out_shape=[jax.ShapeDtypeStruct((padded, columns), BF16)] * n
+        + [jax.ShapeDtypeStruct((1, padded), F32), jax.ShapeDtypeStruct(queries.shape, BF16)],
         scratch_shapes=[pltpu.VMEM(x.shape, BF16) for x in fresh]
-        + [pltpu.SemaphoreType.DMA((2, n))],
+        + [pltpu.VMEM(victims.shape, jnp.int32), pltpu.SemaphoreType.DMA((2, n + 1))],
         compiler_params=pltpu.CompilerParams(vmem_limit_bytes=24 * 1024 * 1024),
         cost_estimate=pl.CostEstimate(
             flops=0, bytes_accessed=4 * n * cache_rows * columns, transcendentals=0
         ),
         name="load",
-    )(*[pltpu.with_memory_space_constraint(x, pltpu.HBM) for x in (*cached, *fresh)], after)
+    )(*[pltpu.with_memory_space_constraint(x, pltpu.HBM) for x in held], after)
 
 
 def merged(arrays, heads, last):
@@ -261,45 +284,37 @@
     shape = factors(members)
     a_n, b_n, c_n = shape
     heads = queries.shape[1] // HD
-    block_count = cache_keys.shape[0] // BLK
-    block_ids = lax.axis_index("seq") * block_count + jnp.arange(block_count, dtype=jnp.int32)
-    evicted = jnp.any(victims[:, None] == block_ids[None, :], axis=0)
-    bias = jnp.repeat(jnp.where(evicted, NEG, 0.0), BLK)[None, :]
-    tok = new_keys.shape[0]
-    fresh_bias = jnp.where(jnp.arange(-(-tok // BLK) * BLK) < tok, 0.0, NEG)[None, :]
-    bias = jnp.concatenate([bias, fresh_bias], axis=1)
-
-    def fetch(x, by):
-        return lax.ppermute(x, "seq", shift_perm(shape, by))
-
-    def give(x, by):
-        return lax.ppermute(x, "seq", shift_perm(shape, [-d for d in by]))
-
-    far_first = sorted(range(1, a_n), key=lambda d: -min(d, a_n - d))
+
+    def fetch(x, *by):
+        return lax.ppermute(x, "seq", partner_perm(shape, by, False))
+
+    def give(x, *by):
+        return lax.ppermute(x, "seq", partner_perm(shape, by, True))
+
+    far_first = range(a_n - 1, 0, -1)
     line = [queries] + [None] * (a_n - 1)
-    for d in far_first:
-        line[d] = fetch(queries, (d, 0, 0))
-    lines = [line] + [[fetch(x, (0, d, 0)) for x in line] for d in range(1, b_n)]
-    last = line[far_first[-1]] if far_first else queries
-    keys, values = load((cache_keys, cache_values), (new_keys, new_values), last)
-
-    home = [join([join([queries])] + line[1:])] + [join(x, (keys,)) for x in lines[1:]]
-    away = [[fetch(x, (0, 0, c)) for x in home] for c in range(1, c_n)]
-    blocks = home + [x for core in away for x in core]
+    for a in far_first:
+        line[a] = fetch(queries, a, 0, 0)
+    lines = [line] + [[fetch(x, 0, b, 0) for x in line] for b in range(1, b_n)]
+    keys, values, bias, line[0] = load(
+        (cache_keys, cache_values), (new_keys, new_values), victims[None], queries, line[-1]
+    )
+    plane = join([x for pieces in lines for x in pieces])
+    planes = [plane] + [fetch(plane, 0, 0, c) for c in range(1, c_n)]
     kinds = [F32] * b_n + [BF16] * (b_n * (c_n - 1))
-    blocks = attend(blocks, kinds, keys, values, bias)
-    home, away = blocks[:b_n], blocks[b_n:]
+    sums = attend(planes, b_n, kinds, keys, values, bias)
 
     def over_cores(b, kind):
-        got = [give(away[c * b_n + b], (0, 0, c + 1)) for c in range(c_n - 1)]
-        return merge_rows([home[b]] + got, heads, a_n, [kind] * a_n)
-
-    got = [[give(x, (0, d, 0)) for x in over_cores(d, BF16)] for d in range(1, b_n)]
+        got = [give(sums[c * b_n + b], 0, 0, c) for c in range(1, c_n)]
+        return merge_rows([sums[b]] + got, heads, a_n, [kind] * a_n)
+
+    got = [[give(x, 0, b, 0) for x in over_cores(b, BF16)] for b in range(1, b_n)]
     own = over_cores(0, F32)
-    sums = [[own[d]] + [pieces[d] for pieces in got] for d in range(a_n)]
-    for d in far_first:
-        sums[d] = [give(merge_rows(sums[d], heads, 1, [BF16])[0], (d, 0, 0))]
-    return finish([x for pieces in sums for x in pieces], heads)
+    total = [[own[a]] + [pieces[a] for pieces in got] for a in range(a_n)]
+    last = [
+        give(merge_rows(total[a], heads, 1, [BF16])[0], a, 0, 0) for a in far_first
+    ]
+    return finish([*merge_rows(total[0], heads, 1, [F32]), *last], heads)
 
 
 def solution(mesh):

time: 37.6 us -> 36.1 us (0.960)
  starting transfers between devices: 18.2 us -> 20 us
  waiting for transfers between devices: 8.44 us -> 6.78 us
  other arithmetic: 0.86 us -> 0 us
  local copies, waits for them, and re-layouts: 0.85 us -> 0 us
    ppermute x18 -> x17, starting transfers between devices: 18.2 us -> 20 us  [the longest x8 10.7 us: fetch(): return lax.ppermute(x, 'seq', partner_perm(shape, by, False))]
    ppermute x18 -> x17, waiting for transfers between devices: 8.44 us -> 6.78 us  [the longest x8 3.55 us: fetch(): return lax.ppermute(x, 'seq', partner_perm(shape, by, False))]
    reduce_or x1 -> x0, other arithmetic: 0.84 us -> none  [per_device(): evicted = jnp.any(victims[:, None] == block_ids[None, :], axis=0)]
    unnamed x2 -> x0, local copies, waits for them, and re-layouts: 0.78 us -> none
    pallas_call x9 -> x8, Pallas kernels: 1.95 us -> 2.07 us  [call_merge(): pl.pallas_call(body, in_specs=[pl.BlockSpec(memory_space=pltpu.VMEM)] * l...]
  transfers between devices with their start and end apart: 18 -> 17, of which waited for: 9 -> 5; matrix products, arithmetic and copies ran while one was open for 2% -> 0% of each run, Pallas kernels for 10% -> 11%
where the time goes in v6:
time: 36.1 us; the launch traced here: 35.9 us
  starting transfers between devices  20 us (55%)
  Pallas kernels  9.04 us (25%)
  waiting for transfers between devices  6.78 us (19%)
    ppermute x8, starting transfers between devices, fetch(): return lax.ppermute(x, 'seq', partner_perm(shape, by, False))  10.7 us
    ppermute x9, starting transfers between devices, give(): return lax.ppermute(x, 'seq', partner_perm(shape, by, True))  9.28 us
    pallas_call x1, Pallas kernels, attend(): pl.pallas_call(body, in_specs=[pl.BlockSpec(memory_space=pltpu.VMEM)] * (...  4.33 us
    ppermute x8, waiting for transfers between devices, fetch(): return lax.ppermute(x, 'seq', partner_perm(shape, by, False))  3.55 us
    ppermute x9, waiting for transfers between devices, give(): return lax.ppermute(x, 'seq', partner_perm(shape, by, True))  3.23 us
    pallas_call x1, Pallas kernels, load(): pl.pallas_call(body, in_specs=[in_hbm] * len(held) + [pl.BlockSpec(memory...  2.65 us
    pallas_call x8, Pallas kernels, call_merge(): pl.pallas_call(body, in_specs=[pl.BlockSpec(memory_space=pltpu.VMEM)] * l...  2.07 us
  transfers between devices with their start and end apart: 17, of which 5 were waited for; matrix products, arithmetic and copies ran while one was open for 0% of the time, Pallas kernels for 11%

profile of v6, /device:TPU:0, one launch (start us, length us, event | category | flops | bytes accessed | tf_op | source)
XLA Modules:
  0.0 35.9 jit_solution(13902951299113096892)
XLA Ops:
  0.0 3.0 %collective-permute-start.1 = (bf16[8,2560]{1,0:T(8,128)(2,1)}, bf16[8,2560]{1,0:T(8,128)(2,1)S(1)}, u32[]{:S(2)}, u32[]{:S(2)}) collective-permute-start(bf16[8,2560]{1,0:T(8,128)(2,1)} %refs_5_.1), channel_id=1, source_target_pairs={{4,0},{5,1},{6,2},{7,3},{0,4},{1,5},{2,6},{3,7},{12,8},{13,9},{14,... | collective-permute-start | bytes 122888 | tf_op jit(solution)/shard_map/ppermute | solution.py:289
  3.0 2.5 %collective-permute-start = (bf16[8,2560]{1,0:T(8,128)(2,1)}, bf16[8,2560]{1,0:T(8,128)(2,1)S(1)}, u32[]{:S(2)}, u32[]{:S(2)}) collective-permute-start(bf16[8,2560]{1,0:T(8,128)(2,1)} %refs_5_.1), channel_id=1, source_target_pairs={{12,0},{13,1},{14,2},{15,3},{8,4},{9,5},{10,6},{11,7},{4,8},{5,9},... | collective-permute-start | bytes 122888 | tf_op jit(solution)/shard_map/ppermute | solution.py:289
  5.5 0.1 collective-permute-start.2
  5.6 1.5 %collective-permute-start.3 = (bf16[8,2560]{1,0:T(8,128)(2,1)}, bf16[8,2560]{1,0:T(8,128)(2,1)S(1)}, u32[]{:S(2)}, u32[]{:S(2)}) collective-permute-start(bf16[8,2560]{1,0:T(8,128)(2,1)} %refs_5_.1), channel_id=1, source_target_pairs={{2,0},{3,1},{0,2},{1,3},{6,4},{7,5},{4,6},{5,7},{10,8},{11,9},{8,1... | collective-permute-start | bytes 122888 | tf_op jit(solution)/shard_map/ppermute | solution.py:289
  7.1 0.0 collective-permute-done.1.refs_1_
  7.1 0.5 %collective-permute-start.4 = (bf16[8,2560]{1,0:T(8,128)(2,1)S(1)}, bf16[8,2560]{1,0:T(8,128)(2,1)S(1)}, u32[]{:S(2)}, u32[]{:S(2)}) collective-permute-start(bf16[8,2560]{1,0:T(8,128)(2,1)S(1)} %collective-permute-done.1.refs_1_), channel_id=1, source_target_pairs={{2,0},{3,1},{0,2},{1,3},{6,4},{7,5},{4,6},{5,7},{10,8},{11,9},{8,1... | collective-permute-start | bytes 122888 | tf_op jit(solution)/shard_map/ppermute | solution.py:289
  7.6 1.9 %collective-permute-done.refs_6_.refs_3_ = bf16[8,2560]{1,0:T(8,128)(2,1)S(1)} collective-permute-done((bf16[8,2560]{1,0:T(8,128)(2,1)}, bf16[8,2560]{1,0:T(8,128)(2,1)S(1)}, u32[]{:S(2)}, u32[]{:S(2)}) %collective-permute-start) | collective-permute-done | bytes 40992 | tf_op jit(solution)/shard_map/ppermute | solution.py:289
  9.6 1.5 %collective-permute-start.6 = (bf16[8,2560]{1,0:T(8,128)(2,1)S(1)}, bf16[8,2560]{1,0:T(8,128)(2,1)S(1)}, u32[]{:S(2)}, u32[]{:S(2)}) collective-permute-start(bf16[8,2560]{1,0:T(8,128)(2,1)S(1)} %collective-permute-done.refs_6_.refs_3_), channel_id=1, source_target_pairs={{2,0},{3,1},{0,2},{1,3},{6,4},{7,5},{4,6},{5,7},{10,8},{11,9},{8,1... | collective-permute-start | bytes 122888 | tf_op jit(solution)/shard_map/ppermute | solution.py:289
  11.1 1.5 %collective-permute-start.5 = (bf16[8,2560]{1,0:T(8,128)(2,1)S(1)}, bf16[8,2560]{1,0:T(8,128)(2,1)S(1)}, u32[]{:S(2)}, u32[]{:S(2)}) collective-permute-start(bf16[8,2560]{1,0:T(8,128)(2,1)S(1)} %collective-permute-done.2.refs_2_), channel_id=1, source_target_pairs={{2,0},{3,1},{0,2},{1,3},{6,4},{7,5},{4,6},{5,7},{10,8},{11,9},{8,1... | collective-permute-start | bytes 122888 | tf_op jit(solution)/shard_map/ppermute | solution.py:289
  12.6 2.6 %load.1 = (bf16[640,2560]{1,0:T(8,128)(2,1)S(1)}, bf16[640,2560]{1,0:T(8,128)(2,1)S(1)}, f32[1,640]{1,0:T(1,128)S(1)}, bf16[8,2560]{1,0:T(8,128)(2,1)S(1)}) custom-call(bf16[512,2560]{1,0:T(8,128)(2,1)} %refs_0_.1, bf16[512,2560]{1,0:T(8,128)(2,1)} %refs_1_.1, bf16[8,2560]{1,0:T(8,128)(2,1)} %refs_2_.1, bf16[8,2560]{1,0:T(8,128)(2,1)} %refs_3_.1, ...), custom_call_target="tpu_custom_call" | custom-call | bytes 10485760 | tf_op jit(solution)/shard_map/load/pallas_call | solution.py:194
  15.3 0.1 collective-permute-start.7
  15.4 1.6 %collective-permute-done.7.refs_2_ = bf16[64,2560]{1,0:T(8,128)(2,1)S(1)} collective-permute-done((bf16[64,2560]{1,0:T(8,128)(2,1)S(1)}, bf16[64,2560]{1,0:T(8,128)(2,1)S(1)}, u32[]{:S(2)}, u32[]{:S(2)}) %collective-permute-start.7) | collective-permute-done | bytes 327712 | tf_op jit(solution)/shard_map/ppermute | solution.py:289
  17.0 4.3 %attend.1 = (f32[32,2688]{1,0:T(8,128)S(1)}, f32[32,2688]{1,0:T(8,128)S(1)}, bf16[32,2688]{1,0:T(8,128)(2,1)S(1)}, bf16[32,2688]{1,0:T(8,128)(2,1)S(1)}) custom-call(f32[1,640]{1,0:T(1,128)S(1)} %get-tuple-element.21.refs_0_, bf16[64,2560]{1,0:T(8,128)(2,1)S(1)} %merge.8.refs_1_, bf16[64,2560]{1,0:T(8,128)(2,1)S(1)} %collective-permute-done.7.refs_2_, ...), custom_call_target="tpu_custom_call" | custom-call | flops 838860800 | bytes 6553600 | tf_op jit(solution)/shard_map/attend/pallas_call | solution.py:134
  21.3 0.2 collective-permute-start.9
  21.5 0.4 %collective-permute-start.8 = (bf16[32,2688]{1,0:T(8,128)(2,1)S(1)}, bf16[32,2688]{1,0:T(8,128)(2,1)S(1)}, u32[]{:S(2)}, u32[]{:S(2)}) collective-permute-start(bf16[32,2688]{1,0:T(8,128)(2,1)S(1)} %get-tuple-element.26), channel_id=1, source_target_pairs={{0,1},{1,0},{2,3},{3,2},{4,5},{5,4},{6,7},{7,6},{8,9},{9,8},{10,11... | collective-permute-start | bytes 516104 | tf_op jit(solution)/shard_map/ppermute | solution.py:292
  21.9 0.9 %collective-permute-done.9.refs_1_ = bf16[32,2688]{1,0:T(8,128)(2,1)S(1)} collective-permute-done((bf16[32,2688]{1,0:T(8,128)(2,1)S(1)}, bf16[32,2688]{1,0:T(8,128)(2,1)S(1)}, u32[]{:S(2)}, u32[]{:S(2)}) %collective-permute-start.9) | collective-permute-done | bytes 172064 | tf_op jit(solution)/shard_map/ppermute | solution.py:292
  22.8 0.3 merge.10
  23.1 1.4 %collective-permute-start.11 = (bf16[8,2688]{1,0:T(8,128)(2,1)S(1)}, bf16[8,2688]{1,0:T(8,128)(2,1)S(1)}, u32[]{:S(2)}, u32[]{:S(2)}) collective-permute-start(bf16[8,2688]{1,0:T(8,128)(2,1)S(1)} %get-tuple-element.32), channel_id=1, source_target_pairs={{0,2},{1,3},{2,0},{3,1},{4,6},{5,7},{6,4},{7,5},{8,10},{9,11},{10,... | collective-permute-start | bytes 129032 | tf_op jit(solution)/shard_map/ppermute | solution.py:292
  24.5 0.7 %collective-permute-start.13 = (bf16[8,2688]{1,0:T(8,128)(2,1)S(1)}, bf16[8,2688]{1,0:T(8,128)(2,1)S(1)}, u32[]{:S(2)}, u32[]{:S(2)}) collective-permute-start(bf16[8,2688]{1,0:T(8,128)(2,1)S(1)} %get-tuple-element.34), channel_id=1, source_target_pairs={{0,2},{1,3},{2,0},{3,1},{4,6},{5,7},{6,4},{7,5},{8,10},{9,11},{10,... | collective-permute-start | bytes 129032 | tf_op jit(solution)/shard_map/ppermute | solution.py:292
  25.2 1.3 %collective-permute-start.15 = (bf16[8,2688]{1,0:T(8,128)(2,1)S(1)}, bf16[8,2688]{1,0:T(8,128)(2,1)S(1)}, u32[]{:S(2)}, u32[]{:S(2)}) collective-permute-start(bf16[8,2688]{1,0:T(8,128)(2,1)S(1)} %get-tuple-element.36), channel_id=1, source_target_pairs={{0,2},{1,3},{2,0},{3,1},{4,6},{5,7},{6,4},{7,5},{8,10},{9,11},{10,... | collective-permute-start | bytes 129032 | tf_op jit(solution)/shard_map/ppermute | solution.py:292
  26.5 0.7 %collective-permute-start.10 = (bf16[8,2688]{1,0:T(8,128)(2,1)S(1)}, bf16[8,2688]{1,0:T(8,128)(2,1)S(1)}, u32[]{:S(2)}, u32[]{:S(2)}) collective-permute-start(bf16[8,2688]{1,0:T(8,128)(2,1)S(1)} %get-tuple-element.30), channel_id=1, source_target_pairs={{0,2},{1,3},{2,0},{3,1},{4,6},{5,7},{6,4},{7,5},{8,10},{9,11},{10,... | collective-permute-start | bytes 129032 | tf_op jit(solution)/shard_map/ppermute | solution.py:292
  27.2 0.3 merge.9
  27.5 0.1 merge.12
  27.7 2.0 %collective-permute-start.12 = (bf16[8,2688]{1,0:T(8,128)(2,1)S(1)}, bf16[8,2688]{1,0:T(8,128)(2,1)S(1)}, u32[]{:S(2)}, u32[]{:S(2)}) collective-permute-start(bf16[8,2688]{1,0:T(8,128)(2,1)S(1)} %merge.12), channel_id=1, source_target_pairs={{0,12},{1,13},{2,14},{3,15},{4,8},{5,9},{6,10},{7,11},{8,4},{9,5},... | collective-permute-start | bytes 129032 | tf_op jit(solution)/shard_map/ppermute | solution.py:292
  29.7 0.1 merge.13
  29.9 0.4 %collective-permute-start.14 = (bf16[8,2688]{1,0:T(8,128)(2,1)S(1)}, bf16[8,2688]{1,0:T(8,128)(2,1)S(1)}, u32[]{:S(2)}, u32[]{:S(2)}) collective-permute-start(bf16[8,2688]{1,0:T(8,128)(2,1)S(1)} %merge.13), channel_id=1, source_target_pairs={{0,8},{1,9},{2,10},{3,11},{4,12},{5,13},{6,14},{7,15},{8,0},{9,1},... | collective-permute-start | bytes 129032 | tf_op jit(solution)/shard_map/ppermute | solution.py:292
  30.2 0.1 merge.14
  30.4 2.2 %collective-permute-start.16 = (bf16[8,2688]{1,0:T(8,128)(2,1)S(1)}, bf16[8,2688]{1,0:T(8,128)(2,1)S(1)}, u32[]{:S(2)}, u32[]{:S(2)}) collective-permute-start(bf16[8,2688]{1,0:T(8,128)(2,1)S(1)} %merge.14), channel_id=1, source_target_pairs={{0,4},{1,5},{2,6},{3,7},{4,0},{5,1},{6,2},{7,3},{8,12},{9,13},{10,... | collective-permute-start | bytes 129032 | tf_op jit(solution)/shard_map/ppermute | solution.py:292
  32.6 0.1 merge.11.refs_0_
  32.7 1.0 %collective-permute-done.12.refs_1_ = bf16[8,2688]{1,0:T(8,128)(2,1)S(1)} collective-permute-done((bf16[8,2688]{1,0:T(8,128)(2,1)S(1)}, bf16[8,2688]{1,0:T(8,128)(2,1)S(1)}, u32[]{:S(2)}, u32[]{:S(2)}) %collective-permute-start.12) | collective-permute-done | bytes 43040 | tf_op jit(solution)/shard_map/ppermute | solution.py:292
  33.8 1.3 %collective-permute-done.14.refs_2_ = bf16[8,2688]{1,0:T(8,128)(2,1)S(1)} collective-permute-done((bf16[8,2688]{1,0:T(8,128)(2,1)S(1)}, bf16[8,2688]{1,0:T(8,128)(2,1)S(1)}, u32[]{:S(2)}, u32[]{:S(2)}) %collective-permute-start.14) | collective-permute-done | bytes 43040 | tf_op jit(solution)/shard_map/ppermute | solution.py:292
  35.0 0.9 %merge.15 = bf16[8,2560]{1,0:T(8,128)(2,1)} custom-call(f32[8,2688]{1,0:T(8,128)S(1)} %merge.11.refs_0_, bf16[8,2688]{1,0:T(8,128)(2,1)S(1)} %collective-permute-done.12.refs_1_, bf16[8,2688]{1,0:T(8,128)(2,1)S(1)} %collective-permute-done.14.refs_2_, bf16[8,2688]{1,0:T(8,128)(2,1)S(1)} %collective-permute-done.16.refs_3_), custom_call_target="tpu_custom_call" | custom-call | flops 344064 | bytes 344064 | tf_op jit(solution)/shard_map/merge/pallas_call | solution.py:270
  (12 shorter events, 0.1 us)
Async XLA Ops:
  0.0 7.1 %collective-permute-start.1 = (bf16[8,2560]{1,0:T(8,128)(2,1)}, bf16[8,2560]{1,0:T(8,128)(2,1)S(1)}, u32[]{:S(2)}, u32[]{:S(2)}) collective-permute-start(bf16[8,2560]{1,0:T(8,128)(2,1)} %refs_5_.1), channel_id=1, source_target_pairs={{4,0},{5,1},{6,2},{7,3},{0,4},{1,5},{2,6},{3,7},{12,8},{13,9},{14,... | collective-permute-start | bytes 122888 | tf_op jit(solution)/shard_map/ppermute | solution.py:289
  3.0 6.5 %collective-permute-start = (bf16[8,2560]{1,0:T(8,128)(2,1)}, bf16[8,2560]{1,0:T(8,128)(2,1)S(1)}, u32[]{:S(2)}, u32[]{:S(2)}) collective-permute-start(bf16[8,2560]{1,0:T(8,128)(2,1)} %refs_5_.1), channel_id=1, source_target_pairs={{12,0},{13,1},{14,2},{15,3},{8,4},{9,5},{10,6},{11,7},{4,8},{5,9},... | collective-permute-start | bytes 122888 | tf_op jit(solution)/shard_map/ppermute | solution.py:289
  5.5 5.6 %collective-permute-start.2 = (bf16[8,2560]{1,0:T(8,128)(2,1)}, bf16[8,2560]{1,0:T(8,128)(2,1)S(1)}, u32[]{:S(2)}, u32[]{:S(2)}) collective-permute-start(bf16[8,2560]{1,0:T(8,128)(2,1)} %refs_5_.1), channel_id=1, source_target_pairs={{8,0},{9,1},{10,2},{11,3},{12,4},{13,5},{14,6},{15,7},{0,8},{1,9},... | collective-permute-start | bytes 122888 | tf_op jit(solution)/shard_map/ppermute | solution.py:289
  5.6 9.6 %collective-permute-start.3 = (bf16[8,2560]{1,0:T(8,128)(2,1)}, bf16[8,2560]{1,0:T(8,128)(2,1)S(1)}, u32[]{:S(2)}, u32[]{:S(2)}) collective-permute-start(bf16[8,2560]{1,0:T(8,128)(2,1)} %refs_5_.1), channel_id=1, source_target_pairs={{2,0},{3,1},{0,2},{1,3},{6,4},{7,5},{4,6},{5,7},{10,8},{11,9},{8,1... | collective-permute-start | bytes 122888 | tf_op jit(solution)/shard_map/ppermute | solution.py:289
  7.1 8.1 %collective-permute-start.4 = (bf16[8,2560]{1,0:T(8,128)(2,1)S(1)}, bf16[8,2560]{1,0:T(8,128)(2,1)S(1)}, u32[]{:S(2)}, u32[]{:S(2)}) collective-permute-start(bf16[8,2560]{1,0:T(8,128)(2,1)S(1)} %collective-permute-done.1.refs_1_), channel_id=1, source_target_pairs={{2,0},{3,1},{0,2},{1,3},{6,4},{7,5},{4,6},{5,7},{10,8},{11,9},{8,1... | collective-permute-start | bytes 122888 | tf_op jit(solution)/shard_map/ppermute | solution.py:289
  9.6 5.7 %collective-permute-start.6 = (bf16[8,2560]{1,0:T(8,128)(2,1)S(1)}, bf16[8,2560]{1,0:T(8,128)(2,1)S(1)}, u32[]{:S(2)}, u32[]{:S(2)}) collective-permute-start(bf16[8,2560]{1,0:T(8,128)(2,1)S(1)} %collective-permute-done.refs_6_.refs_3_), channel_id=1, source_target_pairs={{2,0},{3,1},{0,2},{1,3},{6,4},{7,5},{4,6},{5,7},{10,8},{11,9},{8,1... | collective-permute-start | bytes 122888 | tf_op jit(solution)/shard_map/ppermute | solution.py:289
  11.1 4.2 %collective-permute-start.5 = (bf16[8,2560]{1,0:T(8,128)(2,1)S(1)}, bf16[8,2560]{1,0:T(8,128)(2,1)S(1)}, u32[]{:S(2)}, u32[]{:S(2)}) collective-permute-start(bf16[8,2560]{1,0:T(8,128)(2,1)S(1)} %collective-permute-done.2.refs_2_), channel_id=1, source_target_pairs={{2,0},{3,1},{0,2},{1,3},{6,4},{7,5},{4,6},{5,7},{10,8},{11,9},{8,1... | collective-permute-start | bytes 122888 | tf_op jit(solution)/shard_map/ppermute | solution.py:289
  15.3 1.7 %collective-permute-start.7 = (bf16[64,2560]{1,0:T(8,128)(2,1)S(1)}, bf16[64,2560]{1,0:T(8,128)(2,1)S(1)}, u32[]{:S(2)}, u32[]{:S(2)}) collective-permute-start(bf16[64,2560]{1,0:T(8,128)(2,1)S(1)} %merge.8.refs_1_), channel_id=1, source_target_pairs={{1,0},{0,1},{3,2},{2,3},{5,4},{4,5},{7,6},{6,7},{9,8},{8,9},{11,10... | collective-permute-start | bytes 983048 | tf_op jit(solution)/shard_map/ppermute | solution.py:289
  21.3 1.5 %collective-permute-start.9 = (bf16[32,2688]{1,0:T(8,128)(2,1)S(1)}, bf16[32,2688]{1,0:T(8,128)(2,1)S(1)}, u32[]{:S(2)}, u32[]{:S(2)}) collective-permute-start(bf16[32,2688]{1,0:T(8,128)(2,1)S(1)} %get-tuple-element.29), channel_id=1, source_target_pairs={{0,1},{1,0},{2,3},{3,2},{4,5},{5,4},{6,7},{7,6},{8,9},{9,8},{10,11... | collective-permute-start | bytes 516104 | tf_op jit(solution)/shard_map/ppermute | solution.py:292
  21.5 5.7 %collective-permute-start.8 = (bf16[32,2688]{1,0:T(8,128)(2,1)S(1)}, bf16[32,2688]{1,0:T(8,128)(2,1)S(1)}, u32[]{:S(2)}, u32[]{:S(2)}) collective-permute-start(bf16[32,2688]{1,0:T(8,128)(2,1)S(1)} %get-tuple-element.26), channel_id=1, source_target_pairs={{0,1},{1,0},{2,3},{3,2},{4,5},{5,4},{6,7},{7,6},{8,9},{9,8},{10,11... | collective-permute-start | bytes 516104 | tf_op jit(solution)/shard_map/ppermute | solution.py:292
  23.1 4.4 %collective-permute-start.11 = (bf16[8,2688]{1,0:T(8,128)(2,1)S(1)}, bf16[8,2688]{1,0:T(8,128)(2,1)S(1)}, u32[]{:S(2)}, u32[]{:S(2)}) collective-permute-start(bf16[8,2688]{1,0:T(8,128)(2,1)S(1)} %get-tuple-element.32), channel_id=1, source_target_pairs={{0,2},{1,3},{2,0},{3,1},{4,6},{5,7},{6,4},{7,5},{8,10},{9,11},{10,... | collective-permute-start | bytes 129032 | tf_op jit(solution)/shard_map/ppermute | solution.py:292
  24.5 5.3 %collective-permute-start.13 = (bf16[8,2688]{1,0:T(8,128)(2,1)S(1)}, bf16[8,2688]{1,0:T(8,128)(2,1)S(1)}, u32[]{:S(2)}, u32[]{:S(2)}) collective-permute-start(bf16[8,2688]{1,0:T(8,128)(2,1)S(1)} %get-tuple-element.34), channel_id=1, source_target_pairs={{0,2},{1,3},{2,0},{3,1},{4,6},{5,7},{6,4},{7,5},{8,10},{9,11},{10,... | collective-permute-start | bytes 129032 | tf_op jit(solution)/shard_map/ppermute | solution.py:292
  25.2 5.0 %collective-permute-start.15 = (bf16[8,2688]{1,0:T(8,128)(2,1)S(1)}, bf16[8,2688]{1,0:T(8,128)(2,1)S(1)}, u32[]{:S(2)}, u32[]{:S(2)}) collective-permute-start(bf16[8,2688]{1,0:T(8,128)(2,1)S(1)} %get-tuple-element.36), channel_id=1, source_target_pairs={{0,2},{1,3},{2,0},{3,1},{4,6},{5,7},{6,4},{7,5},{8,10},{9,11},{10,... | collective-permute-start | bytes 129032 | tf_op jit(solution)/shard_map/ppermute | solution.py:292
  26.5 6.1 %collective-permute-start.10 = (bf16[8,2688]{1,0:T(8,128)(2,1)S(1)}, bf16[8,2688]{1,0:T(8,128)(2,1)S(1)}, u32[]{:S(2)}, u32[]{:S(2)}) collective-permute-start(bf16[8,2688]{1,0:T(8,128)(2,1)S(1)} %get-tuple-element.30), channel_id=1, source_target_pairs={{0,2},{1,3},{2,0},{3,1},{4,6},{5,7},{6,4},{7,5},{8,10},{9,11},{10,... | collective-permute-start | bytes 129032 | tf_op jit(solution)/shard_map/ppermute | solution.py:292
  27.7 6.1 %collective-permute-start.12 = (bf16[8,2688]{1,0:T(8,128)(2,1)S(1)}, bf16[8,2688]{1,0:T(8,128)(2,1)S(1)}, u32[]{:S(2)}, u32[]{:S(2)}) collective-permute-start(bf16[8,2688]{1,0:T(8,128)(2,1)S(1)} %merge.12), channel_id=1, source_target_pairs={{0,12},{1,13},{2,14},{3,15},{4,8},{5,9},{6,10},{7,11},{8,4},{9,5},... | collective-permute-start | bytes 129032 | tf_op jit(solution)/shard_map/ppermute | solution.py:292
  29.9 5.2 %collective-permute-start.14 = (bf16[8,2688]{1,0:T(8,128)(2,1)S(1)}, bf16[8,2688]{1,0:T(8,128)(2,1)S(1)}, u32[]{:S(2)}, u32[]{:S(2)}) collective-permute-start(bf16[8,2688]{1,0:T(8,128)(2,1)S(1)} %merge.13), channel_id=1, source_target_pairs={{0,8},{1,9},{2,10},{3,11},{4,12},{5,13},{6,14},{7,15},{8,0},{9,1},... | collective-permute-start | bytes 129032 | tf_op jit(solution)/shard_map/ppermute | solution.py:292
  30.4 4.6 %collective-permute-start.16 = (bf16[8,2688]{1,0:T(8,128)(2,1)S(1)}, bf16[8,2688]{1,0:T(8,128)(2,1)S(1)}, u32[]{:S(2)}, u32[]{:S(2)}) collective-permute-start(bf16[8,2688]{1,0:T(8,128)(2,1)S(1)} %merge.14), channel_id=1, source_target_pairs={{0,4},{1,5},{2,6},{3,7},{4,0},{5,1},{6,2},{7,3},{8,12},{9,13},{10,... | collective-permute-start | bytes 129032 | tf_op jit(solution)/shard_map/ppermute | solution.py:292

commit v7 on v6

--- a/solution.py
+++ b/solution.py
@@ -147,32 +147,32 @@
     )(bias, *planes, keys, values)
 
 
-def load(cached, fresh, victims, queries, after):
+def load(cached, fresh, victims, after):
     cache_rows, columns = cached[0].shape
     tok = fresh[0].shape[0]
     padded = cache_rows + -(-tok // BLK) * BLK
+    blocks = cache_rows // BLK
     n = len(cached)
 
     def body(*refs):
-        cached_refs, fresh_refs, victims_ref, queries_ref = refs[:n], refs[n : 2 * n], *refs[2 * n : 2 * n + 2]
-        refs = refs[2 * n + 3 :]
-        outs, bias_ref, q_ref, tails, ids_ref, sems = (
-            refs[:n], refs[n], refs[n + 1], refs[n + 2 : 2 * n + 2], *refs[2 * n + 2 :]
-        )
-        ids = pltpu.make_async_copy(victims_ref, ids_ref, sems.at[1, n])
-        rest = pltpu.make_async_copy(queries_ref, q_ref, sems.at[0, n])
+        cached_refs, fresh_refs, victims_ref = refs[:n], refs[n : 2 * n], refs[2 * n]
+        refs = refs[2 * n + 2 :]
+        outs, bias_ref, tails, ids_ref, sems = refs[:n], refs[n], refs[n + 1 : 2 * n + 1], *refs[2 * n + 1 :]
+        ids = pltpu.make_async_copy(victims_ref, ids_ref, sems.at[n, 0])
         small = [
-            pltpu.make_async_copy(src, dst, sems.at[1, i])
+            pltpu.make_async_copy(src, dst, sems.at[i, blocks])
             for i, (src, dst) in enumerate(zip(fresh_refs, tails))
         ]
         large = [
-            pltpu.make_async_copy(src, dst.at[pl.ds(0, cache_rows), :], sems.at[0, i])
+            pltpu.make_async_copy(
+                src.at[pl.ds(j * BLK, BLK), :], dst.at[pl.ds(j * BLK, BLK), :], sems.at[i, j]
+            )
             for i, (src, dst) in enumerate(zip(cached_refs, outs))
+            for j in range(blocks)
         ]
-        for copy in [ids] + small + large + [rest]:
+        for copy in [ids] + small + large:
             copy.start()
         ids.wait()
-        blocks = cache_rows // BLK
         first = lax.axis_index("seq") * blocks
         for block in range(blocks):
             hits = jnp.where(ids_ref[...] == first + block, 1.0, 0.0)
@@ -186,19 +186,19 @@
             zeros = jnp.zeros((padded - cache_rows - tok, columns), F32)
             rows = jnp.concatenate([tail[...].astype(F32), zeros], axis=0)
             out[cache_rows:, :] = rows.astype(out.dtype)
-        for copy in large + [rest]:
+        for copy in large:
             copy.wait()
 
     in_hbm = pl.BlockSpec(memory_space=pltpu.HBM)
-    held = (*cached, *fresh, victims, queries)
+    held = (*cached, *fresh, victims)
     return pl.pallas_call(
         body,
         in_specs=[in_hbm] * len(held) + [pl.BlockSpec(memory_space=pl.ANY)],
-        out_specs=[pl.BlockSpec(memory_space=pltpu.VMEM)] * (n + 2),
+        out_specs=[pl.BlockSpec(memory_space=pltpu.VMEM)] * (n + 1),
         out_shape=[jax.ShapeDtypeStruct((padded, columns), BF16)] * n
-        + [jax.ShapeDtypeStruct((1, padded), F32), jax.ShapeDtypeStruct(queries.shape, BF16)],
+        + [jax.ShapeDtypeStruct((1, padded), F32)],
         scratch_shapes=[pltpu.VMEM(x.shape, BF16) for x in fresh]
-        + [pltpu.VMEM(victims.shape, jnp.int32), pltpu.SemaphoreType.DMA((2, n + 1))],
+        + [pltpu.VMEM(victims.shape, jnp.int32), pltpu.SemaphoreType.DMA((n + 1, blocks + 1))],
         compiler_params=pltpu.CompilerParams(vmem_limit_bytes=24 * 1024 * 1024),
         cost_estimate=pl.CostEstimate(
             flops=0, bytes_accessed=4 * n * cache_rows * columns, transcendentals=0
@@ -229,17 +229,18 @@
     return lambda cols: ref[(*index, slice(None), cols)].astype(F32)
 
 
-def merge_rows(ins, heads, pieces, kinds):
+def merge_rows(ins, heads, pieces, kinds, after=()):
     rows, width = ins[0].shape
     per = rows // pieces
 
     def body(*refs):
-        outs = refs[len(ins) :]
+        outs = refs[len(ins) + len(after) :]
         for cols, total in merged([getter(r) for r in refs[: len(ins)]], heads, False):
             for j, out in enumerate(outs):
                 out[:, cols] = total[j * per : (j + 1) * per].astype(out.dtype)
 
-    return call_merge(body, ins, [jax.ShapeDtypeStruct((per, width), kind) for kind in kinds])
+    shapes = [jax.ShapeDtypeStruct((per, width), kind) for kind in kinds]
+    return call_merge(body, ins, shapes, after)
 
 
 def finish(ins, heads):
@@ -291,30 +292,37 @@
     def give(x, *by):
         return lax.ppermute(x, "seq", partner_perm(shape, by, True))
 
-    far_first = range(a_n - 1, 0, -1)
-    line = [queries] + [None] * (a_n - 1)
-    for a in far_first:
-        line[a] = fetch(queries, a, 0, 0)
-    lines = [line] + [[fetch(x, 0, b, 0) for x in line] for b in range(1, b_n)]
-    keys, values, bias, line[0] = load(
-        (cache_keys, cache_values), (new_keys, new_values), victims[None], queries, line[-1]
-    )
-    plane = join([x for pieces in lines for x in pieces])
+    pieces = [join([queries])] + [fetch(queries, a, 0, 0) for a in range(1, a_n)]
+    runs = [pieces[:2], pieces[2:-1], pieces[-1:]] if a_n > 3 else [pieces]
+    runs = [x[0] if len(x) == 1 else join(x) for x in runs]
+    lines = [runs] + [[fetch(x, 0, b, 0) for x in runs] for b in range(1, b_n)]
+    keys, values, bias = load((cache_keys, cache_values), (new_keys, new_values), victims[None], runs[-1])
+    plane = join([x for pieces in lines for x in pieces], (keys,))
     planes = [plane] + [fetch(plane, 0, 0, c) for c in range(1, c_n)]
     kinds = [F32] * b_n + [BF16] * (b_n * (c_n - 1))
     sums = attend(planes, b_n, kinds, keys, values, bias)
 
+    halves = 2 if a_n % 2 == 0 else 1
+    per = a_n // halves
+
     def over_cores(b, kind):
         got = [give(sums[c * b_n + b], 0, 0, c) for c in range(1, c_n)]
-        return merge_rows([sums[b]] + got, heads, a_n, [kind] * a_n)
-
-    got = [[give(x, 0, b, 0) for x in over_cores(b, BF16)] for b in range(1, b_n)]
+        return merge_rows([sums[b]] + got, heads, halves, [kind] * halves)
+
+    got = [over_cores(b, BF16) for b in range(1, b_n)]
+    got = [[give(x, 0, b, 0) for x in half[::-1]][::-1] for b, half in enumerate(got, 1)]
     own = over_cores(0, F32)
-    total = [[own[a]] + [pieces[a] for pieces in got] for a in range(a_n)]
-    last = [
-        give(merge_rows(total[a], heads, 1, [BF16])[0], a, 0, 0) for a in far_first
+    pieces = []
+    for h in range(halves)[::-1]:
+        kinds = [BF16 if h + j else F32 for j in range(per)]
+        parts = [own[h]] + [half[h] for half in got]
+        pieces = [*merge_rows(parts, heads, per, kinds, pieces[:1]), *pieces]
+    near, far = [
+        [give(pieces[a], a, 0, 0) for a in part] for part in (range(1, per), range(max(per, 1), a_n))
     ]
-    return finish([*merge_rows(total[0], heads, 1, [F32]), *last], heads)
+    if far:
+        pieces[:1] = merge_rows([pieces[0]] + far, heads, 1, [F32])
+    return finish([pieces[0]] + near, heads)
 
 
 def solution(mesh):

time: 36.1 us -> 37.1 us (1.028)
  waiting for transfers between devices: 6.78 us -> 9.59 us
  starting transfers between devices: 20 us -> 17.5 us
  local copies, waits for them, and re-layouts: 0 us -> 0.81 us
    ppermute x9 -> x7, waiting for transfers between devices: 3.23 us -> 6.43 us  [give(): return lax.ppermute(x, 'seq', partner_perm(shape, by, True))]
    ppermute x9 -> x7, starting transfers between devices: 9.28 us -> 7.18 us  [give(): return lax.ppermute(x, 'seq', partner_perm(shape, by, True))]
    unnamed x0 -> x2, local copies, waits for them, and re-layouts: none -> 0.81 us
    ppermute x8 -> x7, starting transfers between devices: 10.7 us -> 10.3 us  [fetch(): return lax.ppermute(x, 'seq', partner_perm(shape, by, False))]
    ppermute x8 -> x7, waiting for transfers between devices: 3.55 us -> 3.17 us  [fetch(): return lax.ppermute(x, 'seq', partner_perm(shape, by, False))]
    pallas_call x8 -> x9, Pallas kernels: 2.07 us -> 2.01 us  [call_merge(): pl.pallas_call(body, in_specs=[pl.BlockSpec(memory_space=pltpu.VMEM)] * l...]
  transfers between devices with their start and end apart: 17 -> 14, of which waited for: 5 -> 6; matrix products, arithmetic and copies ran while one was open for 0% -> 0% of each run, Pallas kernels for 11% -> 10%
where the time goes in v7:
time: 37.1 us; the launch traced here: 37 us
  starting transfers between devices  17.5 us (47%)
  waiting for transfers between devices  9.59 us (26%)
  Pallas kernels  9 us (24%)
  local copies, waits for them, and re-layouts  0.81 us (2%)
    ppermute x7, starting transfers between devices, fetch(): return lax.ppermute(x, 'seq', partner_perm(shape, by, False))  10.3 us
    ppermute x7, starting transfers between devices, give(): return lax.ppermute(x, 'seq', partner_perm(shape, by, True))  7.18 us
    ppermute x7, waiting for transfers between devices, give(): return lax.ppermute(x, 'seq', partner_perm(shape, by, True))  6.43 us
    pallas_call x1, Pallas kernels, attend(): pl.pallas_call(body, in_specs=[pl.BlockSpec(memory_space=pltpu.VMEM)] * (...  4.33 us
    ppermute x7, waiting for transfers between devices, fetch(): return lax.ppermute(x, 'seq', partner_perm(shape, by, False))  3.17 us
    pallas_call x1, Pallas kernels, load(): pl.pallas_call(body, in_specs=[in_hbm] * len(held) + [pl.BlockSpec(memory...  2.66 us
    pallas_call x9, Pallas kernels, call_merge(): pl.pallas_call(body, in_specs=[pl.BlockSpec(memory_space=pltpu.VMEM)] * l...  2.01 us
    unnamed x2, local copies, waits for them, and re-layouts  0.81 us
  transfers between devices with their start and end apart: 14, of which 6 were waited for; matrix products, arithmetic and copies ran while one was open for 0% of the time, Pallas kernels for 10%

profile of v7, /device:TPU:0, one launch (start us, length us, event | category | flops | bytes accessed | tf_op | source)
XLA Modules:
  0.0 37.0 jit_solution(17227572057074563513)
XLA Ops:
  0.0 3.0 %collective-permute-start.1 = (bf16[8,2560]{1,0:T(8,128)(2,1)}, bf16[8,2560]{1,0:T(8,128)(2,1)S(1)}, u32[]{:S(2)}, u32[]{:S(2)}) collective-permute-start(bf16[8,2560]{1,0:T(8,128)(2,1)} %refs_0_.3), channel_id=1, source_target_pairs={{4,0},{5,1},{6,2},{7,3},{0,4},{1,5},{2,6},{3,7},{12,8},{13,9},{14,... | collective-permute-start | bytes 122888 | tf_op jit(solution)/shard_map/ppermute | solution.py:290
  3.0 2.5 %collective-permute-start = (bf16[8,2560]{1,0:T(8,128)(2,1)}, bf16[8,2560]{1,0:T(8,128)(2,1)S(1)}, u32[]{:S(2)}, u32[]{:S(2)}) collective-permute-start(bf16[8,2560]{1,0:T(8,128)(2,1)} %refs_0_.3), channel_id=1, source_target_pairs={{12,0},{13,1},{14,2},{15,3},{8,4},{9,5},{10,6},{11,7},{4,8},{5,9},... | collective-permute-start | bytes 122888 | tf_op jit(solution)/shard_map/ppermute | solution.py:290
  5.5 0.1 collective-permute-start.2
  5.6 0.8 %copy-done = bf16[8,2560]{1,0:T(8,128)(2,1)S(1)} copy-done((bf16[8,2560]{1,0:T(8,128)(2,1)S(1)}, bf16[8,2560]{1,0:T(8,128)(2,1)}, u32[]{:S(2)}) %copy-start) | copy-done | bytes 40984
  6.4 0.0 collective-permute-done.1.refs_1_
  6.4 1.6 %collective-permute-start.3 = (bf16[16,2560]{1,0:T(8,128)(2,1)S(1)}, bf16[16,2560]{1,0:T(8,128)(2,1)S(1)}, u32[]{:S(2)}, u32[]{:S(2)}) collective-permute-start(bf16[16,2560]{1,0:T(8,128)(2,1)S(1)} %merge.10.refs_0_), channel_id=1, source_target_pairs={{2,0},{3,1},{0,2},{1,3},{6,4},{7,5},{4,6},{5,7},{10,8},{11,9},{8,1... | collective-permute-start | bytes 245768 | tf_op jit(solution)/shard_map/ppermute | solution.py:290
  8.0 1.5 %collective-permute-done.refs_5_.refs_2_ = bf16[8,2560]{1,0:T(8,128)(2,1)S(1)} collective-permute-done((bf16[8,2560]{1,0:T(8,128)(2,1)}, bf16[8,2560]{1,0:T(8,128)(2,1)S(1)}, u32[]{:S(2)}, u32[]{:S(2)}) %collective-permute-start) | collective-permute-done | bytes 40992 | tf_op jit(solution)/shard_map/ppermute | solution.py:290
  9.6 1.5 %collective-permute-start.5 = (bf16[8,2560]{1,0:T(8,128)(2,1)S(1)}, bf16[8,2560]{1,0:T(8,128)(2,1)S(1)}, u32[]{:S(2)}, u32[]{:S(2)}) collective-permute-start(bf16[8,2560]{1,0:T(8,128)(2,1)S(1)} %collective-permute-done.refs_5_.refs_2_), channel_id=1, source_target_pairs={{2,0},{3,1},{0,2},{1,3},{6,4},{7,5},{4,6},{5,7},{10,8},{11,9},{8,1... | collective-permute-start | bytes 122888 | tf_op jit(solution)/shard_map/ppermute | solution.py:290
  11.1 1.5 %collective-permute-start.4 = (bf16[8,2560]{1,0:T(8,128)(2,1)S(1)}, bf16[8,2560]{1,0:T(8,128)(2,1)S(1)}, u32[]{:S(2)}, u32[]{:S(2)}) collective-permute-start(bf16[8,2560]{1,0:T(8,128)(2,1)S(1)} %collective-permute-done.2.refs_1_), channel_id=1, source_target_pairs={{2,0},{3,1},{0,2},{1,3},{6,4},{7,5},{4,6},{5,7},{10,8},{11,9},{8,1... | collective-permute-start | bytes 122888 | tf_op jit(solution)/shard_map/ppermute | solution.py:290
  12.6 2.7 %load.1 = (bf16[640,2560]{1,0:T(8,128)(2,1)S(1)}, bf16[640,2560]{1,0:T(8,128)(2,1)S(1)}, f32[1,640]{1,0:T(1,128)S(1)}) custom-call(bf16[512,2560]{1,0:T(8,128)(2,1)} %refs_0_.2, bf16[512,2560]{1,0:T(8,128)(2,1)} %refs_1_.1, bf16[8,2560]{1,0:T(8,128)(2,1)} %refs_2_.1, bf16[8,2560]{1,0:T(8,128)(2,1)} %refs_3_.1, s32[1,16]{1,0:T(1,128)} %bitcast.1, ...), custom_call_target="tpu_custom_call" | custom-call | bytes 10485760 | tf_op jit(solution)/shard_map/load/pallas_call | solution.py:194
  15.2 0.0 collective-permute-done.5.refs_5_
  15.3 0.0 collective-permute-done.4.refs_4_
  15.3 0.1 collective-permute-start.6
  15.4 1.6 %collective-permute-done.6.refs_2_ = bf16[64,2560]{1,0:T(8,128)(2,1)S(1)} collective-permute-done((bf16[64,2560]{1,0:T(8,128)(2,1)S(1)}, bf16[64,2560]{1,0:T(8,128)(2,1)S(1)}, u32[]{:S(2)}, u32[]{:S(2)}) %collective-permute-start.6) | collective-permute-done | bytes 327712 | tf_op jit(solution)/shard_map/ppermute | solution.py:290
  17.0 4.3 %attend.1 = (f32[32,2688]{1,0:T(8,128)S(1)}, f32[32,2688]{1,0:T(8,128)S(1)}, bf16[32,2688]{1,0:T(8,128)(2,1)S(1)}, bf16[32,2688]{1,0:T(8,128)(2,1)S(1)}) custom-call(f32[1,640]{1,0:T(1,128)S(1)} %get-tuple-element.20.refs_0_, bf16[64,2560]{1,0:T(8,128)(2,1)S(1)} %merge.11.refs_1_, bf16[64,2560]{1,0:T(8,128)(2,1)S(1)} %collective-permute-done.6.refs_2_, ...), custom_call_target="tpu_custom_call" | custom-call | flops 838860800 | bytes 6553600 | tf_op jit(solution)/shard_map/attend/pallas_call | solution.py:134
  21.3 0.2 collective-permute-start.8
  21.5 0.4 %collective-permute-start.7 = (bf16[32,2688]{1,0:T(8,128)(2,1)S(1)}, bf16[32,2688]{1,0:T(8,128)(2,1)S(1)}, u32[]{:S(2)}, u32[]{:S(2)}) collective-permute-start(bf16[32,2688]{1,0:T(8,128)(2,1)S(1)} %get-tuple-element.24), channel_id=1, source_target_pairs={{0,1},{1,0},{2,3},{3,2},{4,5},{5,4},{6,7},{7,6},{8,9},{9,8},{10,11... | collective-permute-start | bytes 516104 | tf_op jit(solution)/shard_map/ppermute | solution.py:293
  21.9 0.9 %collective-permute-done.8.refs_1_ = bf16[32,2688]{1,0:T(8,128)(2,1)S(1)} collective-permute-done((bf16[32,2688]{1,0:T(8,128)(2,1)S(1)}, bf16[32,2688]{1,0:T(8,128)(2,1)S(1)}, u32[]{:S(2)}, u32[]{:S(2)}) %collective-permute-start.8) | collective-permute-done | bytes 172064 | tf_op jit(solution)/shard_map/ppermute | solution.py:293
  22.8 0.3 merge.13
  23.1 1.4 %collective-permute-start.10 = (bf16[16,2688]{1,0:T(8,128)(2,1)S(1)}, bf16[16,2688]{1,0:T(8,128)(2,1)S(1)}, u32[]{:S(2)}, u32[]{:S(2)}) collective-permute-start(bf16[16,2688]{1,0:T(8,128)(2,1)S(1)} %get-tuple-element.30), channel_id=1, source_target_pairs={{0,2},{1,3},{2,0},{3,1},{4,6},{5,7},{6,4},{7,5},{8,10},{9,11},{10,... | collective-permute-start | bytes 258056 | tf_op jit(solution)/shard_map/ppermute | solution.py:293
  24.5 0.7 %collective-permute-start.9 = (bf16[16,2688]{1,0:T(8,128)(2,1)S(1)}, bf16[16,2688]{1,0:T(8,128)(2,1)S(1)}, u32[]{:S(2)}, u32[]{:S(2)}) collective-permute-start(bf16[16,2688]{1,0:T(8,128)(2,1)S(1)} %get-tuple-element.28), channel_id=1, source_target_pairs={{0,2},{1,3},{2,0},{3,1},{4,6},{5,7},{6,4},{7,5},{8,10},{9,11},{10,... | collective-permute-start | bytes 258056 | tf_op jit(solution)/shard_map/ppermute | solution.py:293
  25.2 0.0 collective-permute-done.7.refs_1_
  25.2 0.3 merge.12
  25.5 3.1 %collective-permute-done.10.refs_1_ = bf16[16,2688]{1,0:T(8,128)(2,1)S(1)} collective-permute-done((bf16[16,2688]{1,0:T(8,128)(2,1)S(1)}, bf16[16,2688]{1,0:T(8,128)(2,1)S(1)}, u32[]{:S(2)}, u32[]{:S(2)}) %collective-permute-start.10) | collective-permute-done | bytes 86048 | tf_op jit(solution)/shard_map/ppermute | solution.py:293
  28.5 0.2 merge.14
  28.7 1.9 %collective-permute-start.12 = (bf16[8,2688]{1,0:T(8,128)(2,1)S(1)}, bf16[8,2688]{1,0:T(8,128)(2,1)S(1)}, u32[]{:S(2)}, u32[]{:S(2)}) collective-permute-start(bf16[8,2688]{1,0:T(8,128)(2,1)S(1)} %get-tuple-element.33), channel_id=1, source_target_pairs={{0,12},{1,13},{2,14},{3,15},{4,8},{5,9},{6,10},{7,11},{8,4},{9,5},... | collective-permute-start | bytes 129032 | tf_op jit(solution)/shard_map/ppermute | solution.py:293
  30.7 0.2 merge.15
  30.9 2.6 %collective-permute-start.13 = (bf16[8,2688]{1,0:T(8,128)(2,1)S(1)}, bf16[8,2688]{1,0:T(8,128)(2,1)S(1)}, u32[]{:S(2)}, u32[]{:S(2)}) collective-permute-start(bf16[8,2688]{1,0:T(8,128)(2,1)S(1)} %get-tuple-element.34), channel_id=1, source_target_pairs={{0,4},{1,5},{2,6},{3,7},{4,0},{5,1},{6,2},{7,3},{8,12},{9,13},{10,... | collective-permute-start | bytes 129032 | tf_op jit(solution)/shard_map/ppermute | solution.py:293
  33.5 1.3 %collective-permute-done.12.refs_2_ = bf16[8,2688]{1,0:T(8,128)(2,1)S(1)} collective-permute-done((bf16[8,2688]{1,0:T(8,128)(2,1)S(1)}, bf16[8,2688]{1,0:T(8,128)(2,1)S(1)}, u32[]{:S(2)}, u32[]{:S(2)}) %collective-permute-start.12) | collective-permute-done | bytes 43040 | tf_op jit(solution)/shard_map/ppermute | solution.py:293
  34.8 1.2 %collective-permute-done.11.refs_1_ = bf16[8,2688]{1,0:T(8,128)(2,1)S(1)} collective-permute-done((bf16[8,2688]{1,0:T(8,128)(2,1)S(1)}, bf16[8,2688]{1,0:T(8,128)(2,1)S(1)}, u32[]{:S(2)}, u32[]{:S(2)}) %collective-permute-start.11) | collective-permute-done | bytes 43040 | tf_op jit(solution)/shard_map/ppermute | solution.py:293
  35.9 0.2 merge.16.refs_0_
  36.1 0.8 %merge.17 = bf16[8,2560]{1,0:T(8,128)(2,1)} custom-call(f32[8,2688]{1,0:T(8,128)S(1)} %merge.16.refs_0_, bf16[8,2688]{1,0:T(8,128)(2,1)S(1)} %collective-permute-done.13.refs_1_), custom_call_target="tpu_custom_call" | custom-call | flops 172032 | bytes 172032 | tf_op jit(solution)/shard_map/merge/pallas_call | solution.py:271
  (9 shorter events, 0.0 us)
Async XLA Ops:
  0.0 6.4 %collective-permute-start.1 = (bf16[8,2560]{1,0:T(8,128)(2,1)}, bf16[8,2560]{1,0:T(8,128)(2,1)S(1)}, u32[]{:S(2)}, u32[]{:S(2)}) collective-permute-start(bf16[8,2560]{1,0:T(8,128)(2,1)} %refs_0_.3), channel_id=1, source_target_pairs={{4,0},{5,1},{6,2},{7,3},{0,4},{1,5},{2,6},{3,7},{12,8},{13,9},{14,... | collective-permute-start | bytes 122888 | tf_op jit(solution)/shard_map/ppermute | solution.py:290
  3.0 6.5 %collective-permute-start = (bf16[8,2560]{1,0:T(8,128)(2,1)}, bf16[8,2560]{1,0:T(8,128)(2,1)S(1)}, u32[]{:S(2)}, u32[]{:S(2)}) collective-permute-start(bf16[8,2560]{1,0:T(8,128)(2,1)} %refs_0_.3), channel_id=1, source_target_pairs={{12,0},{13,1},{14,2},{15,3},{8,4},{9,5},{10,6},{11,7},{4,8},{5,9},... | collective-permute-start | bytes 122888 | tf_op jit(solution)/shard_map/ppermute | solution.py:290
  5.5 5.6 %collective-permute-start.2 = (bf16[8,2560]{1,0:T(8,128)(2,1)}, bf16[8,2560]{1,0:T(8,128)(2,1)S(1)}, u32[]{:S(2)}, u32[]{:S(2)}) collective-permute-start(bf16[8,2560]{1,0:T(8,128)(2,1)} %refs_0_.3), channel_id=1, source_target_pairs={{8,0},{9,1},{10,2},{11,3},{12,4},{13,5},{14,6},{15,7},{0,8},{1,9},... | collective-permute-start | bytes 122888 | tf_op jit(solution)/shard_map/ppermute | solution.py:290
  5.6 0.8 %copy-start = (bf16[8,2560]{1,0:T(8,128)(2,1)S(1)}, bf16[8,2560]{1,0:T(8,128)(2,1)}, u32[]{:S(2)}) copy-start(bf16[8,2560]{1,0:T(8,128)(2,1)} %refs_0_.3) | copy-start | bytes 122884
  6.4 8.8 %collective-permute-start.3 = (bf16[16,2560]{1,0:T(8,128)(2,1)S(1)}, bf16[16,2560]{1,0:T(8,128)(2,1)S(1)}, u32[]{:S(2)}, u32[]{:S(2)}) collective-permute-start(bf16[16,2560]{1,0:T(8,128)(2,1)S(1)} %merge.10.refs_0_), channel_id=1, source_target_pairs={{2,0},{3,1},{0,2},{1,3},{6,4},{7,5},{4,6},{5,7},{10,8},{11,9},{8,1... | collective-permute-start | bytes 245768 | tf_op jit(solution)/shard_map/ppermute | solution.py:290
  9.6 5.7 %collective-permute-start.5 = (bf16[8,2560]{1,0:T(8,128)(2,1)S(1)}, bf16[8,2560]{1,0:T(8,128)(2,1)S(1)}, u32[]{:S(2)}, u32[]{:S(2)}) collective-permute-start(bf16[8,2560]{1,0:T(8,128)(2,1)S(1)} %collective-permute-done.refs_5_.refs_2_), channel_id=1, source_target_pairs={{2,0},{3,1},{0,2},{1,3},{6,4},{7,5},{4,6},{5,7},{10,8},{11,9},{8,1... | collective-permute-start | bytes 122888 | tf_op jit(solution)/shard_map/ppermute | solution.py:290
  11.1 4.2 %collective-permute-start.4 = (bf16[8,2560]{1,0:T(8,128)(2,1)S(1)}, bf16[8,2560]{1,0:T(8,128)(2,1)S(1)}, u32[]{:S(2)}, u32[]{:S(2)}) collective-permute-start(bf16[8,2560]{1,0:T(8,128)(2,1)S(1)} %collective-permute-done.2.refs_1_), channel_id=1, source_target_pairs={{2,0},{3,1},{0,2},{1,3},{6,4},{7,5},{4,6},{5,7},{10,8},{11,9},{8,1... | collective-permute-start | bytes 122888 | tf_op jit(solution)/shard_map/ppermute | solution.py:290
  15.3 1.7 %collective-permute-start.6 = (bf16[64,2560]{1,0:T(8,128)(2,1)S(1)}, bf16[64,2560]{1,0:T(8,128)(2,1)S(1)}, u32[]{:S(2)}, u32[]{:S(2)}) collective-permute-start(bf16[64,2560]{1,0:T(8,128)(2,1)S(1)} %merge.11.refs_1_), channel_id=1, source_target_pairs={{1,0},{0,1},{3,2},{2,3},{5,4},{4,5},{7,6},{6,7},{9,8},{8,9},{11,10... | collective-permute-start | bytes 983048 | tf_op jit(solution)/shard_map/ppermute | solution.py:290
  21.3 1.5 %collective-permute-start.8 = (bf16[32,2688]{1,0:T(8,128)(2,1)S(1)}, bf16[32,2688]{1,0:T(8,128)(2,1)S(1)}, u32[]{:S(2)}, u32[]{:S(2)}) collective-permute-start(bf16[32,2688]{1,0:T(8,128)(2,1)S(1)} %get-tuple-element.27), channel_id=1, source_target_pairs={{0,1},{1,0},{2,3},{3,2},{4,5},{5,4},{6,7},{7,6},{8,9},{9,8},{10,11... | collective-permute-start | bytes 516104 | tf_op jit(solution)/shard_map/ppermute | solution.py:293
  21.5 3.7 %collective-permute-start.7 = (bf16[32,2688]{1,0:T(8,128)(2,1)S(1)}, bf16[32,2688]{1,0:T(8,128)(2,1)S(1)}, u32[]{:S(2)}, u32[]{:S(2)}) collective-permute-start(bf16[32,2688]{1,0:T(8,128)(2,1)S(1)} %get-tuple-element.24), channel_id=1, source_target_pairs={{0,1},{1,0},{2,3},{3,2},{4,5},{5,4},{6,7},{7,6},{8,9},{9,8},{10,11... | collective-permute-start | bytes 516104 | tf_op jit(solution)/shard_map/ppermute | solution.py:293
  23.1 5.4 %collective-permute-start.10 = (bf16[16,2688]{1,0:T(8,128)(2,1)S(1)}, bf16[16,2688]{1,0:T(8,128)(2,1)S(1)}, u32[]{:S(2)}, u32[]{:S(2)}) collective-permute-start(bf16[16,2688]{1,0:T(8,128)(2,1)S(1)} %get-tuple-element.30), channel_id=1, source_target_pairs={{0,2},{1,3},{2,0},{3,1},{4,6},{5,7},{6,4},{7,5},{8,10},{9,11},{10,... | collective-permute-start | bytes 258056 | tf_op jit(solution)/shard_map/ppermute | solution.py:293
  24.5 6.2 %collective-permute-start.9 = (bf16[16,2688]{1,0:T(8,128)(2,1)S(1)}, bf16[16,2688]{1,0:T(8,128)(2,1)S(1)}, u32[]{:S(2)}, u32[]{:S(2)}) collective-permute-start(bf16[16,2688]{1,0:T(8,128)(2,1)S(1)} %get-tuple-element.28), channel_id=1, source_target_pairs={{0,2},{1,3},{2,0},{3,1},{4,6},{5,7},{6,4},{7,5},{8,10},{9,11},{10,... | collective-permute-start | bytes 258056 | tf_op jit(solution)/shard_map/ppermute | solution.py:293
  28.7 6.0 %collective-permute-start.12 = (bf16[8,2688]{1,0:T(8,128)(2,1)S(1)}, bf16[8,2688]{1,0:T(8,128)(2,1)S(1)}, u32[]{:S(2)}, u32[]{:S(2)}) collective-permute-start(bf16[8,2688]{1,0:T(8,128)(2,1)S(1)} %get-tuple-element.33), channel_id=1, source_target_pairs={{0,12},{1,13},{2,14},{3,15},{4,8},{5,9},{6,10},{7,11},{8,4},{9,5},... | collective-permute-start | bytes 129032 | tf_op jit(solution)/shard_map/ppermute | solution.py:293
  30.7 5.3 %collective-permute-start.11 = (bf16[8,2688]{1,0:T(8,128)(2,1)S(1)}, bf16[8,2688]{1,0:T(8,128)(2,1)S(1)}, u32[]{:S(2)}, u32[]{:S(2)}) collective-permute-start(bf16[8,2688]{1,0:T(8,128)(2,1)S(1)} %get-tuple-element.31.refs_2_), channel_id=1, source_target_pairs={{0,8},{1,9},{2,10},{3,11},{4,12},{5,13},{6,14},{7,15},{8,0},{9,1},... | collective-permute-start | bytes 129032 | tf_op jit(solution)/shard_map/ppermute | solution.py:293
  30.9 5.2 %collective-permute-start.13 = (bf16[8,2688]{1,0:T(8,128)(2,1)S(1)}, bf16[8,2688]{1,0:T(8,128)(2,1)S(1)}, u32[]{:S(2)}, u32[]{:S(2)}) collective-permute-start(bf16[8,2688]{1,0:T(8,128)(2,1)S(1)} %get-tuple-element.34), channel_id=1, source_target_pairs={{0,4},{1,5},{2,6},{3,7},{4,0},{5,1},{6,2},{7,3},{8,12},{9,13},{10,... | collective-permute-start | bytes 129032 | tf_op jit(solution)/shard_map/ppermute | solution.py:293

commit v8 on v7

--- a/solution.py
+++ b/solution.py
@@ -21,7 +21,9 @@
 def factors(members):
     cores = 2 if members % 2 == 0 else 1
     chips = members // cores
-    far = next(a for a in range(1, chips + 1) if chips % a == 0 and a * a >= chips)
+    far = next(
+        a for a in range(1, chips + 1) if chips % a == 0 and a * a >= chips and a % (chips // a) == 0
+    )
     return far, chips // far, cores
 
 
@@ -29,13 +31,23 @@
     return at ^ by if size & (size - 1) == 0 else (at + by) % size
 
 
-def partner_perm(shape, by, back):
+def role_perm(shape, mine, others, back=False):
     def flat(place):
         return functools.reduce(lambda at, kn: at * kn[1] + kn[0], zip(place, shape), 0)
 
-    places = itertools.product(*map(range, shape))
-    pairs = [(flat([partner(*x) for x in zip(at, by, shape)]), flat(at)) for at in places]
-    return [pair[::-1] for pair in pairs] if back else pairs
+    pairs = []
+    for at in itertools.product(*map(range, shape)):
+        step = mine if is_first(at[2], shape[2]) else others
+        to = list(at)
+        if step is not None:
+            axis, by = step
+            to[axis] = partner(at[axis], by, shape[axis])
+        pairs.append((flat(at), flat(to)) if back else (flat(to), flat(at)))
+    return pairs
+
+
+def is_first(core, cores):
+    return core == cores - 1
 
 
 def lanes(rows):
@@ -229,27 +241,84 @@
     return lambda cols: ref[(*index, slice(None), cols)].astype(F32)
 
 
-def merge_rows(ins, heads, pieces, kinds, after=()):
+def role_kernel(role, one, other):
+    if one is other:
+        return one()
+    pl.when(role() == 1)(one)
+    pl.when(role() != 1)(other)
+
+
+def put(merged_rows, outs):
+    for cols, total in merged_rows:
+        per = total.shape[0] // len(outs)
+        for j, out in enumerate(outs):
+            if out is not None:
+                out[:, cols] = total[j * per : (j + 1) * per].astype(out.dtype)
+
+
+def merge_rows(ins, heads, kinds):
     rows, width = ins[0].shape
-    per = rows // pieces
-
-    def body(*refs):
-        outs = refs[len(ins) + len(after) :]
-        for cols, total in merged([getter(r) for r in refs[: len(ins)]], heads, False):
-            for j, out in enumerate(outs):
-                out[:, cols] = total[j * per : (j + 1) * per].astype(out.dtype)
-
-    shapes = [jax.ShapeDtypeStruct((per, width), kind) for kind in kinds]
-    return call_merge(body, ins, shapes, after)
-
-
-def finish(ins, heads):
-    rows = ins[0].shape[0]
+    n = len(ins)
+    per = rows // len(kinds)
+    flat = [kind for pair in kinds for kind in pair]
+
+    def body(*refs):
+        outs = iter(refs[n:])
+        outs = [[next(outs) for _ in pair] for pair in kinds]
+        for cols, total in merged([getter(r) for r in refs[:n]], heads, False):
+            for j, pair in enumerate(outs):
+                for out in pair:
+                    out[:, cols] = total[j * per : (j + 1) * per].astype(out.dtype)
+
+    return call_merge(body, ins, [jax.ShapeDtypeStruct((per, width), kind) for kind in flat])
+
+
+def merge_unit(role, heads, slots, mine, others, own):
+    ins = [*mine, *others] + ([own] if own is not None else [])
+    rows, width = ins[0].shape
+    per = rows // slots
+    n = len(mine)
+
+    def body(*refs):
+        first, pieces = refs[len(ins)], refs[len(ins) + 1 :]
+
+        def one():
+            parts = [getter(r) for r in refs[:n]]
+            if own is None:
+                put(merged(parts, heads, False), [first, *pieces])
+            else:
+                put(merged(parts, heads, False), pieces)
+                first[...] = refs[len(ins) - 1][...]
+
+        def other():
+            parts = [getter(r) for r in refs[n : n + len(others)]]
+            skip = [] if own is None else [None]
+            put(merged(parts, heads, False), [first, *pieces[len(skip) :]])
+
+        if not others:
+            pl.when(role() == 1)(one)
+        elif others is mine:
+            one()
+        else:
+            role_kernel(role, one, other)
+
+    sent = slots if own is not None else slots - 1
+    shapes = [jax.ShapeDtypeStruct((per, width), F32)]
+    shapes += [jax.ShapeDtypeStruct((per, width), BF16)] * sent
+    return call_merge(body, ins, shapes)
+
+
+def finish(role, own, got, near, heads):
+    rows = own.shape[0]
+    ins = [own, *got]
 
     def body(*refs):
         out = refs[len(ins)]
-        for cols, total in merged([getter(r) for r in refs[: len(ins)]], heads, True):
-            out[:, cols] = total.astype(out.dtype)
+
+        def add(parts):
+            return lambda: put(merged([getter(r) for r in parts], heads, True), [out])
+
+        role_kernel(role, add(refs[: len(ins)]), add([refs[0], *refs[len(ins) - near : len(ins)]]))
 
     return call_merge(body, ins, [jax.ShapeDtypeStruct((rows, heads * HD), BF16)])[0]
 
@@ -264,6 +333,26 @@
 
     shape = jax.ShapeDtypeStruct((rows, pieces[0].shape[1]), pieces[0].dtype)
     return call_merge(body, pieces, [shape], after)[0]
+
+
+def choose(role, mine, others, after=()):
+    ins = [*mine, *others]
+    rows = sum(p.shape[0] for p in mine)
+
+    def body(*refs):
+        out = refs[-1]
+
+        def fill(parts):
+            def store():
+                rows = [r[...].astype(F32) for r in parts]
+                out[...] = jnp.concatenate(rows, axis=0).astype(out.dtype)
+
+            return store
+
+        role_kernel(role, fill(refs[: len(mine)]), fill(refs[len(mine) : len(ins)]))
+
+    shape = jax.ShapeDtypeStruct((rows, mine[0].shape[1]), mine[0].dtype)
+    return call_merge(body, ins, [shape], after)[0]
 
 
 def call_merge(body, ins, shapes, after=()):
@@ -286,43 +375,68 @@
     a_n, b_n, c_n = shape
     heads = queries.shape[1] // HD
 
-    def fetch(x, *by):
-        return lax.ppermute(x, "seq", partner_perm(shape, by, False))
-
-    def give(x, *by):
-        return lax.ppermute(x, "seq", partner_perm(shape, by, True))
-
-    pieces = [join([queries])] + [fetch(queries, a, 0, 0) for a in range(1, a_n)]
-    runs = [pieces[:2], pieces[2:-1], pieces[-1:]] if a_n > 3 else [pieces]
-    runs = [x[0] if len(x) == 1 else join(x) for x in runs]
-    lines = [runs] + [[fetch(x, 0, b, 0) for x in runs] for b in range(1, b_n)]
-    keys, values, bias = load((cache_keys, cache_values), (new_keys, new_values), victims[None], runs[-1])
-    plane = join([x for pieces in lines for x in pieces], (keys,))
-    planes = [plane] + [fetch(plane, 0, 0, c) for c in range(1, c_n)]
+    def role():
+        core = lax.rem(lax.axis_index("seq"), c_n)
+        return jnp.where(core == c_n - 1, 1, 0)
+
+    def swap(x, mine, others, back=False):
+        return lax.ppermute(x, "seq", role_perm(shape, mine, others, back))
+
+    far_a = [0, *range(a_n - 1, 0, -1)]
+    far_b = [0, *range(b_n - 1, 0, -1)]
+    ratio = a_n // b_n
+    crossing = a_n - ratio
+
+    slots = [join([queries])]
+    for s in range(1, a_n):
+        slots.append(swap(queries, (0, far_a[s]), (1, far_b[s]) if s < b_n else None))
+    units = [join(slots[:b_n])]
+    units += [
+        choose(role, slots[i * b_n : (i + 1) * b_n], units[:1]) for i in range(1, ratio)
+    ]
+
+    def steps(j):
+        return (1, far_b[j // ratio + 1]) if j < crossing else None, (0, far_a[j + 1])
+
+    got = [
+        swap(units[j % ratio] if j < crossing else units[0], *steps(j)) for j in range(a_n - 1)
+    ]
+    keys, values, bias = load(
+        (cache_keys, cache_values), (new_keys, new_values), victims[None], slots[-1]
+    )
+    mine = [*units, *got[:crossing]]
+    others = [units[0], *got[crossing:], *got[:crossing]]
+    plane = choose(role, mine, others, (keys,))
+    planes = [plane] + [swap(plane, (2, c), (2, c)) for c in range(1, c_n)]
+
     kinds = [F32] * b_n + [BF16] * (b_n * (c_n - 1))
     sums = attend(planes, b_n, kinds, keys, values, bias)
 
-    halves = 2 if a_n % 2 == 0 else 1
-    per = a_n // halves
-
-    def over_cores(b, kind):
-        got = [give(sums[c * b_n + b], 0, 0, c) for c in range(1, c_n)]
-        return merge_rows([sums[b]] + got, heads, halves, [kind] * halves)
-
-    got = [over_cores(b, BF16) for b in range(1, b_n)]
-    got = [[give(x, 0, b, 0) for x in half[::-1]][::-1] for b, half in enumerate(got, 1)]
-    own = over_cores(0, F32)
-    pieces = []
-    for h in range(halves)[::-1]:
-        kinds = [BF16 if h + j else F32 for j in range(per)]
-        parts = [own[h]] + [half[h] for half in got]
-        pieces = [*merge_rows(parts, heads, per, kinds, pieces[:1]), *pieces]
-    near, far = [
-        [give(pieces[a], a, 0, 0) for a in part] for part in (range(1, per), range(max(per, 1), a_n))
-    ]
-    if far:
-        pieces[:1] = merge_rows([pieces[0]] + far, heads, 1, [F32])
-    return finish([pieces[0]] + near, heads)
+    def over_cores(b, pairs):
+        back = [swap(sums[c * b_n + b], (2, c), (2, c), True) for c in range(1, c_n)]
+        return merge_rows([sums[b]] + back, heads, pairs)
+
+    sent = [x for b in range(1, b_n) for x in over_cores(b, [[BF16]] * ratio)]
+    kept = over_cores(0, [[F32]] + [[F32, BF16]] * (ratio - 1))
+    sent += kept[2::2]
+    kept = [kept[0], *kept[1::2]]
+    got = [swap(x, *steps(j), True) for j, x in enumerate(sent)]
+
+    own, pieces = None, []
+    for i in range(ratio):
+        part = [kept[i], *got[i:crossing:ratio]]
+        if i < ratio - 1:
+            rest = []
+        else:
+            rest = part if ratio == 1 else [kept[0], *got]
+        out = merge_unit(role, heads, b_n, part, rest, own)
+        own, pieces = out[0], pieces + list(out[1:])
+    got = []
+    for s in range(1, a_n):
+        near = s - (a_n - b_n)
+        step = (1, far_b[near]) if near > 0 else None
+        got.append(swap(pieces[s - 1], (0, far_a[s]), step, True))
+    return finish(role, own, got, b_n - 1, heads)
 
 
 def solution(mesh):

time: 37.1 us -> 44.1 us (1.19)
  the two profiles are of different devices: /device:TPU:0 before, /device:TPU:1 now
where the time goes in v8:
time: 44.1 us; the launch traced here: 43.8 us
  starting transfers between devices  21.7 us (49%)
  waiting for transfers between devices  12.2 us (28%)
  Pallas kernels  8.91 us (20%)
  local copies, waits for them, and re-layouts  0.78 us (2%)
    ppermute x15, starting transfers between devices, swap(): return lax.ppermute(x, 'seq', role_perm(shape, mine, others, back))  21.7 us
    ppermute x15, waiting for transfers between devices, swap(): return lax.ppermute(x, 'seq', role_perm(shape, mine, others, back))  12.2 us
    pallas_call x1, Pallas kernels, attend(): pl.pallas_call(body, in_specs=[pl.BlockSpec(memory_space=pltpu.VMEM)] * (...  4.33 us
    pallas_call x1, Pallas kernels, load(): pl.pallas_call(body, in_specs=[in_hbm] * len(held) + [pl.BlockSpec(memory...  2.66 us
    pallas_call x9, Pallas kernels, call_merge(): pl.pallas_call(body, in_specs=[pl.BlockSpec(memory_space=pltpu.VMEM)] * l...  1.91 us
  transfers between devices with their start and end apart: 15, of which 6 were waited for; matrix products, arithmetic and copies ran while one was open for 0% of the time, Pallas kernels for 8%

profile of v8, /device:TPU:1, one launch (start us, length us, event | category | flops | bytes accessed | tf_op | source)
XLA Modules:
  0.0 43.8 jit_solution(12802869734156565336)
XLA Ops:
  0.0 4.2 %collective-permute-start.1 = (bf16[8,2560]{1,0:T(8,128)(2,1)}, bf16[8,2560]{1,0:T(8,128)(2,1)S(1)}, u32[]{:S(2)}, u32[]{:S(2)}) collective-permute-start(bf16[8,2560]{1,0:T(8,128)(2,1)} %refs_0_.3), channel_id=1, source_target_pairs={{2,0},{13,1},{0,2},{15,3},{6,4},{9,5},{4,6},{11,7},{10,8},{5,9},{8... | collective-permute-start | bytes 122888 | tf_op jit(solution)/shard_map/ppermute | solution.py:383
  4.2 1.9 %collective-permute-start = (bf16[8,2560]{1,0:T(8,128)(2,1)}, bf16[8,2560]{1,0:T(8,128)(2,1)S(1)}, u32[]{:S(2)}, u32[]{:S(2)}) collective-permute-start(bf16[8,2560]{1,0:T(8,128)(2,1)} %refs_0_.3), channel_id=1, source_target_pairs={{0,0},{5,1},{2,2},{7,3},{4,4},{1,5},{6,6},{3,7},{8,8},{13,9},{10,1... | collective-permute-start | bytes 122888 | tf_op jit(solution)/shard_map/ppermute | solution.py:383
  6.1 2.2 %collective-permute-start.2 = (bf16[8,2560]{1,0:T(8,128)(2,1)}, bf16[8,2560]{1,0:T(8,128)(2,1)S(1)}, u32[]{:S(2)}, u32[]{:S(2)}) collective-permute-start(bf16[8,2560]{1,0:T(8,128)(2,1)} %refs_0_.3), channel_id=1, source_target_pairs={{0,0},{9,1},{2,2},{11,3},{4,4},{13,5},{6,6},{15,7},{8,8},{1,9},{10... | collective-permute-start | bytes 122888 | tf_op jit(solution)/shard_map/ppermute | solution.py:383
  8.3 0.8 %copy-done = bf16[8,2560]{1,0:T(8,128)(2,1)S(1)} copy-done((bf16[8,2560]{1,0:T(8,128)(2,1)S(1)}, bf16[8,2560]{1,0:T(8,128)(2,1)}, u32[]{:S(2)}) %copy-start) | copy-done | bytes 40984
  9.1 0.0 collective-permute-done.1.refs_1_
  9.1 0.0 collective-permute-done.refs_5_.refs_1_
  9.1 4.1 %collective-permute-done.2.refs_0_ = bf16[8,2560]{1,0:T(8,128)(2,1)S(1)} collective-permute-done((bf16[8,2560]{1,0:T(8,128)(2,1)}, bf16[8,2560]{1,0:T(8,128)(2,1)S(1)}, u32[]{:S(2)}, u32[]{:S(2)}) %collective-permute-start.2) | collective-permute-done | bytes 40992 | tf_op jit(solution)/shard_map/ppermute | solution.py:383
  13.3 0.7 %collective-permute-start.5 = (bf16[16,2560]{1,0:T(8,128)(2,1)S(1)}, bf16[16,2560]{1,0:T(8,128)(2,1)S(1)}, u32[]{:S(2)}, u32[]{:S(2)}) collective-permute-start(bf16[16,2560]{1,0:T(8,128)(2,1)S(1)} %merge.10.refs_2_.refs_0_.refs_4_), channel_id=1, source_target_pairs={{4,0},{1,1},{6,2},{3,3},{0,4},{5,5},{2,6},{7,7},{12,8},{9,9},{14,1... | collective-permute-start | bytes 245768 | tf_op jit(solution)/shard_map/ppermute | solution.py:383
  13.9 1.5 %collective-permute-start.3 = (bf16[16,2560]{1,0:T(8,128)(2,1)S(1)}, bf16[16,2560]{1,0:T(8,128)(2,1)S(1)}, u32[]{:S(2)}, u32[]{:S(2)}) collective-permute-start(bf16[16,2560]{1,0:T(8,128)(2,1)S(1)} %merge.10.refs_2_.refs_0_.refs_4_), channel_id=1, source_target_pairs={{12,0},{3,1},{14,2},{1,3},{8,4},{7,5},{10,6},{5,7},{4,8},{11,9},{6... | collective-permute-start | bytes 245768 | tf_op jit(solution)/shard_map/ppermute | solution.py:383
  15.4 2.7 %load.1 = (bf16[640,2560]{1,0:T(8,128)(2,1)S(1)}, bf16[640,2560]{1,0:T(8,128)(2,1)S(1)}, f32[1,640]{1,0:T(1,128)S(1)}) custom-call(bf16[512,2560]{1,0:T(8,128)(2,1)} %refs_0_.2, bf16[512,2560]{1,0:T(8,128)(2,1)} %refs_1_.1, bf16[8,2560]{1,0:T(8,128)(2,1)} %refs_2_.1, bf16[8,2560]{1,0:T(8,128)(2,1)} %refs_3_.1, s32[1,16]{1,0:T(1,128)} %bitcast.1, ...), custom_call_target="tpu_custom_call" | custom-call | bytes 10485760 | tf_op jit(solution)/shard_map/load/pallas_call | solution.py:206
  18.1 0.0 collective-permute-done.5.refs_5_
  18.1 0.0 collective-permute-done.3.refs_2_.refs_6_
  18.2 1.1 %collective-permute-start.6 = (bf16[64,2560]{1,0:T(8,128)(2,1)S(1)}, bf16[64,2560]{1,0:T(8,128)(2,1)S(1)}, u32[]{:S(2)}, u32[]{:S(2)}) collective-permute-start(bf16[64,2560]{1,0:T(8,128)(2,1)S(1)} %merge.12.refs_1_), channel_id=1, source_target_pairs={{1,0},{0,1},{3,2},{2,3},{5,4},{4,5},{7,6},{6,7},{9,8},{8,9},{11,10... | collective-permute-start | bytes 983048 | tf_op jit(solution)/shard_map/ppermute | solution.py:383
  19.3 1.3 %collective-permute-done.6.refs_2_ = bf16[64,2560]{1,0:T(8,128)(2,1)S(1)} collective-permute-done((bf16[64,2560]{1,0:T(8,128)(2,1)S(1)}, bf16[64,2560]{1,0:T(8,128)(2,1)S(1)}, u32[]{:S(2)}, u32[]{:S(2)}) %collective-permute-start.6) | collective-permute-done | bytes 327712 | tf_op jit(solution)/shard_map/ppermute | solution.py:383
  20.5 4.3 %attend.1 = (f32[32,2688]{1,0:T(8,128)S(1)}, f32[32,2688]{1,0:T(8,128)S(1)}, bf16[32,2688]{1,0:T(8,128)(2,1)S(1)}, bf16[32,2688]{1,0:T(8,128)(2,1)S(1)}) custom-call(f32[1,640]{1,0:T(1,128)S(1)} %get-tuple-element.22.refs_0_, bf16[64,2560]{1,0:T(8,128)(2,1)S(1)} %merge.12.refs_1_, bf16[64,2560]{1,0:T(8,128)(2,1)S(1)} %collective-permute-done.6.refs_2_, ...), custom_call_target="tpu_custom_call" | custom-call | flops 838860800 | bytes 6553600 | tf_op jit(solution)/shard_map/attend/pallas_call | solution.py:146
  24.8 0.4 %collective-permute-start.8 = (bf16[32,2688]{1,0:T(8,128)(2,1)S(1)}, bf16[32,2688]{1,0:T(8,128)(2,1)S(1)}, u32[]{:S(2)}, u32[]{:S(2)}) collective-permute-start(bf16[32,2688]{1,0:T(8,128)(2,1)S(1)} %get-tuple-element.29), channel_id=1, source_target_pairs={{0,1},{1,0},{2,3},{3,2},{4,5},{5,4},{6,7},{7,6},{8,9},{9,8},{10,11... | collective-permute-start | bytes 516104 | tf_op jit(solution)/shard_map/ppermute | solution.py:383
  25.3 0.1 collective-permute-start.7
  25.4 0.9 %collective-permute-done.8.refs_1_ = bf16[32,2688]{1,0:T(8,128)(2,1)S(1)} collective-permute-done((bf16[32,2688]{1,0:T(8,128)(2,1)S(1)}, bf16[32,2688]{1,0:T(8,128)(2,1)S(1)}, u32[]{:S(2)}, u32[]{:S(2)}) %collective-permute-start.8) | collective-permute-done | bytes 172064 | tf_op jit(solution)/shard_map/ppermute | solution.py:383
  26.3 0.3 merge.14
  26.6 0.4 collective-permute-start.10
  27.0 0.3 merge.13
  27.3 0.7 %collective-permute-start.11 = (bf16[16,2688]{1,0:T(8,128)(2,1)S(1)}, bf16[16,2688]{1,0:T(8,128)(2,1)S(1)}, u32[]{:S(2)}, u32[]{:S(2)}) collective-permute-start(bf16[16,2688]{1,0:T(8,128)(2,1)S(1)} %get-tuple-element.33), channel_id=1, source_target_pairs={{0,4},{1,1},{2,6},{3,3},{4,0},{5,5},{6,2},{7,7},{8,12},{9,9},{10,1... | collective-permute-start | bytes 258056 | tf_op jit(solution)/shard_map/ppermute | solution.py:383
  27.9 1.2 %collective-permute-start.9 = (bf16[16,2688]{1,0:T(8,128)(2,1)S(1)}, bf16[16,2688]{1,0:T(8,128)(2,1)S(1)}, u32[]{:S(2)}, u32[]{:S(2)}) collective-permute-start(bf16[16,2688]{1,0:T(8,128)(2,1)S(1)} %get-tuple-element.30), channel_id=1, source_target_pairs={{0,8},{1,3},{2,10},{3,1},{4,12},{5,7},{6,14},{7,5},{8,0},{9,11},{1... | collective-permute-start | bytes 258056 | tf_op jit(solution)/shard_map/ppermute | solution.py:383
  29.2 0.8 %collective-permute-done.10.refs_1_.refs_3_ = bf16[16,2688]{1,0:T(8,128)(2,1)S(1)} collective-permute-done((bf16[16,2688]{1,0:T(8,128)(2,1)S(1)}, bf16[16,2688]{1,0:T(8,128)(2,1)S(1)}, u32[]{:S(2)}, u32[]{:S(2)}) %collective-permute-start.10) | collective-permute-done | bytes 86048 | tf_op jit(solution)/shard_map/ppermute | solution.py:383
  30.0 0.2 merge.15
  30.2 1.1 %collective-permute-done.9.refs_1_.refs_4_ = bf16[16,2688]{1,0:T(8,128)(2,1)S(1)} collective-permute-done((bf16[16,2688]{1,0:T(8,128)(2,1)S(1)}, bf16[16,2688]{1,0:T(8,128)(2,1)S(1)}, u32[]{:S(2)}, u32[]{:S(2)}) %collective-permute-start.9) | collective-permute-done | bytes 86048 | tf_op jit(solution)/shard_map/ppermute | solution.py:383
  31.3 0.2 merge.16
  31.5 1.9 %collective-permute-start.13 = (bf16[8,2688]{1,0:T(8,128)(2,1)S(1)}, bf16[8,2688]{1,0:T(8,128)(2,1)S(1)}, u32[]{:S(2)}, u32[]{:S(2)}) collective-permute-start(bf16[8,2688]{1,0:T(8,128)(2,1)S(1)} %get-tuple-element.37), channel_id=1, source_target_pairs={{0,0},{1,9},{2,2},{3,11},{4,4},{5,13},{6,6},{7,15},{8,8},{9,1},{10... | collective-permute-start | bytes 129032 | tf_op jit(solution)/shard_map/ppermute | solution.py:383
  33.5 2.8 %collective-permute-start.14 = (bf16[8,2688]{1,0:T(8,128)(2,1)S(1)}, bf16[8,2688]{1,0:T(8,128)(2,1)S(1)}, u32[]{:S(2)}, u32[]{:S(2)}) collective-permute-start(bf16[8,2688]{1,0:T(8,128)(2,1)S(1)} %get-tuple-element.38), channel_id=1, source_target_pairs={{0,2},{1,5},{2,0},{3,7},{4,6},{5,1},{6,4},{7,3},{8,10},{9,13},{10,... | collective-permute-start | bytes 129032 | tf_op jit(solution)/shard_map/ppermute | solution.py:383
  36.3 2.7 %collective-permute-start.12 = (bf16[8,2688]{1,0:T(8,128)(2,1)S(1)}, bf16[8,2688]{1,0:T(8,128)(2,1)S(1)}, u32[]{:S(2)}, u32[]{:S(2)}) collective-permute-start(bf16[8,2688]{1,0:T(8,128)(2,1)S(1)} %get-tuple-element.36), channel_id=1, source_target_pairs={{0,0},{1,13},{2,2},{3,15},{4,4},{5,9},{6,6},{7,11},{8,8},{9,5},{10... | collective-permute-start | bytes 129032 | tf_op jit(solution)/shard_map/ppermute | solution.py:383
  39.0 3.9 %collective-permute-done.12.refs_1_ = bf16[8,2688]{1,0:T(8,128)(2,1)S(1)} collective-permute-done((bf16[8,2688]{1,0:T(8,128)(2,1)S(1)}, bf16[8,2688]{1,0:T(8,128)(2,1)S(1)}, u32[]{:S(2)}, u32[]{:S(2)}) %collective-permute-start.12) | collective-permute-done | bytes 43040 | tf_op jit(solution)/shard_map/ppermute | solution.py:383
  42.9 0.9 %merge.17 = bf16[8,2560]{1,0:T(8,128)(2,1)} custom-call(f32[8,2688]{1,0:T(8,128)S(1)} %get-tuple-element.35.refs_0_, bf16[8,2688]{1,0:T(8,128)(2,1)S(1)} %collective-permute-done.12.refs_1_, bf16[8,2688]{1,0:T(8,128)(2,1)S(1)} %collective-permute-done.13.refs_2_, bf16[8,2688]{1,0:T(8,128)(2,1)S(1)} %collective-permute-done.14.refs_3_), custom_call_target="tpu_custom_call" | custom-call | flops 344064 | bytes 344064 | tf_op jit(solution)/shard_map/merge/pallas_call | solution.py:360
  (11 shorter events, 0.1 us)
Async XLA Ops:
  0.0 9.1 %collective-permute-start.1 = (bf16[8,2560]{1,0:T(8,128)(2,1)}, bf16[8,2560]{1,0:T(8,128)(2,1)S(1)}, u32[]{:S(2)}, u32[]{:S(2)}) collective-permute-start(bf16[8,2560]{1,0:T(8,128)(2,1)} %refs_0_.3), channel_id=1, source_target_pairs={{2,0},{13,1},{0,2},{15,3},{6,4},{9,5},{4,6},{11,7},{10,8},{5,9},{8... | collective-permute-start | bytes 122888 | tf_op jit(solution)/shard_map/ppermute | solution.py:383
  4.2 4.9 %collective-permute-start = (bf16[8,2560]{1,0:T(8,128)(2,1)}, bf16[8,2560]{1,0:T(8,128)(2,1)S(1)}, u32[]{:S(2)}, u32[]{:S(2)}) collective-permute-start(bf16[8,2560]{1,0:T(8,128)(2,1)} %refs_0_.3), channel_id=1, source_target_pairs={{0,0},{5,1},{2,2},{7,3},{4,4},{1,5},{6,6},{3,7},{8,8},{13,9},{10,1... | collective-permute-start | bytes 122888 | tf_op jit(solution)/shard_map/ppermute | solution.py:383
  6.1 7.2 %collective-permute-start.2 = (bf16[8,2560]{1,0:T(8,128)(2,1)}, bf16[8,2560]{1,0:T(8,128)(2,1)S(1)}, u32[]{:S(2)}, u32[]{:S(2)}) collective-permute-start(bf16[8,2560]{1,0:T(8,128)(2,1)} %refs_0_.3), channel_id=1, source_target_pairs={{0,0},{9,1},{2,2},{11,3},{4,4},{13,5},{6,6},{15,7},{8,8},{1,9},{10... | collective-permute-start | bytes 122888 | tf_op jit(solution)/shard_map/ppermute | solution.py:383
  8.3 0.8 %copy-start = (bf16[8,2560]{1,0:T(8,128)(2,1)S(1)}, bf16[8,2560]{1,0:T(8,128)(2,1)}, u32[]{:S(2)}) copy-start(bf16[8,2560]{1,0:T(8,128)(2,1)} %refs_0_.3) | copy-start | bytes 122884
  13.2 4.9 %collective-permute-start.4 = (bf16[16,2560]{1,0:T(8,128)(2,1)S(1)}, bf16[16,2560]{1,0:T(8,128)(2,1)S(1)}, u32[]{:S(2)}, u32[]{:S(2)}) collective-permute-start(bf16[16,2560]{1,0:T(8,128)(2,1)S(1)} %merge.11.refs_1_), channel_id=1, source_target_pairs={{8,0},{3,1},{10,2},{1,3},{12,4},{7,5},{14,6},{5,7},{0,8},{11,9},{2... | collective-permute-start | bytes 245768 | tf_op jit(solution)/shard_map/ppermute | solution.py:383
  13.3 4.9 %collective-permute-start.5 = (bf16[16,2560]{1,0:T(8,128)(2,1)S(1)}, bf16[16,2560]{1,0:T(8,128)(2,1)S(1)}, u32[]{:S(2)}, u32[]{:S(2)}) collective-permute-start(bf16[16,2560]{1,0:T(8,128)(2,1)S(1)} %merge.10.refs_2_.refs_0_.refs_4_), channel_id=1, source_target_pairs={{4,0},{1,1},{6,2},{3,3},{0,4},{5,5},{2,6},{7,7},{12,8},{9,9},{14,1... | collective-permute-start | bytes 245768 | tf_op jit(solution)/shard_map/ppermute | solution.py:383
  13.9 4.2 %collective-permute-start.3 = (bf16[16,2560]{1,0:T(8,128)(2,1)S(1)}, bf16[16,2560]{1,0:T(8,128)(2,1)S(1)}, u32[]{:S(2)}, u32[]{:S(2)}) collective-permute-start(bf16[16,2560]{1,0:T(8,128)(2,1)S(1)} %merge.10.refs_2_.refs_0_.refs_4_), channel_id=1, source_target_pairs={{12,0},{3,1},{14,2},{1,3},{8,4},{7,5},{10,6},{5,7},{4,8},{11,9},{6... | collective-permute-start | bytes 245768 | tf_op jit(solution)/shard_map/ppermute | solution.py:383
  18.2 2.3 %collective-permute-start.6 = (bf16[64,2560]{1,0:T(8,128)(2,1)S(1)}, bf16[64,2560]{1,0:T(8,128)(2,1)S(1)}, u32[]{:S(2)}, u32[]{:S(2)}) collective-permute-start(bf16[64,2560]{1,0:T(8,128)(2,1)S(1)} %merge.12.refs_1_), channel_id=1, source_target_pairs={{1,0},{0,1},{3,2},{2,3},{5,4},{4,5},{7,6},{6,7},{9,8},{8,9},{11,10... | collective-permute-start | bytes 983048 | tf_op jit(solution)/shard_map/ppermute | solution.py:383
  24.8 1.5 %collective-permute-start.8 = (bf16[32,2688]{1,0:T(8,128)(2,1)S(1)}, bf16[32,2688]{1,0:T(8,128)(2,1)S(1)}, u32[]{:S(2)}, u32[]{:S(2)}) collective-permute-start(bf16[32,2688]{1,0:T(8,128)(2,1)S(1)} %get-tuple-element.29), channel_id=1, source_target_pairs={{0,1},{1,0},{2,3},{3,2},{4,5},{5,4},{6,7},{7,6},{8,9},{9,8},{10,11... | collective-permute-start | bytes 516104 | tf_op jit(solution)/shard_map/ppermute | solution.py:383
  25.3 1.7 %collective-permute-start.7 = (bf16[32,2688]{1,0:T(8,128)(2,1)S(1)}, bf16[32,2688]{1,0:T(8,128)(2,1)S(1)}, u32[]{:S(2)}, u32[]{:S(2)}) collective-permute-start(bf16[32,2688]{1,0:T(8,128)(2,1)S(1)} %get-tuple-element.26), channel_id=1, source_target_pairs={{0,1},{1,0},{2,3},{3,2},{4,5},{5,4},{6,7},{7,6},{8,9},{9,8},{10,11... | collective-permute-start | bytes 516104 | tf_op jit(solution)/shard_map/ppermute | solution.py:383
  26.6 3.4 %collective-permute-start.10 = (bf16[16,2688]{1,0:T(8,128)(2,1)S(1)}, bf16[16,2688]{1,0:T(8,128)(2,1)S(1)}, u32[]{:S(2)}, u32[]{:S(2)}) collective-permute-start(bf16[16,2688]{1,0:T(8,128)(2,1)S(1)} %get-tuple-element.32), channel_id=1, source_target_pairs={{0,12},{1,3},{2,14},{3,1},{4,8},{5,7},{6,10},{7,5},{8,4},{9,11},{1... | collective-permute-start | bytes 258056 | tf_op jit(solution)/shard_map/ppermute | solution.py:383
  27.3 3.0 %collective-permute-start.11 = (bf16[16,2688]{1,0:T(8,128)(2,1)S(1)}, bf16[16,2688]{1,0:T(8,128)(2,1)S(1)}, u32[]{:S(2)}, u32[]{:S(2)}) collective-permute-start(bf16[16,2688]{1,0:T(8,128)(2,1)S(1)} %get-tuple-element.33), channel_id=1, source_target_pairs={{0,4},{1,1},{2,6},{3,3},{4,0},{5,5},{6,2},{7,7},{8,12},{9,9},{10,1... | collective-permute-start | bytes 258056 | tf_op jit(solution)/shard_map/ppermute | solution.py:383
  27.9 3.4 %collective-permute-start.9 = (bf16[16,2688]{1,0:T(8,128)(2,1)S(1)}, bf16[16,2688]{1,0:T(8,128)(2,1)S(1)}, u32[]{:S(2)}, u32[]{:S(2)}) collective-permute-start(bf16[16,2688]{1,0:T(8,128)(2,1)S(1)} %get-tuple-element.30), channel_id=1, source_target_pairs={{0,8},{1,3},{2,10},{3,1},{4,12},{5,7},{6,14},{7,5},{8,0},{9,11},{1... | collective-permute-start | bytes 258056 | tf_op jit(solution)/shard_map/ppermute | solution.py:383
  31.5 7.4 %collective-permute-start.13 = (bf16[8,2688]{1,0:T(8,128)(2,1)S(1)}, bf16[8,2688]{1,0:T(8,128)(2,1)S(1)}, u32[]{:S(2)}, u32[]{:S(2)}) collective-permute-start(bf16[8,2688]{1,0:T(8,128)(2,1)S(1)} %get-tuple-element.37), channel_id=1, source_target_pairs={{0,0},{1,9},{2,2},{3,11},{4,4},{5,13},{6,6},{7,15},{8,8},{9,1},{10... | collective-permute-start | bytes 129032 | tf_op jit(solution)/shard_map/ppermute | solution.py:383
  33.5 5.5 %collective-permute-start.14 = (bf16[8,2688]{1,0:T(8,128)(2,1)S(1)}, bf16[8,2688]{1,0:T(8,128)(2,1)S(1)}, u32[]{:S(2)}, u32[]{:S(2)}) collective-permute-start(bf16[8,2688]{1,0:T(8,128)(2,1)S(1)} %get-tuple-element.38), channel_id=1, source_target_pairs={{0,2},{1,5},{2,0},{3,7},{4,6},{5,1},{6,4},{7,3},{8,10},{9,13},{10,... | collective-permute-start | bytes 129032 | tf_op jit(solution)/shard_map/ppermute | solution.py:383
  36.3 6.6 %collective-permute-start.12 = (bf16[8,2688]{1,0:T(8,128)(2,1)S(1)}, bf16[8,2688]{1,0:T(8,128)(2,1)S(1)}, u32[]{:S(2)}, u32[]{:S(2)}) collective-permute-start(bf16[8,2688]{1,0:T(8,128)(2,1)S(1)} %get-tuple-element.36), channel_id=1, source_target_pairs={{0,0},{1,13},{2,2},{3,15},{4,4},{5,9},{6,6},{7,11},{8,8},{9,5},{10... | collective-permute-start | bytes 129032 | tf_op jit(solution)/shard_map/ppermute | solution.py:383

commit v9 on v6

--- a/solution.py
+++ b/solution.py
@@ -58,9 +58,8 @@
     rows = tile * len(outs)
     line_rows = outs[0].shape[0]
     wide = pack * HD
-    lane = lanes(rows)
     contract_last = (((1,), (1,)), ((), ()))
-    bias = bias_ref[...]
+    contract_first = (((0,), (0,)), ((), ()))
     mine = [lax.broadcasted_iota(jnp.int32, (rows, wide), 1) // HD == k for k in range(pack)]
 
     def row_tile(r, carry):
@@ -79,34 +78,34 @@
                 if pack > 1:
                     zero = jnp.zeros_like(q)
                     q = jnp.concatenate([jnp.where(m, q, zero) for m in mine], axis=0)
-                return lax.dot_general(q, k_ref[:, cols], contract_last, preferred_element_type=F32)
-
-            tops = top_acc[...]
-            masses = mass_acc[...]
+                return lax.dot_general(k_ref[:, cols], q, contract_last, preferred_element_type=F32)
+
             ahead = scores(0)
             for i in range(group):
                 score = ahead
                 if i + 1 < group:
                     ahead = scores(i + 1)
+                bias = jnp.concatenate([bias_ref[...]] * (pack * rows // STAT), axis=1)
                 score = score * scale + bias
-                top = jnp.max(score, axis=1, keepdims=True).astype(BF16).astype(F32)
+                top = jnp.max(score, axis=0, keepdims=True).astype(BF16).astype(F32)
                 score = jnp.exp2(score - top)
-                mass = jnp.sum(score, axis=1, keepdims=True)
-                out = jnp.dot(score.astype(BF16), v_ref[:, columns(i)], preferred_element_type=F32)
+                mass = jnp.sum(score, axis=0, keepdims=True)
+                score = score.astype(BF16)
                 for k in range(pack):
                     head = (step * group + i) * pack + k
                     cols = pl.ds(pl.multiple_of(head * HD, HD), HD)
-                    one = out[k * rows : (k + 1) * rows, k * HD : (k + 1) * HD]
+                    part = slice(k * rows, (k + 1) * rows)
+                    one = lax.dot_general(
+                        score[:, part], v_ref[:, cols], contract_first, preferred_element_type=F32
+                    )
                     for p, o_ref in enumerate(outs):
                         o_ref[at, cols] = one[p * tile : (p + 1) * tile].astype(o_ref.dtype)
-                    tops = jnp.where(lane == head, top[k * rows : (k + 1) * rows], tops)
-                    masses = jnp.where(lane == head, mass[k * rows : (k + 1) * rows], masses)
-            top_acc[...] = tops
-            mass_acc[...] = masses
+                    top_acc[pl.ds(head, 1), :] = top[:, part]
+                    mass_acc[pl.ds(head, 1), :] = mass[:, part]
             return carry
 
         lax.fori_loop(0, steps, heads_of, 0)
-        packed = pack_stats(top_acc[...], mass_acc[...])
+        packed = pack_stats(top_acc[...].T, mass_acc[...].T)
         for p, o_ref in enumerate(outs):
             width = o_ref.shape[1]
             o_ref[at, width - STAT :] = packed[p * tile : (p + 1) * tile].astype(o_ref.dtype)
@@ -136,7 +135,7 @@
         in_specs=[pl.BlockSpec(memory_space=pltpu.VMEM)] * (n + 3),
         out_specs=[pl.BlockSpec(memory_space=pltpu.VMEM)] * m,
         out_shape=[jax.ShapeDtypeStruct((rows, width), kind) for kind in kinds],
-        scratch_shapes=[pltpu.VMEM((tile * m, STAT), F32)] * 2,
+        scratch_shapes=[pltpu.VMEM((STAT, tile * m), F32)] * 2,
         compiler_params=pltpu.CompilerParams(vmem_limit_bytes=40 * 1024 * 1024),
         cost_estimate=pl.CostEstimate(
             flops=4 * m * rows * keys.shape[0] * columns,
@@ -150,7 +149,7 @@
 def load(cached, fresh, victims, queries, after):
     cache_rows, columns = cached[0].shape
     tok = fresh[0].shape[0]
-    padded = cache_rows + -(-tok // BLK) * BLK
+    padded = cache_rows + -(-tok // 16) * 16
     n = len(cached)
 
     def body(*refs):
@@ -178,9 +177,9 @@
             hits = jnp.where(ids_ref[...] == first + block, 1.0, 0.0)
             hit = jnp.max(hits, axis=1, keepdims=True)
             gone = jnp.where(hit > 0.0, NEG, 0.0)
-            bias_ref[:, block * BLK : (block + 1) * BLK] = jnp.broadcast_to(gone, (1, BLK))
-        token = lax.broadcasted_iota(jnp.int32, (1, padded - cache_rows), 1)
-        bias_ref[:, cache_rows:] = jnp.where(token < tok, 0.0, NEG)
+            bias_ref[block * BLK : (block + 1) * BLK, :] = jnp.broadcast_to(gone, (BLK, STAT))
+        token = lax.broadcasted_iota(jnp.int32, (padded - cache_rows, STAT), 0)
+        bias_ref[cache_rows:, :] = jnp.where(token < tok, 0.0, NEG)
         for copy, tail, out in zip(small, tails, outs):
             copy.wait()
             zeros = jnp.zeros((padded - cache_rows - tok, columns), F32)
@@ -196,7 +195,7 @@
         in_specs=[in_hbm] * len(held) + [pl.BlockSpec(memory_space=pl.ANY)],
         out_specs=[pl.BlockSpec(memory_space=pltpu.VMEM)] * (n + 2),
         out_shape=[jax.ShapeDtypeStruct((padded, columns), BF16)] * n
-        + [jax.ShapeDtypeStruct((1, padded), F32), jax.ShapeDtypeStruct(queries.shape, BF16)],
+        + [jax.ShapeDtypeStruct((padded, STAT), F32), jax.ShapeDtypeStruct(queries.shape, BF16)],
         scratch_shapes=[pltpu.VMEM(x.shape, BF16) for x in fresh]
         + [pltpu.VMEM(victims.shape, jnp.int32), pltpu.SemaphoreType.DMA((2, n + 1))],
         compiler_params=pltpu.CompilerParams(vmem_limit_bytes=24 * 1024 * 1024),
@@ -229,17 +228,17 @@
     return lambda cols: ref[(*index, slice(None), cols)].astype(F32)
 
 
-def merge_rows(ins, heads, pieces, kinds):
-    rows, width = ins[0].shape
-    per = rows // pieces
-
-    def body(*refs):
-        outs = refs[len(ins) :]
+def merge_rows(ins, heads, cuts, rows, after=()):
+    width = ins[0].shape[1]
+
+    def body(*refs):
+        outs = refs[len(ins) + len(after) :]
         for cols, total in merged([getter(r) for r in refs[: len(ins)]], heads, False):
-            for j, out in enumerate(outs):
-                out[:, cols] = total[j * per : (j + 1) * per].astype(out.dtype)
-
-    return call_merge(body, ins, [jax.ShapeDtypeStruct((per, width), kind) for kind in kinds])
+            for (start, _), out in zip(cuts, outs):
+                out[:, cols] = total[start : start + rows].astype(out.dtype)
+
+    shapes = [jax.ShapeDtypeStruct((rows, width), kind) for _, kind in cuts]
+    return call_merge(body, ins, shapes, after)
 
 
 def finish(ins, heads):
@@ -284,6 +283,7 @@
     shape = factors(members)
     a_n, b_n, c_n = shape
     heads = queries.shape[1] // HD
+    tok = queries.shape[0]
 
     def fetch(x, *by):
         return lax.ppermute(x, "seq", partner_perm(shape, by, False))
@@ -304,17 +304,22 @@
     kinds = [F32] * b_n + [BF16] * (b_n * (c_n - 1))
     sums = attend(planes, b_n, kinds, keys, values, bias)
 
-    def over_cores(b, kind):
-        got = [give(sums[c * b_n + b], 0, 0, c) for c in range(1, c_n)]
-        return merge_rows([sums[b]] + got, heads, a_n, [kind] * a_n)
-
-    got = [[give(x, 0, b, 0) for x in over_cores(b, BF16)] for b in range(1, b_n)]
-    own = over_cores(0, F32)
-    total = [[own[a]] + [pieces[a] for pieces in got] for a in range(a_n)]
-    last = [
-        give(merge_rows(total[a], heads, 1, [BF16])[0], a, 0, 0) for a in far_first
-    ]
-    return finish([*merge_rows(total[0], heads, 1, [F32]), *last], heads)
+    def over_cores(b, first, kinds, after=()):
+        cuts = [(first + j) * tok for j in range(len(kinds))]
+        return merge_rows([sums[b]] + back[b], heads, list(zip(cuts, kinds)), tok, after)
+
+    back = [[give(sums[c * b_n + b], 0, 0, c) for c in range(1, c_n)] for b in range(b_n)]
+    far = [over_cores(b, 1, [BF16] * (a_n - 1)) for b in range(1, b_n)]
+    far = [[give(x, 0, b, 0) for x in pieces[::-1]] for b, pieces in enumerate(far, 1)]
+    own = over_cores(0, 0, [F32] * a_n)
+    total, last = [], []
+    for j, a in enumerate(range(a_n - 1, 0, -1)):
+        total += merge_rows([own[a]] + [x[j] for x in far], heads, [(0, BF16)], tok)
+        last.append(give(total[-1], a, 0, 0))
+    near = [over_cores(b, 0, [BF16], total[:1])[0] for b in range(1, b_n)]
+    near = [give(x, 0, b, 0) for b, x in enumerate(near, 1)]
+    first = merge_rows([own[0]] + near, heads, [(0, F32)], tok)[0] if near else own[0]
+    return finish([first] + last, heads)
 
 
 def solution(mesh):

time: 36.1 us -> 37.2 us (1.030)
  waiting for transfers between devices: 6.78 us -> 7.43 us
  starting transfers between devices: 20 us -> 20.5 us
    ppermute x9, waiting for transfers between devices: 3.23 us -> 3.87 us  [give(): return lax.ppermute(x, 'seq', partner_perm(shape, by, True))]
    ppermute x9, starting transfers between devices: 9.28 us -> 9.75 us  [give(): return lax.ppermute(x, 'seq', partner_perm(shape, by, True))]
    pallas_call x8 -> x9, Pallas kernels: 2.07 us -> 2.17 us  [call_merge(): pl.pallas_call(body, in_specs=[pl.BlockSpec(memory_space=pltpu.VMEM)] * l...]
  transfers between devices with their start and end apart: 17 -> 17, of which waited for: 5 -> 7; matrix products, arithmetic and copies ran while one was open for 0% -> 0% of each run, Pallas kernels for 11% -> 10%
where the time goes in v9:
time: 37.2 us; the launch traced here: 37.1 us
  starting transfers between devices  20.5 us (55%)
  Pallas kernels  9.03 us (24%)
  waiting for transfers between devices  7.43 us (20%)
    ppermute x8, starting transfers between devices, fetch(): return lax.ppermute(x, 'seq', partner_perm(shape, by, False))  10.7 us
    ppermute x9, starting transfers between devices, give(): return lax.ppermute(x, 'seq', partner_perm(shape, by, True))  9.75 us
    pallas_call x1, Pallas kernels, attend(): pl.pallas_call(body, in_specs=[pl.BlockSpec(memory_space=pltpu.VMEM)] * (...  4.22 us
    ppermute x9, waiting for transfers between devices, give(): return lax.ppermute(x, 'seq', partner_perm(shape, by, True))  3.87 us
    ppermute x8, waiting for transfers between devices, fetch(): return lax.ppermute(x, 'seq', partner_perm(shape, by, False))  3.55 us
    pallas_call x1, Pallas kernels, load(): pl.pallas_call(body, in_specs=[in_hbm] * len(held) + [pl.BlockSpec(memory...  2.65 us
    pallas_call x9, Pallas kernels, call_merge(): pl.pallas_call(body, in_specs=[pl.BlockSpec(memory_space=pltpu.VMEM)] * l...  2.17 us
  transfers between devices with their start and end apart: 17, of which 7 were waited for; matrix products, arithmetic and copies ran while one was open for 0% of the time, Pallas kernels for 10%

profile of v9, /device:TPU:0, one launch (start us, length us, event | category | flops | bytes accessed | tf_op | source)
XLA Modules:
  0.0 37.1 jit_solution(3509682657104075121)
XLA Ops:
  0.0 3.0 %collective-permute-start.1 = (bf16[8,2560]{1,0:T(8,128)(2,1)}, bf16[8,2560]{1,0:T(8,128)(2,1)S(1)}, u32[]{:S(2)}, u32[]{:S(2)}) collective-permute-start(bf16[8,2560]{1,0:T(8,128)(2,1)} %refs_5_.1), channel_id=1, source_target_pairs={{4,0},{5,1},{6,2},{7,3},{0,4},{1,5},{2,6},{3,7},{12,8},{13,9},{14,... | collective-permute-start | bytes 122888 | tf_op jit(solution)/shard_map/ppermute | solution.py:289
  3.0 2.5 %collective-permute-start = (bf16[8,2560]{1,0:T(8,128)(2,1)}, bf16[8,2560]{1,0:T(8,128)(2,1)S(1)}, u32[]{:S(2)}, u32[]{:S(2)}) collective-permute-start(bf16[8,2560]{1,0:T(8,128)(2,1)} %refs_5_.1), channel_id=1, source_target_pairs={{12,0},{13,1},{14,2},{15,3},{8,4},{9,5},{10,6},{11,7},{4,8},{5,9},... | collective-permute-start | bytes 122888 | tf_op jit(solution)/shard_map/ppermute | solution.py:289
  5.5 0.1 collective-permute-start.2
  5.6 1.5 %collective-permute-start.3 = (bf16[8,2560]{1,0:T(8,128)(2,1)}, bf16[8,2560]{1,0:T(8,128)(2,1)S(1)}, u32[]{:S(2)}, u32[]{:S(2)}) collective-permute-start(bf16[8,2560]{1,0:T(8,128)(2,1)} %refs_5_.1), channel_id=1, source_target_pairs={{2,0},{3,1},{0,2},{1,3},{6,4},{7,5},{4,6},{5,7},{10,8},{11,9},{8,1... | collective-permute-start | bytes 122888 | tf_op jit(solution)/shard_map/ppermute | solution.py:289
  7.1 0.5 %collective-permute-start.4 = (bf16[8,2560]{1,0:T(8,128)(2,1)S(1)}, bf16[8,2560]{1,0:T(8,128)(2,1)S(1)}, u32[]{:S(2)}, u32[]{:S(2)}) collective-permute-start(bf16[8,2560]{1,0:T(8,128)(2,1)S(1)} %collective-permute-done.1.refs_1_), channel_id=1, source_target_pairs={{2,0},{3,1},{0,2},{1,3},{6,4},{7,5},{4,6},{5,7},{10,8},{11,9},{8,1... | collective-permute-start | bytes 122888 | tf_op jit(solution)/shard_map/ppermute | solution.py:289
  7.6 1.9 %collective-permute-done.refs_6_.refs_3_ = bf16[8,2560]{1,0:T(8,128)(2,1)S(1)} collective-permute-done((bf16[8,2560]{1,0:T(8,128)(2,1)}, bf16[8,2560]{1,0:T(8,128)(2,1)S(1)}, u32[]{:S(2)}, u32[]{:S(2)}) %collective-permute-start) | collective-permute-done | bytes 40992 | tf_op jit(solution)/shard_map/ppermute | solution.py:289
  9.6 1.5 %collective-permute-start.6 = (bf16[8,2560]{1,0:T(8,128)(2,1)S(1)}, bf16[8,2560]{1,0:T(8,128)(2,1)S(1)}, u32[]{:S(2)}, u32[]{:S(2)}) collective-permute-start(bf16[8,2560]{1,0:T(8,128)(2,1)S(1)} %collective-permute-done.refs_6_.refs_3_), channel_id=1, source_target_pairs={{2,0},{3,1},{0,2},{1,3},{6,4},{7,5},{4,6},{5,7},{10,8},{11,9},{8,1... | collective-permute-start | bytes 122888 | tf_op jit(solution)/shard_map/ppermute | solution.py:289
  11.1 1.5 %collective-permute-start.5 = (bf16[8,2560]{1,0:T(8,128)(2,1)S(1)}, bf16[8,2560]{1,0:T(8,128)(2,1)S(1)}, u32[]{:S(2)}, u32[]{:S(2)}) collective-permute-start(bf16[8,2560]{1,0:T(8,128)(2,1)S(1)} %collective-permute-done.2.refs_2_), channel_id=1, source_target_pairs={{2,0},{3,1},{0,2},{1,3},{6,4},{7,5},{4,6},{5,7},{10,8},{11,9},{8,1... | collective-permute-start | bytes 122888 | tf_op jit(solution)/shard_map/ppermute | solution.py:289
  12.6 2.6 %load.1 = (bf16[528,2560]{1,0:T(8,128)(2,1)S(1)}, bf16[528,2560]{1,0:T(8,128)(2,1)S(1)}, f32[528,128]{1,0:T(8,128)S(1)}, bf16[8,2560]{1,0:T(8,128)(2,1)S(1)}) custom-call(bf16[512,2560]{1,0:T(8,128)(2,1)} %refs_0_.1, bf16[512,2560]{1,0:T(8,128)(2,1)} %refs_1_.1, bf16[8,2560]{1,0:T(8,128)(2,1)} %refs_2_.1, bf16[8,2560]{1,0:T(8,128)(2,1)} %refs_3_.1, ...), custom_call_target="tpu_custom_call" | custom-call | bytes 10485760 | tf_op jit(solution)/shard_map/load/pallas_call | solution.py:193
  15.4 1.6 %collective-permute-done.7.refs_2_ = bf16[64,2560]{1,0:T(8,128)(2,1)S(1)} collective-permute-done((bf16[64,2560]{1,0:T(8,128)(2,1)S(1)}, bf16[64,2560]{1,0:T(8,128)(2,1)S(1)}, u32[]{:S(2)}, u32[]{:S(2)}) %collective-permute-start.7) | collective-permute-done | bytes 327712 | tf_op jit(solution)/shard_map/ppermute | solution.py:289
  17.0 4.2 %attend.1 = (f32[32,2688]{1,0:T(8,128)S(1)}, f32[32,2688]{1,0:T(8,128)S(1)}, bf16[32,2688]{1,0:T(8,128)(2,1)S(1)}, bf16[32,2688]{1,0:T(8,128)(2,1)S(1)}) custom-call(f32[528,128]{1,0:T(8,128)S(1)} %get-tuple-element.20.refs_0_, bf16[64,2560]{1,0:T(8,128)(2,1)S(1)} %merge.9.refs_1_, bf16[64,2560]{1,0:T(8,128)(2,1)S(1)} %collective-permute-done.7.refs_2_, ...), custom_call_target="tpu_custom_call" | custom-call | flops 692060160 | bytes 5406720 | tf_op jit(solution)/shard_map/attend/pallas_call | solution.py:133
  21.2 0.2 collective-permute-start.9
  21.4 0.4 collective-permute-start.8
  21.8 0.9 %collective-permute-done.9.refs_1_ = bf16[32,2688]{1,0:T(8,128)(2,1)S(1)} collective-permute-done((bf16[32,2688]{1,0:T(8,128)(2,1)S(1)}, bf16[32,2688]{1,0:T(8,128)(2,1)S(1)}, u32[]{:S(2)}, u32[]{:S(2)}) %collective-permute-start.9) | collective-permute-done | bytes 172064 | tf_op jit(solution)/shard_map/ppermute | solution.py:292
  22.7 0.2 merge.11
  22.9 1.4 %collective-permute-start.10 = (bf16[8,2688]{1,0:T(8,128)(2,1)S(1)}, bf16[8,2688]{1,0:T(8,128)(2,1)S(1)}, u32[]{:S(2)}, u32[]{:S(2)}) collective-permute-start(bf16[8,2688]{1,0:T(8,128)(2,1)S(1)} %get-tuple-element.30), channel_id=1, source_target_pairs={{0,2},{1,3},{2,0},{3,1},{4,6},{5,7},{6,4},{7,5},{8,10},{9,11},{10,... | collective-permute-start | bytes 129032 | tf_op jit(solution)/shard_map/ppermute | solution.py:292
  24.3 0.7 %collective-permute-start.13 = (bf16[8,2688]{1,0:T(8,128)(2,1)S(1)}, bf16[8,2688]{1,0:T(8,128)(2,1)S(1)}, u32[]{:S(2)}, u32[]{:S(2)}) collective-permute-start(bf16[8,2688]{1,0:T(8,128)(2,1)S(1)} %get-tuple-element.32), channel_id=1, source_target_pairs={{0,2},{1,3},{2,0},{3,1},{4,6},{5,7},{6,4},{7,5},{8,10},{9,11},{10,... | collective-permute-start | bytes 129032 | tf_op jit(solution)/shard_map/ppermute | solution.py:292
  25.0 1.3 %collective-permute-start.15 = (bf16[8,2688]{1,0:T(8,128)(2,1)S(1)}, bf16[8,2688]{1,0:T(8,128)(2,1)S(1)}, u32[]{:S(2)}, u32[]{:S(2)}) collective-permute-start(bf16[8,2688]{1,0:T(8,128)(2,1)S(1)} %get-tuple-element.34), channel_id=1, source_target_pairs={{0,2},{1,3},{2,0},{3,1},{4,6},{5,7},{6,4},{7,5},{8,10},{9,11},{10,... | collective-permute-start | bytes 129032 | tf_op jit(solution)/shard_map/ppermute | solution.py:292
  26.3 0.3 merge.10
  26.6 0.7 %collective-permute-done.10.refs_1_ = bf16[8,2688]{1,0:T(8,128)(2,1)S(1)} collective-permute-done((bf16[8,2688]{1,0:T(8,128)(2,1)S(1)}, bf16[8,2688]{1,0:T(8,128)(2,1)S(1)}, u32[]{:S(2)}, u32[]{:S(2)}) %collective-permute-start.10) | collective-permute-done | bytes 43040 | tf_op jit(solution)/shard_map/ppermute | solution.py:292
  27.3 0.1 merge.12.refs_2_
  27.4 2.1 %collective-permute-start.12 = (bf16[8,2688]{1,0:T(8,128)(2,1)S(1)}, bf16[8,2688]{1,0:T(8,128)(2,1)S(1)}, u32[]{:S(2)}, u32[]{:S(2)}) collective-permute-start(bf16[8,2688]{1,0:T(8,128)(2,1)S(1)} %merge.12.refs_2_), channel_id=1, source_target_pairs={{0,12},{1,13},{2,14},{3,15},{4,8},{5,9},{6,10},{7,11},{8,4},{9,5},... | collective-permute-start | bytes 129032 | tf_op jit(solution)/shard_map/ppermute | solution.py:292
  29.5 0.1 merge.13
  29.7 1.2 %collective-permute-start.11 = (bf16[8,2688]{1,0:T(8,128)(2,1)S(1)}, bf16[8,2688]{1,0:T(8,128)(2,1)S(1)}, u32[]{:S(2)}, u32[]{:S(2)}) collective-permute-start(bf16[8,2688]{1,0:T(8,128)(2,1)S(1)} %merge.13), channel_id=1, source_target_pairs={{0,2},{1,3},{2,0},{3,1},{4,6},{5,7},{6,4},{7,5},{8,10},{9,11},{10,... | collective-permute-start | bytes 129032 | tf_op jit(solution)/shard_map/ppermute | solution.py:292
  30.8 0.1 merge.15
  31.0 0.1 collective-permute-start.14
  31.1 0.1 merge.16
  31.2 2.5 %collective-permute-start.16 = (bf16[8,2688]{1,0:T(8,128)(2,1)S(1)}, bf16[8,2688]{1,0:T(8,128)(2,1)S(1)}, u32[]{:S(2)}, u32[]{:S(2)}) collective-permute-start(bf16[8,2688]{1,0:T(8,128)(2,1)S(1)} %merge.16), channel_id=1, source_target_pairs={{0,4},{1,5},{2,6},{3,7},{4,0},{5,1},{6,2},{7,3},{8,12},{9,13},{10,... | collective-permute-start | bytes 129032 | tf_op jit(solution)/shard_map/ppermute | solution.py:292
  33.7 0.1 collective-permute-done.11.refs_1_
  33.8 0.1 merge.14.refs_0_
  33.9 2.2 %collective-permute-done.14.refs_2_ = bf16[8,2688]{1,0:T(8,128)(2,1)S(1)} collective-permute-done((bf16[8,2688]{1,0:T(8,128)(2,1)S(1)}, bf16[8,2688]{1,0:T(8,128)(2,1)S(1)}, u32[]{:S(2)}, u32[]{:S(2)}) %collective-permute-start.14) | collective-permute-done | bytes 43040 | tf_op jit(solution)/shard_map/ppermute | solution.py:292
  36.2 0.9 %merge.17 = bf16[8,2560]{1,0:T(8,128)(2,1)} custom-call(f32[8,2688]{1,0:T(8,128)S(1)} %merge.14.refs_0_, bf16[8,2688]{1,0:T(8,128)(2,1)S(1)} %collective-permute-done.12.refs_1_, bf16[8,2688]{1,0:T(8,128)(2,1)S(1)} %collective-permute-done.14.refs_2_, bf16[8,2688]{1,0:T(8,128)(2,1)S(1)} %collective-permute-done.16.refs_3_), custom_call_target="tpu_custom_call" | custom-call | flops 344064 | bytes 344064 | tf_op jit(solution)/shard_map/merge/pallas_call | solution.py:269
  (13 shorter events, 0.2 us)
Async XLA Ops:
  0.0 7.1 %collective-permute-start.1 = (bf16[8,2560]{1,0:T(8,128)(2,1)}, bf16[8,2560]{1,0:T(8,128)(2,1)S(1)}, u32[]{:S(2)}, u32[]{:S(2)}) collective-permute-start(bf16[8,2560]{1,0:T(8,128)(2,1)} %refs_5_.1), channel_id=1, source_target_pairs={{4,0},{5,1},{6,2},{7,3},{0,4},{1,5},{2,6},{3,7},{12,8},{13,9},{14,... | collective-permute-start | bytes 122888 | tf_op jit(solution)/shard_map/ppermute | solution.py:289
  3.0 6.5 %collective-permute-start = (bf16[8,2560]{1,0:T(8,128)(2,1)}, bf16[8,2560]{1,0:T(8,128)(2,1)S(1)}, u32[]{:S(2)}, u32[]{:S(2)}) collective-permute-start(bf16[8,2560]{1,0:T(8,128)(2,1)} %refs_5_.1), channel_id=1, source_target_pairs={{12,0},{13,1},{14,2},{15,3},{8,4},{9,5},{10,6},{11,7},{4,8},{5,9},... | collective-permute-start | bytes 122888 | tf_op jit(solution)/shard_map/ppermute | solution.py:289
  5.5 5.6 %collective-permute-start.2 = (bf16[8,2560]{1,0:T(8,128)(2,1)}, bf16[8,2560]{1,0:T(8,128)(2,1)S(1)}, u32[]{:S(2)}, u32[]{:S(2)}) collective-permute-start(bf16[8,2560]{1,0:T(8,128)(2,1)} %refs_5_.1), channel_id=1, source_target_pairs={{8,0},{9,1},{10,2},{11,3},{12,4},{13,5},{14,6},{15,7},{0,8},{1,9},... | collective-permute-start | bytes 122888 | tf_op jit(solution)/shard_map/ppermute | solution.py:289
  5.6 9.6 %collective-permute-start.3 = (bf16[8,2560]{1,0:T(8,128)(2,1)}, bf16[8,2560]{1,0:T(8,128)(2,1)S(1)}, u32[]{:S(2)}, u32[]{:S(2)}) collective-permute-start(bf16[8,2560]{1,0:T(8,128)(2,1)} %refs_5_.1), channel_id=1, source_target_pairs={{2,0},{3,1},{0,2},{1,3},{6,4},{7,5},{4,6},{5,7},{10,8},{11,9},{8,1... | collective-permute-start | bytes 122888 | tf_op jit(solution)/shard_map/ppermute | solution.py:289
  7.1 8.1 %collective-permute-start.4 = (bf16[8,2560]{1,0:T(8,128)(2,1)S(1)}, bf16[8,2560]{1,0:T(8,128)(2,1)S(1)}, u32[]{:S(2)}, u32[]{:S(2)}) collective-permute-start(bf16[8,2560]{1,0:T(8,128)(2,1)S(1)} %collective-permute-done.1.refs_1_), channel_id=1, source_target_pairs={{2,0},{3,1},{0,2},{1,3},{6,4},{7,5},{4,6},{5,7},{10,8},{11,9},{8,1... | collective-permute-start | bytes 122888 | tf_op jit(solution)/shard_map/ppermute | solution.py:289
  9.6 5.7 %collective-permute-start.6 = (bf16[8,2560]{1,0:T(8,128)(2,1)S(1)}, bf16[8,2560]{1,0:T(8,128)(2,1)S(1)}, u32[]{:S(2)}, u32[]{:S(2)}) collective-permute-start(bf16[8,2560]{1,0:T(8,128)(2,1)S(1)} %collective-permute-done.refs_6_.refs_3_), channel_id=1, source_target_pairs={{2,0},{3,1},{0,2},{1,3},{6,4},{7,5},{4,6},{5,7},{10,8},{11,9},{8,1... | collective-permute-start | bytes 122888 | tf_op jit(solution)/shard_map/ppermute | solution.py:289
  11.1 4.2 %collective-permute-start.5 = (bf16[8,2560]{1,0:T(8,128)(2,1)S(1)}, bf16[8,2560]{1,0:T(8,128)(2,1)S(1)}, u32[]{:S(2)}, u32[]{:S(2)}) collective-permute-start(bf16[8,2560]{1,0:T(8,128)(2,1)S(1)} %collective-permute-done.2.refs_2_), channel_id=1, source_target_pairs={{2,0},{3,1},{0,2},{1,3},{6,4},{7,5},{4,6},{5,7},{10,8},{11,9},{8,1... | collective-permute-start | bytes 122888 | tf_op jit(solution)/shard_map/ppermute | solution.py:289
  15.3 1.7 %collective-permute-start.7 = (bf16[64,2560]{1,0:T(8,128)(2,1)S(1)}, bf16[64,2560]{1,0:T(8,128)(2,1)S(1)}, u32[]{:S(2)}, u32[]{:S(2)}) collective-permute-start(bf16[64,2560]{1,0:T(8,128)(2,1)S(1)} %merge.9.refs_1_), channel_id=1, source_target_pairs={{1,0},{0,1},{3,2},{2,3},{5,4},{4,5},{7,6},{6,7},{9,8},{8,9},{11,10... | collective-permute-start | bytes 983048 | tf_op jit(solution)/shard_map/ppermute | solution.py:289
  21.2 1.5 %collective-permute-start.9 = (bf16[32,2688]{1,0:T(8,128)(2,1)S(1)}, bf16[32,2688]{1,0:T(8,128)(2,1)S(1)}, u32[]{:S(2)}, u32[]{:S(2)}) collective-permute-start(bf16[32,2688]{1,0:T(8,128)(2,1)S(1)} %get-tuple-element.28), channel_id=1, source_target_pairs={{0,1},{1,0},{2,3},{3,2},{4,5},{5,4},{6,7},{7,6},{8,9},{9,8},{10,11... | collective-permute-start | bytes 516104 | tf_op jit(solution)/shard_map/ppermute | solution.py:292
  21.4 4.9 %collective-permute-start.8 = (bf16[32,2688]{1,0:T(8,128)(2,1)S(1)}, bf16[32,2688]{1,0:T(8,128)(2,1)S(1)}, u32[]{:S(2)}, u32[]{:S(2)}) collective-permute-start(bf16[32,2688]{1,0:T(8,128)(2,1)S(1)} %get-tuple-element.25), channel_id=1, source_target_pairs={{0,1},{1,0},{2,3},{3,2},{4,5},{5,4},{6,7},{7,6},{8,9},{9,8},{10,11... | collective-permute-start | bytes 516104 | tf_op jit(solution)/shard_map/ppermute | solution.py:292
  22.9 4.3 %collective-permute-start.10 = (bf16[8,2688]{1,0:T(8,128)(2,1)S(1)}, bf16[8,2688]{1,0:T(8,128)(2,1)S(1)}, u32[]{:S(2)}, u32[]{:S(2)}) collective-permute-start(bf16[8,2688]{1,0:T(8,128)(2,1)S(1)} %get-tuple-element.30), channel_id=1, source_target_pairs={{0,2},{1,3},{2,0},{3,1},{4,6},{5,7},{6,4},{7,5},{8,10},{9,11},{10,... | collective-permute-start | bytes 129032 | tf_op jit(solution)/shard_map/ppermute | solution.py:292
  24.3 6.5 %collective-permute-start.13 = (bf16[8,2688]{1,0:T(8,128)(2,1)S(1)}, bf16[8,2688]{1,0:T(8,128)(2,1)S(1)}, u32[]{:S(2)}, u32[]{:S(2)}) collective-permute-start(bf16[8,2688]{1,0:T(8,128)(2,1)S(1)} %get-tuple-element.32), channel_id=1, source_target_pairs={{0,2},{1,3},{2,0},{3,1},{4,6},{5,7},{6,4},{7,5},{8,10},{9,11},{10,... | collective-permute-start | bytes 129032 | tf_op jit(solution)/shard_map/ppermute | solution.py:292
  25.0 6.1 %collective-permute-start.15 = (bf16[8,2688]{1,0:T(8,128)(2,1)S(1)}, bf16[8,2688]{1,0:T(8,128)(2,1)S(1)}, u32[]{:S(2)}, u32[]{:S(2)}) collective-permute-start(bf16[8,2688]{1,0:T(8,128)(2,1)S(1)} %get-tuple-element.34), channel_id=1, source_target_pairs={{0,2},{1,3},{2,0},{3,1},{4,6},{5,7},{6,4},{7,5},{8,10},{9,11},{10,... | collective-permute-start | bytes 129032 | tf_op jit(solution)/shard_map/ppermute | solution.py:292
  27.4 6.5 %collective-permute-start.12 = (bf16[8,2688]{1,0:T(8,128)(2,1)S(1)}, bf16[8,2688]{1,0:T(8,128)(2,1)S(1)}, u32[]{:S(2)}, u32[]{:S(2)}) collective-permute-start(bf16[8,2688]{1,0:T(8,128)(2,1)S(1)} %merge.12.refs_2_), channel_id=1, source_target_pairs={{0,12},{1,13},{2,14},{3,15},{4,8},{5,9},{6,10},{7,11},{8,4},{9,5},... | collective-permute-start | bytes 129032 | tf_op jit(solution)/shard_map/ppermute | solution.py:292
  29.7 4.1 %collective-permute-start.11 = (bf16[8,2688]{1,0:T(8,128)(2,1)S(1)}, bf16[8,2688]{1,0:T(8,128)(2,1)S(1)}, u32[]{:S(2)}, u32[]{:S(2)}) collective-permute-start(bf16[8,2688]{1,0:T(8,128)(2,1)S(1)} %merge.13), channel_id=1, source_target_pairs={{0,2},{1,3},{2,0},{3,1},{4,6},{5,7},{6,4},{7,5},{8,10},{9,11},{10,... | collective-permute-start | bytes 129032 | tf_op jit(solution)/shard_map/ppermute | solution.py:292
  31.0 5.1 %collective-permute-start.14 = (bf16[8,2688]{1,0:T(8,128)(2,1)S(1)}, bf16[8,2688]{1,0:T(8,128)(2,1)S(1)}, u32[]{:S(2)}, u32[]{:S(2)}) collective-permute-start(bf16[8,2688]{1,0:T(8,128)(2,1)S(1)} %merge.15), channel_id=1, source_target_pairs={{0,8},{1,9},{2,10},{3,11},{4,12},{5,13},{6,14},{7,15},{8,0},{9,1},... | collective-permute-start | bytes 129032 | tf_op jit(solution)/shard_map/ppermute | solution.py:292
  31.2 4.9 %collective-permute-start.16 = (bf16[8,2688]{1,0:T(8,128)(2,1)S(1)}, bf16[8,2688]{1,0:T(8,128)(2,1)S(1)}, u32[]{:S(2)}, u32[]{:S(2)}) collective-permute-start(bf16[8,2688]{1,0:T(8,128)(2,1)S(1)} %merge.16), channel_id=1, source_target_pairs={{0,4},{1,5},{2,6},{3,7},{4,0},{5,1},{6,2},{7,3},{8,12},{9,13},{10,... | collective-permute-start | bytes 129032 | tf_op jit(solution)/shard_map/ppermute | solution.py:292

commit v10 on v9

--- a/solution.py
+++ b/solution.py
@@ -119,7 +119,7 @@
     rows, columns = planes[0].shape[0] // lines, planes[0].shape[1]
     heads = columns // HD
     pack = 2 if heads % 2 == 0 else 1
-    group = next(g for g in (2, 1) if heads % (g * pack) == 0)
+    group = next(g for g in (10, 5, 4, 3, 2, 1) if heads % (g * pack) == 0)
     tile = next(t for t in (32, 16, rows) if rows % t == 0)
     width = columns + STAT
     scale = math.log2(math.e) / math.sqrt(HD)
@@ -228,17 +228,17 @@
     return lambda cols: ref[(*index, slice(None), cols)].astype(F32)
 
 
-def merge_rows(ins, heads, cuts, rows, after=()):
-    width = ins[0].shape[1]
-
-    def body(*refs):
-        outs = refs[len(ins) + len(after) :]
+def merge_rows(ins, heads, pieces, kinds):
+    rows, width = ins[0].shape
+    per = rows // pieces
+
+    def body(*refs):
+        outs = refs[len(ins) :]
         for cols, total in merged([getter(r) for r in refs[: len(ins)]], heads, False):
-            for (start, _), out in zip(cuts, outs):
-                out[:, cols] = total[start : start + rows].astype(out.dtype)
-
-    shapes = [jax.ShapeDtypeStruct((rows, width), kind) for _, kind in cuts]
-    return call_merge(body, ins, shapes, after)
+            for j, out in enumerate(outs):
+                out[:, cols] = total[j * per : (j + 1) * per].astype(out.dtype)
+
+    return call_merge(body, ins, [jax.ShapeDtypeStruct((per, width), kind) for kind in kinds])
 
 
 def finish(ins, heads):
@@ -304,22 +304,17 @@
     kinds = [F32] * b_n + [BF16] * (b_n * (c_n - 1))
     sums = attend(planes, b_n, kinds, keys, values, bias)
 
-    def over_cores(b, first, kinds, after=()):
-        cuts = [(first + j) * tok for j in range(len(kinds))]
-        return merge_rows([sums[b]] + back[b], heads, list(zip(cuts, kinds)), tok, after)
-
-    back = [[give(sums[c * b_n + b], 0, 0, c) for c in range(1, c_n)] for b in range(b_n)]
-    far = [over_cores(b, 1, [BF16] * (a_n - 1)) for b in range(1, b_n)]
-    far = [[give(x, 0, b, 0) for x in pieces[::-1]] for b, pieces in enumerate(far, 1)]
-    own = over_cores(0, 0, [F32] * a_n)
-    total, last = [], []
-    for j, a in enumerate(range(a_n - 1, 0, -1)):
-        total += merge_rows([own[a]] + [x[j] for x in far], heads, [(0, BF16)], tok)
-        last.append(give(total[-1], a, 0, 0))
-    near = [over_cores(b, 0, [BF16], total[:1])[0] for b in range(1, b_n)]
-    near = [give(x, 0, b, 0) for b, x in enumerate(near, 1)]
-    first = merge_rows([own[0]] + near, heads, [(0, F32)], tok)[0] if near else own[0]
-    return finish([first] + last, heads)
+    def over_cores(b, kind):
+        got = [give(sums[c * b_n + b], 0, 0, c) for c in range(1, c_n)]
+        return merge_rows([sums[b]] + got, heads, a_n, [kind] * a_n)
+
+    got = [[give(x, 0, b, 0) for x in over_cores(b, BF16)] for b in range(1, b_n)]
+    own = over_cores(0, F32)
+    total = [[own[a]] + [pieces[a] for pieces in got] for a in range(a_n)]
+    last = [
+        give(merge_rows(total[a], heads, 1, [BF16])[0], a, 0, 0) for a in far_first
+    ]
+    return finish([*merge_rows(total[0], heads, 1, [F32]), *last], heads)
 
 
 def solution(mesh):

time: 37.2 us -> 34.8 us (0.935)
  Pallas kernels: 9.03 us -> 7.78 us
  waiting for transfers between devices: 7.43 us -> 6.78 us
  starting transfers between devices: 20.5 us -> 20 us
    pallas_call x1, Pallas kernels: 4.22 us -> 3.07 us  [attend(): pl.pallas_call(body, in_specs=[pl.BlockSpec(memory_space=pltpu.VMEM)] * (...]
    ppermute x9, waiting for transfers between devices: 3.87 us -> 3.23 us  [give(): return lax.ppermute(x, 'seq', partner_perm(shape, by, True))]
    ppermute x9, starting transfers between devices: 9.75 us -> 9.28 us  [give(): return lax.ppermute(x, 'seq', partner_perm(shape, by, True))]
    pallas_call x9 -> x8, Pallas kernels: 2.17 us -> 2.07 us  [call_merge(): pl.pallas_call(body, in_specs=[pl.BlockSpec(memory_space=pltpu.VMEM)] * l...]
  transfers between devices with their start and end apart: 17 -> 17, of which waited for: 7 -> 5; matrix products, arithmetic and copies ran while one was open for 0% -> 0% of each run, Pallas kernels for 10% -> 11%
where the time goes in v10:
time: 34.8 us; the launch traced here: 34.7 us
  starting transfers between devices  20 us (57%)
  Pallas kernels  7.78 us (22%)
  waiting for transfers between devices  6.78 us (19%)
    ppermute x8, starting transfers between devices, fetch(): return lax.ppermute(x, 'seq', partner_perm(shape, by, False))  10.7 us
    ppermute x9, starting transfers between devices, give(): return lax.ppermute(x, 'seq', partner_perm(shape, by, True))  9.28 us
    ppermute x8, waiting for transfers between devices, fetch(): return lax.ppermute(x, 'seq', partner_perm(shape, by, False))  3.55 us
    ppermute x9, waiting for transfers between devices, give(): return lax.ppermute(x, 'seq', partner_perm(shape, by, True))  3.23 us
    pallas_call x1, Pallas kernels, attend(): pl.pallas_call(body, in_specs=[pl.BlockSpec(memory_space=pltpu.VMEM)] * (...  3.07 us
    pallas_call x1, Pallas kernels, load(): pl.pallas_call(body, in_specs=[in_hbm] * len(held) + [pl.BlockSpec(memory...  2.65 us
    pallas_call x8, Pallas kernels, call_merge(): pl.pallas_call(body, in_specs=[pl.BlockSpec(memory_space=pltpu.VMEM)] * l...  2.07 us
  transfers between devices with their start and end apart: 17, of which 5 were waited for; matrix products, arithmetic and copies ran while one was open for 0% of the time, Pallas kernels for 11%

profile of v10, /device:TPU:0, one launch (start us, length us, event | category | flops | bytes accessed | tf_op | source)
XLA Modules:
  0.0 34.7 jit_solution(8315697370995466538)
XLA Ops:
  0.0 3.0 %collective-permute-start.1 = (bf16[8,2560]{1,0:T(8,128)(2,1)}, bf16[8,2560]{1,0:T(8,128)(2,1)S(1)}, u32[]{:S(2)}, u32[]{:S(2)}) collective-permute-start(bf16[8,2560]{1,0:T(8,128)(2,1)} %refs_5_.1), channel_id=1, source_target_pairs={{4,0},{5,1},{6,2},{7,3},{0,4},{1,5},{2,6},{3,7},{12,8},{13,9},{14,... | collective-permute-start | bytes 122888 | tf_op jit(solution)/shard_map/ppermute | solution.py:289
  3.0 2.5 %collective-permute-start = (bf16[8,2560]{1,0:T(8,128)(2,1)}, bf16[8,2560]{1,0:T(8,128)(2,1)S(1)}, u32[]{:S(2)}, u32[]{:S(2)}) collective-permute-start(bf16[8,2560]{1,0:T(8,128)(2,1)} %refs_5_.1), channel_id=1, source_target_pairs={{12,0},{13,1},{14,2},{15,3},{8,4},{9,5},{10,6},{11,7},{4,8},{5,9},... | collective-permute-start | bytes 122888 | tf_op jit(solution)/shard_map/ppermute | solution.py:289
  5.5 0.1 collective-permute-start.2
  5.6 1.5 %collective-permute-start.3 = (bf16[8,2560]{1,0:T(8,128)(2,1)}, bf16[8,2560]{1,0:T(8,128)(2,1)S(1)}, u32[]{:S(2)}, u32[]{:S(2)}) collective-permute-start(bf16[8,2560]{1,0:T(8,128)(2,1)} %refs_5_.1), channel_id=1, source_target_pairs={{2,0},{3,1},{0,2},{1,3},{6,4},{7,5},{4,6},{5,7},{10,8},{11,9},{8,1... | collective-permute-start | bytes 122888 | tf_op jit(solution)/shard_map/ppermute | solution.py:289
  7.1 0.0 collective-permute-done.1.refs_1_
  7.1 0.5 %collective-permute-start.4 = (bf16[8,2560]{1,0:T(8,128)(2,1)S(1)}, bf16[8,2560]{1,0:T(8,128)(2,1)S(1)}, u32[]{:S(2)}, u32[]{:S(2)}) collective-permute-start(bf16[8,2560]{1,0:T(8,128)(2,1)S(1)} %collective-permute-done.1.refs_1_), channel_id=1, source_target_pairs={{2,0},{3,1},{0,2},{1,3},{6,4},{7,5},{4,6},{5,7},{10,8},{11,9},{8,1... | collective-permute-start | bytes 122888 | tf_op jit(solution)/shard_map/ppermute | solution.py:289
  7.6 1.9 %collective-permute-done.refs_6_.refs_3_ = bf16[8,2560]{1,0:T(8,128)(2,1)S(1)} collective-permute-done((bf16[8,2560]{1,0:T(8,128)(2,1)}, bf16[8,2560]{1,0:T(8,128)(2,1)S(1)}, u32[]{:S(2)}, u32[]{:S(2)}) %collective-permute-start) | collective-permute-done | bytes 40992 | tf_op jit(solution)/shard_map/ppermute | solution.py:289
  9.6 1.5 %collective-permute-start.6 = (bf16[8,2560]{1,0:T(8,128)(2,1)S(1)}, bf16[8,2560]{1,0:T(8,128)(2,1)S(1)}, u32[]{:S(2)}, u32[]{:S(2)}) collective-permute-start(bf16[8,2560]{1,0:T(8,128)(2,1)S(1)} %collective-permute-done.refs_6_.refs_3_), channel_id=1, source_target_pairs={{2,0},{3,1},{0,2},{1,3},{6,4},{7,5},{4,6},{5,7},{10,8},{11,9},{8,1... | collective-permute-start | bytes 122888 | tf_op jit(solution)/shard_map/ppermute | solution.py:289
  11.1 1.5 %collective-permute-start.5 = (bf16[8,2560]{1,0:T(8,128)(2,1)S(1)}, bf16[8,2560]{1,0:T(8,128)(2,1)S(1)}, u32[]{:S(2)}, u32[]{:S(2)}) collective-permute-start(bf16[8,2560]{1,0:T(8,128)(2,1)S(1)} %collective-permute-done.2.refs_2_), channel_id=1, source_target_pairs={{2,0},{3,1},{0,2},{1,3},{6,4},{7,5},{4,6},{5,7},{10,8},{11,9},{8,1... | collective-permute-start | bytes 122888 | tf_op jit(solution)/shard_map/ppermute | solution.py:289
  12.6 2.6 %load.1 = (bf16[528,2560]{1,0:T(8,128)(2,1)S(1)}, bf16[528,2560]{1,0:T(8,128)(2,1)S(1)}, f32[528,128]{1,0:T(8,128)S(1)}, bf16[8,2560]{1,0:T(8,128)(2,1)S(1)}) custom-call(bf16[512,2560]{1,0:T(8,128)(2,1)} %refs_0_.1, bf16[512,2560]{1,0:T(8,128)(2,1)} %refs_1_.1, bf16[8,2560]{1,0:T(8,128)(2,1)} %refs_2_.1, bf16[8,2560]{1,0:T(8,128)(2,1)} %refs_3_.1, ...), custom_call_target="tpu_custom_call" | custom-call | bytes 10485760 | tf_op jit(solution)/shard_map/load/pallas_call | solution.py:193
  15.3 0.1 collective-permute-start.7
  15.4 1.6 %collective-permute-done.7.refs_2_ = bf16[64,2560]{1,0:T(8,128)(2,1)S(1)} collective-permute-done((bf16[64,2560]{1,0:T(8,128)(2,1)S(1)}, bf16[64,2560]{1,0:T(8,128)(2,1)S(1)}, u32[]{:S(2)}, u32[]{:S(2)}) %collective-permute-start.7) | collective-permute-done | bytes 327712 | tf_op jit(solution)/shard_map/ppermute | solution.py:289
  17.0 3.1 %attend.1 = (f32[32,2688]{1,0:T(8,128)S(1)}, f32[32,2688]{1,0:T(8,128)S(1)}, bf16[32,2688]{1,0:T(8,128)(2,1)S(1)}, bf16[32,2688]{1,0:T(8,128)(2,1)S(1)}) custom-call(f32[528,128]{1,0:T(8,128)S(1)} %get-tuple-element.21.refs_0_, bf16[64,2560]{1,0:T(8,128)(2,1)S(1)} %merge.8.refs_1_, bf16[64,2560]{1,0:T(8,128)(2,1)S(1)} %collective-permute-done.7.refs_2_, ...), custom_call_target="tpu_custom_call" | custom-call | flops 692060160 | bytes 5406720 | tf_op jit(solution)/shard_map/attend/pallas_call | solution.py:133
  20.1 0.2 collective-permute-start.9
  20.3 0.4 %collective-permute-start.8 = (bf16[32,2688]{1,0:T(8,128)(2,1)S(1)}, bf16[32,2688]{1,0:T(8,128)(2,1)S(1)}, u32[]{:S(2)}, u32[]{:S(2)}) collective-permute-start(bf16[32,2688]{1,0:T(8,128)(2,1)S(1)} %get-tuple-element.26), channel_id=1, source_target_pairs={{0,1},{1,0},{2,3},{3,2},{4,5},{5,4},{6,7},{7,6},{8,9},{9,8},{10,11... | collective-permute-start | bytes 516104 | tf_op jit(solution)/shard_map/ppermute | solution.py:292
  20.7 0.9 %collective-permute-done.9.refs_1_ = bf16[32,2688]{1,0:T(8,128)(2,1)S(1)} collective-permute-done((bf16[32,2688]{1,0:T(8,128)(2,1)S(1)}, bf16[32,2688]{1,0:T(8,128)(2,1)S(1)}, u32[]{:S(2)}, u32[]{:S(2)}) %collective-permute-start.9) | collective-permute-done | bytes 172064 | tf_op jit(solution)/shard_map/ppermute | solution.py:292
  21.5 0.3 merge.10
  21.8 1.4 %collective-permute-start.11 = (bf16[8,2688]{1,0:T(8,128)(2,1)S(1)}, bf16[8,2688]{1,0:T(8,128)(2,1)S(1)}, u32[]{:S(2)}, u32[]{:S(2)}) collective-permute-start(bf16[8,2688]{1,0:T(8,128)(2,1)S(1)} %get-tuple-element.32), channel_id=1, source_target_pairs={{0,2},{1,3},{2,0},{3,1},{4,6},{5,7},{6,4},{7,5},{8,10},{9,11},{10,... | collective-permute-start | bytes 129032 | tf_op jit(solution)/shard_map/ppermute | solution.py:292
  23.2 0.7 %collective-permute-start.13 = (bf16[8,2688]{1,0:T(8,128)(2,1)S(1)}, bf16[8,2688]{1,0:T(8,128)(2,1)S(1)}, u32[]{:S(2)}, u32[]{:S(2)}) collective-permute-start(bf16[8,2688]{1,0:T(8,128)(2,1)S(1)} %get-tuple-element.34), channel_id=1, source_target_pairs={{0,2},{1,3},{2,0},{3,1},{4,6},{5,7},{6,4},{7,5},{8,10},{9,11},{10,... | collective-permute-start | bytes 129032 | tf_op jit(solution)/shard_map/ppermute | solution.py:292
  23.9 1.3 %collective-permute-start.15 = (bf16[8,2688]{1,0:T(8,128)(2,1)S(1)}, bf16[8,2688]{1,0:T(8,128)(2,1)S(1)}, u32[]{:S(2)}, u32[]{:S(2)}) collective-permute-start(bf16[8,2688]{1,0:T(8,128)(2,1)S(1)} %get-tuple-element.36), channel_id=1, source_target_pairs={{0,2},{1,3},{2,0},{3,1},{4,6},{5,7},{6,4},{7,5},{8,10},{9,11},{10,... | collective-permute-start | bytes 129032 | tf_op jit(solution)/shard_map/ppermute | solution.py:292
  25.2 0.7 %collective-permute-start.10 = (bf16[8,2688]{1,0:T(8,128)(2,1)S(1)}, bf16[8,2688]{1,0:T(8,128)(2,1)S(1)}, u32[]{:S(2)}, u32[]{:S(2)}) collective-permute-start(bf16[8,2688]{1,0:T(8,128)(2,1)S(1)} %get-tuple-element.30), channel_id=1, source_target_pairs={{0,2},{1,3},{2,0},{3,1},{4,6},{5,7},{6,4},{7,5},{8,10},{9,11},{10,... | collective-permute-start | bytes 129032 | tf_op jit(solution)/shard_map/ppermute | solution.py:292
  26.0 0.3 merge.9
  26.3 0.1 merge.12
  26.4 2.1 %collective-permute-start.12 = (bf16[8,2688]{1,0:T(8,128)(2,1)S(1)}, bf16[8,2688]{1,0:T(8,128)(2,1)S(1)}, u32[]{:S(2)}, u32[]{:S(2)}) collective-permute-start(bf16[8,2688]{1,0:T(8,128)(2,1)S(1)} %merge.12), channel_id=1, source_target_pairs={{0,12},{1,13},{2,14},{3,15},{4,8},{5,9},{6,10},{7,11},{8,4},{9,5},... | collective-permute-start | bytes 129032 | tf_op jit(solution)/shard_map/ppermute | solution.py:292
  28.5 0.1 merge.13
  28.6 0.4 %collective-permute-start.14 = (bf16[8,2688]{1,0:T(8,128)(2,1)S(1)}, bf16[8,2688]{1,0:T(8,128)(2,1)S(1)}, u32[]{:S(2)}, u32[]{:S(2)}) collective-permute-start(bf16[8,2688]{1,0:T(8,128)(2,1)S(1)} %merge.13), channel_id=1, source_target_pairs={{0,8},{1,9},{2,10},{3,11},{4,12},{5,13},{6,14},{7,15},{8,0},{9,1},... | collective-permute-start | bytes 129032 | tf_op jit(solution)/shard_map/ppermute | solution.py:292
  29.0 0.1 merge.14
  29.1 2.2 %collective-permute-start.16 = (bf16[8,2688]{1,0:T(8,128)(2,1)S(1)}, bf16[8,2688]{1,0:T(8,128)(2,1)S(1)}, u32[]{:S(2)}, u32[]{:S(2)}) collective-permute-start(bf16[8,2688]{1,0:T(8,128)(2,1)S(1)} %merge.14), channel_id=1, source_target_pairs={{0,4},{1,5},{2,6},{3,7},{4,0},{5,1},{6,2},{7,3},{8,12},{9,13},{10,... | collective-permute-start | bytes 129032 | tf_op jit(solution)/shard_map/ppermute | solution.py:292
  31.3 0.1 merge.11.refs_0_
  31.4 1.0 %collective-permute-done.12.refs_1_ = bf16[8,2688]{1,0:T(8,128)(2,1)S(1)} collective-permute-done((bf16[8,2688]{1,0:T(8,128)(2,1)S(1)}, bf16[8,2688]{1,0:T(8,128)(2,1)S(1)}, u32[]{:S(2)}, u32[]{:S(2)}) %collective-permute-start.12) | collective-permute-done | bytes 43040 | tf_op jit(solution)/shard_map/ppermute | solution.py:292
  32.5 1.3 %collective-permute-done.14.refs_2_ = bf16[8,2688]{1,0:T(8,128)(2,1)S(1)} collective-permute-done((bf16[8,2688]{1,0:T(8,128)(2,1)S(1)}, bf16[8,2688]{1,0:T(8,128)(2,1)S(1)}, u32[]{:S(2)}, u32[]{:S(2)}) %collective-permute-start.14) | collective-permute-done | bytes 43040 | tf_op jit(solution)/shard_map/ppermute | solution.py:292
  33.8 0.9 %merge.15 = bf16[8,2560]{1,0:T(8,128)(2,1)} custom-call(f32[8,2688]{1,0:T(8,128)S(1)} %merge.11.refs_0_, bf16[8,2688]{1,0:T(8,128)(2,1)S(1)} %collective-permute-done.12.refs_1_, bf16[8,2688]{1,0:T(8,128)(2,1)S(1)} %collective-permute-done.14.refs_2_, bf16[8,2688]{1,0:T(8,128)(2,1)S(1)} %collective-permute-done.16.refs_3_), custom_call_target="tpu_custom_call" | custom-call | flops 344064 | bytes 344064 | tf_op jit(solution)/shard_map/merge/pallas_call | solution.py:269
  (12 shorter events, 0.1 us)
Async XLA Ops:
  0.0 7.1 %collective-permute-start.1 = (bf16[8,2560]{1,0:T(8,128)(2,1)}, bf16[8,2560]{1,0:T(8,128)(2,1)S(1)}, u32[]{:S(2)}, u32[]{:S(2)}) collective-permute-start(bf16[8,2560]{1,0:T(8,128)(2,1)} %refs_5_.1), channel_id=1, source_target_pairs={{4,0},{5,1},{6,2},{7,3},{0,4},{1,5},{2,6},{3,7},{12,8},{13,9},{14,... | collective-permute-start | bytes 122888 | tf_op jit(solution)/shard_map/ppermute | solution.py:289
  3.0 6.5 %collective-permute-start = (bf16[8,2560]{1,0:T(8,128)(2,1)}, bf16[8,2560]{1,0:T(8,128)(2,1)S(1)}, u32[]{:S(2)}, u32[]{:S(2)}) collective-permute-start(bf16[8,2560]{1,0:T(8,128)(2,1)} %refs_5_.1), channel_id=1, source_target_pairs={{12,0},{13,1},{14,2},{15,3},{8,4},{9,5},{10,6},{11,7},{4,8},{5,9},... | collective-permute-start | bytes 122888 | tf_op jit(solution)/shard_map/ppermute | solution.py:289
  5.5 5.6 %collective-permute-start.2 = (bf16[8,2560]{1,0:T(8,128)(2,1)}, bf16[8,2560]{1,0:T(8,128)(2,1)S(1)}, u32[]{:S(2)}, u32[]{:S(2)}) collective-permute-start(bf16[8,2560]{1,0:T(8,128)(2,1)} %refs_5_.1), channel_id=1, source_target_pairs={{8,0},{9,1},{10,2},{11,3},{12,4},{13,5},{14,6},{15,7},{0,8},{1,9},... | collective-permute-start | bytes 122888 | tf_op jit(solution)/shard_map/ppermute | solution.py:289
  5.6 9.6 %collective-permute-start.3 = (bf16[8,2560]{1,0:T(8,128)(2,1)}, bf16[8,2560]{1,0:T(8,128)(2,1)S(1)}, u32[]{:S(2)}, u32[]{:S(2)}) collective-permute-start(bf16[8,2560]{1,0:T(8,128)(2,1)} %refs_5_.1), channel_id=1, source_target_pairs={{2,0},{3,1},{0,2},{1,3},{6,4},{7,5},{4,6},{5,7},{10,8},{11,9},{8,1... | collective-permute-start | bytes 122888 | tf_op jit(solution)/shard_map/ppermute | solution.py:289
  7.1 8.1 %collective-permute-start.4 = (bf16[8,2560]{1,0:T(8,128)(2,1)S(1)}, bf16[8,2560]{1,0:T(8,128)(2,1)S(1)}, u32[]{:S(2)}, u32[]{:S(2)}) collective-permute-start(bf16[8,2560]{1,0:T(8,128)(2,1)S(1)} %collective-permute-done.1.refs_1_), channel_id=1, source_target_pairs={{2,0},{3,1},{0,2},{1,3},{6,4},{7,5},{4,6},{5,7},{10,8},{11,9},{8,1... | collective-permute-start | bytes 122888 | tf_op jit(solution)/shard_map/ppermute | solution.py:289
  9.6 5.7 %collective-permute-start.6 = (bf16[8,2560]{1,0:T(8,128)(2,1)S(1)}, bf16[8,2560]{1,0:T(8,128)(2,1)S(1)}, u32[]{:S(2)}, u32[]{:S(2)}) collective-permute-start(bf16[8,2560]{1,0:T(8,128)(2,1)S(1)} %collective-permute-done.refs_6_.refs_3_), channel_id=1, source_target_pairs={{2,0},{3,1},{0,2},{1,3},{6,4},{7,5},{4,6},{5,7},{10,8},{11,9},{8,1... | collective-permute-start | bytes 122888 | tf_op jit(solution)/shard_map/ppermute | solution.py:289
  11.1 4.2 %collective-permute-start.5 = (bf16[8,2560]{1,0:T(8,128)(2,1)S(1)}, bf16[8,2560]{1,0:T(8,128)(2,1)S(1)}, u32[]{:S(2)}, u32[]{:S(2)}) collective-permute-start(bf16[8,2560]{1,0:T(8,128)(2,1)S(1)} %collective-permute-done.2.refs_2_), channel_id=1, source_target_pairs={{2,0},{3,1},{0,2},{1,3},{6,4},{7,5},{4,6},{5,7},{10,8},{11,9},{8,1... | collective-permute-start | bytes 122888 | tf_op jit(solution)/shard_map/ppermute | solution.py:289
  15.3 1.7 %collective-permute-start.7 = (bf16[64,2560]{1,0:T(8,128)(2,1)S(1)}, bf16[64,2560]{1,0:T(8,128)(2,1)S(1)}, u32[]{:S(2)}, u32[]{:S(2)}) collective-permute-start(bf16[64,2560]{1,0:T(8,128)(2,1)S(1)} %merge.8.refs_1_), channel_id=1, source_target_pairs={{1,0},{0,1},{3,2},{2,3},{5,4},{4,5},{7,6},{6,7},{9,8},{8,9},{11,10... | collective-permute-start | bytes 983048 | tf_op jit(solution)/shard_map/ppermute | solution.py:289
  20.1 1.5 %collective-permute-start.9 = (bf16[32,2688]{1,0:T(8,128)(2,1)S(1)}, bf16[32,2688]{1,0:T(8,128)(2,1)S(1)}, u32[]{:S(2)}, u32[]{:S(2)}) collective-permute-start(bf16[32,2688]{1,0:T(8,128)(2,1)S(1)} %get-tuple-element.29), channel_id=1, source_target_pairs={{0,1},{1,0},{2,3},{3,2},{4,5},{5,4},{6,7},{7,6},{8,9},{9,8},{10,11... | collective-permute-start | bytes 516104 | tf_op jit(solution)/shard_map/ppermute | solution.py:292
  20.3 5.7 %collective-permute-start.8 = (bf16[32,2688]{1,0:T(8,128)(2,1)S(1)}, bf16[32,2688]{1,0:T(8,128)(2,1)S(1)}, u32[]{:S(2)}, u32[]{:S(2)}) collective-permute-start(bf16[32,2688]{1,0:T(8,128)(2,1)S(1)} %get-tuple-element.26), channel_id=1, source_target_pairs={{0,1},{1,0},{2,3},{3,2},{4,5},{5,4},{6,7},{7,6},{8,9},{9,8},{10,11... | collective-permute-start | bytes 516104 | tf_op jit(solution)/shard_map/ppermute | solution.py:292
  21.8 4.4 %collective-permute-start.11 = (bf16[8,2688]{1,0:T(8,128)(2,1)S(1)}, bf16[8,2688]{1,0:T(8,128)(2,1)S(1)}, u32[]{:S(2)}, u32[]{:S(2)}) collective-permute-start(bf16[8,2688]{1,0:T(8,128)(2,1)S(1)} %get-tuple-element.32), channel_id=1, source_target_pairs={{0,2},{1,3},{2,0},{3,1},{4,6},{5,7},{6,4},{7,5},{8,10},{9,11},{10,... | collective-permute-start | bytes 129032 | tf_op jit(solution)/shard_map/ppermute | solution.py:292
  23.2 5.3 %collective-permute-start.13 = (bf16[8,2688]{1,0:T(8,128)(2,1)S(1)}, bf16[8,2688]{1,0:T(8,128)(2,1)S(1)}, u32[]{:S(2)}, u32[]{:S(2)}) collective-permute-start(bf16[8,2688]{1,0:T(8,128)(2,1)S(1)} %get-tuple-element.34), channel_id=1, source_target_pairs={{0,2},{1,3},{2,0},{3,1},{4,6},{5,7},{6,4},{7,5},{8,10},{9,11},{10,... | collective-permute-start | bytes 129032 | tf_op jit(solution)/shard_map/ppermute | solution.py:292
  23.9 5.0 %collective-permute-start.15 = (bf16[8,2688]{1,0:T(8,128)(2,1)S(1)}, bf16[8,2688]{1,0:T(8,128)(2,1)S(1)}, u32[]{:S(2)}, u32[]{:S(2)}) collective-permute-start(bf16[8,2688]{1,0:T(8,128)(2,1)S(1)} %get-tuple-element.36), channel_id=1, source_target_pairs={{0,2},{1,3},{2,0},{3,1},{4,6},{5,7},{6,4},{7,5},{8,10},{9,11},{10,... | collective-permute-start | bytes 129032 | tf_op jit(solution)/shard_map/ppermute | solution.py:292
  25.2 6.1 %collective-permute-start.10 = (bf16[8,2688]{1,0:T(8,128)(2,1)S(1)}, bf16[8,2688]{1,0:T(8,128)(2,1)S(1)}, u32[]{:S(2)}, u32[]{:S(2)}) collective-permute-start(bf16[8,2688]{1,0:T(8,128)(2,1)S(1)} %get-tuple-element.30), channel_id=1, source_target_pairs={{0,2},{1,3},{2,0},{3,1},{4,6},{5,7},{6,4},{7,5},{8,10},{9,11},{10,... | collective-permute-start | bytes 129032 | tf_op jit(solution)/shard_map/ppermute | solution.py:292
  26.4 6.1 %collective-permute-start.12 = (bf16[8,2688]{1,0:T(8,128)(2,1)S(1)}, bf16[8,2688]{1,0:T(8,128)(2,1)S(1)}, u32[]{:S(2)}, u32[]{:S(2)}) collective-permute-start(bf16[8,2688]{1,0:T(8,128)(2,1)S(1)} %merge.12), channel_id=1, source_target_pairs={{0,12},{1,13},{2,14},{3,15},{4,8},{5,9},{6,10},{7,11},{8,4},{9,5},... | collective-permute-start | bytes 129032 | tf_op jit(solution)/shard_map/ppermute | solution.py:292
  28.6 5.2 %collective-permute-start.14 = (bf16[8,2688]{1,0:T(8,128)(2,1)S(1)}, bf16[8,2688]{1,0:T(8,128)(2,1)S(1)}, u32[]{:S(2)}, u32[]{:S(2)}) collective-permute-start(bf16[8,2688]{1,0:T(8,128)(2,1)S(1)} %merge.13), channel_id=1, source_target_pairs={{0,8},{1,9},{2,10},{3,11},{4,12},{5,13},{6,14},{7,15},{8,0},{9,1},... | collective-permute-start | bytes 129032 | tf_op jit(solution)/shard_map/ppermute | solution.py:292
  29.1 4.6 %collective-permute-start.16 = (bf16[8,2688]{1,0:T(8,128)(2,1)S(1)}, bf16[8,2688]{1,0:T(8,128)(2,1)S(1)}, u32[]{:S(2)}, u32[]{:S(2)}) collective-permute-start(bf16[8,2688]{1,0:T(8,128)(2,1)S(1)} %merge.14), channel_id=1, source_target_pairs={{0,4},{1,5},{2,6},{3,7},{4,0},{5,1},{6,2},{7,3},{8,12},{9,13},{10,... | collective-permute-start | bytes 129032 | tf_op jit(solution)/shard_map/ppermute | solution.py:292

commit v11 on v10

--- a/solution.py
+++ b/solution.py
@@ -80,28 +80,41 @@
                     q = jnp.concatenate([jnp.where(m, q, zero) for m in mine], axis=0)
                 return lax.dot_general(k_ref[:, cols], q, contract_last, preferred_element_type=F32)
 
-            ahead = scores(0)
-            for i in range(group):
-                score = ahead
-                if i + 1 < group:
-                    ahead = scores(i + 1)
+            def weigh(i, score):
                 bias = jnp.concatenate([bias_ref[...]] * (pack * rows // STAT), axis=1)
                 score = score * scale + bias
                 top = jnp.max(score, axis=0, keepdims=True).astype(BF16).astype(F32)
                 score = jnp.exp2(score - top)
                 mass = jnp.sum(score, axis=0, keepdims=True)
-                score = score.astype(BF16)
+                for k in range(pack):
+                    head = (step * group + i) * pack + k
+                    part = slice(k * rows, (k + 1) * rows)
+                    top_acc[pl.ds(head, 1), :] = top[:, part]
+                    mass_acc[pl.ds(head, 1), :] = mass[:, part]
+                return score.astype(BF16)
+
+            def gather_values(i, weights):
                 for k in range(pack):
                     head = (step * group + i) * pack + k
                     cols = pl.ds(pl.multiple_of(head * HD, HD), HD)
-                    part = slice(k * rows, (k + 1) * rows)
                     one = lax.dot_general(
-                        score[:, part], v_ref[:, cols], contract_first, preferred_element_type=F32
+                        weights[:, k * rows : (k + 1) * rows],
+                        v_ref[:, cols],
+                        contract_first,
+                        preferred_element_type=F32,
                     )
                     for p, o_ref in enumerate(outs):
                         o_ref[at, cols] = one[p * tile : (p + 1) * tile].astype(o_ref.dtype)
-                    top_acc[pl.ds(head, 1), :] = top[:, part]
-                    mass_acc[pl.ds(head, 1), :] = mass[:, part]
+
+            ahead = [scores(i) for i in range(min(2, group))]
+            weights = None
+            for i in range(group):
+                if i + 2 < group:
+                    ahead.append(scores(i + 2))
+                done, weights = weights, weigh(i, ahead[i])
+                if i > 0:
+                    gather_values(i - 1, done)
+            gather_values(group - 1, weights)
             return carry
 
         lax.fori_loop(0, steps, heads_of, 0)
@@ -291,13 +304,11 @@
     def give(x, *by):
         return lax.ppermute(x, "seq", partner_perm(shape, by, True))
 
-    far_first = range(a_n - 1, 0, -1)
-    line = [queries] + [None] * (a_n - 1)
-    for a in far_first:
-        line[a] = fetch(queries, a, 0, 0)
+    far_first = [0, *range(a_n - 1, 0, -1)]
+    line = [queries] + [fetch(queries, a, 0, 0) for a in far_first[1:]]
     lines = [line] + [[fetch(x, 0, b, 0) for x in line] for b in range(1, b_n)]
     keys, values, bias, line[0] = load(
-        (cache_keys, cache_values), (new_keys, new_values), victims[None], queries, line[-1]
+        (cache_keys, cache_values), (new_keys, new_values), victims[None], queries, line[min(2, a_n - 1)]
     )
     plane = join([x for pieces in lines for x in pieces])
     planes = [plane] + [fetch(plane, 0, 0, c) for c in range(1, c_n)]
@@ -310,9 +321,9 @@
 
     got = [[give(x, 0, b, 0) for x in over_cores(b, BF16)] for b in range(1, b_n)]
     own = over_cores(0, F32)
-    total = [[own[a]] + [pieces[a] for pieces in got] for a in range(a_n)]
+    total = [[own[s]] + [pieces[s] for pieces in got] for s in range(a_n)]
     last = [
-        give(merge_rows(total[a], heads, 1, [BF16])[0], a, 0, 0) for a in far_first
+        give(merge_rows(total[s], heads, 1, [BF16])[0], far_first[s], 0, 0) for s in range(1, a_n)
     ]
     return finish([*merge_rows(total[0], heads, 1, [F32]), *last], heads)
 

time: 34.8 us -> 34.7 us (level)
  Pallas kernels: 7.78 us -> 7.23 us
  starting transfers between devices: 20 us -> 20.5 us
    pallas_call x1, Pallas kernels: 3.07 us -> 2.53 us  [attend(): pl.pallas_call(body, in_specs=[pl.BlockSpec(memory_space=pltpu.VMEM)] * (...]
    ppermute x8, starting transfers between devices: 10.7 us -> 11.2 us  [fetch(): return lax.ppermute(x, 'seq', partner_perm(shape, by, False))]
  transfers between devices with their start and end apart: 17 -> 17, of which waited for: 5 -> 7; matrix products, arithmetic and copies ran while one was open for 0% -> 0% of each run, Pallas kernels for 11% -> 11%
where the time goes in v11:
time: 34.7 us; the launch traced here: 34.5 us
  starting transfers between devices  20.5 us (59%)
  Pallas kernels  7.23 us (21%)
  waiting for transfers between devices  6.68 us (19%)
    ppermute x8, starting transfers between devices, fetch(): return lax.ppermute(x, 'seq', partner_perm(shape, by, False))  11.2 us
    ppermute x9, starting transfers between devices, give(): return lax.ppermute(x, 'seq', partner_perm(shape, by, True))  9.26 us
    ppermute x8, waiting for transfers between devices, fetch(): return lax.ppermute(x, 'seq', partner_perm(shape, by, False))  3.46 us
    ppermute x9, waiting for transfers between devices, give(): return lax.ppermute(x, 'seq', partner_perm(shape, by, True))  3.22 us
    pallas_call x1, Pallas kernels, load(): pl.pallas_call(body, in_specs=[in_hbm] * len(held) + [pl.BlockSpec(memory...  2.65 us
    pallas_call x1, Pallas kernels, attend(): pl.pallas_call(body, in_specs=[pl.BlockSpec(memory_space=pltpu.VMEM)] * (...  2.53 us
    pallas_call x8, Pallas kernels, call_merge(): pl.pallas_call(body, in_specs=[pl.BlockSpec(memory_space=pltpu.VMEM)] * l...  2.06 us
  transfers between devices with their start and end apart: 17, of which 7 were waited for; matrix products, arithmetic and copies ran while one was open for 0% of the time, Pallas kernels for 11%

profile of v11, /device:TPU:0, one launch (start us, length us, event | category | flops | bytes accessed | tf_op | source)
XLA Modules:
  0.0 34.5 jit_solution(1206877802541690027)
XLA Ops:
  0.0 5.0 %collective-permute-start.1 = (bf16[8,2560]{1,0:T(8,128)(2,1)}, bf16[8,2560]{1,0:T(8,128)(2,1)S(1)}, u32[]{:S(2)}, u32[]{:S(2)}) collective-permute-start(bf16[8,2560]{1,0:T(8,128)(2,1)} %refs_5_.1), channel_id=1, source_target_pairs={{12,0},{13,1},{14,2},{15,3},{8,4},{9,5},{10,6},{11,7},{4,8},{5,9},... | collective-permute-start | bytes 122888 | tf_op jit(solution)/shard_map/ppermute | solution.py:302
  5.1 0.6 %collective-permute-start.2 = (bf16[8,2560]{1,0:T(8,128)(2,1)}, bf16[8,2560]{1,0:T(8,128)(2,1)S(1)}, u32[]{:S(2)}, u32[]{:S(2)}) collective-permute-start(bf16[8,2560]{1,0:T(8,128)(2,1)} %refs_5_.1), channel_id=1, source_target_pairs={{4,0},{5,1},{6,2},{7,3},{0,4},{1,5},{2,6},{3,7},{12,8},{13,9},{14,... | collective-permute-start | bytes 122888 | tf_op jit(solution)/shard_map/ppermute | solution.py:302
  5.6 1.8 %collective-permute-start.3 = (bf16[8,2560]{1,0:T(8,128)(2,1)}, bf16[8,2560]{1,0:T(8,128)(2,1)S(1)}, u32[]{:S(2)}, u32[]{:S(2)}) collective-permute-start(bf16[8,2560]{1,0:T(8,128)(2,1)} %refs_5_.1), channel_id=1, source_target_pairs={{2,0},{3,1},{0,2},{1,3},{6,4},{7,5},{4,6},{5,7},{10,8},{11,9},{8,1... | collective-permute-start | bytes 122888 | tf_op jit(solution)/shard_map/ppermute | solution.py:302
  7.4 1.8 %collective-permute-start.4 = (bf16[8,2560]{1,0:T(8,128)(2,1)S(1)}, bf16[8,2560]{1,0:T(8,128)(2,1)S(1)}, u32[]{:S(2)}, u32[]{:S(2)}) collective-permute-start(bf16[8,2560]{1,0:T(8,128)(2,1)S(1)} %collective-permute-done.1.refs_1_), channel_id=1, source_target_pairs={{2,0},{3,1},{0,2},{1,3},{6,4},{7,5},{4,6},{5,7},{10,8},{11,9},{8,1... | collective-permute-start | bytes 122888 | tf_op jit(solution)/shard_map/ppermute | solution.py:302
  9.1 1.0 %collective-permute-done.refs_6_.refs_2_ = bf16[8,2560]{1,0:T(8,128)(2,1)S(1)} collective-permute-done((bf16[8,2560]{1,0:T(8,128)(2,1)}, bf16[8,2560]{1,0:T(8,128)(2,1)S(1)}, u32[]{:S(2)}, u32[]{:S(2)}) %collective-permute-start) | collective-permute-done | bytes 40992 | tf_op jit(solution)/shard_map/ppermute | solution.py:302
  10.2 1.5 %collective-permute-start.5 = (bf16[8,2560]{1,0:T(8,128)(2,1)S(1)}, bf16[8,2560]{1,0:T(8,128)(2,1)S(1)}, u32[]{:S(2)}, u32[]{:S(2)}) collective-permute-start(bf16[8,2560]{1,0:T(8,128)(2,1)S(1)} %collective-permute-done.refs_6_.refs_2_), channel_id=1, source_target_pairs={{2,0},{3,1},{0,2},{1,3},{6,4},{7,5},{4,6},{5,7},{10,8},{11,9},{8,1... | collective-permute-start | bytes 122888 | tf_op jit(solution)/shard_map/ppermute | solution.py:302
  11.7 0.5 %collective-permute-start.6 = (bf16[8,2560]{1,0:T(8,128)(2,1)S(1)}, bf16[8,2560]{1,0:T(8,128)(2,1)S(1)}, u32[]{:S(2)}, u32[]{:S(2)}) collective-permute-start(bf16[8,2560]{1,0:T(8,128)(2,1)S(1)} %collective-permute-done.2.refs_3_), channel_id=1, source_target_pairs={{2,0},{3,1},{0,2},{1,3},{6,4},{7,5},{4,6},{5,7},{10,8},{11,9},{8,1... | collective-permute-start | bytes 122888 | tf_op jit(solution)/shard_map/ppermute | solution.py:302
  12.2 2.6 %load.1 = (bf16[528,2560]{1,0:T(8,128)(2,1)S(1)}, bf16[528,2560]{1,0:T(8,128)(2,1)S(1)}, f32[528,128]{1,0:T(8,128)S(1)}, bf16[8,2560]{1,0:T(8,128)(2,1)S(1)}) custom-call(bf16[512,2560]{1,0:T(8,128)(2,1)} %refs_0_.1, bf16[512,2560]{1,0:T(8,128)(2,1)} %refs_1_.1, bf16[8,2560]{1,0:T(8,128)(2,1)} %refs_2_.1, bf16[8,2560]{1,0:T(8,128)(2,1)} %refs_3_.1, ...), custom_call_target="tpu_custom_call" | custom-call | bytes 10485760 | tf_op jit(solution)/shard_map/load/pallas_call | solution.py:206
  14.9 0.8 %collective-permute-done.6.refs_7_ = bf16[8,2560]{1,0:T(8,128)(2,1)S(1)} collective-permute-done((bf16[8,2560]{1,0:T(8,128)(2,1)S(1)}, bf16[8,2560]{1,0:T(8,128)(2,1)S(1)}, u32[]{:S(2)}, u32[]{:S(2)}) %collective-permute-start.6) | collective-permute-done | bytes 40992 | tf_op jit(solution)/shard_map/ppermute | solution.py:302
  15.7 0.1 collective-permute-start.7
  15.8 1.6 %collective-permute-done.7.refs_2_ = bf16[64,2560]{1,0:T(8,128)(2,1)S(1)} collective-permute-done((bf16[64,2560]{1,0:T(8,128)(2,1)S(1)}, bf16[64,2560]{1,0:T(8,128)(2,1)S(1)}, u32[]{:S(2)}, u32[]{:S(2)}) %collective-permute-start.7) | collective-permute-done | bytes 327712 | tf_op jit(solution)/shard_map/ppermute | solution.py:302
  17.4 2.5 %attend.1 = (f32[32,2688]{1,0:T(8,128)S(1)}, f32[32,2688]{1,0:T(8,128)S(1)}, bf16[32,2688]{1,0:T(8,128)(2,1)S(1)}, bf16[32,2688]{1,0:T(8,128)(2,1)S(1)}) custom-call(f32[528,128]{1,0:T(8,128)S(1)} %get-tuple-element.21.refs_0_, bf16[64,2560]{1,0:T(8,128)(2,1)S(1)} %merge.8.refs_1_, bf16[64,2560]{1,0:T(8,128)(2,1)S(1)} %collective-permute-done.7.refs_2_, ...), custom_call_target="tpu_custom_call" | custom-call | flops 692060160 | bytes 5406720 | tf_op jit(solution)/shard_map/attend/pallas_call | solution.py:146
  19.9 0.2 collective-permute-start.9
  20.1 0.4 %collective-permute-start.8 = (bf16[32,2688]{1,0:T(8,128)(2,1)S(1)}, bf16[32,2688]{1,0:T(8,128)(2,1)S(1)}, u32[]{:S(2)}, u32[]{:S(2)}) collective-permute-start(bf16[32,2688]{1,0:T(8,128)(2,1)S(1)} %get-tuple-element.26), channel_id=1, source_target_pairs={{0,1},{1,0},{2,3},{3,2},{4,5},{5,4},{6,7},{7,6},{8,9},{9,8},{10,11... | collective-permute-start | bytes 516104 | tf_op jit(solution)/shard_map/ppermute | solution.py:305
  20.5 0.9 %collective-permute-done.9.refs_1_ = bf16[32,2688]{1,0:T(8,128)(2,1)S(1)} collective-permute-done((bf16[32,2688]{1,0:T(8,128)(2,1)S(1)}, bf16[32,2688]{1,0:T(8,128)(2,1)S(1)}, u32[]{:S(2)}, u32[]{:S(2)}) %collective-permute-start.9) | collective-permute-done | bytes 172064 | tf_op jit(solution)/shard_map/ppermute | solution.py:305
  21.4 0.3 merge.10
  21.7 0.8 %collective-permute-start.11 = (bf16[8,2688]{1,0:T(8,128)(2,1)S(1)}, bf16[8,2688]{1,0:T(8,128)(2,1)S(1)}, u32[]{:S(2)}, u32[]{:S(2)}) collective-permute-start(bf16[8,2688]{1,0:T(8,128)(2,1)S(1)} %get-tuple-element.32), channel_id=1, source_target_pairs={{0,2},{1,3},{2,0},{3,1},{4,6},{5,7},{6,4},{7,5},{8,10},{9,11},{10,... | collective-permute-start | bytes 129032 | tf_op jit(solution)/shard_map/ppermute | solution.py:305
  22.5 1.3 %collective-permute-start.13 = (bf16[8,2688]{1,0:T(8,128)(2,1)S(1)}, bf16[8,2688]{1,0:T(8,128)(2,1)S(1)}, u32[]{:S(2)}, u32[]{:S(2)}) collective-permute-start(bf16[8,2688]{1,0:T(8,128)(2,1)S(1)} %get-tuple-element.34), channel_id=1, source_target_pairs={{0,2},{1,3},{2,0},{3,1},{4,6},{5,7},{6,4},{7,5},{8,10},{9,11},{10,... | collective-permute-start | bytes 129032 | tf_op jit(solution)/shard_map/ppermute | solution.py:305
  23.8 0.7 %collective-permute-start.15 = (bf16[8,2688]{1,0:T(8,128)(2,1)S(1)}, bf16[8,2688]{1,0:T(8,128)(2,1)S(1)}, u32[]{:S(2)}, u32[]{:S(2)}) collective-permute-start(bf16[8,2688]{1,0:T(8,128)(2,1)S(1)} %get-tuple-element.36), channel_id=1, source_target_pairs={{0,2},{1,3},{2,0},{3,1},{4,6},{5,7},{6,4},{7,5},{8,10},{9,11},{10,... | collective-permute-start | bytes 129032 | tf_op jit(solution)/shard_map/ppermute | solution.py:305
  24.5 1.3 %collective-permute-start.10 = (bf16[8,2688]{1,0:T(8,128)(2,1)S(1)}, bf16[8,2688]{1,0:T(8,128)(2,1)S(1)}, u32[]{:S(2)}, u32[]{:S(2)}) collective-permute-start(bf16[8,2688]{1,0:T(8,128)(2,1)S(1)} %get-tuple-element.30), channel_id=1, source_target_pairs={{0,2},{1,3},{2,0},{3,1},{4,6},{5,7},{6,4},{7,5},{8,10},{9,11},{10,... | collective-permute-start | bytes 129032 | tf_op jit(solution)/shard_map/ppermute | solution.py:305
  25.8 0.3 merge.9
  26.1 0.1 merge.12
  26.3 1.9 %collective-permute-start.12 = (bf16[8,2688]{1,0:T(8,128)(2,1)S(1)}, bf16[8,2688]{1,0:T(8,128)(2,1)S(1)}, u32[]{:S(2)}, u32[]{:S(2)}) collective-permute-start(bf16[8,2688]{1,0:T(8,128)(2,1)S(1)} %merge.12), channel_id=1, source_target_pairs={{0,12},{1,13},{2,14},{3,15},{4,8},{5,9},{6,10},{7,11},{8,4},{9,5},... | collective-permute-start | bytes 129032 | tf_op jit(solution)/shard_map/ppermute | solution.py:305
  28.2 0.1 merge.13
  28.3 0.1 collective-permute-start.14
  28.4 0.1 merge.14
  28.5 2.6 %collective-permute-start.16 = (bf16[8,2688]{1,0:T(8,128)(2,1)S(1)}, bf16[8,2688]{1,0:T(8,128)(2,1)S(1)}, u32[]{:S(2)}, u32[]{:S(2)}) collective-permute-start(bf16[8,2688]{1,0:T(8,128)(2,1)S(1)} %merge.14), channel_id=1, source_target_pairs={{0,4},{1,5},{2,6},{3,7},{4,0},{5,1},{6,2},{7,3},{8,12},{9,13},{10,... | collective-permute-start | bytes 129032 | tf_op jit(solution)/shard_map/ppermute | solution.py:305
  31.2 0.1 merge.11.refs_0_
  31.3 1.0 %collective-permute-done.12.refs_1_ = bf16[8,2688]{1,0:T(8,128)(2,1)S(1)} collective-permute-done((bf16[8,2688]{1,0:T(8,128)(2,1)S(1)}, bf16[8,2688]{1,0:T(8,128)(2,1)S(1)}, u32[]{:S(2)}, u32[]{:S(2)}) %collective-permute-start.12) | collective-permute-done | bytes 43040 | tf_op jit(solution)/shard_map/ppermute | solution.py:305
  32.3 1.2 %collective-permute-done.14.refs_2_ = bf16[8,2688]{1,0:T(8,128)(2,1)S(1)} collective-permute-done((bf16[8,2688]{1,0:T(8,128)(2,1)S(1)}, bf16[8,2688]{1,0:T(8,128)(2,1)S(1)}, u32[]{:S(2)}, u32[]{:S(2)}) %collective-permute-start.14) | collective-permute-done | bytes 43040 | tf_op jit(solution)/shard_map/ppermute | solution.py:305
  33.5 0.1 collective-permute-done.16.refs_3_
  33.6 0.9 %merge.15 = bf16[8,2560]{1,0:T(8,128)(2,1)} custom-call(f32[8,2688]{1,0:T(8,128)S(1)} %merge.11.refs_0_, bf16[8,2688]{1,0:T(8,128)(2,1)S(1)} %collective-permute-done.12.refs_1_, bf16[8,2688]{1,0:T(8,128)(2,1)S(1)} %collective-permute-done.14.refs_2_, bf16[8,2688]{1,0:T(8,128)(2,1)S(1)} %collective-permute-done.16.refs_3_), custom_call_target="tpu_custom_call" | custom-call | flops 344064 | bytes 344064 | tf_op jit(solution)/shard_map/merge/pallas_call | solution.py:282
  (12 shorter events, 0.1 us)
Async XLA Ops:
  0.0 7.4 %collective-permute-start.1 = (bf16[8,2560]{1,0:T(8,128)(2,1)}, bf16[8,2560]{1,0:T(8,128)(2,1)S(1)}, u32[]{:S(2)}, u32[]{:S(2)}) collective-permute-start(bf16[8,2560]{1,0:T(8,128)(2,1)} %refs_5_.1), channel_id=1, source_target_pairs={{12,0},{13,1},{14,2},{15,3},{8,4},{9,5},{10,6},{11,7},{4,8},{5,9},... | collective-permute-start | bytes 122888 | tf_op jit(solution)/shard_map/ppermute | solution.py:302
  5.0 5.1 %collective-permute-start = (bf16[8,2560]{1,0:T(8,128)(2,1)}, bf16[8,2560]{1,0:T(8,128)(2,1)S(1)}, u32[]{:S(2)}, u32[]{:S(2)}) collective-permute-start(bf16[8,2560]{1,0:T(8,128)(2,1)} %refs_5_.1), channel_id=1, source_target_pairs={{8,0},{9,1},{10,2},{11,3},{12,4},{13,5},{14,6},{15,7},{0,8},{1,9},... | collective-permute-start | bytes 122888 | tf_op jit(solution)/shard_map/ppermute | solution.py:302
  5.1 6.6 %collective-permute-start.2 = (bf16[8,2560]{1,0:T(8,128)(2,1)}, bf16[8,2560]{1,0:T(8,128)(2,1)S(1)}, u32[]{:S(2)}, u32[]{:S(2)}) collective-permute-start(bf16[8,2560]{1,0:T(8,128)(2,1)} %refs_5_.1), channel_id=1, source_target_pairs={{4,0},{5,1},{6,2},{7,3},{0,4},{1,5},{2,6},{3,7},{12,8},{13,9},{14,... | collective-permute-start | bytes 122888 | tf_op jit(solution)/shard_map/ppermute | solution.py:302
  5.6 9.2 %collective-permute-start.3 = (bf16[8,2560]{1,0:T(8,128)(2,1)}, bf16[8,2560]{1,0:T(8,128)(2,1)S(1)}, u32[]{:S(2)}, u32[]{:S(2)}) collective-permute-start(bf16[8,2560]{1,0:T(8,128)(2,1)} %refs_5_.1), channel_id=1, source_target_pairs={{2,0},{3,1},{0,2},{1,3},{6,4},{7,5},{4,6},{5,7},{10,8},{11,9},{8,1... | collective-permute-start | bytes 122888 | tf_op jit(solution)/shard_map/ppermute | solution.py:302
  7.4 7.5 %collective-permute-start.4 = (bf16[8,2560]{1,0:T(8,128)(2,1)S(1)}, bf16[8,2560]{1,0:T(8,128)(2,1)S(1)}, u32[]{:S(2)}, u32[]{:S(2)}) collective-permute-start(bf16[8,2560]{1,0:T(8,128)(2,1)S(1)} %collective-permute-done.1.refs_1_), channel_id=1, source_target_pairs={{2,0},{3,1},{0,2},{1,3},{6,4},{7,5},{4,6},{5,7},{10,8},{11,9},{8,1... | collective-permute-start | bytes 122888 | tf_op jit(solution)/shard_map/ppermute | solution.py:302
  10.2 4.7 %collective-permute-start.5 = (bf16[8,2560]{1,0:T(8,128)(2,1)S(1)}, bf16[8,2560]{1,0:T(8,128)(2,1)S(1)}, u32[]{:S(2)}, u32[]{:S(2)}) collective-permute-start(bf16[8,2560]{1,0:T(8,128)(2,1)S(1)} %collective-permute-done.refs_6_.refs_2_), channel_id=1, source_target_pairs={{2,0},{3,1},{0,2},{1,3},{6,4},{7,5},{4,6},{5,7},{10,8},{11,9},{8,1... | collective-permute-start | bytes 122888 | tf_op jit(solution)/shard_map/ppermute | solution.py:302
  11.7 4.0 %collective-permute-start.6 = (bf16[8,2560]{1,0:T(8,128)(2,1)S(1)}, bf16[8,2560]{1,0:T(8,128)(2,1)S(1)}, u32[]{:S(2)}, u32[]{:S(2)}) collective-permute-start(bf16[8,2560]{1,0:T(8,128)(2,1)S(1)} %collective-permute-done.2.refs_3_), channel_id=1, source_target_pairs={{2,0},{3,1},{0,2},{1,3},{6,4},{7,5},{4,6},{5,7},{10,8},{11,9},{8,1... | collective-permute-start | bytes 122888 | tf_op jit(solution)/shard_map/ppermute | solution.py:302
  15.7 1.7 %collective-permute-start.7 = (bf16[64,2560]{1,0:T(8,128)(2,1)S(1)}, bf16[64,2560]{1,0:T(8,128)(2,1)S(1)}, u32[]{:S(2)}, u32[]{:S(2)}) collective-permute-start(bf16[64,2560]{1,0:T(8,128)(2,1)S(1)} %merge.8.refs_1_), channel_id=1, source_target_pairs={{1,0},{0,1},{3,2},{2,3},{5,4},{4,5},{7,6},{6,7},{9,8},{8,9},{11,10... | collective-permute-start | bytes 983048 | tf_op jit(solution)/shard_map/ppermute | solution.py:302
  19.9 1.5 %collective-permute-start.9 = (bf16[32,2688]{1,0:T(8,128)(2,1)S(1)}, bf16[32,2688]{1,0:T(8,128)(2,1)S(1)}, u32[]{:S(2)}, u32[]{:S(2)}) collective-permute-start(bf16[32,2688]{1,0:T(8,128)(2,1)S(1)} %get-tuple-element.29), channel_id=1, source_target_pairs={{0,1},{1,0},{2,3},{3,2},{4,5},{5,4},{6,7},{7,6},{8,9},{9,8},{10,11... | collective-permute-start | bytes 516104 | tf_op jit(solution)/shard_map/ppermute | solution.py:305
  20.1 5.7 %collective-permute-start.8 = (bf16[32,2688]{1,0:T(8,128)(2,1)S(1)}, bf16[32,2688]{1,0:T(8,128)(2,1)S(1)}, u32[]{:S(2)}, u32[]{:S(2)}) collective-permute-start(bf16[32,2688]{1,0:T(8,128)(2,1)S(1)} %get-tuple-element.26), channel_id=1, source_target_pairs={{0,1},{1,0},{2,3},{3,2},{4,5},{5,4},{6,7},{7,6},{8,9},{9,8},{10,11... | collective-permute-start | bytes 516104 | tf_op jit(solution)/shard_map/ppermute | solution.py:305
  21.7 4.4 %collective-permute-start.11 = (bf16[8,2688]{1,0:T(8,128)(2,1)S(1)}, bf16[8,2688]{1,0:T(8,128)(2,1)S(1)}, u32[]{:S(2)}, u32[]{:S(2)}) collective-permute-start(bf16[8,2688]{1,0:T(8,128)(2,1)S(1)} %get-tuple-element.32), channel_id=1, source_target_pairs={{0,2},{1,3},{2,0},{3,1},{4,6},{5,7},{6,4},{7,5},{8,10},{9,11},{10,... | collective-permute-start | bytes 129032 | tf_op jit(solution)/shard_map/ppermute | solution.py:305
  22.5 5.7 %collective-permute-start.13 = (bf16[8,2688]{1,0:T(8,128)(2,1)S(1)}, bf16[8,2688]{1,0:T(8,128)(2,1)S(1)}, u32[]{:S(2)}, u32[]{:S(2)}) collective-permute-start(bf16[8,2688]{1,0:T(8,128)(2,1)S(1)} %get-tuple-element.34), channel_id=1, source_target_pairs={{0,2},{1,3},{2,0},{3,1},{4,6},{5,7},{6,4},{7,5},{8,10},{9,11},{10,... | collective-permute-start | bytes 129032 | tf_op jit(solution)/shard_map/ppermute | solution.py:305
  23.8 4.6 %collective-permute-start.15 = (bf16[8,2688]{1,0:T(8,128)(2,1)S(1)}, bf16[8,2688]{1,0:T(8,128)(2,1)S(1)}, u32[]{:S(2)}, u32[]{:S(2)}) collective-permute-start(bf16[8,2688]{1,0:T(8,128)(2,1)S(1)} %get-tuple-element.36), channel_id=1, source_target_pairs={{0,2},{1,3},{2,0},{3,1},{4,6},{5,7},{6,4},{7,5},{8,10},{9,11},{10,... | collective-permute-start | bytes 129032 | tf_op jit(solution)/shard_map/ppermute | solution.py:305
  24.5 6.6 %collective-permute-start.10 = (bf16[8,2688]{1,0:T(8,128)(2,1)S(1)}, bf16[8,2688]{1,0:T(8,128)(2,1)S(1)}, u32[]{:S(2)}, u32[]{:S(2)}) collective-permute-start(bf16[8,2688]{1,0:T(8,128)(2,1)S(1)} %get-tuple-element.30), channel_id=1, source_target_pairs={{0,2},{1,3},{2,0},{3,1},{4,6},{5,7},{6,4},{7,5},{8,10},{9,11},{10,... | collective-permute-start | bytes 129032 | tf_op jit(solution)/shard_map/ppermute | solution.py:305
  26.3 6.0 %collective-permute-start.12 = (bf16[8,2688]{1,0:T(8,128)(2,1)S(1)}, bf16[8,2688]{1,0:T(8,128)(2,1)S(1)}, u32[]{:S(2)}, u32[]{:S(2)}) collective-permute-start(bf16[8,2688]{1,0:T(8,128)(2,1)S(1)} %merge.12), channel_id=1, source_target_pairs={{0,12},{1,13},{2,14},{3,15},{4,8},{5,9},{6,10},{7,11},{8,4},{9,5},... | collective-permute-start | bytes 129032 | tf_op jit(solution)/shard_map/ppermute | solution.py:305
  28.3 5.2 %collective-permute-start.14 = (bf16[8,2688]{1,0:T(8,128)(2,1)S(1)}, bf16[8,2688]{1,0:T(8,128)(2,1)S(1)}, u32[]{:S(2)}, u32[]{:S(2)}) collective-permute-start(bf16[8,2688]{1,0:T(8,128)(2,1)S(1)} %merge.13), channel_id=1, source_target_pairs={{0,8},{1,9},{2,10},{3,11},{4,12},{5,13},{6,14},{7,15},{8,0},{9,1},... | collective-permute-start | bytes 129032 | tf_op jit(solution)/shard_map/ppermute | solution.py:305
  28.5 5.1 %collective-permute-start.16 = (bf16[8,2688]{1,0:T(8,128)(2,1)S(1)}, bf16[8,2688]{1,0:T(8,128)(2,1)S(1)}, u32[]{:S(2)}, u32[]{:S(2)}) collective-permute-start(bf16[8,2688]{1,0:T(8,128)(2,1)S(1)} %merge.14), channel_id=1, source_target_pairs={{0,4},{1,5},{2,6},{3,7},{4,0},{5,1},{6,2},{7,3},{8,12},{9,13},{10,... | collective-permute-start | bytes 129032 | tf_op jit(solution)/shard_map/ppermute | solution.py:305

commit v12 on v11

--- a/solution.py
+++ b/solution.py
@@ -159,61 +159,66 @@
     )(bias, *planes, keys, values)
 
 
-def load(cached, fresh, victims, queries, after):
-    cache_rows, columns = cached[0].shape
-    tok = fresh[0].shape[0]
+def load(cached, fresh, after, victims=None, queries=None):
+    cache_rows, columns = cached.shape
+    tok = fresh.shape[0]
     padded = cache_rows + -(-tok // 16) * 16
-    n = len(cached)
-
-    def body(*refs):
-        cached_refs, fresh_refs, victims_ref, queries_ref = refs[:n], refs[n : 2 * n], *refs[2 * n : 2 * n + 2]
-        refs = refs[2 * n + 3 :]
-        outs, bias_ref, q_ref, tails, ids_ref, sems = (
-            refs[:n], refs[n], refs[n + 1], refs[n + 2 : 2 * n + 2], *refs[2 * n + 2 :]
-        )
-        ids = pltpu.make_async_copy(victims_ref, ids_ref, sems.at[1, n])
-        rest = pltpu.make_async_copy(queries_ref, q_ref, sems.at[0, n])
-        small = [
-            pltpu.make_async_copy(src, dst, sems.at[1, i])
-            for i, (src, dst) in enumerate(zip(fresh_refs, tails))
-        ]
-        large = [
-            pltpu.make_async_copy(src, dst.at[pl.ds(0, cache_rows), :], sems.at[0, i])
-            for i, (src, dst) in enumerate(zip(cached_refs, outs))
-        ]
-        for copy in [ids] + small + large + [rest]:
-            copy.start()
-        ids.wait()
-        blocks = cache_rows // BLK
-        first = lax.axis_index("seq") * blocks
-        for block in range(blocks):
-            hits = jnp.where(ids_ref[...] == first + block, 1.0, 0.0)
-            hit = jnp.max(hits, axis=1, keepdims=True)
-            gone = jnp.where(hit > 0.0, NEG, 0.0)
-            bias_ref[block * BLK : (block + 1) * BLK, :] = jnp.broadcast_to(gone, (BLK, STAT))
-        token = lax.broadcasted_iota(jnp.int32, (padded - cache_rows, STAT), 0)
-        bias_ref[cache_rows:, :] = jnp.where(token < tok, 0.0, NEG)
-        for copy, tail, out in zip(small, tails, outs):
-            copy.wait()
-            zeros = jnp.zeros((padded - cache_rows - tok, columns), F32)
-            rows = jnp.concatenate([tail[...].astype(F32), zeros], axis=0)
-            out[cache_rows:, :] = rows.astype(out.dtype)
-        for copy in large + [rest]:
-            copy.wait()
+    blocks = cache_rows // BLK
+    extra = victims is not None
+
+    def body(*refs):
+        refs = iter(refs)
+        take = lambda n: [next(refs) for _ in range(n)]
+        cached_ref, fresh_ref = take(2)
+        sides = take(2) if extra else []
+        take(1)
+        out, = take(1)
+        bias_ref, q_ref = take(2) if extra else (None, None)
+        tail, sems = take(2)
+        large = pltpu.make_async_copy(cached_ref, out.at[pl.ds(0, cache_rows), :], sems.at[0])
+        small = pltpu.make_async_copy(fresh_ref, tail, sems.at[1])
+        small.start()
+        if extra:
+            ids_ref, = take(1)
+            ids = pltpu.make_async_copy(sides[0], ids_ref, sems.at[2])
+            rest = pltpu.make_async_copy(sides[1], q_ref, sems.at[3])
+            ids.start()
+        large.start()
+        if extra:
+            rest.start()
+            ids.wait()
+            first = lax.axis_index("seq") * blocks
+            for block in range(blocks):
+                hits = jnp.where(ids_ref[...] == first + block, 1.0, 0.0)
+                hit = jnp.max(hits, axis=1, keepdims=True)
+                gone = jnp.where(hit > 0.0, NEG, 0.0)
+                bias_ref[block * BLK : (block + 1) * BLK, :] = jnp.broadcast_to(gone, (BLK, STAT))
+            token = lax.broadcasted_iota(jnp.int32, (padded - cache_rows, STAT), 0)
+            bias_ref[cache_rows:, :] = jnp.where(token < tok, 0.0, NEG)
+        small.wait()
+        zeros = jnp.zeros((padded - cache_rows - tok, columns), F32)
+        rows = [tail[...].astype(F32)] + ([zeros] if zeros.shape[0] else [])
+        out[cache_rows:, :] = jnp.concatenate(rows, axis=0).astype(out.dtype)
+        if extra:
+            rest.wait()
+        large.wait()
 
     in_hbm = pl.BlockSpec(memory_space=pltpu.HBM)
-    held = (*cached, *fresh, victims, queries)
+    held = (cached, fresh) + ((victims, queries) if extra else ())
+    shapes = [jax.ShapeDtypeStruct((padded, columns), BF16)]
+    scratch = [pltpu.VMEM(fresh.shape, BF16), pltpu.SemaphoreType.DMA((4,))]
+    if extra:
+        shapes += [jax.ShapeDtypeStruct((padded, STAT), F32), jax.ShapeDtypeStruct(queries.shape, BF16)]
+        scratch += [pltpu.VMEM(victims.shape, jnp.int32)]
     return pl.pallas_call(
         body,
         in_specs=[in_hbm] * len(held) + [pl.BlockSpec(memory_space=pl.ANY)],
-        out_specs=[pl.BlockSpec(memory_space=pltpu.VMEM)] * (n + 2),
-        out_shape=[jax.ShapeDtypeStruct((padded, columns), BF16)] * n
-        + [jax.ShapeDtypeStruct((padded, STAT), F32), jax.ShapeDtypeStruct(queries.shape, BF16)],
-        scratch_shapes=[pltpu.VMEM(x.shape, BF16) for x in fresh]
-        + [pltpu.VMEM(victims.shape, jnp.int32), pltpu.SemaphoreType.DMA((2, n + 1))],
+        out_specs=[pl.BlockSpec(memory_space=pltpu.VMEM)] * len(shapes),
+        out_shape=shapes,
+        scratch_shapes=scratch,
         compiler_params=pltpu.CompilerParams(vmem_limit_bytes=24 * 1024 * 1024),
         cost_estimate=pl.CostEstimate(
-            flops=0, bytes_accessed=4 * n * cache_rows * columns, transcendentals=0
+            flops=0, bytes_accessed=4 * cache_rows * columns, transcendentals=0
         ),
         name="load",
     )(*[pltpu.with_memory_space_constraint(x, pltpu.HBM) for x in held], after)
@@ -305,27 +310,39 @@
         return lax.ppermute(x, "seq", partner_perm(shape, by, True))
 
     far_first = [0, *range(a_n - 1, 0, -1)]
+    staged = max(a_n - 1, 1)
     line = [queries] + [fetch(queries, a, 0, 0) for a in far_first[1:]]
-    lines = [line] + [[fetch(x, 0, b, 0) for x in line] for b in range(1, b_n)]
-    keys, values, bias, line[0] = load(
-        (cache_keys, cache_values), (new_keys, new_values), victims[None], queries, line[min(2, a_n - 1)]
+    lines = [line]
+    for b in range(1, b_n):
+        direct = [fetch(queries, a, b, 0) for a in far_first[staged:]]
+        lines.append([fetch(x, 0, b, 0) for x in line[:staged]] + direct)
+    keys, bias, line[0] = load(
+        cache_keys, new_keys, line[min(2, a_n - 1)], victims[None], queries
     )
-    plane = join([x for pieces in lines for x in pieces])
+    plane = join([x for pieces in lines for x in pieces], (keys,))
     planes = [plane] + [fetch(plane, 0, 0, c) for c in range(1, c_n)]
+    values = load(cache_values, new_values, plane)[0]
     kinds = [F32] * b_n + [BF16] * (b_n * (c_n - 1))
     sums = attend(planes, b_n, kinds, keys, values, bias)
 
-    def over_cores(b, kind):
+    def over_cores(b, kinds):
         got = [give(sums[c * b_n + b], 0, 0, c) for c in range(1, c_n)]
-        return merge_rows([sums[b]] + got, heads, a_n, [kind] * a_n)
-
-    got = [[give(x, 0, b, 0) for x in over_cores(b, BF16)] for b in range(1, b_n)]
-    own = over_cores(0, F32)
-    total = [[own[s]] + [pieces[s] for pieces in got] for s in range(a_n)]
+        return merge_rows([sums[b]] + got, heads, a_n, kinds)
+
+    got = [over_cores(b, [BF16] * a_n) for b in range(1, b_n)]
+    own = over_cores(0, [F32] * staged + [BF16] * (a_n - staged))
+    near = [
+        give(pieces[s], far_first[s], b, 0)
+        for s in range(staged, a_n)
+        for b, pieces in enumerate([own, *got])
+    ]
+    got = [[give(x, 0, b, 0) for x in pieces[:staged]] for b, pieces in enumerate(got, 1)]
+    total = [[own[s]] + [pieces[s] for pieces in got] for s in range(staged)]
     last = [
-        give(merge_rows(total[s], heads, 1, [BF16])[0], far_first[s], 0, 0) for s in range(1, a_n)
+        give(merge_rows(total[s], heads, 1, [BF16])[0], far_first[s], 0, 0)
+        for s in range(1, staged)
     ]
-    return finish([*merge_rows(total[0], heads, 1, [F32]), *last], heads)
+    return finish([*merge_rows(total[0] + near, heads, 1, [F32]), *last], heads)
 
 
 def solution(mesh):

time: 34.7 us -> 36.2 us (1.043)
  Pallas kernels: 7.23 us -> 8.1 us
  starting transfers between devices: 20.5 us -> 21 us
    ppermute x9, waiting for transfers between devices: 3.22 us -> 6.08 us  [give(): return lax.ppermute(x, 'seq', partner_perm(shape, by, True))]
    ppermute x8, waiting for transfers between devices: 3.46 us -> 0.68 us  [fetch(): return lax.ppermute(x, 'seq', partner_perm(shape, by, False))]
    pallas_call x1 -> x2, Pallas kernels: 2.65 us -> 3.62 us  [load(): pl.pallas_call(body, in_specs=[in_hbm] * len(held) + [pl.BlockSpec(memory...]
    ppermute x8, starting transfers between devices: 11.2 us -> 11.7 us  [fetch(): return lax.ppermute(x, 'seq', partner_perm(shape, by, False))]
    pallas_call x8 -> x7, Pallas kernels: 2.06 us -> 1.96 us  [call_merge(): pl.pallas_call(body, in_specs=[pl.BlockSpec(memory_space=pltpu.VMEM)] * l...]
  transfers between devices with their start and end apart: 17 -> 17, of which waited for: 7 -> 5; matrix products, arithmetic and copies ran while one was open for 0% -> 0% of each run, Pallas kernels for 11% -> 13%
where the time goes in v12:
time: 36.2 us; the launch traced here: 36 us
  starting transfers between devices  21 us (58%)
  Pallas kernels  8.1 us (22%)
  waiting for transfers between devices  6.75 us (19%)
    ppermute x8, starting transfers between devices, fetch(): return lax.ppermute(x, 'seq', partner_perm(shape, by, False))  11.7 us
    ppermute x9, starting transfers between devices, give(): return lax.ppermute(x, 'seq', partner_perm(shape, by, True))  9.3 us
    ppermute x9, waiting for transfers between devices, give(): return lax.ppermute(x, 'seq', partner_perm(shape, by, True))  6.08 us
    pallas_call x2, Pallas kernels, load(): pl.pallas_call(body, in_specs=[in_hbm] * len(held) + [pl.BlockSpec(memory...  3.62 us
    pallas_call x1, Pallas kernels, attend(): pl.pallas_call(body, in_specs=[pl.BlockSpec(memory_space=pltpu.VMEM)] * (...  2.53 us
    pallas_call x7, Pallas kernels, call_merge(): pl.pallas_call(body, in_specs=[pl.BlockSpec(memory_space=pltpu.VMEM)] * l...  1.96 us
  transfers between devices with their start and end apart: 17, of which 5 were waited for; matrix products, arithmetic and copies ran while one was open for 0% of the time, Pallas kernels for 13%

profile of v12, /device:TPU:0, one launch (start us, length us, event | category | flops | bytes accessed | tf_op | source)
XLA Modules:
  0.0 36.0 jit_solution(9643154104668635725)
XLA Ops:
  0.0 5.0 %collective-permute-start.1 = (bf16[8,2560]{1,0:T(8,128)(2,1)}, bf16[8,2560]{1,0:T(8,128)(2,1)S(1)}, u32[]{:S(2)}, u32[]{:S(2)}) collective-permute-start(bf16[8,2560]{1,0:T(8,128)(2,1)} %refs_3_.1), channel_id=1, source_target_pairs={{12,0},{13,1},{14,2},{15,3},{8,4},{9,5},{10,6},{11,7},{4,8},{5,9},... | collective-permute-start | bytes 122888 | tf_op jit(solution)/shard_map/ppermute | solution.py:307
  5.0 0.0 collective-permute-start
  5.1 0.6 %collective-permute-start.2 = (bf16[8,2560]{1,0:T(8,128)(2,1)}, bf16[8,2560]{1,0:T(8,128)(2,1)S(1)}, u32[]{:S(2)}, u32[]{:S(2)}) collective-permute-start(bf16[8,2560]{1,0:T(8,128)(2,1)} %refs_3_.1), channel_id=1, source_target_pairs={{4,0},{5,1},{6,2},{7,3},{0,4},{1,5},{2,6},{3,7},{12,8},{13,9},{14,... | collective-permute-start | bytes 122888 | tf_op jit(solution)/shard_map/ppermute | solution.py:307
  5.6 2.4 %collective-permute-start.6 = (bf16[8,2560]{1,0:T(8,128)(2,1)}, bf16[8,2560]{1,0:T(8,128)(2,1)S(1)}, u32[]{:S(2)}, u32[]{:S(2)}) collective-permute-start(bf16[8,2560]{1,0:T(8,128)(2,1)} %refs_3_.1), channel_id=1, source_target_pairs={{6,0},{7,1},{4,2},{5,3},{2,4},{3,5},{0,6},{1,7},{14,8},{15,9},{12,... | collective-permute-start | bytes 122888 | tf_op jit(solution)/shard_map/ppermute | solution.py:307
  8.0 0.5 %collective-permute-start.3 = (bf16[8,2560]{1,0:T(8,128)(2,1)}, bf16[8,2560]{1,0:T(8,128)(2,1)S(1)}, u32[]{:S(2)}, u32[]{:S(2)}) collective-permute-start(bf16[8,2560]{1,0:T(8,128)(2,1)} %refs_3_.1), channel_id=1, source_target_pairs={{2,0},{3,1},{0,2},{1,3},{6,4},{7,5},{4,6},{5,7},{10,8},{11,9},{8,1... | collective-permute-start | bytes 122888 | tf_op jit(solution)/shard_map/ppermute | solution.py:307
  8.5 0.0 collective-permute-done.1.refs_1_
  8.5 1.5 %collective-permute-start.4 = (bf16[8,2560]{1,0:T(8,128)(2,1)S(1)}, bf16[8,2560]{1,0:T(8,128)(2,1)S(1)}, u32[]{:S(2)}, u32[]{:S(2)}) collective-permute-start(bf16[8,2560]{1,0:T(8,128)(2,1)S(1)} %collective-permute-done.1.refs_1_), channel_id=1, source_target_pairs={{2,0},{3,1},{0,2},{1,3},{6,4},{7,5},{4,6},{5,7},{10,8},{11,9},{8,1... | collective-permute-start | bytes 122888 | tf_op jit(solution)/shard_map/ppermute | solution.py:307
  10.1 0.1 collective-permute-done.refs_4_.refs_2_
  10.2 1.6 %collective-permute-start.5 = (bf16[8,2560]{1,0:T(8,128)(2,1)S(1)}, bf16[8,2560]{1,0:T(8,128)(2,1)S(1)}, u32[]{:S(2)}, u32[]{:S(2)}) collective-permute-start(bf16[8,2560]{1,0:T(8,128)(2,1)S(1)} %collective-permute-done.refs_4_.refs_2_), channel_id=1, source_target_pairs={{2,0},{3,1},{0,2},{1,3},{6,4},{7,5},{4,6},{5,7},{10,8},{11,9},{8,1... | collective-permute-start | bytes 122888 | tf_op jit(solution)/shard_map/ppermute | solution.py:307
  11.7 1.8 %load.2 = (bf16[528,2560]{1,0:T(8,128)(2,1)S(1)}, f32[528,128]{1,0:T(8,128)S(1)}, bf16[8,2560]{1,0:T(8,128)(2,1)S(1)}) custom-call(bf16[512,2560]{1,0:T(8,128)(2,1)} %refs_0_.2, bf16[8,2560]{1,0:T(8,128)(2,1)} %refs_1_.2, s32[1,16]{1,0:T(1,128)} %bitcast.1, bf16[8,2560]{1,0:T(8,128)(2,1)} %refs_3_.1, bf16[8,2560]{1,0:T(8,128)(2,1)S(1)} %collective-permute-done.refs_4_.refs_2_), custom_call_target="tpu_custom_call" | custom-call | bytes 5242880 | tf_op jit(solution)/shard_map/load/pallas_call | solution.py:213
  13.6 0.6 %collective-permute-done.5.refs_6_ = bf16[8,2560]{1,0:T(8,128)(2,1)S(1)} collective-permute-done((bf16[8,2560]{1,0:T(8,128)(2,1)S(1)}, bf16[8,2560]{1,0:T(8,128)(2,1)S(1)}, u32[]{:S(2)}, u32[]{:S(2)}) %collective-permute-start.5) | collective-permute-done | bytes 40992 | tf_op jit(solution)/shard_map/ppermute | solution.py:307
  14.2 0.1 collective-permute-start.7
  14.3 1.8 %load.3.refs_4_ = bf16[528,2560]{1,0:T(8,128)(2,1)S(1)} custom-call(bf16[512,2560]{1,0:T(8,128)(2,1)} %refs_0_.3, bf16[8,2560]{1,0:T(8,128)(2,1)} %refs_1_.3, bf16[64,2560]{1,0:T(8,128)(2,1)S(1)} %merge.7.refs_2_.refs_1_), custom_call_target="tpu_custom_call" | custom-call | bytes 5242880 | tf_op jit(solution)/shard_map/load/pallas_call | solution.py:213
  16.1 2.5 %attend.1 = (f32[32,2688]{1,0:T(8,128)S(1)}, f32[32,2688]{1,0:T(8,128)S(1)}, bf16[32,2688]{1,0:T(8,128)(2,1)S(1)}, bf16[32,2688]{1,0:T(8,128)(2,1)S(1)}) custom-call(f32[528,128]{1,0:T(8,128)S(1)} %get-tuple-element.20.refs_0_, bf16[64,2560]{1,0:T(8,128)(2,1)S(1)} %merge.7.refs_2_.refs_1_, bf16[64,2560]{1,0:T(8,128)(2,1)S(1)} %collective-permute-done.7.refs_2_, ...), custom_call_target="tpu_custom_call" | custom-call | flops 692060160 | bytes 5406720 | tf_op jit(solution)/shard_map/attend/pallas_call | solution.py:146
  18.6 0.6 %collective-permute-start.9 = (bf16[32,2688]{1,0:T(8,128)(2,1)S(1)}, bf16[32,2688]{1,0:T(8,128)(2,1)S(1)}, u32[]{:S(2)}, u32[]{:S(2)}) collective-permute-start(bf16[32,2688]{1,0:T(8,128)(2,1)S(1)} %get-tuple-element.27), channel_id=1, source_target_pairs={{0,1},{1,0},{2,3},{3,2},{4,5},{5,4},{6,7},{7,6},{8,9},{9,8},{10,11... | collective-permute-start | bytes 516104 | tf_op jit(solution)/shard_map/ppermute | solution.py:310
  19.2 0.1 collective-permute-start.8
  19.3 1.0 %collective-permute-done.9.refs_1_ = bf16[32,2688]{1,0:T(8,128)(2,1)S(1)} collective-permute-done((bf16[32,2688]{1,0:T(8,128)(2,1)S(1)}, bf16[32,2688]{1,0:T(8,128)(2,1)S(1)}, u32[]{:S(2)}, u32[]{:S(2)}) %collective-permute-start.9) | collective-permute-done | bytes 172064 | tf_op jit(solution)/shard_map/ppermute | solution.py:310
  20.2 0.3 merge.9
  20.5 1.7 %collective-permute-start.13 = (bf16[8,2688]{1,0:T(8,128)(2,1)S(1)}, bf16[8,2688]{1,0:T(8,128)(2,1)S(1)}, u32[]{:S(2)}, u32[]{:S(2)}) collective-permute-start(bf16[8,2688]{1,0:T(8,128)(2,1)S(1)} %get-tuple-element.32), channel_id=1, source_target_pairs={{0,2},{1,3},{2,0},{3,1},{4,6},{5,7},{6,4},{7,5},{8,10},{9,11},{10,... | collective-permute-start | bytes 129032 | tf_op jit(solution)/shard_map/ppermute | solution.py:310
  22.2 0.4 %collective-permute-start.15 = (bf16[8,2688]{1,0:T(8,128)(2,1)S(1)}, bf16[8,2688]{1,0:T(8,128)(2,1)S(1)}, u32[]{:S(2)}, u32[]{:S(2)}) collective-permute-start(bf16[8,2688]{1,0:T(8,128)(2,1)S(1)} %get-tuple-element.34), channel_id=1, source_target_pairs={{0,2},{1,3},{2,0},{3,1},{4,6},{5,7},{6,4},{7,5},{8,10},{9,11},{10,... | collective-permute-start | bytes 129032 | tf_op jit(solution)/shard_map/ppermute | solution.py:310
  22.6 0.3 merge.8
  22.9 0.8 %collective-permute-start.11 = (bf16[8,2688]{1,0:T(8,128)(2,1)S(1)}, bf16[8,2688]{1,0:T(8,128)(2,1)S(1)}, u32[]{:S(2)}, u32[]{:S(2)}) collective-permute-start(bf16[8,2688]{1,0:T(8,128)(2,1)S(1)} %get-tuple-element.29), channel_id=1, source_target_pairs={{0,4},{1,5},{2,6},{3,7},{4,0},{5,1},{6,2},{7,3},{8,12},{9,13},{10,... | collective-permute-start | bytes 129032 | tf_op jit(solution)/shard_map/ppermute | solution.py:310
  23.7 1.0 %collective-permute-start.10 = (bf16[8,2688]{1,0:T(8,128)(2,1)S(1)}, bf16[8,2688]{1,0:T(8,128)(2,1)S(1)}, u32[]{:S(2)}, u32[]{:S(2)}) collective-permute-start(bf16[8,2688]{1,0:T(8,128)(2,1)S(1)} %get-tuple-element.28), channel_id=1, source_target_pairs={{0,2},{1,3},{2,0},{3,1},{4,6},{5,7},{6,4},{7,5},{8,10},{9,11},{10,... | collective-permute-start | bytes 129032 | tf_op jit(solution)/shard_map/ppermute | solution.py:310
  24.6 1.8 %collective-permute-start.12 = (bf16[8,2688]{1,0:T(8,128)(2,1)S(1)}, bf16[8,2688]{1,0:T(8,128)(2,1)S(1)}, u32[]{:S(2)}, u32[]{:S(2)}) collective-permute-start(bf16[8,2688]{1,0:T(8,128)(2,1)S(1)} %get-tuple-element.30), channel_id=1, source_target_pairs={{0,6},{1,7},{2,4},{3,5},{4,2},{5,3},{6,0},{7,1},{8,14},{9,15},{10,... | collective-permute-start | bytes 129032 | tf_op jit(solution)/shard_map/ppermute | solution.py:310
  26.5 0.1 merge.11
  26.6 2.9 %collective-permute-start.14 = (bf16[8,2688]{1,0:T(8,128)(2,1)S(1)}, bf16[8,2688]{1,0:T(8,128)(2,1)S(1)}, u32[]{:S(2)}, u32[]{:S(2)}) collective-permute-start(bf16[8,2688]{1,0:T(8,128)(2,1)S(1)} %merge.11), channel_id=1, source_target_pairs={{0,12},{1,13},{2,14},{3,15},{4,8},{5,9},{6,10},{7,11},{8,4},{9,5},... | collective-permute-start | bytes 129032 | tf_op jit(solution)/shard_map/ppermute | solution.py:310
  29.6 0.1 merge.12
  29.7 0.1 collective-permute-start.16
  29.8 0.2 merge.10.refs_0_
  30.0 2.9 %collective-permute-done.14.refs_1_ = bf16[8,2688]{1,0:T(8,128)(2,1)S(1)} collective-permute-done((bf16[8,2688]{1,0:T(8,128)(2,1)S(1)}, bf16[8,2688]{1,0:T(8,128)(2,1)S(1)}, u32[]{:S(2)}, u32[]{:S(2)}) %collective-permute-start.14) | collective-permute-done | bytes 43040 | tf_op jit(solution)/shard_map/ppermute | solution.py:310
  32.9 2.2 %collective-permute-done.16.refs_2_ = bf16[8,2688]{1,0:T(8,128)(2,1)S(1)} collective-permute-done((bf16[8,2688]{1,0:T(8,128)(2,1)S(1)}, bf16[8,2688]{1,0:T(8,128)(2,1)S(1)}, u32[]{:S(2)}, u32[]{:S(2)}) %collective-permute-start.16) | collective-permute-done | bytes 43040 | tf_op jit(solution)/shard_map/ppermute | solution.py:310
  35.1 0.9 %merge.13 = bf16[8,2560]{1,0:T(8,128)(2,1)} custom-call(f32[8,2688]{1,0:T(8,128)S(1)} %merge.10.refs_0_, bf16[8,2688]{1,0:T(8,128)(2,1)S(1)} %collective-permute-done.14.refs_1_, bf16[8,2688]{1,0:T(8,128)(2,1)S(1)} %collective-permute-done.16.refs_2_), custom_call_target="tpu_custom_call" | custom-call | flops 258048 | bytes 258048 | tf_op jit(solution)/shard_map/merge/pallas_call | solution.py:287
  (12 shorter events, 0.1 us)
Async XLA Ops:
  0.0 8.5 %collective-permute-start.1 = (bf16[8,2560]{1,0:T(8,128)(2,1)}, bf16[8,2560]{1,0:T(8,128)(2,1)S(1)}, u32[]{:S(2)}, u32[]{:S(2)}) collective-permute-start(bf16[8,2560]{1,0:T(8,128)(2,1)} %refs_3_.1), channel_id=1, source_target_pairs={{12,0},{13,1},{14,2},{15,3},{8,4},{9,5},{10,6},{11,7},{4,8},{5,9},... | collective-permute-start | bytes 122888 | tf_op jit(solution)/shard_map/ppermute | solution.py:307
  5.0 5.1 %collective-permute-start = (bf16[8,2560]{1,0:T(8,128)(2,1)}, bf16[8,2560]{1,0:T(8,128)(2,1)S(1)}, u32[]{:S(2)}, u32[]{:S(2)}) collective-permute-start(bf16[8,2560]{1,0:T(8,128)(2,1)} %refs_3_.1), channel_id=1, source_target_pairs={{8,0},{9,1},{10,2},{11,3},{12,4},{13,5},{14,6},{15,7},{0,8},{1,9},... | collective-permute-start | bytes 122888 | tf_op jit(solution)/shard_map/ppermute | solution.py:307
  5.1 8.5 %collective-permute-start.2 = (bf16[8,2560]{1,0:T(8,128)(2,1)}, bf16[8,2560]{1,0:T(8,128)(2,1)S(1)}, u32[]{:S(2)}, u32[]{:S(2)}) collective-permute-start(bf16[8,2560]{1,0:T(8,128)(2,1)} %refs_3_.1), channel_id=1, source_target_pairs={{4,0},{5,1},{6,2},{7,3},{0,4},{1,5},{2,6},{3,7},{12,8},{13,9},{14,... | collective-permute-start | bytes 122888 | tf_op jit(solution)/shard_map/ppermute | solution.py:307
  5.6 8.0 %collective-permute-start.6 = (bf16[8,2560]{1,0:T(8,128)(2,1)}, bf16[8,2560]{1,0:T(8,128)(2,1)S(1)}, u32[]{:S(2)}, u32[]{:S(2)}) collective-permute-start(bf16[8,2560]{1,0:T(8,128)(2,1)} %refs_3_.1), channel_id=1, source_target_pairs={{6,0},{7,1},{4,2},{5,3},{2,4},{3,5},{0,6},{1,7},{14,8},{15,9},{12,... | collective-permute-start | bytes 122888 | tf_op jit(solution)/shard_map/ppermute | solution.py:307
  8.0 5.5 %collective-permute-start.3 = (bf16[8,2560]{1,0:T(8,128)(2,1)}, bf16[8,2560]{1,0:T(8,128)(2,1)S(1)}, u32[]{:S(2)}, u32[]{:S(2)}) collective-permute-start(bf16[8,2560]{1,0:T(8,128)(2,1)} %refs_3_.1), channel_id=1, source_target_pairs={{2,0},{3,1},{0,2},{1,3},{6,4},{7,5},{4,6},{5,7},{10,8},{11,9},{8,1... | collective-permute-start | bytes 122888 | tf_op jit(solution)/shard_map/ppermute | solution.py:307
  8.5 5.0 %collective-permute-start.4 = (bf16[8,2560]{1,0:T(8,128)(2,1)S(1)}, bf16[8,2560]{1,0:T(8,128)(2,1)S(1)}, u32[]{:S(2)}, u32[]{:S(2)}) collective-permute-start(bf16[8,2560]{1,0:T(8,128)(2,1)S(1)} %collective-permute-done.1.refs_1_), channel_id=1, source_target_pairs={{2,0},{3,1},{0,2},{1,3},{6,4},{7,5},{4,6},{5,7},{10,8},{11,9},{8,1... | collective-permute-start | bytes 122888 | tf_op jit(solution)/shard_map/ppermute | solution.py:307
  10.2 4.0 %collective-permute-start.5 = (bf16[8,2560]{1,0:T(8,128)(2,1)S(1)}, bf16[8,2560]{1,0:T(8,128)(2,1)S(1)}, u32[]{:S(2)}, u32[]{:S(2)}) collective-permute-start(bf16[8,2560]{1,0:T(8,128)(2,1)S(1)} %collective-permute-done.refs_4_.refs_2_), channel_id=1, source_target_pairs={{2,0},{3,1},{0,2},{1,3},{6,4},{7,5},{4,6},{5,7},{10,8},{11,9},{8,1... | collective-permute-start | bytes 122888 | tf_op jit(solution)/shard_map/ppermute | solution.py:307
  14.2 1.9 %collective-permute-start.7 = (bf16[64,2560]{1,0:T(8,128)(2,1)S(1)}, bf16[64,2560]{1,0:T(8,128)(2,1)S(1)}, u32[]{:S(2)}, u32[]{:S(2)}) collective-permute-start(bf16[64,2560]{1,0:T(8,128)(2,1)S(1)} %merge.7.refs_2_.refs_1_), channel_id=1, source_target_pairs={{1,0},{0,1},{3,2},{2,3},{5,4},{4,5},{7,6},{6,7},{9,8},{8,9},{11,10... | collective-permute-start | bytes 983048 | tf_op jit(solution)/shard_map/ppermute | solution.py:307
  18.6 1.6 %collective-permute-start.9 = (bf16[32,2688]{1,0:T(8,128)(2,1)S(1)}, bf16[32,2688]{1,0:T(8,128)(2,1)S(1)}, u32[]{:S(2)}, u32[]{:S(2)}) collective-permute-start(bf16[32,2688]{1,0:T(8,128)(2,1)S(1)} %get-tuple-element.27), channel_id=1, source_target_pairs={{0,1},{1,0},{2,3},{3,2},{4,5},{5,4},{6,7},{7,6},{8,9},{9,8},{10,11... | collective-permute-start | bytes 516104 | tf_op jit(solution)/shard_map/ppermute | solution.py:310
  19.2 3.4 %collective-permute-start.8 = (bf16[32,2688]{1,0:T(8,128)(2,1)S(1)}, bf16[32,2688]{1,0:T(8,128)(2,1)S(1)}, u32[]{:S(2)}, u32[]{:S(2)}) collective-permute-start(bf16[32,2688]{1,0:T(8,128)(2,1)S(1)} %get-tuple-element.24), channel_id=1, source_target_pairs={{0,1},{1,0},{2,3},{3,2},{4,5},{5,4},{6,7},{7,6},{8,9},{9,8},{10,11... | collective-permute-start | bytes 516104 | tf_op jit(solution)/shard_map/ppermute | solution.py:310
  20.5 6.0 %collective-permute-start.13 = (bf16[8,2688]{1,0:T(8,128)(2,1)S(1)}, bf16[8,2688]{1,0:T(8,128)(2,1)S(1)}, u32[]{:S(2)}, u32[]{:S(2)}) collective-permute-start(bf16[8,2688]{1,0:T(8,128)(2,1)S(1)} %get-tuple-element.32), channel_id=1, source_target_pairs={{0,2},{1,3},{2,0},{3,1},{4,6},{5,7},{6,4},{7,5},{8,10},{9,11},{10,... | collective-permute-start | bytes 129032 | tf_op jit(solution)/shard_map/ppermute | solution.py:310
  22.2 7.4 %collective-permute-start.15 = (bf16[8,2688]{1,0:T(8,128)(2,1)S(1)}, bf16[8,2688]{1,0:T(8,128)(2,1)S(1)}, u32[]{:S(2)}, u32[]{:S(2)}) collective-permute-start(bf16[8,2688]{1,0:T(8,128)(2,1)S(1)} %get-tuple-element.34), channel_id=1, source_target_pairs={{0,2},{1,3},{2,0},{3,1},{4,6},{5,7},{6,4},{7,5},{8,10},{9,11},{10,... | collective-permute-start | bytes 129032 | tf_op jit(solution)/shard_map/ppermute | solution.py:310
  22.9 6.9 %collective-permute-start.11 = (bf16[8,2688]{1,0:T(8,128)(2,1)S(1)}, bf16[8,2688]{1,0:T(8,128)(2,1)S(1)}, u32[]{:S(2)}, u32[]{:S(2)}) collective-permute-start(bf16[8,2688]{1,0:T(8,128)(2,1)S(1)} %get-tuple-element.29), channel_id=1, source_target_pairs={{0,4},{1,5},{2,6},{3,7},{4,0},{5,1},{6,2},{7,3},{8,12},{9,13},{10,... | collective-permute-start | bytes 129032 | tf_op jit(solution)/shard_map/ppermute | solution.py:310
  23.7 6.1 %collective-permute-start.10 = (bf16[8,2688]{1,0:T(8,128)(2,1)S(1)}, bf16[8,2688]{1,0:T(8,128)(2,1)S(1)}, u32[]{:S(2)}, u32[]{:S(2)}) collective-permute-start(bf16[8,2688]{1,0:T(8,128)(2,1)S(1)} %get-tuple-element.28), channel_id=1, source_target_pairs={{0,2},{1,3},{2,0},{3,1},{4,6},{5,7},{6,4},{7,5},{8,10},{9,11},{10,... | collective-permute-start | bytes 129032 | tf_op jit(solution)/shard_map/ppermute | solution.py:310
  24.6 5.2 %collective-permute-start.12 = (bf16[8,2688]{1,0:T(8,128)(2,1)S(1)}, bf16[8,2688]{1,0:T(8,128)(2,1)S(1)}, u32[]{:S(2)}, u32[]{:S(2)}) collective-permute-start(bf16[8,2688]{1,0:T(8,128)(2,1)S(1)} %get-tuple-element.30), channel_id=1, source_target_pairs={{0,6},{1,7},{2,4},{3,5},{4,2},{5,3},{6,0},{7,1},{8,14},{9,15},{10,... | collective-permute-start | bytes 129032 | tf_op jit(solution)/shard_map/ppermute | solution.py:310
  26.6 6.3 %collective-permute-start.14 = (bf16[8,2688]{1,0:T(8,128)(2,1)S(1)}, bf16[8,2688]{1,0:T(8,128)(2,1)S(1)}, u32[]{:S(2)}, u32[]{:S(2)}) collective-permute-start(bf16[8,2688]{1,0:T(8,128)(2,1)S(1)} %merge.11), channel_id=1, source_target_pairs={{0,12},{1,13},{2,14},{3,15},{4,8},{5,9},{6,10},{7,11},{8,4},{9,5},... | collective-permute-start | bytes 129032 | tf_op jit(solution)/shard_map/ppermute | solution.py:310
  29.7 5.4 %collective-permute-start.16 = (bf16[8,2688]{1,0:T(8,128)(2,1)S(1)}, bf16[8,2688]{1,0:T(8,128)(2,1)S(1)}, u32[]{:S(2)}, u32[]{:S(2)}) collective-permute-start(bf16[8,2688]{1,0:T(8,128)(2,1)S(1)} %merge.12), channel_id=1, source_target_pairs={{0,8},{1,9},{2,10},{3,11},{4,12},{5,13},{6,14},{7,15},{8,0},{9,1},... | collective-permute-start | bytes 129032 | tf_op jit(solution)/shard_map/ppermute | solution.py:310

commit v13 on v11

--- a/solution.py
+++ b/solution.py
@@ -53,7 +53,7 @@
     return jnp.where(used, packed, 0.0), jnp.where(used, mass, 0.0)
 
 
-def attend_kernel(sizes, scale, bias_ref, q_refs, k_ref, v_ref, outs, top_acc, mass_acc):
+def attend_kernel(sizes, scale, bias_ref, q_refs, k_ref, v_refs, outs, top_acc, mass_acc):
     tile, steps, group, pack, lines = sizes
     rows = tile * len(outs)
     line_rows = outs[0].shape[0]
@@ -97,12 +97,13 @@
                 for k in range(pack):
                     head = (step * group + i) * pack + k
                     cols = pl.ds(pl.multiple_of(head * HD, HD), HD)
-                    one = lax.dot_general(
-                        weights[:, k * rows : (k + 1) * rows],
-                        v_ref[:, cols],
-                        contract_first,
-                        preferred_element_type=F32,
-                    )
+                    one, start = 0.0, 0
+                    for v_ref in v_refs:
+                        part = weights[start : start + v_ref.shape[0], k * rows : (k + 1) * rows]
+                        start += v_ref.shape[0]
+                        one += lax.dot_general(
+                            part, v_ref[:, cols], contract_first, preferred_element_type=F32
+                        )
                     for p, o_ref in enumerate(outs):
                         o_ref[at, cols] = one[p * tile : (p + 1) * tile].astype(o_ref.dtype)
 
@@ -128,7 +129,7 @@
 
 
 def attend(planes, lines, kinds, keys, values, bias):
-    n, m = len(planes), len(kinds)
+    n, m, v = len(planes), len(kinds), len(values)
     rows, columns = planes[0].shape[0] // lines, planes[0].shape[1]
     heads = columns // HD
     pack = 2 if heads % 2 == 0 else 1
@@ -140,12 +141,13 @@
     def body(*refs):
         attend_kernel(
             (tile, heads // (group * pack), group, pack, lines), scale, refs[0], refs[1 : 1 + n],
-            *refs[1 + n : 3 + n], refs[3 + n : 3 + n + m], *refs[3 + n + m :],
+            refs[1 + n], refs[2 + n : 2 + n + v], refs[2 + n + v : 2 + n + v + m],
+            *refs[2 + n + v + m :],
         )
 
     return pl.pallas_call(
         body,
-        in_specs=[pl.BlockSpec(memory_space=pltpu.VMEM)] * (n + 3),
+        in_specs=[pl.BlockSpec(memory_space=pltpu.VMEM)] * (n + v + 2),
         out_specs=[pl.BlockSpec(memory_space=pltpu.VMEM)] * m,
         out_shape=[jax.ShapeDtypeStruct((rows, width), kind) for kind in kinds],
         scratch_shapes=[pltpu.VMEM((STAT, tile * m), F32)] * 2,
@@ -156,64 +158,84 @@
             transcendentals=m * rows * keys.shape[0] * heads,
         ),
         name="attend",
-    )(bias, *planes, keys, values)
-
-
-def load(cached, fresh, victims, queries, after):
-    cache_rows, columns = cached[0].shape
-    tok = fresh[0].shape[0]
-    padded = cache_rows + -(-tok // 16) * 16
-    n = len(cached)
-
-    def body(*refs):
-        cached_refs, fresh_refs, victims_ref, queries_ref = refs[:n], refs[n : 2 * n], *refs[2 * n : 2 * n + 2]
-        refs = refs[2 * n + 3 :]
-        outs, bias_ref, q_ref, tails, ids_ref, sems = (
-            refs[:n], refs[n], refs[n + 1], refs[n + 2 : 2 * n + 2], *refs[2 * n + 2 :]
-        )
-        ids = pltpu.make_async_copy(victims_ref, ids_ref, sems.at[1, n])
-        rest = pltpu.make_async_copy(queries_ref, q_ref, sems.at[0, n])
-        small = [
-            pltpu.make_async_copy(src, dst, sems.at[1, i])
-            for i, (src, dst) in enumerate(zip(fresh_refs, tails))
-        ]
-        large = [
-            pltpu.make_async_copy(src, dst.at[pl.ds(0, cache_rows), :], sems.at[0, i])
-            for i, (src, dst) in enumerate(zip(cached_refs, outs))
-        ]
-        for copy in [ids] + small + large + [rest]:
-            copy.start()
-        ids.wait()
-        blocks = cache_rows // BLK
+    )(bias, *planes, keys, *values)
+
+
+def load(parts, after, victims=None, queries=None):
+    shapes, scratch, held, plans = [], [], [], []
+    for cached, start, rows, fresh in parts:
+        tok = 0 if fresh is None else fresh.shape[0]
+        padded = rows + -(-tok // 16) * 16
+        columns = cached.shape[1]
+        shapes.append(jax.ShapeDtypeStruct((padded, columns), BF16))
+        plans.append((start, rows, tok, padded, columns))
+        held += [cached] if fresh is None else [cached, fresh]
+        scratch += [] if fresh is None else [pltpu.VMEM(fresh.shape, BF16)]
+    extra = victims is not None
+    if extra:
+        held += [victims, queries]
+        all_rows = parts[0][0].shape[0]
+        tok = queries.shape[0]
+        mask_rows = all_rows + -(-tok // 16) * 16
+        shapes += [jax.ShapeDtypeStruct((mask_rows, STAT), F32), jax.ShapeDtypeStruct(queries.shape, BF16)]
+        scratch += [pltpu.VMEM(victims.shape, jnp.int32)]
+
+    def fill_mask(ids_ref, bias_ref):
+        blocks = all_rows // BLK
         first = lax.axis_index("seq") * blocks
         for block in range(blocks):
             hits = jnp.where(ids_ref[...] == first + block, 1.0, 0.0)
             hit = jnp.max(hits, axis=1, keepdims=True)
             gone = jnp.where(hit > 0.0, NEG, 0.0)
             bias_ref[block * BLK : (block + 1) * BLK, :] = jnp.broadcast_to(gone, (BLK, STAT))
-        token = lax.broadcasted_iota(jnp.int32, (padded - cache_rows, STAT), 0)
-        bias_ref[cache_rows:, :] = jnp.where(token < tok, 0.0, NEG)
-        for copy, tail, out in zip(small, tails, outs):
+        token = lax.broadcasted_iota(jnp.int32, (mask_rows - all_rows, STAT), 0)
+        bias_ref[all_rows:, :] = jnp.where(token < tok, 0.0, NEG)
+
+    def body(*refs):
+        ins, outs = refs[: len(held)], refs[len(held) + 1 : len(held) + 1 + len(shapes)]
+        work, sems = refs[len(held) + 1 + len(shapes) : -1], refs[-1]
+        ins, work = iter(ins), iter(work)
+        large, small, tails = [], [], []
+        for i, ((start, rows, tok_i, _, _), out) in enumerate(zip(plans, outs)):
+            src = next(ins).at[pl.ds(start, rows), :]
+            large.append(pltpu.make_async_copy(src, out.at[pl.ds(0, rows), :], sems.at[0, i]))
+            if tok_i:
+                tail = next(work)
+                small.append(pltpu.make_async_copy(next(ins), tail, sems.at[1, i]))
+                tails.append((tail, out, plans[i]))
+        if extra:
+            ids_ref = next(work)
+            ids = pltpu.make_async_copy(next(ins), ids_ref, sems.at[0, len(plans)])
+            rest = pltpu.make_async_copy(next(ins), outs[-1], sems.at[1, len(plans)])
+            ids.start()
+        for copy in small + large:
+            copy.start()
+        if extra:
+            rest.start()
+            ids.wait()
+            fill_mask(ids_ref, outs[-2])
+        for copy, (tail, out, (_, rows, tok_i, padded, columns)) in zip(small, tails):
             copy.wait()
-            zeros = jnp.zeros((padded - cache_rows - tok, columns), F32)
-            rows = jnp.concatenate([tail[...].astype(F32), zeros], axis=0)
-            out[cache_rows:, :] = rows.astype(out.dtype)
-        for copy in large + [rest]:
+            filled = tail[...].astype(F32)
+            if padded > rows + tok_i:
+                zeros = jnp.zeros((padded - rows - tok_i, columns), F32)
+                filled = jnp.concatenate([filled, zeros], axis=0)
+            out[rows:, :] = filled.astype(out.dtype)
+        for copy in large + ([rest] if extra else []):
             copy.wait()
 
     in_hbm = pl.BlockSpec(memory_space=pltpu.HBM)
-    held = (*cached, *fresh, victims, queries)
     return pl.pallas_call(
         body,
         in_specs=[in_hbm] * len(held) + [pl.BlockSpec(memory_space=pl.ANY)],
-        out_specs=[pl.BlockSpec(memory_space=pltpu.VMEM)] * (n + 2),
-        out_shape=[jax.ShapeDtypeStruct((padded, columns), BF16)] * n
-        + [jax.ShapeDtypeStruct((padded, STAT), F32), jax.ShapeDtypeStruct(queries.shape, BF16)],
-        scratch_shapes=[pltpu.VMEM(x.shape, BF16) for x in fresh]
-        + [pltpu.VMEM(victims.shape, jnp.int32), pltpu.SemaphoreType.DMA((2, n + 1))],
+        out_specs=[pl.BlockSpec(memory_space=pltpu.VMEM)] * len(shapes),
+        out_shape=shapes,
+        scratch_shapes=scratch + [pltpu.SemaphoreType.DMA((2, len(plans) + 1))],
         compiler_params=pltpu.CompilerParams(vmem_limit_bytes=24 * 1024 * 1024),
         cost_estimate=pl.CostEstimate(
-            flops=0, bytes_accessed=4 * n * cache_rows * columns, transcendentals=0
+            flops=0,
+            bytes_accessed=4 * sum(math.prod(x.shape) for x in shapes),
+            transcendentals=0,
         ),
         name="load",
     )(*[pltpu.with_memory_space_constraint(x, pltpu.HBM) for x in held], after)
@@ -304,28 +326,40 @@
     def give(x, *by):
         return lax.ppermute(x, "seq", partner_perm(shape, by, True))
 
-    far_first = [0, *range(a_n - 1, 0, -1)]
-    line = [queries] + [fetch(queries, a, 0, 0) for a in far_first[1:]]
+    line = [queries] + [None] * (a_n - 1)
+    for a in range(a_n - 1, 0, -1):
+        line[a] = fetch(queries, a, 0, 0)
     lines = [line] + [[fetch(x, 0, b, 0) for x in line] for b in range(1, b_n)]
-    keys, values, bias, line[0] = load(
-        (cache_keys, cache_values), (new_keys, new_values), victims[None], queries, line[min(2, a_n - 1)]
+    cache_rows = cache_keys.shape[0]
+    half = cache_rows // 2 if cache_rows % 32 == 0 else cache_rows
+    keys, first_values, bias, line[0] = load(
+        [(cache_keys, 0, cache_rows, new_keys), (cache_values, 0, half, None)],
+        line[-1], victims[None], queries,
     )
-    plane = join([x for pieces in lines for x in pieces])
+    plane = join([x for pieces in lines for x in pieces], (keys,))
     planes = [plane] + [fetch(plane, 0, 0, c) for c in range(1, c_n)]
+    last_values = load([(cache_values, half, cache_rows - half, new_values)], plane)[0]
     kinds = [F32] * b_n + [BF16] * (b_n * (c_n - 1))
-    sums = attend(planes, b_n, kinds, keys, values, bias)
+    sums = attend(planes, b_n, kinds, keys, [first_values, last_values], bias)
 
     def over_cores(b, kind):
         got = [give(sums[c * b_n + b], 0, 0, c) for c in range(1, c_n)]
         return merge_rows([sums[b]] + got, heads, a_n, [kind] * a_n)
 
-    got = [[give(x, 0, b, 0) for x in over_cores(b, BF16)] for b in range(1, b_n)]
+    def total(a, kind, more=()):
+        parts = [own[a]] + [pieces[a] for pieces in got] + list(more)
+        return merge_rows(parts, heads, 1, [kind])[0]
+
+    got = [over_cores(b, BF16) for b in range(1, b_n)]
+    got = [[give(x, 0, b, 0) for x in pieces[::-1]][::-1] for b, pieces in enumerate(got, 1)]
     own = over_cores(0, F32)
-    total = [[own[s]] + [pieces[s] for pieces in got] for s in range(a_n)]
-    last = [
-        give(merge_rows(total[s], heads, 1, [BF16])[0], far_first[s], 0, 0) for s in range(1, a_n)
-    ]
-    return finish([*merge_rows(total[0], heads, 1, [F32]), *last], heads)
+    pair = 2 if a_n & (a_n - 1) == 0 and a_n > 2 else 1
+    near = {
+        f: [give(total(f + n, BF16), n, 0, 0) for n in range(1, pair)]
+        for f in range(a_n - pair, -1, -pair)
+    }
+    far = [give(total(f, BF16, near[f]), f, 0, 0) for f in range(a_n - pair, 0, -pair)]
+    return finish([total(0, F32, near[0])] + far, heads)
 
 
 def solution(mesh):

time: 34.7 us -> 35.8 us (1.032)
  Pallas kernels: 7.23 us -> 8.22 us
    ppermute x8, waiting for transfers between devices: 3.46 us -> 2.45 us  [fetch(): return lax.ppermute(x, 'seq', partner_perm(shape, by, False))]
    ppermute x9, waiting for transfers between devices: 3.22 us -> 4.21 us  [give(): return lax.ppermute(x, 'seq', partner_perm(shape, by, True))]
    pallas_call x1 -> x2, Pallas kernels: 2.65 us -> 3.58 us  [load(): pl.pallas_call(body, in_specs=[in_hbm] * len(held) + [pl.BlockSpec(memory...]
    ppermute x9, starting transfers between devices: 9.26 us -> 10 us  [give(): return lax.ppermute(x, 'seq', partner_perm(shape, by, True))]
    ppermute x8, starting transfers between devices: 11.2 us -> 10.7 us  [fetch(): return lax.ppermute(x, 'seq', partner_perm(shape, by, False))]
  transfers between devices with their start and end apart: 17 -> 17, of which waited for: 7 -> 8; matrix products, arithmetic and copies ran while one was open for 0% -> 0% of each run, Pallas kernels for 11% -> 13%
where the time goes in v13:
time: 35.8 us; the launch traced here: 35.7 us
  starting transfers between devices  20.7 us (58%)
  Pallas kernels  8.22 us (23%)
  waiting for transfers between devices  6.66 us (19%)
    ppermute x8, starting transfers between devices, fetch(): return lax.ppermute(x, 'seq', partner_perm(shape, by, False))  10.7 us
    ppermute x9, starting transfers between devices, give(): return lax.ppermute(x, 'seq', partner_perm(shape, by, True))  10 us
    ppermute x9, waiting for transfers between devices, give(): return lax.ppermute(x, 'seq', partner_perm(shape, by, True))  4.21 us
    pallas_call x2, Pallas kernels, load(): pl.pallas_call(body, in_specs=[in_hbm] * len(held) + [pl.BlockSpec(memory...  3.58 us
    pallas_call x1, Pallas kernels, attend(): pl.pallas_call(body, in_specs=[pl.BlockSpec(memory_space=pltpu.VMEM)] * (...  2.58 us
    ppermute x8, waiting for transfers between devices, fetch(): return lax.ppermute(x, 'seq', partner_perm(shape, by, False))  2.45 us
    pallas_call x8, Pallas kernels, call_merge(): pl.pallas_call(body, in_specs=[pl.BlockSpec(memory_space=pltpu.VMEM)] * l...  2.07 us
  transfers between devices with their start and end apart: 17, of which 8 were waited for; matrix products, arithmetic and copies ran while one was open for 0% of the time, Pallas kernels for 13%

profile of v13, /device:TPU:0, one launch (start us, length us, event | category | flops | bytes accessed | tf_op | source)
XLA Modules:
  0.0 35.7 jit_solution(1248493083963246672)
XLA Ops:
  0.0 3.0 %collective-permute-start.1 = (bf16[8,2560]{1,0:T(8,128)(2,1)}, bf16[8,2560]{1,0:T(8,128)(2,1)S(1)}, u32[]{:S(2)}, u32[]{:S(2)}) collective-permute-start(bf16[8,2560]{1,0:T(8,128)(2,1)} %refs_4_.1), channel_id=1, source_target_pairs={{4,0},{5,1},{6,2},{7,3},{0,4},{1,5},{2,6},{3,7},{12,8},{13,9},{14,... | collective-permute-start | bytes 122888 | tf_op jit(solution)/shard_map/ppermute | solution.py:324
  3.0 2.5 %collective-permute-start = (bf16[8,2560]{1,0:T(8,128)(2,1)}, bf16[8,2560]{1,0:T(8,128)(2,1)S(1)}, u32[]{:S(2)}, u32[]{:S(2)}) collective-permute-start(bf16[8,2560]{1,0:T(8,128)(2,1)} %refs_4_.1), channel_id=1, source_target_pairs={{12,0},{13,1},{14,2},{15,3},{8,4},{9,5},{10,6},{11,7},{4,8},{5,9},... | collective-permute-start | bytes 122888 | tf_op jit(solution)/shard_map/ppermute | solution.py:324
  5.6 1.5 %collective-permute-start.3 = (bf16[8,2560]{1,0:T(8,128)(2,1)}, bf16[8,2560]{1,0:T(8,128)(2,1)S(1)}, u32[]{:S(2)}, u32[]{:S(2)}) collective-permute-start(bf16[8,2560]{1,0:T(8,128)(2,1)} %refs_4_.1), channel_id=1, source_target_pairs={{2,0},{3,1},{0,2},{1,3},{6,4},{7,5},{4,6},{5,7},{10,8},{11,9},{8,1... | collective-permute-start | bytes 122888 | tf_op jit(solution)/shard_map/ppermute | solution.py:324
  7.1 0.5 %collective-permute-start.4 = (bf16[8,2560]{1,0:T(8,128)(2,1)S(1)}, bf16[8,2560]{1,0:T(8,128)(2,1)S(1)}, u32[]{:S(2)}, u32[]{:S(2)}) collective-permute-start(bf16[8,2560]{1,0:T(8,128)(2,1)S(1)} %collective-permute-done.1.refs_1_), channel_id=1, source_target_pairs={{2,0},{3,1},{0,2},{1,3},{6,4},{7,5},{4,6},{5,7},{10,8},{11,9},{8,1... | collective-permute-start | bytes 122888 | tf_op jit(solution)/shard_map/ppermute | solution.py:324
  7.6 1.9 %collective-permute-done.refs_5_.refs_3_ = bf16[8,2560]{1,0:T(8,128)(2,1)S(1)} collective-permute-done((bf16[8,2560]{1,0:T(8,128)(2,1)}, bf16[8,2560]{1,0:T(8,128)(2,1)S(1)}, u32[]{:S(2)}, u32[]{:S(2)}) %collective-permute-start) | collective-permute-done | bytes 40992 | tf_op jit(solution)/shard_map/ppermute | solution.py:324
  9.6 1.5 %collective-permute-start.6 = (bf16[8,2560]{1,0:T(8,128)(2,1)S(1)}, bf16[8,2560]{1,0:T(8,128)(2,1)S(1)}, u32[]{:S(2)}, u32[]{:S(2)}) collective-permute-start(bf16[8,2560]{1,0:T(8,128)(2,1)S(1)} %collective-permute-done.refs_5_.refs_3_), channel_id=1, source_target_pairs={{2,0},{3,1},{0,2},{1,3},{6,4},{7,5},{4,6},{5,7},{10,8},{11,9},{8,1... | collective-permute-start | bytes 122888 | tf_op jit(solution)/shard_map/ppermute | solution.py:324
  11.1 1.5 %collective-permute-start.5 = (bf16[8,2560]{1,0:T(8,128)(2,1)S(1)}, bf16[8,2560]{1,0:T(8,128)(2,1)S(1)}, u32[]{:S(2)}, u32[]{:S(2)}) collective-permute-start(bf16[8,2560]{1,0:T(8,128)(2,1)S(1)} %collective-permute-done.2.refs_2_), channel_id=1, source_target_pairs={{2,0},{3,1},{0,2},{1,3},{6,4},{7,5},{4,6},{5,7},{10,8},{11,9},{8,1... | collective-permute-start | bytes 122888 | tf_op jit(solution)/shard_map/ppermute | solution.py:324
  12.6 2.2 %load.2 = (bf16[528,2560]{1,0:T(8,128)(2,1)S(1)}, bf16[256,2560]{1,0:T(8,128)(2,1)S(1)}, f32[528,128]{1,0:T(8,128)S(1)}, bf16[8,2560]{1,0:T(8,128)(2,1)S(1)}) custom-call(bf16[512,2560]{1,0:T(8,128)(2,1)} %refs_0_.2, bf16[8,2560]{1,0:T(8,128)(2,1)} %refs_1_.2, bf16[512,2560]{1,0:T(8,128)(2,1)} %refs_0_.3, s32[1,16]{1,0:T(1,128)} %bitcast.1, ...), custom_call_target="tpu_custom_call" | custom-call | bytes 8380416 | tf_op jit(solution)/shard_map/load/pallas_call | solution.py:228
  14.8 0.3 collective-permute-done.5.refs_6_
  15.2 1.4 %load.3.refs_5_ = bf16[272,2560]{1,0:T(8,128)(2,1)S(1)} custom-call(bf16[512,2560]{1,0:T(8,128)(2,1)} %refs_0_.3, bf16[8,2560]{1,0:T(8,128)(2,1)} %refs_1_.3, bf16[64,2560]{1,0:T(8,128)(2,1)S(1)} %merge.8.refs_2_.refs_1_), custom_call_target="tpu_custom_call" | custom-call | bytes 2785280 | tf_op jit(solution)/shard_map/load/pallas_call | solution.py:228
  16.6 0.2 collective-permute-done.7.refs_2_
  16.8 2.6 %attend.1 = (f32[32,2688]{1,0:T(8,128)S(1)}, f32[32,2688]{1,0:T(8,128)S(1)}, bf16[32,2688]{1,0:T(8,128)(2,1)S(1)}, bf16[32,2688]{1,0:T(8,128)(2,1)S(1)}) custom-call(f32[528,128]{1,0:T(8,128)S(1)} %get-tuple-element.21.refs_0_, bf16[64,2560]{1,0:T(8,128)(2,1)S(1)} %merge.8.refs_2_.refs_1_, bf16[64,2560]{1,0:T(8,128)(2,1)S(1)} %collective-permute-done.7.refs_2_, ...), custom_call_target="tpu_custom_call" | custom-call | flops 692060160 | bytes 5406720 | tf_op jit(solution)/shard_map/attend/pallas_call | solution.py:148
  19.4 0.3 collective-permute-start.9
  19.8 0.2 collective-permute-start.8
  20.0 0.9 %collective-permute-done.9.refs_1_ = bf16[32,2688]{1,0:T(8,128)(2,1)S(1)} collective-permute-done((bf16[32,2688]{1,0:T(8,128)(2,1)S(1)}, bf16[32,2688]{1,0:T(8,128)(2,1)S(1)}, u32[]{:S(2)}, u32[]{:S(2)}) %collective-permute-start.9) | collective-permute-done | bytes 172064 | tf_op jit(solution)/shard_map/ppermute | solution.py:327
  20.9 0.3 merge.10
  21.2 1.5 %collective-permute-start.14 = (bf16[8,2688]{1,0:T(8,128)(2,1)S(1)}, bf16[8,2688]{1,0:T(8,128)(2,1)S(1)}, u32[]{:S(2)}, u32[]{:S(2)}) collective-permute-start(bf16[8,2688]{1,0:T(8,128)(2,1)S(1)} %get-tuple-element.36), channel_id=1, source_target_pairs={{0,2},{1,3},{2,0},{3,1},{4,6},{5,7},{6,4},{7,5},{8,10},{9,11},{10,... | collective-permute-start | bytes 129032 | tf_op jit(solution)/shard_map/ppermute | solution.py:327
  22.7 0.6 %collective-permute-start.11 = (bf16[8,2688]{1,0:T(8,128)(2,1)S(1)}, bf16[8,2688]{1,0:T(8,128)(2,1)S(1)}, u32[]{:S(2)}, u32[]{:S(2)}) collective-permute-start(bf16[8,2688]{1,0:T(8,128)(2,1)S(1)} %get-tuple-element.32), channel_id=1, source_target_pairs={{0,2},{1,3},{2,0},{3,1},{4,6},{5,7},{6,4},{7,5},{8,10},{9,11},{10,... | collective-permute-start | bytes 129032 | tf_op jit(solution)/shard_map/ppermute | solution.py:327
  23.3 1.5 %collective-permute-start.13 = (bf16[8,2688]{1,0:T(8,128)(2,1)S(1)}, bf16[8,2688]{1,0:T(8,128)(2,1)S(1)}, u32[]{:S(2)}, u32[]{:S(2)}) collective-permute-start(bf16[8,2688]{1,0:T(8,128)(2,1)S(1)} %get-tuple-element.34), channel_id=1, source_target_pairs={{0,2},{1,3},{2,0},{3,1},{4,6},{5,7},{6,4},{7,5},{8,10},{9,11},{10,... | collective-permute-start | bytes 129032 | tf_op jit(solution)/shard_map/ppermute | solution.py:327
  24.7 0.3 merge.9
  25.0 0.2 collective-permute-done.14.refs_1_
  25.4 0.4 collective-permute-start.15
  25.8 1.8 %collective-permute-start.10 = (bf16[8,2688]{1,0:T(8,128)(2,1)S(1)}, bf16[8,2688]{1,0:T(8,128)(2,1)S(1)}, u32[]{:S(2)}, u32[]{:S(2)}) collective-permute-start(bf16[8,2688]{1,0:T(8,128)(2,1)S(1)} %get-tuple-element.30), channel_id=1, source_target_pairs={{0,2},{1,3},{2,0},{3,1},{4,6},{5,7},{6,4},{7,5},{8,10},{9,11},{10,... | collective-permute-start | bytes 129032 | tf_op jit(solution)/shard_map/ppermute | solution.py:327
  27.5 0.1 merge.11
  27.7 1.8 %collective-permute-start.12 = (bf16[8,2688]{1,0:T(8,128)(2,1)S(1)}, bf16[8,2688]{1,0:T(8,128)(2,1)S(1)}, u32[]{:S(2)}, u32[]{:S(2)}) collective-permute-start(bf16[8,2688]{1,0:T(8,128)(2,1)S(1)} %merge.11), channel_id=1, source_target_pairs={{0,4},{1,5},{2,6},{3,7},{4,0},{5,1},{6,2},{7,3},{8,12},{9,13},{10,... | collective-permute-start | bytes 129032 | tf_op jit(solution)/shard_map/ppermute | solution.py:327
  29.4 0.2 collective-permute-done.15.refs_2_
  29.6 0.2 merge.14
  29.8 2.0 %collective-permute-start.16 = (bf16[8,2688]{1,0:T(8,128)(2,1)S(1)}, bf16[8,2688]{1,0:T(8,128)(2,1)S(1)}, u32[]{:S(2)}, u32[]{:S(2)}) collective-permute-start(bf16[8,2688]{1,0:T(8,128)(2,1)S(1)} %merge.14), channel_id=1, source_target_pairs={{0,8},{1,9},{2,10},{3,11},{4,12},{5,13},{6,14},{7,15},{8,0},{9,1},... | collective-permute-start | bytes 129032 | tf_op jit(solution)/shard_map/ppermute | solution.py:327
  31.8 0.4 %collective-permute-done.12.refs_2_ = bf16[8,2688]{1,0:T(8,128)(2,1)S(1)} collective-permute-done((bf16[8,2688]{1,0:T(8,128)(2,1)S(1)}, bf16[8,2688]{1,0:T(8,128)(2,1)S(1)}, u32[]{:S(2)}, u32[]{:S(2)}) %collective-permute-start.12) | collective-permute-done | bytes 43040 | tf_op jit(solution)/shard_map/ppermute | solution.py:327
  32.2 0.2 merge.12.refs_0_
  32.4 2.4 %collective-permute-done.16.refs_1_ = bf16[8,2688]{1,0:T(8,128)(2,1)S(1)} collective-permute-done((bf16[8,2688]{1,0:T(8,128)(2,1)S(1)}, bf16[8,2688]{1,0:T(8,128)(2,1)S(1)}, u32[]{:S(2)}, u32[]{:S(2)}) %collective-permute-start.16) | collective-permute-done | bytes 43040 | tf_op jit(solution)/shard_map/ppermute | solution.py:327
  34.9 0.8 %merge.15 = bf16[8,2560]{1,0:T(8,128)(2,1)} custom-call(f32[8,2688]{1,0:T(8,128)S(1)} %merge.12.refs_0_, bf16[8,2688]{1,0:T(8,128)(2,1)S(1)} %collective-permute-done.16.refs_1_), custom_call_target="tpu_custom_call" | custom-call | flops 172032 | bytes 172032 | tf_op jit(solution)/shard_map/merge/pallas_call | solution.py:304
  (13 shorter events, 0.4 us)
Async XLA Ops:
  0.0 7.1 %collective-permute-start.1 = (bf16[8,2560]{1,0:T(8,128)(2,1)}, bf16[8,2560]{1,0:T(8,128)(2,1)S(1)}, u32[]{:S(2)}, u32[]{:S(2)}) collective-permute-start(bf16[8,2560]{1,0:T(8,128)(2,1)} %refs_4_.1), channel_id=1, source_target_pairs={{4,0},{5,1},{6,2},{7,3},{0,4},{1,5},{2,6},{3,7},{12,8},{13,9},{14,... | collective-permute-start | bytes 122888 | tf_op jit(solution)/shard_map/ppermute | solution.py:324
  3.0 6.5 %collective-permute-start = (bf16[8,2560]{1,0:T(8,128)(2,1)}, bf16[8,2560]{1,0:T(8,128)(2,1)S(1)}, u32[]{:S(2)}, u32[]{:S(2)}) collective-permute-start(bf16[8,2560]{1,0:T(8,128)(2,1)} %refs_4_.1), channel_id=1, source_target_pairs={{12,0},{13,1},{14,2},{15,3},{8,4},{9,5},{10,6},{11,7},{4,8},{5,9},... | collective-permute-start | bytes 122888 | tf_op jit(solution)/shard_map/ppermute | solution.py:324
  5.5 5.6 %collective-permute-start.2 = (bf16[8,2560]{1,0:T(8,128)(2,1)}, bf16[8,2560]{1,0:T(8,128)(2,1)S(1)}, u32[]{:S(2)}, u32[]{:S(2)}) collective-permute-start(bf16[8,2560]{1,0:T(8,128)(2,1)} %refs_4_.1), channel_id=1, source_target_pairs={{8,0},{9,1},{10,2},{11,3},{12,4},{13,5},{14,6},{15,7},{0,8},{1,9},... | collective-permute-start | bytes 122888 | tf_op jit(solution)/shard_map/ppermute | solution.py:324
  5.6 9.2 %collective-permute-start.3 = (bf16[8,2560]{1,0:T(8,128)(2,1)}, bf16[8,2560]{1,0:T(8,128)(2,1)S(1)}, u32[]{:S(2)}, u32[]{:S(2)}) collective-permute-start(bf16[8,2560]{1,0:T(8,128)(2,1)} %refs_4_.1), channel_id=1, source_target_pairs={{2,0},{3,1},{0,2},{1,3},{6,4},{7,5},{4,6},{5,7},{10,8},{11,9},{8,1... | collective-permute-start | bytes 122888 | tf_op jit(solution)/shard_map/ppermute | solution.py:324
  7.1 7.6 %collective-permute-start.4 = (bf16[8,2560]{1,0:T(8,128)(2,1)S(1)}, bf16[8,2560]{1,0:T(8,128)(2,1)S(1)}, u32[]{:S(2)}, u32[]{:S(2)}) collective-permute-start(bf16[8,2560]{1,0:T(8,128)(2,1)S(1)} %collective-permute-done.1.refs_1_), channel_id=1, source_target_pairs={{2,0},{3,1},{0,2},{1,3},{6,4},{7,5},{4,6},{5,7},{10,8},{11,9},{8,1... | collective-permute-start | bytes 122888 | tf_op jit(solution)/shard_map/ppermute | solution.py:324
  9.6 5.2 %collective-permute-start.6 = (bf16[8,2560]{1,0:T(8,128)(2,1)S(1)}, bf16[8,2560]{1,0:T(8,128)(2,1)S(1)}, u32[]{:S(2)}, u32[]{:S(2)}) collective-permute-start(bf16[8,2560]{1,0:T(8,128)(2,1)S(1)} %collective-permute-done.refs_5_.refs_3_), channel_id=1, source_target_pairs={{2,0},{3,1},{0,2},{1,3},{6,4},{7,5},{4,6},{5,7},{10,8},{11,9},{8,1... | collective-permute-start | bytes 122888 | tf_op jit(solution)/shard_map/ppermute | solution.py:324
  11.1 4.0 %collective-permute-start.5 = (bf16[8,2560]{1,0:T(8,128)(2,1)S(1)}, bf16[8,2560]{1,0:T(8,128)(2,1)S(1)}, u32[]{:S(2)}, u32[]{:S(2)}) collective-permute-start(bf16[8,2560]{1,0:T(8,128)(2,1)S(1)} %collective-permute-done.2.refs_2_), channel_id=1, source_target_pairs={{2,0},{3,1},{0,2},{1,3},{6,4},{7,5},{4,6},{5,7},{10,8},{11,9},{8,1... | collective-permute-start | bytes 122888 | tf_op jit(solution)/shard_map/ppermute | solution.py:324
  15.1 1.7 %collective-permute-start.7 = (bf16[64,2560]{1,0:T(8,128)(2,1)S(1)}, bf16[64,2560]{1,0:T(8,128)(2,1)S(1)}, u32[]{:S(2)}, u32[]{:S(2)}) collective-permute-start(bf16[64,2560]{1,0:T(8,128)(2,1)S(1)} %merge.8.refs_2_.refs_1_), channel_id=1, source_target_pairs={{1,0},{0,1},{3,2},{2,3},{5,4},{4,5},{7,6},{6,7},{9,8},{8,9},{11,10... | collective-permute-start | bytes 983048 | tf_op jit(solution)/shard_map/ppermute | solution.py:324
  19.4 1.5 %collective-permute-start.9 = (bf16[32,2688]{1,0:T(8,128)(2,1)S(1)}, bf16[32,2688]{1,0:T(8,128)(2,1)S(1)}, u32[]{:S(2)}, u32[]{:S(2)}) collective-permute-start(bf16[32,2688]{1,0:T(8,128)(2,1)S(1)} %get-tuple-element.29), channel_id=1, source_target_pairs={{0,1},{1,0},{2,3},{3,2},{4,5},{5,4},{6,7},{7,6},{8,9},{9,8},{10,11... | collective-permute-start | bytes 516104 | tf_op jit(solution)/shard_map/ppermute | solution.py:327
  19.8 5.0 %collective-permute-start.8 = (bf16[32,2688]{1,0:T(8,128)(2,1)S(1)}, bf16[32,2688]{1,0:T(8,128)(2,1)S(1)}, u32[]{:S(2)}, u32[]{:S(2)}) collective-permute-start(bf16[32,2688]{1,0:T(8,128)(2,1)S(1)} %get-tuple-element.26), channel_id=1, source_target_pairs={{0,1},{1,0},{2,3},{3,2},{4,5},{5,4},{6,7},{7,6},{8,9},{9,8},{10,11... | collective-permute-start | bytes 516104 | tf_op jit(solution)/shard_map/ppermute | solution.py:327
  21.2 4.1 %collective-permute-start.14 = (bf16[8,2688]{1,0:T(8,128)(2,1)S(1)}, bf16[8,2688]{1,0:T(8,128)(2,1)S(1)}, u32[]{:S(2)}, u32[]{:S(2)}) collective-permute-start(bf16[8,2688]{1,0:T(8,128)(2,1)S(1)} %get-tuple-element.36), channel_id=1, source_target_pairs={{0,2},{1,3},{2,0},{3,1},{4,6},{5,7},{6,4},{7,5},{8,10},{9,11},{10,... | collective-permute-start | bytes 129032 | tf_op jit(solution)/shard_map/ppermute | solution.py:327
  22.7 4.8 %collective-permute-start.11 = (bf16[8,2688]{1,0:T(8,128)(2,1)S(1)}, bf16[8,2688]{1,0:T(8,128)(2,1)S(1)}, u32[]{:S(2)}, u32[]{:S(2)}) collective-permute-start(bf16[8,2688]{1,0:T(8,128)(2,1)S(1)} %get-tuple-element.32), channel_id=1, source_target_pairs={{0,2},{1,3},{2,0},{3,1},{4,6},{5,7},{6,4},{7,5},{8,10},{9,11},{10,... | collective-permute-start | bytes 129032 | tf_op jit(solution)/shard_map/ppermute | solution.py:327
  23.3 6.2 %collective-permute-start.13 = (bf16[8,2688]{1,0:T(8,128)(2,1)S(1)}, bf16[8,2688]{1,0:T(8,128)(2,1)S(1)}, u32[]{:S(2)}, u32[]{:S(2)}) collective-permute-start(bf16[8,2688]{1,0:T(8,128)(2,1)S(1)} %get-tuple-element.34), channel_id=1, source_target_pairs={{0,2},{1,3},{2,0},{3,1},{4,6},{5,7},{6,4},{7,5},{8,10},{9,11},{10,... | collective-permute-start | bytes 129032 | tf_op jit(solution)/shard_map/ppermute | solution.py:327
  25.4 4.2 %collective-permute-start.15 = (bf16[8,2688]{1,0:T(8,128)(2,1)S(1)}, bf16[8,2688]{1,0:T(8,128)(2,1)S(1)}, u32[]{:S(2)}, u32[]{:S(2)}) collective-permute-start(bf16[8,2688]{1,0:T(8,128)(2,1)S(1)} %merge.13), channel_id=1, source_target_pairs={{0,4},{1,5},{2,6},{3,7},{4,0},{5,1},{6,2},{7,3},{8,12},{9,13},{10,... | collective-permute-start | bytes 129032 | tf_op jit(solution)/shard_map/ppermute | solution.py:327
  25.8 6.0 %collective-permute-start.10 = (bf16[8,2688]{1,0:T(8,128)(2,1)S(1)}, bf16[8,2688]{1,0:T(8,128)(2,1)S(1)}, u32[]{:S(2)}, u32[]{:S(2)}) collective-permute-start(bf16[8,2688]{1,0:T(8,128)(2,1)S(1)} %get-tuple-element.30), channel_id=1, source_target_pairs={{0,2},{1,3},{2,0},{3,1},{4,6},{5,7},{6,4},{7,5},{8,10},{9,11},{10,... | collective-permute-start | bytes 129032 | tf_op jit(solution)/shard_map/ppermute | solution.py:327
  27.7 4.6 %collective-permute-start.12 = (bf16[8,2688]{1,0:T(8,128)(2,1)S(1)}, bf16[8,2688]{1,0:T(8,128)(2,1)S(1)}, u32[]{:S(2)}, u32[]{:S(2)}) collective-permute-start(bf16[8,2688]{1,0:T(8,128)(2,1)S(1)} %merge.11), channel_id=1, source_target_pairs={{0,4},{1,5},{2,6},{3,7},{4,0},{5,1},{6,2},{7,3},{8,12},{9,13},{10,... | collective-permute-start | bytes 129032 | tf_op jit(solution)/shard_map/ppermute | solution.py:327
  29.8 5.1 %collective-permute-start.16 = (bf16[8,2688]{1,0:T(8,128)(2,1)S(1)}, bf16[8,2688]{1,0:T(8,128)(2,1)S(1)}, u32[]{:S(2)}, u32[]{:S(2)}) collective-permute-start(bf16[8,2688]{1,0:T(8,128)(2,1)S(1)} %merge.14), channel_id=1, source_target_pairs={{0,8},{1,9},{2,10},{3,11},{4,12},{5,13},{6,14},{7,15},{8,0},{9,1},... | collective-permute-start | bytes 129032 | tf_op jit(solution)/shard_map/ppermute | solution.py:327

commit v14 on v11

--- a/solution.py
+++ b/solution.py
@@ -13,6 +13,7 @@
 BLK = 128
 STAT = 128
 LANE = STAT // 3
+PACK = 2
 NEG = -1e30
 F32 = jnp.float32
 BF16 = jnp.bfloat16
@@ -47,20 +48,25 @@
     return top + pltpu.roll(high, LANE, 1) + pltpu.roll(mass - high, 2 * LANE, 1)
 
 
-def unpack_stats(packed, heads):
-    used = lanes(packed.shape[0]) < heads
+def unpack_stats(packed):
+    used = lanes(packed.shape[0]) < LANE
     mass = pltpu.roll(packed, STAT - LANE, 1) + pltpu.roll(packed, STAT - 2 * LANE, 1)
     return jnp.where(used, packed, 0.0), jnp.where(used, mass, 0.0)
 
 
-def attend_kernel(sizes, scale, bias_ref, q_refs, k_ref, v_ref, outs, top_acc, mass_acc):
-    tile, steps, group, pack, lines = sizes
-    rows = tile * len(outs)
+def lane_of(head):
+    return head % PACK * (LANE // PACK) + head // PACK
+
+
+def attend_kernel(sizes, scale, bias_ref, q_ref, k_ref, v_ref, outs, top_acc, mass_acc):
+    tile, steps, group = sizes
+    lines = len(outs)
+    rows = tile * lines
     line_rows = outs[0].shape[0]
-    wide = pack * HD
+    wide = PACK * HD
     contract_last = (((1,), (1,)), ((), ()))
     contract_first = (((0,), (0,)), ((), ()))
-    mine = [lax.broadcasted_iota(jnp.int32, (rows, wide), 1) // HD == k for k in range(pack)]
+    mine = [lax.broadcasted_iota(jnp.int32, (rows, wide), 1) // HD == k for k in range(PACK)]
 
     def row_tile(r, carry):
         at = pl.ds(pl.multiple_of(r * tile, tile), tile)
@@ -74,37 +80,30 @@
 
             def scores(i):
                 cols = columns(i)
-                q = jnp.concatenate([ref[rs, cols] for ref in q_refs for rs in in_plane], axis=0)
-                if pack > 1:
-                    zero = jnp.zeros_like(q)
-                    q = jnp.concatenate([jnp.where(m, q, zero) for m in mine], axis=0)
+                q = jnp.concatenate([q_ref[rs, cols] for rs in in_plane], axis=0)
+                q = jnp.concatenate([jnp.where(m, q, jnp.zeros_like(q)) for m in mine], axis=0)
                 return lax.dot_general(k_ref[:, cols], q, contract_last, preferred_element_type=F32)
 
             def weigh(i, score):
-                bias = jnp.concatenate([bias_ref[...]] * (pack * rows // STAT), axis=1)
+                bias = jnp.concatenate([bias_ref[...]] * (PACK * rows // STAT), axis=1)
                 score = score * scale + bias
                 top = jnp.max(score, axis=0, keepdims=True).astype(BF16).astype(F32)
                 score = jnp.exp2(score - top)
-                mass = jnp.sum(score, axis=0, keepdims=True)
-                for k in range(pack):
-                    head = (step * group + i) * pack + k
-                    part = slice(k * rows, (k + 1) * rows)
-                    top_acc[pl.ds(head, 1), :] = top[:, part]
-                    mass_acc[pl.ds(head, 1), :] = mass[:, part]
+                top_acc[pl.ds(step * group + i, 1), :] = top
+                mass_acc[pl.ds(step * group + i, 1), :] = jnp.sum(score, axis=0, keepdims=True)
                 return score.astype(BF16)
 
             def gather_values(i, weights):
-                for k in range(pack):
-                    head = (step * group + i) * pack + k
-                    cols = pl.ds(pl.multiple_of(head * HD, HD), HD)
-                    one = lax.dot_general(
-                        weights[:, k * rows : (k + 1) * rows],
-                        v_ref[:, cols],
-                        contract_first,
-                        preferred_element_type=F32,
-                    )
-                    for p, o_ref in enumerate(outs):
-                        o_ref[at, cols] = one[p * tile : (p + 1) * tile].astype(o_ref.dtype)
+                both = lax.dot_general(
+                    weights, v_ref[:, columns(i)], contract_first, preferred_element_type=F32
+                )
+                for k in range(PACK):
+                    at_head = ((step * group + i) * PACK + k) * HD
+                    cols = pl.ds(pl.multiple_of(at_head, HD), HD)
+                    for b, o_ref in enumerate(outs):
+                        start = k * rows + b * tile
+                        one = both[start : start + tile, k * HD : (k + 1) * HD]
+                        o_ref[at, cols] = one.astype(o_ref.dtype)
 
             ahead = [scores(i) for i in range(min(2, group))]
             weights = None
@@ -118,45 +117,50 @@
             return carry
 
         lax.fori_loop(0, steps, heads_of, 0)
-        packed = pack_stats(top_acc[...].T, mass_acc[...].T)
-        for p, o_ref in enumerate(outs):
+        tops, masses = top_acc[...].T, mass_acc[...].T
+        packed = 0.0
+        for k in range(PACK):
+            part = slice(k * rows, (k + 1) * rows)
+            stats = pack_stats(tops[part], masses[part])
+            packed += pltpu.roll(stats, k * (LANE // PACK), 1) if k else stats
+        for b, o_ref in enumerate(outs):
             width = o_ref.shape[1]
-            o_ref[at, width - STAT :] = packed[p * tile : (p + 1) * tile].astype(o_ref.dtype)
+            o_ref[at, width - STAT :] = packed[b * tile : (b + 1) * tile].astype(o_ref.dtype)
         return carry
 
     lax.fori_loop(0, line_rows // tile, row_tile, 0)
 
 
-def attend(planes, lines, kinds, keys, values, bias):
-    n, m = len(planes), len(kinds)
-    rows, columns = planes[0].shape[0] // lines, planes[0].shape[1]
+def attend(plane, lines, kind, keys, values, bias, after=()):
+    rows, columns = plane.shape[0] // lines, plane.shape[1]
     heads = columns // HD
-    pack = 2 if heads % 2 == 0 else 1
-    group = next(g for g in (10, 5, 4, 3, 2, 1) if heads % (g * pack) == 0)
+    pairs = heads // PACK
+    group = next(g for g in (10, 5, 4, 3, 2, 1) if pairs % g == 0)
     tile = next(t for t in (32, 16, rows) if rows % t == 0)
     width = columns + STAT
     scale = math.log2(math.e) / math.sqrt(HD)
 
     def body(*refs):
+        work = refs[4 + len(after) :]
         attend_kernel(
-            (tile, heads // (group * pack), group, pack, lines), scale, refs[0], refs[1 : 1 + n],
-            *refs[1 + n : 3 + n], refs[3 + n : 3 + n + m], *refs[3 + n + m :],
+            (tile, pairs // group, group), scale, *refs[:4], work[:lines], *work[lines:]
         )
 
     return pl.pallas_call(
         body,
-        in_specs=[pl.BlockSpec(memory_space=pltpu.VMEM)] * (n + 3),
-        out_specs=[pl.BlockSpec(memory_space=pltpu.VMEM)] * m,
-        out_shape=[jax.ShapeDtypeStruct((rows, width), kind) for kind in kinds],
-        scratch_shapes=[pltpu.VMEM((STAT, tile * m), F32)] * 2,
+        in_specs=[pl.BlockSpec(memory_space=pltpu.VMEM)] * 4
+        + [pl.BlockSpec(memory_space=pl.ANY)] * len(after),
+        out_specs=[pl.BlockSpec(memory_space=pltpu.VMEM)] * lines,
+        out_shape=[jax.ShapeDtypeStruct((rows, width), kind)] * lines,
+        scratch_shapes=[pltpu.VMEM((STAT, PACK * tile * lines), F32)] * 2,
         compiler_params=pltpu.CompilerParams(vmem_limit_bytes=40 * 1024 * 1024),
         cost_estimate=pl.CostEstimate(
-            flops=4 * m * rows * keys.shape[0] * columns,
+            flops=4 * lines * rows * keys.shape[0] * columns,
             bytes_accessed=4 * keys.shape[0] * columns,
-            transcendentals=m * rows * keys.shape[0] * heads,
+            transcendentals=lines * rows * keys.shape[0] * heads,
         ),
         name="attend",
-    )(bias, *planes, keys, values)
+    )(bias, plane, keys, values, *after)
 
 
 def load(cached, fresh, victims, queries, after):
@@ -221,17 +225,17 @@
 
 def merged(arrays, heads, last):
     columns = heads * HD
-    stats = [unpack_stats(get(slice(columns, columns + STAT)), heads) for get in arrays]
+    stats = [unpack_stats(get(slice(columns, columns + STAT))) for get in arrays]
     top = functools.reduce(jnp.maximum, [t for t, _ in stats])
     weights = [jnp.exp2(t - top) for t, _ in stats]
     mass = functools.reduce(jnp.add, [w * m for w, (_, m) in zip(weights, stats)])
     if last:
-        inverse = 1.0 / jnp.where(lanes(mass.shape[0]) < heads, mass, 1.0)
+        inverse = 1.0 / jnp.where(mass > 0.0, mass, 1.0)
         weights = [w * inverse for w in weights]
     for head in range(heads):
         cols = slice(head * HD, (head + 1) * HD)
         yield cols, functools.reduce(
-            jnp.add, [get(cols) * w[:, head : head + 1] for get, w in zip(arrays, weights)]
+            jnp.add, [get(cols) * w[:, lane_of(head) : lane_of(head) + 1] for get, w in zip(arrays, weights)]
         )
     if not last:
         yield slice(columns, columns + STAT), pack_stats(top, mass)
@@ -304,16 +308,18 @@
     def give(x, *by):
         return lax.ppermute(x, "seq", partner_perm(shape, by, True))
 
-    far_first = [0, *range(a_n - 1, 0, -1)]
-    line = [queries] + [fetch(queries, a, 0, 0) for a in far_first[1:]]
+    line = [queries] + [None] * (a_n - 1)
+    for a in range(a_n - 1, 0, -1):
+        line[a] = fetch(queries, a, 0, 0)
     lines = [line] + [[fetch(x, 0, b, 0) for x in line] for b in range(1, b_n)]
     keys, values, bias, line[0] = load(
-        (cache_keys, cache_values), (new_keys, new_values), victims[None], queries, line[min(2, a_n - 1)]
+        (cache_keys, cache_values), (new_keys, new_values), victims[None], queries, line[-1]
     )
     plane = join([x for pieces in lines for x in pieces])
     planes = [plane] + [fetch(plane, 0, 0, c) for c in range(1, c_n)]
-    kinds = [F32] * b_n + [BF16] * (b_n * (c_n - 1))
-    sums = attend(planes, b_n, kinds, keys, values, bias)
+    sums = []
+    for c, rows in enumerate(planes):
+        sums += attend(rows, b_n, BF16 if c else F32, keys, values, bias, sums[:1])
 
     def over_cores(b, kind):
         got = [give(sums[c * b_n + b], 0, 0, c) for c in range(1, c_n)]
@@ -321,9 +327,9 @@
 
     got = [[give(x, 0, b, 0) for x in over_cores(b, BF16)] for b in range(1, b_n)]
     own = over_cores(0, F32)
-    total = [[own[s]] + [pieces[s] for pieces in got] for s in range(a_n)]
+    total = [[own[a]] + [pieces[a] for pieces in got] for a in range(a_n)]
     last = [
-        give(merge_rows(total[s], heads, 1, [BF16])[0], far_first[s], 0, 0) for s in range(1, a_n)
+        give(merge_rows(total[a], heads, 1, [BF16])[0], a, 0, 0) for a in range(a_n - 1, 0, -1)
     ]
     return finish([*merge_rows(total[0], heads, 1, [F32]), *last], heads)
 

time: 34.7 us -> 33.8 us (0.974)
  waiting for transfers between devices: 6.68 us -> 5.25 us
  Pallas kernels: 7.23 us -> 8.18 us
  starting transfers between devices: 20.5 us -> 20.1 us
    ppermute x8, waiting for transfers between devices: 3.46 us -> 1.94 us  [fetch(): return lax.ppermute(x, 'seq', partner_perm(shape, by, False))]
    pallas_call x1 -> x2, Pallas kernels: 2.53 us -> 3.46 us  [attend(): pl.pallas_call(body, in_specs=[pl.BlockSpec(memory_space=pltpu.VMEM)] * 4...]
    ppermute x8, starting transfers between devices: 11.2 us -> 10.7 us  [fetch(): return lax.ppermute(x, 'seq', partner_perm(shape, by, False))]
  transfers between devices with their start and end apart: 17 -> 17, of which waited for: 7 -> 4; matrix products, arithmetic and copies ran while one was open for 0% -> 0% of each run, Pallas kernels for 11% -> 16%
where the time goes in v14:
time: 33.8 us; the launch traced here: 33.6 us
  starting transfers between devices  20.1 us (59%)
  Pallas kernels  8.18 us (24%)
  waiting for transfers between devices  5.25 us (16%)
    ppermute x8, starting transfers between devices, fetch(): return lax.ppermute(x, 'seq', partner_perm(shape, by, False))  10.7 us
    ppermute x9, starting transfers between devices, give(): return lax.ppermute(x, 'seq', partner_perm(shape, by, True))  9.35 us
    pallas_call x2, Pallas kernels, attend(): pl.pallas_call(body, in_specs=[pl.BlockSpec(memory_space=pltpu.VMEM)] * 4...  3.46 us
    ppermute x9, waiting for transfers between devices, give(): return lax.ppermute(x, 'seq', partner_perm(shape, by, True))  3.31 us
    pallas_call x1, Pallas kernels, load(): pl.pallas_call(body, in_specs=[in_hbm] * len(held) + [pl.BlockSpec(memory...  2.65 us
    pallas_call x8, Pallas kernels, call_merge(): pl.pallas_call(body, in_specs=[pl.BlockSpec(memory_space=pltpu.VMEM)] * l...  2.07 us
    ppermute x8, waiting for transfers between devices, fetch(): return lax.ppermute(x, 'seq', partner_perm(shape, by, False))  1.94 us
  transfers between devices with their start and end apart: 17, of which 4 were waited for; matrix products, arithmetic and copies ran while one was open for 0% of the time, Pallas kernels for 16%

profile of v14, /device:TPU:0, one launch (start us, length us, event | category | flops | bytes accessed | tf_op | source)
XLA Modules:
  0.0 33.6 jit_solution(12075614090766509114)
XLA Ops:
  0.0 3.0 %collective-permute-start.1 = (bf16[8,2560]{1,0:T(8,128)(2,1)}, bf16[8,2560]{1,0:T(8,128)(2,1)S(1)}, u32[]{:S(2)}, u32[]{:S(2)}) collective-permute-start(bf16[8,2560]{1,0:T(8,128)(2,1)} %refs_5_.1), channel_id=1, source_target_pairs={{4,0},{5,1},{6,2},{7,3},{0,4},{1,5},{2,6},{3,7},{12,8},{13,9},{14,... | collective-permute-start | bytes 122888 | tf_op jit(solution)/shard_map/ppermute | solution.py:306
  3.0 2.5 %collective-permute-start = (bf16[8,2560]{1,0:T(8,128)(2,1)}, bf16[8,2560]{1,0:T(8,128)(2,1)S(1)}, u32[]{:S(2)}, u32[]{:S(2)}) collective-permute-start(bf16[8,2560]{1,0:T(8,128)(2,1)} %refs_5_.1), channel_id=1, source_target_pairs={{12,0},{13,1},{14,2},{15,3},{8,4},{9,5},{10,6},{11,7},{4,8},{5,9},... | collective-permute-start | bytes 122888 | tf_op jit(solution)/shard_map/ppermute | solution.py:306
  5.5 0.1 collective-permute-start.2
  5.6 1.5 %collective-permute-start.3 = (bf16[8,2560]{1,0:T(8,128)(2,1)}, bf16[8,2560]{1,0:T(8,128)(2,1)S(1)}, u32[]{:S(2)}, u32[]{:S(2)}) collective-permute-start(bf16[8,2560]{1,0:T(8,128)(2,1)} %refs_5_.1), channel_id=1, source_target_pairs={{2,0},{3,1},{0,2},{1,3},{6,4},{7,5},{4,6},{5,7},{10,8},{11,9},{8,1... | collective-permute-start | bytes 122888 | tf_op jit(solution)/shard_map/ppermute | solution.py:306
  7.1 0.0 collective-permute-done.1.refs_1_
  7.1 0.5 %collective-permute-start.4 = (bf16[8,2560]{1,0:T(8,128)(2,1)S(1)}, bf16[8,2560]{1,0:T(8,128)(2,1)S(1)}, u32[]{:S(2)}, u32[]{:S(2)}) collective-permute-start(bf16[8,2560]{1,0:T(8,128)(2,1)S(1)} %collective-permute-done.1.refs_1_), channel_id=1, source_target_pairs={{2,0},{3,1},{0,2},{1,3},{6,4},{7,5},{4,6},{5,7},{10,8},{11,9},{8,1... | collective-permute-start | bytes 122888 | tf_op jit(solution)/shard_map/ppermute | solution.py:306
  7.6 1.9 %collective-permute-done.refs_6_.refs_3_ = bf16[8,2560]{1,0:T(8,128)(2,1)S(1)} collective-permute-done((bf16[8,2560]{1,0:T(8,128)(2,1)}, bf16[8,2560]{1,0:T(8,128)(2,1)S(1)}, u32[]{:S(2)}, u32[]{:S(2)}) %collective-permute-start) | collective-permute-done | bytes 40992 | tf_op jit(solution)/shard_map/ppermute | solution.py:306
  9.6 1.5 %collective-permute-start.6 = (bf16[8,2560]{1,0:T(8,128)(2,1)S(1)}, bf16[8,2560]{1,0:T(8,128)(2,1)S(1)}, u32[]{:S(2)}, u32[]{:S(2)}) collective-permute-start(bf16[8,2560]{1,0:T(8,128)(2,1)S(1)} %collective-permute-done.refs_6_.refs_3_), channel_id=1, source_target_pairs={{2,0},{3,1},{0,2},{1,3},{6,4},{7,5},{4,6},{5,7},{10,8},{11,9},{8,1... | collective-permute-start | bytes 122888 | tf_op jit(solution)/shard_map/ppermute | solution.py:306
  11.1 1.5 %collective-permute-start.5 = (bf16[8,2560]{1,0:T(8,128)(2,1)S(1)}, bf16[8,2560]{1,0:T(8,128)(2,1)S(1)}, u32[]{:S(2)}, u32[]{:S(2)}) collective-permute-start(bf16[8,2560]{1,0:T(8,128)(2,1)S(1)} %collective-permute-done.2.refs_2_), channel_id=1, source_target_pairs={{2,0},{3,1},{0,2},{1,3},{6,4},{7,5},{4,6},{5,7},{10,8},{11,9},{8,1... | collective-permute-start | bytes 122888 | tf_op jit(solution)/shard_map/ppermute | solution.py:306
  12.6 2.6 %load.1 = (bf16[528,2560]{1,0:T(8,128)(2,1)S(1)}, bf16[528,2560]{1,0:T(8,128)(2,1)S(1)}, f32[528,128]{1,0:T(8,128)S(1)}, bf16[8,2560]{1,0:T(8,128)(2,1)S(1)}) custom-call(bf16[512,2560]{1,0:T(8,128)(2,1)} %refs_0_.1, bf16[512,2560]{1,0:T(8,128)(2,1)} %refs_1_.1, bf16[8,2560]{1,0:T(8,128)(2,1)} %refs_2_.1, bf16[8,2560]{1,0:T(8,128)(2,1)} %refs_3_.1, ...), custom_call_target="tpu_custom_call" | custom-call | bytes 10485760 | tf_op jit(solution)/shard_map/load/pallas_call | solution.py:210
  15.3 0.1 collective-permute-start.7
  15.4 1.7 %attend.2 = (f32[32,2688]{1,0:T(8,128)S(1)}, f32[32,2688]{1,0:T(8,128)S(1)}) custom-call(f32[528,128]{1,0:T(8,128)S(1)} %get-tuple-element.21.refs_0_, bf16[64,2560]{1,0:T(8,128)(2,1)S(1)} %merge.8.refs_1_, bf16[528,2560]{1,0:T(8,128)(2,1)S(1)} %get-tuple-element.23.refs_2_, bf16[528,2560]{1,0:T(8,128)(2,1)S(1)} %get-tuple-element.24.refs_3_), custom_call_target="tpu_custom_call" | custom-call | flops 346030080 | bytes 5406720 | tf_op jit(solution)/shard_map/attend/pallas_call | solution.py:149
  17.1 1.7 %attend.3 = (bf16[32,2688]{1,0:T(8,128)(2,1)S(1)}, bf16[32,2688]{1,0:T(8,128)(2,1)S(1)}) custom-call(f32[528,128]{1,0:T(8,128)S(1)} %get-tuple-element.21.refs_0_, bf16[64,2560]{1,0:T(8,128)(2,1)S(1)} %collective-permute-done.7.refs_1_, bf16[528,2560]{1,0:T(8,128)(2,1)S(1)} %get-tuple-element.23.refs_2_, bf16[528,2560]{1,0:T(8,128)(2,1)S(1)} %get-tuple-element.24.refs_3_, ...), custom_call_target="tpu_custom_call" | custom-call | flops 346030080 | bytes 5406720 | tf_op jit(solution)/shard_map/attend/pallas_call | solution.py:149
  18.9 0.6 %collective-permute-start.9 = (bf16[32,2688]{1,0:T(8,128)(2,1)S(1)}, bf16[32,2688]{1,0:T(8,128)(2,1)S(1)}, u32[]{:S(2)}, u32[]{:S(2)}) collective-permute-start(bf16[32,2688]{1,0:T(8,128)(2,1)S(1)} %get-tuple-element.29), channel_id=1, source_target_pairs={{0,1},{1,0},{2,3},{3,2},{4,5},{5,4},{6,7},{7,6},{8,9},{9,8},{10,11... | collective-permute-start | bytes 516104 | tf_op jit(solution)/shard_map/ppermute | solution.py:309
  19.4 0.1 collective-permute-start.8
  19.5 1.0 %collective-permute-done.9.refs_1_ = bf16[32,2688]{1,0:T(8,128)(2,1)S(1)} collective-permute-done((bf16[32,2688]{1,0:T(8,128)(2,1)S(1)}, bf16[32,2688]{1,0:T(8,128)(2,1)S(1)}, u32[]{:S(2)}, u32[]{:S(2)}) %collective-permute-start.9) | collective-permute-done | bytes 172064 | tf_op jit(solution)/shard_map/ppermute | solution.py:309
  20.5 0.3 merge.10
  20.8 1.4 %collective-permute-start.11 = (bf16[8,2688]{1,0:T(8,128)(2,1)S(1)}, bf16[8,2688]{1,0:T(8,128)(2,1)S(1)}, u32[]{:S(2)}, u32[]{:S(2)}) collective-permute-start(bf16[8,2688]{1,0:T(8,128)(2,1)S(1)} %get-tuple-element.32), channel_id=1, source_target_pairs={{0,2},{1,3},{2,0},{3,1},{4,6},{5,7},{6,4},{7,5},{8,10},{9,11},{10,... | collective-permute-start | bytes 129032 | tf_op jit(solution)/shard_map/ppermute | solution.py:309
  22.1 0.7 %collective-permute-start.13 = (bf16[8,2688]{1,0:T(8,128)(2,1)S(1)}, bf16[8,2688]{1,0:T(8,128)(2,1)S(1)}, u32[]{:S(2)}, u32[]{:S(2)}) collective-permute-start(bf16[8,2688]{1,0:T(8,128)(2,1)S(1)} %get-tuple-element.34), channel_id=1, source_target_pairs={{0,2},{1,3},{2,0},{3,1},{4,6},{5,7},{6,4},{7,5},{8,10},{9,11},{10,... | collective-permute-start | bytes 129032 | tf_op jit(solution)/shard_map/ppermute | solution.py:309
  22.9 1.3 %collective-permute-start.15 = (bf16[8,2688]{1,0:T(8,128)(2,1)S(1)}, bf16[8,2688]{1,0:T(8,128)(2,1)S(1)}, u32[]{:S(2)}, u32[]{:S(2)}) collective-permute-start(bf16[8,2688]{1,0:T(8,128)(2,1)S(1)} %get-tuple-element.36), channel_id=1, source_target_pairs={{0,2},{1,3},{2,0},{3,1},{4,6},{5,7},{6,4},{7,5},{8,10},{9,11},{10,... | collective-permute-start | bytes 129032 | tf_op jit(solution)/shard_map/ppermute | solution.py:309
  24.2 0.7 %collective-permute-start.10 = (bf16[8,2688]{1,0:T(8,128)(2,1)S(1)}, bf16[8,2688]{1,0:T(8,128)(2,1)S(1)}, u32[]{:S(2)}, u32[]{:S(2)}) collective-permute-start(bf16[8,2688]{1,0:T(8,128)(2,1)S(1)} %get-tuple-element.30), channel_id=1, source_target_pairs={{0,2},{1,3},{2,0},{3,1},{4,6},{5,7},{6,4},{7,5},{8,10},{9,11},{10,... | collective-permute-start | bytes 129032 | tf_op jit(solution)/shard_map/ppermute | solution.py:309
  24.9 0.3 merge.9
  25.2 0.1 merge.12
  25.3 1.9 %collective-permute-start.12 = (bf16[8,2688]{1,0:T(8,128)(2,1)S(1)}, bf16[8,2688]{1,0:T(8,128)(2,1)S(1)}, u32[]{:S(2)}, u32[]{:S(2)}) collective-permute-start(bf16[8,2688]{1,0:T(8,128)(2,1)S(1)} %merge.12), channel_id=1, source_target_pairs={{0,12},{1,13},{2,14},{3,15},{4,8},{5,9},{6,10},{7,11},{8,4},{9,5},... | collective-permute-start | bytes 129032 | tf_op jit(solution)/shard_map/ppermute | solution.py:309
  27.3 0.1 merge.13
  27.4 0.5 %collective-permute-start.14 = (bf16[8,2688]{1,0:T(8,128)(2,1)S(1)}, bf16[8,2688]{1,0:T(8,128)(2,1)S(1)}, u32[]{:S(2)}, u32[]{:S(2)}) collective-permute-start(bf16[8,2688]{1,0:T(8,128)(2,1)S(1)} %merge.13), channel_id=1, source_target_pairs={{0,8},{1,9},{2,10},{3,11},{4,12},{5,13},{6,14},{7,15},{8,0},{9,1},... | collective-permute-start | bytes 129032 | tf_op jit(solution)/shard_map/ppermute | solution.py:309
  27.9 0.1 merge.14
  28.0 2.2 %collective-permute-start.16 = (bf16[8,2688]{1,0:T(8,128)(2,1)S(1)}, bf16[8,2688]{1,0:T(8,128)(2,1)S(1)}, u32[]{:S(2)}, u32[]{:S(2)}) collective-permute-start(bf16[8,2688]{1,0:T(8,128)(2,1)S(1)} %merge.14), channel_id=1, source_target_pairs={{0,4},{1,5},{2,6},{3,7},{4,0},{5,1},{6,2},{7,3},{8,12},{9,13},{10,... | collective-permute-start | bytes 129032 | tf_op jit(solution)/shard_map/ppermute | solution.py:309
  30.2 0.1 merge.11.refs_0_
  30.4 0.8 %collective-permute-done.12.refs_1_ = bf16[8,2688]{1,0:T(8,128)(2,1)S(1)} collective-permute-done((bf16[8,2688]{1,0:T(8,128)(2,1)S(1)}, bf16[8,2688]{1,0:T(8,128)(2,1)S(1)}, u32[]{:S(2)}, u32[]{:S(2)}) %collective-permute-start.12) | collective-permute-done | bytes 43040 | tf_op jit(solution)/shard_map/ppermute | solution.py:309
  31.2 1.5 %collective-permute-done.14.refs_2_ = bf16[8,2688]{1,0:T(8,128)(2,1)S(1)} collective-permute-done((bf16[8,2688]{1,0:T(8,128)(2,1)S(1)}, bf16[8,2688]{1,0:T(8,128)(2,1)S(1)}, u32[]{:S(2)}, u32[]{:S(2)}) %collective-permute-start.14) | collective-permute-done | bytes 43040 | tf_op jit(solution)/shard_map/ppermute | solution.py:309
  32.7 0.9 %merge.15 = bf16[8,2560]{1,0:T(8,128)(2,1)} custom-call(f32[8,2688]{1,0:T(8,128)S(1)} %merge.11.refs_0_, bf16[8,2688]{1,0:T(8,128)(2,1)S(1)} %collective-permute-done.12.refs_1_, bf16[8,2688]{1,0:T(8,128)(2,1)S(1)} %collective-permute-done.14.refs_2_, bf16[8,2688]{1,0:T(8,128)(2,1)S(1)} %collective-permute-done.16.refs_3_), custom_call_target="tpu_custom_call" | custom-call | flops 344064 | bytes 344064 | tf_op jit(solution)/shard_map/merge/pallas_call | solution.py:286
  (13 shorter events, 0.1 us)
Async XLA Ops:
  0.0 7.1 %collective-permute-start.1 = (bf16[8,2560]{1,0:T(8,128)(2,1)}, bf16[8,2560]{1,0:T(8,128)(2,1)S(1)}, u32[]{:S(2)}, u32[]{:S(2)}) collective-permute-start(bf16[8,2560]{1,0:T(8,128)(2,1)} %refs_5_.1), channel_id=1, source_target_pairs={{4,0},{5,1},{6,2},{7,3},{0,4},{1,5},{2,6},{3,7},{12,8},{13,9},{14,... | collective-permute-start | bytes 122888 | tf_op jit(solution)/shard_map/ppermute | solution.py:306
  3.0 6.5 %collective-permute-start = (bf16[8,2560]{1,0:T(8,128)(2,1)}, bf16[8,2560]{1,0:T(8,128)(2,1)S(1)}, u32[]{:S(2)}, u32[]{:S(2)}) collective-permute-start(bf16[8,2560]{1,0:T(8,128)(2,1)} %refs_5_.1), channel_id=1, source_target_pairs={{12,0},{13,1},{14,2},{15,3},{8,4},{9,5},{10,6},{11,7},{4,8},{5,9},... | collective-permute-start | bytes 122888 | tf_op jit(solution)/shard_map/ppermute | solution.py:306
  5.5 5.6 %collective-permute-start.2 = (bf16[8,2560]{1,0:T(8,128)(2,1)}, bf16[8,2560]{1,0:T(8,128)(2,1)S(1)}, u32[]{:S(2)}, u32[]{:S(2)}) collective-permute-start(bf16[8,2560]{1,0:T(8,128)(2,1)} %refs_5_.1), channel_id=1, source_target_pairs={{8,0},{9,1},{10,2},{11,3},{12,4},{13,5},{14,6},{15,7},{0,8},{1,9},... | collective-permute-start | bytes 122888 | tf_op jit(solution)/shard_map/ppermute | solution.py:306
  5.6 9.6 %collective-permute-start.3 = (bf16[8,2560]{1,0:T(8,128)(2,1)}, bf16[8,2560]{1,0:T(8,128)(2,1)S(1)}, u32[]{:S(2)}, u32[]{:S(2)}) collective-permute-start(bf16[8,2560]{1,0:T(8,128)(2,1)} %refs_5_.1), channel_id=1, source_target_pairs={{2,0},{3,1},{0,2},{1,3},{6,4},{7,5},{4,6},{5,7},{10,8},{11,9},{8,1... | collective-permute-start | bytes 122888 | tf_op jit(solution)/shard_map/ppermute | solution.py:306
  7.1 8.1 %collective-permute-start.4 = (bf16[8,2560]{1,0:T(8,128)(2,1)S(1)}, bf16[8,2560]{1,0:T(8,128)(2,1)S(1)}, u32[]{:S(2)}, u32[]{:S(2)}) collective-permute-start(bf16[8,2560]{1,0:T(8,128)(2,1)S(1)} %collective-permute-done.1.refs_1_), channel_id=1, source_target_pairs={{2,0},{3,1},{0,2},{1,3},{6,4},{7,5},{4,6},{5,7},{10,8},{11,9},{8,1... | collective-permute-start | bytes 122888 | tf_op jit(solution)/shard_map/ppermute | solution.py:306
  9.6 5.7 %collective-permute-start.6 = (bf16[8,2560]{1,0:T(8,128)(2,1)S(1)}, bf16[8,2560]{1,0:T(8,128)(2,1)S(1)}, u32[]{:S(2)}, u32[]{:S(2)}) collective-permute-start(bf16[8,2560]{1,0:T(8,128)(2,1)S(1)} %collective-permute-done.refs_6_.refs_3_), channel_id=1, source_target_pairs={{2,0},{3,1},{0,2},{1,3},{6,4},{7,5},{4,6},{5,7},{10,8},{11,9},{8,1... | collective-permute-start | bytes 122888 | tf_op jit(solution)/shard_map/ppermute | solution.py:306
  11.1 4.2 %collective-permute-start.5 = (bf16[8,2560]{1,0:T(8,128)(2,1)S(1)}, bf16[8,2560]{1,0:T(8,128)(2,1)S(1)}, u32[]{:S(2)}, u32[]{:S(2)}) collective-permute-start(bf16[8,2560]{1,0:T(8,128)(2,1)S(1)} %collective-permute-done.2.refs_2_), channel_id=1, source_target_pairs={{2,0},{3,1},{0,2},{1,3},{6,4},{7,5},{4,6},{5,7},{10,8},{11,9},{8,1... | collective-permute-start | bytes 122888 | tf_op jit(solution)/shard_map/ppermute | solution.py:306
  15.3 1.8 %collective-permute-start.7 = (bf16[64,2560]{1,0:T(8,128)(2,1)S(1)}, bf16[64,2560]{1,0:T(8,128)(2,1)S(1)}, u32[]{:S(2)}, u32[]{:S(2)}) collective-permute-start(bf16[64,2560]{1,0:T(8,128)(2,1)S(1)} %merge.8.refs_1_), channel_id=1, source_target_pairs={{1,0},{0,1},{3,2},{2,3},{5,4},{4,5},{7,6},{6,7},{9,8},{8,9},{11,10... | collective-permute-start | bytes 983048 | tf_op jit(solution)/shard_map/ppermute | solution.py:306
  18.9 1.6 %collective-permute-start.9 = (bf16[32,2688]{1,0:T(8,128)(2,1)S(1)}, bf16[32,2688]{1,0:T(8,128)(2,1)S(1)}, u32[]{:S(2)}, u32[]{:S(2)}) collective-permute-start(bf16[32,2688]{1,0:T(8,128)(2,1)S(1)} %get-tuple-element.29), channel_id=1, source_target_pairs={{0,1},{1,0},{2,3},{3,2},{4,5},{5,4},{6,7},{7,6},{8,9},{9,8},{10,11... | collective-permute-start | bytes 516104 | tf_op jit(solution)/shard_map/ppermute | solution.py:309
  19.4 5.5 %collective-permute-start.8 = (bf16[32,2688]{1,0:T(8,128)(2,1)S(1)}, bf16[32,2688]{1,0:T(8,128)(2,1)S(1)}, u32[]{:S(2)}, u32[]{:S(2)}) collective-permute-start(bf16[32,2688]{1,0:T(8,128)(2,1)S(1)} %get-tuple-element.26), channel_id=1, source_target_pairs={{0,1},{1,0},{2,3},{3,2},{4,5},{5,4},{6,7},{7,6},{8,9},{9,8},{10,11... | collective-permute-start | bytes 516104 | tf_op jit(solution)/shard_map/ppermute | solution.py:309
  20.8 4.4 %collective-permute-start.11 = (bf16[8,2688]{1,0:T(8,128)(2,1)S(1)}, bf16[8,2688]{1,0:T(8,128)(2,1)S(1)}, u32[]{:S(2)}, u32[]{:S(2)}) collective-permute-start(bf16[8,2688]{1,0:T(8,128)(2,1)S(1)} %get-tuple-element.32), channel_id=1, source_target_pairs={{0,2},{1,3},{2,0},{3,1},{4,6},{5,7},{6,4},{7,5},{8,10},{9,11},{10,... | collective-permute-start | bytes 129032 | tf_op jit(solution)/shard_map/ppermute | solution.py:309
  22.1 5.1 %collective-permute-start.13 = (bf16[8,2688]{1,0:T(8,128)(2,1)S(1)}, bf16[8,2688]{1,0:T(8,128)(2,1)S(1)}, u32[]{:S(2)}, u32[]{:S(2)}) collective-permute-start(bf16[8,2688]{1,0:T(8,128)(2,1)S(1)} %get-tuple-element.34), channel_id=1, source_target_pairs={{0,2},{1,3},{2,0},{3,1},{4,6},{5,7},{6,4},{7,5},{8,10},{9,11},{10,... | collective-permute-start | bytes 129032 | tf_op jit(solution)/shard_map/ppermute | solution.py:309
  22.9 5.0 %collective-permute-start.15 = (bf16[8,2688]{1,0:T(8,128)(2,1)S(1)}, bf16[8,2688]{1,0:T(8,128)(2,1)S(1)}, u32[]{:S(2)}, u32[]{:S(2)}) collective-permute-start(bf16[8,2688]{1,0:T(8,128)(2,1)S(1)} %get-tuple-element.36), channel_id=1, source_target_pairs={{0,2},{1,3},{2,0},{3,1},{4,6},{5,7},{6,4},{7,5},{8,10},{9,11},{10,... | collective-permute-start | bytes 129032 | tf_op jit(solution)/shard_map/ppermute | solution.py:309
  24.2 6.1 %collective-permute-start.10 = (bf16[8,2688]{1,0:T(8,128)(2,1)S(1)}, bf16[8,2688]{1,0:T(8,128)(2,1)S(1)}, u32[]{:S(2)}, u32[]{:S(2)}) collective-permute-start(bf16[8,2688]{1,0:T(8,128)(2,1)S(1)} %get-tuple-element.30), channel_id=1, source_target_pairs={{0,2},{1,3},{2,0},{3,1},{4,6},{5,7},{6,4},{7,5},{8,10},{9,11},{10,... | collective-permute-start | bytes 129032 | tf_op jit(solution)/shard_map/ppermute | solution.py:309
  25.3 5.9 %collective-permute-start.12 = (bf16[8,2688]{1,0:T(8,128)(2,1)S(1)}, bf16[8,2688]{1,0:T(8,128)(2,1)S(1)}, u32[]{:S(2)}, u32[]{:S(2)}) collective-permute-start(bf16[8,2688]{1,0:T(8,128)(2,1)S(1)} %merge.12), channel_id=1, source_target_pairs={{0,12},{1,13},{2,14},{3,15},{4,8},{5,9},{6,10},{7,11},{8,4},{9,5},... | collective-permute-start | bytes 129032 | tf_op jit(solution)/shard_map/ppermute | solution.py:309
  27.4 5.3 %collective-permute-start.14 = (bf16[8,2688]{1,0:T(8,128)(2,1)S(1)}, bf16[8,2688]{1,0:T(8,128)(2,1)S(1)}, u32[]{:S(2)}, u32[]{:S(2)}) collective-permute-start(bf16[8,2688]{1,0:T(8,128)(2,1)S(1)} %merge.13), channel_id=1, source_target_pairs={{0,8},{1,9},{2,10},{3,11},{4,12},{5,13},{6,14},{7,15},{8,0},{9,1},... | collective-permute-start | bytes 129032 | tf_op jit(solution)/shard_map/ppermute | solution.py:309
  28.0 4.7 %collective-permute-start.16 = (bf16[8,2688]{1,0:T(8,128)(2,1)S(1)}, bf16[8,2688]{1,0:T(8,128)(2,1)S(1)}, u32[]{:S(2)}, u32[]{:S(2)}) collective-permute-start(bf16[8,2688]{1,0:T(8,128)(2,1)S(1)} %merge.14), channel_id=1, source_target_pairs={{0,4},{1,5},{2,6},{3,7},{4,0},{5,1},{6,2},{7,3},{8,12},{9,13},{10,... | collective-permute-start | bytes 129032 | tf_op jit(solution)/shard_map/ppermute | solution.py:309

commit v15 on v14

--- a/solution.py
+++ b/solution.py
@@ -308,9 +308,8 @@
     def give(x, *by):
         return lax.ppermute(x, "seq", partner_perm(shape, by, True))
 
-    line = [queries] + [None] * (a_n - 1)
-    for a in range(a_n - 1, 0, -1):
-        line[a] = fetch(queries, a, 0, 0)
+    far_first = [0, *range(a_n - 1, 0, -1)]
+    line = [queries] + [fetch(queries, a, 0, 0) for a in far_first[1:]]
     lines = [line] + [[fetch(x, 0, b, 0) for x in line] for b in range(1, b_n)]
     keys, values, bias, line[0] = load(
         (cache_keys, cache_values), (new_keys, new_values), victims[None], queries, line[-1]
@@ -327,9 +326,9 @@
 
     got = [[give(x, 0, b, 0) for x in over_cores(b, BF16)] for b in range(1, b_n)]
     own = over_cores(0, F32)
-    total = [[own[a]] + [pieces[a] for pieces in got] for a in range(a_n)]
+    total = [[own[s]] + [pieces[s] for pieces in got] for s in range(a_n)]
     last = [
-        give(merge_rows(total[a], heads, 1, [BF16])[0], a, 0, 0) for a in range(a_n - 1, 0, -1)
+        give(merge_rows(total[s], heads, 1, [BF16])[0], far_first[s], 0, 0) for s in range(1, a_n)
     ]
     return finish([*merge_rows(total[0], heads, 1, [F32]), *last], heads)
 

time: 33.8 us -> 34 us (level)
  starting transfers between devices: 20.1 us -> 21 us
  waiting for transfers between devices: 5.25 us -> 4.52 us
    ppermute x8, waiting for transfers between devices: 1.94 us -> 0.51 us  [fetch(): return lax.ppermute(x, 'seq', partner_perm(shape, by, False))]
    ppermute x8, starting transfers between devices: 10.7 us -> 11.7 us  [fetch(): return lax.ppermute(x, 'seq', partner_perm(shape, by, False))]
    ppermute x9, waiting for transfers between devices: 3.31 us -> 4 us  [give(): return lax.ppermute(x, 'seq', partner_perm(shape, by, True))]
  transfers between devices with their start and end apart: 17 -> 17, of which waited for: 4 -> 5; matrix products, arithmetic and copies ran while one was open for 0% -> 0% of each run, Pallas kernels for 16% -> 16%
where the time goes in v15:
time: 34 us; the launch traced here: 33.8 us
  starting transfers between devices  21 us (62%)
  Pallas kernels  8.17 us (24%)
  waiting for transfers between devices  4.52 us (13%)
    ppermute x8, starting transfers between devices, fetch(): return lax.ppermute(x, 'seq', partner_perm(shape, by, False))  11.7 us
    ppermute x9, starting transfers between devices, give(): return lax.ppermute(x, 'seq', partner_perm(shape, by, True))  9.36 us
    ppermute x9, waiting for transfers between devices, give(): return lax.ppermute(x, 'seq', partner_perm(shape, by, True))  4 us
    pallas_call x2, Pallas kernels, attend(): pl.pallas_call(body, in_specs=[pl.BlockSpec(memory_space=pltpu.VMEM)] * 4...  3.46 us
    pallas_call x1, Pallas kernels, load(): pl.pallas_call(body, in_specs=[in_hbm] * len(held) + [pl.BlockSpec(memory...  2.65 us
    pallas_call x8, Pallas kernels, call_merge(): pl.pallas_call(body, in_specs=[pl.BlockSpec(memory_space=pltpu.VMEM)] * l...  2.06 us
  transfers between devices with their start and end apart: 17, of which 5 were waited for; matrix products, arithmetic and copies ran while one was open for 0% of the time, Pallas kernels for 16%

profile of v15, /device:TPU:0, one launch (start us, length us, event | category | flops | bytes accessed | tf_op | source)
XLA Modules:
  0.0 33.8 jit_solution(8980769731703812145)
XLA Ops:
  0.0 5.0 %collective-permute-start.1 = (bf16[8,2560]{1,0:T(8,128)(2,1)}, bf16[8,2560]{1,0:T(8,128)(2,1)S(1)}, u32[]{:S(2)}, u32[]{:S(2)}) collective-permute-start(bf16[8,2560]{1,0:T(8,128)(2,1)} %refs_5_.1), channel_id=1, source_target_pairs={{12,0},{13,1},{14,2},{15,3},{8,4},{9,5},{10,6},{11,7},{4,8},{5,9},... | collective-permute-start | bytes 122888 | tf_op jit(solution)/shard_map/ppermute | solution.py:306
  5.1 0.6 %collective-permute-start.2 = (bf16[8,2560]{1,0:T(8,128)(2,1)}, bf16[8,2560]{1,0:T(8,128)(2,1)S(1)}, u32[]{:S(2)}, u32[]{:S(2)}) collective-permute-start(bf16[8,2560]{1,0:T(8,128)(2,1)} %refs_5_.1), channel_id=1, source_target_pairs={{8,0},{9,1},{10,2},{11,3},{12,4},{13,5},{14,6},{15,7},{0,8},{1,9},... | collective-permute-start | bytes 122888 | tf_op jit(solution)/shard_map/ppermute | solution.py:306
  5.6 1.8 %collective-permute-start.3 = (bf16[8,2560]{1,0:T(8,128)(2,1)}, bf16[8,2560]{1,0:T(8,128)(2,1)S(1)}, u32[]{:S(2)}, u32[]{:S(2)}) collective-permute-start(bf16[8,2560]{1,0:T(8,128)(2,1)} %refs_5_.1), channel_id=1, source_target_pairs={{2,0},{3,1},{0,2},{1,3},{6,4},{7,5},{4,6},{5,7},{10,8},{11,9},{8,1... | collective-permute-start | bytes 122888 | tf_op jit(solution)/shard_map/ppermute | solution.py:306
  7.4 1.6 %collective-permute-start.4 = (bf16[8,2560]{1,0:T(8,128)(2,1)S(1)}, bf16[8,2560]{1,0:T(8,128)(2,1)S(1)}, u32[]{:S(2)}, u32[]{:S(2)}) collective-permute-start(bf16[8,2560]{1,0:T(8,128)(2,1)S(1)} %collective-permute-done.1.refs_1_), channel_id=1, source_target_pairs={{2,0},{3,1},{0,2},{1,3},{6,4},{7,5},{4,6},{5,7},{10,8},{11,9},{8,1... | collective-permute-start | bytes 122888 | tf_op jit(solution)/shard_map/ppermute | solution.py:306
  9.0 0.3 collective-permute-done.refs_6_.refs_3_
  9.3 1.5 %collective-permute-start.6 = (bf16[8,2560]{1,0:T(8,128)(2,1)S(1)}, bf16[8,2560]{1,0:T(8,128)(2,1)S(1)}, u32[]{:S(2)}, u32[]{:S(2)}) collective-permute-start(bf16[8,2560]{1,0:T(8,128)(2,1)S(1)} %collective-permute-done.refs_6_.refs_3_), channel_id=1, source_target_pairs={{2,0},{3,1},{0,2},{1,3},{6,4},{7,5},{4,6},{5,7},{10,8},{11,9},{8,1... | collective-permute-start | bytes 122888 | tf_op jit(solution)/shard_map/ppermute | solution.py:306
  10.8 1.1 %collective-permute-start.5 = (bf16[8,2560]{1,0:T(8,128)(2,1)S(1)}, bf16[8,2560]{1,0:T(8,128)(2,1)S(1)}, u32[]{:S(2)}, u32[]{:S(2)}) collective-permute-start(bf16[8,2560]{1,0:T(8,128)(2,1)S(1)} %collective-permute-done.2.refs_2_), channel_id=1, source_target_pairs={{2,0},{3,1},{0,2},{1,3},{6,4},{7,5},{4,6},{5,7},{10,8},{11,9},{8,1... | collective-permute-start | bytes 122888 | tf_op jit(solution)/shard_map/ppermute | solution.py:306
  11.9 2.6 %load.1 = (bf16[528,2560]{1,0:T(8,128)(2,1)S(1)}, bf16[528,2560]{1,0:T(8,128)(2,1)S(1)}, f32[528,128]{1,0:T(8,128)S(1)}, bf16[8,2560]{1,0:T(8,128)(2,1)S(1)}) custom-call(bf16[512,2560]{1,0:T(8,128)(2,1)} %refs_0_.1, bf16[512,2560]{1,0:T(8,128)(2,1)} %refs_1_.1, bf16[8,2560]{1,0:T(8,128)(2,1)} %refs_2_.1, bf16[8,2560]{1,0:T(8,128)(2,1)} %refs_3_.1, ...), custom_call_target="tpu_custom_call" | custom-call | bytes 10485760 | tf_op jit(solution)/shard_map/load/pallas_call | solution.py:210
  14.6 0.2 collective-permute-done.5.refs_6_
  14.8 0.1 collective-permute-start.7
  14.9 1.7 %attend.2 = (f32[32,2688]{1,0:T(8,128)S(1)}, f32[32,2688]{1,0:T(8,128)S(1)}) custom-call(f32[528,128]{1,0:T(8,128)S(1)} %get-tuple-element.21.refs_0_, bf16[64,2560]{1,0:T(8,128)(2,1)S(1)} %merge.8.refs_1_, bf16[528,2560]{1,0:T(8,128)(2,1)S(1)} %get-tuple-element.23.refs_2_, bf16[528,2560]{1,0:T(8,128)(2,1)S(1)} %get-tuple-element.24.refs_3_), custom_call_target="tpu_custom_call" | custom-call | flops 346030080 | bytes 5406720 | tf_op jit(solution)/shard_map/attend/pallas_call | solution.py:149
  16.6 1.7 %attend.3 = (bf16[32,2688]{1,0:T(8,128)(2,1)S(1)}, bf16[32,2688]{1,0:T(8,128)(2,1)S(1)}) custom-call(f32[528,128]{1,0:T(8,128)S(1)} %get-tuple-element.21.refs_0_, bf16[64,2560]{1,0:T(8,128)(2,1)S(1)} %collective-permute-done.7.refs_1_, bf16[528,2560]{1,0:T(8,128)(2,1)S(1)} %get-tuple-element.23.refs_2_, bf16[528,2560]{1,0:T(8,128)(2,1)S(1)} %get-tuple-element.24.refs_3_, ...), custom_call_target="tpu_custom_call" | custom-call | flops 346030080 | bytes 5406720 | tf_op jit(solution)/shard_map/attend/pallas_call | solution.py:149
  18.4 0.6 %collective-permute-start.9 = (bf16[32,2688]{1,0:T(8,128)(2,1)S(1)}, bf16[32,2688]{1,0:T(8,128)(2,1)S(1)}, u32[]{:S(2)}, u32[]{:S(2)}) collective-permute-start(bf16[32,2688]{1,0:T(8,128)(2,1)S(1)} %get-tuple-element.29), channel_id=1, source_target_pairs={{0,1},{1,0},{2,3},{3,2},{4,5},{5,4},{6,7},{7,6},{8,9},{9,8},{10,11... | collective-permute-start | bytes 516104 | tf_op jit(solution)/shard_map/ppermute | solution.py:309
  18.9 0.1 collective-permute-start.8
  19.0 1.0 %collective-permute-done.9.refs_1_ = bf16[32,2688]{1,0:T(8,128)(2,1)S(1)} collective-permute-done((bf16[32,2688]{1,0:T(8,128)(2,1)S(1)}, bf16[32,2688]{1,0:T(8,128)(2,1)S(1)}, u32[]{:S(2)}, u32[]{:S(2)}) %collective-permute-start.9) | collective-permute-done | bytes 172064 | tf_op jit(solution)/shard_map/ppermute | solution.py:309
  20.0 0.3 merge.10
  20.3 1.2 %collective-permute-start.11 = (bf16[8,2688]{1,0:T(8,128)(2,1)S(1)}, bf16[8,2688]{1,0:T(8,128)(2,1)S(1)}, u32[]{:S(2)}, u32[]{:S(2)}) collective-permute-start(bf16[8,2688]{1,0:T(8,128)(2,1)S(1)} %get-tuple-element.32), channel_id=1, source_target_pairs={{0,2},{1,3},{2,0},{3,1},{4,6},{5,7},{6,4},{7,5},{8,10},{9,11},{10,... | collective-permute-start | bytes 129032 | tf_op jit(solution)/shard_map/ppermute | solution.py:309
  21.4 0.9 %collective-permute-start.13 = (bf16[8,2688]{1,0:T(8,128)(2,1)S(1)}, bf16[8,2688]{1,0:T(8,128)(2,1)S(1)}, u32[]{:S(2)}, u32[]{:S(2)}) collective-permute-start(bf16[8,2688]{1,0:T(8,128)(2,1)S(1)} %get-tuple-element.34), channel_id=1, source_target_pairs={{0,2},{1,3},{2,0},{3,1},{4,6},{5,7},{6,4},{7,5},{8,10},{9,11},{10,... | collective-permute-start | bytes 129032 | tf_op jit(solution)/shard_map/ppermute | solution.py:309
  22.4 1.1 %collective-permute-start.15 = (bf16[8,2688]{1,0:T(8,128)(2,1)S(1)}, bf16[8,2688]{1,0:T(8,128)(2,1)S(1)}, u32[]{:S(2)}, u32[]{:S(2)}) collective-permute-start(bf16[8,2688]{1,0:T(8,128)(2,1)S(1)} %get-tuple-element.36), channel_id=1, source_target_pairs={{0,2},{1,3},{2,0},{3,1},{4,6},{5,7},{6,4},{7,5},{8,10},{9,11},{10,... | collective-permute-start | bytes 129032 | tf_op jit(solution)/shard_map/ppermute | solution.py:309
  23.5 0.9 %collective-permute-start.10 = (bf16[8,2688]{1,0:T(8,128)(2,1)S(1)}, bf16[8,2688]{1,0:T(8,128)(2,1)S(1)}, u32[]{:S(2)}, u32[]{:S(2)}) collective-permute-start(bf16[8,2688]{1,0:T(8,128)(2,1)S(1)} %get-tuple-element.30), channel_id=1, source_target_pairs={{0,2},{1,3},{2,0},{3,1},{4,6},{5,7},{6,4},{7,5},{8,10},{9,11},{10,... | collective-permute-start | bytes 129032 | tf_op jit(solution)/shard_map/ppermute | solution.py:309
  24.4 0.3 merge.9
  24.7 0.1 merge.12
  24.9 2.8 %collective-permute-start.12 = (bf16[8,2688]{1,0:T(8,128)(2,1)S(1)}, bf16[8,2688]{1,0:T(8,128)(2,1)S(1)}, u32[]{:S(2)}, u32[]{:S(2)}) collective-permute-start(bf16[8,2688]{1,0:T(8,128)(2,1)S(1)} %merge.12), channel_id=1, source_target_pairs={{0,12},{1,13},{2,14},{3,15},{4,8},{5,9},{6,10},{7,11},{8,4},{9,5},... | collective-permute-start | bytes 129032 | tf_op jit(solution)/shard_map/ppermute | solution.py:309
  27.6 0.1 merge.13
  27.8 0.4 %collective-permute-start.14 = (bf16[8,2688]{1,0:T(8,128)(2,1)S(1)}, bf16[8,2688]{1,0:T(8,128)(2,1)S(1)}, u32[]{:S(2)}, u32[]{:S(2)}) collective-permute-start(bf16[8,2688]{1,0:T(8,128)(2,1)S(1)} %merge.13), channel_id=1, source_target_pairs={{0,8},{1,9},{2,10},{3,11},{4,12},{5,13},{6,14},{7,15},{8,0},{9,1},... | collective-permute-start | bytes 129032 | tf_op jit(solution)/shard_map/ppermute | solution.py:309
  28.2 0.1 merge.14
  28.4 1.4 %collective-permute-start.16 = (bf16[8,2688]{1,0:T(8,128)(2,1)S(1)}, bf16[8,2688]{1,0:T(8,128)(2,1)S(1)}, u32[]{:S(2)}, u32[]{:S(2)}) collective-permute-start(bf16[8,2688]{1,0:T(8,128)(2,1)S(1)} %merge.14), channel_id=1, source_target_pairs={{0,4},{1,5},{2,6},{3,7},{4,0},{5,1},{6,2},{7,3},{8,12},{9,13},{10,... | collective-permute-start | bytes 129032 | tf_op jit(solution)/shard_map/ppermute | solution.py:309
  29.7 0.1 merge.11.refs_0_
  29.9 0.9 %collective-permute-done.12.refs_1_ = bf16[8,2688]{1,0:T(8,128)(2,1)S(1)} collective-permute-done((bf16[8,2688]{1,0:T(8,128)(2,1)S(1)}, bf16[8,2688]{1,0:T(8,128)(2,1)S(1)}, u32[]{:S(2)}, u32[]{:S(2)}) %collective-permute-start.12) | collective-permute-done | bytes 43040 | tf_op jit(solution)/shard_map/ppermute | solution.py:309
  30.7 2.1 %collective-permute-done.14.refs_2_ = bf16[8,2688]{1,0:T(8,128)(2,1)S(1)} collective-permute-done((bf16[8,2688]{1,0:T(8,128)(2,1)S(1)}, bf16[8,2688]{1,0:T(8,128)(2,1)S(1)}, u32[]{:S(2)}, u32[]{:S(2)}) %collective-permute-start.14) | collective-permute-done | bytes 43040 | tf_op jit(solution)/shard_map/ppermute | solution.py:309
  32.9 0.0 collective-permute-done.16.refs_3_
  32.9 0.9 %merge.15 = bf16[8,2560]{1,0:T(8,128)(2,1)} custom-call(f32[8,2688]{1,0:T(8,128)S(1)} %merge.11.refs_0_, bf16[8,2688]{1,0:T(8,128)(2,1)S(1)} %collective-permute-done.12.refs_1_, bf16[8,2688]{1,0:T(8,128)(2,1)S(1)} %collective-permute-done.14.refs_2_, bf16[8,2688]{1,0:T(8,128)(2,1)S(1)} %collective-permute-done.16.refs_3_), custom_call_target="tpu_custom_call" | custom-call | flops 344064 | bytes 344064 | tf_op jit(solution)/shard_map/merge/pallas_call | solution.py:286
  (13 shorter events, 0.1 us)
Async XLA Ops:
  0.0 7.4 %collective-permute-start.1 = (bf16[8,2560]{1,0:T(8,128)(2,1)}, bf16[8,2560]{1,0:T(8,128)(2,1)S(1)}, u32[]{:S(2)}, u32[]{:S(2)}) collective-permute-start(bf16[8,2560]{1,0:T(8,128)(2,1)} %refs_5_.1), channel_id=1, source_target_pairs={{12,0},{13,1},{14,2},{15,3},{8,4},{9,5},{10,6},{11,7},{4,8},{5,9},... | collective-permute-start | bytes 122888 | tf_op jit(solution)/shard_map/ppermute | solution.py:306
  5.0 4.2 %collective-permute-start = (bf16[8,2560]{1,0:T(8,128)(2,1)}, bf16[8,2560]{1,0:T(8,128)(2,1)S(1)}, u32[]{:S(2)}, u32[]{:S(2)}) collective-permute-start(bf16[8,2560]{1,0:T(8,128)(2,1)} %refs_5_.1), channel_id=1, source_target_pairs={{4,0},{5,1},{6,2},{7,3},{0,4},{1,5},{2,6},{3,7},{12,8},{13,9},{14,... | collective-permute-start | bytes 122888 | tf_op jit(solution)/shard_map/ppermute | solution.py:306
  5.1 5.7 %collective-permute-start.2 = (bf16[8,2560]{1,0:T(8,128)(2,1)}, bf16[8,2560]{1,0:T(8,128)(2,1)S(1)}, u32[]{:S(2)}, u32[]{:S(2)}) collective-permute-start(bf16[8,2560]{1,0:T(8,128)(2,1)} %refs_5_.1), channel_id=1, source_target_pairs={{8,0},{9,1},{10,2},{11,3},{12,4},{13,5},{14,6},{15,7},{0,8},{1,9},... | collective-permute-start | bytes 122888 | tf_op jit(solution)/shard_map/ppermute | solution.py:306
  5.6 8.9 %collective-permute-start.3 = (bf16[8,2560]{1,0:T(8,128)(2,1)}, bf16[8,2560]{1,0:T(8,128)(2,1)S(1)}, u32[]{:S(2)}, u32[]{:S(2)}) collective-permute-start(bf16[8,2560]{1,0:T(8,128)(2,1)} %refs_5_.1), channel_id=1, source_target_pairs={{2,0},{3,1},{0,2},{1,3},{6,4},{7,5},{4,6},{5,7},{10,8},{11,9},{8,1... | collective-permute-start | bytes 122888 | tf_op jit(solution)/shard_map/ppermute | solution.py:306
  7.4 7.2 %collective-permute-start.4 = (bf16[8,2560]{1,0:T(8,128)(2,1)S(1)}, bf16[8,2560]{1,0:T(8,128)(2,1)S(1)}, u32[]{:S(2)}, u32[]{:S(2)}) collective-permute-start(bf16[8,2560]{1,0:T(8,128)(2,1)S(1)} %collective-permute-done.1.refs_1_), channel_id=1, source_target_pairs={{2,0},{3,1},{0,2},{1,3},{6,4},{7,5},{4,6},{5,7},{10,8},{11,9},{8,1... | collective-permute-start | bytes 122888 | tf_op jit(solution)/shard_map/ppermute | solution.py:306
  9.3 5.3 %collective-permute-start.6 = (bf16[8,2560]{1,0:T(8,128)(2,1)S(1)}, bf16[8,2560]{1,0:T(8,128)(2,1)S(1)}, u32[]{:S(2)}, u32[]{:S(2)}) collective-permute-start(bf16[8,2560]{1,0:T(8,128)(2,1)S(1)} %collective-permute-done.refs_6_.refs_3_), channel_id=1, source_target_pairs={{2,0},{3,1},{0,2},{1,3},{6,4},{7,5},{4,6},{5,7},{10,8},{11,9},{8,1... | collective-permute-start | bytes 122888 | tf_op jit(solution)/shard_map/ppermute | solution.py:306
  10.8 4.0 %collective-permute-start.5 = (bf16[8,2560]{1,0:T(8,128)(2,1)S(1)}, bf16[8,2560]{1,0:T(8,128)(2,1)S(1)}, u32[]{:S(2)}, u32[]{:S(2)}) collective-permute-start(bf16[8,2560]{1,0:T(8,128)(2,1)S(1)} %collective-permute-done.2.refs_2_), channel_id=1, source_target_pairs={{2,0},{3,1},{0,2},{1,3},{6,4},{7,5},{4,6},{5,7},{10,8},{11,9},{8,1... | collective-permute-start | bytes 122888 | tf_op jit(solution)/shard_map/ppermute | solution.py:306
  14.8 1.8 %collective-permute-start.7 = (bf16[64,2560]{1,0:T(8,128)(2,1)S(1)}, bf16[64,2560]{1,0:T(8,128)(2,1)S(1)}, u32[]{:S(2)}, u32[]{:S(2)}) collective-permute-start(bf16[64,2560]{1,0:T(8,128)(2,1)S(1)} %merge.8.refs_1_), channel_id=1, source_target_pairs={{1,0},{0,1},{3,2},{2,3},{5,4},{4,5},{7,6},{6,7},{9,8},{8,9},{11,10... | collective-permute-start | bytes 983048 | tf_op jit(solution)/shard_map/ppermute | solution.py:306
  18.4 1.6 %collective-permute-start.9 = (bf16[32,2688]{1,0:T(8,128)(2,1)S(1)}, bf16[32,2688]{1,0:T(8,128)(2,1)S(1)}, u32[]{:S(2)}, u32[]{:S(2)}) collective-permute-start(bf16[32,2688]{1,0:T(8,128)(2,1)S(1)} %get-tuple-element.29), channel_id=1, source_target_pairs={{0,1},{1,0},{2,3},{3,2},{4,5},{5,4},{6,7},{7,6},{8,9},{9,8},{10,11... | collective-permute-start | bytes 516104 | tf_op jit(solution)/shard_map/ppermute | solution.py:309
  18.9 5.5 %collective-permute-start.8 = (bf16[32,2688]{1,0:T(8,128)(2,1)S(1)}, bf16[32,2688]{1,0:T(8,128)(2,1)S(1)}, u32[]{:S(2)}, u32[]{:S(2)}) collective-permute-start(bf16[32,2688]{1,0:T(8,128)(2,1)S(1)} %get-tuple-element.26), channel_id=1, source_target_pairs={{0,1},{1,0},{2,3},{3,2},{4,5},{5,4},{6,7},{7,6},{8,9},{9,8},{10,11... | collective-permute-start | bytes 516104 | tf_op jit(solution)/shard_map/ppermute | solution.py:309
  20.3 4.4 %collective-permute-start.11 = (bf16[8,2688]{1,0:T(8,128)(2,1)S(1)}, bf16[8,2688]{1,0:T(8,128)(2,1)S(1)}, u32[]{:S(2)}, u32[]{:S(2)}) collective-permute-start(bf16[8,2688]{1,0:T(8,128)(2,1)S(1)} %get-tuple-element.32), channel_id=1, source_target_pairs={{0,2},{1,3},{2,0},{3,1},{4,6},{5,7},{6,4},{7,5},{8,10},{9,11},{10,... | collective-permute-start | bytes 129032 | tf_op jit(solution)/shard_map/ppermute | solution.py:309
  21.4 6.2 %collective-permute-start.13 = (bf16[8,2688]{1,0:T(8,128)(2,1)S(1)}, bf16[8,2688]{1,0:T(8,128)(2,1)S(1)}, u32[]{:S(2)}, u32[]{:S(2)}) collective-permute-start(bf16[8,2688]{1,0:T(8,128)(2,1)S(1)} %get-tuple-element.34), channel_id=1, source_target_pairs={{0,2},{1,3},{2,0},{3,1},{4,6},{5,7},{6,4},{7,5},{8,10},{9,11},{10,... | collective-permute-start | bytes 129032 | tf_op jit(solution)/shard_map/ppermute | solution.py:309
  22.4 5.8 %collective-permute-start.15 = (bf16[8,2688]{1,0:T(8,128)(2,1)S(1)}, bf16[8,2688]{1,0:T(8,128)(2,1)S(1)}, u32[]{:S(2)}, u32[]{:S(2)}) collective-permute-start(bf16[8,2688]{1,0:T(8,128)(2,1)S(1)} %get-tuple-element.36), channel_id=1, source_target_pairs={{0,2},{1,3},{2,0},{3,1},{4,6},{5,7},{6,4},{7,5},{8,10},{9,11},{10,... | collective-permute-start | bytes 129032 | tf_op jit(solution)/shard_map/ppermute | solution.py:309
  23.5 6.3 %collective-permute-start.10 = (bf16[8,2688]{1,0:T(8,128)(2,1)S(1)}, bf16[8,2688]{1,0:T(8,128)(2,1)S(1)}, u32[]{:S(2)}, u32[]{:S(2)}) collective-permute-start(bf16[8,2688]{1,0:T(8,128)(2,1)S(1)} %get-tuple-element.30), channel_id=1, source_target_pairs={{0,2},{1,3},{2,0},{3,1},{4,6},{5,7},{6,4},{7,5},{8,10},{9,11},{10,... | collective-permute-start | bytes 129032 | tf_op jit(solution)/shard_map/ppermute | solution.py:309
  24.9 5.9 %collective-permute-start.12 = (bf16[8,2688]{1,0:T(8,128)(2,1)S(1)}, bf16[8,2688]{1,0:T(8,128)(2,1)S(1)}, u32[]{:S(2)}, u32[]{:S(2)}) collective-permute-start(bf16[8,2688]{1,0:T(8,128)(2,1)S(1)} %merge.12), channel_id=1, source_target_pairs={{0,12},{1,13},{2,14},{3,15},{4,8},{5,9},{6,10},{7,11},{8,4},{9,5},... | collective-permute-start | bytes 129032 | tf_op jit(solution)/shard_map/ppermute | solution.py:309
  27.8 5.1 %collective-permute-start.14 = (bf16[8,2688]{1,0:T(8,128)(2,1)S(1)}, bf16[8,2688]{1,0:T(8,128)(2,1)S(1)}, u32[]{:S(2)}, u32[]{:S(2)}) collective-permute-start(bf16[8,2688]{1,0:T(8,128)(2,1)S(1)} %merge.13), channel_id=1, source_target_pairs={{0,8},{1,9},{2,10},{3,11},{4,12},{5,13},{6,14},{7,15},{8,0},{9,1},... | collective-permute-start | bytes 129032 | tf_op jit(solution)/shard_map/ppermute | solution.py:309
  28.4 4.6 %collective-permute-start.16 = (bf16[8,2688]{1,0:T(8,128)(2,1)S(1)}, bf16[8,2688]{1,0:T(8,128)(2,1)S(1)}, u32[]{:S(2)}, u32[]{:S(2)}) collective-permute-start(bf16[8,2688]{1,0:T(8,128)(2,1)S(1)} %merge.14), channel_id=1, source_target_pairs={{0,4},{1,5},{2,6},{3,7},{4,0},{5,1},{6,2},{7,3},{8,12},{9,13},{10,... | collective-permute-start | bytes 129032 | tf_op jit(solution)/shard_map/ppermute | solution.py:309

commit v16 on v15

--- a/solution.py
+++ b/solution.py
@@ -245,17 +245,17 @@
     return lambda cols: ref[(*index, slice(None), cols)].astype(F32)
 
 
-def merge_rows(ins, heads, pieces, kinds):
-    rows, width = ins[0].shape
-    per = rows // pieces
-
-    def body(*refs):
-        outs = refs[len(ins) :]
+def merge_rows(ins, heads, cuts, after=()):
+    width = ins[0].shape[1]
+    starts = [sum(n for n, _ in cuts[:j]) for j in range(len(cuts))]
+
+    def body(*refs):
         for cols, total in merged([getter(r) for r in refs[: len(ins)]], heads, False):
-            for j, out in enumerate(outs):
-                out[:, cols] = total[j * per : (j + 1) * per].astype(out.dtype)
-
-    return call_merge(body, ins, [jax.ShapeDtypeStruct((per, width), kind) for kind in kinds])
+            for (n, _), start, out in zip(cuts, starts, refs[len(ins) + len(after) :]):
+                out[:, cols] = total[start : start + n].astype(out.dtype)
+
+    shapes = [jax.ShapeDtypeStruct((n, width), kind) for n, kind in cuts]
+    return call_merge(body, ins, shapes, after)
 
 
 def finish(ins, heads):
@@ -301,6 +301,7 @@
     a_n, b_n, c_n = shape
     heads = queries.shape[1] // HD
     tok = queries.shape[0]
+    tok = queries.shape[0]
 
     def fetch(x, *by):
         return lax.ppermute(x, "seq", partner_perm(shape, by, False))
@@ -308,11 +309,11 @@
     def give(x, *by):
         return lax.ppermute(x, "seq", partner_perm(shape, by, True))
 
-    far_first = [0, *range(a_n - 1, 0, -1)]
-    line = [queries] + [fetch(queries, a, 0, 0) for a in far_first[1:]]
+    order = [*range(a_n - 1, -1, -1)]
+    line = [fetch(queries, a, 0, 0) for a in order[:-1]] + [queries]
     lines = [line] + [[fetch(x, 0, b, 0) for x in line] for b in range(1, b_n)]
-    keys, values, bias, line[0] = load(
-        (cache_keys, cache_values), (new_keys, new_values), victims[None], queries, line[-1]
+    keys, values, bias, line[-1] = load(
+        (cache_keys, cache_values), (new_keys, new_values), victims[None], queries, line[min(2, a_n - 1)]
     )
     plane = join([x for pieces in lines for x in pieces])
     planes = [plane] + [fetch(plane, 0, 0, c) for c in range(1, c_n)]
@@ -320,17 +321,23 @@
     for c, rows in enumerate(planes):
         sums += attend(rows, b_n, BF16 if c else F32, keys, values, bias, sums[:1])
 
-    def over_cores(b, kind):
+    def over_cores(b, cuts, kind):
         got = [give(sums[c * b_n + b], 0, 0, c) for c in range(1, c_n)]
-        return merge_rows([sums[b]] + got, heads, a_n, [kind] * a_n)
-
-    got = [[give(x, 0, b, 0) for x in over_cores(b, BF16)] for b in range(1, b_n)]
-    own = over_cores(0, F32)
-    total = [[own[s]] + [pieces[s] for pieces in got] for s in range(a_n)]
-    last = [
-        give(merge_rows(total[s], heads, 1, [BF16])[0], far_first[s], 0, 0) for s in range(1, a_n)
-    ]
-    return finish([*merge_rows(total[0], heads, 1, [F32]), *last], heads)
+        return merge_rows([sums[b]] + got, heads, [(n * tok, kind) for n in cuts])
+
+    cuts = [2] * ((a_n - 2) // 2) + [1] * (a_n - max(a_n - 2, 0) // 2 * 2)
+    got = [over_cores(b, cuts, BF16) for b in range(1, b_n)]
+    got = [[give(x, 0, b, 0) for x in runs] for b, runs in enumerate(got, 1)]
+    own = over_cores(0, cuts, F32)
+    sent, first = [], ()
+    for i, size in enumerate(cuts):
+        slots = order[sum(cuts[:i]) :][:size]
+        kinds = [(tok, BF16 if a else F32) for a in slots]
+        pieces = merge_rows([own[i]] + [runs[i] for runs in got], heads, kinds, first)
+        first = pieces[:1] if not first else first
+        sent += [give(x, a, 0, 0) for x, a in zip(pieces, slots) if a]
+    far, near = sent[:-1], sent[-1:]
+    return finish([*merge_rows([pieces[-1], *far], heads, [(tok, F32)]), *near], heads)
 
 
 def solution(mesh):

time: 34 us -> 35.2 us (1.035)
  waiting for transfers between devices: 4.52 us -> 7.09 us
  starting transfers between devices: 21 us -> 19.6 us
    ppermute x9 -> x8, waiting for transfers between devices: 4 us -> 6.58 us  [give(): return lax.ppermute(x, 'seq', partner_perm(shape, by, True))]
    ppermute x9 -> x8, starting transfers between devices: 9.36 us -> 7.96 us  [give(): return lax.ppermute(x, 'seq', partner_perm(shape, by, True))]
  transfers between devices with their start and end apart: 17 -> 16, of which waited for: 5 -> 7; matrix products, arithmetic and copies ran while one was open for 0% -> 0% of each run, Pallas kernels for 16% -> 16%
where the time goes in v16:
time: 35.2 us; the launch traced here: 35 us
  starting transfers between devices  19.6 us (56%)
  Pallas kernels  8.19 us (23%)
  waiting for transfers between devices  7.09 us (20%)
    ppermute x8, starting transfers between devices, fetch(): return lax.ppermute(x, 'seq', partner_perm(shape, by, False))  11.7 us
    ppermute x8, starting transfers between devices, give(): return lax.ppermute(x, 'seq', partner_perm(shape, by, True))  7.96 us
    ppermute x8, waiting for transfers between devices, give(): return lax.ppermute(x, 'seq', partner_perm(shape, by, True))  6.58 us
    pallas_call x2, Pallas kernels, attend(): pl.pallas_call(body, in_specs=[pl.BlockSpec(memory_space=pltpu.VMEM)] * 4...  3.46 us
    pallas_call x1, Pallas kernels, load(): pl.pallas_call(body, in_specs=[in_hbm] * len(held) + [pl.BlockSpec(memory...  2.65 us
    pallas_call x8, Pallas kernels, call_merge(): pl.pallas_call(body, in_specs=[pl.BlockSpec(memory_space=pltpu.VMEM)] * l...  2.08 us
  transfers between devices with their start and end apart: 16, of which 7 were waited for; matrix products, arithmetic and copies ran while one was open for 0% of the time, Pallas kernels for 16%

profile of v16, /device:TPU:0, one launch (start us, length us, event | category | flops | bytes accessed | tf_op | source)
XLA Modules:
  0.0 35.0 jit_solution(11121924928357003161)
XLA Ops:
  0.0 5.0 %collective-permute-start.1 = (bf16[8,2560]{1,0:T(8,128)(2,1)}, bf16[8,2560]{1,0:T(8,128)(2,1)S(1)}, u32[]{:S(2)}, u32[]{:S(2)}) collective-permute-start(bf16[8,2560]{1,0:T(8,128)(2,1)} %refs_5_.1), channel_id=1, source_target_pairs={{12,0},{13,1},{14,2},{15,3},{8,4},{9,5},{10,6},{11,7},{4,8},{5,9},... | collective-permute-start | bytes 122888 | tf_op jit(solution)/shard_map/ppermute | solution.py:307
  5.1 0.6 %collective-permute-start.2 = (bf16[8,2560]{1,0:T(8,128)(2,1)}, bf16[8,2560]{1,0:T(8,128)(2,1)S(1)}, u32[]{:S(2)}, u32[]{:S(2)}) collective-permute-start(bf16[8,2560]{1,0:T(8,128)(2,1)} %refs_5_.1), channel_id=1, source_target_pairs={{8,0},{9,1},{10,2},{11,3},{12,4},{13,5},{14,6},{15,7},{0,8},{1,9},... | collective-permute-start | bytes 122888 | tf_op jit(solution)/shard_map/ppermute | solution.py:307
  5.6 1.8 %collective-permute-start.6 = (bf16[8,2560]{1,0:T(8,128)(2,1)}, bf16[8,2560]{1,0:T(8,128)(2,1)S(1)}, u32[]{:S(2)}, u32[]{:S(2)}) collective-permute-start(bf16[8,2560]{1,0:T(8,128)(2,1)} %refs_5_.1), channel_id=1, source_target_pairs={{2,0},{3,1},{0,2},{1,3},{6,4},{7,5},{4,6},{5,7},{10,8},{11,9},{8,1... | collective-permute-start | bytes 122888 | tf_op jit(solution)/shard_map/ppermute | solution.py:307
  7.4 1.6 %collective-permute-start.3 = (bf16[8,2560]{1,0:T(8,128)(2,1)S(1)}, bf16[8,2560]{1,0:T(8,128)(2,1)S(1)}, u32[]{:S(2)}, u32[]{:S(2)}) collective-permute-start(bf16[8,2560]{1,0:T(8,128)(2,1)S(1)} %collective-permute-done.1.refs_0_), channel_id=1, source_target_pairs={{2,0},{3,1},{0,2},{1,3},{6,4},{7,5},{4,6},{5,7},{10,8},{11,9},{8,1... | collective-permute-start | bytes 122888 | tf_op jit(solution)/shard_map/ppermute | solution.py:307
  9.0 0.3 collective-permute-done.refs_6_.refs_2_
  9.3 1.5 %collective-permute-start.5 = (bf16[8,2560]{1,0:T(8,128)(2,1)S(1)}, bf16[8,2560]{1,0:T(8,128)(2,1)S(1)}, u32[]{:S(2)}, u32[]{:S(2)}) collective-permute-start(bf16[8,2560]{1,0:T(8,128)(2,1)S(1)} %collective-permute-done.refs_6_.refs_2_), channel_id=1, source_target_pairs={{2,0},{3,1},{0,2},{1,3},{6,4},{7,5},{4,6},{5,7},{10,8},{11,9},{8,1... | collective-permute-start | bytes 122888 | tf_op jit(solution)/shard_map/ppermute | solution.py:307
  10.8 1.1 %collective-permute-start.4 = (bf16[8,2560]{1,0:T(8,128)(2,1)S(1)}, bf16[8,2560]{1,0:T(8,128)(2,1)S(1)}, u32[]{:S(2)}, u32[]{:S(2)}) collective-permute-start(bf16[8,2560]{1,0:T(8,128)(2,1)S(1)} %collective-permute-done.2.refs_1_), channel_id=1, source_target_pairs={{2,0},{3,1},{0,2},{1,3},{6,4},{7,5},{4,6},{5,7},{10,8},{11,9},{8,1... | collective-permute-start | bytes 122888 | tf_op jit(solution)/shard_map/ppermute | solution.py:307
  11.9 2.6 %load.1 = (bf16[528,2560]{1,0:T(8,128)(2,1)S(1)}, bf16[528,2560]{1,0:T(8,128)(2,1)S(1)}, f32[528,128]{1,0:T(8,128)S(1)}, bf16[8,2560]{1,0:T(8,128)(2,1)S(1)}) custom-call(bf16[512,2560]{1,0:T(8,128)(2,1)} %refs_0_.1, bf16[512,2560]{1,0:T(8,128)(2,1)} %refs_1_.1, bf16[8,2560]{1,0:T(8,128)(2,1)} %refs_2_.1, bf16[8,2560]{1,0:T(8,128)(2,1)} %refs_3_.1, ...), custom_call_target="tpu_custom_call" | custom-call | bytes 10485760 | tf_op jit(solution)/shard_map/load/pallas_call | solution.py:210
  14.6 0.2 collective-permute-done.4.refs_5_
  14.8 0.1 collective-permute-start.7
  14.9 1.7 %attend.2 = (f32[32,2688]{1,0:T(8,128)S(1)}, f32[32,2688]{1,0:T(8,128)S(1)}) custom-call(f32[528,128]{1,0:T(8,128)S(1)} %get-tuple-element.21.refs_0_, bf16[64,2560]{1,0:T(8,128)(2,1)S(1)} %merge.8.refs_1_, bf16[528,2560]{1,0:T(8,128)(2,1)S(1)} %get-tuple-element.23.refs_2_, bf16[528,2560]{1,0:T(8,128)(2,1)S(1)} %get-tuple-element.24.refs_3_), custom_call_target="tpu_custom_call" | custom-call | flops 346030080 | bytes 5406720 | tf_op jit(solution)/shard_map/attend/pallas_call | solution.py:149
  16.6 1.7 %attend.3 = (bf16[32,2688]{1,0:T(8,128)(2,1)S(1)}, bf16[32,2688]{1,0:T(8,128)(2,1)S(1)}) custom-call(f32[528,128]{1,0:T(8,128)S(1)} %get-tuple-element.21.refs_0_, bf16[64,2560]{1,0:T(8,128)(2,1)S(1)} %collective-permute-done.7.refs_1_, bf16[528,2560]{1,0:T(8,128)(2,1)S(1)} %get-tuple-element.23.refs_2_, bf16[528,2560]{1,0:T(8,128)(2,1)S(1)} %get-tuple-element.24.refs_3_, ...), custom_call_target="tpu_custom_call" | custom-call | flops 346030080 | bytes 5406720 | tf_op jit(solution)/shard_map/attend/pallas_call | solution.py:149
  18.4 0.6 %collective-permute-start.9 = (bf16[32,2688]{1,0:T(8,128)(2,1)S(1)}, bf16[32,2688]{1,0:T(8,128)(2,1)S(1)}, u32[]{:S(2)}, u32[]{:S(2)}) collective-permute-start(bf16[32,2688]{1,0:T(8,128)(2,1)S(1)} %get-tuple-element.29), channel_id=1, source_target_pairs={{0,1},{1,0},{2,3},{3,2},{4,5},{5,4},{6,7},{7,6},{8,9},{9,8},{10,11... | collective-permute-start | bytes 516104 | tf_op jit(solution)/shard_map/ppermute | solution.py:310
  18.9 0.1 collective-permute-start.8
  19.0 1.0 %collective-permute-done.9.refs_1_ = bf16[32,2688]{1,0:T(8,128)(2,1)S(1)} collective-permute-done((bf16[32,2688]{1,0:T(8,128)(2,1)S(1)}, bf16[32,2688]{1,0:T(8,128)(2,1)S(1)}, u32[]{:S(2)}, u32[]{:S(2)}) %collective-permute-start.9) | collective-permute-done | bytes 172064 | tf_op jit(solution)/shard_map/ppermute | solution.py:310
  20.0 0.3 merge.10
  20.3 1.2 %collective-permute-start.11 = (bf16[16,2688]{1,0:T(8,128)(2,1)S(1)}, bf16[16,2688]{1,0:T(8,128)(2,1)S(1)}, u32[]{:S(2)}, u32[]{:S(2)}) collective-permute-start(bf16[16,2688]{1,0:T(8,128)(2,1)S(1)} %get-tuple-element.32), channel_id=1, source_target_pairs={{0,2},{1,3},{2,0},{3,1},{4,6},{5,7},{6,4},{7,5},{8,10},{9,11},{10,... | collective-permute-start | bytes 258056 | tf_op jit(solution)/shard_map/ppermute | solution.py:310
  21.4 0.9 %collective-permute-start.14 = (bf16[8,2688]{1,0:T(8,128)(2,1)S(1)}, bf16[8,2688]{1,0:T(8,128)(2,1)S(1)}, u32[]{:S(2)}, u32[]{:S(2)}) collective-permute-start(bf16[8,2688]{1,0:T(8,128)(2,1)S(1)} %get-tuple-element.36), channel_id=1, source_target_pairs={{0,2},{1,3},{2,0},{3,1},{4,6},{5,7},{6,4},{7,5},{8,10},{9,11},{10,... | collective-permute-start | bytes 129032 | tf_op jit(solution)/shard_map/ppermute | solution.py:310
  22.4 1.1 %collective-permute-start.10 = (bf16[8,2688]{1,0:T(8,128)(2,1)S(1)}, bf16[8,2688]{1,0:T(8,128)(2,1)S(1)}, u32[]{:S(2)}, u32[]{:S(2)}) collective-permute-start(bf16[8,2688]{1,0:T(8,128)(2,1)S(1)} %get-tuple-element.30), channel_id=1, source_target_pairs={{0,2},{1,3},{2,0},{3,1},{4,6},{5,7},{6,4},{7,5},{8,10},{9,11},{10,... | collective-permute-start | bytes 129032 | tf_op jit(solution)/shard_map/ppermute | solution.py:310
  23.5 0.3 merge.9
  23.8 1.9 %collective-permute-done.11.refs_1_ = bf16[16,2688]{1,0:T(8,128)(2,1)S(1)} collective-permute-done((bf16[16,2688]{1,0:T(8,128)(2,1)S(1)}, bf16[16,2688]{1,0:T(8,128)(2,1)S(1)}, u32[]{:S(2)}, u32[]{:S(2)}) %collective-permute-start.11) | collective-permute-done | bytes 86048 | tf_op jit(solution)/shard_map/ppermute | solution.py:310
  25.7 0.2 merge.11
  25.9 0.8 %collective-permute-start.13 = (bf16[8,2688]{1,0:T(8,128)(2,1)S(1)}, bf16[8,2688]{1,0:T(8,128)(2,1)S(1)}, u32[]{:S(2)}, u32[]{:S(2)}) collective-permute-start(bf16[8,2688]{1,0:T(8,128)(2,1)S(1)} %get-tuple-element.34), channel_id=1, source_target_pairs={{0,8},{1,9},{2,10},{3,11},{4,12},{5,13},{6,14},{7,15},{8,0},{9,1},... | collective-permute-start | bytes 129032 | tf_op jit(solution)/shard_map/ppermute | solution.py:310
  26.7 3.2 %collective-permute-start.12 = (bf16[8,2688]{1,0:T(8,128)(2,1)S(1)}, bf16[8,2688]{1,0:T(8,128)(2,1)S(1)}, u32[]{:S(2)}, u32[]{:S(2)}) collective-permute-start(bf16[8,2688]{1,0:T(8,128)(2,1)S(1)} %get-tuple-element.33.refs_2_), channel_id=1, source_target_pairs={{0,12},{1,13},{2,14},{3,15},{4,8},{5,9},{6,10},{7,11},{8,4},{9,5},... | collective-permute-start | bytes 129032 | tf_op jit(solution)/shard_map/ppermute | solution.py:310
  29.9 0.1 merge.14
  30.1 0.1 collective-permute-start.15
  30.2 0.1 merge.12.refs_0_
  30.3 1.1 %collective-permute-done.13.refs_2_ = bf16[8,2688]{1,0:T(8,128)(2,1)S(1)} collective-permute-done((bf16[8,2688]{1,0:T(8,128)(2,1)S(1)}, bf16[8,2688]{1,0:T(8,128)(2,1)S(1)}, u32[]{:S(2)}, u32[]{:S(2)}) %collective-permute-start.13) | collective-permute-done | bytes 43040 | tf_op jit(solution)/shard_map/ppermute | solution.py:310
  31.4 1.4 %collective-permute-done.12.refs_1_ = bf16[8,2688]{1,0:T(8,128)(2,1)S(1)} collective-permute-done((bf16[8,2688]{1,0:T(8,128)(2,1)S(1)}, bf16[8,2688]{1,0:T(8,128)(2,1)S(1)}, u32[]{:S(2)}, u32[]{:S(2)}) %collective-permute-start.12) | collective-permute-done | bytes 43040 | tf_op jit(solution)/shard_map/ppermute | solution.py:310
  32.8 0.2 merge.13.refs_0_
  33.0 1.2 %collective-permute-done.15.refs_1_ = bf16[8,2688]{1,0:T(8,128)(2,1)S(1)} collective-permute-done((bf16[8,2688]{1,0:T(8,128)(2,1)S(1)}, bf16[8,2688]{1,0:T(8,128)(2,1)S(1)}, u32[]{:S(2)}, u32[]{:S(2)}) %collective-permute-start.15) | collective-permute-done | bytes 43040 | tf_op jit(solution)/shard_map/ppermute | solution.py:310
  34.2 0.8 %merge.15 = bf16[8,2560]{1,0:T(8,128)(2,1)} custom-call(f32[8,2688]{1,0:T(8,128)S(1)} %merge.13.refs_0_, bf16[8,2688]{1,0:T(8,128)(2,1)S(1)} %collective-permute-done.15.refs_1_), custom_call_target="tpu_custom_call" | custom-call | flops 172032 | bytes 172032 | tf_op jit(solution)/shard_map/merge/pallas_call | solution.py:286
  (11 shorter events, 0.0 us)
Async XLA Ops:
  0.0 7.4 %collective-permute-start.1 = (bf16[8,2560]{1,0:T(8,128)(2,1)}, bf16[8,2560]{1,0:T(8,128)(2,1)S(1)}, u32[]{:S(2)}, u32[]{:S(2)}) collective-permute-start(bf16[8,2560]{1,0:T(8,128)(2,1)} %refs_5_.1), channel_id=1, source_target_pairs={{12,0},{13,1},{14,2},{15,3},{8,4},{9,5},{10,6},{11,7},{4,8},{5,9},... | collective-permute-start | bytes 122888 | tf_op jit(solution)/shard_map/ppermute | solution.py:307
  5.0 4.2 %collective-permute-start = (bf16[8,2560]{1,0:T(8,128)(2,1)}, bf16[8,2560]{1,0:T(8,128)(2,1)S(1)}, u32[]{:S(2)}, u32[]{:S(2)}) collective-permute-start(bf16[8,2560]{1,0:T(8,128)(2,1)} %refs_5_.1), channel_id=1, source_target_pairs={{4,0},{5,1},{6,2},{7,3},{0,4},{1,5},{2,6},{3,7},{12,8},{13,9},{14,... | collective-permute-start | bytes 122888 | tf_op jit(solution)/shard_map/ppermute | solution.py:307
  5.1 5.7 %collective-permute-start.2 = (bf16[8,2560]{1,0:T(8,128)(2,1)}, bf16[8,2560]{1,0:T(8,128)(2,1)S(1)}, u32[]{:S(2)}, u32[]{:S(2)}) collective-permute-start(bf16[8,2560]{1,0:T(8,128)(2,1)} %refs_5_.1), channel_id=1, source_target_pairs={{8,0},{9,1},{10,2},{11,3},{12,4},{13,5},{14,6},{15,7},{0,8},{1,9},... | collective-permute-start | bytes 122888 | tf_op jit(solution)/shard_map/ppermute | solution.py:307
  5.6 8.9 %collective-permute-start.6 = (bf16[8,2560]{1,0:T(8,128)(2,1)}, bf16[8,2560]{1,0:T(8,128)(2,1)S(1)}, u32[]{:S(2)}, u32[]{:S(2)}) collective-permute-start(bf16[8,2560]{1,0:T(8,128)(2,1)} %refs_5_.1), channel_id=1, source_target_pairs={{2,0},{3,1},{0,2},{1,3},{6,4},{7,5},{4,6},{5,7},{10,8},{11,9},{8,1... | collective-permute-start | bytes 122888 | tf_op jit(solution)/shard_map/ppermute | solution.py:307
  7.4 7.2 %collective-permute-start.3 = (bf16[8,2560]{1,0:T(8,128)(2,1)S(1)}, bf16[8,2560]{1,0:T(8,128)(2,1)S(1)}, u32[]{:S(2)}, u32[]{:S(2)}) collective-permute-start(bf16[8,2560]{1,0:T(8,128)(2,1)S(1)} %collective-permute-done.1.refs_0_), channel_id=1, source_target_pairs={{2,0},{3,1},{0,2},{1,3},{6,4},{7,5},{4,6},{5,7},{10,8},{11,9},{8,1... | collective-permute-start | bytes 122888 | tf_op jit(solution)/shard_map/ppermute | solution.py:307
  9.3 5.3 %collective-permute-start.5 = (bf16[8,2560]{1,0:T(8,128)(2,1)S(1)}, bf16[8,2560]{1,0:T(8,128)(2,1)S(1)}, u32[]{:S(2)}, u32[]{:S(2)}) collective-permute-start(bf16[8,2560]{1,0:T(8,128)(2,1)S(1)} %collective-permute-done.refs_6_.refs_2_), channel_id=1, source_target_pairs={{2,0},{3,1},{0,2},{1,3},{6,4},{7,5},{4,6},{5,7},{10,8},{11,9},{8,1... | collective-permute-start | bytes 122888 | tf_op jit(solution)/shard_map/ppermute | solution.py:307
  10.8 4.0 %collective-permute-start.4 = (bf16[8,2560]{1,0:T(8,128)(2,1)S(1)}, bf16[8,2560]{1,0:T(8,128)(2,1)S(1)}, u32[]{:S(2)}, u32[]{:S(2)}) collective-permute-start(bf16[8,2560]{1,0:T(8,128)(2,1)S(1)} %collective-permute-done.2.refs_1_), channel_id=1, source_target_pairs={{2,0},{3,1},{0,2},{1,3},{6,4},{7,5},{4,6},{5,7},{10,8},{11,9},{8,1... | collective-permute-start | bytes 122888 | tf_op jit(solution)/shard_map/ppermute | solution.py:307
  14.8 1.8 %collective-permute-start.7 = (bf16[64,2560]{1,0:T(8,128)(2,1)S(1)}, bf16[64,2560]{1,0:T(8,128)(2,1)S(1)}, u32[]{:S(2)}, u32[]{:S(2)}) collective-permute-start(bf16[64,2560]{1,0:T(8,128)(2,1)S(1)} %merge.8.refs_1_), channel_id=1, source_target_pairs={{1,0},{0,1},{3,2},{2,3},{5,4},{4,5},{7,6},{6,7},{9,8},{8,9},{11,10... | collective-permute-start | bytes 983048 | tf_op jit(solution)/shard_map/ppermute | solution.py:307
  18.4 1.6 %collective-permute-start.9 = (bf16[32,2688]{1,0:T(8,128)(2,1)S(1)}, bf16[32,2688]{1,0:T(8,128)(2,1)S(1)}, u32[]{:S(2)}, u32[]{:S(2)}) collective-permute-start(bf16[32,2688]{1,0:T(8,128)(2,1)S(1)} %get-tuple-element.29), channel_id=1, source_target_pairs={{0,1},{1,0},{2,3},{3,2},{4,5},{5,4},{6,7},{7,6},{8,9},{9,8},{10,11... | collective-permute-start | bytes 516104 | tf_op jit(solution)/shard_map/ppermute | solution.py:310
  18.9 4.5 %collective-permute-start.8 = (bf16[32,2688]{1,0:T(8,128)(2,1)S(1)}, bf16[32,2688]{1,0:T(8,128)(2,1)S(1)}, u32[]{:S(2)}, u32[]{:S(2)}) collective-permute-start(bf16[32,2688]{1,0:T(8,128)(2,1)S(1)} %get-tuple-element.26), channel_id=1, source_target_pairs={{0,1},{1,0},{2,3},{3,2},{4,5},{5,4},{6,7},{7,6},{8,9},{9,8},{10,11... | collective-permute-start | bytes 516104 | tf_op jit(solution)/shard_map/ppermute | solution.py:310
  20.3 5.4 %collective-permute-start.11 = (bf16[16,2688]{1,0:T(8,128)(2,1)S(1)}, bf16[16,2688]{1,0:T(8,128)(2,1)S(1)}, u32[]{:S(2)}, u32[]{:S(2)}) collective-permute-start(bf16[16,2688]{1,0:T(8,128)(2,1)S(1)} %get-tuple-element.32), channel_id=1, source_target_pairs={{0,2},{1,3},{2,0},{3,1},{4,6},{5,7},{6,4},{7,5},{8,10},{9,11},{10,... | collective-permute-start | bytes 258056 | tf_op jit(solution)/shard_map/ppermute | solution.py:310
  21.4 8.5 %collective-permute-start.14 = (bf16[8,2688]{1,0:T(8,128)(2,1)S(1)}, bf16[8,2688]{1,0:T(8,128)(2,1)S(1)}, u32[]{:S(2)}, u32[]{:S(2)}) collective-permute-start(bf16[8,2688]{1,0:T(8,128)(2,1)S(1)} %get-tuple-element.36), channel_id=1, source_target_pairs={{0,2},{1,3},{2,0},{3,1},{4,6},{5,7},{6,4},{7,5},{8,10},{9,11},{10,... | collective-permute-start | bytes 129032 | tf_op jit(solution)/shard_map/ppermute | solution.py:310
  22.4 7.8 %collective-permute-start.10 = (bf16[8,2688]{1,0:T(8,128)(2,1)S(1)}, bf16[8,2688]{1,0:T(8,128)(2,1)S(1)}, u32[]{:S(2)}, u32[]{:S(2)}) collective-permute-start(bf16[8,2688]{1,0:T(8,128)(2,1)S(1)} %get-tuple-element.30), channel_id=1, source_target_pairs={{0,2},{1,3},{2,0},{3,1},{4,6},{5,7},{6,4},{7,5},{8,10},{9,11},{10,... | collective-permute-start | bytes 129032 | tf_op jit(solution)/shard_map/ppermute | solution.py:310
  25.9 5.5 %collective-permute-start.13 = (bf16[8,2688]{1,0:T(8,128)(2,1)S(1)}, bf16[8,2688]{1,0:T(8,128)(2,1)S(1)}, u32[]{:S(2)}, u32[]{:S(2)}) collective-permute-start(bf16[8,2688]{1,0:T(8,128)(2,1)S(1)} %get-tuple-element.34), channel_id=1, source_target_pairs={{0,8},{1,9},{2,10},{3,11},{4,12},{5,13},{6,14},{7,15},{8,0},{9,1},... | collective-permute-start | bytes 129032 | tf_op jit(solution)/shard_map/ppermute | solution.py:310
  26.7 6.1 %collective-permute-start.12 = (bf16[8,2688]{1,0:T(8,128)(2,1)S(1)}, bf16[8,2688]{1,0:T(8,128)(2,1)S(1)}, u32[]{:S(2)}, u32[]{:S(2)}) collective-permute-start(bf16[8,2688]{1,0:T(8,128)(2,1)S(1)} %get-tuple-element.33.refs_2_), channel_id=1, source_target_pairs={{0,12},{1,13},{2,14},{3,15},{4,8},{5,9},{6,10},{7,11},{8,4},{9,5},... | collective-permute-start | bytes 129032 | tf_op jit(solution)/shard_map/ppermute | solution.py:310
  30.1 4.1 %collective-permute-start.15 = (bf16[8,2688]{1,0:T(8,128)(2,1)S(1)}, bf16[8,2688]{1,0:T(8,128)(2,1)S(1)}, u32[]{:S(2)}, u32[]{:S(2)}) collective-permute-start(bf16[8,2688]{1,0:T(8,128)(2,1)S(1)} %merge.14), channel_id=1, source_target_pairs={{0,4},{1,5},{2,6},{3,7},{4,0},{5,1},{6,2},{7,3},{8,12},{9,13},{10,... | collective-permute-start | bytes 129032 | tf_op jit(solution)/shard_map/ppermute | solution.py:310

commit v17 on v15

v17 whole, which is shorter than its diff:
```python
import functools
import itertools
import math

import jax
import jax.numpy as jnp
from jax import lax
from jax.experimental import pallas as pl
from jax.experimental.pallas import tpu as pltpu
from jax.sharding import PartitionSpec as P

HD = 128
BLK = 128
STAT = 128
LANE = STAT // 3
PACK = 2
NEG = -1e30
F32 = jnp.float32
BF16 = jnp.bfloat16


def factors(members):
    cores = 2 if members % 2 == 0 else 1
    chips = members // cores
    far = next(a for a in range(1, chips + 1) if chips % a == 0 and a * a >= chips)
    return far, chips // far, cores


def partner(at, by, size):
    return at ^ by if size & (size - 1) == 0 else (at + by) % size


def partner_perm(shape, by, back):
    def flat(place):
        return functools.reduce(lambda at, kn: at * kn[1] + kn[0], zip(place, shape), 0)

    places = itertools.product(*map(range, shape))
    pairs = [(flat([partner(*x) for x in zip(at, by, shape)]), flat(at)) for at in places]
    return [pair[::-1] for pair in pairs] if back else pairs


def lanes(rows):
    return lax.broadcasted_iota(jnp.int32, (rows, STAT), 1)


def pack_stats(top, mass):
    high = mass.astype(BF16).astype(F32)
    return top + pltpu.roll(high, LANE, 1) + pltpu.roll(mass - high, 2 * LANE, 1)


def unpack_stats(packed):
    used = lanes(packed.shape[0]) < LANE
    mass = pltpu.roll(packed, STAT - LANE, 1) + pltpu.roll(packed, STAT - 2 * LANE, 1)
    return jnp.where(used, packed, 0.0), jnp.where(used, mass, 0.0)


def lane_of(head):
    return head % PACK * (LANE // PACK) + head // PACK


def attend_kernel(scale, bias_ref, q_refs, k_refs, v_refs, outs, top_acc, mass_acc):
    tok = q_refs[0].shape[0]
    rows = tok * len(q_refs)
    wide = PACK * HD
    pairs = q_refs[0].shape[1] // wide
    contract_last = (((1,), (1,)), ((), ()))
    contract_first = (((0,), (0,)), ((), ()))
    mine = [lax.broadcasted_iota(jnp.int32, (rows, wide), 1) // HD == k for k in range(PACK)]
    starts = [sum(r.shape[0] for r in k_refs[:j]) for j in range(len(k_refs))]
    top_acc[...] = jnp.zeros_like(top_acc)
    mass_acc[...] = jnp.zeros_like(mass_acc)

    def scores(i):
        cols = slice(i * wide, (i + 1) * wide)
        q = jnp.concatenate([ref[:, cols].astype(F32) for ref in q_refs], axis=0)
        q = jnp.concatenate([jnp.where(m, q, 0.0) for m in mine], axis=0).astype(BF16)
        return [
            lax.dot_general(k[:, cols], q, contract_last, preferred_element_type=F32) for k in k_refs
        ]

    def weigh(i, parts):
        masked = []
        for start, score in zip(starts, parts):
            bias = bias_ref[start : start + score.shape[0], :]
            bias = jnp.concatenate([bias] * (PACK * rows // STAT), axis=1)
            masked.append(score * scale + bias)
        tops = [jnp.max(score, axis=0, keepdims=True) for score in masked]
        top = functools.reduce(jnp.maximum, tops).astype(BF16).astype(F32)
        parts = [jnp.exp2(score - top) for score in masked]
        masses = [jnp.sum(part, axis=0, keepdims=True) for part in parts]
        top_acc[i : i + 1, :] = top
        mass_acc[i : i + 1, :] = functools.reduce(jnp.add, masses)
        return [part.astype(BF16) for part in parts]

    def gather_values(i, weights):
        cols = slice(i * wide, (i + 1) * wide)
        both = functools.reduce(
            jnp.add,
            [
                lax.dot_general(w, v[:, cols], contract_first, preferred_element_type=F32)
                for w, v in zip(weights, v_refs)
            ],
        )
        for k in range(PACK):
            one = both[k * rows : (k + 1) * rows, k * HD : (k + 1) * HD]
            at_head = (i * PACK + k) * HD
            for p, o_ref in enumerate(outs):
                o_ref[:, at_head : at_head + HD] = one[p * tok : (p + 1) * tok].astype(o_ref.dtype)

    ahead = [scores(i) for i in range(min(2, pairs))]
    weights = None
    for i in range(pairs):
        if i + 2 < pairs:
            ahead.append(scores(i + 2))
        done, weights = weights, weigh(i, ahead[i])
        if i > 0:
            gather_values(i - 1, done)
    gather_values(pairs - 1, weights)

    tops, masses = top_acc[...].T, mass_acc[...].T
    packed = 0.0
    for k in range(PACK):
        part = slice(k * rows, (k + 1) * rows)
        stats = pack_stats(tops[part], masses[part])
        packed += pltpu.roll(stats, k * (LANE // PACK), 1) if k else stats
    for p, o_ref in enumerate(outs):
        width = o_ref.shape[1]
        o_ref[:, width - STAT :] = packed[p * tok : (p + 1) * tok].astype(o_ref.dtype)


def attend(blocks, kinds, keys, values, bias):
    n, m = len(blocks), len(keys)
    tok, columns = blocks[0].shape
    total = sum(k.shape[0] for k in keys)

    def body(*refs):
        bias_ref, refs = refs[0], refs[1:]
        attend_kernel(
            math.log2(math.e) / math.sqrt(HD), bias_ref, refs[:n], refs[n : n + m],
            refs[n + m : n + 2 * m], refs[n + 2 * m : 2 * n + 2 * m], *refs[2 * n + 2 * m :],
        )

    return pl.pallas_call(
        body,
        in_specs=[pl.BlockSpec(memory_space=pltpu.VMEM)] * (1 + n + 2 * m),
        out_specs=[pl.BlockSpec(memory_space=pltpu.VMEM)] * n,
        out_shape=[jax.ShapeDtypeStruct((tok, columns + STAT), kind) for kind in kinds],
        scratch_shapes=[pltpu.VMEM((STAT, PACK * tok * n), F32)] * 2,
        compiler_params=pltpu.CompilerParams(vmem_limit_bytes=32 * 1024 * 1024),
        cost_estimate=pl.CostEstimate(
            flops=4 * n * tok * total * columns,
            bytes_accessed=4 * total * columns,
            transcendentals=n * tok * total * columns // HD,
        ),
        name="attend",
    )(bias, *blocks, *keys, *values)


def load(cached, fresh, victims, queries, cores, after):
    cache_rows, columns = cached[0].shape
    tok = queries.shape[0]
    fresh_rows = tok * len(fresh[0])
    padded = cache_rows + -(-fresh_rows // 16) * 16
    mask_rows = padded + (cores - 1) * cache_rows
    blocks = cache_rows // BLK
    n, m = len(cached), len(fresh[0])
    flat = [x for parts in fresh for x in parts]

    def body(*refs):
        cached_refs, fresh_refs = refs[:n], refs[n : n + n * m]
        victims_ref, queries_ref = refs[n + n * m : n + n * m + 2]
        refs = refs[n + n * m + 3 :]
        outs, bias_ref, q_ref, refs = refs[:n], refs[n], refs[n + 1], refs[n + 2 :]
        tails, ids_ref, sems = refs[: n * m], refs[n * m], refs[n * m + 1]
        ids = pltpu.make_async_copy(victims_ref, ids_ref, sems.at[n * m + n])
        rest = pltpu.make_async_copy(queries_ref, q_ref, sems.at[n * m + n + 1])
        small = [
            pltpu.make_async_copy(src, dst, sems.at[i])
            for i, (src, dst) in enumerate(zip(fresh_refs, tails))
        ]
        large = [
            pltpu.make_async_copy(src, dst.at[pl.ds(0, cache_rows), :], sems.at[n * m + i])
            for i, (src, dst) in enumerate(zip(cached_refs, outs))
        ]
        for copy in [ids] + small + large + [rest]:
            copy.start()
        ids.wait()
        me = lax.axis_index("seq")
        core = lax.rem(me, cores)

        def mask(first, start):
            for block in range(blocks):
                hits = jnp.where(ids_ref[...] == first + block, 1.0, 0.0)
                hit = jnp.max(hits, axis=1, keepdims=True)
                gone = jnp.where(hit > 0.0, NEG, 0.0)
                at = start + block * BLK
                bias_ref[at : at + BLK, :] = jnp.broadcast_to(gone, (BLK, STAT))

        mask(me * blocks, 0)
        token = lax.broadcasted_iota(jnp.int32, (padded - cache_rows, STAT), 0)
        bias_ref[cache_rows:padded, :] = jnp.where(token < fresh_rows, 0.0, NEG)
        for c in range(1, cores):
            other = me - core + lax.rem(core + c, cores)
            mask(other * blocks, padded + (c - 1) * cache_rows)
        for copy in small:
            copy.wait()
        for i, out in enumerate(outs):
            rows = [t[...].astype(F32) for t in tails[i * m : (i + 1) * m]]
            if padded - cache_rows > fresh_rows:
                rows.append(jnp.zeros((padded - cache_rows - fresh_rows, columns), F32))
            out[cache_rows:, :] = jnp.concatenate(rows, axis=0).astype(out.dtype)
        for copy in large + [rest]:
            copy.wait()

    hbm = lambda x: pltpu.with_memory_space_constraint(x, pltpu.HBM)
    in_hbm = pl.BlockSpec(memory_space=pltpu.HBM)
    anywhere = pl.BlockSpec(memory_space=pl.ANY)
    return pl.pallas_call(
        body,
        in_specs=[in_hbm] * n
        + [in_hbm if i % m == 0 else anywhere for i in range(n * m)]
        + [in_hbm] * 2
        + [anywhere],
        out_specs=[pl.BlockSpec(memory_space=pltpu.VMEM)] * (n + 2),
        out_shape=[jax.ShapeDtypeStruct((padded, columns), BF16)] * n
        + [jax.ShapeDtypeStruct((mask_rows, STAT), F32), jax.ShapeDtypeStruct(queries.shape, BF16)],
        scratch_shapes=[pltpu.VMEM(queries.shape, BF16)] * (n * m)
        + [pltpu.VMEM(victims.shape, jnp.int32), pltpu.SemaphoreType.DMA((n * m + n + 2,))],
        compiler_params=pltpu.CompilerParams(vmem_limit_bytes=16 * 1024 * 1024),
        cost_estimate=pl.CostEstimate(
            flops=0, bytes_accessed=4 * n * cache_rows * columns, transcendentals=0
        ),
        name="load",
    )(
        *[hbm(x) for x in cached],
        *[hbm(x) if i % m == 0 else x for i, x in enumerate(flat)],
        hbm(victims), hbm(queries), after,
    )


def merged(arrays, heads, last):
    columns = heads * HD
    stats = [unpack_stats(get(slice(columns, columns + STAT))) for get in arrays]
    top = functools.reduce(jnp.maximum, [t for t, _ in stats])
    weights = [jnp.exp2(t - top) for t, _ in stats]
    mass = functools.reduce(jnp.add, [w * m for w, (_, m) in zip(weights, stats)])
    if last:
        inverse = 1.0 / jnp.where(mass > 0.0, mass, 1.0)
        weights = [w * inverse for w in weights]
    for head in range(heads):
        cols = slice(head * HD, (head + 1) * HD)
        yield cols, functools.reduce(
            jnp.add, [get(cols) * w[:, lane_of(head) : lane_of(head) + 1] for get, w in zip(arrays, weights)]
        )
    if not last:
        yield slice(columns, columns + STAT), pack_stats(top, mass)


def getter(ref, *index):
    return lambda cols: ref[(*index, slice(None), cols)].astype(F32)


def merge_rows(ins, heads, pieces, kinds):
    rows, width = ins[0].shape
    per = rows // pieces

    def body(*refs):
        outs = refs[len(ins) :]
        for cols, total in merged([getter(r) for r in refs[: len(ins)]], heads, False):
            for j, out in enumerate(outs):
                out[:, cols] = total[j * per : (j + 1) * per].astype(out.dtype)

    return call_merge(body, ins, [jax.ShapeDtypeStruct((per, width), kind) for kind in kinds])


def finish(ins, heads):
    rows = ins[0].shape[0]

    def body(*refs):
        out = refs[len(ins)]
        for cols, total in merged([getter(r) for r in refs[: len(ins)]], heads, True):
            out[:, cols] = total.astype(out.dtype)

    return call_merge(body, ins, [jax.ShapeDtypeStruct((rows, heads * HD), BF16)])[0]


def join(pieces, after=()):
    rows = sum(p.shape[0] for p in pieces)

    def body(*refs):
        out = refs[-1]
        ins = [r[...].astype(F32) for r in refs[: len(pieces)]]
        out[...] = jnp.concatenate(ins, axis=0).astype(out.dtype)

    shape = jax.ShapeDtypeStruct((rows, pieces[0].shape[1]), pieces[0].dtype)
    return call_merge(body, pieces, [shape], after)[0]


def call_merge(body, ins, shapes, after=()):
    size = sum(math.prod(x.shape) for x in ins)
    return pl.pallas_call(
        body,
        in_specs=[pl.BlockSpec(memory_space=pltpu.VMEM)] * len(ins)
        + [pl.BlockSpec(memory_space=pl.ANY)] * len(after),
        out_specs=[pl.BlockSpec(memory_space=pltpu.VMEM)] * len(shapes),
        out_shape=shapes,
        compiler_params=pltpu.CompilerParams(vmem_limit_bytes=48 * 1024 * 1024),
        cost_estimate=pl.CostEstimate(flops=4 * size, bytes_accessed=4 * size, transcendentals=0),
        name="merge",
    )(*ins, *after)


def per_device(queries, new_keys, new_values, cache_keys, cache_values, victims):
    members = lax.axis_size("seq")
    shape = factors(members)
    a_n, b_n, c_n = shape
    heads = queries.shape[1] // HD
    tok = queries.shape[0]
    tok = queries.shape[0]

    def fetch(x, *by):
        return lax.ppermute(x, "seq", partner_perm(shape, by, False))

    def give(x, *by):
        return lax.ppermute(x, "seq", partner_perm(shape, by, True))

    others = [[fetch(x, 0, 0, c) for c in range(1, c_n)] for x in (cache_keys, cache_values)]
    fresh = [[x] + [fetch(x, 0, 0, c) for c in range(1, c_n)] for x in (new_keys, new_values)]

    far_first = [0, *range(a_n - 1, 0, -1)]
    line = [queries] + [fetch(queries, a, 0, 0) for a in far_first[1:]]
    lines = [line] + [[fetch(x, 0, b, 0) for x in line] for b in range(1, b_n)]
    keys, values, bias, line[0] = load(
        (cache_keys, cache_values), fresh, victims[None], queries, c_n, line[min(2, a_n - 1)]
    )
    keys, values = [keys, *others[0]], [values, *others[1]]
    at_once = next(n for n in range(b_n, 0, -1) if b_n % n == 0 and n * a_n * tok <= max(64, a_n * tok))
    sums = []
    for start in range(0, b_n, at_once):
        blocks = [x for pieces in lines[start : start + at_once] for x in pieces]
        kinds = [F32 if start * a_n + i < a_n else BF16 for i in range(len(blocks))]
        sums += attend(blocks, kinds, keys, values, bias)

    own = sums[:a_n]
    got = [[give(x, 0, b, 0) for x in sums[b * a_n : (b + 1) * a_n]] for b in range(1, b_n)]
    total = [[own[s]] + [pieces[s] for pieces in got] for s in range(a_n)]
    last = [
        give(merge_rows(total[s], heads, 1, [BF16])[0], far_first[s], 0, 0) for s in range(1, a_n)
    ]
    return finish([*merge_rows(total[0], heads, 1, [F32]), *last], heads)


def solution(mesh):
    rows = P(("groups", "seq"), None)
    return jax.shard_map(
        per_device,
        mesh=mesh,
        in_specs=(rows, rows, rows, rows, rows, P("groups")),
        out_specs=rows,
        check_vma=False,
    )
```

time: 34 us -> 39.5 us (1.16)
  starting transfers between devices: 21 us -> 25.4 us
  waiting for transfers between devices: 4.52 us -> 6.81 us
  Pallas kernels: 8.17 us -> 7.08 us
    ppermute x8 -> x11, starting transfers between devices: 11.7 us -> 16.5 us  [fetch(): return lax.ppermute(x, 'seq', partner_perm(shape, by, False))]
    ppermute x8 -> x11, waiting for transfers between devices: 0.51 us -> 3.58 us  [fetch(): return lax.ppermute(x, 'seq', partner_perm(shape, by, False))]
    ppermute x9 -> x7, waiting for transfers between devices: 4 us -> 3.24 us  [give(): return lax.ppermute(x, 'seq', partner_perm(shape, by, True))]
    pallas_call x8 -> x5, Pallas kernels: 2.06 us -> 1.47 us  [call_merge(): pl.pallas_call(body, in_specs=[pl.BlockSpec(memory_space=pltpu.VMEM)] * l...]
    pallas_call x3 -> x2, Pallas kernels: 6.1 us -> 5.6 us  [the longest x1 2.92 us: attend(): pl.pallas_call(body, in_specs=[pl.BlockSpec(memory_space=pltpu.VMEM)] * (...]
    ppermute x9 -> x7, starting transfers between devices: 9.36 us -> 8.87 us  [give(): return lax.ppermute(x, 'seq', partner_perm(shape, by, True))]
  transfers between devices with their start and end apart: 17 -> 18, of which waited for: 5 -> 4; matrix products, arithmetic and copies ran while one was open for 0% -> 0% of each run, Pallas kernels for 16% -> 8%
where the time goes in v17:
time: 39.5 us; the launch traced here: 39.4 us
  starting transfers between devices  25.4 us (64%)
  Pallas kernels  7.08 us (18%)
  waiting for transfers between devices  6.81 us (17%)
    ppermute x11, starting transfers between devices, fetch(): return lax.ppermute(x, 'seq', partner_perm(shape, by, False))  16.5 us
    ppermute x7, starting transfers between devices, give(): return lax.ppermute(x, 'seq', partner_perm(shape, by, True))  8.87 us
    ppermute x11, waiting for transfers between devices, fetch(): return lax.ppermute(x, 'seq', partner_perm(shape, by, False))  3.58 us
    ppermute x7, waiting for transfers between devices, give(): return lax.ppermute(x, 'seq', partner_perm(shape, by, True))  3.24 us
    pallas_call x1, Pallas kernels, attend(): pl.pallas_call(body, in_specs=[pl.BlockSpec(memory_space=pltpu.VMEM)] * (...  2.92 us
    pallas_call x1, Pallas kernels, load(): pl.pallas_call(body, in_specs=[in_hbm] * n + [in_hbm if i % m == 0 else a...  2.69 us
    pallas_call x5, Pallas kernels, call_merge(): pl.pallas_call(body, in_specs=[pl.BlockSpec(memory_space=pltpu.VMEM)] * l...  1.47 us
  transfers between devices with their start and end apart: 18, of which 4 were waited for; matrix products, arithmetic and copies ran while one was open for 0% of the time, Pallas kernels for 8%

profile of v17, /device:TPU:0, one launch (start us, length us, event | category | flops | bytes accessed | tf_op | source)
XLA Modules:
  0.0 39.4 jit_solution(7625632772958843970)
XLA Ops:
  0.0 0.5 %collective-permute-start.9 = (bf16[512,2560]{1,0:T(8,128)(2,1)}, bf16[512,2560]{1,0:T(8,128)(2,1)S(1)}, u32[]{:S(2)}, u32[]{:S(2)}) collective-permute-start(bf16[512,2560]{1,0:T(8,128)(2,1)} %refs_0_.1), channel_id=1, source_target_pairs={{1,0},{0,1},{3,2},{2,3},{5,4},{4,5},{7,6},{6,7},{9,8},{8,9},{11,10... | collective-permute-start | bytes 7864328 | tf_op jit(solution)/shard_map/ppermute | solution.py:322
  0.5 0.1 collective-permute-start.10
  0.5 0.5 %collective-permute-start = (bf16[8,2560]{1,0:T(8,128)(2,1)}, bf16[8,2560]{1,0:T(8,128)(2,1)S(1)}, u32[]{:S(2)}, u32[]{:S(2)}) collective-permute-start(bf16[8,2560]{1,0:T(8,128)(2,1)} %refs_2_.1), channel_id=1, source_target_pairs={{1,0},{0,1},{3,2},{2,3},{5,4},{4,5},{7,6},{6,7},{9,8},{8,9},{11,10... | collective-permute-start | bytes 122888 | tf_op jit(solution)/shard_map/ppermute | solution.py:322
  1.0 0.1 collective-permute-start.1
  1.0 5.0 %collective-permute-start.3 = (bf16[8,2560]{1,0:T(8,128)(2,1)}, bf16[8,2560]{1,0:T(8,128)(2,1)S(1)}, u32[]{:S(2)}, u32[]{:S(2)}) collective-permute-start(bf16[8,2560]{1,0:T(8,128)(2,1)} %refs_7_.1), channel_id=1, source_target_pairs={{12,0},{13,1},{14,2},{15,3},{8,4},{9,5},{10,6},{11,7},{4,8},{5,9},... | collective-permute-start | bytes 122888 | tf_op jit(solution)/shard_map/ppermute | solution.py:322
  6.1 2.9 %collective-permute-done.refs_3_ = bf16[8,2560]{1,0:T(8,128)(2,1)S(1)} collective-permute-done((bf16[8,2560]{1,0:T(8,128)(2,1)}, bf16[8,2560]{1,0:T(8,128)(2,1)S(1)}, u32[]{:S(2)}, u32[]{:S(2)}) %collective-permute-start) | collective-permute-done | bytes 40992 | tf_op jit(solution)/shard_map/ppermute | solution.py:322
  9.0 4.0 %collective-permute-start.2 = (bf16[8,2560]{1,0:T(8,128)(2,1)}, bf16[8,2560]{1,0:T(8,128)(2,1)S(1)}, u32[]{:S(2)}, u32[]{:S(2)}) collective-permute-start(bf16[8,2560]{1,0:T(8,128)(2,1)} %refs_7_.1), channel_id=1, source_target_pairs={{8,0},{9,1},{10,2},{11,3},{12,4},{13,5},{14,6},{15,7},{0,8},{1,9},... | collective-permute-start | bytes 122888 | tf_op jit(solution)/shard_map/ppermute | solution.py:322
  13.0 1.5 %collective-permute-start.5 = (bf16[8,2560]{1,0:T(8,128)(2,1)}, bf16[8,2560]{1,0:T(8,128)(2,1)S(1)}, u32[]{:S(2)}, u32[]{:S(2)}) collective-permute-start(bf16[8,2560]{1,0:T(8,128)(2,1)} %refs_7_.1), channel_id=1, source_target_pairs={{2,0},{3,1},{0,2},{1,3},{6,4},{7,5},{4,6},{5,7},{10,8},{11,9},{8,1... | collective-permute-start | bytes 122888 | tf_op jit(solution)/shard_map/ppermute | solution.py:322
  14.5 0.0 collective-permute-done.3.refs_2_
  14.5 1.6 %collective-permute-start.4 = (bf16[8,2560]{1,0:T(8,128)(2,1)}, bf16[8,2560]{1,0:T(8,128)(2,1)S(1)}, u32[]{:S(2)}, u32[]{:S(2)}) collective-permute-start(bf16[8,2560]{1,0:T(8,128)(2,1)} %refs_7_.1), channel_id=1, source_target_pairs={{4,0},{5,1},{6,2},{7,3},{0,4},{1,5},{2,6},{3,7},{12,8},{13,9},{14,... | collective-permute-start | bytes 122888 | tf_op jit(solution)/shard_map/ppermute | solution.py:322
  16.1 0.0 collective-permute-done.2.refs_8_.refs_3_
  16.1 1.4 %collective-permute-start.6 = (bf16[8,2560]{1,0:T(8,128)(2,1)S(1)}, bf16[8,2560]{1,0:T(8,128)(2,1)S(1)}, u32[]{:S(2)}, u32[]{:S(2)}) collective-permute-start(bf16[8,2560]{1,0:T(8,128)(2,1)S(1)} %collective-permute-done.3.refs_2_), channel_id=1, source_target_pairs={{2,0},{3,1},{0,2},{1,3},{6,4},{7,5},{4,6},{5,7},{10,8},{11,9},{8,1... | collective-permute-start | bytes 122888 | tf_op jit(solution)/shard_map/ppermute | solution.py:322
  17.5 0.0 collective-permute-done.5.refs_5_
  17.5 1.4 %collective-permute-start.7 = (bf16[8,2560]{1,0:T(8,128)(2,1)S(1)}, bf16[8,2560]{1,0:T(8,128)(2,1)S(1)}, u32[]{:S(2)}, u32[]{:S(2)}) collective-permute-start(bf16[8,2560]{1,0:T(8,128)(2,1)S(1)} %collective-permute-done.2.refs_8_.refs_3_), channel_id=1, source_target_pairs={{2,0},{3,1},{0,2},{1,3},{6,4},{7,5},{4,6},{5,7},{10,8},{11,9},{8,1... | collective-permute-start | bytes 122888 | tf_op jit(solution)/shard_map/ppermute | solution.py:322
  18.8 0.7 %collective-permute-start.8 = (bf16[8,2560]{1,0:T(8,128)(2,1)S(1)}, bf16[8,2560]{1,0:T(8,128)(2,1)S(1)}, u32[]{:S(2)}, u32[]{:S(2)}) collective-permute-start(bf16[8,2560]{1,0:T(8,128)(2,1)S(1)} %collective-permute-done.4.refs_4_), channel_id=1, source_target_pairs={{2,0},{3,1},{0,2},{1,3},{6,4},{7,5},{4,6},{5,7},{10,8},{11,9},{8,1... | collective-permute-start | bytes 122888 | tf_op jit(solution)/shard_map/ppermute | solution.py:322
  19.5 2.7 %load.1 = (bf16[528,2560]{1,0:T(8,128)(2,1)S(1)}, bf16[528,2560]{1,0:T(8,128)(2,1)S(1)}, f32[1040,128]{1,0:T(8,128)S(1)}, bf16[8,2560]{1,0:T(8,128)(2,1)S(1)}) custom-call(bf16[512,2560]{1,0:T(8,128)(2,1)} %refs_0_.1, bf16[512,2560]{1,0:T(8,128)(2,1)} %refs_1_.1, bf16[8,2560]{1,0:T(8,128)(2,1)} %refs_2_.1, bf16[8,2560]{1,0:T(8,128)(2,1)S(1)} %collective-permute-done.refs_3_, ...), custom_call_target="tpu_custom_call" | custom-call | bytes 10485760 | tf_op jit(solution)/shard_map/load/pallas_call | solution.py:218
  22.2 0.6 %collective-permute-done.8.refs_8_ = bf16[8,2560]{1,0:T(8,128)(2,1)S(1)} collective-permute-done((bf16[8,2560]{1,0:T(8,128)(2,1)S(1)}, bf16[8,2560]{1,0:T(8,128)(2,1)S(1)}, u32[]{:S(2)}, u32[]{:S(2)}) %collective-permute-start.8) | collective-permute-done | bytes 40992 | tf_op jit(solution)/shard_map/ppermute | solution.py:322
  22.8 2.9 %attend.1 = (f32[8,2688]{1,0:T(8,128)S(1)}, f32[8,2688]{1,0:T(8,128)S(1)}, f32[8,2688]{1,0:T(8,128)S(1)}, f32[8,2688]{1,0:T(8,128)S(1)}, bf16[8,2688]{1,0:T(8,12...) custom-call(f32[1040,128]{1,0:T(8,128)S(1)} %get-tuple-element.17.refs_0_, ...), custom_call_target="tpu_custom_call" | custom-call | flops 681574400 | bytes 10649600 | tf_op jit(solution)/shard_map/attend/pallas_call | solution.py:143
  25.7 0.8 %collective-permute-start.12 = (bf16[8,2688]{1,0:T(8,128)(2,1)S(1)}, bf16[8,2688]{1,0:T(8,128)(2,1)S(1)}, u32[]{:S(2)}, u32[]{:S(2)}) collective-permute-start(bf16[8,2688]{1,0:T(8,128)(2,1)S(1)} %get-tuple-element.24), channel_id=1, source_target_pairs={{0,2},{1,3},{2,0},{3,1},{4,6},{5,7},{6,4},{7,5},{8,10},{9,11},{10,... | collective-permute-start | bytes 129032 | tf_op jit(solution)/shard_map/ppermute | solution.py:325
  26.6 1.3 %collective-permute-start.14 = (bf16[8,2688]{1,0:T(8,128)(2,1)S(1)}, bf16[8,2688]{1,0:T(8,128)(2,1)S(1)}, u32[]{:S(2)}, u32[]{:S(2)}) collective-permute-start(bf16[8,2688]{1,0:T(8,128)(2,1)S(1)} %get-tuple-element.26), channel_id=1, source_target_pairs={{0,2},{1,3},{2,0},{3,1},{4,6},{5,7},{6,4},{7,5},{8,10},{9,11},{10,... | collective-permute-start | bytes 129032 | tf_op jit(solution)/shard_map/ppermute | solution.py:325
  27.8 0.8 %collective-permute-start.16 = (bf16[8,2688]{1,0:T(8,128)(2,1)S(1)}, bf16[8,2688]{1,0:T(8,128)(2,1)S(1)}, u32[]{:S(2)}, u32[]{:S(2)}) collective-permute-start(bf16[8,2688]{1,0:T(8,128)(2,1)S(1)} %get-tuple-element.28), channel_id=1, source_target_pairs={{0,2},{1,3},{2,0},{3,1},{4,6},{5,7},{6,4},{7,5},{8,10},{9,11},{10,... | collective-permute-start | bytes 129032 | tf_op jit(solution)/shard_map/ppermute | solution.py:325
  28.6 1.3 %collective-permute-start.11 = (bf16[8,2688]{1,0:T(8,128)(2,1)S(1)}, bf16[8,2688]{1,0:T(8,128)(2,1)S(1)}, u32[]{:S(2)}, u32[]{:S(2)}) collective-permute-start(bf16[8,2688]{1,0:T(8,128)(2,1)S(1)} %get-tuple-element.22), channel_id=1, source_target_pairs={{0,2},{1,3},{2,0},{3,1},{4,6},{5,7},{6,4},{7,5},{8,10},{9,11},{10,... | collective-permute-start | bytes 129032 | tf_op jit(solution)/shard_map/ppermute | solution.py:325
  29.9 0.1 merge.6
  30.0 3.3 %collective-permute-start.13 = (bf16[8,2688]{1,0:T(8,128)(2,1)S(1)}, bf16[8,2688]{1,0:T(8,128)(2,1)S(1)}, u32[]{:S(2)}, u32[]{:S(2)}) collective-permute-start(bf16[8,2688]{1,0:T(8,128)(2,1)S(1)} %merge.6), channel_id=1, source_target_pairs={{0,12},{1,13},{2,14},{3,15},{4,8},{5,9},{6,10},{7,11},{8,4},{9,5},... | collective-permute-start | bytes 129032 | tf_op jit(solution)/shard_map/ppermute | solution.py:325
  33.3 0.1 merge.7
  33.5 0.1 collective-permute-start.15
  33.6 0.1 merge.8
  33.7 1.4 %collective-permute-start.17 = (bf16[8,2688]{1,0:T(8,128)(2,1)S(1)}, bf16[8,2688]{1,0:T(8,128)(2,1)S(1)}, u32[]{:S(2)}, u32[]{:S(2)}) collective-permute-start(bf16[8,2688]{1,0:T(8,128)(2,1)S(1)} %merge.8), channel_id=1, source_target_pairs={{0,4},{1,5},{2,6},{3,7},{4,0},{5,1},{6,2},{7,3},{8,12},{9,13},{10,... | collective-permute-start | bytes 129032 | tf_op jit(solution)/shard_map/ppermute | solution.py:325
  35.1 0.1 merge.5.refs_0_
  35.2 0.9 %collective-permute-done.13.refs_1_ = bf16[8,2688]{1,0:T(8,128)(2,1)S(1)} collective-permute-done((bf16[8,2688]{1,0:T(8,128)(2,1)S(1)}, bf16[8,2688]{1,0:T(8,128)(2,1)S(1)}, u32[]{:S(2)}, u32[]{:S(2)}) %collective-permute-start.13) | collective-permute-done | bytes 43040 | tf_op jit(solution)/shard_map/ppermute | solution.py:325
  36.2 2.3 %collective-permute-done.15.refs_2_ = bf16[8,2688]{1,0:T(8,128)(2,1)S(1)} collective-permute-done((bf16[8,2688]{1,0:T(8,128)(2,1)S(1)}, bf16[8,2688]{1,0:T(8,128)(2,1)S(1)}, u32[]{:S(2)}, u32[]{:S(2)}) %collective-permute-start.15) | collective-permute-done | bytes 43040 | tf_op jit(solution)/shard_map/ppermute | solution.py:325
  38.5 0.9 %merge.9 = bf16[8,2560]{1,0:T(8,128)(2,1)} custom-call(f32[8,2688]{1,0:T(8,128)S(1)} %merge.5.refs_0_, bf16[8,2688]{1,0:T(8,128)(2,1)S(1)} %collective-permute-done.13.refs_1_, bf16[8,2688]{1,0:T(8,128)(2,1)S(1)} %collective-permute-done.15.refs_2_, bf16[8,2688]{1,0:T(8,128)(2,1)S(1)} %collective-permute-done.17.refs_3_), custom_call_target="tpu_custom_call" | custom-call | flops 344064 | bytes 344064 | tf_op jit(solution)/shard_map/merge/pallas_call | solution.py:301
  (11 shorter events, 0.0 us)
Async XLA Ops:
  0.0 22.8 %collective-permute-start.9 = (bf16[512,2560]{1,0:T(8,128)(2,1)}, bf16[512,2560]{1,0:T(8,128)(2,1)S(1)}, u32[]{:S(2)}, u32[]{:S(2)}) collective-permute-start(bf16[512,2560]{1,0:T(8,128)(2,1)} %refs_0_.1), channel_id=1, source_target_pairs={{1,0},{0,1},{3,2},{2,3},{5,4},{4,5},{7,6},{6,7},{9,8},{8,9},{11,10... | collective-permute-start | bytes 7864328 | tf_op jit(solution)/shard_map/ppermute | solution.py:322
  0.5 22.4 %collective-permute-start.10 = (bf16[512,2560]{1,0:T(8,128)(2,1)}, bf16[512,2560]{1,0:T(8,128)(2,1)S(1)}, u32[]{:S(2)}, u32[]{:S(2)}) collective-permute-start(bf16[512,2560]{1,0:T(8,128)(2,1)} %refs_1_.1), channel_id=1, source_target_pairs={{1,0},{0,1},{3,2},{2,3},{5,4},{4,5},{7,6},{6,7},{9,8},{8,9},{11,10... | collective-permute-start | bytes 7864328 | tf_op jit(solution)/shard_map/ppermute | solution.py:322
  0.5 8.5 %collective-permute-start = (bf16[8,2560]{1,0:T(8,128)(2,1)}, bf16[8,2560]{1,0:T(8,128)(2,1)S(1)}, u32[]{:S(2)}, u32[]{:S(2)}) collective-permute-start(bf16[8,2560]{1,0:T(8,128)(2,1)} %refs_2_.1), channel_id=1, source_target_pairs={{1,0},{0,1},{3,2},{2,3},{5,4},{4,5},{7,6},{6,7},{9,8},{8,9},{11,10... | collective-permute-start | bytes 122888 | tf_op jit(solution)/shard_map/ppermute | solution.py:322
  1.0 12.0 %collective-permute-start.1 = (bf16[8,2560]{1,0:T(8,128)(2,1)}, bf16[8,2560]{1,0:T(8,128)(2,1)S(1)}, u32[]{:S(2)}, u32[]{:S(2)}) collective-permute-start(bf16[8,2560]{1,0:T(8,128)(2,1)} %refs_4_.1), channel_id=1, source_target_pairs={{1,0},{0,1},{3,2},{2,3},{5,4},{4,5},{7,6},{6,7},{9,8},{8,9},{11,10... | collective-permute-start | bytes 122888 | tf_op jit(solution)/shard_map/ppermute | solution.py:322
  1.0 13.5 %collective-permute-start.3 = (bf16[8,2560]{1,0:T(8,128)(2,1)}, bf16[8,2560]{1,0:T(8,128)(2,1)S(1)}, u32[]{:S(2)}, u32[]{:S(2)}) collective-permute-start(bf16[8,2560]{1,0:T(8,128)(2,1)} %refs_7_.1), channel_id=1, source_target_pairs={{12,0},{13,1},{14,2},{15,3},{8,4},{9,5},{10,6},{11,7},{4,8},{5,9},... | collective-permute-start | bytes 122888 | tf_op jit(solution)/shard_map/ppermute | solution.py:322
  9.0 7.1 %collective-permute-start.2 = (bf16[8,2560]{1,0:T(8,128)(2,1)}, bf16[8,2560]{1,0:T(8,128)(2,1)S(1)}, u32[]{:S(2)}, u32[]{:S(2)}) collective-permute-start(bf16[8,2560]{1,0:T(8,128)(2,1)} %refs_7_.1), channel_id=1, source_target_pairs={{8,0},{9,1},{10,2},{11,3},{12,4},{13,5},{14,6},{15,7},{0,8},{1,9},... | collective-permute-start | bytes 122888 | tf_op jit(solution)/shard_map/ppermute | solution.py:322
  13.0 4.5 %collective-permute-start.5 = (bf16[8,2560]{1,0:T(8,128)(2,1)}, bf16[8,2560]{1,0:T(8,128)(2,1)S(1)}, u32[]{:S(2)}, u32[]{:S(2)}) collective-permute-start(bf16[8,2560]{1,0:T(8,128)(2,1)} %refs_7_.1), channel_id=1, source_target_pairs={{2,0},{3,1},{0,2},{1,3},{6,4},{7,5},{4,6},{5,7},{10,8},{11,9},{8,1... | collective-permute-start | bytes 122888 | tf_op jit(solution)/shard_map/ppermute | solution.py:322
  14.5 4.3 %collective-permute-start.4 = (bf16[8,2560]{1,0:T(8,128)(2,1)}, bf16[8,2560]{1,0:T(8,128)(2,1)S(1)}, u32[]{:S(2)}, u32[]{:S(2)}) collective-permute-start(bf16[8,2560]{1,0:T(8,128)(2,1)} %refs_7_.1), channel_id=1, source_target_pairs={{4,0},{5,1},{6,2},{7,3},{0,4},{1,5},{2,6},{3,7},{12,8},{13,9},{14,... | collective-permute-start | bytes 122888 | tf_op jit(solution)/shard_map/ppermute | solution.py:322
  16.1 6.1 %collective-permute-start.6 = (bf16[8,2560]{1,0:T(8,128)(2,1)S(1)}, bf16[8,2560]{1,0:T(8,128)(2,1)S(1)}, u32[]{:S(2)}, u32[]{:S(2)}) collective-permute-start(bf16[8,2560]{1,0:T(8,128)(2,1)S(1)} %collective-permute-done.3.refs_2_), channel_id=1, source_target_pairs={{2,0},{3,1},{0,2},{1,3},{6,4},{7,5},{4,6},{5,7},{10,8},{11,9},{8,1... | collective-permute-start | bytes 122888 | tf_op jit(solution)/shard_map/ppermute | solution.py:322
  17.5 4.7 %collective-permute-start.7 = (bf16[8,2560]{1,0:T(8,128)(2,1)S(1)}, bf16[8,2560]{1,0:T(8,128)(2,1)S(1)}, u32[]{:S(2)}, u32[]{:S(2)}) collective-permute-start(bf16[8,2560]{1,0:T(8,128)(2,1)S(1)} %collective-permute-done.2.refs_8_.refs_3_), channel_id=1, source_target_pairs={{2,0},{3,1},{0,2},{1,3},{6,4},{7,5},{4,6},{5,7},{10,8},{11,9},{8,1... | collective-permute-start | bytes 122888 | tf_op jit(solution)/shard_map/ppermute | solution.py:322
  18.8 4.0 %collective-permute-start.8 = (bf16[8,2560]{1,0:T(8,128)(2,1)S(1)}, bf16[8,2560]{1,0:T(8,128)(2,1)S(1)}, u32[]{:S(2)}, u32[]{:S(2)}) collective-permute-start(bf16[8,2560]{1,0:T(8,128)(2,1)S(1)} %collective-permute-done.4.refs_4_), channel_id=1, source_target_pairs={{2,0},{3,1},{0,2},{1,3},{6,4},{7,5},{4,6},{5,7},{10,8},{11,9},{8,1... | collective-permute-start | bytes 122888 | tf_op jit(solution)/shard_map/ppermute | solution.py:322
  25.7 4.1 %collective-permute-start.12 = (bf16[8,2688]{1,0:T(8,128)(2,1)S(1)}, bf16[8,2688]{1,0:T(8,128)(2,1)S(1)}, u32[]{:S(2)}, u32[]{:S(2)}) collective-permute-start(bf16[8,2688]{1,0:T(8,128)(2,1)S(1)} %get-tuple-element.24), channel_id=1, source_target_pairs={{0,2},{1,3},{2,0},{3,1},{4,6},{5,7},{6,4},{7,5},{8,10},{9,11},{10,... | collective-permute-start | bytes 129032 | tf_op jit(solution)/shard_map/ppermute | solution.py:325
  26.6 6.8 %collective-permute-start.14 = (bf16[8,2688]{1,0:T(8,128)(2,1)S(1)}, bf16[8,2688]{1,0:T(8,128)(2,1)S(1)}, u32[]{:S(2)}, u32[]{:S(2)}) collective-permute-start(bf16[8,2688]{1,0:T(8,128)(2,1)S(1)} %get-tuple-element.26), channel_id=1, source_target_pairs={{0,2},{1,3},{2,0},{3,1},{4,6},{5,7},{6,4},{7,5},{8,10},{9,11},{10,... | collective-permute-start | bytes 129032 | tf_op jit(solution)/shard_map/ppermute | solution.py:325
  27.8 5.7 %collective-permute-start.16 = (bf16[8,2688]{1,0:T(8,128)(2,1)S(1)}, bf16[8,2688]{1,0:T(8,128)(2,1)S(1)}, u32[]{:S(2)}, u32[]{:S(2)}) collective-permute-start(bf16[8,2688]{1,0:T(8,128)(2,1)S(1)} %get-tuple-element.28), channel_id=1, source_target_pairs={{0,2},{1,3},{2,0},{3,1},{4,6},{5,7},{6,4},{7,5},{8,10},{9,11},{10,... | collective-permute-start | bytes 129032 | tf_op jit(solution)/shard_map/ppermute | solution.py:325
  28.6 6.5 %collective-permute-start.11 = (bf16[8,2688]{1,0:T(8,128)(2,1)S(1)}, bf16[8,2688]{1,0:T(8,128)(2,1)S(1)}, u32[]{:S(2)}, u32[]{:S(2)}) collective-permute-start(bf16[8,2688]{1,0:T(8,128)(2,1)S(1)} %get-tuple-element.22), channel_id=1, source_target_pairs={{0,2},{1,3},{2,0},{3,1},{4,6},{5,7},{6,4},{7,5},{8,10},{9,11},{10,... | collective-permute-start | bytes 129032 | tf_op jit(solution)/shard_map/ppermute | solution.py:325
  30.0 6.1 %collective-permute-start.13 = (bf16[8,2688]{1,0:T(8,128)(2,1)S(1)}, bf16[8,2688]{1,0:T(8,128)(2,1)S(1)}, u32[]{:S(2)}, u32[]{:S(2)}) collective-permute-start(bf16[8,2688]{1,0:T(8,128)(2,1)S(1)} %merge.6), channel_id=1, source_target_pairs={{0,12},{1,13},{2,14},{3,15},{4,8},{5,9},{6,10},{7,11},{8,4},{9,5},... | collective-permute-start | bytes 129032 | tf_op jit(solution)/shard_map/ppermute | solution.py:325
  33.5 5.0 %collective-permute-start.15 = (bf16[8,2688]{1,0:T(8,128)(2,1)S(1)}, bf16[8,2688]{1,0:T(8,128)(2,1)S(1)}, u32[]{:S(2)}, u32[]{:S(2)}) collective-permute-start(bf16[8,2688]{1,0:T(8,128)(2,1)S(1)} %merge.7), channel_id=1, source_target_pairs={{0,8},{1,9},{2,10},{3,11},{4,12},{5,13},{6,14},{7,15},{8,0},{9,1},... | collective-permute-start | bytes 129032 | tf_op jit(solution)/shard_map/ppermute | solution.py:325
  33.7 4.8 %collective-permute-start.17 = (bf16[8,2688]{1,0:T(8,128)(2,1)S(1)}, bf16[8,2688]{1,0:T(8,128)(2,1)S(1)}, u32[]{:S(2)}, u32[]{:S(2)}) collective-permute-start(bf16[8,2688]{1,0:T(8,128)(2,1)S(1)} %merge.8), channel_id=1, source_target_pairs={{0,4},{1,5},{2,6},{3,7},{4,0},{5,1},{6,2},{7,3},{8,12},{9,13},{10,... | collective-permute-start | bytes 129032 | tf_op jit(solution)/shard_map/ppermute | solution.py:325

commit v18 on v17

--- a/solution.py
+++ b/solution.py
@@ -324,8 +324,9 @@
     def give(x, *by):
         return lax.ppermute(x, "seq", partner_perm(shape, by, True))
 
-    others = [[fetch(x, 0, 0, c) for c in range(1, c_n)] for x in (cache_keys, cache_values)]
     fresh = [[x] + [fetch(x, 0, 0, c) for c in range(1, c_n)] for x in (new_keys, new_values)]
+    bulk, fresh = lax.optimization_barrier(((cache_keys, cache_values), fresh))
+    others = [[fetch(x, 0, 0, c) for c in range(1, c_n)] for x in bulk]
 
     far_first = [0, *range(a_n - 1, 0, -1)]
     line = [queries] + [fetch(queries, a, 0, 0) for a in far_first[1:]]

time: 39.5 us -> 35.4 us (0.90)
  starting transfers between devices: 25.4 us -> 20.8 us
  waiting for transfers between devices: 6.81 us -> 7.32 us
    ppermute x11, starting transfers between devices: 16.5 us -> 11.6 us  [fetch(): return lax.ppermute(x, 'seq', partner_perm(shape, by, False))]
    ppermute x11, waiting for transfers between devices: 3.58 us -> 4.33 us  [fetch(): return lax.ppermute(x, 'seq', partner_perm(shape, by, False))]
  transfers between devices with their start and end apart: 18 -> 18, of which waited for: 4 -> 6; matrix products, arithmetic and copies ran while one was open for 0% -> 0% of each run, Pallas kernels for 8% -> 9%
where the time goes in v18:
time: 35.4 us; the launch traced here: 35.3 us
  starting transfers between devices  20.8 us (59%)
  waiting for transfers between devices  7.32 us (21%)
  Pallas kernels  7.08 us (20%)
    ppermute x11, starting transfers between devices, fetch(): return lax.ppermute(x, 'seq', partner_perm(shape, by, False))  11.6 us
    ppermute x7, starting transfers between devices, give(): return lax.ppermute(x, 'seq', partner_perm(shape, by, True))  9.19 us
    ppermute x11, waiting for transfers between devices, fetch(): return lax.ppermute(x, 'seq', partner_perm(shape, by, False))  4.33 us
    ppermute x7, waiting for transfers between devices, give(): return lax.ppermute(x, 'seq', partner_perm(shape, by, True))  3 us
    pallas_call x1, Pallas kernels, attend(): pl.pallas_call(body, in_specs=[pl.BlockSpec(memory_space=pltpu.VMEM)] * (...  2.92 us
    pallas_call x1, Pallas kernels, load(): pl.pallas_call(body, in_specs=[in_hbm] * n + [in_hbm if i % m == 0 else a...  2.69 us
    pallas_call x5, Pallas kernels, call_merge(): pl.pallas_call(body, in_specs=[pl.BlockSpec(memory_space=pltpu.VMEM)] * l...  1.47 us
  transfers between devices with their start and end apart: 18, of which 6 were waited for; matrix products, arithmetic and copies ran while one was open for 0% of the time, Pallas kernels for 9%

profile of v18, /device:TPU:0, one launch (start us, length us, event | category | flops | bytes accessed | tf_op | source)
XLA Modules:
  0.0 35.3 jit_solution(6886513863256130600)
XLA Ops:
  0.0 0.5 %collective-permute-start = (bf16[8,2560]{1,0:T(8,128)(2,1)}, bf16[8,2560]{1,0:T(8,128)(2,1)S(1)}, u32[]{:S(2)}, u32[]{:S(2)}) collective-permute-start(bf16[8,2560]{1,0:T(8,128)(2,1)} %refs_2_), channel_id=1, source_target_pairs={{1,0},{0,1},{3,2},{2,3},{5,4},{4,5},{7,6},{6,7},{9,8},{8,9},{11,10... | collective-permute-start | bytes 122888 | tf_op jit(solution)/shard_map/ppermute | solution.py:322
  0.5 0.1 collective-permute-start.1
  0.5 1.0 %collective-permute-done.refs_3_ = bf16[8,2560]{1,0:T(8,128)(2,1)S(1)} collective-permute-done((bf16[8,2560]{1,0:T(8,128)(2,1)}, bf16[8,2560]{1,0:T(8,128)(2,1)S(1)}, u32[]{:S(2)}, u32[]{:S(2)}) %collective-permute-start) | collective-permute-done | bytes 40992 | tf_op jit(solution)/shard_map/ppermute | solution.py:322
  1.5 0.3 collective-permute-done.1.refs_5_
  1.9 0.2 collective-permute-start.9
  2.0 0.3 collective-permute-start.10
  2.4 4.8 %collective-permute-start.3 = (bf16[8,2560]{1,0:T(8,128)(2,1)}, bf16[8,2560]{1,0:T(8,128)(2,1)S(1)}, u32[]{:S(2)}, u32[]{:S(2)}) collective-permute-start(bf16[8,2560]{1,0:T(8,128)(2,1)} %refs_7_.1), channel_id=1, source_target_pairs={{12,0},{13,1},{14,2},{15,3},{8,4},{9,5},{10,6},{11,7},{4,8},{5,9},... | collective-permute-start | bytes 122888 | tf_op jit(solution)/shard_map/ppermute | solution.py:322
  7.2 1.5 %collective-permute-start.5 = (bf16[8,2560]{1,0:T(8,128)(2,1)}, bf16[8,2560]{1,0:T(8,128)(2,1)S(1)}, u32[]{:S(2)}, u32[]{:S(2)}) collective-permute-start(bf16[8,2560]{1,0:T(8,128)(2,1)} %refs_7_.1), channel_id=1, source_target_pairs={{2,0},{3,1},{0,2},{1,3},{6,4},{7,5},{4,6},{5,7},{10,8},{11,9},{8,1... | collective-permute-start | bytes 122888 | tf_op jit(solution)/shard_map/ppermute | solution.py:322
  8.7 0.9 %collective-permute-done.3.refs_2_ = bf16[8,2560]{1,0:T(8,128)(2,1)S(1)} collective-permute-done((bf16[8,2560]{1,0:T(8,128)(2,1)}, bf16[8,2560]{1,0:T(8,128)(2,1)S(1)}, u32[]{:S(2)}, u32[]{:S(2)}) %collective-permute-start.3) | collective-permute-done | bytes 40992 | tf_op jit(solution)/shard_map/ppermute | solution.py:322
  9.5 0.7 %collective-permute-start.4 = (bf16[8,2560]{1,0:T(8,128)(2,1)}, bf16[8,2560]{1,0:T(8,128)(2,1)S(1)}, u32[]{:S(2)}, u32[]{:S(2)}) collective-permute-start(bf16[8,2560]{1,0:T(8,128)(2,1)} %refs_7_.1), channel_id=1, source_target_pairs={{4,0},{5,1},{6,2},{7,3},{0,4},{1,5},{2,6},{3,7},{12,8},{13,9},{14,... | collective-permute-start | bytes 122888 | tf_op jit(solution)/shard_map/ppermute | solution.py:322
  10.2 2.1 %collective-permute-done.2.refs_8_.refs_3_ = bf16[8,2560]{1,0:T(8,128)(2,1)S(1)} collective-permute-done((bf16[8,2560]{1,0:T(8,128)(2,1)}, bf16[8,2560]{1,0:T(8,128)(2,1)S(1)}, u32[]{:S(2)}, u32[]{:S(2)}) %collective-permute-start.2) | collective-permute-done | bytes 40992 | tf_op jit(solution)/shard_map/ppermute | solution.py:322
  12.3 1.6 %collective-permute-start.6 = (bf16[8,2560]{1,0:T(8,128)(2,1)S(1)}, bf16[8,2560]{1,0:T(8,128)(2,1)S(1)}, u32[]{:S(2)}, u32[]{:S(2)}) collective-permute-start(bf16[8,2560]{1,0:T(8,128)(2,1)S(1)} %collective-permute-done.3.refs_2_), channel_id=1, source_target_pairs={{2,0},{3,1},{0,2},{1,3},{6,4},{7,5},{4,6},{5,7},{10,8},{11,9},{8,1... | collective-permute-start | bytes 122888 | tf_op jit(solution)/shard_map/ppermute | solution.py:322
  13.9 0.4 %collective-permute-start.7 = (bf16[8,2560]{1,0:T(8,128)(2,1)S(1)}, bf16[8,2560]{1,0:T(8,128)(2,1)S(1)}, u32[]{:S(2)}, u32[]{:S(2)}) collective-permute-start(bf16[8,2560]{1,0:T(8,128)(2,1)S(1)} %collective-permute-done.2.refs_8_.refs_3_), channel_id=1, source_target_pairs={{2,0},{3,1},{0,2},{1,3},{6,4},{7,5},{4,6},{5,7},{10,8},{11,9},{8,1... | collective-permute-start | bytes 122888 | tf_op jit(solution)/shard_map/ppermute | solution.py:322
  14.3 0.0 collective-permute-done.4.refs_4_
  14.3 1.6 %collective-permute-start.8 = (bf16[8,2560]{1,0:T(8,128)(2,1)S(1)}, bf16[8,2560]{1,0:T(8,128)(2,1)S(1)}, u32[]{:S(2)}, u32[]{:S(2)}) collective-permute-start(bf16[8,2560]{1,0:T(8,128)(2,1)S(1)} %collective-permute-done.4.refs_4_), channel_id=1, source_target_pairs={{2,0},{3,1},{0,2},{1,3},{6,4},{7,5},{4,6},{5,7},{10,8},{11,9},{8,1... | collective-permute-start | bytes 122888 | tf_op jit(solution)/shard_map/ppermute | solution.py:322
  15.9 2.7 %load.1 = (bf16[528,2560]{1,0:T(8,128)(2,1)S(1)}, bf16[528,2560]{1,0:T(8,128)(2,1)S(1)}, f32[1040,128]{1,0:T(8,128)S(1)}, bf16[8,2560]{1,0:T(8,128)(2,1)S(1)}) custom-call(bf16[512,2560]{1,0:T(8,128)(2,1)} %refs_0_.1, bf16[512,2560]{1,0:T(8,128)(2,1)} %refs_1_.1, bf16[8,2560]{1,0:T(8,128)(2,1)} %refs_2_, bf16[8,2560]{1,0:T(8,128)(2,1)S(1)} %collective-permute-done.refs_3_, ...), custom_call_target="tpu_custom_call" | custom-call | bytes 10485760 | tf_op jit(solution)/shard_map/load/pallas_call | solution.py:218
  18.6 0.0 collective-permute-done.7.refs_7_
  18.7 2.9 %attend.1 = (f32[8,2688]{1,0:T(8,128)S(1)}, f32[8,2688]{1,0:T(8,128)S(1)}, f32[8,2688]{1,0:T(8,128)S(1)}, f32[8,2688]{1,0:T(8,128)S(1)}, bf16[8,2688]{1,0:T(8,12...) custom-call(f32[1040,128]{1,0:T(8,128)S(1)} %get-tuple-element.27.refs_0_, ...), custom_call_target="tpu_custom_call" | custom-call | flops 681574400 | bytes 10649600 | tf_op jit(solution)/shard_map/attend/pallas_call | solution.py:143
  21.6 1.3 %collective-permute-start.12 = (bf16[8,2688]{1,0:T(8,128)(2,1)S(1)}, bf16[8,2688]{1,0:T(8,128)(2,1)S(1)}, u32[]{:S(2)}, u32[]{:S(2)}) collective-permute-start(bf16[8,2688]{1,0:T(8,128)(2,1)S(1)} %get-tuple-element.36), channel_id=1, source_target_pairs={{0,2},{1,3},{2,0},{3,1},{4,6},{5,7},{6,4},{7,5},{8,10},{9,11},{10,... | collective-permute-start | bytes 129032 | tf_op jit(solution)/shard_map/ppermute | solution.py:325
  22.9 0.8 %collective-permute-start.14 = (bf16[8,2688]{1,0:T(8,128)(2,1)S(1)}, bf16[8,2688]{1,0:T(8,128)(2,1)S(1)}, u32[]{:S(2)}, u32[]{:S(2)}) collective-permute-start(bf16[8,2688]{1,0:T(8,128)(2,1)S(1)} %get-tuple-element.38), channel_id=1, source_target_pairs={{0,2},{1,3},{2,0},{3,1},{4,6},{5,7},{6,4},{7,5},{8,10},{9,11},{10,... | collective-permute-start | bytes 129032 | tf_op jit(solution)/shard_map/ppermute | solution.py:325
  23.7 1.3 %collective-permute-start.16 = (bf16[8,2688]{1,0:T(8,128)(2,1)S(1)}, bf16[8,2688]{1,0:T(8,128)(2,1)S(1)}, u32[]{:S(2)}, u32[]{:S(2)}) collective-permute-start(bf16[8,2688]{1,0:T(8,128)(2,1)S(1)} %get-tuple-element.40), channel_id=1, source_target_pairs={{0,2},{1,3},{2,0},{3,1},{4,6},{5,7},{6,4},{7,5},{8,10},{9,11},{10,... | collective-permute-start | bytes 129032 | tf_op jit(solution)/shard_map/ppermute | solution.py:325
  24.9 0.8 %collective-permute-start.11 = (bf16[8,2688]{1,0:T(8,128)(2,1)S(1)}, bf16[8,2688]{1,0:T(8,128)(2,1)S(1)}, u32[]{:S(2)}, u32[]{:S(2)}) collective-permute-start(bf16[8,2688]{1,0:T(8,128)(2,1)S(1)} %get-tuple-element.34), channel_id=1, source_target_pairs={{0,2},{1,3},{2,0},{3,1},{4,6},{5,7},{6,4},{7,5},{8,10},{9,11},{10,... | collective-permute-start | bytes 129032 | tf_op jit(solution)/shard_map/ppermute | solution.py:325
  25.7 0.1 merge.6
  25.9 3.4 %collective-permute-start.13 = (bf16[8,2688]{1,0:T(8,128)(2,1)S(1)}, bf16[8,2688]{1,0:T(8,128)(2,1)S(1)}, u32[]{:S(2)}, u32[]{:S(2)}) collective-permute-start(bf16[8,2688]{1,0:T(8,128)(2,1)S(1)} %merge.6), channel_id=1, source_target_pairs={{0,12},{1,13},{2,14},{3,15},{4,8},{5,9},{6,10},{7,11},{8,4},{9,5},... | collective-permute-start | bytes 129032 | tf_op jit(solution)/shard_map/ppermute | solution.py:325
  29.3 0.1 merge.7
  29.4 0.1 collective-permute-start.15
  29.5 0.1 merge.8
  29.7 1.6 %collective-permute-start.17 = (bf16[8,2688]{1,0:T(8,128)(2,1)S(1)}, bf16[8,2688]{1,0:T(8,128)(2,1)S(1)}, u32[]{:S(2)}, u32[]{:S(2)}) collective-permute-start(bf16[8,2688]{1,0:T(8,128)(2,1)S(1)} %merge.8), channel_id=1, source_target_pairs={{0,4},{1,5},{2,6},{3,7},{4,0},{5,1},{6,2},{7,3},{8,12},{9,13},{10,... | collective-permute-start | bytes 129032 | tf_op jit(solution)/shard_map/ppermute | solution.py:325
  31.3 0.1 merge.5.refs_0_
  31.4 0.3 collective-permute-done.13.refs_1_
  31.8 2.6 %collective-permute-done.15.refs_2_ = bf16[8,2688]{1,0:T(8,128)(2,1)S(1)} collective-permute-done((bf16[8,2688]{1,0:T(8,128)(2,1)S(1)}, bf16[8,2688]{1,0:T(8,128)(2,1)S(1)}, u32[]{:S(2)}, u32[]{:S(2)}) %collective-permute-start.15) | collective-permute-done | bytes 43040 | tf_op jit(solution)/shard_map/ppermute | solution.py:325
  34.4 0.9 %merge.9 = bf16[8,2560]{1,0:T(8,128)(2,1)} custom-call(f32[8,2688]{1,0:T(8,128)S(1)} %merge.5.refs_0_, bf16[8,2688]{1,0:T(8,128)(2,1)S(1)} %collective-permute-done.13.refs_1_, bf16[8,2688]{1,0:T(8,128)(2,1)S(1)} %collective-permute-done.15.refs_2_, bf16[8,2688]{1,0:T(8,128)(2,1)S(1)} %collective-permute-done.17.refs_3_), custom_call_target="tpu_custom_call" | custom-call | flops 344064 | bytes 344064 | tf_op jit(solution)/shard_map/merge/pallas_call | solution.py:301
  (11 shorter events, 0.0 us)
Async XLA Ops:
  0.0 1.5 %collective-permute-start = (bf16[8,2560]{1,0:T(8,128)(2,1)}, bf16[8,2560]{1,0:T(8,128)(2,1)S(1)}, u32[]{:S(2)}, u32[]{:S(2)}) collective-permute-start(bf16[8,2560]{1,0:T(8,128)(2,1)} %refs_2_), channel_id=1, source_target_pairs={{1,0},{0,1},{3,2},{2,3},{5,4},{4,5},{7,6},{6,7},{9,8},{8,9},{11,10... | collective-permute-start | bytes 122888 | tf_op jit(solution)/shard_map/ppermute | solution.py:322
  0.5 1.4 %collective-permute-start.1 = (bf16[8,2560]{1,0:T(8,128)(2,1)}, bf16[8,2560]{1,0:T(8,128)(2,1)S(1)}, u32[]{:S(2)}, u32[]{:S(2)}) collective-permute-start(bf16[8,2560]{1,0:T(8,128)(2,1)} %refs_4_), channel_id=1, source_target_pairs={{1,0},{0,1},{3,2},{2,3},{5,4},{4,5},{7,6},{6,7},{9,8},{8,9},{11,10... | collective-permute-start | bytes 122888 | tf_op jit(solution)/shard_map/ppermute | solution.py:322
  1.9 16.8 %collective-permute-start.9 = (bf16[512,2560]{1,0:T(8,128)(2,1)}, bf16[512,2560]{1,0:T(8,128)(2,1)S(1)}, u32[]{:S(2)}, u32[]{:S(2)}) collective-permute-start(bf16[512,2560]{1,0:T(8,128)(2,1)} %refs_0_.1), channel_id=1, source_target_pairs={{1,0},{0,1},{3,2},{2,3},{5,4},{4,5},{7,6},{6,7},{9,8},{8,9},{11,10... | collective-permute-start | bytes 7864328 | tf_op jit(solution)/shard_map/ppermute | solution.py:322
  2.0 16.6 %collective-permute-start.10 = (bf16[512,2560]{1,0:T(8,128)(2,1)}, bf16[512,2560]{1,0:T(8,128)(2,1)S(1)}, u32[]{:S(2)}, u32[]{:S(2)}) collective-permute-start(bf16[512,2560]{1,0:T(8,128)(2,1)} %refs_1_.1), channel_id=1, source_target_pairs={{1,0},{0,1},{3,2},{2,3},{5,4},{4,5},{7,6},{6,7},{9,8},{8,9},{11,10... | collective-permute-start | bytes 7864328 | tf_op jit(solution)/shard_map/ppermute | solution.py:322
  2.4 7.2 %collective-permute-start.3 = (bf16[8,2560]{1,0:T(8,128)(2,1)}, bf16[8,2560]{1,0:T(8,128)(2,1)S(1)}, u32[]{:S(2)}, u32[]{:S(2)}) collective-permute-start(bf16[8,2560]{1,0:T(8,128)(2,1)} %refs_7_.1), channel_id=1, source_target_pairs={{12,0},{13,1},{14,2},{15,3},{8,4},{9,5},{10,6},{11,7},{4,8},{5,9},... | collective-permute-start | bytes 122888 | tf_op jit(solution)/shard_map/ppermute | solution.py:322
  7.2 5.1 %collective-permute-start.2 = (bf16[8,2560]{1,0:T(8,128)(2,1)}, bf16[8,2560]{1,0:T(8,128)(2,1)S(1)}, u32[]{:S(2)}, u32[]{:S(2)}) collective-permute-start(bf16[8,2560]{1,0:T(8,128)(2,1)} %refs_7_.1), channel_id=1, source_target_pairs={{8,0},{9,1},{10,2},{11,3},{12,4},{13,5},{14,6},{15,7},{0,8},{1,9},... | collective-permute-start | bytes 122888 | tf_op jit(solution)/shard_map/ppermute | solution.py:322
  7.2 6.7 %collective-permute-start.5 = (bf16[8,2560]{1,0:T(8,128)(2,1)}, bf16[8,2560]{1,0:T(8,128)(2,1)S(1)}, u32[]{:S(2)}, u32[]{:S(2)}) collective-permute-start(bf16[8,2560]{1,0:T(8,128)(2,1)} %refs_7_.1), channel_id=1, source_target_pairs={{2,0},{3,1},{0,2},{1,3},{6,4},{7,5},{4,6},{5,7},{10,8},{11,9},{8,1... | collective-permute-start | bytes 122888 | tf_op jit(solution)/shard_map/ppermute | solution.py:322
  9.5 4.8 %collective-permute-start.4 = (bf16[8,2560]{1,0:T(8,128)(2,1)}, bf16[8,2560]{1,0:T(8,128)(2,1)S(1)}, u32[]{:S(2)}, u32[]{:S(2)}) collective-permute-start(bf16[8,2560]{1,0:T(8,128)(2,1)} %refs_7_.1), channel_id=1, source_target_pairs={{4,0},{5,1},{6,2},{7,3},{0,4},{1,5},{2,6},{3,7},{12,8},{13,9},{14,... | collective-permute-start | bytes 122888 | tf_op jit(solution)/shard_map/ppermute | solution.py:322
  12.3 6.3 %collective-permute-start.6 = (bf16[8,2560]{1,0:T(8,128)(2,1)S(1)}, bf16[8,2560]{1,0:T(8,128)(2,1)S(1)}, u32[]{:S(2)}, u32[]{:S(2)}) collective-permute-start(bf16[8,2560]{1,0:T(8,128)(2,1)S(1)} %collective-permute-done.3.refs_2_), channel_id=1, source_target_pairs={{2,0},{3,1},{0,2},{1,3},{6,4},{7,5},{4,6},{5,7},{10,8},{11,9},{8,1... | collective-permute-start | bytes 122888 | tf_op jit(solution)/shard_map/ppermute | solution.py:322
  13.9 4.7 %collective-permute-start.7 = (bf16[8,2560]{1,0:T(8,128)(2,1)S(1)}, bf16[8,2560]{1,0:T(8,128)(2,1)S(1)}, u32[]{:S(2)}, u32[]{:S(2)}) collective-permute-start(bf16[8,2560]{1,0:T(8,128)(2,1)S(1)} %collective-permute-done.2.refs_8_.refs_3_), channel_id=1, source_target_pairs={{2,0},{3,1},{0,2},{1,3},{6,4},{7,5},{4,6},{5,7},{10,8},{11,9},{8,1... | collective-permute-start | bytes 122888 | tf_op jit(solution)/shard_map/ppermute | solution.py:322
  14.3 4.3 %collective-permute-start.8 = (bf16[8,2560]{1,0:T(8,128)(2,1)S(1)}, bf16[8,2560]{1,0:T(8,128)(2,1)S(1)}, u32[]{:S(2)}, u32[]{:S(2)}) collective-permute-start(bf16[8,2560]{1,0:T(8,128)(2,1)S(1)} %collective-permute-done.4.refs_4_), channel_id=1, source_target_pairs={{2,0},{3,1},{0,2},{1,3},{6,4},{7,5},{4,6},{5,7},{10,8},{11,9},{8,1... | collective-permute-start | bytes 122888 | tf_op jit(solution)/shard_map/ppermute | solution.py:322
  21.6 4.1 %collective-permute-start.12 = (bf16[8,2688]{1,0:T(8,128)(2,1)S(1)}, bf16[8,2688]{1,0:T(8,128)(2,1)S(1)}, u32[]{:S(2)}, u32[]{:S(2)}) collective-permute-start(bf16[8,2688]{1,0:T(8,128)(2,1)S(1)} %get-tuple-element.36), channel_id=1, source_target_pairs={{0,2},{1,3},{2,0},{3,1},{4,6},{5,7},{6,4},{7,5},{8,10},{9,11},{10,... | collective-permute-start | bytes 129032 | tf_op jit(solution)/shard_map/ppermute | solution.py:325
  22.9 6.3 %collective-permute-start.14 = (bf16[8,2688]{1,0:T(8,128)(2,1)S(1)}, bf16[8,2688]{1,0:T(8,128)(2,1)S(1)}, u32[]{:S(2)}, u32[]{:S(2)}) collective-permute-start(bf16[8,2688]{1,0:T(8,128)(2,1)S(1)} %get-tuple-element.38), channel_id=1, source_target_pairs={{0,2},{1,3},{2,0},{3,1},{4,6},{5,7},{6,4},{7,5},{8,10},{9,11},{10,... | collective-permute-start | bytes 129032 | tf_op jit(solution)/shard_map/ppermute | solution.py:325
  23.7 5.8 %collective-permute-start.16 = (bf16[8,2688]{1,0:T(8,128)(2,1)S(1)}, bf16[8,2688]{1,0:T(8,128)(2,1)S(1)}, u32[]{:S(2)}, u32[]{:S(2)}) collective-permute-start(bf16[8,2688]{1,0:T(8,128)(2,1)S(1)} %get-tuple-element.40), channel_id=1, source_target_pairs={{0,2},{1,3},{2,0},{3,1},{4,6},{5,7},{6,4},{7,5},{8,10},{9,11},{10,... | collective-permute-start | bytes 129032 | tf_op jit(solution)/shard_map/ppermute | solution.py:325
  24.9 6.3 %collective-permute-start.11 = (bf16[8,2688]{1,0:T(8,128)(2,1)S(1)}, bf16[8,2688]{1,0:T(8,128)(2,1)S(1)}, u32[]{:S(2)}, u32[]{:S(2)}) collective-permute-start(bf16[8,2688]{1,0:T(8,128)(2,1)S(1)} %get-tuple-element.34), channel_id=1, source_target_pairs={{0,2},{1,3},{2,0},{3,1},{4,6},{5,7},{6,4},{7,5},{8,10},{9,11},{10,... | collective-permute-start | bytes 129032 | tf_op jit(solution)/shard_map/ppermute | solution.py:325
  25.9 5.9 %collective-permute-start.13 = (bf16[8,2688]{1,0:T(8,128)(2,1)S(1)}, bf16[8,2688]{1,0:T(8,128)(2,1)S(1)}, u32[]{:S(2)}, u32[]{:S(2)}) collective-permute-start(bf16[8,2688]{1,0:T(8,128)(2,1)S(1)} %merge.6), channel_id=1, source_target_pairs={{0,12},{1,13},{2,14},{3,15},{4,8},{5,9},{6,10},{7,11},{8,4},{9,5},... | collective-permute-start | bytes 129032 | tf_op jit(solution)/shard_map/ppermute | solution.py:325
  29.4 5.0 %collective-permute-start.15 = (bf16[8,2688]{1,0:T(8,128)(2,1)S(1)}, bf16[8,2688]{1,0:T(8,128)(2,1)S(1)}, u32[]{:S(2)}, u32[]{:S(2)}) collective-permute-start(bf16[8,2688]{1,0:T(8,128)(2,1)S(1)} %merge.7), channel_id=1, source_target_pairs={{0,8},{1,9},{2,10},{3,11},{4,12},{5,13},{6,14},{7,15},{8,0},{9,1},... | collective-permute-start | bytes 129032 | tf_op jit(solution)/shard_map/ppermute | solution.py:325
  29.7 4.8 %collective-permute-start.17 = (bf16[8,2688]{1,0:T(8,128)(2,1)S(1)}, bf16[8,2688]{1,0:T(8,128)(2,1)S(1)}, u32[]{:S(2)}, u32[]{:S(2)}) collective-permute-start(bf16[8,2688]{1,0:T(8,128)(2,1)S(1)} %merge.8), channel_id=1, source_target_pairs={{0,4},{1,5},{2,6},{3,7},{4,0},{5,1},{6,2},{7,3},{8,12},{9,13},{10,... | collective-permute-start | bytes 129032 | tf_op jit(solution)/shard_map/ppermute | solution.py:325

commit v19 on v17

--- a/solution.py
+++ b/solution.py
@@ -58,6 +58,18 @@
     return head % PACK * (LANE // PACK) + head // PACK
 
 
+def whole_tiles(rows):
+    return -(-rows // 16) * 16
+
+
+def filled(ref, cols):
+    rows, missing = ref.shape[0], whole_tiles(ref.shape[0]) - ref.shape[0]
+    if not missing:
+        return ref[:, cols]
+    block = ref[:, cols].astype(F32)
+    return jnp.concatenate([block, jnp.zeros((missing, block.shape[1]), F32)], axis=0).astype(BF16)
+
+
 def attend_kernel(scale, bias_ref, q_refs, k_refs, v_refs, outs, top_acc, mass_acc):
     tok = q_refs[0].shape[0]
     rows = tok * len(q_refs)
@@ -66,7 +78,7 @@
     contract_last = (((1,), (1,)), ((), ()))
     contract_first = (((0,), (0,)), ((), ()))
     mine = [lax.broadcasted_iota(jnp.int32, (rows, wide), 1) // HD == k for k in range(PACK)]
-    starts = [sum(r.shape[0] for r in k_refs[:j]) for j in range(len(k_refs))]
+    starts = [sum(whole_tiles(r.shape[0]) for r in k_refs[:j]) for j in range(len(k_refs))]
     top_acc[...] = jnp.zeros_like(top_acc)
     mass_acc[...] = jnp.zeros_like(mass_acc)
 
@@ -75,7 +87,8 @@
         q = jnp.concatenate([ref[:, cols].astype(F32) for ref in q_refs], axis=0)
         q = jnp.concatenate([jnp.where(m, q, 0.0) for m in mine], axis=0).astype(BF16)
         return [
-            lax.dot_general(k[:, cols], q, contract_last, preferred_element_type=F32) for k in k_refs
+            lax.dot_general(filled(k, cols), q, contract_last, preferred_element_type=F32)
+            for k in k_refs
         ]
 
     def weigh(i, parts):
@@ -97,7 +110,7 @@
         both = functools.reduce(
             jnp.add,
             [
-                lax.dot_general(w, v[:, cols], contract_first, preferred_element_type=F32)
+                lax.dot_general(w, filled(v, cols), contract_first, preferred_element_type=F32)
                 for w, v in zip(weights, v_refs)
             ],
         )
@@ -159,27 +172,24 @@
 def load(cached, fresh, victims, queries, cores, after):
     cache_rows, columns = cached[0].shape
     tok = queries.shape[0]
-    fresh_rows = tok * len(fresh[0])
-    padded = cache_rows + -(-fresh_rows // 16) * 16
-    mask_rows = padded + (cores - 1) * cache_rows
+    padded = cache_rows + whole_tiles(tok)
+    mask_rows = padded * cores
     blocks = cache_rows // BLK
-    n, m = len(cached), len(fresh[0])
-    flat = [x for parts in fresh for x in parts]
-
-    def body(*refs):
-        cached_refs, fresh_refs = refs[:n], refs[n : n + n * m]
-        victims_ref, queries_ref = refs[n + n * m : n + n * m + 2]
-        refs = refs[n + n * m + 3 :]
+    n = len(cached)
+
+    def body(*refs):
+        cached_refs, fresh_refs, (victims_ref, queries_ref) = refs[:n], refs[n : 2 * n], refs[2 * n : 2 * n + 2]
+        refs = refs[2 * n + 3 :]
         outs, bias_ref, q_ref, refs = refs[:n], refs[n], refs[n + 1], refs[n + 2 :]
-        tails, ids_ref, sems = refs[: n * m], refs[n * m], refs[n * m + 1]
-        ids = pltpu.make_async_copy(victims_ref, ids_ref, sems.at[n * m + n])
-        rest = pltpu.make_async_copy(queries_ref, q_ref, sems.at[n * m + n + 1])
+        tails, ids_ref, sems = refs[:n], refs[n], refs[n + 1]
+        ids = pltpu.make_async_copy(victims_ref, ids_ref, sems.at[2 * n])
+        rest = pltpu.make_async_copy(queries_ref, q_ref, sems.at[2 * n + 1])
         small = [
             pltpu.make_async_copy(src, dst, sems.at[i])
             for i, (src, dst) in enumerate(zip(fresh_refs, tails))
         ]
         large = [
-            pltpu.make_async_copy(src, dst.at[pl.ds(0, cache_rows), :], sems.at[n * m + i])
+            pltpu.make_async_copy(src, dst.at[pl.ds(0, cache_rows), :], sems.at[n + i])
             for i, (src, dst) in enumerate(zip(cached_refs, outs))
         ]
         for copy in [ids] + small + large + [rest]:
@@ -187,55 +197,44 @@
         ids.wait()
         me = lax.axis_index("seq")
         core = lax.rem(me, cores)
-
-        def mask(first, start):
+        token = lax.broadcasted_iota(jnp.int32, (padded - cache_rows, STAT), 0)
+        unused = jnp.where(token < tok, 0.0, NEG)
+        bias_ref[cache_rows:padded, :] = unused
+        for c in range(cores):
+            start = padded + (c - 1) * cache_rows if c else 0
+            first = (me - core + lax.rem(core + c, cores)) * blocks
             for block in range(blocks):
                 hits = jnp.where(ids_ref[...] == first + block, 1.0, 0.0)
                 hit = jnp.max(hits, axis=1, keepdims=True)
                 gone = jnp.where(hit > 0.0, NEG, 0.0)
                 at = start + block * BLK
                 bias_ref[at : at + BLK, :] = jnp.broadcast_to(gone, (BLK, STAT))
-
-        mask(me * blocks, 0)
-        token = lax.broadcasted_iota(jnp.int32, (padded - cache_rows, STAT), 0)
-        bias_ref[cache_rows:padded, :] = jnp.where(token < fresh_rows, 0.0, NEG)
-        for c in range(1, cores):
-            other = me - core + lax.rem(core + c, cores)
-            mask(other * blocks, padded + (c - 1) * cache_rows)
+            if c:
+                at = padded + (cores - 1) * cache_rows + (c - 1) * (padded - cache_rows)
+                bias_ref[at : at + padded - cache_rows, :] = unused
         for copy in small:
             copy.wait()
-        for i, out in enumerate(outs):
-            rows = [t[...].astype(F32) for t in tails[i * m : (i + 1) * m]]
-            if padded - cache_rows > fresh_rows:
-                rows.append(jnp.zeros((padded - cache_rows - fresh_rows, columns), F32))
-            out[cache_rows:, :] = jnp.concatenate(rows, axis=0).astype(out.dtype)
+        for tail, out in zip(tails, outs):
+            out[cache_rows:, :] = filled(tail, slice(0, columns))
         for copy in large + [rest]:
             copy.wait()
 
-    hbm = lambda x: pltpu.with_memory_space_constraint(x, pltpu.HBM)
-    in_hbm = pl.BlockSpec(memory_space=pltpu.HBM)
-    anywhere = pl.BlockSpec(memory_space=pl.ANY)
+    held = (*cached, *fresh, victims, queries)
     return pl.pallas_call(
         body,
-        in_specs=[in_hbm] * n
-        + [in_hbm if i % m == 0 else anywhere for i in range(n * m)]
-        + [in_hbm] * 2
-        + [anywhere],
+        in_specs=[pl.BlockSpec(memory_space=pltpu.HBM)] * len(held)
+        + [pl.BlockSpec(memory_space=pl.ANY)],
         out_specs=[pl.BlockSpec(memory_space=pltpu.VMEM)] * (n + 2),
         out_shape=[jax.ShapeDtypeStruct((padded, columns), BF16)] * n
         + [jax.ShapeDtypeStruct((mask_rows, STAT), F32), jax.ShapeDtypeStruct(queries.shape, BF16)],
-        scratch_shapes=[pltpu.VMEM(queries.shape, BF16)] * (n * m)
-        + [pltpu.VMEM(victims.shape, jnp.int32), pltpu.SemaphoreType.DMA((n * m + n + 2,))],
+        scratch_shapes=[pltpu.VMEM(queries.shape, BF16)] * n
+        + [pltpu.VMEM(victims.shape, jnp.int32), pltpu.SemaphoreType.DMA((2 * n + 2,))],
         compiler_params=pltpu.CompilerParams(vmem_limit_bytes=16 * 1024 * 1024),
         cost_estimate=pl.CostEstimate(
             flops=0, bytes_accessed=4 * n * cache_rows * columns, transcendentals=0
         ),
         name="load",
-    )(
-        *[hbm(x) for x in cached],
-        *[hbm(x) if i % m == 0 else x for i, x in enumerate(flat)],
-        hbm(victims), hbm(queries), after,
-    )
+    )(*[pltpu.with_memory_space_constraint(x, pltpu.HBM) for x in held], after)
 
 
 def merged(arrays, heads, last):
@@ -324,16 +323,26 @@
     def give(x, *by):
         return lax.ppermute(x, "seq", partner_perm(shape, by, True))
 
-    others = [[fetch(x, 0, 0, c) for c in range(1, c_n)] for x in (cache_keys, cache_values)]
-    fresh = [[x] + [fetch(x, 0, 0, c) for c in range(1, c_n)] for x in (new_keys, new_values)]
+    def other_cores(x):
+        return [fetch(x, 0, 0, c) for c in range(1, c_n)]
+
+    def other_cores(x):
+        return [fetch(x, 0, 0, c) for c in range(1, c_n)]
 
     far_first = [0, *range(a_n - 1, 0, -1)]
+    other_keys, other_values = other_cores(cache_keys), other_cores(cache_values)
     line = [queries] + [fetch(queries, a, 0, 0) for a in far_first[1:]]
-    lines = [line] + [[fetch(x, 0, b, 0) for x in line] for b in range(1, b_n)]
+    own = queries
+    if a_n > 2:
+        own, line[1] = lax.optimization_barrier((own, line[1]))
+    lines = [line] + [[fetch(x, 0, b, 0) for x in [own] + line[1:]] for b in range(1, b_n)]
     keys, values, bias, line[0] = load(
-        (cache_keys, cache_values), fresh, victims[None], queries, c_n, line[min(2, a_n - 1)]
+        (cache_keys, cache_values), (new_keys, new_values), victims[None], queries, c_n, lines[-1][0]
     )
-    keys, values = [keys, *others[0]], [values, *others[1]]
+    held, bias = lax.optimization_barrier(((new_keys, new_values), bias))
+    other_fresh = [other_cores(x) for x in held]
+    keys = [keys, *other_keys, *other_fresh[0]]
+    values = [values, *other_values, *other_fresh[1]]
     at_once = next(n for n in range(b_n, 0, -1) if b_n % n == 0 and n * a_n * tok <= max(64, a_n * tok))
     sums = []
     for start in range(0, b_n, at_once):

time: 39.5 us -> 35.8 us (0.906)
  starting transfers between devices: 25.4 us -> 21.7 us
    ppermute x11, starting transfers between devices: 16.5 us -> 12.4 us  [fetch(): return lax.ppermute(x, 'seq', partner_perm(shape, by, False))]
    ppermute x11, waiting for transfers between devices: 3.58 us -> 3.06 us  [fetch(): return lax.ppermute(x, 'seq', partner_perm(shape, by, False))]
  transfers between devices with their start and end apart: 18 -> 18, of which waited for: 4 -> 7; matrix products, arithmetic and copies ran while one was open for 0% -> 0% of each run, Pallas kernels for 8% -> 9%
where the time goes in v19:
time: 35.8 us; the launch traced here: 35.7 us
  starting transfers between devices  21.7 us (61%)
  Pallas kernels  7.23 us (20%)
  waiting for transfers between devices  6.69 us (19%)
    ppermute x11, starting transfers between devices, fetch(): return lax.ppermute(x, 'seq', partner_perm(shape, by, False))  12.4 us
    ppermute x7, starting transfers between devices, give(): return lax.ppermute(x, 'seq', partner_perm(shape, by, True))  9.22 us
    ppermute x7, waiting for transfers between devices, give(): return lax.ppermute(x, 'seq', partner_perm(shape, by, True))  3.63 us
    pallas_call x1, Pallas kernels, attend(): pl.pallas_call(body, in_specs=[pl.BlockSpec(memory_space=pltpu.VMEM)] * (...  3.11 us
    ppermute x11, waiting for transfers between devices, fetch(): return lax.ppermute(x, 'seq', partner_perm(shape, by, False))  3.06 us
    pallas_call x1, Pallas kernels, load(): pl.pallas_call(body, in_specs=[pl.BlockSpec(memory_space=pltpu.HBM)] * le...  2.65 us
    pallas_call x5, Pallas kernels, call_merge(): pl.pallas_call(body, in_specs=[pl.BlockSpec(memory_space=pltpu.VMEM)] * l...  1.47 us
  transfers between devices with their start and end apart: 18, of which 7 were waited for; matrix products, arithmetic and copies ran while one was open for 0% of the time, Pallas kernels for 9%

profile of v19, /device:TPU:0, one launch (start us, length us, event | category | flops | bytes accessed | tf_op | source)
XLA Modules:
  0.0 35.7 jit_solution(6360607902931598870)
XLA Ops:
  0.0 0.5 %collective-permute-start.7 = (bf16[512,2560]{1,0:T(8,128)(2,1)}, bf16[512,2560]{1,0:T(8,128)(2,1)S(1)}, u32[]{:S(2)}, u32[]{:S(2)}) collective-permute-start(bf16[512,2560]{1,0:T(8,128)(2,1)} %refs_0_.1), channel_id=1, source_target_pairs={{1,0},{0,1},{3,2},{2,3},{5,4},{4,5},{7,6},{6,7},{9,8},{8,9},{11,10... | collective-permute-start | bytes 7864328 | tf_op jit(solution)/shard_map/ppermute | solution.py:321
  0.5 0.1 collective-permute-start.9
  0.5 5.0 %collective-permute-start = (bf16[8,2560]{1,0:T(8,128)(2,1)}, bf16[8,2560]{1,0:T(8,128)(2,1)S(1)}, u32[]{:S(2)}, u32[]{:S(2)}) collective-permute-start(bf16[8,2560]{1,0:T(8,128)(2,1)} %refs_5_.1), channel_id=1, source_target_pairs={{12,0},{13,1},{14,2},{15,3},{8,4},{9,5},{10,6},{11,7},{4,8},{5,9},... | collective-permute-start | bytes 122888 | tf_op jit(solution)/shard_map/ppermute | solution.py:321
  5.6 0.0 collective-permute-start.3
  5.6 0.6 %collective-permute-start.2 = (bf16[8,2560]{1,0:T(8,128)(2,1)}, bf16[8,2560]{1,0:T(8,128)(2,1)S(1)}, u32[]{:S(2)}, u32[]{:S(2)}) collective-permute-start(bf16[8,2560]{1,0:T(8,128)(2,1)} %refs_5_.1), channel_id=1, source_target_pairs={{8,0},{9,1},{10,2},{11,3},{12,4},{13,5},{14,6},{15,7},{0,8},{1,9},... | collective-permute-start | bytes 122888 | tf_op jit(solution)/shard_map/ppermute | solution.py:321
  6.1 1.8 %collective-permute-done.refs_2_ = bf16[8,2560]{1,0:T(8,128)(2,1)S(1)} collective-permute-done((bf16[8,2560]{1,0:T(8,128)(2,1)}, bf16[8,2560]{1,0:T(8,128)(2,1)S(1)}, u32[]{:S(2)}, u32[]{:S(2)}) %collective-permute-start) | collective-permute-done | bytes 40992 | tf_op jit(solution)/shard_map/ppermute | solution.py:321
  7.9 1.6 %collective-permute-start.1 = (bf16[8,2560]{1,0:T(8,128)(2,1)}, bf16[8,2560]{1,0:T(8,128)(2,1)S(1)}, u32[]{:S(2)}, u32[]{:S(2)}) collective-permute-start(bf16[8,2560]{1,0:T(8,128)(2,1)} %refs_5_.1), channel_id=1, source_target_pairs={{2,0},{3,1},{0,2},{1,3},{6,4},{7,5},{4,6},{5,7},{10,8},{11,9},{8,1... | collective-permute-start | bytes 122888 | tf_op jit(solution)/shard_map/ppermute | solution.py:321
  9.5 0.4 %collective-permute-done.3.refs_4_ = bf16[8,2560]{1,0:T(8,128)(2,1)S(1)} collective-permute-done((bf16[8,2560]{1,0:T(8,128)(2,1)}, bf16[8,2560]{1,0:T(8,128)(2,1)S(1)}, u32[]{:S(2)}, u32[]{:S(2)}) %collective-permute-start.3) | collective-permute-done | bytes 40992 | tf_op jit(solution)/shard_map/ppermute | solution.py:321
  9.9 1.5 %collective-permute-start.4 = (bf16[8,2560]{1,0:T(8,128)(2,1)S(1)}, bf16[8,2560]{1,0:T(8,128)(2,1)S(1)}, u32[]{:S(2)}, u32[]{:S(2)}) collective-permute-start(bf16[8,2560]{1,0:T(8,128)(2,1)S(1)} %collective-permute-done.refs_2_), channel_id=1, source_target_pairs={{2,0},{3,1},{0,2},{1,3},{6,4},{7,5},{4,6},{5,7},{10,8},{11,9},{8,1... | collective-permute-start | bytes 122888 | tf_op jit(solution)/shard_map/ppermute | solution.py:321
  11.4 1.2 %collective-permute-start.6 = (bf16[8,2560]{1,0:T(8,128)(2,1)S(1)}, bf16[8,2560]{1,0:T(8,128)(2,1)S(1)}, u32[]{:S(2)}, u32[]{:S(2)}) collective-permute-start(bf16[8,2560]{1,0:T(8,128)(2,1)S(1)} %collective-permute-done.3.refs_4_), channel_id=1, source_target_pairs={{2,0},{3,1},{0,2},{1,3},{6,4},{7,5},{4,6},{5,7},{10,8},{11,9},{8,1... | collective-permute-start | bytes 122888 | tf_op jit(solution)/shard_map/ppermute | solution.py:321
  12.6 1.5 %collective-permute-start.5 = (bf16[8,2560]{1,0:T(8,128)(2,1)S(1)}, bf16[8,2560]{1,0:T(8,128)(2,1)S(1)}, u32[]{:S(2)}, u32[]{:S(2)}) collective-permute-start(bf16[8,2560]{1,0:T(8,128)(2,1)S(1)} %collective-permute-done.2.refs_3_), channel_id=1, source_target_pairs={{2,0},{3,1},{0,2},{1,3},{6,4},{7,5},{4,6},{5,7},{10,8},{11,9},{8,1... | collective-permute-start | bytes 122888 | tf_op jit(solution)/shard_map/ppermute | solution.py:321
  14.1 2.7 %load.1 = (bf16[528,2560]{1,0:T(8,128)(2,1)S(1)}, bf16[528,2560]{1,0:T(8,128)(2,1)S(1)}, f32[1056,128]{1,0:T(8,128)S(1)}, bf16[8,2560]{1,0:T(8,128)(2,1)S(1)}) custom-call(bf16[512,2560]{1,0:T(8,128)(2,1)} %refs_0_.1, bf16[512,2560]{1,0:T(8,128)(2,1)} %refs_1_.1, bf16[8,2560]{1,0:T(8,128)(2,1)} %refs_2_.1, bf16[8,2560]{1,0:T(8,128)(2,1)} %refs_3_.1, ...), custom_call_target="tpu_custom_call" | custom-call | bytes 10485760 | tf_op jit(solution)/shard_map/load/pallas_call | solution.py:223
  16.7 0.1 collective-permute-start.8
  16.8 0.5 %collective-permute-start.10 = (bf16[8,2560]{1,0:T(8,128)(2,1)S(1)}, bf16[8,2560]{1,0:T(8,128)(2,1)S(1)}, u32[]{:S(2)}, u32[]{:S(2)}) collective-permute-start(bf16[8,2560]{1,0:T(8,128)(2,1)S(1)} %copy-done.1), channel_id=1, source_target_pairs={{1,0},{0,1},{3,2},{2,3},{5,4},{4,5},{7,6},{6,7},{9,8},{8,9},{11,10... | collective-permute-start | bytes 122888 | tf_op jit(solution)/shard_map/ppermute | solution.py:321
  17.3 0.7 %collective-permute-done.8.refs_11_ = bf16[8,2560]{1,0:T(8,128)(2,1)S(1)} collective-permute-done((bf16[8,2560]{1,0:T(8,128)(2,1)S(1)}, bf16[8,2560]{1,0:T(8,128)(2,1)S(1)}, u32[]{:S(2)}, u32[]{:S(2)}) %collective-permute-start.8) | collective-permute-done | bytes 40992 | tf_op jit(solution)/shard_map/ppermute | solution.py:321
  18.0 0.2 collective-permute-done.10.refs_14_
  18.2 3.1 %attend.1 = (f32[8,2688]{1,0:T(8,128)S(1)}, f32[8,2688]{1,0:T(8,128)S(1)}, f32[8,2688]{1,0:T(8,128)S(1)}, f32[8,2688]{1,0:T(8,128)S(1)}, bf16[8,2688]{1,0:T(8,12...) custom-call(f32[1056,128]{1,0:T(8,128)S(1)} %get-tuple-element.24.refs_0_, ...), custom_call_target="tpu_custom_call" | custom-call | flops 686817280 | bytes 10731520 | tf_op jit(solution)/shard_map/attend/pallas_call | solution.py:156
  21.3 0.6 %collective-permute-start.12 = (bf16[8,2688]{1,0:T(8,128)(2,1)S(1)}, bf16[8,2688]{1,0:T(8,128)(2,1)S(1)}, u32[]{:S(2)}, u32[]{:S(2)}) collective-permute-start(bf16[8,2688]{1,0:T(8,128)(2,1)S(1)} %get-tuple-element.34), channel_id=1, source_target_pairs={{0,2},{1,3},{2,0},{3,1},{4,6},{5,7},{6,4},{7,5},{8,10},{9,11},{10,... | collective-permute-start | bytes 129032 | tf_op jit(solution)/shard_map/ppermute | solution.py:324
  21.9 1.5 %collective-permute-start.14 = (bf16[8,2688]{1,0:T(8,128)(2,1)S(1)}, bf16[8,2688]{1,0:T(8,128)(2,1)S(1)}, u32[]{:S(2)}, u32[]{:S(2)}) collective-permute-start(bf16[8,2688]{1,0:T(8,128)(2,1)S(1)} %get-tuple-element.36), channel_id=1, source_target_pairs={{0,2},{1,3},{2,0},{3,1},{4,6},{5,7},{6,4},{7,5},{8,10},{9,11},{10,... | collective-permute-start | bytes 129032 | tf_op jit(solution)/shard_map/ppermute | solution.py:324
  23.4 0.5 %collective-permute-start.16 = (bf16[8,2688]{1,0:T(8,128)(2,1)S(1)}, bf16[8,2688]{1,0:T(8,128)(2,1)S(1)}, u32[]{:S(2)}, u32[]{:S(2)}) collective-permute-start(bf16[8,2688]{1,0:T(8,128)(2,1)S(1)} %get-tuple-element.38), channel_id=1, source_target_pairs={{0,2},{1,3},{2,0},{3,1},{4,6},{5,7},{6,4},{7,5},{8,10},{9,11},{10,... | collective-permute-start | bytes 129032 | tf_op jit(solution)/shard_map/ppermute | solution.py:324
  23.9 1.5 %collective-permute-start.11 = (bf16[8,2688]{1,0:T(8,128)(2,1)S(1)}, bf16[8,2688]{1,0:T(8,128)(2,1)S(1)}, u32[]{:S(2)}, u32[]{:S(2)}) collective-permute-start(bf16[8,2688]{1,0:T(8,128)(2,1)S(1)} %get-tuple-element.32), channel_id=1, source_target_pairs={{0,2},{1,3},{2,0},{3,1},{4,6},{5,7},{6,4},{7,5},{8,10},{9,11},{10,... | collective-permute-start | bytes 129032 | tf_op jit(solution)/shard_map/ppermute | solution.py:324
  25.4 0.3 collective-permute-done.12.refs_1_
  25.7 0.1 merge.6
  25.9 3.8 %collective-permute-start.13 = (bf16[8,2688]{1,0:T(8,128)(2,1)S(1)}, bf16[8,2688]{1,0:T(8,128)(2,1)S(1)}, u32[]{:S(2)}, u32[]{:S(2)}) collective-permute-start(bf16[8,2688]{1,0:T(8,128)(2,1)S(1)} %merge.6), channel_id=1, source_target_pairs={{0,12},{1,13},{2,14},{3,15},{4,8},{5,9},{6,10},{7,11},{8,4},{9,5},... | collective-permute-start | bytes 129032 | tf_op jit(solution)/shard_map/ppermute | solution.py:324
  29.6 0.1 merge.7
  29.8 0.1 collective-permute-start.15
  29.9 0.1 merge.8
  30.0 1.2 %collective-permute-start.17 = (bf16[8,2688]{1,0:T(8,128)(2,1)S(1)}, bf16[8,2688]{1,0:T(8,128)(2,1)S(1)}, u32[]{:S(2)}, u32[]{:S(2)}) collective-permute-start(bf16[8,2688]{1,0:T(8,128)(2,1)S(1)} %merge.8), channel_id=1, source_target_pairs={{0,4},{1,5},{2,6},{3,7},{4,0},{5,1},{6,2},{7,3},{8,12},{9,13},{10,... | collective-permute-start | bytes 129032 | tf_op jit(solution)/shard_map/ppermute | solution.py:324
  31.3 0.1 merge.5.refs_0_
  31.4 0.3 collective-permute-done.13.refs_1_
  31.8 3.0 %collective-permute-done.15.refs_2_ = bf16[8,2688]{1,0:T(8,128)(2,1)S(1)} collective-permute-done((bf16[8,2688]{1,0:T(8,128)(2,1)S(1)}, bf16[8,2688]{1,0:T(8,128)(2,1)S(1)}, u32[]{:S(2)}, u32[]{:S(2)}) %collective-permute-start.15) | collective-permute-done | bytes 43040 | tf_op jit(solution)/shard_map/ppermute | solution.py:324
  34.8 0.9 %merge.9 = bf16[8,2560]{1,0:T(8,128)(2,1)} custom-call(f32[8,2688]{1,0:T(8,128)S(1)} %merge.5.refs_0_, bf16[8,2688]{1,0:T(8,128)(2,1)S(1)} %collective-permute-done.13.refs_1_, bf16[8,2688]{1,0:T(8,128)(2,1)S(1)} %collective-permute-done.15.refs_2_, bf16[8,2688]{1,0:T(8,128)(2,1)S(1)} %collective-permute-done.17.refs_3_), custom_call_target="tpu_custom_call" | custom-call | flops 344064 | bytes 344064 | tf_op jit(solution)/shard_map/merge/pallas_call | solution.py:300
  (15 shorter events, 0.0 us)
Async XLA Ops:
  0.0 18.2 %collective-permute-start.7 = (bf16[512,2560]{1,0:T(8,128)(2,1)}, bf16[512,2560]{1,0:T(8,128)(2,1)S(1)}, u32[]{:S(2)}, u32[]{:S(2)}) collective-permute-start(bf16[512,2560]{1,0:T(8,128)(2,1)} %refs_0_.1), channel_id=1, source_target_pairs={{1,0},{0,1},{3,2},{2,3},{5,4},{4,5},{7,6},{6,7},{9,8},{8,9},{11,10... | collective-permute-start | bytes 7864328 | tf_op jit(solution)/shard_map/ppermute | solution.py:321
  0.5 17.8 %collective-permute-start.9 = (bf16[512,2560]{1,0:T(8,128)(2,1)}, bf16[512,2560]{1,0:T(8,128)(2,1)S(1)}, u32[]{:S(2)}, u32[]{:S(2)}) collective-permute-start(bf16[512,2560]{1,0:T(8,128)(2,1)} %refs_1_.1), channel_id=1, source_target_pairs={{1,0},{0,1},{3,2},{2,3},{5,4},{4,5},{7,6},{6,7},{9,8},{8,9},{11,10... | collective-permute-start | bytes 7864328 | tf_op jit(solution)/shard_map/ppermute | solution.py:321
  0.5 7.4 %collective-permute-start = (bf16[8,2560]{1,0:T(8,128)(2,1)}, bf16[8,2560]{1,0:T(8,128)(2,1)S(1)}, u32[]{:S(2)}, u32[]{:S(2)}) collective-permute-start(bf16[8,2560]{1,0:T(8,128)(2,1)} %refs_5_.1), channel_id=1, source_target_pairs={{12,0},{13,1},{14,2},{15,3},{8,4},{9,5},{10,6},{11,7},{4,8},{5,9},... | collective-permute-start | bytes 122888 | tf_op jit(solution)/shard_map/ppermute | solution.py:321
  5.6 4.3 %collective-permute-start.3 = (bf16[8,2560]{1,0:T(8,128)(2,1)}, bf16[8,2560]{1,0:T(8,128)(2,1)S(1)}, u32[]{:S(2)}, u32[]{:S(2)}) collective-permute-start(bf16[8,2560]{1,0:T(8,128)(2,1)} %refs_5_.1), channel_id=1, source_target_pairs={{4,0},{5,1},{6,2},{7,3},{0,4},{1,5},{2,6},{3,7},{12,8},{13,9},{14,... | collective-permute-start | bytes 122888 | tf_op jit(solution)/shard_map/ppermute | solution.py:321
  5.6 5.8 %collective-permute-start.2 = (bf16[8,2560]{1,0:T(8,128)(2,1)}, bf16[8,2560]{1,0:T(8,128)(2,1)S(1)}, u32[]{:S(2)}, u32[]{:S(2)}) collective-permute-start(bf16[8,2560]{1,0:T(8,128)(2,1)} %refs_5_.1), channel_id=1, source_target_pairs={{8,0},{9,1},{10,2},{11,3},{12,4},{13,5},{14,6},{15,7},{0,8},{1,9},... | collective-permute-start | bytes 122888 | tf_op jit(solution)/shard_map/ppermute | solution.py:321
  7.9 4.6 %collective-permute-start.1 = (bf16[8,2560]{1,0:T(8,128)(2,1)}, bf16[8,2560]{1,0:T(8,128)(2,1)S(1)}, u32[]{:S(2)}, u32[]{:S(2)}) collective-permute-start(bf16[8,2560]{1,0:T(8,128)(2,1)} %refs_5_.1), channel_id=1, source_target_pairs={{2,0},{3,1},{0,2},{1,3},{6,4},{7,5},{4,6},{5,7},{10,8},{11,9},{8,1... | collective-permute-start | bytes 122888 | tf_op jit(solution)/shard_map/ppermute | solution.py:321
  9.9 6.9 %collective-permute-start.4 = (bf16[8,2560]{1,0:T(8,128)(2,1)S(1)}, bf16[8,2560]{1,0:T(8,128)(2,1)S(1)}, u32[]{:S(2)}, u32[]{:S(2)}) collective-permute-start(bf16[8,2560]{1,0:T(8,128)(2,1)S(1)} %collective-permute-done.refs_2_), channel_id=1, source_target_pairs={{2,0},{3,1},{0,2},{1,3},{6,4},{7,5},{4,6},{5,7},{10,8},{11,9},{8,1... | collective-permute-start | bytes 122888 | tf_op jit(solution)/shard_map/ppermute | solution.py:321
  11.4 5.4 %collective-permute-start.6 = (bf16[8,2560]{1,0:T(8,128)(2,1)S(1)}, bf16[8,2560]{1,0:T(8,128)(2,1)S(1)}, u32[]{:S(2)}, u32[]{:S(2)}) collective-permute-start(bf16[8,2560]{1,0:T(8,128)(2,1)S(1)} %collective-permute-done.3.refs_4_), channel_id=1, source_target_pairs={{2,0},{3,1},{0,2},{1,3},{6,4},{7,5},{4,6},{5,7},{10,8},{11,9},{8,1... | collective-permute-start | bytes 122888 | tf_op jit(solution)/shard_map/ppermute | solution.py:321
  12.6 4.8 %collective-permute-start.5 = (bf16[8,2560]{1,0:T(8,128)(2,1)S(1)}, bf16[8,2560]{1,0:T(8,128)(2,1)S(1)}, u32[]{:S(2)}, u32[]{:S(2)}) collective-permute-start(bf16[8,2560]{1,0:T(8,128)(2,1)S(1)} %collective-permute-done.2.refs_3_), channel_id=1, source_target_pairs={{2,0},{3,1},{0,2},{1,3},{6,4},{7,5},{4,6},{5,7},{10,8},{11,9},{8,1... | collective-permute-start | bytes 122888 | tf_op jit(solution)/shard_map/ppermute | solution.py:321
  14.1 2.7 %copy-start = (bf16[8,2560]{1,0:T(8,128)(2,1)S(1)}, bf16[8,2560]{1,0:T(8,128)(2,1)}, u32[]{:S(2)}) copy-start(bf16[8,2560]{1,0:T(8,128)(2,1)} %refs_2_.1) | copy-start | bytes 122884
  14.1 2.8 %copy-start.1 = (bf16[8,2560]{1,0:T(8,128)(2,1)S(1)}, bf16[8,2560]{1,0:T(8,128)(2,1)}, u32[]{:S(2)}) copy-start(bf16[8,2560]{1,0:T(8,128)(2,1)} %refs_3_.1) | copy-start | bytes 122884
  16.7 1.3 %collective-permute-start.8 = (bf16[8,2560]{1,0:T(8,128)(2,1)S(1)}, bf16[8,2560]{1,0:T(8,128)(2,1)S(1)}, u32[]{:S(2)}, u32[]{:S(2)}) collective-permute-start(bf16[8,2560]{1,0:T(8,128)(2,1)S(1)} %copy-done), channel_id=1, source_target_pairs={{1,0},{0,1},{3,2},{2,3},{5,4},{4,5},{7,6},{6,7},{9,8},{8,9},{11,10... | collective-permute-start | bytes 122888 | tf_op jit(solution)/shard_map/ppermute | solution.py:321
  16.8 1.4 %collective-permute-start.10 = (bf16[8,2560]{1,0:T(8,128)(2,1)S(1)}, bf16[8,2560]{1,0:T(8,128)(2,1)S(1)}, u32[]{:S(2)}, u32[]{:S(2)}) collective-permute-start(bf16[8,2560]{1,0:T(8,128)(2,1)S(1)} %copy-done.1), channel_id=1, source_target_pairs={{1,0},{0,1},{3,2},{2,3},{5,4},{4,5},{7,6},{6,7},{9,8},{8,9},{11,10... | collective-permute-start | bytes 122888 | tf_op jit(solution)/shard_map/ppermute | solution.py:321
  21.3 4.4 %collective-permute-start.12 = (bf16[8,2688]{1,0:T(8,128)(2,1)S(1)}, bf16[8,2688]{1,0:T(8,128)(2,1)S(1)}, u32[]{:S(2)}, u32[]{:S(2)}) collective-permute-start(bf16[8,2688]{1,0:T(8,128)(2,1)S(1)} %get-tuple-element.34), channel_id=1, source_target_pairs={{0,2},{1,3},{2,0},{3,1},{4,6},{5,7},{6,4},{7,5},{8,10},{9,11},{10,... | collective-permute-start | bytes 129032 | tf_op jit(solution)/shard_map/ppermute | solution.py:324
  21.9 7.7 %collective-permute-start.14 = (bf16[8,2688]{1,0:T(8,128)(2,1)S(1)}, bf16[8,2688]{1,0:T(8,128)(2,1)S(1)}, u32[]{:S(2)}, u32[]{:S(2)}) collective-permute-start(bf16[8,2688]{1,0:T(8,128)(2,1)S(1)} %get-tuple-element.36), channel_id=1, source_target_pairs={{0,2},{1,3},{2,0},{3,1},{4,6},{5,7},{6,4},{7,5},{8,10},{9,11},{10,... | collective-permute-start | bytes 129032 | tf_op jit(solution)/shard_map/ppermute | solution.py:324
  23.4 6.5 %collective-permute-start.16 = (bf16[8,2688]{1,0:T(8,128)(2,1)S(1)}, bf16[8,2688]{1,0:T(8,128)(2,1)S(1)}, u32[]{:S(2)}, u32[]{:S(2)}) collective-permute-start(bf16[8,2688]{1,0:T(8,128)(2,1)S(1)} %get-tuple-element.38), channel_id=1, source_target_pairs={{0,2},{1,3},{2,0},{3,1},{4,6},{5,7},{6,4},{7,5},{8,10},{9,11},{10,... | collective-permute-start | bytes 129032 | tf_op jit(solution)/shard_map/ppermute | solution.py:324
  23.9 7.3 %collective-permute-start.11 = (bf16[8,2688]{1,0:T(8,128)(2,1)S(1)}, bf16[8,2688]{1,0:T(8,128)(2,1)S(1)}, u32[]{:S(2)}, u32[]{:S(2)}) collective-permute-start(bf16[8,2688]{1,0:T(8,128)(2,1)S(1)} %get-tuple-element.32), channel_id=1, source_target_pairs={{0,2},{1,3},{2,0},{3,1},{4,6},{5,7},{6,4},{7,5},{8,10},{9,11},{10,... | collective-permute-start | bytes 129032 | tf_op jit(solution)/shard_map/ppermute | solution.py:324
  25.9 5.9 %collective-permute-start.13 = (bf16[8,2688]{1,0:T(8,128)(2,1)S(1)}, bf16[8,2688]{1,0:T(8,128)(2,1)S(1)}, u32[]{:S(2)}, u32[]{:S(2)}) collective-permute-start(bf16[8,2688]{1,0:T(8,128)(2,1)S(1)} %merge.6), channel_id=1, source_target_pairs={{0,12},{1,13},{2,14},{3,15},{4,8},{5,9},{6,10},{7,11},{8,4},{9,5},... | collective-permute-start | bytes 129032 | tf_op jit(solution)/shard_map/ppermute | solution.py:324
  29.8 5.0 %collective-permute-start.15 = (bf16[8,2688]{1,0:T(8,128)(2,1)S(1)}, bf16[8,2688]{1,0:T(8,128)(2,1)S(1)}, u32[]{:S(2)}, u32[]{:S(2)}) collective-permute-start(bf16[8,2688]{1,0:T(8,128)(2,1)S(1)} %merge.7), channel_id=1, source_target_pairs={{0,8},{1,9},{2,10},{3,11},{4,12},{5,13},{6,14},{7,15},{8,0},{9,1},... | collective-permute-start | bytes 129032 | tf_op jit(solution)/shard_map/ppermute | solution.py:324
  30.0 4.8 %collective-permute-start.17 = (bf16[8,2688]{1,0:T(8,128)(2,1)S(1)}, bf16[8,2688]{1,0:T(8,128)(2,1)S(1)}, u32[]{:S(2)}, u32[]{:S(2)}) collective-permute-start(bf16[8,2688]{1,0:T(8,128)(2,1)S(1)} %merge.8), channel_id=1, source_target_pairs={{0,4},{1,5},{2,6},{3,7},{4,0},{5,1},{6,2},{7,3},{8,12},{9,13},{10,... | collective-permute-start | bytes 129032 | tf_op jit(solution)/shard_map/ppermute | solution.py:324

commit v20 on v15

--- a/solution.py
+++ b/solution.py
@@ -59,10 +59,9 @@
 
 
 def attend_kernel(sizes, scale, bias_ref, q_ref, k_ref, v_ref, outs, top_acc, mass_acc):
-    tile, steps, group = sizes
+    tile, steps, group, line_rows = sizes
     lines = len(outs)
     rows = tile * lines
-    line_rows = outs[0].shape[0]
     wide = PACK * HD
     contract_last = (((1,), (1,)), ((), ()))
     contract_first = (((0,), (0,)), ((), ()))
@@ -131,27 +130,35 @@
     lax.fori_loop(0, line_rows // tile, row_tile, 0)
 
 
-def attend(plane, lines, kind, keys, values, bias, after=()):
+def attend(plane, lines, kind, keys, values, bias, after=(), extra=0):
     rows, columns = plane.shape[0] // lines, plane.shape[1]
     heads = columns // HD
     pairs = heads // PACK
     group = next(g for g in (10, 5, 4, 3, 2, 1) if pairs % g == 0)
     tile = next(t for t in (32, 16, rows) if rows % t == 0)
     width = columns + STAT
+    more = -(-extra // 16) * 16
     scale = math.log2(math.e) / math.sqrt(HD)
 
     def body(*refs):
         work = refs[4 + len(after) :]
         attend_kernel(
-            (tile, pairs // group, group), scale, *refs[:4], work[:lines], *work[lines:]
+            (tile, pairs // group, group, rows), scale, *refs[:4], work[:lines], *work[lines:]
         )
+        if extra:
+            for home, out in list(zip(refs[4:], work[:lines]))[1:]:
+                block = home[:extra, :].astype(F32)
+                block = jnp.concatenate([block, jnp.zeros((more - extra, width), F32)], axis=0)
+                out[rows:, :] = block.astype(out.dtype)
 
     return pl.pallas_call(
         body,
         in_specs=[pl.BlockSpec(memory_space=pltpu.VMEM)] * 4
-        + [pl.BlockSpec(memory_space=pl.ANY)] * len(after),
+        + [pl.BlockSpec(memory_space=pltpu.VMEM if extra else pl.ANY)] * len(after),
         out_specs=[pl.BlockSpec(memory_space=pltpu.VMEM)] * lines,
-        out_shape=[jax.ShapeDtypeStruct((rows, width), kind)] * lines,
+        out_shape=[
+            jax.ShapeDtypeStruct((rows + (more if b else 0), width), kind) for b in range(lines)
+        ],
         scratch_shapes=[pltpu.VMEM((STAT, PACK * tile * lines), F32)] * 2,
         compiler_params=pltpu.CompilerParams(vmem_limit_bytes=40 * 1024 * 1024),
         cost_estimate=pl.CostEstimate(
@@ -258,6 +265,39 @@
     return call_merge(body, ins, [jax.ShapeDtypeStruct((per, width), kind) for kind in kinds])
 
 
+def merge_line(home, got, away, heads, tok):
+    rows, width = home.shape
+    per = -(-tok // 16) * 16
+
+    def body(home_ref, got_ref, away_ref, *outs):
+        get = lambda ref, start, n: lambda cols: ref[start : start + n, cols].astype(F32)
+        for cols, total in merged([get(home_ref, 0, rows), get(got_ref, 0, rows)], heads, False):
+            for j, out in enumerate(outs[:-1]):
+                out[:, cols] = total[j * tok : (j + 1) * tok].astype(out.dtype)
+        for cols, total in merged([get(away_ref, 0, per), get(got_ref, rows, per)], heads, False):
+            outs[-1][:, cols] = total[:tok].astype(outs[-1].dtype)
+
+    shapes = [jax.ShapeDtypeStruct((tok, width), BF16)] * (rows // tok + 1)
+    return call_merge(body, [home, got, away], shapes)
+
+
+def merge_own(own, last, first, cores, heads):
+    n = len(last)
+
+    def body(*refs):
+        out = refs[-1]
+        on_last = lax.rem(lax.axis_index("seq"), cores) == cores - 1
+
+        def either(one, other):
+            return lambda cols: jnp.where(on_last, one[:, cols], other[:, cols]).astype(F32)
+
+        parts = [getter(refs[0])] + [either(refs[1 + i], refs[1 + n + i]) for i in range(n)]
+        for cols, total in merged(parts, heads, False):
+            out[:, cols] = total.astype(out.dtype)
+
+    return call_merge(body, [own, *last, *first], [jax.ShapeDtypeStruct(own.shape, F32)])[0]
+
+
 def finish(ins, heads):
     rows = ins[0].shape[0]
 
@@ -301,6 +341,7 @@
     a_n, b_n, c_n = shape
     heads = queries.shape[1] // HD
     tok = queries.shape[0]
+    tok = queries.shape[0]
 
     def fetch(x, *by):
         return lax.ppermute(x, "seq", partner_perm(shape, by, False))
@@ -316,21 +357,41 @@
     )
     plane = join([x for pieces in lines for x in pieces])
     planes = [plane] + [fetch(plane, 0, 0, c) for c in range(1, c_n)]
+    shared = c_n == 2 and b_n > 1
     sums = []
     for c, rows in enumerate(planes):
-        sums += attend(rows, b_n, BF16 if c else F32, keys, values, bias, sums[:1])
+        extra = tok if c and shared else 0
+        sums += attend(rows, b_n, BF16 if c else F32, keys, values, bias, sums[:b_n], extra)
 
     def over_cores(b, kind):
         got = [give(sums[c * b_n + b], 0, 0, c) for c in range(1, c_n)]
+        if b and shared:
+            return merge_line(sums[b], got[0], sums[b_n + b], heads, tok)
         return merge_rows([sums[b]] + got, heads, a_n, [kind] * a_n)
 
-    got = [[give(x, 0, b, 0) for x in over_cores(b, BF16)] for b in range(1, b_n)]
+    def give_from_last(x, by, core):
+        pairs = partner_perm(shape, (0, by, 0), True)
+        pairs = [(i, j - j % c_n + core) for i, j in pairs if i % c_n == c_n - 1]
+        return lax.ppermute(x, "seq", pairs)
+
+    got, first = [], [[], []]
+    for b in range(1, b_n):
+        pieces = over_cores(b, BF16)
+        start = 1 if shared else 0
+        got.append([None] * start + [give(x, 0, b, 0) for x in pieces[start:a_n]])
+        if shared:
+            first[0].append(give_from_last(pieces[0], b, c_n - 1))
+            first[1].append(give_from_last(pieces[a_n], b, 0))
     own = over_cores(0, F32)
-    total = [[own[s]] + [pieces[s] for pieces in got] for s in range(a_n)]
-    last = [
-        give(merge_rows(total[s], heads, 1, [BF16])[0], far_first[s], 0, 0) for s in range(1, a_n)
-    ]
-    return finish([*merge_rows(total[0], heads, 1, [F32]), *last], heads)
+    last = []
+    for s in range(1, a_n):
+        total = [own[s]] + [pieces[s] for pieces in got]
+        last.append(give(merge_rows(total, heads, 1, [BF16])[0], far_first[s], 0, 0))
+    if shared:
+        mine = merge_own(own[0], *first, c_n, heads)
+    else:
+        mine = merge_rows([own[0]] + [pieces[0] for pieces in got], heads, 1, [F32])[0]
+    return finish([mine, *last], heads)
 
 
 def solution(mesh):

time: 34 us -> 36.3 us (1.068)
  waiting for transfers between devices: 4.52 us -> 5.67 us
  starting transfers between devices: 21 us -> 22.1 us
    ppermute x0 -> x2, starting transfers between devices: none -> 1.96 us  [give_from_last(): return lax.ppermute(x, 'seq', pairs)]
    ppermute x9 -> x8, waiting for transfers between devices: 4 us -> 5.15 us  [give(): return lax.ppermute(x, 'seq', partner_perm(shape, by, True))]
    ppermute x9 -> x8, starting transfers between devices: 9.36 us -> 8.43 us  [give(): return lax.ppermute(x, 'seq', partner_perm(shape, by, True))]
  transfers between devices with their start and end apart: 17 -> 18, of which waited for: 5 -> 6; matrix products, arithmetic and copies ran while one was open for 0% -> 0% of each run, Pallas kernels for 16% -> 16%
where the time goes in v20:
time: 36.3 us; the launch traced here: 36.1 us
  starting transfers between devices  22.1 us (61%)
  Pallas kernels  8.27 us (23%)
  waiting for transfers between devices  5.67 us (16%)
    ppermute x8, starting transfers between devices, fetch(): return lax.ppermute(x, 'seq', partner_perm(shape, by, False))  11.7 us
    ppermute x8, starting transfers between devices, give(): return lax.ppermute(x, 'seq', partner_perm(shape, by, True))  8.43 us
    ppermute x8, waiting for transfers between devices, give(): return lax.ppermute(x, 'seq', partner_perm(shape, by, True))  5.15 us
    pallas_call x2, Pallas kernels, attend(): pl.pallas_call(body, in_specs=[pl.BlockSpec(memory_space=pltpu.VMEM)] * 4...  3.46 us
    pallas_call x1, Pallas kernels, load(): pl.pallas_call(body, in_specs=[in_hbm] * len(held) + [pl.BlockSpec(memory...  2.65 us
    pallas_call x8, Pallas kernels, call_merge(): pl.pallas_call(body, in_specs=[pl.BlockSpec(memory_space=pltpu.VMEM)] * l...  2.16 us
    ppermute x2, starting transfers between devices, give_from_last(): return lax.ppermute(x, 'seq', pairs)  1.96 us
  transfers between devices with their start and end apart: 18, of which 6 were waited for; matrix products, arithmetic and copies ran while one was open for 0% of the time, Pallas kernels for 16%

profile of v20, /device:TPU:0, one launch (start us, length us, event | category | flops | bytes accessed | tf_op | source)
XLA Modules:
  0.0 36.1 jit_solution(7581816717920233761)
XLA Ops:
  0.0 5.0 %collective-permute-start.1 = (bf16[8,2560]{1,0:T(8,128)(2,1)}, bf16[8,2560]{1,0:T(8,128)(2,1)S(1)}, u32[]{:S(2)}, u32[]{:S(2)}) collective-permute-start(bf16[8,2560]{1,0:T(8,128)(2,1)} %refs_5_.1), channel_id=1, source_target_pairs={{12,0},{13,1},{14,2},{15,3},{8,4},{9,5},{10,6},{11,7},{4,8},{5,9},... | collective-permute-start | bytes 122888 | tf_op jit(solution)/shard_map/ppermute | solution.py:347
  5.1 0.6 %collective-permute-start.2 = (bf16[8,2560]{1,0:T(8,128)(2,1)}, bf16[8,2560]{1,0:T(8,128)(2,1)S(1)}, u32[]{:S(2)}, u32[]{:S(2)}) collective-permute-start(bf16[8,2560]{1,0:T(8,128)(2,1)} %refs_5_.1), channel_id=1, source_target_pairs={{8,0},{9,1},{10,2},{11,3},{12,4},{13,5},{14,6},{15,7},{0,8},{1,9},... | collective-permute-start | bytes 122888 | tf_op jit(solution)/shard_map/ppermute | solution.py:347
  5.6 1.8 %collective-permute-start.3 = (bf16[8,2560]{1,0:T(8,128)(2,1)}, bf16[8,2560]{1,0:T(8,128)(2,1)S(1)}, u32[]{:S(2)}, u32[]{:S(2)}) collective-permute-start(bf16[8,2560]{1,0:T(8,128)(2,1)} %refs_5_.1), channel_id=1, source_target_pairs={{2,0},{3,1},{0,2},{1,3},{6,4},{7,5},{4,6},{5,7},{10,8},{11,9},{8,1... | collective-permute-start | bytes 122888 | tf_op jit(solution)/shard_map/ppermute | solution.py:347
  7.4 1.6 %collective-permute-start.4 = (bf16[8,2560]{1,0:T(8,128)(2,1)S(1)}, bf16[8,2560]{1,0:T(8,128)(2,1)S(1)}, u32[]{:S(2)}, u32[]{:S(2)}) collective-permute-start(bf16[8,2560]{1,0:T(8,128)(2,1)S(1)} %collective-permute-done.1.refs_1_), channel_id=1, source_target_pairs={{2,0},{3,1},{0,2},{1,3},{6,4},{7,5},{4,6},{5,7},{10,8},{11,9},{8,1... | collective-permute-start | bytes 122888 | tf_op jit(solution)/shard_map/ppermute | solution.py:347
  9.0 0.3 collective-permute-done.refs_6_.refs_3_
  9.3 1.5 %collective-permute-start.6 = (bf16[8,2560]{1,0:T(8,128)(2,1)S(1)}, bf16[8,2560]{1,0:T(8,128)(2,1)S(1)}, u32[]{:S(2)}, u32[]{:S(2)}) collective-permute-start(bf16[8,2560]{1,0:T(8,128)(2,1)S(1)} %collective-permute-done.refs_6_.refs_3_), channel_id=1, source_target_pairs={{2,0},{3,1},{0,2},{1,3},{6,4},{7,5},{4,6},{5,7},{10,8},{11,9},{8,1... | collective-permute-start | bytes 122888 | tf_op jit(solution)/shard_map/ppermute | solution.py:347
  10.8 1.1 %collective-permute-start.5 = (bf16[8,2560]{1,0:T(8,128)(2,1)S(1)}, bf16[8,2560]{1,0:T(8,128)(2,1)S(1)}, u32[]{:S(2)}, u32[]{:S(2)}) collective-permute-start(bf16[8,2560]{1,0:T(8,128)(2,1)S(1)} %collective-permute-done.2.refs_2_), channel_id=1, source_target_pairs={{2,0},{3,1},{0,2},{1,3},{6,4},{7,5},{4,6},{5,7},{10,8},{11,9},{8,1... | collective-permute-start | bytes 122888 | tf_op jit(solution)/shard_map/ppermute | solution.py:347
  11.9 2.6 %load.1 = (bf16[528,2560]{1,0:T(8,128)(2,1)S(1)}, bf16[528,2560]{1,0:T(8,128)(2,1)S(1)}, f32[528,128]{1,0:T(8,128)S(1)}, bf16[8,2560]{1,0:T(8,128)(2,1)S(1)}) custom-call(bf16[512,2560]{1,0:T(8,128)(2,1)} %refs_0_.1, bf16[512,2560]{1,0:T(8,128)(2,1)} %refs_1_.1, bf16[8,2560]{1,0:T(8,128)(2,1)} %refs_2_.1, bf16[8,2560]{1,0:T(8,128)(2,1)} %refs_3_.1, ...), custom_call_target="tpu_custom_call" | custom-call | bytes 10485760 | tf_op jit(solution)/shard_map/load/pallas_call | solution.py:217
  14.6 0.2 collective-permute-done.5.refs_6_
  14.9 1.7 %attend.2 = (f32[32,2688]{1,0:T(8,128)S(1)}, f32[32,2688]{1,0:T(8,128)S(1)}) custom-call(f32[528,128]{1,0:T(8,128)S(1)} %get-tuple-element.22.refs_0_, bf16[64,2560]{1,0:T(8,128)(2,1)S(1)} %merge.8.refs_1_, bf16[528,2560]{1,0:T(8,128)(2,1)S(1)} %get-tuple-element.24.refs_2_, bf16[528,2560]{1,0:T(8,128)(2,1)S(1)} %get-tuple-element.25.refs_3_), custom_call_target="tpu_custom_call" | custom-call | flops 346030080 | bytes 5406720 | tf_op jit(solution)/shard_map/attend/pallas_call | solution.py:154
  16.6 1.7 %attend.3 = (bf16[32,2688]{1,0:T(8,128)(2,1)S(1)}, bf16[48,2688]{1,0:T(8,128)(2,1)S(1)}) custom-call(f32[528,128]{1,0:T(8,128)S(1)} %get-tuple-element.22.refs_0_, bf16[64,2560]{1,0:T(8,128)(2,1)S(1)} %collective-permute-done.7.refs_1_, bf16[528,2560]{1,0:T(8,128)(2,1)S(1)} %get-tuple-element.24.refs_2_, bf16[528,2560]{1,0:T(8,128)(2,1)S(1)} %get-tuple-element.25.refs_3_, ...), custom_call_target="tpu_custom_call" | custom-call | flops 346030080 | bytes 5406720 | tf_op jit(solution)/shard_map/attend/pallas_call | solution.py:154
  18.4 0.6 %collective-permute-start.9 = (bf16[48,2688]{1,0:T(8,128)(2,1)S(1)}, bf16[48,2688]{1,0:T(8,128)(2,1)S(1)}, u32[]{:S(2)}, u32[]{:S(2)}) collective-permute-start(bf16[48,2688]{1,0:T(8,128)(2,1)S(1)} %get-tuple-element.30.away_ref), channel_id=1, source_target_pairs={{0,1},{1,0},{2,3},{3,2},{4,5},{5,4},{6,7},{7,6},{8,9},{9,8},{10,11... | collective-permute-start | bytes 774152 | tf_op jit(solution)/shard_map/ppermute | solution.py:350
  18.9 0.1 collective-permute-start.8
  19.0 1.1 %collective-permute-done.9.got_ref = bf16[48,2688]{1,0:T(8,128)(2,1)S(1)} collective-permute-done((bf16[48,2688]{1,0:T(8,128)(2,1)S(1)}, bf16[48,2688]{1,0:T(8,128)(2,1)S(1)}, u32[]{:S(2)}, u32[]{:S(2)}) %collective-permute-start.9) | collective-permute-done | bytes 258080 | tf_op jit(solution)/shard_map/ppermute | solution.py:350
  20.1 0.4 %merge.10 = (bf16[8,2688]{1,0:T(8,128)(2,1)S(1)}, bf16[8,2688]{1,0:T(8,128)(2,1)S(1)}, bf16[8,2688]{1,0:T(8,128)(2,1)S(1)}, bf16[8,2688]{1,0:T(8,128)(2,1)S(1)}, bf16[8,2688]{1,0:T(8,128)(2,1)S(1)}) custom-call(f32[32,2688]{1,0:T(8,128)S(1)} %get-tuple-element.27.refs_5_.home_ref, bf16[48,2688]{1,0:T(8,128)(2,1)S(1)} %collective-permute-done.9.got_ref, ...), custom_call_target="tpu_custom_call" | custom-call | flops 1376256 | bytes 1376256 | tf_op jit(solution)/shard_map/merge/pallas_call | solution.py:326
  20.5 1.2 %collective-permute-start.12 = (bf16[8,2688]{1,0:T(8,128)(2,1)S(1)}, bf16[8,2688]{1,0:T(8,128)(2,1)S(1)}, u32[]{:S(2)}, u32[]{:S(2)}) collective-permute-start(bf16[8,2688]{1,0:T(8,128)(2,1)S(1)} %get-tuple-element.34), channel_id=1, source_target_pairs={{0,2},{1,3},{2,0},{3,1},{4,6},{5,7},{6,4},{7,5},{8,10},{9,11},{10,... | collective-permute-start | bytes 129032 | tf_op jit(solution)/shard_map/ppermute | solution.py:350
  21.6 0.9 %collective-permute-start.14 = (bf16[8,2688]{1,0:T(8,128)(2,1)S(1)}, bf16[8,2688]{1,0:T(8,128)(2,1)S(1)}, u32[]{:S(2)}, u32[]{:S(2)}) collective-permute-start(bf16[8,2688]{1,0:T(8,128)(2,1)S(1)} %get-tuple-element.36), channel_id=1, source_target_pairs={{0,2},{1,3},{2,0},{3,1},{4,6},{5,7},{6,4},{7,5},{8,10},{9,11},{10,... | collective-permute-start | bytes 129032 | tf_op jit(solution)/shard_map/ppermute | solution.py:350
  22.6 1.1 %collective-permute-start.16 = (bf16[8,2688]{1,0:T(8,128)(2,1)S(1)}, bf16[8,2688]{1,0:T(8,128)(2,1)S(1)}, u32[]{:S(2)}, u32[]{:S(2)}) collective-permute-start(bf16[8,2688]{1,0:T(8,128)(2,1)S(1)} %get-tuple-element.38), channel_id=1, source_target_pairs={{0,2},{1,3},{2,0},{3,1},{4,6},{5,7},{6,4},{7,5},{8,10},{9,11},{10,... | collective-permute-start | bytes 129032 | tf_op jit(solution)/shard_map/ppermute | solution.py:350
  23.7 0.3 merge.9
  24.0 0.7 %collective-permute-start.10 = (bf16[8,2688]{1,0:T(8,128)(2,1)S(1)}, bf16[8,2688]{1,0:T(8,128)(2,1)S(1)}, u32[]{:S(2)}, u32[]{:S(2)}) collective-permute-start(bf16[8,2688]{1,0:T(8,128)(2,1)S(1)} %get-tuple-element.31), channel_id=1, source_target_pairs={{1,3},{3,1},{5,7},{7,5},{9,11},{11,9},{13,15},{15,13},{17,19},{19,... | collective-permute-start | bytes 129032 | tf_op jit(solution)/shard_map/ppermute | solution.py:375
  24.6 1.3 %collective-permute-start.11 = (bf16[8,2688]{1,0:T(8,128)(2,1)S(1)}, bf16[8,2688]{1,0:T(8,128)(2,1)S(1)}, u32[]{:S(2)}, u32[]{:S(2)}) collective-permute-start(bf16[8,2688]{1,0:T(8,128)(2,1)S(1)} %get-tuple-element.32), channel_id=1, source_target_pairs={{1,2},{3,0},{5,6},{7,4},{9,10},{11,8},{13,14},{15,12},{17,18},{19,... | collective-permute-start | bytes 129032 | tf_op jit(solution)/shard_map/ppermute | solution.py:375
  25.9 0.1 merge.12
  26.1 3.0 %collective-permute-start.13 = (bf16[8,2688]{1,0:T(8,128)(2,1)S(1)}, bf16[8,2688]{1,0:T(8,128)(2,1)S(1)}, u32[]{:S(2)}, u32[]{:S(2)}) collective-permute-start(bf16[8,2688]{1,0:T(8,128)(2,1)S(1)} %merge.12), channel_id=1, source_target_pairs={{0,12},{1,13},{2,14},{3,15},{4,8},{5,9},{6,10},{7,11},{8,4},{9,5},... | collective-permute-start | bytes 129032 | tf_op jit(solution)/shard_map/ppermute | solution.py:350
  29.1 0.1 merge.13
  29.2 0.4 %collective-permute-start.15 = (bf16[8,2688]{1,0:T(8,128)(2,1)S(1)}, bf16[8,2688]{1,0:T(8,128)(2,1)S(1)}, u32[]{:S(2)}, u32[]{:S(2)}) collective-permute-start(bf16[8,2688]{1,0:T(8,128)(2,1)S(1)} %merge.13), channel_id=1, source_target_pairs={{0,8},{1,9},{2,10},{3,11},{4,12},{5,13},{6,14},{7,15},{8,0},{9,1},... | collective-permute-start | bytes 129032 | tf_op jit(solution)/shard_map/ppermute | solution.py:350
  29.7 0.1 merge.14
  29.8 1.2 %collective-permute-start.17 = (bf16[8,2688]{1,0:T(8,128)(2,1)S(1)}, bf16[8,2688]{1,0:T(8,128)(2,1)S(1)}, u32[]{:S(2)}, u32[]{:S(2)}) collective-permute-start(bf16[8,2688]{1,0:T(8,128)(2,1)S(1)} %merge.14), channel_id=1, source_target_pairs={{0,4},{1,5},{2,6},{3,7},{4,0},{5,1},{6,2},{7,3},{8,12},{9,13},{10,... | collective-permute-start | bytes 129032 | tf_op jit(solution)/shard_map/ppermute | solution.py:350
  31.0 0.2 merge.11.refs_0_
  31.2 0.9 %collective-permute-done.13.refs_1_ = bf16[8,2688]{1,0:T(8,128)(2,1)S(1)} collective-permute-done((bf16[8,2688]{1,0:T(8,128)(2,1)S(1)}, bf16[8,2688]{1,0:T(8,128)(2,1)S(1)}, u32[]{:S(2)}, u32[]{:S(2)}) %collective-permute-start.13) | collective-permute-done | bytes 43040 | tf_op jit(solution)/shard_map/ppermute | solution.py:350
  32.1 2.5 %collective-permute-done.15.refs_2_ = bf16[8,2688]{1,0:T(8,128)(2,1)S(1)} collective-permute-done((bf16[8,2688]{1,0:T(8,128)(2,1)S(1)}, bf16[8,2688]{1,0:T(8,128)(2,1)S(1)}, u32[]{:S(2)}, u32[]{:S(2)}) %collective-permute-start.15) | collective-permute-done | bytes 43040 | tf_op jit(solution)/shard_map/ppermute | solution.py:350
  34.6 0.6 %collective-permute-done.17.refs_3_ = bf16[8,2688]{1,0:T(8,128)(2,1)S(1)} collective-permute-done((bf16[8,2688]{1,0:T(8,128)(2,1)S(1)}, bf16[8,2688]{1,0:T(8,128)(2,1)S(1)}, u32[]{:S(2)}, u32[]{:S(2)}) %collective-permute-start.17) | collective-permute-done | bytes 43040 | tf_op jit(solution)/shard_map/ppermute | solution.py:350
  35.2 0.9 %merge.15 = bf16[8,2560]{1,0:T(8,128)(2,1)} custom-call(f32[8,2688]{1,0:T(8,128)S(1)} %merge.11.refs_0_, bf16[8,2688]{1,0:T(8,128)(2,1)S(1)} %collective-permute-done.13.refs_1_, bf16[8,2688]{1,0:T(8,128)(2,1)S(1)} %collective-permute-done.15.refs_2_, bf16[8,2688]{1,0:T(8,128)(2,1)S(1)} %collective-permute-done.17.refs_3_), custom_call_target="tpu_custom_call" | custom-call | flops 344064 | bytes 344064 | tf_op jit(solution)/shard_map/merge/pallas_call | solution.py:326
  (15 shorter events, 0.1 us)
Async XLA Ops:
  0.0 7.4 %collective-permute-start.1 = (bf16[8,2560]{1,0:T(8,128)(2,1)}, bf16[8,2560]{1,0:T(8,128)(2,1)S(1)}, u32[]{:S(2)}, u32[]{:S(2)}) collective-permute-start(bf16[8,2560]{1,0:T(8,128)(2,1)} %refs_5_.1), channel_id=1, source_target_pairs={{12,0},{13,1},{14,2},{15,3},{8,4},{9,5},{10,6},{11,7},{4,8},{5,9},... | collective-permute-start | bytes 122888 | tf_op jit(solution)/shard_map/ppermute | solution.py:347
  5.0 4.2 %collective-permute-start = (bf16[8,2560]{1,0:T(8,128)(2,1)}, bf16[8,2560]{1,0:T(8,128)(2,1)S(1)}, u32[]{:S(2)}, u32[]{:S(2)}) collective-permute-start(bf16[8,2560]{1,0:T(8,128)(2,1)} %refs_5_.1), channel_id=1, source_target_pairs={{4,0},{5,1},{6,2},{7,3},{0,4},{1,5},{2,6},{3,7},{12,8},{13,9},{14,... | collective-permute-start | bytes 122888 | tf_op jit(solution)/shard_map/ppermute | solution.py:347
  5.1 5.7 %collective-permute-start.2 = (bf16[8,2560]{1,0:T(8,128)(2,1)}, bf16[8,2560]{1,0:T(8,128)(2,1)S(1)}, u32[]{:S(2)}, u32[]{:S(2)}) collective-permute-start(bf16[8,2560]{1,0:T(8,128)(2,1)} %refs_5_.1), channel_id=1, source_target_pairs={{8,0},{9,1},{10,2},{11,3},{12,4},{13,5},{14,6},{15,7},{0,8},{1,9},... | collective-permute-start | bytes 122888 | tf_op jit(solution)/shard_map/ppermute | solution.py:347
  5.6 8.9 %collective-permute-start.3 = (bf16[8,2560]{1,0:T(8,128)(2,1)}, bf16[8,2560]{1,0:T(8,128)(2,1)S(1)}, u32[]{:S(2)}, u32[]{:S(2)}) collective-permute-start(bf16[8,2560]{1,0:T(8,128)(2,1)} %refs_5_.1), channel_id=1, source_target_pairs={{2,0},{3,1},{0,2},{1,3},{6,4},{7,5},{4,6},{5,7},{10,8},{11,9},{8,1... | collective-permute-start | bytes 122888 | tf_op jit(solution)/shard_map/ppermute | solution.py:347
  7.4 7.2 %collective-permute-start.4 = (bf16[8,2560]{1,0:T(8,128)(2,1)S(1)}, bf16[8,2560]{1,0:T(8,128)(2,1)S(1)}, u32[]{:S(2)}, u32[]{:S(2)}) collective-permute-start(bf16[8,2560]{1,0:T(8,128)(2,1)S(1)} %collective-permute-done.1.refs_1_), channel_id=1, source_target_pairs={{2,0},{3,1},{0,2},{1,3},{6,4},{7,5},{4,6},{5,7},{10,8},{11,9},{8,1... | collective-permute-start | bytes 122888 | tf_op jit(solution)/shard_map/ppermute | solution.py:347
  9.3 5.3 %collective-permute-start.6 = (bf16[8,2560]{1,0:T(8,128)(2,1)S(1)}, bf16[8,2560]{1,0:T(8,128)(2,1)S(1)}, u32[]{:S(2)}, u32[]{:S(2)}) collective-permute-start(bf16[8,2560]{1,0:T(8,128)(2,1)S(1)} %collective-permute-done.refs_6_.refs_3_), channel_id=1, source_target_pairs={{2,0},{3,1},{0,2},{1,3},{6,4},{7,5},{4,6},{5,7},{10,8},{11,9},{8,1... | collective-permute-start | bytes 122888 | tf_op jit(solution)/shard_map/ppermute | solution.py:347
  10.8 4.0 %collective-permute-start.5 = (bf16[8,2560]{1,0:T(8,128)(2,1)S(1)}, bf16[8,2560]{1,0:T(8,128)(2,1)S(1)}, u32[]{:S(2)}, u32[]{:S(2)}) collective-permute-start(bf16[8,2560]{1,0:T(8,128)(2,1)S(1)} %collective-permute-done.2.refs_2_), channel_id=1, source_target_pairs={{2,0},{3,1},{0,2},{1,3},{6,4},{7,5},{4,6},{5,7},{10,8},{11,9},{8,1... | collective-permute-start | bytes 122888 | tf_op jit(solution)/shard_map/ppermute | solution.py:347
  14.8 1.8 %collective-permute-start.7 = (bf16[64,2560]{1,0:T(8,128)(2,1)S(1)}, bf16[64,2560]{1,0:T(8,128)(2,1)S(1)}, u32[]{:S(2)}, u32[]{:S(2)}) collective-permute-start(bf16[64,2560]{1,0:T(8,128)(2,1)S(1)} %merge.8.refs_1_), channel_id=1, source_target_pairs={{1,0},{0,1},{3,2},{2,3},{5,4},{4,5},{7,6},{6,7},{9,8},{8,9},{11,10... | collective-permute-start | bytes 983048 | tf_op jit(solution)/shard_map/ppermute | solution.py:347
  18.4 1.7 %collective-permute-start.9 = (bf16[48,2688]{1,0:T(8,128)(2,1)S(1)}, bf16[48,2688]{1,0:T(8,128)(2,1)S(1)}, u32[]{:S(2)}, u32[]{:S(2)}) collective-permute-start(bf16[48,2688]{1,0:T(8,128)(2,1)S(1)} %get-tuple-element.30.away_ref), channel_id=1, source_target_pairs={{0,1},{1,0},{2,3},{3,2},{4,5},{5,4},{6,7},{7,6},{8,9},{9,8},{10,11... | collective-permute-start | bytes 774152 | tf_op jit(solution)/shard_map/ppermute | solution.py:350
  18.9 4.7 %collective-permute-start.8 = (bf16[32,2688]{1,0:T(8,128)(2,1)S(1)}, bf16[32,2688]{1,0:T(8,128)(2,1)S(1)}, u32[]{:S(2)}, u32[]{:S(2)}) collective-permute-start(bf16[32,2688]{1,0:T(8,128)(2,1)S(1)} %get-tuple-element.28), channel_id=1, source_target_pairs={{0,1},{1,0},{2,3},{3,2},{4,5},{5,4},{6,7},{7,6},{8,9},{9,8},{10,11... | collective-permute-start | bytes 516104 | tf_op jit(solution)/shard_map/ppermute | solution.py:350
  20.5 5.5 %collective-permute-start.12 = (bf16[8,2688]{1,0:T(8,128)(2,1)S(1)}, bf16[8,2688]{1,0:T(8,128)(2,1)S(1)}, u32[]{:S(2)}, u32[]{:S(2)}) collective-permute-start(bf16[8,2688]{1,0:T(8,128)(2,1)S(1)} %get-tuple-element.34), channel_id=1, source_target_pairs={{0,2},{1,3},{2,0},{3,1},{4,6},{5,7},{6,4},{7,5},{8,10},{9,11},{10,... | collective-permute-start | bytes 129032 | tf_op jit(solution)/shard_map/ppermute | solution.py:350
  21.6 7.4 %collective-permute-start.14 = (bf16[8,2688]{1,0:T(8,128)(2,1)S(1)}, bf16[8,2688]{1,0:T(8,128)(2,1)S(1)}, u32[]{:S(2)}, u32[]{:S(2)}) collective-permute-start(bf16[8,2688]{1,0:T(8,128)(2,1)S(1)} %get-tuple-element.36), channel_id=1, source_target_pairs={{0,2},{1,3},{2,0},{3,1},{4,6},{5,7},{6,4},{7,5},{8,10},{9,11},{10,... | collective-permute-start | bytes 129032 | tf_op jit(solution)/shard_map/ppermute | solution.py:350
  22.6 7.1 %collective-permute-start.16 = (bf16[8,2688]{1,0:T(8,128)(2,1)S(1)}, bf16[8,2688]{1,0:T(8,128)(2,1)S(1)}, u32[]{:S(2)}, u32[]{:S(2)}) collective-permute-start(bf16[8,2688]{1,0:T(8,128)(2,1)S(1)} %get-tuple-element.38), channel_id=1, source_target_pairs={{0,2},{1,3},{2,0},{3,1},{4,6},{5,7},{6,4},{7,5},{8,10},{9,11},{10,... | collective-permute-start | bytes 129032 | tf_op jit(solution)/shard_map/ppermute | solution.py:350
  24.0 7.0 %collective-permute-start.10 = (bf16[8,2688]{1,0:T(8,128)(2,1)S(1)}, bf16[8,2688]{1,0:T(8,128)(2,1)S(1)}, u32[]{:S(2)}, u32[]{:S(2)}) collective-permute-start(bf16[8,2688]{1,0:T(8,128)(2,1)S(1)} %get-tuple-element.31), channel_id=1, source_target_pairs={{1,3},{3,1},{5,7},{7,5},{9,11},{11,9},{13,15},{15,13},{17,19},{19,... | collective-permute-start | bytes 129032 | tf_op jit(solution)/shard_map/ppermute | solution.py:375
  24.6 6.4 %collective-permute-start.11 = (bf16[8,2688]{1,0:T(8,128)(2,1)S(1)}, bf16[8,2688]{1,0:T(8,128)(2,1)S(1)}, u32[]{:S(2)}, u32[]{:S(2)}) collective-permute-start(bf16[8,2688]{1,0:T(8,128)(2,1)S(1)} %get-tuple-element.32), channel_id=1, source_target_pairs={{1,2},{3,0},{5,6},{7,4},{9,10},{11,8},{13,14},{15,12},{17,18},{19,... | collective-permute-start | bytes 129032 | tf_op jit(solution)/shard_map/ppermute | solution.py:375
  26.1 6.0 %collective-permute-start.13 = (bf16[8,2688]{1,0:T(8,128)(2,1)S(1)}, bf16[8,2688]{1,0:T(8,128)(2,1)S(1)}, u32[]{:S(2)}, u32[]{:S(2)}) collective-permute-start(bf16[8,2688]{1,0:T(8,128)(2,1)S(1)} %merge.12), channel_id=1, source_target_pairs={{0,12},{1,13},{2,14},{3,15},{4,8},{5,9},{6,10},{7,11},{8,4},{9,5},... | collective-permute-start | bytes 129032 | tf_op jit(solution)/shard_map/ppermute | solution.py:350
  29.2 5.4 %collective-permute-start.15 = (bf16[8,2688]{1,0:T(8,128)(2,1)S(1)}, bf16[8,2688]{1,0:T(8,128)(2,1)S(1)}, u32[]{:S(2)}, u32[]{:S(2)}) collective-permute-start(bf16[8,2688]{1,0:T(8,128)(2,1)S(1)} %merge.13), channel_id=1, source_target_pairs={{0,8},{1,9},{2,10},{3,11},{4,12},{5,13},{6,14},{7,15},{8,0},{9,1},... | collective-permute-start | bytes 129032 | tf_op jit(solution)/shard_map/ppermute | solution.py:350
  29.8 5.4 %collective-permute-start.17 = (bf16[8,2688]{1,0:T(8,128)(2,1)S(1)}, bf16[8,2688]{1,0:T(8,128)(2,1)S(1)}, u32[]{:S(2)}, u32[]{:S(2)}) collective-permute-start(bf16[8,2688]{1,0:T(8,128)(2,1)S(1)} %merge.14), channel_id=1, source_target_pairs={{0,4},{1,5},{2,6},{3,7},{4,0},{5,1},{6,2},{7,3},{8,12},{9,13},{10,... | collective-permute-start | bytes 129032 | tf_op jit(solution)/shard_map/ppermute | solution.py:350

commit v21 on v15

--- a/solution.py
+++ b/solution.py
@@ -56,6 +56,17 @@
 
 def lane_of(head):
     return head % PACK * (LANE // PACK) + head // PACK
+
+
+def loop(steps, body):
+    if steps == 1:
+        body(0, 0)
+    else:
+        lax.fori_loop(0, steps, body, 0)
+
+
+def span(start, size, unit):
+    return pl.ds(start if isinstance(start, int) else pl.multiple_of(start, unit), size)
 
 
 def attend_kernel(sizes, scale, bias_ref, q_ref, k_ref, v_ref, outs, top_acc, mass_acc):
@@ -69,14 +80,14 @@
     mine = [lax.broadcasted_iota(jnp.int32, (rows, wide), 1) // HD == k for k in range(PACK)]
 
     def row_tile(r, carry):
-        at = pl.ds(pl.multiple_of(r * tile, tile), tile)
-        in_plane = [pl.ds(pl.multiple_of(b * line_rows + r * tile, tile), tile) for b in range(lines)]
+        at = span(r * tile, tile, tile)
+        in_plane = [span(b * line_rows + r * tile, tile, tile) for b in range(lines)]
         top_acc[...] = jnp.zeros_like(top_acc)
         mass_acc[...] = jnp.zeros_like(mass_acc)
 
         def heads_of(step, carry):
             def columns(i):
-                return pl.ds(pl.multiple_of((step * group + i) * wide, HD), wide)
+                return span((step * group + i) * wide, wide, HD)
 
             def scores(i):
                 cols = columns(i)
@@ -98,8 +109,7 @@
                     weights, v_ref[:, columns(i)], contract_first, preferred_element_type=F32
                 )
                 for k in range(PACK):
-                    at_head = ((step * group + i) * PACK + k) * HD
-                    cols = pl.ds(pl.multiple_of(at_head, HD), HD)
+                    cols = span(((step * group + i) * PACK + k) * HD, HD, HD)
                     for b, o_ref in enumerate(outs):
                         start = k * rows + b * tile
                         one = both[start : start + tile, k * HD : (k + 1) * HD]
@@ -116,7 +126,7 @@
             gather_values(group - 1, weights)
             return carry
 
-        lax.fori_loop(0, steps, heads_of, 0)
+        loop(steps, heads_of)
         tops, masses = top_acc[...].T, mass_acc[...].T
         packed = 0.0
         for k in range(PACK):
@@ -128,7 +138,7 @@
             o_ref[at, width - STAT :] = packed[b * tile : (b + 1) * tile].astype(o_ref.dtype)
         return carry
 
-    lax.fori_loop(0, line_rows // tile, row_tile, 0)
+    loop(line_rows // tile, row_tile)
 
 
 def attend(plane, lines, kind, keys, values, bias, after=()):
@@ -258,6 +268,26 @@
     return call_merge(body, ins, [jax.ShapeDtypeStruct((per, width), kind) for kind in kinds])
 
 
+def merge_piece(lines, s, pieces, heads, tok, kind):
+    rows, width = tok, lines[0].shape[1]
+
+    def rows_of(ref):
+        start = s * rows
+        if ref.dtype == F32:
+            return lambda cols: ref[start : start + rows, cols]
+        first = start // 16 * 16
+        last = min(-(-(start + rows) // 16) * 16, ref.shape[0])
+        return lambda cols: ref[first:last, cols].astype(F32)[start - first :][:rows]
+
+    def body(*refs):
+        out = refs[-1]
+        parts = [rows_of(r) for r in refs[: len(lines)]] + [getter(r) for r in refs[len(lines) : -1]]
+        for cols, total in merged(parts, heads, False):
+            out[:, cols] = total.astype(out.dtype)
+
+    return call_merge(body, [*lines, *pieces], [jax.ShapeDtypeStruct((rows, width), kind)])[0]
+
+
 def finish(ins, heads):
     rows = ins[0].shape[0]
 
@@ -325,12 +355,13 @@
         return merge_rows([sums[b]] + got, heads, a_n, [kind] * a_n)
 
     got = [[give(x, 0, b, 0) for x in over_cores(b, BF16)] for b in range(1, b_n)]
-    own = over_cores(0, F32)
-    total = [[own[s]] + [pieces[s] for pieces in got] for s in range(a_n)]
-    last = [
-        give(merge_rows(total[s], heads, 1, [BF16])[0], far_first[s], 0, 0) for s in range(1, a_n)
-    ]
-    return finish([*merge_rows(total[0], heads, 1, [F32]), *last], heads)
+    own = [sums[0]] + [give(sums[c * b_n], 0, 0, c) for c in range(1, c_n)]
+
+    def total(s, kind):
+        return merge_piece(own, s, [pieces[s] for pieces in got], heads, tok, kind)
+
+    last = [give(total(s, BF16), far_first[s], 0, 0) for s in range(1, a_n)]
+    return finish([total(0, F32), *last], heads)
 
 
 def solution(mesh):

time: 34 us -> 33.9 us (level)
    pallas_call x8 -> x7, Pallas kernels: 2.06 us -> 1.91 us  [call_merge(): pl.pallas_call(body, in_specs=[pl.BlockSpec(memory_space=pltpu.VMEM)] * l...]
  transfers between devices with their start and end apart: 17 -> 17, of which waited for: 5 -> 6; matrix products, arithmetic and copies ran while one was open for 0% -> 0% of each run, Pallas kernels for 16% -> 16%
where the time goes in v21:
time: 33.9 us; the launch traced here: 33.7 us
  starting transfers between devices  21 us (62%)
  Pallas kernels  8.01 us (24%)
  waiting for transfers between devices  4.6 us (14%)
    ppermute x8, starting transfers between devices, fetch(): return lax.ppermute(x, 'seq', partner_perm(shape, by, False))  11.7 us
    ppermute x9, starting transfers between devices, give(): return lax.ppermute(x, 'seq', partner_perm(shape, by, True))  9.36 us
    ppermute x9, waiting for transfers between devices, give(): return lax.ppermute(x, 'seq', partner_perm(shape, by, True))  4.08 us
    pallas_call x2, Pallas kernels, attend(): pl.pallas_call(body, in_specs=[pl.BlockSpec(memory_space=pltpu.VMEM)] * 4...  3.46 us
    pallas_call x1, Pallas kernels, load(): pl.pallas_call(body, in_specs=[in_hbm] * len(held) + [pl.BlockSpec(memory...  2.65 us
    pallas_call x7, Pallas kernels, call_merge(): pl.pallas_call(body, in_specs=[pl.BlockSpec(memory_space=pltpu.VMEM)] * l...  1.91 us
  transfers between devices with their start and end apart: 17, of which 6 were waited for; matrix products, arithmetic and copies ran while one was open for 0% of the time, Pallas kernels for 16%

profile of v21, /device:TPU:0, one launch (start us, length us, event | category | flops | bytes accessed | tf_op | source)
XLA Modules:
  0.0 33.7 jit_solution(6759054689694727904)
XLA Ops:
  0.0 5.0 %collective-permute-start.1 = (bf16[8,2560]{1,0:T(8,128)(2,1)}, bf16[8,2560]{1,0:T(8,128)(2,1)S(1)}, u32[]{:S(2)}, u32[]{:S(2)}) collective-permute-start(bf16[8,2560]{1,0:T(8,128)(2,1)} %refs_5_.1), channel_id=1, source_target_pairs={{12,0},{13,1},{14,2},{15,3},{8,4},{9,5},{10,6},{11,7},{4,8},{5,9},... | collective-permute-start | bytes 122888 | tf_op jit(solution)/shard_map/ppermute | solution.py:336
  5.1 0.6 %collective-permute-start.2 = (bf16[8,2560]{1,0:T(8,128)(2,1)}, bf16[8,2560]{1,0:T(8,128)(2,1)S(1)}, u32[]{:S(2)}, u32[]{:S(2)}) collective-permute-start(bf16[8,2560]{1,0:T(8,128)(2,1)} %refs_5_.1), channel_id=1, source_target_pairs={{8,0},{9,1},{10,2},{11,3},{12,4},{13,5},{14,6},{15,7},{0,8},{1,9},... | collective-permute-start | bytes 122888 | tf_op jit(solution)/shard_map/ppermute | solution.py:336
  5.6 1.8 %collective-permute-start.3 = (bf16[8,2560]{1,0:T(8,128)(2,1)}, bf16[8,2560]{1,0:T(8,128)(2,1)S(1)}, u32[]{:S(2)}, u32[]{:S(2)}) collective-permute-start(bf16[8,2560]{1,0:T(8,128)(2,1)} %refs_5_.1), channel_id=1, source_target_pairs={{2,0},{3,1},{0,2},{1,3},{6,4},{7,5},{4,6},{5,7},{10,8},{11,9},{8,1... | collective-permute-start | bytes 122888 | tf_op jit(solution)/shard_map/ppermute | solution.py:336
  7.4 0.0 collective-permute-done.1.refs_1_
  7.4 1.6 %collective-permute-start.4 = (bf16[8,2560]{1,0:T(8,128)(2,1)S(1)}, bf16[8,2560]{1,0:T(8,128)(2,1)S(1)}, u32[]{:S(2)}, u32[]{:S(2)}) collective-permute-start(bf16[8,2560]{1,0:T(8,128)(2,1)S(1)} %collective-permute-done.1.refs_1_), channel_id=1, source_target_pairs={{2,0},{3,1},{0,2},{1,3},{6,4},{7,5},{4,6},{5,7},{10,8},{11,9},{8,1... | collective-permute-start | bytes 122888 | tf_op jit(solution)/shard_map/ppermute | solution.py:336
  9.0 0.3 collective-permute-done.refs_6_.refs_3_
  9.3 1.5 %collective-permute-start.6 = (bf16[8,2560]{1,0:T(8,128)(2,1)S(1)}, bf16[8,2560]{1,0:T(8,128)(2,1)S(1)}, u32[]{:S(2)}, u32[]{:S(2)}) collective-permute-start(bf16[8,2560]{1,0:T(8,128)(2,1)S(1)} %collective-permute-done.refs_6_.refs_3_), channel_id=1, source_target_pairs={{2,0},{3,1},{0,2},{1,3},{6,4},{7,5},{4,6},{5,7},{10,8},{11,9},{8,1... | collective-permute-start | bytes 122888 | tf_op jit(solution)/shard_map/ppermute | solution.py:336
  10.8 1.1 %collective-permute-start.5 = (bf16[8,2560]{1,0:T(8,128)(2,1)S(1)}, bf16[8,2560]{1,0:T(8,128)(2,1)S(1)}, u32[]{:S(2)}, u32[]{:S(2)}) collective-permute-start(bf16[8,2560]{1,0:T(8,128)(2,1)S(1)} %collective-permute-done.2.refs_2_), channel_id=1, source_target_pairs={{2,0},{3,1},{0,2},{1,3},{6,4},{7,5},{4,6},{5,7},{10,8},{11,9},{8,1... | collective-permute-start | bytes 122888 | tf_op jit(solution)/shard_map/ppermute | solution.py:336
  11.9 2.6 %load.1 = (bf16[528,2560]{1,0:T(8,128)(2,1)S(1)}, bf16[528,2560]{1,0:T(8,128)(2,1)S(1)}, f32[528,128]{1,0:T(8,128)S(1)}, bf16[8,2560]{1,0:T(8,128)(2,1)S(1)}) custom-call(bf16[512,2560]{1,0:T(8,128)(2,1)} %refs_0_.1, bf16[512,2560]{1,0:T(8,128)(2,1)} %refs_1_.1, bf16[8,2560]{1,0:T(8,128)(2,1)} %refs_2_.1, bf16[8,2560]{1,0:T(8,128)(2,1)} %refs_3_.1, ...), custom_call_target="tpu_custom_call" | custom-call | bytes 10485760 | tf_op jit(solution)/shard_map/load/pallas_call | solution.py:220
  14.6 0.2 collective-permute-done.5.refs_6_
  14.8 0.1 collective-permute-start.7
  14.9 1.7 %attend.2 = (f32[32,2688]{1,0:T(8,128)S(1)}, f32[32,2688]{1,0:T(8,128)S(1)}) custom-call(f32[528,128]{1,0:T(8,128)S(1)} %get-tuple-element.17.refs_0_, bf16[64,2560]{1,0:T(8,128)(2,1)S(1)} %merge.7.refs_1_, bf16[528,2560]{1,0:T(8,128)(2,1)S(1)} %get-tuple-element.19.refs_2_, bf16[528,2560]{1,0:T(8,128)(2,1)S(1)} %get-tuple-element.20.refs_3_), custom_call_target="tpu_custom_call" | custom-call | flops 346030080 | bytes 5406720 | tf_op jit(solution)/shard_map/attend/pallas_call | solution.py:159
  16.6 1.7 %attend.3 = (bf16[32,2688]{1,0:T(8,128)(2,1)S(1)}, bf16[32,2688]{1,0:T(8,128)(2,1)S(1)}) custom-call(f32[528,128]{1,0:T(8,128)S(1)} %get-tuple-element.17.refs_0_, bf16[64,2560]{1,0:T(8,128)(2,1)S(1)} %collective-permute-done.7.refs_1_, bf16[528,2560]{1,0:T(8,128)(2,1)S(1)} %get-tuple-element.19.refs_2_, bf16[528,2560]{1,0:T(8,128)(2,1)S(1)} %get-tuple-element.20.refs_3_, ...), custom_call_target="tpu_custom_call" | custom-call | flops 346030080 | bytes 5406720 | tf_op jit(solution)/shard_map/attend/pallas_call | solution.py:159
  18.4 0.6 %collective-permute-start.9 = (bf16[32,2688]{1,0:T(8,128)(2,1)S(1)}, bf16[32,2688]{1,0:T(8,128)(2,1)S(1)}, u32[]{:S(2)}, u32[]{:S(2)}) collective-permute-start(bf16[32,2688]{1,0:T(8,128)(2,1)S(1)} %get-tuple-element.24), channel_id=1, source_target_pairs={{0,1},{1,0},{2,3},{3,2},{4,5},{5,4},{6,7},{7,6},{8,9},{9,8},{10,11... | collective-permute-start | bytes 516104 | tf_op jit(solution)/shard_map/ppermute | solution.py:339
  18.9 0.1 collective-permute-start.8
  19.0 1.0 %collective-permute-done.9.refs_1_ = bf16[32,2688]{1,0:T(8,128)(2,1)S(1)} collective-permute-done((bf16[32,2688]{1,0:T(8,128)(2,1)S(1)}, bf16[32,2688]{1,0:T(8,128)(2,1)S(1)}, u32[]{:S(2)}, u32[]{:S(2)}) %collective-permute-start.9) | collective-permute-done | bytes 172064 | tf_op jit(solution)/shard_map/ppermute | solution.py:339
  20.0 0.3 merge.8
  20.3 1.2 %collective-permute-start.11 = (bf16[8,2688]{1,0:T(8,128)(2,1)S(1)}, bf16[8,2688]{1,0:T(8,128)(2,1)S(1)}, u32[]{:S(2)}, u32[]{:S(2)}) collective-permute-start(bf16[8,2688]{1,0:T(8,128)(2,1)S(1)} %get-tuple-element.26), channel_id=1, source_target_pairs={{0,2},{1,3},{2,0},{3,1},{4,6},{5,7},{6,4},{7,5},{8,10},{9,11},{10,... | collective-permute-start | bytes 129032 | tf_op jit(solution)/shard_map/ppermute | solution.py:339
  21.4 0.9 %collective-permute-start.13 = (bf16[8,2688]{1,0:T(8,128)(2,1)S(1)}, bf16[8,2688]{1,0:T(8,128)(2,1)S(1)}, u32[]{:S(2)}, u32[]{:S(2)}) collective-permute-start(bf16[8,2688]{1,0:T(8,128)(2,1)S(1)} %get-tuple-element.27), channel_id=1, source_target_pairs={{0,2},{1,3},{2,0},{3,1},{4,6},{5,7},{6,4},{7,5},{8,10},{9,11},{10,... | collective-permute-start | bytes 129032 | tf_op jit(solution)/shard_map/ppermute | solution.py:339
  22.4 1.1 %collective-permute-start.15 = (bf16[8,2688]{1,0:T(8,128)(2,1)S(1)}, bf16[8,2688]{1,0:T(8,128)(2,1)S(1)}, u32[]{:S(2)}, u32[]{:S(2)}) collective-permute-start(bf16[8,2688]{1,0:T(8,128)(2,1)S(1)} %get-tuple-element.28), channel_id=1, source_target_pairs={{0,2},{1,3},{2,0},{3,1},{4,6},{5,7},{6,4},{7,5},{8,10},{9,11},{10,... | collective-permute-start | bytes 129032 | tf_op jit(solution)/shard_map/ppermute | solution.py:339
  23.5 0.9 %collective-permute-start.10 = (bf16[8,2688]{1,0:T(8,128)(2,1)S(1)}, bf16[8,2688]{1,0:T(8,128)(2,1)S(1)}, u32[]{:S(2)}, u32[]{:S(2)}) collective-permute-start(bf16[8,2688]{1,0:T(8,128)(2,1)S(1)} %get-tuple-element.25), channel_id=1, source_target_pairs={{0,2},{1,3},{2,0},{3,1},{4,6},{5,7},{6,4},{7,5},{8,10},{9,11},{10,... | collective-permute-start | bytes 129032 | tf_op jit(solution)/shard_map/ppermute | solution.py:339
  24.4 0.2 collective-permute-done.11.refs_2_
  24.6 0.2 merge.10
  24.8 2.7 %collective-permute-start.12 = (bf16[8,2688]{1,0:T(8,128)(2,1)S(1)}, bf16[8,2688]{1,0:T(8,128)(2,1)S(1)}, u32[]{:S(2)}, u32[]{:S(2)}) collective-permute-start(bf16[8,2688]{1,0:T(8,128)(2,1)S(1)} %merge.10), channel_id=1, source_target_pairs={{0,12},{1,13},{2,14},{3,15},{4,8},{5,9},{6,10},{7,11},{8,4},{9,5},... | collective-permute-start | bytes 129032 | tf_op jit(solution)/shard_map/ppermute | solution.py:339
  27.5 0.2 merge.11
  27.7 0.4 %collective-permute-start.14 = (bf16[8,2688]{1,0:T(8,128)(2,1)S(1)}, bf16[8,2688]{1,0:T(8,128)(2,1)S(1)}, u32[]{:S(2)}, u32[]{:S(2)}) collective-permute-start(bf16[8,2688]{1,0:T(8,128)(2,1)S(1)} %merge.11), channel_id=1, source_target_pairs={{0,8},{1,9},{2,10},{3,11},{4,12},{5,13},{6,14},{7,15},{8,0},{9,1},... | collective-permute-start | bytes 129032 | tf_op jit(solution)/shard_map/ppermute | solution.py:339
  28.1 0.2 merge.12
  28.3 1.5 %collective-permute-start.16 = (bf16[8,2688]{1,0:T(8,128)(2,1)S(1)}, bf16[8,2688]{1,0:T(8,128)(2,1)S(1)}, u32[]{:S(2)}, u32[]{:S(2)}) collective-permute-start(bf16[8,2688]{1,0:T(8,128)(2,1)S(1)} %merge.12), channel_id=1, source_target_pairs={{0,4},{1,5},{2,6},{3,7},{4,0},{5,1},{6,2},{7,3},{8,12},{9,13},{10,... | collective-permute-start | bytes 129032 | tf_op jit(solution)/shard_map/ppermute | solution.py:339
  29.8 0.2 merge.9.refs_0_
  29.9 0.8 %collective-permute-done.12.refs_1_ = bf16[8,2688]{1,0:T(8,128)(2,1)S(1)} collective-permute-done((bf16[8,2688]{1,0:T(8,128)(2,1)S(1)}, bf16[8,2688]{1,0:T(8,128)(2,1)S(1)}, u32[]{:S(2)}, u32[]{:S(2)}) %collective-permute-start.12) | collective-permute-done | bytes 43040 | tf_op jit(solution)/shard_map/ppermute | solution.py:339
  30.7 2.1 %collective-permute-done.14.refs_2_ = bf16[8,2688]{1,0:T(8,128)(2,1)S(1)} collective-permute-done((bf16[8,2688]{1,0:T(8,128)(2,1)S(1)}, bf16[8,2688]{1,0:T(8,128)(2,1)S(1)}, u32[]{:S(2)}, u32[]{:S(2)}) %collective-permute-start.14) | collective-permute-done | bytes 43040 | tf_op jit(solution)/shard_map/ppermute | solution.py:339
  32.8 0.9 %merge.13 = bf16[8,2560]{1,0:T(8,128)(2,1)} custom-call(f32[8,2688]{1,0:T(8,128)S(1)} %merge.9.refs_0_, bf16[8,2688]{1,0:T(8,128)(2,1)S(1)} %collective-permute-done.12.refs_1_, bf16[8,2688]{1,0:T(8,128)(2,1)S(1)} %collective-permute-done.14.refs_2_, bf16[8,2688]{1,0:T(8,128)(2,1)S(1)} %collective-permute-done.16.refs_3_), custom_call_target="tpu_custom_call" | custom-call | flops 344064 | bytes 344064 | tf_op jit(solution)/shard_map/merge/pallas_call | solution.py:316
  (12 shorter events, 0.1 us)
Async XLA Ops:
  0.0 7.4 %collective-permute-start.1 = (bf16[8,2560]{1,0:T(8,128)(2,1)}, bf16[8,2560]{1,0:T(8,128)(2,1)S(1)}, u32[]{:S(2)}, u32[]{:S(2)}) collective-permute-start(bf16[8,2560]{1,0:T(8,128)(2,1)} %refs_5_.1), channel_id=1, source_target_pairs={{12,0},{13,1},{14,2},{15,3},{8,4},{9,5},{10,6},{11,7},{4,8},{5,9},... | collective-permute-start | bytes 122888 | tf_op jit(solution)/shard_map/ppermute | solution.py:336
  5.0 4.2 %collective-permute-start = (bf16[8,2560]{1,0:T(8,128)(2,1)}, bf16[8,2560]{1,0:T(8,128)(2,1)S(1)}, u32[]{:S(2)}, u32[]{:S(2)}) collective-permute-start(bf16[8,2560]{1,0:T(8,128)(2,1)} %refs_5_.1), channel_id=1, source_target_pairs={{4,0},{5,1},{6,2},{7,3},{0,4},{1,5},{2,6},{3,7},{12,8},{13,9},{14,... | collective-permute-start | bytes 122888 | tf_op jit(solution)/shard_map/ppermute | solution.py:336
  5.1 5.7 %collective-permute-start.2 = (bf16[8,2560]{1,0:T(8,128)(2,1)}, bf16[8,2560]{1,0:T(8,128)(2,1)S(1)}, u32[]{:S(2)}, u32[]{:S(2)}) collective-permute-start(bf16[8,2560]{1,0:T(8,128)(2,1)} %refs_5_.1), channel_id=1, source_target_pairs={{8,0},{9,1},{10,2},{11,3},{12,4},{13,5},{14,6},{15,7},{0,8},{1,9},... | collective-permute-start | bytes 122888 | tf_op jit(solution)/shard_map/ppermute | solution.py:336
  5.6 8.9 %collective-permute-start.3 = (bf16[8,2560]{1,0:T(8,128)(2,1)}, bf16[8,2560]{1,0:T(8,128)(2,1)S(1)}, u32[]{:S(2)}, u32[]{:S(2)}) collective-permute-start(bf16[8,2560]{1,0:T(8,128)(2,1)} %refs_5_.1), channel_id=1, source_target_pairs={{2,0},{3,1},{0,2},{1,3},{6,4},{7,5},{4,6},{5,7},{10,8},{11,9},{8,1... | collective-permute-start | bytes 122888 | tf_op jit(solution)/shard_map/ppermute | solution.py:336
  7.4 7.2 %collective-permute-start.4 = (bf16[8,2560]{1,0:T(8,128)(2,1)S(1)}, bf16[8,2560]{1,0:T(8,128)(2,1)S(1)}, u32[]{:S(2)}, u32[]{:S(2)}) collective-permute-start(bf16[8,2560]{1,0:T(8,128)(2,1)S(1)} %collective-permute-done.1.refs_1_), channel_id=1, source_target_pairs={{2,0},{3,1},{0,2},{1,3},{6,4},{7,5},{4,6},{5,7},{10,8},{11,9},{8,1... | collective-permute-start | bytes 122888 | tf_op jit(solution)/shard_map/ppermute | solution.py:336
  9.3 5.3 %collective-permute-start.6 = (bf16[8,2560]{1,0:T(8,128)(2,1)S(1)}, bf16[8,2560]{1,0:T(8,128)(2,1)S(1)}, u32[]{:S(2)}, u32[]{:S(2)}) collective-permute-start(bf16[8,2560]{1,0:T(8,128)(2,1)S(1)} %collective-permute-done.refs_6_.refs_3_), channel_id=1, source_target_pairs={{2,0},{3,1},{0,2},{1,3},{6,4},{7,5},{4,6},{5,7},{10,8},{11,9},{8,1... | collective-permute-start | bytes 122888 | tf_op jit(solution)/shard_map/ppermute | solution.py:336
  10.8 4.0 %collective-permute-start.5 = (bf16[8,2560]{1,0:T(8,128)(2,1)S(1)}, bf16[8,2560]{1,0:T(8,128)(2,1)S(1)}, u32[]{:S(2)}, u32[]{:S(2)}) collective-permute-start(bf16[8,2560]{1,0:T(8,128)(2,1)S(1)} %collective-permute-done.2.refs_2_), channel_id=1, source_target_pairs={{2,0},{3,1},{0,2},{1,3},{6,4},{7,5},{4,6},{5,7},{10,8},{11,9},{8,1... | collective-permute-start | bytes 122888 | tf_op jit(solution)/shard_map/ppermute | solution.py:336
  14.8 1.8 %collective-permute-start.7 = (bf16[64,2560]{1,0:T(8,128)(2,1)S(1)}, bf16[64,2560]{1,0:T(8,128)(2,1)S(1)}, u32[]{:S(2)}, u32[]{:S(2)}) collective-permute-start(bf16[64,2560]{1,0:T(8,128)(2,1)S(1)} %merge.7.refs_1_), channel_id=1, source_target_pairs={{1,0},{0,1},{3,2},{2,3},{5,4},{4,5},{7,6},{6,7},{9,8},{8,9},{11,10... | collective-permute-start | bytes 983048 | tf_op jit(solution)/shard_map/ppermute | solution.py:336
  18.4 1.6 %collective-permute-start.9 = (bf16[32,2688]{1,0:T(8,128)(2,1)S(1)}, bf16[32,2688]{1,0:T(8,128)(2,1)S(1)}, u32[]{:S(2)}, u32[]{:S(2)}) collective-permute-start(bf16[32,2688]{1,0:T(8,128)(2,1)S(1)} %get-tuple-element.24), channel_id=1, source_target_pairs={{0,1},{1,0},{2,3},{3,2},{4,5},{5,4},{6,7},{7,6},{8,9},{9,8},{10,11... | collective-permute-start | bytes 516104 | tf_op jit(solution)/shard_map/ppermute | solution.py:339
  18.9 5.5 %collective-permute-start.8 = (bf16[32,2688]{1,0:T(8,128)(2,1)S(1)}, bf16[32,2688]{1,0:T(8,128)(2,1)S(1)}, u32[]{:S(2)}, u32[]{:S(2)}) collective-permute-start(bf16[32,2688]{1,0:T(8,128)(2,1)S(1)} %get-tuple-element.22), channel_id=1, source_target_pairs={{0,1},{1,0},{2,3},{3,2},{4,5},{5,4},{6,7},{7,6},{8,9},{9,8},{10,11... | collective-permute-start | bytes 516104 | tf_op jit(solution)/shard_map/ppermute | solution.py:339
  20.3 4.4 %collective-permute-start.11 = (bf16[8,2688]{1,0:T(8,128)(2,1)S(1)}, bf16[8,2688]{1,0:T(8,128)(2,1)S(1)}, u32[]{:S(2)}, u32[]{:S(2)}) collective-permute-start(bf16[8,2688]{1,0:T(8,128)(2,1)S(1)} %get-tuple-element.26), channel_id=1, source_target_pairs={{0,2},{1,3},{2,0},{3,1},{4,6},{5,7},{6,4},{7,5},{8,10},{9,11},{10,... | collective-permute-start | bytes 129032 | tf_op jit(solution)/shard_map/ppermute | solution.py:339
  21.4 6.0 %collective-permute-start.13 = (bf16[8,2688]{1,0:T(8,128)(2,1)S(1)}, bf16[8,2688]{1,0:T(8,128)(2,1)S(1)}, u32[]{:S(2)}, u32[]{:S(2)}) collective-permute-start(bf16[8,2688]{1,0:T(8,128)(2,1)S(1)} %get-tuple-element.27), channel_id=1, source_target_pairs={{0,2},{1,3},{2,0},{3,1},{4,6},{5,7},{6,4},{7,5},{8,10},{9,11},{10,... | collective-permute-start | bytes 129032 | tf_op jit(solution)/shard_map/ppermute | solution.py:339
  22.4 5.7 %collective-permute-start.15 = (bf16[8,2688]{1,0:T(8,128)(2,1)S(1)}, bf16[8,2688]{1,0:T(8,128)(2,1)S(1)}, u32[]{:S(2)}, u32[]{:S(2)}) collective-permute-start(bf16[8,2688]{1,0:T(8,128)(2,1)S(1)} %get-tuple-element.28), channel_id=1, source_target_pairs={{0,2},{1,3},{2,0},{3,1},{4,6},{5,7},{6,4},{7,5},{8,10},{9,11},{10,... | collective-permute-start | bytes 129032 | tf_op jit(solution)/shard_map/ppermute | solution.py:339
  23.5 6.3 %collective-permute-start.10 = (bf16[8,2688]{1,0:T(8,128)(2,1)S(1)}, bf16[8,2688]{1,0:T(8,128)(2,1)S(1)}, u32[]{:S(2)}, u32[]{:S(2)}) collective-permute-start(bf16[8,2688]{1,0:T(8,128)(2,1)S(1)} %get-tuple-element.25), channel_id=1, source_target_pairs={{0,2},{1,3},{2,0},{3,1},{4,6},{5,7},{6,4},{7,5},{8,10},{9,11},{10,... | collective-permute-start | bytes 129032 | tf_op jit(solution)/shard_map/ppermute | solution.py:339
  24.8 5.9 %collective-permute-start.12 = (bf16[8,2688]{1,0:T(8,128)(2,1)S(1)}, bf16[8,2688]{1,0:T(8,128)(2,1)S(1)}, u32[]{:S(2)}, u32[]{:S(2)}) collective-permute-start(bf16[8,2688]{1,0:T(8,128)(2,1)S(1)} %merge.10), channel_id=1, source_target_pairs={{0,12},{1,13},{2,14},{3,15},{4,8},{5,9},{6,10},{7,11},{8,4},{9,5},... | collective-permute-start | bytes 129032 | tf_op jit(solution)/shard_map/ppermute | solution.py:339
  27.7 5.2 %collective-permute-start.14 = (bf16[8,2688]{1,0:T(8,128)(2,1)S(1)}, bf16[8,2688]{1,0:T(8,128)(2,1)S(1)}, u32[]{:S(2)}, u32[]{:S(2)}) collective-permute-start(bf16[8,2688]{1,0:T(8,128)(2,1)S(1)} %merge.11), channel_id=1, source_target_pairs={{0,8},{1,9},{2,10},{3,11},{4,12},{5,13},{6,14},{7,15},{8,0},{9,1},... | collective-permute-start | bytes 129032 | tf_op jit(solution)/shard_map/ppermute | solution.py:339
  28.3 4.6 %collective-permute-start.16 = (bf16[8,2688]{1,0:T(8,128)(2,1)S(1)}, bf16[8,2688]{1,0:T(8,128)(2,1)S(1)}, u32[]{:S(2)}, u32[]{:S(2)}) collective-permute-start(bf16[8,2688]{1,0:T(8,128)(2,1)S(1)} %merge.12), channel_id=1, source_target_pairs={{0,4},{1,5},{2,6},{3,7},{4,0},{5,1},{6,2},{7,3},{8,12},{9,13},{10,... | collective-permute-start | bytes 129032 | tf_op jit(solution)/shard_map/ppermute | solution.py:339

commit v22 on v15

--- a/solution.py
+++ b/solution.py
@@ -84,10 +84,13 @@
                 q = jnp.concatenate([jnp.where(m, q, jnp.zeros_like(q)) for m in mine], axis=0)
                 return lax.dot_general(k_ref[:, cols], q, contract_last, preferred_element_type=F32)
 
-            def weigh(i, score):
+            def masked(score):
                 bias = jnp.concatenate([bias_ref[...]] * (PACK * rows // STAT), axis=1)
                 score = score * scale + bias
                 top = jnp.max(score, axis=0, keepdims=True).astype(BF16).astype(F32)
+                return score, top
+
+            def weigh(i, score, top):
                 score = jnp.exp2(score - top)
                 top_acc[pl.ds(step * group + i, 1), :] = top
                 mass_acc[pl.ds(step * group + i, 1), :] = jnp.sum(score, axis=0, keepdims=True)
@@ -105,15 +108,16 @@
                         one = both[start : start + tile, k * HD : (k + 1) * HD]
                         o_ref[at, cols] = one.astype(o_ref.dtype)
 
-            ahead = [scores(i) for i in range(min(2, group))]
-            weights = None
-            for i in range(group):
-                if i + 2 < group:
-                    ahead.append(scores(i + 2))
-                done, weights = weights, weigh(i, ahead[i])
-                if i > 0:
-                    gather_values(i - 1, done)
-            gather_values(group - 1, weights)
+            score, top, weights = {}, {}, {}
+            for t in range(-3, group + 1):
+                if 0 <= t + 3 < group:
+                    score[t + 3] = scores(t + 3)
+                if 0 <= t + 1 < group:
+                    score[t + 1], top[t + 1] = masked(score[t + 1])
+                if 0 <= t < group:
+                    weights[t] = weigh(t, score.pop(t), top.pop(t))
+                if 0 <= t - 1:
+                    gather_values(t - 1, weights.pop(t - 1))
             return carry
 
         lax.fori_loop(0, steps, heads_of, 0)

time: 34 us -> 33.8 us (level)
  no operation moved by 1% of the time
where the time goes in v22:
time: 33.8 us; the launch traced here: 33.7 us
  starting transfers between devices  21 us (62%)
  Pallas kernels  8.01 us (24%)
  waiting for transfers between devices  4.52 us (13%)
    ppermute x8, starting transfers between devices, fetch(): return lax.ppermute(x, 'seq', partner_perm(shape, by, False))  11.7 us
    ppermute x9, starting transfers between devices, give(): return lax.ppermute(x, 'seq', partner_perm(shape, by, True))  9.35 us
    ppermute x9, waiting for transfers between devices, give(): return lax.ppermute(x, 'seq', partner_perm(shape, by, True))  4.01 us
    pallas_call x2, Pallas kernels, attend(): pl.pallas_call(body, in_specs=[pl.BlockSpec(memory_space=pltpu.VMEM)] * 4...  3.3 us
    pallas_call x1, Pallas kernels, load(): pl.pallas_call(body, in_specs=[in_hbm] * len(held) + [pl.BlockSpec(memory...  2.65 us
    pallas_call x8, Pallas kernels, call_merge(): pl.pallas_call(body, in_specs=[pl.BlockSpec(memory_space=pltpu.VMEM)] * l...  2.06 us
  transfers between devices with their start and end apart: 17, of which 5 were waited for; matrix products, arithmetic and copies ran while one was open for 0% of the time, Pallas kernels for 16%

profile of v22, /device:TPU:0, one launch (start us, length us, event | category | flops | bytes accessed | tf_op | source)
XLA Modules:
  0.0 33.7 jit_solution(5995498043494419184)
XLA Ops:
  0.0 5.0 %collective-permute-start.1 = (bf16[8,2560]{1,0:T(8,128)(2,1)}, bf16[8,2560]{1,0:T(8,128)(2,1)S(1)}, u32[]{:S(2)}, u32[]{:S(2)}) collective-permute-start(bf16[8,2560]{1,0:T(8,128)(2,1)} %refs_5_.1), channel_id=1, source_target_pairs={{12,0},{13,1},{14,2},{15,3},{8,4},{9,5},{10,6},{11,7},{4,8},{5,9},... | collective-permute-start | bytes 122888 | tf_op jit(solution)/shard_map/ppermute | solution.py:310
  5.1 0.6 %collective-permute-start.2 = (bf16[8,2560]{1,0:T(8,128)(2,1)}, bf16[8,2560]{1,0:T(8,128)(2,1)S(1)}, u32[]{:S(2)}, u32[]{:S(2)}) collective-permute-start(bf16[8,2560]{1,0:T(8,128)(2,1)} %refs_5_.1), channel_id=1, source_target_pairs={{8,0},{9,1},{10,2},{11,3},{12,4},{13,5},{14,6},{15,7},{0,8},{1,9},... | collective-permute-start | bytes 122888 | tf_op jit(solution)/shard_map/ppermute | solution.py:310
  5.6 1.8 %collective-permute-start.3 = (bf16[8,2560]{1,0:T(8,128)(2,1)}, bf16[8,2560]{1,0:T(8,128)(2,1)S(1)}, u32[]{:S(2)}, u32[]{:S(2)}) collective-permute-start(bf16[8,2560]{1,0:T(8,128)(2,1)} %refs_5_.1), channel_id=1, source_target_pairs={{2,0},{3,1},{0,2},{1,3},{6,4},{7,5},{4,6},{5,7},{10,8},{11,9},{8,1... | collective-permute-start | bytes 122888 | tf_op jit(solution)/shard_map/ppermute | solution.py:310
  7.4 1.6 %collective-permute-start.4 = (bf16[8,2560]{1,0:T(8,128)(2,1)S(1)}, bf16[8,2560]{1,0:T(8,128)(2,1)S(1)}, u32[]{:S(2)}, u32[]{:S(2)}) collective-permute-start(bf16[8,2560]{1,0:T(8,128)(2,1)S(1)} %collective-permute-done.1.refs_1_), channel_id=1, source_target_pairs={{2,0},{3,1},{0,2},{1,3},{6,4},{7,5},{4,6},{5,7},{10,8},{11,9},{8,1... | collective-permute-start | bytes 122888 | tf_op jit(solution)/shard_map/ppermute | solution.py:310
  9.0 0.3 collective-permute-done.refs_6_.refs_3_
  9.3 1.5 %collective-permute-start.6 = (bf16[8,2560]{1,0:T(8,128)(2,1)S(1)}, bf16[8,2560]{1,0:T(8,128)(2,1)S(1)}, u32[]{:S(2)}, u32[]{:S(2)}) collective-permute-start(bf16[8,2560]{1,0:T(8,128)(2,1)S(1)} %collective-permute-done.refs_6_.refs_3_), channel_id=1, source_target_pairs={{2,0},{3,1},{0,2},{1,3},{6,4},{7,5},{4,6},{5,7},{10,8},{11,9},{8,1... | collective-permute-start | bytes 122888 | tf_op jit(solution)/shard_map/ppermute | solution.py:310
  10.8 1.1 %collective-permute-start.5 = (bf16[8,2560]{1,0:T(8,128)(2,1)S(1)}, bf16[8,2560]{1,0:T(8,128)(2,1)S(1)}, u32[]{:S(2)}, u32[]{:S(2)}) collective-permute-start(bf16[8,2560]{1,0:T(8,128)(2,1)S(1)} %collective-permute-done.2.refs_2_), channel_id=1, source_target_pairs={{2,0},{3,1},{0,2},{1,3},{6,4},{7,5},{4,6},{5,7},{10,8},{11,9},{8,1... | collective-permute-start | bytes 122888 | tf_op jit(solution)/shard_map/ppermute | solution.py:310
  11.9 2.6 %load.1 = (bf16[528,2560]{1,0:T(8,128)(2,1)S(1)}, bf16[528,2560]{1,0:T(8,128)(2,1)S(1)}, f32[528,128]{1,0:T(8,128)S(1)}, bf16[8,2560]{1,0:T(8,128)(2,1)S(1)}) custom-call(bf16[512,2560]{1,0:T(8,128)(2,1)} %refs_0_.1, bf16[512,2560]{1,0:T(8,128)(2,1)} %refs_1_.1, bf16[8,2560]{1,0:T(8,128)(2,1)} %refs_2_.1, bf16[8,2560]{1,0:T(8,128)(2,1)} %refs_3_.1, ...), custom_call_target="tpu_custom_call" | custom-call | bytes 10485760 | tf_op jit(solution)/shard_map/load/pallas_call | solution.py:214
  14.6 0.2 collective-permute-done.5.refs_6_
  14.8 0.1 collective-permute-start.7
  14.9 1.6 %attend.2 = (f32[32,2688]{1,0:T(8,128)S(1)}, f32[32,2688]{1,0:T(8,128)S(1)}) custom-call(f32[528,128]{1,0:T(8,128)S(1)} %get-tuple-element.21.refs_0_, bf16[64,2560]{1,0:T(8,128)(2,1)S(1)} %merge.8.refs_1_, bf16[528,2560]{1,0:T(8,128)(2,1)S(1)} %get-tuple-element.23.refs_2_, bf16[528,2560]{1,0:T(8,128)(2,1)S(1)} %get-tuple-element.24.refs_3_), custom_call_target="tpu_custom_call" | custom-call | flops 346030080 | bytes 5406720 | tf_op jit(solution)/shard_map/attend/pallas_call | solution.py:153
  16.6 1.7 %attend.3 = (bf16[32,2688]{1,0:T(8,128)(2,1)S(1)}, bf16[32,2688]{1,0:T(8,128)(2,1)S(1)}) custom-call(f32[528,128]{1,0:T(8,128)S(1)} %get-tuple-element.21.refs_0_, bf16[64,2560]{1,0:T(8,128)(2,1)S(1)} %collective-permute-done.7.refs_1_, bf16[528,2560]{1,0:T(8,128)(2,1)S(1)} %get-tuple-element.23.refs_2_, bf16[528,2560]{1,0:T(8,128)(2,1)S(1)} %get-tuple-element.24.refs_3_, ...), custom_call_target="tpu_custom_call" | custom-call | flops 346030080 | bytes 5406720 | tf_op jit(solution)/shard_map/attend/pallas_call | solution.py:153
  18.2 0.6 %collective-permute-start.9 = (bf16[32,2688]{1,0:T(8,128)(2,1)S(1)}, bf16[32,2688]{1,0:T(8,128)(2,1)S(1)}, u32[]{:S(2)}, u32[]{:S(2)}) collective-permute-start(bf16[32,2688]{1,0:T(8,128)(2,1)S(1)} %get-tuple-element.29), channel_id=1, source_target_pairs={{0,1},{1,0},{2,3},{3,2},{4,5},{5,4},{6,7},{7,6},{8,9},{9,8},{10,11... | collective-permute-start | bytes 516104 | tf_op jit(solution)/shard_map/ppermute | solution.py:313
  18.8 0.1 collective-permute-start.8
  18.9 1.0 %collective-permute-done.9.refs_1_ = bf16[32,2688]{1,0:T(8,128)(2,1)S(1)} collective-permute-done((bf16[32,2688]{1,0:T(8,128)(2,1)S(1)}, bf16[32,2688]{1,0:T(8,128)(2,1)S(1)}, u32[]{:S(2)}, u32[]{:S(2)}) %collective-permute-start.9) | collective-permute-done | bytes 172064 | tf_op jit(solution)/shard_map/ppermute | solution.py:313
  19.8 0.3 merge.10
  20.1 1.2 %collective-permute-start.11 = (bf16[8,2688]{1,0:T(8,128)(2,1)S(1)}, bf16[8,2688]{1,0:T(8,128)(2,1)S(1)}, u32[]{:S(2)}, u32[]{:S(2)}) collective-permute-start(bf16[8,2688]{1,0:T(8,128)(2,1)S(1)} %get-tuple-element.32), channel_id=1, source_target_pairs={{0,2},{1,3},{2,0},{3,1},{4,6},{5,7},{6,4},{7,5},{8,10},{9,11},{10,... | collective-permute-start | bytes 129032 | tf_op jit(solution)/shard_map/ppermute | solution.py:313
  21.3 0.9 %collective-permute-start.13 = (bf16[8,2688]{1,0:T(8,128)(2,1)S(1)}, bf16[8,2688]{1,0:T(8,128)(2,1)S(1)}, u32[]{:S(2)}, u32[]{:S(2)}) collective-permute-start(bf16[8,2688]{1,0:T(8,128)(2,1)S(1)} %get-tuple-element.34), channel_id=1, source_target_pairs={{0,2},{1,3},{2,0},{3,1},{4,6},{5,7},{6,4},{7,5},{8,10},{9,11},{10,... | collective-permute-start | bytes 129032 | tf_op jit(solution)/shard_map/ppermute | solution.py:313
  22.2 1.1 %collective-permute-start.15 = (bf16[8,2688]{1,0:T(8,128)(2,1)S(1)}, bf16[8,2688]{1,0:T(8,128)(2,1)S(1)}, u32[]{:S(2)}, u32[]{:S(2)}) collective-permute-start(bf16[8,2688]{1,0:T(8,128)(2,1)S(1)} %get-tuple-element.36), channel_id=1, source_target_pairs={{0,2},{1,3},{2,0},{3,1},{4,6},{5,7},{6,4},{7,5},{8,10},{9,11},{10,... | collective-permute-start | bytes 129032 | tf_op jit(solution)/shard_map/ppermute | solution.py:313
  23.3 0.9 %collective-permute-start.10 = (bf16[8,2688]{1,0:T(8,128)(2,1)S(1)}, bf16[8,2688]{1,0:T(8,128)(2,1)S(1)}, u32[]{:S(2)}, u32[]{:S(2)}) collective-permute-start(bf16[8,2688]{1,0:T(8,128)(2,1)S(1)} %get-tuple-element.30), channel_id=1, source_target_pairs={{0,2},{1,3},{2,0},{3,1},{4,6},{5,7},{6,4},{7,5},{8,10},{9,11},{10,... | collective-permute-start | bytes 129032 | tf_op jit(solution)/shard_map/ppermute | solution.py:313
  24.2 0.3 merge.9
  24.5 0.1 merge.12
  24.7 2.8 %collective-permute-start.12 = (bf16[8,2688]{1,0:T(8,128)(2,1)S(1)}, bf16[8,2688]{1,0:T(8,128)(2,1)S(1)}, u32[]{:S(2)}, u32[]{:S(2)}) collective-permute-start(bf16[8,2688]{1,0:T(8,128)(2,1)S(1)} %merge.12), channel_id=1, source_target_pairs={{0,12},{1,13},{2,14},{3,15},{4,8},{5,9},{6,10},{7,11},{8,4},{9,5},... | collective-permute-start | bytes 129032 | tf_op jit(solution)/shard_map/ppermute | solution.py:313
  27.5 0.1 merge.13
  27.6 0.4 %collective-permute-start.14 = (bf16[8,2688]{1,0:T(8,128)(2,1)S(1)}, bf16[8,2688]{1,0:T(8,128)(2,1)S(1)}, u32[]{:S(2)}, u32[]{:S(2)}) collective-permute-start(bf16[8,2688]{1,0:T(8,128)(2,1)S(1)} %merge.13), channel_id=1, source_target_pairs={{0,8},{1,9},{2,10},{3,11},{4,12},{5,13},{6,14},{7,15},{8,0},{9,1},... | collective-permute-start | bytes 129032 | tf_op jit(solution)/shard_map/ppermute | solution.py:313
  28.1 0.1 merge.14
  28.2 1.4 %collective-permute-start.16 = (bf16[8,2688]{1,0:T(8,128)(2,1)S(1)}, bf16[8,2688]{1,0:T(8,128)(2,1)S(1)}, u32[]{:S(2)}, u32[]{:S(2)}) collective-permute-start(bf16[8,2688]{1,0:T(8,128)(2,1)S(1)} %merge.14), channel_id=1, source_target_pairs={{0,4},{1,5},{2,6},{3,7},{4,0},{5,1},{6,2},{7,3},{8,12},{9,13},{10,... | collective-permute-start | bytes 129032 | tf_op jit(solution)/shard_map/ppermute | solution.py:313
  29.6 0.1 merge.11.refs_0_
  29.7 0.9 %collective-permute-done.12.refs_1_ = bf16[8,2688]{1,0:T(8,128)(2,1)S(1)} collective-permute-done((bf16[8,2688]{1,0:T(8,128)(2,1)S(1)}, bf16[8,2688]{1,0:T(8,128)(2,1)S(1)}, u32[]{:S(2)}, u32[]{:S(2)}) %collective-permute-start.12) | collective-permute-done | bytes 43040 | tf_op jit(solution)/shard_map/ppermute | solution.py:313
  30.6 2.1 %collective-permute-done.14.refs_2_ = bf16[8,2688]{1,0:T(8,128)(2,1)S(1)} collective-permute-done((bf16[8,2688]{1,0:T(8,128)(2,1)S(1)}, bf16[8,2688]{1,0:T(8,128)(2,1)S(1)}, u32[]{:S(2)}, u32[]{:S(2)}) %collective-permute-start.14) | collective-permute-done | bytes 43040 | tf_op jit(solution)/shard_map/ppermute | solution.py:313
  32.7 0.0 collective-permute-done.16.refs_3_
  32.8 0.9 %merge.15 = bf16[8,2560]{1,0:T(8,128)(2,1)} custom-call(f32[8,2688]{1,0:T(8,128)S(1)} %merge.11.refs_0_, bf16[8,2688]{1,0:T(8,128)(2,1)S(1)} %collective-permute-done.12.refs_1_, bf16[8,2688]{1,0:T(8,128)(2,1)S(1)} %collective-permute-done.14.refs_2_, bf16[8,2688]{1,0:T(8,128)(2,1)S(1)} %collective-permute-done.16.refs_3_), custom_call_target="tpu_custom_call" | custom-call | flops 344064 | bytes 344064 | tf_op jit(solution)/shard_map/merge/pallas_call | solution.py:290
  (13 shorter events, 0.1 us)
Async XLA Ops:
  0.0 7.4 %collective-permute-start.1 = (bf16[8,2560]{1,0:T(8,128)(2,1)}, bf16[8,2560]{1,0:T(8,128)(2,1)S(1)}, u32[]{:S(2)}, u32[]{:S(2)}) collective-permute-start(bf16[8,2560]{1,0:T(8,128)(2,1)} %refs_5_.1), channel_id=1, source_target_pairs={{12,0},{13,1},{14,2},{15,3},{8,4},{9,5},{10,6},{11,7},{4,8},{5,9},... | collective-permute-start | bytes 122888 | tf_op jit(solution)/shard_map/ppermute | solution.py:310
  5.0 4.2 %collective-permute-start = (bf16[8,2560]{1,0:T(8,128)(2,1)}, bf16[8,2560]{1,0:T(8,128)(2,1)S(1)}, u32[]{:S(2)}, u32[]{:S(2)}) collective-permute-start(bf16[8,2560]{1,0:T(8,128)(2,1)} %refs_5_.1), channel_id=1, source_target_pairs={{4,0},{5,1},{6,2},{7,3},{0,4},{1,5},{2,6},{3,7},{12,8},{13,9},{14,... | collective-permute-start | bytes 122888 | tf_op jit(solution)/shard_map/ppermute | solution.py:310
  5.1 5.7 %collective-permute-start.2 = (bf16[8,2560]{1,0:T(8,128)(2,1)}, bf16[8,2560]{1,0:T(8,128)(2,1)S(1)}, u32[]{:S(2)}, u32[]{:S(2)}) collective-permute-start(bf16[8,2560]{1,0:T(8,128)(2,1)} %refs_5_.1), channel_id=1, source_target_pairs={{8,0},{9,1},{10,2},{11,3},{12,4},{13,5},{14,6},{15,7},{0,8},{1,9},... | collective-permute-start | bytes 122888 | tf_op jit(solution)/shard_map/ppermute | solution.py:310
  5.6 8.9 %collective-permute-start.3 = (bf16[8,2560]{1,0:T(8,128)(2,1)}, bf16[8,2560]{1,0:T(8,128)(2,1)S(1)}, u32[]{:S(2)}, u32[]{:S(2)}) collective-permute-start(bf16[8,2560]{1,0:T(8,128)(2,1)} %refs_5_.1), channel_id=1, source_target_pairs={{2,0},{3,1},{0,2},{1,3},{6,4},{7,5},{4,6},{5,7},{10,8},{11,9},{8,1... | collective-permute-start | bytes 122888 | tf_op jit(solution)/shard_map/ppermute | solution.py:310
  7.4 7.2 %collective-permute-start.4 = (bf16[8,2560]{1,0:T(8,128)(2,1)S(1)}, bf16[8,2560]{1,0:T(8,128)(2,1)S(1)}, u32[]{:S(2)}, u32[]{:S(2)}) collective-permute-start(bf16[8,2560]{1,0:T(8,128)(2,1)S(1)} %collective-permute-done.1.refs_1_), channel_id=1, source_target_pairs={{2,0},{3,1},{0,2},{1,3},{6,4},{7,5},{4,6},{5,7},{10,8},{11,9},{8,1... | collective-permute-start | bytes 122888 | tf_op jit(solution)/shard_map/ppermute | solution.py:310
  9.3 5.3 %collective-permute-start.6 = (bf16[8,2560]{1,0:T(8,128)(2,1)S(1)}, bf16[8,2560]{1,0:T(8,128)(2,1)S(1)}, u32[]{:S(2)}, u32[]{:S(2)}) collective-permute-start(bf16[8,2560]{1,0:T(8,128)(2,1)S(1)} %collective-permute-done.refs_6_.refs_3_), channel_id=1, source_target_pairs={{2,0},{3,1},{0,2},{1,3},{6,4},{7,5},{4,6},{5,7},{10,8},{11,9},{8,1... | collective-permute-start | bytes 122888 | tf_op jit(solution)/shard_map/ppermute | solution.py:310
  10.8 4.0 %collective-permute-start.5 = (bf16[8,2560]{1,0:T(8,128)(2,1)S(1)}, bf16[8,2560]{1,0:T(8,128)(2,1)S(1)}, u32[]{:S(2)}, u32[]{:S(2)}) collective-permute-start(bf16[8,2560]{1,0:T(8,128)(2,1)S(1)} %collective-permute-done.2.refs_2_), channel_id=1, source_target_pairs={{2,0},{3,1},{0,2},{1,3},{6,4},{7,5},{4,6},{5,7},{10,8},{11,9},{8,1... | collective-permute-start | bytes 122888 | tf_op jit(solution)/shard_map/ppermute | solution.py:310
  14.8 1.7 %collective-permute-start.7 = (bf16[64,2560]{1,0:T(8,128)(2,1)S(1)}, bf16[64,2560]{1,0:T(8,128)(2,1)S(1)}, u32[]{:S(2)}, u32[]{:S(2)}) collective-permute-start(bf16[64,2560]{1,0:T(8,128)(2,1)S(1)} %merge.8.refs_1_), channel_id=1, source_target_pairs={{1,0},{0,1},{3,2},{2,3},{5,4},{4,5},{7,6},{6,7},{9,8},{8,9},{11,10... | collective-permute-start | bytes 983048 | tf_op jit(solution)/shard_map/ppermute | solution.py:310
  18.2 1.6 %collective-permute-start.9 = (bf16[32,2688]{1,0:T(8,128)(2,1)S(1)}, bf16[32,2688]{1,0:T(8,128)(2,1)S(1)}, u32[]{:S(2)}, u32[]{:S(2)}) collective-permute-start(bf16[32,2688]{1,0:T(8,128)(2,1)S(1)} %get-tuple-element.29), channel_id=1, source_target_pairs={{0,1},{1,0},{2,3},{3,2},{4,5},{5,4},{6,7},{7,6},{8,9},{9,8},{10,11... | collective-permute-start | bytes 516104 | tf_op jit(solution)/shard_map/ppermute | solution.py:313
  18.8 5.5 %collective-permute-start.8 = (bf16[32,2688]{1,0:T(8,128)(2,1)S(1)}, bf16[32,2688]{1,0:T(8,128)(2,1)S(1)}, u32[]{:S(2)}, u32[]{:S(2)}) collective-permute-start(bf16[32,2688]{1,0:T(8,128)(2,1)S(1)} %get-tuple-element.26), channel_id=1, source_target_pairs={{0,1},{1,0},{2,3},{3,2},{4,5},{5,4},{6,7},{7,6},{8,9},{9,8},{10,11... | collective-permute-start | bytes 516104 | tf_op jit(solution)/shard_map/ppermute | solution.py:313
  20.1 4.4 %collective-permute-start.11 = (bf16[8,2688]{1,0:T(8,128)(2,1)S(1)}, bf16[8,2688]{1,0:T(8,128)(2,1)S(1)}, u32[]{:S(2)}, u32[]{:S(2)}) collective-permute-start(bf16[8,2688]{1,0:T(8,128)(2,1)S(1)} %get-tuple-element.32), channel_id=1, source_target_pairs={{0,2},{1,3},{2,0},{3,1},{4,6},{5,7},{6,4},{7,5},{8,10},{9,11},{10,... | collective-permute-start | bytes 129032 | tf_op jit(solution)/shard_map/ppermute | solution.py:313
  21.3 6.2 %collective-permute-start.13 = (bf16[8,2688]{1,0:T(8,128)(2,1)S(1)}, bf16[8,2688]{1,0:T(8,128)(2,1)S(1)}, u32[]{:S(2)}, u32[]{:S(2)}) collective-permute-start(bf16[8,2688]{1,0:T(8,128)(2,1)S(1)} %get-tuple-element.34), channel_id=1, source_target_pairs={{0,2},{1,3},{2,0},{3,1},{4,6},{5,7},{6,4},{7,5},{8,10},{9,11},{10,... | collective-permute-start | bytes 129032 | tf_op jit(solution)/shard_map/ppermute | solution.py:313
  22.2 5.9 %collective-permute-start.15 = (bf16[8,2688]{1,0:T(8,128)(2,1)S(1)}, bf16[8,2688]{1,0:T(8,128)(2,1)S(1)}, u32[]{:S(2)}, u32[]{:S(2)}) collective-permute-start(bf16[8,2688]{1,0:T(8,128)(2,1)S(1)} %get-tuple-element.36), channel_id=1, source_target_pairs={{0,2},{1,3},{2,0},{3,1},{4,6},{5,7},{6,4},{7,5},{8,10},{9,11},{10,... | collective-permute-start | bytes 129032 | tf_op jit(solution)/shard_map/ppermute | solution.py:313
  23.3 6.3 %collective-permute-start.10 = (bf16[8,2688]{1,0:T(8,128)(2,1)S(1)}, bf16[8,2688]{1,0:T(8,128)(2,1)S(1)}, u32[]{:S(2)}, u32[]{:S(2)}) collective-permute-start(bf16[8,2688]{1,0:T(8,128)(2,1)S(1)} %get-tuple-element.30), channel_id=1, source_target_pairs={{0,2},{1,3},{2,0},{3,1},{4,6},{5,7},{6,4},{7,5},{8,10},{9,11},{10,... | collective-permute-start | bytes 129032 | tf_op jit(solution)/shard_map/ppermute | solution.py:313
  24.7 5.9 %collective-permute-start.12 = (bf16[8,2688]{1,0:T(8,128)(2,1)S(1)}, bf16[8,2688]{1,0:T(8,128)(2,1)S(1)}, u32[]{:S(2)}, u32[]{:S(2)}) collective-permute-start(bf16[8,2688]{1,0:T(8,128)(2,1)S(1)} %merge.12), channel_id=1, source_target_pairs={{0,12},{1,13},{2,14},{3,15},{4,8},{5,9},{6,10},{7,11},{8,4},{9,5},... | collective-permute-start | bytes 129032 | tf_op jit(solution)/shard_map/ppermute | solution.py:313
  27.6 5.1 %collective-permute-start.14 = (bf16[8,2688]{1,0:T(8,128)(2,1)S(1)}, bf16[8,2688]{1,0:T(8,128)(2,1)S(1)}, u32[]{:S(2)}, u32[]{:S(2)}) collective-permute-start(bf16[8,2688]{1,0:T(8,128)(2,1)S(1)} %merge.13), channel_id=1, source_target_pairs={{0,8},{1,9},{2,10},{3,11},{4,12},{5,13},{6,14},{7,15},{8,0},{9,1},... | collective-permute-start | bytes 129032 | tf_op jit(solution)/shard_map/ppermute | solution.py:313
  28.2 4.6 %collective-permute-start.16 = (bf16[8,2688]{1,0:T(8,128)(2,1)S(1)}, bf16[8,2688]{1,0:T(8,128)(2,1)S(1)}, u32[]{:S(2)}, u32[]{:S(2)}) collective-permute-start(bf16[8,2688]{1,0:T(8,128)(2,1)S(1)} %merge.14), channel_id=1, source_target_pairs={{0,4},{1,5},{2,6},{3,7},{4,0},{5,1},{6,2},{7,3},{8,12},{9,13},{10,... | collective-permute-start | bytes 129032 | tf_op jit(solution)/shard_map/ppermute | solution.py:313

commit v23 on v22

--- a/solution.py
+++ b/solution.py
@@ -262,6 +262,18 @@
     return call_merge(body, ins, [jax.ShapeDtypeStruct((per, width), kind) for kind in kinds])
 
 
+def merge_cuts(ins, heads, cuts, rows, after=()):
+    width = ins[0].shape[1]
+
+    def body(*refs):
+        outs = refs[len(ins) + len(after) :]
+        for cols, total in merged([getter(r) for r in refs[: len(ins)]], heads, False):
+            for start, out in zip(cuts, outs):
+                out[:, cols] = total[start : start + rows].astype(out.dtype)
+
+    return call_merge(body, ins, [jax.ShapeDtypeStruct((rows, width), BF16)] * len(cuts), after)
+
+
 def finish(ins, heads):
     rows = ins[0].shape[0]
 
@@ -324,17 +336,23 @@
     for c, rows in enumerate(planes):
         sums += attend(rows, b_n, BF16 if c else F32, keys, values, bias, sums[:1])
 
-    def over_cores(b, kind):
-        got = [give(sums[c * b_n + b], 0, 0, c) for c in range(1, c_n)]
-        return merge_rows([sums[b]] + got, heads, a_n, [kind] * a_n)
-
-    got = [[give(x, 0, b, 0) for x in over_cores(b, BF16)] for b in range(1, b_n)]
-    own = over_cores(0, F32)
-    total = [[own[s]] + [pieces[s] for pieces in got] for s in range(a_n)]
-    last = [
-        give(merge_rows(total[s], heads, 1, [BF16])[0], far_first[s], 0, 0) for s in range(1, a_n)
+    back = [[give(sums[c * b_n + b], 0, 0, c) for c in range(1, c_n)] for b in range(b_n)]
+    cuts = [s * tok for s in range(a_n)]
+    got = []
+    for b in range(1, b_n):
+        pieces = merge_cuts([sums[b]] + back[b], heads, cuts[1:], tok)
+        got.append([give(x, 0, b, 0) for x in pieces])
+    own = merge_rows([sums[0]] + back[0], heads, a_n, [F32] * a_n)
+    sent = [
+        merge_rows([own[s]] + [pieces[s - 1] for pieces in got], heads, 1, [BF16])[0]
+        for s in range(1, a_n)
     ]
-    return finish([*merge_rows(total[0], heads, 1, [F32]), *last], heads)
+    last = [give(x, a, 0, 0) for x, a in zip(sent, far_first[1:])]
+    near = [
+        give(merge_cuts([sums[b]] + back[b], heads, cuts[:1], tok, sent[-1:])[0], 0, b, 0)
+        for b in range(1, b_n)
+    ]
+    return finish([*merge_rows([own[0], *last], heads, 1, [F32]), *near], heads)
 
 
 def solution(mesh):

time: 33.8 us -> 34.7 us (1.027)
  starting transfers between devices: 21 us -> 21.4 us
  waiting for transfers between devices: 4.52 us -> 4.87 us
    ppermute x9, starting transfers between devices: 9.35 us -> 9.78 us  [give(): return lax.ppermute(x, 'seq', partner_perm(shape, by, True))]
    ppermute x9, waiting for transfers between devices: 4.01 us -> 4.36 us  [give(): return lax.ppermute(x, 'seq', partner_perm(shape, by, True))]
    pallas_call x8 -> x9, Pallas kernels: 2.06 us -> 2.16 us  [call_merge(): pl.pallas_call(body, in_specs=[pl.BlockSpec(memory_space=pltpu.VMEM)] * l...]
  transfers between devices with their start and end apart: 17 -> 17, of which waited for: 5 -> 6; matrix products, arithmetic and copies ran while one was open for 0% -> 0% of each run, Pallas kernels for 16% -> 16%
where the time goes in v23:
time: 34.7 us; the launch traced here: 34.5 us
  starting transfers between devices  21.4 us (62%)
  Pallas kernels  8.1 us (23%)
  waiting for transfers between devices  4.87 us (14%)
    ppermute x8, starting transfers between devices, fetch(): return lax.ppermute(x, 'seq', partner_perm(shape, by, False))  11.7 us
    ppermute x9, starting transfers between devices, give(): return lax.ppermute(x, 'seq', partner_perm(shape, by, True))  9.78 us
    ppermute x9, waiting for transfers between devices, give(): return lax.ppermute(x, 'seq', partner_perm(shape, by, True))  4.36 us
    pallas_call x2, Pallas kernels, attend(): pl.pallas_call(body, in_specs=[pl.BlockSpec(memory_space=pltpu.VMEM)] * 4...  3.3 us
    pallas_call x1, Pallas kernels, load(): pl.pallas_call(body, in_specs=[in_hbm] * len(held) + [pl.BlockSpec(memory...  2.65 us
    pallas_call x9, Pallas kernels, call_merge(): pl.pallas_call(body, in_specs=[pl.BlockSpec(memory_space=pltpu.VMEM)] * l...  2.16 us
  transfers between devices with their start and end apart: 17, of which 6 were waited for; matrix products, arithmetic and copies ran while one was open for 0% of the time, Pallas kernels for 16%

profile of v23, /device:TPU:0, one launch (start us, length us, event | category | flops | bytes accessed | tf_op | source)
XLA Modules:
  0.0 34.5 jit_solution(17162540983268814127)
XLA Ops:
  0.0 5.0 %collective-permute-start.1 = (bf16[8,2560]{1,0:T(8,128)(2,1)}, bf16[8,2560]{1,0:T(8,128)(2,1)S(1)}, u32[]{:S(2)}, u32[]{:S(2)}) collective-permute-start(bf16[8,2560]{1,0:T(8,128)(2,1)} %refs_5_.1), channel_id=1, source_target_pairs={{12,0},{13,1},{14,2},{15,3},{8,4},{9,5},{10,6},{11,7},{4,8},{5,9},... | collective-permute-start | bytes 122888 | tf_op jit(solution)/shard_map/ppermute | solution.py:322
  5.1 0.6 %collective-permute-start.2 = (bf16[8,2560]{1,0:T(8,128)(2,1)}, bf16[8,2560]{1,0:T(8,128)(2,1)S(1)}, u32[]{:S(2)}, u32[]{:S(2)}) collective-permute-start(bf16[8,2560]{1,0:T(8,128)(2,1)} %refs_5_.1), channel_id=1, source_target_pairs={{8,0},{9,1},{10,2},{11,3},{12,4},{13,5},{14,6},{15,7},{0,8},{1,9},... | collective-permute-start | bytes 122888 | tf_op jit(solution)/shard_map/ppermute | solution.py:322
  5.6 1.8 %collective-permute-start.3 = (bf16[8,2560]{1,0:T(8,128)(2,1)}, bf16[8,2560]{1,0:T(8,128)(2,1)S(1)}, u32[]{:S(2)}, u32[]{:S(2)}) collective-permute-start(bf16[8,2560]{1,0:T(8,128)(2,1)} %refs_5_.1), channel_id=1, source_target_pairs={{2,0},{3,1},{0,2},{1,3},{6,4},{7,5},{4,6},{5,7},{10,8},{11,9},{8,1... | collective-permute-start | bytes 122888 | tf_op jit(solution)/shard_map/ppermute | solution.py:322
  7.4 1.6 %collective-permute-start.4 = (bf16[8,2560]{1,0:T(8,128)(2,1)S(1)}, bf16[8,2560]{1,0:T(8,128)(2,1)S(1)}, u32[]{:S(2)}, u32[]{:S(2)}) collective-permute-start(bf16[8,2560]{1,0:T(8,128)(2,1)S(1)} %collective-permute-done.1.refs_1_), channel_id=1, source_target_pairs={{2,0},{3,1},{0,2},{1,3},{6,4},{7,5},{4,6},{5,7},{10,8},{11,9},{8,1... | collective-permute-start | bytes 122888 | tf_op jit(solution)/shard_map/ppermute | solution.py:322
  9.0 0.3 collective-permute-done.refs_6_.refs_3_
  9.3 1.5 %collective-permute-start.6 = (bf16[8,2560]{1,0:T(8,128)(2,1)S(1)}, bf16[8,2560]{1,0:T(8,128)(2,1)S(1)}, u32[]{:S(2)}, u32[]{:S(2)}) collective-permute-start(bf16[8,2560]{1,0:T(8,128)(2,1)S(1)} %collective-permute-done.refs_6_.refs_3_), channel_id=1, source_target_pairs={{2,0},{3,1},{0,2},{1,3},{6,4},{7,5},{4,6},{5,7},{10,8},{11,9},{8,1... | collective-permute-start | bytes 122888 | tf_op jit(solution)/shard_map/ppermute | solution.py:322
  10.8 1.1 %collective-permute-start.5 = (bf16[8,2560]{1,0:T(8,128)(2,1)S(1)}, bf16[8,2560]{1,0:T(8,128)(2,1)S(1)}, u32[]{:S(2)}, u32[]{:S(2)}) collective-permute-start(bf16[8,2560]{1,0:T(8,128)(2,1)S(1)} %collective-permute-done.2.refs_2_), channel_id=1, source_target_pairs={{2,0},{3,1},{0,2},{1,3},{6,4},{7,5},{4,6},{5,7},{10,8},{11,9},{8,1... | collective-permute-start | bytes 122888 | tf_op jit(solution)/shard_map/ppermute | solution.py:322
  11.9 2.6 %load.1 = (bf16[528,2560]{1,0:T(8,128)(2,1)S(1)}, bf16[528,2560]{1,0:T(8,128)(2,1)S(1)}, f32[528,128]{1,0:T(8,128)S(1)}, bf16[8,2560]{1,0:T(8,128)(2,1)S(1)}) custom-call(bf16[512,2560]{1,0:T(8,128)(2,1)} %refs_0_.1, bf16[512,2560]{1,0:T(8,128)(2,1)} %refs_1_.1, bf16[8,2560]{1,0:T(8,128)(2,1)} %refs_2_.1, bf16[8,2560]{1,0:T(8,128)(2,1)} %refs_3_.1, ...), custom_call_target="tpu_custom_call" | custom-call | bytes 10485760 | tf_op jit(solution)/shard_map/load/pallas_call | solution.py:214
  14.6 0.2 collective-permute-done.5.refs_6_
  14.9 1.6 %attend.2 = (f32[32,2688]{1,0:T(8,128)S(1)}, f32[32,2688]{1,0:T(8,128)S(1)}) custom-call(f32[528,128]{1,0:T(8,128)S(1)} %get-tuple-element.20.refs_0_, bf16[64,2560]{1,0:T(8,128)(2,1)S(1)} %merge.9.refs_1_, bf16[528,2560]{1,0:T(8,128)(2,1)S(1)} %get-tuple-element.22.refs_2_, bf16[528,2560]{1,0:T(8,128)(2,1)S(1)} %get-tuple-element.23.refs_3_), custom_call_target="tpu_custom_call" | custom-call | flops 346030080 | bytes 5406720 | tf_op jit(solution)/shard_map/attend/pallas_call | solution.py:153
  16.6 1.7 %attend.3 = (bf16[32,2688]{1,0:T(8,128)(2,1)S(1)}, bf16[32,2688]{1,0:T(8,128)(2,1)S(1)}) custom-call(f32[528,128]{1,0:T(8,128)S(1)} %get-tuple-element.20.refs_0_, bf16[64,2560]{1,0:T(8,128)(2,1)S(1)} %collective-permute-done.7.refs_1_, bf16[528,2560]{1,0:T(8,128)(2,1)S(1)} %get-tuple-element.22.refs_2_, bf16[528,2560]{1,0:T(8,128)(2,1)S(1)} %get-tuple-element.23.refs_3_, ...), custom_call_target="tpu_custom_call" | custom-call | flops 346030080 | bytes 5406720 | tf_op jit(solution)/shard_map/attend/pallas_call | solution.py:153
  18.2 0.6 %collective-permute-start.9 = (bf16[32,2688]{1,0:T(8,128)(2,1)S(1)}, bf16[32,2688]{1,0:T(8,128)(2,1)S(1)}, u32[]{:S(2)}, u32[]{:S(2)}) collective-permute-start(bf16[32,2688]{1,0:T(8,128)(2,1)S(1)} %get-tuple-element.29), channel_id=1, source_target_pairs={{0,1},{1,0},{2,3},{3,2},{4,5},{5,4},{6,7},{7,6},{8,9},{9,8},{10,11... | collective-permute-start | bytes 516104 | tf_op jit(solution)/shard_map/ppermute | solution.py:325
  18.8 0.1 collective-permute-start.8
  18.9 1.0 %collective-permute-done.9.refs_1_ = bf16[32,2688]{1,0:T(8,128)(2,1)S(1)} collective-permute-done((bf16[32,2688]{1,0:T(8,128)(2,1)S(1)}, bf16[32,2688]{1,0:T(8,128)(2,1)S(1)}, u32[]{:S(2)}, u32[]{:S(2)}) %collective-permute-start.9) | collective-permute-done | bytes 172064 | tf_op jit(solution)/shard_map/ppermute | solution.py:325
  19.8 0.2 merge.11
  20.1 1.2 %collective-permute-start.10 = (bf16[8,2688]{1,0:T(8,128)(2,1)S(1)}, bf16[8,2688]{1,0:T(8,128)(2,1)S(1)}, u32[]{:S(2)}, u32[]{:S(2)}) collective-permute-start(bf16[8,2688]{1,0:T(8,128)(2,1)S(1)} %get-tuple-element.30), channel_id=1, source_target_pairs={{0,2},{1,3},{2,0},{3,1},{4,6},{5,7},{6,4},{7,5},{8,10},{9,11},{10,... | collective-permute-start | bytes 129032 | tf_op jit(solution)/shard_map/ppermute | solution.py:325
  21.2 0.9 %collective-permute-start.12 = (bf16[8,2688]{1,0:T(8,128)(2,1)S(1)}, bf16[8,2688]{1,0:T(8,128)(2,1)S(1)}, u32[]{:S(2)}, u32[]{:S(2)}) collective-permute-start(bf16[8,2688]{1,0:T(8,128)(2,1)S(1)} %get-tuple-element.32), channel_id=1, source_target_pairs={{0,2},{1,3},{2,0},{3,1},{4,6},{5,7},{6,4},{7,5},{8,10},{9,11},{10,... | collective-permute-start | bytes 129032 | tf_op jit(solution)/shard_map/ppermute | solution.py:325
  22.2 1.1 %collective-permute-start.14 = (bf16[8,2688]{1,0:T(8,128)(2,1)S(1)}, bf16[8,2688]{1,0:T(8,128)(2,1)S(1)}, u32[]{:S(2)}, u32[]{:S(2)}) collective-permute-start(bf16[8,2688]{1,0:T(8,128)(2,1)S(1)} %get-tuple-element.34), channel_id=1, source_target_pairs={{0,2},{1,3},{2,0},{3,1},{4,6},{5,7},{6,4},{7,5},{8,10},{9,11},{10,... | collective-permute-start | bytes 129032 | tf_op jit(solution)/shard_map/ppermute | solution.py:325
  23.3 0.3 merge.10
  23.6 0.9 %collective-permute-done.10.refs_1_ = bf16[8,2688]{1,0:T(8,128)(2,1)S(1)} collective-permute-done((bf16[8,2688]{1,0:T(8,128)(2,1)S(1)}, bf16[8,2688]{1,0:T(8,128)(2,1)S(1)}, u32[]{:S(2)}, u32[]{:S(2)}) %collective-permute-start.10) | collective-permute-done | bytes 43040 | tf_op jit(solution)/shard_map/ppermute | solution.py:325
  24.4 0.1 merge.12
  24.6 2.7 %collective-permute-start.11 = (bf16[8,2688]{1,0:T(8,128)(2,1)S(1)}, bf16[8,2688]{1,0:T(8,128)(2,1)S(1)}, u32[]{:S(2)}, u32[]{:S(2)}) collective-permute-start(bf16[8,2688]{1,0:T(8,128)(2,1)S(1)} %merge.12), channel_id=1, source_target_pairs={{0,12},{1,13},{2,14},{3,15},{4,8},{5,9},{6,10},{7,11},{8,4},{9,5},... | collective-permute-start | bytes 129032 | tf_op jit(solution)/shard_map/ppermute | solution.py:325
  27.2 0.1 merge.13
  27.4 0.4 %collective-permute-start.13 = (bf16[8,2688]{1,0:T(8,128)(2,1)S(1)}, bf16[8,2688]{1,0:T(8,128)(2,1)S(1)}, u32[]{:S(2)}, u32[]{:S(2)}) collective-permute-start(bf16[8,2688]{1,0:T(8,128)(2,1)S(1)} %merge.13), channel_id=1, source_target_pairs={{0,8},{1,9},{2,10},{3,11},{4,12},{5,13},{6,14},{7,15},{8,0},{9,1},... | collective-permute-start | bytes 129032 | tf_op jit(solution)/shard_map/ppermute | solution.py:325
  27.8 0.1 merge.14.refs_2_
  28.0 1.5 %collective-permute-start.15 = (bf16[8,2688]{1,0:T(8,128)(2,1)S(1)}, bf16[8,2688]{1,0:T(8,128)(2,1)S(1)}, u32[]{:S(2)}, u32[]{:S(2)}) collective-permute-start(bf16[8,2688]{1,0:T(8,128)(2,1)S(1)} %merge.14.refs_2_), channel_id=1, source_target_pairs={{0,4},{1,5},{2,6},{3,7},{4,0},{5,1},{6,2},{7,3},{8,12},{9,13},{10,... | collective-permute-start | bytes 129032 | tf_op jit(solution)/shard_map/ppermute | solution.py:325
  29.5 0.1 merge.16
  29.6 1.4 %collective-permute-start.16 = (bf16[8,2688]{1,0:T(8,128)(2,1)S(1)}, bf16[8,2688]{1,0:T(8,128)(2,1)S(1)}, u32[]{:S(2)}, u32[]{:S(2)}) collective-permute-start(bf16[8,2688]{1,0:T(8,128)(2,1)S(1)} %merge.16), channel_id=1, source_target_pairs={{0,2},{1,3},{2,0},{3,1},{4,6},{5,7},{6,4},{7,5},{8,10},{9,11},{10,... | collective-permute-start | bytes 129032 | tf_op jit(solution)/shard_map/ppermute | solution.py:325
  31.0 1.6 %collective-permute-done.13.refs_2_ = bf16[8,2688]{1,0:T(8,128)(2,1)S(1)} collective-permute-done((bf16[8,2688]{1,0:T(8,128)(2,1)S(1)}, bf16[8,2688]{1,0:T(8,128)(2,1)S(1)}, u32[]{:S(2)}, u32[]{:S(2)}) %collective-permute-start.13) | collective-permute-done | bytes 43040 | tf_op jit(solution)/shard_map/ppermute | solution.py:325
  32.5 0.2 merge.15.refs_0_
  32.7 1.0 %collective-permute-done.16.refs_1_ = bf16[8,2688]{1,0:T(8,128)(2,1)S(1)} collective-permute-done((bf16[8,2688]{1,0:T(8,128)(2,1)S(1)}, bf16[8,2688]{1,0:T(8,128)(2,1)S(1)}, u32[]{:S(2)}, u32[]{:S(2)}) %collective-permute-start.16) | collective-permute-done | bytes 43040 | tf_op jit(solution)/shard_map/ppermute | solution.py:325
  33.7 0.8 %merge.17 = bf16[8,2560]{1,0:T(8,128)(2,1)} custom-call(f32[8,2688]{1,0:T(8,128)S(1)} %merge.15.refs_0_, bf16[8,2688]{1,0:T(8,128)(2,1)S(1)} %collective-permute-done.16.refs_1_), custom_call_target="tpu_custom_call" | custom-call | flops 172032 | bytes 172032 | tf_op jit(solution)/shard_map/merge/pallas_call | solution.py:302
  (14 shorter events, 0.1 us)
Async XLA Ops:
  0.0 7.4 %collective-permute-start.1 = (bf16[8,2560]{1,0:T(8,128)(2,1)}, bf16[8,2560]{1,0:T(8,128)(2,1)S(1)}, u32[]{:S(2)}, u32[]{:S(2)}) collective-permute-start(bf16[8,2560]{1,0:T(8,128)(2,1)} %refs_5_.1), channel_id=1, source_target_pairs={{12,0},{13,1},{14,2},{15,3},{8,4},{9,5},{10,6},{11,7},{4,8},{5,9},... | collective-permute-start | bytes 122888 | tf_op jit(solution)/shard_map/ppermute | solution.py:322
  5.0 4.2 %collective-permute-start = (bf16[8,2560]{1,0:T(8,128)(2,1)}, bf16[8,2560]{1,0:T(8,128)(2,1)S(1)}, u32[]{:S(2)}, u32[]{:S(2)}) collective-permute-start(bf16[8,2560]{1,0:T(8,128)(2,1)} %refs_5_.1), channel_id=1, source_target_pairs={{4,0},{5,1},{6,2},{7,3},{0,4},{1,5},{2,6},{3,7},{12,8},{13,9},{14,... | collective-permute-start | bytes 122888 | tf_op jit(solution)/shard_map/ppermute | solution.py:322
  5.1 5.7 %collective-permute-start.2 = (bf16[8,2560]{1,0:T(8,128)(2,1)}, bf16[8,2560]{1,0:T(8,128)(2,1)S(1)}, u32[]{:S(2)}, u32[]{:S(2)}) collective-permute-start(bf16[8,2560]{1,0:T(8,128)(2,1)} %refs_5_.1), channel_id=1, source_target_pairs={{8,0},{9,1},{10,2},{11,3},{12,4},{13,5},{14,6},{15,7},{0,8},{1,9},... | collective-permute-start | bytes 122888 | tf_op jit(solution)/shard_map/ppermute | solution.py:322
  5.6 8.9 %collective-permute-start.3 = (bf16[8,2560]{1,0:T(8,128)(2,1)}, bf16[8,2560]{1,0:T(8,128)(2,1)S(1)}, u32[]{:S(2)}, u32[]{:S(2)}) collective-permute-start(bf16[8,2560]{1,0:T(8,128)(2,1)} %refs_5_.1), channel_id=1, source_target_pairs={{2,0},{3,1},{0,2},{1,3},{6,4},{7,5},{4,6},{5,7},{10,8},{11,9},{8,1... | collective-permute-start | bytes 122888 | tf_op jit(solution)/shard_map/ppermute | solution.py:322
  7.4 7.2 %collective-permute-start.4 = (bf16[8,2560]{1,0:T(8,128)(2,1)S(1)}, bf16[8,2560]{1,0:T(8,128)(2,1)S(1)}, u32[]{:S(2)}, u32[]{:S(2)}) collective-permute-start(bf16[8,2560]{1,0:T(8,128)(2,1)S(1)} %collective-permute-done.1.refs_1_), channel_id=1, source_target_pairs={{2,0},{3,1},{0,2},{1,3},{6,4},{7,5},{4,6},{5,7},{10,8},{11,9},{8,1... | collective-permute-start | bytes 122888 | tf_op jit(solution)/shard_map/ppermute | solution.py:322
  9.3 5.3 %collective-permute-start.6 = (bf16[8,2560]{1,0:T(8,128)(2,1)S(1)}, bf16[8,2560]{1,0:T(8,128)(2,1)S(1)}, u32[]{:S(2)}, u32[]{:S(2)}) collective-permute-start(bf16[8,2560]{1,0:T(8,128)(2,1)S(1)} %collective-permute-done.refs_6_.refs_3_), channel_id=1, source_target_pairs={{2,0},{3,1},{0,2},{1,3},{6,4},{7,5},{4,6},{5,7},{10,8},{11,9},{8,1... | collective-permute-start | bytes 122888 | tf_op jit(solution)/shard_map/ppermute | solution.py:322
  10.8 4.0 %collective-permute-start.5 = (bf16[8,2560]{1,0:T(8,128)(2,1)S(1)}, bf16[8,2560]{1,0:T(8,128)(2,1)S(1)}, u32[]{:S(2)}, u32[]{:S(2)}) collective-permute-start(bf16[8,2560]{1,0:T(8,128)(2,1)S(1)} %collective-permute-done.2.refs_2_), channel_id=1, source_target_pairs={{2,0},{3,1},{0,2},{1,3},{6,4},{7,5},{4,6},{5,7},{10,8},{11,9},{8,1... | collective-permute-start | bytes 122888 | tf_op jit(solution)/shard_map/ppermute | solution.py:322
  14.8 1.7 %collective-permute-start.7 = (bf16[64,2560]{1,0:T(8,128)(2,1)S(1)}, bf16[64,2560]{1,0:T(8,128)(2,1)S(1)}, u32[]{:S(2)}, u32[]{:S(2)}) collective-permute-start(bf16[64,2560]{1,0:T(8,128)(2,1)S(1)} %merge.9.refs_1_), channel_id=1, source_target_pairs={{1,0},{0,1},{3,2},{2,3},{5,4},{4,5},{7,6},{6,7},{9,8},{8,9},{11,10... | collective-permute-start | bytes 983048 | tf_op jit(solution)/shard_map/ppermute | solution.py:322
  18.2 1.6 %collective-permute-start.9 = (bf16[32,2688]{1,0:T(8,128)(2,1)S(1)}, bf16[32,2688]{1,0:T(8,128)(2,1)S(1)}, u32[]{:S(2)}, u32[]{:S(2)}) collective-permute-start(bf16[32,2688]{1,0:T(8,128)(2,1)S(1)} %get-tuple-element.29), channel_id=1, source_target_pairs={{0,1},{1,0},{2,3},{3,2},{4,5},{5,4},{6,7},{7,6},{8,9},{9,8},{10,11... | collective-permute-start | bytes 516104 | tf_op jit(solution)/shard_map/ppermute | solution.py:325
  18.8 4.5 %collective-permute-start.8 = (bf16[32,2688]{1,0:T(8,128)(2,1)S(1)}, bf16[32,2688]{1,0:T(8,128)(2,1)S(1)}, u32[]{:S(2)}, u32[]{:S(2)}) collective-permute-start(bf16[32,2688]{1,0:T(8,128)(2,1)S(1)} %get-tuple-element.25), channel_id=1, source_target_pairs={{0,1},{1,0},{2,3},{3,2},{4,5},{5,4},{6,7},{7,6},{8,9},{9,8},{10,11... | collective-permute-start | bytes 516104 | tf_op jit(solution)/shard_map/ppermute | solution.py:325
  20.1 4.4 %collective-permute-start.10 = (bf16[8,2688]{1,0:T(8,128)(2,1)S(1)}, bf16[8,2688]{1,0:T(8,128)(2,1)S(1)}, u32[]{:S(2)}, u32[]{:S(2)}) collective-permute-start(bf16[8,2688]{1,0:T(8,128)(2,1)S(1)} %get-tuple-element.30), channel_id=1, source_target_pairs={{0,2},{1,3},{2,0},{3,1},{4,6},{5,7},{6,4},{7,5},{8,10},{9,11},{10,... | collective-permute-start | bytes 129032 | tf_op jit(solution)/shard_map/ppermute | solution.py:325
  21.2 6.0 %collective-permute-start.12 = (bf16[8,2688]{1,0:T(8,128)(2,1)S(1)}, bf16[8,2688]{1,0:T(8,128)(2,1)S(1)}, u32[]{:S(2)}, u32[]{:S(2)}) collective-permute-start(bf16[8,2688]{1,0:T(8,128)(2,1)S(1)} %get-tuple-element.32), channel_id=1, source_target_pairs={{0,2},{1,3},{2,0},{3,1},{4,6},{5,7},{6,4},{7,5},{8,10},{9,11},{10,... | collective-permute-start | bytes 129032 | tf_op jit(solution)/shard_map/ppermute | solution.py:325
  22.2 5.7 %collective-permute-start.14 = (bf16[8,2688]{1,0:T(8,128)(2,1)S(1)}, bf16[8,2688]{1,0:T(8,128)(2,1)S(1)}, u32[]{:S(2)}, u32[]{:S(2)}) collective-permute-start(bf16[8,2688]{1,0:T(8,128)(2,1)S(1)} %get-tuple-element.34), channel_id=1, source_target_pairs={{0,2},{1,3},{2,0},{3,1},{4,6},{5,7},{6,4},{7,5},{8,10},{9,11},{10,... | collective-permute-start | bytes 129032 | tf_op jit(solution)/shard_map/ppermute | solution.py:325
  24.6 6.4 %collective-permute-start.11 = (bf16[8,2688]{1,0:T(8,128)(2,1)S(1)}, bf16[8,2688]{1,0:T(8,128)(2,1)S(1)}, u32[]{:S(2)}, u32[]{:S(2)}) collective-permute-start(bf16[8,2688]{1,0:T(8,128)(2,1)S(1)} %merge.12), channel_id=1, source_target_pairs={{0,12},{1,13},{2,14},{3,15},{4,8},{5,9},{6,10},{7,11},{8,4},{9,5},... | collective-permute-start | bytes 129032 | tf_op jit(solution)/shard_map/ppermute | solution.py:325
  27.4 5.1 %collective-permute-start.13 = (bf16[8,2688]{1,0:T(8,128)(2,1)S(1)}, bf16[8,2688]{1,0:T(8,128)(2,1)S(1)}, u32[]{:S(2)}, u32[]{:S(2)}) collective-permute-start(bf16[8,2688]{1,0:T(8,128)(2,1)S(1)} %merge.13), channel_id=1, source_target_pairs={{0,8},{1,9},{2,10},{3,11},{4,12},{5,13},{6,14},{7,15},{8,0},{9,1},... | collective-permute-start | bytes 129032 | tf_op jit(solution)/shard_map/ppermute | solution.py:325
  28.0 4.6 %collective-permute-start.15 = (bf16[8,2688]{1,0:T(8,128)(2,1)S(1)}, bf16[8,2688]{1,0:T(8,128)(2,1)S(1)}, u32[]{:S(2)}, u32[]{:S(2)}) collective-permute-start(bf16[8,2688]{1,0:T(8,128)(2,1)S(1)} %merge.14.refs_2_), channel_id=1, source_target_pairs={{0,4},{1,5},{2,6},{3,7},{4,0},{5,1},{6,2},{7,3},{8,12},{9,13},{10,... | collective-permute-start | bytes 129032 | tf_op jit(solution)/shard_map/ppermute | solution.py:325
  29.6 4.1 %collective-permute-start.16 = (bf16[8,2688]{1,0:T(8,128)(2,1)S(1)}, bf16[8,2688]{1,0:T(8,128)(2,1)S(1)}, u32[]{:S(2)}, u32[]{:S(2)}) collective-permute-start(bf16[8,2688]{1,0:T(8,128)(2,1)S(1)} %merge.16), channel_id=1, source_target_pairs={{0,2},{1,3},{2,0},{3,1},{4,6},{5,7},{6,4},{7,5},{8,10},{9,11},{10,... | collective-permute-start | bytes 129032 | tf_op jit(solution)/shard_map/ppermute | solution.py:325

commit v24 on v22

--- a/solution.py
+++ b/solution.py
@@ -109,15 +109,15 @@
                         o_ref[at, cols] = one.astype(o_ref.dtype)
 
             score, top, weights = {}, {}, {}
-            for t in range(-3, group + 1):
-                if 0 <= t + 3 < group:
-                    score[t + 3] = scores(t + 3)
+            for t in range(-4, group + 2):
+                if 0 <= t + 4 < group:
+                    score[t + 4] = scores(t + 4)
                 if 0 <= t + 1 < group:
                     score[t + 1], top[t + 1] = masked(score[t + 1])
                 if 0 <= t < group:
                     weights[t] = weigh(t, score.pop(t), top.pop(t))
-                if 0 <= t - 1:
-                    gather_values(t - 1, weights.pop(t - 1))
+                if 0 <= t - 2:
+                    gather_values(t - 2, weights.pop(t - 2))
             return carry
 
         lax.fori_loop(0, steps, heads_of, 0)
@@ -264,13 +264,36 @@
 
 def finish(ins, heads):
     rows = ins[0].shape[0]
-
-    def body(*refs):
-        out = refs[len(ins)]
-        for cols, total in merged([getter(r) for r in refs[: len(ins)]], heads, True):
-            out[:, cols] = total.astype(out.dtype)
-
-    return call_merge(body, ins, [jax.ShapeDtypeStruct((rows, heads * HD), BF16)])[0]
+    runs = next(n for n in (4, 2, 1) if heads % n == 0)
+    wide = heads // runs * HD
+
+    def body(*refs):
+        out, buffer, sems = refs[len(ins) :]
+        copies = []
+        parts = merged([getter(r) for r in refs[: len(ins)]], heads, True)
+        for head, (cols, total) in enumerate(parts):
+            buffer[:, cols] = total.astype(buffer.dtype)
+            if (head + 1) % (heads // runs) == 0:
+                run = pl.ds(len(copies) * wide, wide)
+                copy = pltpu.make_async_copy(
+                    buffer.at[:, run], out.at[:, run], sems.at[len(copies)]
+                )
+                copy.start()
+                copies.append(copy)
+        for copy in copies:
+            copy.wait()
+
+    return pl.pallas_call(
+        body,
+        in_specs=[pl.BlockSpec(memory_space=pltpu.VMEM)] * len(ins),
+        out_specs=pl.BlockSpec(memory_space=pltpu.HBM),
+        out_shape=jax.ShapeDtypeStruct((rows, heads * HD), BF16),
+        scratch_shapes=[
+            pltpu.VMEM((rows, heads * HD), BF16), pltpu.SemaphoreType.DMA((runs,))
+        ],
+        compiler_params=pltpu.CompilerParams(vmem_limit_bytes=48 * 1024 * 1024),
+        name="finish",
+    )(*ins)
 
 
 def join(pieces, after=()):

time: 33.8 us -> 33.6 us (level)
    pallas_call x0 -> x1, Pallas kernels: none -> 0.91 us  [finish(): pl.pallas_call(body, in_specs=[pl.BlockSpec(memory_space=pltpu.VMEM)] * l...]
    pallas_call x8 -> x7, Pallas kernels: 2.06 us -> 1.17 us  [call_merge(): pl.pallas_call(body, in_specs=[pl.BlockSpec(memory_space=pltpu.VMEM)] * l...]
  transfers between devices with their start and end apart: 17 -> 17, of which waited for: 5 -> 7; matrix products, arithmetic and copies ran while one was open for 0% -> 0% of each run, Pallas kernels for 16% -> 16%
where the time goes in v24:
time: 33.6 us; the launch traced here: 33.4 us
  starting transfers between devices  21 us (62%)
  Pallas kernels  7.74 us (23%)
  waiting for transfers between devices  4.6 us (14%)
    ppermute x8, starting transfers between devices, fetch(): return lax.ppermute(x, 'seq', partner_perm(shape, by, False))  11.7 us
    ppermute x9, starting transfers between devices, give(): return lax.ppermute(x, 'seq', partner_perm(shape, by, True))  9.29 us
    ppermute x9, waiting for transfers between devices, give(): return lax.ppermute(x, 'seq', partner_perm(shape, by, True))  3.98 us
    pallas_call x2, Pallas kernels, attend(): pl.pallas_call(body, in_specs=[pl.BlockSpec(memory_space=pltpu.VMEM)] * 4...  3.02 us
    pallas_call x1, Pallas kernels, load(): pl.pallas_call(body, in_specs=[in_hbm] * len(held) + [pl.BlockSpec(memory...  2.65 us
    pallas_call x7, Pallas kernels, call_merge(): pl.pallas_call(body, in_specs=[pl.BlockSpec(memory_space=pltpu.VMEM)] * l...  1.17 us
    pallas_call x1, Pallas kernels, finish(): pl.pallas_call(body, in_specs=[pl.BlockSpec(memory_space=pltpu.VMEM)] * l...  0.91 us
  transfers between devices with their start and end apart: 17, of which 7 were waited for; matrix products, arithmetic and copies ran while one was open for 0% of the time, Pallas kernels for 16%

profile of v24, /device:TPU:0, one launch (start us, length us, event | category | flops | bytes accessed | tf_op | source)
XLA Modules:
  0.0 33.4 jit_solution(8090981191977576510)
XLA Ops:
  0.0 5.0 %collective-permute-start.1 = (bf16[8,2560]{1,0:T(8,128)(2,1)}, bf16[8,2560]{1,0:T(8,128)(2,1)S(1)}, u32[]{:S(2)}, u32[]{:S(2)}) collective-permute-start(bf16[8,2560]{1,0:T(8,128)(2,1)} %refs_5_.1), channel_id=1, source_target_pairs={{12,0},{13,1},{14,2},{15,3},{8,4},{9,5},{10,6},{11,7},{4,8},{5,9},... | collective-permute-start | bytes 122888 | tf_op jit(solution)/shard_map/ppermute | solution.py:333
  5.1 0.6 %collective-permute-start.2 = (bf16[8,2560]{1,0:T(8,128)(2,1)}, bf16[8,2560]{1,0:T(8,128)(2,1)S(1)}, u32[]{:S(2)}, u32[]{:S(2)}) collective-permute-start(bf16[8,2560]{1,0:T(8,128)(2,1)} %refs_5_.1), channel_id=1, source_target_pairs={{8,0},{9,1},{10,2},{11,3},{12,4},{13,5},{14,6},{15,7},{0,8},{1,9},... | collective-permute-start | bytes 122888 | tf_op jit(solution)/shard_map/ppermute | solution.py:333
  5.6 1.8 %collective-permute-start.3 = (bf16[8,2560]{1,0:T(8,128)(2,1)}, bf16[8,2560]{1,0:T(8,128)(2,1)S(1)}, u32[]{:S(2)}, u32[]{:S(2)}) collective-permute-start(bf16[8,2560]{1,0:T(8,128)(2,1)} %refs_5_.1), channel_id=1, source_target_pairs={{2,0},{3,1},{0,2},{1,3},{6,4},{7,5},{4,6},{5,7},{10,8},{11,9},{8,1... | collective-permute-start | bytes 122888 | tf_op jit(solution)/shard_map/ppermute | solution.py:333
  7.4 1.6 %collective-permute-start.4 = (bf16[8,2560]{1,0:T(8,128)(2,1)S(1)}, bf16[8,2560]{1,0:T(8,128)(2,1)S(1)}, u32[]{:S(2)}, u32[]{:S(2)}) collective-permute-start(bf16[8,2560]{1,0:T(8,128)(2,1)S(1)} %collective-permute-done.1.refs_1_), channel_id=1, source_target_pairs={{2,0},{3,1},{0,2},{1,3},{6,4},{7,5},{4,6},{5,7},{10,8},{11,9},{8,1... | collective-permute-start | bytes 122888 | tf_op jit(solution)/shard_map/ppermute | solution.py:333
  9.0 0.3 collective-permute-done.refs_6_.refs_3_
  9.3 1.5 %collective-permute-start.6 = (bf16[8,2560]{1,0:T(8,128)(2,1)S(1)}, bf16[8,2560]{1,0:T(8,128)(2,1)S(1)}, u32[]{:S(2)}, u32[]{:S(2)}) collective-permute-start(bf16[8,2560]{1,0:T(8,128)(2,1)S(1)} %collective-permute-done.refs_6_.refs_3_), channel_id=1, source_target_pairs={{2,0},{3,1},{0,2},{1,3},{6,4},{7,5},{4,6},{5,7},{10,8},{11,9},{8,1... | collective-permute-start | bytes 122888 | tf_op jit(solution)/shard_map/ppermute | solution.py:333
  10.8 1.1 %collective-permute-start.5 = (bf16[8,2560]{1,0:T(8,128)(2,1)S(1)}, bf16[8,2560]{1,0:T(8,128)(2,1)S(1)}, u32[]{:S(2)}, u32[]{:S(2)}) collective-permute-start(bf16[8,2560]{1,0:T(8,128)(2,1)S(1)} %collective-permute-done.2.refs_2_), channel_id=1, source_target_pairs={{2,0},{3,1},{0,2},{1,3},{6,4},{7,5},{4,6},{5,7},{10,8},{11,9},{8,1... | collective-permute-start | bytes 122888 | tf_op jit(solution)/shard_map/ppermute | solution.py:333
  11.9 2.6 %load.1 = (bf16[528,2560]{1,0:T(8,128)(2,1)S(1)}, bf16[528,2560]{1,0:T(8,128)(2,1)S(1)}, f32[528,128]{1,0:T(8,128)S(1)}, bf16[8,2560]{1,0:T(8,128)(2,1)S(1)}) custom-call(bf16[512,2560]{1,0:T(8,128)(2,1)} %refs_0_.1, bf16[512,2560]{1,0:T(8,128)(2,1)} %refs_1_.1, bf16[8,2560]{1,0:T(8,128)(2,1)} %refs_2_.1, bf16[8,2560]{1,0:T(8,128)(2,1)} %refs_3_.1, ...), custom_call_target="tpu_custom_call" | custom-call | bytes 10485760 | tf_op jit(solution)/shard_map/load/pallas_call | solution.py:214
  14.6 0.2 collective-permute-done.5.refs_6_
  14.8 0.1 collective-permute-start.7
  14.9 1.5 %attend.2 = (f32[32,2688]{1,0:T(8,128)S(1)}, f32[32,2688]{1,0:T(8,128)S(1)}) custom-call(f32[528,128]{1,0:T(8,128)S(1)} %get-tuple-element.21.refs_0_, bf16[64,2560]{1,0:T(8,128)(2,1)S(1)} %merge.7.refs_1_, bf16[528,2560]{1,0:T(8,128)(2,1)S(1)} %get-tuple-element.23.refs_2_, bf16[528,2560]{1,0:T(8,128)(2,1)S(1)} %get-tuple-element.24.refs_3_), custom_call_target="tpu_custom_call" | custom-call | flops 346030080 | bytes 5406720 | tf_op jit(solution)/shard_map/attend/pallas_call | solution.py:153
  16.4 0.1 collective-permute-done.7.refs_1_
  16.5 1.5 %attend.3 = (bf16[32,2688]{1,0:T(8,128)(2,1)S(1)}, bf16[32,2688]{1,0:T(8,128)(2,1)S(1)}) custom-call(f32[528,128]{1,0:T(8,128)S(1)} %get-tuple-element.21.refs_0_, bf16[64,2560]{1,0:T(8,128)(2,1)S(1)} %collective-permute-done.7.refs_1_, bf16[528,2560]{1,0:T(8,128)(2,1)S(1)} %get-tuple-element.23.refs_2_, bf16[528,2560]{1,0:T(8,128)(2,1)S(1)} %get-tuple-element.24.refs_3_, ...), custom_call_target="tpu_custom_call" | custom-call | flops 346030080 | bytes 5406720 | tf_op jit(solution)/shard_map/attend/pallas_call | solution.py:153
  18.0 0.5 %collective-permute-start.9 = (bf16[32,2688]{1,0:T(8,128)(2,1)S(1)}, bf16[32,2688]{1,0:T(8,128)(2,1)S(1)}, u32[]{:S(2)}, u32[]{:S(2)}) collective-permute-start(bf16[32,2688]{1,0:T(8,128)(2,1)S(1)} %get-tuple-element.29), channel_id=1, source_target_pairs={{0,1},{1,0},{2,3},{3,2},{4,5},{5,4},{6,7},{7,6},{8,9},{9,8},{10,11... | collective-permute-start | bytes 516104 | tf_op jit(solution)/shard_map/ppermute | solution.py:336
  18.5 0.1 collective-permute-start.8
  18.6 0.9 %collective-permute-done.9.refs_1_ = bf16[32,2688]{1,0:T(8,128)(2,1)S(1)} collective-permute-done((bf16[32,2688]{1,0:T(8,128)(2,1)S(1)}, bf16[32,2688]{1,0:T(8,128)(2,1)S(1)}, u32[]{:S(2)}, u32[]{:S(2)}) %collective-permute-start.9) | collective-permute-done | bytes 172064 | tf_op jit(solution)/shard_map/ppermute | solution.py:336
  19.5 0.3 merge.9
  19.8 1.2 %collective-permute-start.11 = (bf16[8,2688]{1,0:T(8,128)(2,1)S(1)}, bf16[8,2688]{1,0:T(8,128)(2,1)S(1)}, u32[]{:S(2)}, u32[]{:S(2)}) collective-permute-start(bf16[8,2688]{1,0:T(8,128)(2,1)S(1)} %get-tuple-element.32), channel_id=1, source_target_pairs={{0,2},{1,3},{2,0},{3,1},{4,6},{5,7},{6,4},{7,5},{8,10},{9,11},{10,... | collective-permute-start | bytes 129032 | tf_op jit(solution)/shard_map/ppermute | solution.py:336
  21.0 0.9 %collective-permute-start.13 = (bf16[8,2688]{1,0:T(8,128)(2,1)S(1)}, bf16[8,2688]{1,0:T(8,128)(2,1)S(1)}, u32[]{:S(2)}, u32[]{:S(2)}) collective-permute-start(bf16[8,2688]{1,0:T(8,128)(2,1)S(1)} %get-tuple-element.34), channel_id=1, source_target_pairs={{0,2},{1,3},{2,0},{3,1},{4,6},{5,7},{6,4},{7,5},{8,10},{9,11},{10,... | collective-permute-start | bytes 129032 | tf_op jit(solution)/shard_map/ppermute | solution.py:336
  21.9 1.1 %collective-permute-start.15 = (bf16[8,2688]{1,0:T(8,128)(2,1)S(1)}, bf16[8,2688]{1,0:T(8,128)(2,1)S(1)}, u32[]{:S(2)}, u32[]{:S(2)}) collective-permute-start(bf16[8,2688]{1,0:T(8,128)(2,1)S(1)} %get-tuple-element.36), channel_id=1, source_target_pairs={{0,2},{1,3},{2,0},{3,1},{4,6},{5,7},{6,4},{7,5},{8,10},{9,11},{10,... | collective-permute-start | bytes 129032 | tf_op jit(solution)/shard_map/ppermute | solution.py:336
  23.0 0.9 %collective-permute-start.10 = (bf16[8,2688]{1,0:T(8,128)(2,1)S(1)}, bf16[8,2688]{1,0:T(8,128)(2,1)S(1)}, u32[]{:S(2)}, u32[]{:S(2)}) collective-permute-start(bf16[8,2688]{1,0:T(8,128)(2,1)S(1)} %get-tuple-element.30), channel_id=1, source_target_pairs={{0,2},{1,3},{2,0},{3,1},{4,6},{5,7},{6,4},{7,5},{8,10},{9,11},{10,... | collective-permute-start | bytes 129032 | tf_op jit(solution)/shard_map/ppermute | solution.py:336
  24.0 0.3 merge.8
  24.3 0.1 merge.11
  24.4 2.8 %collective-permute-start.12 = (bf16[8,2688]{1,0:T(8,128)(2,1)S(1)}, bf16[8,2688]{1,0:T(8,128)(2,1)S(1)}, u32[]{:S(2)}, u32[]{:S(2)}) collective-permute-start(bf16[8,2688]{1,0:T(8,128)(2,1)S(1)} %merge.11), channel_id=1, source_target_pairs={{0,12},{1,13},{2,14},{3,15},{4,8},{5,9},{6,10},{7,11},{8,4},{9,5},... | collective-permute-start | bytes 129032 | tf_op jit(solution)/shard_map/ppermute | solution.py:336
  27.2 0.1 merge.12
  27.3 0.4 %collective-permute-start.14 = (bf16[8,2688]{1,0:T(8,128)(2,1)S(1)}, bf16[8,2688]{1,0:T(8,128)(2,1)S(1)}, u32[]{:S(2)}, u32[]{:S(2)}) collective-permute-start(bf16[8,2688]{1,0:T(8,128)(2,1)S(1)} %merge.12), channel_id=1, source_target_pairs={{0,8},{1,9},{2,10},{3,11},{4,12},{5,13},{6,14},{7,15},{8,0},{9,1},... | collective-permute-start | bytes 129032 | tf_op jit(solution)/shard_map/ppermute | solution.py:336
  27.8 0.1 merge.13
  27.9 1.4 %collective-permute-start.16 = (bf16[8,2688]{1,0:T(8,128)(2,1)S(1)}, bf16[8,2688]{1,0:T(8,128)(2,1)S(1)}, u32[]{:S(2)}, u32[]{:S(2)}) collective-permute-start(bf16[8,2688]{1,0:T(8,128)(2,1)S(1)} %merge.13), channel_id=1, source_target_pairs={{0,4},{1,5},{2,6},{3,7},{4,0},{5,1},{6,2},{7,3},{8,12},{9,13},{10,... | collective-permute-start | bytes 129032 | tf_op jit(solution)/shard_map/ppermute | solution.py:336
  29.3 0.1 merge.10.refs_0_
  29.4 0.8 %collective-permute-done.12.refs_1_ = bf16[8,2688]{1,0:T(8,128)(2,1)S(1)} collective-permute-done((bf16[8,2688]{1,0:T(8,128)(2,1)S(1)}, bf16[8,2688]{1,0:T(8,128)(2,1)S(1)}, u32[]{:S(2)}, u32[]{:S(2)}) %collective-permute-start.12) | collective-permute-done | bytes 43040 | tf_op jit(solution)/shard_map/ppermute | solution.py:336
  30.3 2.1 %collective-permute-done.14.refs_2_ = bf16[8,2688]{1,0:T(8,128)(2,1)S(1)} collective-permute-done((bf16[8,2688]{1,0:T(8,128)(2,1)S(1)}, bf16[8,2688]{1,0:T(8,128)(2,1)S(1)}, u32[]{:S(2)}, u32[]{:S(2)}) %collective-permute-start.14) | collective-permute-done | bytes 43040 | tf_op jit(solution)/shard_map/ppermute | solution.py:336
  32.5 0.9 %finish.1 = bf16[8,2560]{1,0:T(8,128)(2,1)} custom-call(f32[8,2688]{1,0:T(8,128)S(1)} %merge.10.refs_0_, bf16[8,2688]{1,0:T(8,128)(2,1)S(1)} %collective-permute-done.12.refs_1_, bf16[8,2688]{1,0:T(8,128)(2,1)S(1)} %collective-permute-done.14.refs_2_, bf16[8,2688]{1,0:T(8,128)(2,1)S(1)} %collective-permute-done.16.refs_3_), custom_call_target="tpu_custom_call" | custom-call | tf_op jit(solution)/shard_map/finish/pallas_call | solution.py:286
  (13 shorter events, 0.1 us)
Async XLA Ops:
  0.0 7.4 %collective-permute-start.1 = (bf16[8,2560]{1,0:T(8,128)(2,1)}, bf16[8,2560]{1,0:T(8,128)(2,1)S(1)}, u32[]{:S(2)}, u32[]{:S(2)}) collective-permute-start(bf16[8,2560]{1,0:T(8,128)(2,1)} %refs_5_.1), channel_id=1, source_target_pairs={{12,0},{13,1},{14,2},{15,3},{8,4},{9,5},{10,6},{11,7},{4,8},{5,9},... | collective-permute-start | bytes 122888 | tf_op jit(solution)/shard_map/ppermute | solution.py:333
  5.0 4.2 %collective-permute-start = (bf16[8,2560]{1,0:T(8,128)(2,1)}, bf16[8,2560]{1,0:T(8,128)(2,1)S(1)}, u32[]{:S(2)}, u32[]{:S(2)}) collective-permute-start(bf16[8,2560]{1,0:T(8,128)(2,1)} %refs_5_.1), channel_id=1, source_target_pairs={{4,0},{5,1},{6,2},{7,3},{0,4},{1,5},{2,6},{3,7},{12,8},{13,9},{14,... | collective-permute-start | bytes 122888 | tf_op jit(solution)/shard_map/ppermute | solution.py:333
  5.1 5.7 %collective-permute-start.2 = (bf16[8,2560]{1,0:T(8,128)(2,1)}, bf16[8,2560]{1,0:T(8,128)(2,1)S(1)}, u32[]{:S(2)}, u32[]{:S(2)}) collective-permute-start(bf16[8,2560]{1,0:T(8,128)(2,1)} %refs_5_.1), channel_id=1, source_target_pairs={{8,0},{9,1},{10,2},{11,3},{12,4},{13,5},{14,6},{15,7},{0,8},{1,9},... | collective-permute-start | bytes 122888 | tf_op jit(solution)/shard_map/ppermute | solution.py:333
  5.6 8.9 %collective-permute-start.3 = (bf16[8,2560]{1,0:T(8,128)(2,1)}, bf16[8,2560]{1,0:T(8,128)(2,1)S(1)}, u32[]{:S(2)}, u32[]{:S(2)}) collective-permute-start(bf16[8,2560]{1,0:T(8,128)(2,1)} %refs_5_.1), channel_id=1, source_target_pairs={{2,0},{3,1},{0,2},{1,3},{6,4},{7,5},{4,6},{5,7},{10,8},{11,9},{8,1... | collective-permute-start | bytes 122888 | tf_op jit(solution)/shard_map/ppermute | solution.py:333
  7.4 7.2 %collective-permute-start.4 = (bf16[8,2560]{1,0:T(8,128)(2,1)S(1)}, bf16[8,2560]{1,0:T(8,128)(2,1)S(1)}, u32[]{:S(2)}, u32[]{:S(2)}) collective-permute-start(bf16[8,2560]{1,0:T(8,128)(2,1)S(1)} %collective-permute-done.1.refs_1_), channel_id=1, source_target_pairs={{2,0},{3,1},{0,2},{1,3},{6,4},{7,5},{4,6},{5,7},{10,8},{11,9},{8,1... | collective-permute-start | bytes 122888 | tf_op jit(solution)/shard_map/ppermute | solution.py:333
  9.3 5.3 %collective-permute-start.6 = (bf16[8,2560]{1,0:T(8,128)(2,1)S(1)}, bf16[8,2560]{1,0:T(8,128)(2,1)S(1)}, u32[]{:S(2)}, u32[]{:S(2)}) collective-permute-start(bf16[8,2560]{1,0:T(8,128)(2,1)S(1)} %collective-permute-done.refs_6_.refs_3_), channel_id=1, source_target_pairs={{2,0},{3,1},{0,2},{1,3},{6,4},{7,5},{4,6},{5,7},{10,8},{11,9},{8,1... | collective-permute-start | bytes 122888 | tf_op jit(solution)/shard_map/ppermute | solution.py:333
  10.8 4.0 %collective-permute-start.5 = (bf16[8,2560]{1,0:T(8,128)(2,1)S(1)}, bf16[8,2560]{1,0:T(8,128)(2,1)S(1)}, u32[]{:S(2)}, u32[]{:S(2)}) collective-permute-start(bf16[8,2560]{1,0:T(8,128)(2,1)S(1)} %collective-permute-done.2.refs_2_), channel_id=1, source_target_pairs={{2,0},{3,1},{0,2},{1,3},{6,4},{7,5},{4,6},{5,7},{10,8},{11,9},{8,1... | collective-permute-start | bytes 122888 | tf_op jit(solution)/shard_map/ppermute | solution.py:333
  14.8 1.7 %collective-permute-start.7 = (bf16[64,2560]{1,0:T(8,128)(2,1)S(1)}, bf16[64,2560]{1,0:T(8,128)(2,1)S(1)}, u32[]{:S(2)}, u32[]{:S(2)}) collective-permute-start(bf16[64,2560]{1,0:T(8,128)(2,1)S(1)} %merge.7.refs_1_), channel_id=1, source_target_pairs={{1,0},{0,1},{3,2},{2,3},{5,4},{4,5},{7,6},{6,7},{9,8},{8,9},{11,10... | collective-permute-start | bytes 983048 | tf_op jit(solution)/shard_map/ppermute | solution.py:333
  18.0 1.5 %collective-permute-start.9 = (bf16[32,2688]{1,0:T(8,128)(2,1)S(1)}, bf16[32,2688]{1,0:T(8,128)(2,1)S(1)}, u32[]{:S(2)}, u32[]{:S(2)}) collective-permute-start(bf16[32,2688]{1,0:T(8,128)(2,1)S(1)} %get-tuple-element.29), channel_id=1, source_target_pairs={{0,1},{1,0},{2,3},{3,2},{4,5},{5,4},{6,7},{7,6},{8,9},{9,8},{10,11... | collective-permute-start | bytes 516104 | tf_op jit(solution)/shard_map/ppermute | solution.py:336
  18.5 5.5 %collective-permute-start.8 = (bf16[32,2688]{1,0:T(8,128)(2,1)S(1)}, bf16[32,2688]{1,0:T(8,128)(2,1)S(1)}, u32[]{:S(2)}, u32[]{:S(2)}) collective-permute-start(bf16[32,2688]{1,0:T(8,128)(2,1)S(1)} %get-tuple-element.26), channel_id=1, source_target_pairs={{0,1},{1,0},{2,3},{3,2},{4,5},{5,4},{6,7},{7,6},{8,9},{9,8},{10,11... | collective-permute-start | bytes 516104 | tf_op jit(solution)/shard_map/ppermute | solution.py:336
  19.8 4.4 %collective-permute-start.11 = (bf16[8,2688]{1,0:T(8,128)(2,1)S(1)}, bf16[8,2688]{1,0:T(8,128)(2,1)S(1)}, u32[]{:S(2)}, u32[]{:S(2)}) collective-permute-start(bf16[8,2688]{1,0:T(8,128)(2,1)S(1)} %get-tuple-element.32), channel_id=1, source_target_pairs={{0,2},{1,3},{2,0},{3,1},{4,6},{5,7},{6,4},{7,5},{8,10},{9,11},{10,... | collective-permute-start | bytes 129032 | tf_op jit(solution)/shard_map/ppermute | solution.py:336
  21.0 6.2 %collective-permute-start.13 = (bf16[8,2688]{1,0:T(8,128)(2,1)S(1)}, bf16[8,2688]{1,0:T(8,128)(2,1)S(1)}, u32[]{:S(2)}, u32[]{:S(2)}) collective-permute-start(bf16[8,2688]{1,0:T(8,128)(2,1)S(1)} %get-tuple-element.34), channel_id=1, source_target_pairs={{0,2},{1,3},{2,0},{3,1},{4,6},{5,7},{6,4},{7,5},{8,10},{9,11},{10,... | collective-permute-start | bytes 129032 | tf_op jit(solution)/shard_map/ppermute | solution.py:336
  21.9 5.9 %collective-permute-start.15 = (bf16[8,2688]{1,0:T(8,128)(2,1)S(1)}, bf16[8,2688]{1,0:T(8,128)(2,1)S(1)}, u32[]{:S(2)}, u32[]{:S(2)}) collective-permute-start(bf16[8,2688]{1,0:T(8,128)(2,1)S(1)} %get-tuple-element.36), channel_id=1, source_target_pairs={{0,2},{1,3},{2,0},{3,1},{4,6},{5,7},{6,4},{7,5},{8,10},{9,11},{10,... | collective-permute-start | bytes 129032 | tf_op jit(solution)/shard_map/ppermute | solution.py:336
  23.0 6.3 %collective-permute-start.10 = (bf16[8,2688]{1,0:T(8,128)(2,1)S(1)}, bf16[8,2688]{1,0:T(8,128)(2,1)S(1)}, u32[]{:S(2)}, u32[]{:S(2)}) collective-permute-start(bf16[8,2688]{1,0:T(8,128)(2,1)S(1)} %get-tuple-element.30), channel_id=1, source_target_pairs={{0,2},{1,3},{2,0},{3,1},{4,6},{5,7},{6,4},{7,5},{8,10},{9,11},{10,... | collective-permute-start | bytes 129032 | tf_op jit(solution)/shard_map/ppermute | solution.py:336
  24.4 5.9 %collective-permute-start.12 = (bf16[8,2688]{1,0:T(8,128)(2,1)S(1)}, bf16[8,2688]{1,0:T(8,128)(2,1)S(1)}, u32[]{:S(2)}, u32[]{:S(2)}) collective-permute-start(bf16[8,2688]{1,0:T(8,128)(2,1)S(1)} %merge.11), channel_id=1, source_target_pairs={{0,12},{1,13},{2,14},{3,15},{4,8},{5,9},{6,10},{7,11},{8,4},{9,5},... | collective-permute-start | bytes 129032 | tf_op jit(solution)/shard_map/ppermute | solution.py:336
  27.3 5.1 %collective-permute-start.14 = (bf16[8,2688]{1,0:T(8,128)(2,1)S(1)}, bf16[8,2688]{1,0:T(8,128)(2,1)S(1)}, u32[]{:S(2)}, u32[]{:S(2)}) collective-permute-start(bf16[8,2688]{1,0:T(8,128)(2,1)S(1)} %merge.12), channel_id=1, source_target_pairs={{0,8},{1,9},{2,10},{3,11},{4,12},{5,13},{6,14},{7,15},{8,0},{9,1},... | collective-permute-start | bytes 129032 | tf_op jit(solution)/shard_map/ppermute | solution.py:336
  27.9 4.6 %collective-permute-start.16 = (bf16[8,2688]{1,0:T(8,128)(2,1)S(1)}, bf16[8,2688]{1,0:T(8,128)(2,1)S(1)}, u32[]{:S(2)}, u32[]{:S(2)}) collective-permute-start(bf16[8,2688]{1,0:T(8,128)(2,1)S(1)} %merge.13), channel_id=1, source_target_pairs={{0,4},{1,5},{2,6},{3,7},{4,0},{5,1},{6,2},{7,3},{8,12},{9,13},{10,... | collective-permute-start | bytes 129032 | tf_op jit(solution)/shard_map/ppermute | solution.py:336

commit v25 on v22

--- a/solution.py
+++ b/solution.py
@@ -109,15 +109,15 @@
                         o_ref[at, cols] = one.astype(o_ref.dtype)
 
             score, top, weights = {}, {}, {}
-            for t in range(-3, group + 1):
-                if 0 <= t + 3 < group:
-                    score[t + 3] = scores(t + 3)
-                if 0 <= t + 1 < group:
-                    score[t + 1], top[t + 1] = masked(score[t + 1])
+            for t in range(-6, group + 3):
+                if 0 <= t + 6 < group:
+                    score[t + 6] = scores(t + 6)
+                if 0 <= t + 2 < group:
+                    score[t + 2], top[t + 2] = masked(score[t + 2])
                 if 0 <= t < group:
                     weights[t] = weigh(t, score.pop(t), top.pop(t))
-                if 0 <= t - 1:
-                    gather_values(t - 1, weights.pop(t - 1))
+                if 0 <= t - 3:
+                    gather_values(t - 3, weights.pop(t - 3))
             return carry
 
         lax.fori_loop(0, steps, heads_of, 0)

time: 33.8 us -> 33.5 us (level)
  transfers between devices with their start and end apart: 17 -> 17, of which waited for: 5 -> 6; matrix products, arithmetic and copies ran while one was open for 0% -> 0% of each run, Pallas kernels for 16% -> 16%
where the time goes in v25:
time: 33.5 us; the launch traced here: 33.4 us
  starting transfers between devices  21 us (63%)
  Pallas kernels  7.72 us (23%)
  waiting for transfers between devices  4.6 us (14%)
    ppermute x8, starting transfers between devices, fetch(): return lax.ppermute(x, 'seq', partner_perm(shape, by, False))  11.7 us
    ppermute x9, starting transfers between devices, give(): return lax.ppermute(x, 'seq', partner_perm(shape, by, True))  9.29 us
    ppermute x9, waiting for transfers between devices, give(): return lax.ppermute(x, 'seq', partner_perm(shape, by, True))  3.98 us
    pallas_call x2, Pallas kernels, attend(): pl.pallas_call(body, in_specs=[pl.BlockSpec(memory_space=pltpu.VMEM)] * 4...  3.01 us
    pallas_call x1, Pallas kernels, load(): pl.pallas_call(body, in_specs=[in_hbm] * len(held) + [pl.BlockSpec(memory...  2.65 us
    pallas_call x8, Pallas kernels, call_merge(): pl.pallas_call(body, in_specs=[pl.BlockSpec(memory_space=pltpu.VMEM)] * l...  2.06 us
  transfers between devices with their start and end apart: 17, of which 6 were waited for; matrix products, arithmetic and copies ran while one was open for 0% of the time, Pallas kernels for 16%

profile of v25, /device:TPU:0, one launch (start us, length us, event | category | flops | bytes accessed | tf_op | source)
XLA Modules:
  0.0 33.4 jit_solution(9134110466153837019)
XLA Ops:
  0.0 5.0 %collective-permute-start.1 = (bf16[8,2560]{1,0:T(8,128)(2,1)}, bf16[8,2560]{1,0:T(8,128)(2,1)S(1)}, u32[]{:S(2)}, u32[]{:S(2)}) collective-permute-start(bf16[8,2560]{1,0:T(8,128)(2,1)} %refs_5_.1), channel_id=1, source_target_pairs={{12,0},{13,1},{14,2},{15,3},{8,4},{9,5},{10,6},{11,7},{4,8},{5,9},... | collective-permute-start | bytes 122888 | tf_op jit(solution)/shard_map/ppermute | solution.py:310
  5.1 0.6 %collective-permute-start.2 = (bf16[8,2560]{1,0:T(8,128)(2,1)}, bf16[8,2560]{1,0:T(8,128)(2,1)S(1)}, u32[]{:S(2)}, u32[]{:S(2)}) collective-permute-start(bf16[8,2560]{1,0:T(8,128)(2,1)} %refs_5_.1), channel_id=1, source_target_pairs={{8,0},{9,1},{10,2},{11,3},{12,4},{13,5},{14,6},{15,7},{0,8},{1,9},... | collective-permute-start | bytes 122888 | tf_op jit(solution)/shard_map/ppermute | solution.py:310
  5.6 1.8 %collective-permute-start.3 = (bf16[8,2560]{1,0:T(8,128)(2,1)}, bf16[8,2560]{1,0:T(8,128)(2,1)S(1)}, u32[]{:S(2)}, u32[]{:S(2)}) collective-permute-start(bf16[8,2560]{1,0:T(8,128)(2,1)} %refs_5_.1), channel_id=1, source_target_pairs={{2,0},{3,1},{0,2},{1,3},{6,4},{7,5},{4,6},{5,7},{10,8},{11,9},{8,1... | collective-permute-start | bytes 122888 | tf_op jit(solution)/shard_map/ppermute | solution.py:310
  7.4 1.6 %collective-permute-start.4 = (bf16[8,2560]{1,0:T(8,128)(2,1)S(1)}, bf16[8,2560]{1,0:T(8,128)(2,1)S(1)}, u32[]{:S(2)}, u32[]{:S(2)}) collective-permute-start(bf16[8,2560]{1,0:T(8,128)(2,1)S(1)} %collective-permute-done.1.refs_1_), channel_id=1, source_target_pairs={{2,0},{3,1},{0,2},{1,3},{6,4},{7,5},{4,6},{5,7},{10,8},{11,9},{8,1... | collective-permute-start | bytes 122888 | tf_op jit(solution)/shard_map/ppermute | solution.py:310
  9.0 0.3 collective-permute-done.refs_6_.refs_3_
  9.3 1.5 %collective-permute-start.6 = (bf16[8,2560]{1,0:T(8,128)(2,1)S(1)}, bf16[8,2560]{1,0:T(8,128)(2,1)S(1)}, u32[]{:S(2)}, u32[]{:S(2)}) collective-permute-start(bf16[8,2560]{1,0:T(8,128)(2,1)S(1)} %collective-permute-done.refs_6_.refs_3_), channel_id=1, source_target_pairs={{2,0},{3,1},{0,2},{1,3},{6,4},{7,5},{4,6},{5,7},{10,8},{11,9},{8,1... | collective-permute-start | bytes 122888 | tf_op jit(solution)/shard_map/ppermute | solution.py:310
  10.8 1.1 %collective-permute-start.5 = (bf16[8,2560]{1,0:T(8,128)(2,1)S(1)}, bf16[8,2560]{1,0:T(8,128)(2,1)S(1)}, u32[]{:S(2)}, u32[]{:S(2)}) collective-permute-start(bf16[8,2560]{1,0:T(8,128)(2,1)S(1)} %collective-permute-done.2.refs_2_), channel_id=1, source_target_pairs={{2,0},{3,1},{0,2},{1,3},{6,4},{7,5},{4,6},{5,7},{10,8},{11,9},{8,1... | collective-permute-start | bytes 122888 | tf_op jit(solution)/shard_map/ppermute | solution.py:310
  11.9 2.6 %load.1 = (bf16[528,2560]{1,0:T(8,128)(2,1)S(1)}, bf16[528,2560]{1,0:T(8,128)(2,1)S(1)}, f32[528,128]{1,0:T(8,128)S(1)}, bf16[8,2560]{1,0:T(8,128)(2,1)S(1)}) custom-call(bf16[512,2560]{1,0:T(8,128)(2,1)} %refs_0_.1, bf16[512,2560]{1,0:T(8,128)(2,1)} %refs_1_.1, bf16[8,2560]{1,0:T(8,128)(2,1)} %refs_2_.1, bf16[8,2560]{1,0:T(8,128)(2,1)} %refs_3_.1, ...), custom_call_target="tpu_custom_call" | custom-call | bytes 10485760 | tf_op jit(solution)/shard_map/load/pallas_call | solution.py:214
  14.6 0.2 collective-permute-done.5.refs_6_
  14.8 0.1 collective-permute-start.7
  14.9 1.5 %attend.2 = (f32[32,2688]{1,0:T(8,128)S(1)}, f32[32,2688]{1,0:T(8,128)S(1)}) custom-call(f32[528,128]{1,0:T(8,128)S(1)} %get-tuple-element.21.refs_0_, bf16[64,2560]{1,0:T(8,128)(2,1)S(1)} %merge.8.refs_1_, bf16[528,2560]{1,0:T(8,128)(2,1)S(1)} %get-tuple-element.23.refs_2_, bf16[528,2560]{1,0:T(8,128)(2,1)S(1)} %get-tuple-element.24.refs_3_), custom_call_target="tpu_custom_call" | custom-call | flops 346030080 | bytes 5406720 | tf_op jit(solution)/shard_map/attend/pallas_call | solution.py:153
  16.4 0.1 collective-permute-done.7.refs_1_
  16.5 1.5 %attend.3 = (bf16[32,2688]{1,0:T(8,128)(2,1)S(1)}, bf16[32,2688]{1,0:T(8,128)(2,1)S(1)}) custom-call(f32[528,128]{1,0:T(8,128)S(1)} %get-tuple-element.21.refs_0_, bf16[64,2560]{1,0:T(8,128)(2,1)S(1)} %collective-permute-done.7.refs_1_, bf16[528,2560]{1,0:T(8,128)(2,1)S(1)} %get-tuple-element.23.refs_2_, bf16[528,2560]{1,0:T(8,128)(2,1)S(1)} %get-tuple-element.24.refs_3_, ...), custom_call_target="tpu_custom_call" | custom-call | flops 346030080 | bytes 5406720 | tf_op jit(solution)/shard_map/attend/pallas_call | solution.py:153
  18.0 0.5 %collective-permute-start.9 = (bf16[32,2688]{1,0:T(8,128)(2,1)S(1)}, bf16[32,2688]{1,0:T(8,128)(2,1)S(1)}, u32[]{:S(2)}, u32[]{:S(2)}) collective-permute-start(bf16[32,2688]{1,0:T(8,128)(2,1)S(1)} %get-tuple-element.29), channel_id=1, source_target_pairs={{0,1},{1,0},{2,3},{3,2},{4,5},{5,4},{6,7},{7,6},{8,9},{9,8},{10,11... | collective-permute-start | bytes 516104 | tf_op jit(solution)/shard_map/ppermute | solution.py:313
  18.5 0.1 collective-permute-start.8
  18.6 0.9 %collective-permute-done.9.refs_1_ = bf16[32,2688]{1,0:T(8,128)(2,1)S(1)} collective-permute-done((bf16[32,2688]{1,0:T(8,128)(2,1)S(1)}, bf16[32,2688]{1,0:T(8,128)(2,1)S(1)}, u32[]{:S(2)}, u32[]{:S(2)}) %collective-permute-start.9) | collective-permute-done | bytes 172064 | tf_op jit(solution)/shard_map/ppermute | solution.py:313
  19.5 0.3 merge.10
  19.8 1.2 %collective-permute-start.11 = (bf16[8,2688]{1,0:T(8,128)(2,1)S(1)}, bf16[8,2688]{1,0:T(8,128)(2,1)S(1)}, u32[]{:S(2)}, u32[]{:S(2)}) collective-permute-start(bf16[8,2688]{1,0:T(8,128)(2,1)S(1)} %get-tuple-element.32), channel_id=1, source_target_pairs={{0,2},{1,3},{2,0},{3,1},{4,6},{5,7},{6,4},{7,5},{8,10},{9,11},{10,... | collective-permute-start | bytes 129032 | tf_op jit(solution)/shard_map/ppermute | solution.py:313
  21.0 0.9 %collective-permute-start.13 = (bf16[8,2688]{1,0:T(8,128)(2,1)S(1)}, bf16[8,2688]{1,0:T(8,128)(2,1)S(1)}, u32[]{:S(2)}, u32[]{:S(2)}) collective-permute-start(bf16[8,2688]{1,0:T(8,128)(2,1)S(1)} %get-tuple-element.34), channel_id=1, source_target_pairs={{0,2},{1,3},{2,0},{3,1},{4,6},{5,7},{6,4},{7,5},{8,10},{9,11},{10,... | collective-permute-start | bytes 129032 | tf_op jit(solution)/shard_map/ppermute | solution.py:313
  21.9 1.1 %collective-permute-start.15 = (bf16[8,2688]{1,0:T(8,128)(2,1)S(1)}, bf16[8,2688]{1,0:T(8,128)(2,1)S(1)}, u32[]{:S(2)}, u32[]{:S(2)}) collective-permute-start(bf16[8,2688]{1,0:T(8,128)(2,1)S(1)} %get-tuple-element.36), channel_id=1, source_target_pairs={{0,2},{1,3},{2,0},{3,1},{4,6},{5,7},{6,4},{7,5},{8,10},{9,11},{10,... | collective-permute-start | bytes 129032 | tf_op jit(solution)/shard_map/ppermute | solution.py:313
  23.0 0.9 %collective-permute-start.10 = (bf16[8,2688]{1,0:T(8,128)(2,1)S(1)}, bf16[8,2688]{1,0:T(8,128)(2,1)S(1)}, u32[]{:S(2)}, u32[]{:S(2)}) collective-permute-start(bf16[8,2688]{1,0:T(8,128)(2,1)S(1)} %get-tuple-element.30), channel_id=1, source_target_pairs={{0,2},{1,3},{2,0},{3,1},{4,6},{5,7},{6,4},{7,5},{8,10},{9,11},{10,... | collective-permute-start | bytes 129032 | tf_op jit(solution)/shard_map/ppermute | solution.py:313
  24.0 0.3 merge.9
  24.3 0.1 merge.12
  24.4 2.8 %collective-permute-start.12 = (bf16[8,2688]{1,0:T(8,128)(2,1)S(1)}, bf16[8,2688]{1,0:T(8,128)(2,1)S(1)}, u32[]{:S(2)}, u32[]{:S(2)}) collective-permute-start(bf16[8,2688]{1,0:T(8,128)(2,1)S(1)} %merge.12), channel_id=1, source_target_pairs={{0,12},{1,13},{2,14},{3,15},{4,8},{5,9},{6,10},{7,11},{8,4},{9,5},... | collective-permute-start | bytes 129032 | tf_op jit(solution)/shard_map/ppermute | solution.py:313
  27.2 0.1 merge.13
  27.3 0.4 %collective-permute-start.14 = (bf16[8,2688]{1,0:T(8,128)(2,1)S(1)}, bf16[8,2688]{1,0:T(8,128)(2,1)S(1)}, u32[]{:S(2)}, u32[]{:S(2)}) collective-permute-start(bf16[8,2688]{1,0:T(8,128)(2,1)S(1)} %merge.13), channel_id=1, source_target_pairs={{0,8},{1,9},{2,10},{3,11},{4,12},{5,13},{6,14},{7,15},{8,0},{9,1},... | collective-permute-start | bytes 129032 | tf_op jit(solution)/shard_map/ppermute | solution.py:313
  27.8 0.1 merge.14
  27.9 1.4 %collective-permute-start.16 = (bf16[8,2688]{1,0:T(8,128)(2,1)S(1)}, bf16[8,2688]{1,0:T(8,128)(2,1)S(1)}, u32[]{:S(2)}, u32[]{:S(2)}) collective-permute-start(bf16[8,2688]{1,0:T(8,128)(2,1)S(1)} %merge.14), channel_id=1, source_target_pairs={{0,4},{1,5},{2,6},{3,7},{4,0},{5,1},{6,2},{7,3},{8,12},{9,13},{10,... | collective-permute-start | bytes 129032 | tf_op jit(solution)/shard_map/ppermute | solution.py:313
  29.3 0.1 merge.11.refs_0_
  29.4 0.8 %collective-permute-done.12.refs_1_ = bf16[8,2688]{1,0:T(8,128)(2,1)S(1)} collective-permute-done((bf16[8,2688]{1,0:T(8,128)(2,1)S(1)}, bf16[8,2688]{1,0:T(8,128)(2,1)S(1)}, u32[]{:S(2)}, u32[]{:S(2)}) %collective-permute-start.12) | collective-permute-done | bytes 43040 | tf_op jit(solution)/shard_map/ppermute | solution.py:313
  30.3 2.1 %collective-permute-done.14.refs_2_ = bf16[8,2688]{1,0:T(8,128)(2,1)S(1)} collective-permute-done((bf16[8,2688]{1,0:T(8,128)(2,1)S(1)}, bf16[8,2688]{1,0:T(8,128)(2,1)S(1)}, u32[]{:S(2)}, u32[]{:S(2)}) %collective-permute-start.14) | collective-permute-done | bytes 43040 | tf_op jit(solution)/shard_map/ppermute | solution.py:313
  32.5 0.9 %merge.15 = bf16[8,2560]{1,0:T(8,128)(2,1)} custom-call(f32[8,2688]{1,0:T(8,128)S(1)} %merge.11.refs_0_, bf16[8,2688]{1,0:T(8,128)(2,1)S(1)} %collective-permute-done.12.refs_1_, bf16[8,2688]{1,0:T(8,128)(2,1)S(1)} %collective-permute-done.14.refs_2_, bf16[8,2688]{1,0:T(8,128)(2,1)S(1)} %collective-permute-done.16.refs_3_), custom_call_target="tpu_custom_call" | custom-call | flops 344064 | bytes 344064 | tf_op jit(solution)/shard_map/merge/pallas_call | solution.py:290
  (13 shorter events, 0.1 us)
Async XLA Ops:
  0.0 7.4 %collective-permute-start.1 = (bf16[8,2560]{1,0:T(8,128)(2,1)}, bf16[8,2560]{1,0:T(8,128)(2,1)S(1)}, u32[]{:S(2)}, u32[]{:S(2)}) collective-permute-start(bf16[8,2560]{1,0:T(8,128)(2,1)} %refs_5_.1), channel_id=1, source_target_pairs={{12,0},{13,1},{14,2},{15,3},{8,4},{9,5},{10,6},{11,7},{4,8},{5,9},... | collective-permute-start | bytes 122888 | tf_op jit(solution)/shard_map/ppermute | solution.py:310
  5.0 4.2 %collective-permute-start = (bf16[8,2560]{1,0:T(8,128)(2,1)}, bf16[8,2560]{1,0:T(8,128)(2,1)S(1)}, u32[]{:S(2)}, u32[]{:S(2)}) collective-permute-start(bf16[8,2560]{1,0:T(8,128)(2,1)} %refs_5_.1), channel_id=1, source_target_pairs={{4,0},{5,1},{6,2},{7,3},{0,4},{1,5},{2,6},{3,7},{12,8},{13,9},{14,... | collective-permute-start | bytes 122888 | tf_op jit(solution)/shard_map/ppermute | solution.py:310
  5.1 5.7 %collective-permute-start.2 = (bf16[8,2560]{1,0:T(8,128)(2,1)}, bf16[8,2560]{1,0:T(8,128)(2,1)S(1)}, u32[]{:S(2)}, u32[]{:S(2)}) collective-permute-start(bf16[8,2560]{1,0:T(8,128)(2,1)} %refs_5_.1), channel_id=1, source_target_pairs={{8,0},{9,1},{10,2},{11,3},{12,4},{13,5},{14,6},{15,7},{0,8},{1,9},... | collective-permute-start | bytes 122888 | tf_op jit(solution)/shard_map/ppermute | solution.py:310
  5.6 8.9 %collective-permute-start.3 = (bf16[8,2560]{1,0:T(8,128)(2,1)}, bf16[8,2560]{1,0:T(8,128)(2,1)S(1)}, u32[]{:S(2)}, u32[]{:S(2)}) collective-permute-start(bf16[8,2560]{1,0:T(8,128)(2,1)} %refs_5_.1), channel_id=1, source_target_pairs={{2,0},{3,1},{0,2},{1,3},{6,4},{7,5},{4,6},{5,7},{10,8},{11,9},{8,1... | collective-permute-start | bytes 122888 | tf_op jit(solution)/shard_map/ppermute | solution.py:310
  7.4 7.2 %collective-permute-start.4 = (bf16[8,2560]{1,0:T(8,128)(2,1)S(1)}, bf16[8,2560]{1,0:T(8,128)(2,1)S(1)}, u32[]{:S(2)}, u32[]{:S(2)}) collective-permute-start(bf16[8,2560]{1,0:T(8,128)(2,1)S(1)} %collective-permute-done.1.refs_1_), channel_id=1, source_target_pairs={{2,0},{3,1},{0,2},{1,3},{6,4},{7,5},{4,6},{5,7},{10,8},{11,9},{8,1... | collective-permute-start | bytes 122888 | tf_op jit(solution)/shard_map/ppermute | solution.py:310
  9.3 5.3 %collective-permute-start.6 = (bf16[8,2560]{1,0:T(8,128)(2,1)S(1)}, bf16[8,2560]{1,0:T(8,128)(2,1)S(1)}, u32[]{:S(2)}, u32[]{:S(2)}) collective-permute-start(bf16[8,2560]{1,0:T(8,128)(2,1)S(1)} %collective-permute-done.refs_6_.refs_3_), channel_id=1, source_target_pairs={{2,0},{3,1},{0,2},{1,3},{6,4},{7,5},{4,6},{5,7},{10,8},{11,9},{8,1... | collective-permute-start | bytes 122888 | tf_op jit(solution)/shard_map/ppermute | solution.py:310
  10.8 4.0 %collective-permute-start.5 = (bf16[8,2560]{1,0:T(8,128)(2,1)S(1)}, bf16[8,2560]{1,0:T(8,128)(2,1)S(1)}, u32[]{:S(2)}, u32[]{:S(2)}) collective-permute-start(bf16[8,2560]{1,0:T(8,128)(2,1)S(1)} %collective-permute-done.2.refs_2_), channel_id=1, source_target_pairs={{2,0},{3,1},{0,2},{1,3},{6,4},{7,5},{4,6},{5,7},{10,8},{11,9},{8,1... | collective-permute-start | bytes 122888 | tf_op jit(solution)/shard_map/ppermute | solution.py:310
  14.8 1.7 %collective-permute-start.7 = (bf16[64,2560]{1,0:T(8,128)(2,1)S(1)}, bf16[64,2560]{1,0:T(8,128)(2,1)S(1)}, u32[]{:S(2)}, u32[]{:S(2)}) collective-permute-start(bf16[64,2560]{1,0:T(8,128)(2,1)S(1)} %merge.8.refs_1_), channel_id=1, source_target_pairs={{1,0},{0,1},{3,2},{2,3},{5,4},{4,5},{7,6},{6,7},{9,8},{8,9},{11,10... | collective-permute-start | bytes 983048 | tf_op jit(solution)/shard_map/ppermute | solution.py:310
  18.0 1.5 %collective-permute-start.9 = (bf16[32,2688]{1,0:T(8,128)(2,1)S(1)}, bf16[32,2688]{1,0:T(8,128)(2,1)S(1)}, u32[]{:S(2)}, u32[]{:S(2)}) collective-permute-start(bf16[32,2688]{1,0:T(8,128)(2,1)S(1)} %get-tuple-element.29), channel_id=1, source_target_pairs={{0,1},{1,0},{2,3},{3,2},{4,5},{5,4},{6,7},{7,6},{8,9},{9,8},{10,11... | collective-permute-start | bytes 516104 | tf_op jit(solution)/shard_map/ppermute | solution.py:313
  18.5 5.5 %collective-permute-start.8 = (bf16[32,2688]{1,0:T(8,128)(2,1)S(1)}, bf16[32,2688]{1,0:T(8,128)(2,1)S(1)}, u32[]{:S(2)}, u32[]{:S(2)}) collective-permute-start(bf16[32,2688]{1,0:T(8,128)(2,1)S(1)} %get-tuple-element.26), channel_id=1, source_target_pairs={{0,1},{1,0},{2,3},{3,2},{4,5},{5,4},{6,7},{7,6},{8,9},{9,8},{10,11... | collective-permute-start | bytes 516104 | tf_op jit(solution)/shard_map/ppermute | solution.py:313
  19.8 4.4 %collective-permute-start.11 = (bf16[8,2688]{1,0:T(8,128)(2,1)S(1)}, bf16[8,2688]{1,0:T(8,128)(2,1)S(1)}, u32[]{:S(2)}, u32[]{:S(2)}) collective-permute-start(bf16[8,2688]{1,0:T(8,128)(2,1)S(1)} %get-tuple-element.32), channel_id=1, source_target_pairs={{0,2},{1,3},{2,0},{3,1},{4,6},{5,7},{6,4},{7,5},{8,10},{9,11},{10,... | collective-permute-start | bytes 129032 | tf_op jit(solution)/shard_map/ppermute | solution.py:313
  21.0 6.2 %collective-permute-start.13 = (bf16[8,2688]{1,0:T(8,128)(2,1)S(1)}, bf16[8,2688]{1,0:T(8,128)(2,1)S(1)}, u32[]{:S(2)}, u32[]{:S(2)}) collective-permute-start(bf16[8,2688]{1,0:T(8,128)(2,1)S(1)} %get-tuple-element.34), channel_id=1, source_target_pairs={{0,2},{1,3},{2,0},{3,1},{4,6},{5,7},{6,4},{7,5},{8,10},{9,11},{10,... | collective-permute-start | bytes 129032 | tf_op jit(solution)/shard_map/ppermute | solution.py:313
  21.9 5.9 %collective-permute-start.15 = (bf16[8,2688]{1,0:T(8,128)(2,1)S(1)}, bf16[8,2688]{1,0:T(8,128)(2,1)S(1)}, u32[]{:S(2)}, u32[]{:S(2)}) collective-permute-start(bf16[8,2688]{1,0:T(8,128)(2,1)S(1)} %get-tuple-element.36), channel_id=1, source_target_pairs={{0,2},{1,3},{2,0},{3,1},{4,6},{5,7},{6,4},{7,5},{8,10},{9,11},{10,... | collective-permute-start | bytes 129032 | tf_op jit(solution)/shard_map/ppermute | solution.py:313
  23.0 6.3 %collective-permute-start.10 = (bf16[8,2688]{1,0:T(8,128)(2,1)S(1)}, bf16[8,2688]{1,0:T(8,128)(2,1)S(1)}, u32[]{:S(2)}, u32[]{:S(2)}) collective-permute-start(bf16[8,2688]{1,0:T(8,128)(2,1)S(1)} %get-tuple-element.30), channel_id=1, source_target_pairs={{0,2},{1,3},{2,0},{3,1},{4,6},{5,7},{6,4},{7,5},{8,10},{9,11},{10,... | collective-permute-start | bytes 129032 | tf_op jit(solution)/shard_map/ppermute | solution.py:313
  24.4 5.9 %collective-permute-start.12 = (bf16[8,2688]{1,0:T(8,128)(2,1)S(1)}, bf16[8,2688]{1,0:T(8,128)(2,1)S(1)}, u32[]{:S(2)}, u32[]{:S(2)}) collective-permute-start(bf16[8,2688]{1,0:T(8,128)(2,1)S(1)} %merge.12), channel_id=1, source_target_pairs={{0,12},{1,13},{2,14},{3,15},{4,8},{5,9},{6,10},{7,11},{8,4},{9,5},... | collective-permute-start | bytes 129032 | tf_op jit(solution)/shard_map/ppermute | solution.py:313
  27.3 5.1 %collective-permute-start.14 = (bf16[8,2688]{1,0:T(8,128)(2,1)S(1)}, bf16[8,2688]{1,0:T(8,128)(2,1)S(1)}, u32[]{:S(2)}, u32[]{:S(2)}) collective-permute-start(bf16[8,2688]{1,0:T(8,128)(2,1)S(1)} %merge.13), channel_id=1, source_target_pairs={{0,8},{1,9},{2,10},{3,11},{4,12},{5,13},{6,14},{7,15},{8,0},{9,1},... | collective-permute-start | bytes 129032 | tf_op jit(solution)/shard_map/ppermute | solution.py:313
  27.9 4.6 %collective-permute-start.16 = (bf16[8,2688]{1,0:T(8,128)(2,1)S(1)}, bf16[8,2688]{1,0:T(8,128)(2,1)S(1)}, u32[]{:S(2)}, u32[]{:S(2)}) collective-permute-start(bf16[8,2688]{1,0:T(8,128)(2,1)S(1)} %merge.14), channel_id=1, source_target_pairs={{0,4},{1,5},{2,6},{3,7},{4,0},{5,1},{6,2},{7,3},{8,12},{9,13},{10,... | collective-permute-start | bytes 129032 | tf_op jit(solution)/shard_map/ppermute | solution.py:313

commit v26 on v25

--- a/solution.py
+++ b/solution.py
@@ -157,7 +157,9 @@
         out_specs=[pl.BlockSpec(memory_space=pltpu.VMEM)] * lines,
         out_shape=[jax.ShapeDtypeStruct((rows, width), kind)] * lines,
         scratch_shapes=[pltpu.VMEM((STAT, PACK * tile * lines), F32)] * 2,
-        compiler_params=pltpu.CompilerParams(vmem_limit_bytes=40 * 1024 * 1024),
+        compiler_params=pltpu.CompilerParams(
+            vmem_limit_bytes=40 * 1024 * 1024, fuse_transposed_lhs_in_matmul=True
+        ),
         cost_estimate=pl.CostEstimate(
             flops=4 * lines * rows * keys.shape[0] * columns,
             bytes_accessed=4 * keys.shape[0] * columns,

time: 33.5 us -> 34.4 us (1.027)
  Pallas kernels: 7.72 us -> 8.55 us
    pallas_call x2, Pallas kernels: 3.01 us -> 3.84 us  [attend(): pl.pallas_call(body, in_specs=[pl.BlockSpec(memory_space=pltpu.VMEM)] * 4...]
  transfers between devices with their start and end apart: 17 -> 17, of which waited for: 6 -> 6; matrix products, arithmetic and copies ran while one was open for 0% -> 0% of each run, Pallas kernels for 16% -> 17%
where the time goes in v26:
time: 34.4 us; the launch traced here: 34.2 us
  starting transfers between devices  21 us (61%)
  Pallas kernels  8.55 us (25%)
  waiting for transfers between devices  4.53 us (13%)
    ppermute x8, starting transfers between devices, fetch(): return lax.ppermute(x, 'seq', partner_perm(shape, by, False))  11.7 us
    ppermute x9, starting transfers between devices, give(): return lax.ppermute(x, 'seq', partner_perm(shape, by, True))  9.35 us
    ppermute x9, waiting for transfers between devices, give(): return lax.ppermute(x, 'seq', partner_perm(shape, by, True))  4.02 us
    pallas_call x2, Pallas kernels, attend(): pl.pallas_call(body, in_specs=[pl.BlockSpec(memory_space=pltpu.VMEM)] * 4...  3.84 us
    pallas_call x1, Pallas kernels, load(): pl.pallas_call(body, in_specs=[in_hbm] * len(held) + [pl.BlockSpec(memory...  2.65 us
    pallas_call x8, Pallas kernels, call_merge(): pl.pallas_call(body, in_specs=[pl.BlockSpec(memory_space=pltpu.VMEM)] * l...  2.06 us
  transfers between devices with their start and end apart: 17, of which 6 were waited for; matrix products, arithmetic and copies ran while one was open for 0% of the time, Pallas kernels for 17%

profile of v26, /device:TPU:0, one launch (start us, length us, event | category | flops | bytes accessed | tf_op | source)
XLA Modules:
  0.0 34.2 jit_solution(16983565148707192710)
XLA Ops:
  0.0 5.0 %collective-permute-start.1 = (bf16[8,2560]{1,0:T(8,128)(2,1)}, bf16[8,2560]{1,0:T(8,128)(2,1)S(1)}, u32[]{:S(2)}, u32[]{:S(2)}) collective-permute-start(bf16[8,2560]{1,0:T(8,128)(2,1)} %refs_5_.1), channel_id=1, source_target_pairs={{12,0},{13,1},{14,2},{15,3},{8,4},{9,5},{10,6},{11,7},{4,8},{5,9},... | collective-permute-start | bytes 122888 | tf_op jit(solution)/shard_map/ppermute | solution.py:312
  5.1 0.6 %collective-permute-start.2 = (bf16[8,2560]{1,0:T(8,128)(2,1)}, bf16[8,2560]{1,0:T(8,128)(2,1)S(1)}, u32[]{:S(2)}, u32[]{:S(2)}) collective-permute-start(bf16[8,2560]{1,0:T(8,128)(2,1)} %refs_5_.1), channel_id=1, source_target_pairs={{8,0},{9,1},{10,2},{11,3},{12,4},{13,5},{14,6},{15,7},{0,8},{1,9},... | collective-permute-start | bytes 122888 | tf_op jit(solution)/shard_map/ppermute | solution.py:312
  5.6 1.8 %collective-permute-start.3 = (bf16[8,2560]{1,0:T(8,128)(2,1)}, bf16[8,2560]{1,0:T(8,128)(2,1)S(1)}, u32[]{:S(2)}, u32[]{:S(2)}) collective-permute-start(bf16[8,2560]{1,0:T(8,128)(2,1)} %refs_5_.1), channel_id=1, source_target_pairs={{2,0},{3,1},{0,2},{1,3},{6,4},{7,5},{4,6},{5,7},{10,8},{11,9},{8,1... | collective-permute-start | bytes 122888 | tf_op jit(solution)/shard_map/ppermute | solution.py:312
  7.4 1.6 %collective-permute-start.4 = (bf16[8,2560]{1,0:T(8,128)(2,1)S(1)}, bf16[8,2560]{1,0:T(8,128)(2,1)S(1)}, u32[]{:S(2)}, u32[]{:S(2)}) collective-permute-start(bf16[8,2560]{1,0:T(8,128)(2,1)S(1)} %collective-permute-done.1.refs_1_), channel_id=1, source_target_pairs={{2,0},{3,1},{0,2},{1,3},{6,4},{7,5},{4,6},{5,7},{10,8},{11,9},{8,1... | collective-permute-start | bytes 122888 | tf_op jit(solution)/shard_map/ppermute | solution.py:312
  9.0 0.3 collective-permute-done.refs_6_.refs_3_
  9.3 1.5 %collective-permute-start.6 = (bf16[8,2560]{1,0:T(8,128)(2,1)S(1)}, bf16[8,2560]{1,0:T(8,128)(2,1)S(1)}, u32[]{:S(2)}, u32[]{:S(2)}) collective-permute-start(bf16[8,2560]{1,0:T(8,128)(2,1)S(1)} %collective-permute-done.refs_6_.refs_3_), channel_id=1, source_target_pairs={{2,0},{3,1},{0,2},{1,3},{6,4},{7,5},{4,6},{5,7},{10,8},{11,9},{8,1... | collective-permute-start | bytes 122888 | tf_op jit(solution)/shard_map/ppermute | solution.py:312
  10.8 1.1 %collective-permute-start.5 = (bf16[8,2560]{1,0:T(8,128)(2,1)S(1)}, bf16[8,2560]{1,0:T(8,128)(2,1)S(1)}, u32[]{:S(2)}, u32[]{:S(2)}) collective-permute-start(bf16[8,2560]{1,0:T(8,128)(2,1)S(1)} %collective-permute-done.2.refs_2_), channel_id=1, source_target_pairs={{2,0},{3,1},{0,2},{1,3},{6,4},{7,5},{4,6},{5,7},{10,8},{11,9},{8,1... | collective-permute-start | bytes 122888 | tf_op jit(solution)/shard_map/ppermute | solution.py:312
  11.9 2.6 %load.1 = (bf16[528,2560]{1,0:T(8,128)(2,1)S(1)}, bf16[528,2560]{1,0:T(8,128)(2,1)S(1)}, f32[528,128]{1,0:T(8,128)S(1)}, bf16[8,2560]{1,0:T(8,128)(2,1)S(1)}) custom-call(bf16[512,2560]{1,0:T(8,128)(2,1)} %refs_0_.1, bf16[512,2560]{1,0:T(8,128)(2,1)} %refs_1_.1, bf16[8,2560]{1,0:T(8,128)(2,1)} %refs_2_.1, bf16[8,2560]{1,0:T(8,128)(2,1)} %refs_3_.1, ...), custom_call_target="tpu_custom_call" | custom-call | bytes 10485760 | tf_op jit(solution)/shard_map/load/pallas_call | solution.py:216
  14.6 0.2 collective-permute-done.5.refs_6_
  14.8 0.1 collective-permute-start.7
  14.9 1.9 %attend.2 = (f32[32,2688]{1,0:T(8,128)S(1)}, f32[32,2688]{1,0:T(8,128)S(1)}) custom-call(f32[528,128]{1,0:T(8,128)S(1)} %get-tuple-element.21.refs_0_, bf16[64,2560]{1,0:T(8,128)(2,1)S(1)} %merge.8.refs_1_, bf16[528,2560]{1,0:T(8,128)(2,1)S(1)} %get-tuple-element.23.refs_2_, bf16[528,2560]{1,0:T(8,128)(2,1)S(1)} %get-tuple-element.24.refs_3_), custom_call_target="tpu_custom_call" | custom-call | flops 346030080 | bytes 5406720 | tf_op jit(solution)/shard_map/attend/pallas_call | solution.py:153
  16.8 1.9 %attend.3 = (bf16[32,2688]{1,0:T(8,128)(2,1)S(1)}, bf16[32,2688]{1,0:T(8,128)(2,1)S(1)}) custom-call(f32[528,128]{1,0:T(8,128)S(1)} %get-tuple-element.21.refs_0_, bf16[64,2560]{1,0:T(8,128)(2,1)S(1)} %collective-permute-done.7.refs_1_, bf16[528,2560]{1,0:T(8,128)(2,1)S(1)} %get-tuple-element.23.refs_2_, bf16[528,2560]{1,0:T(8,128)(2,1)S(1)} %get-tuple-element.24.refs_3_, ...), custom_call_target="tpu_custom_call" | custom-call | flops 346030080 | bytes 5406720 | tf_op jit(solution)/shard_map/attend/pallas_call | solution.py:153
  18.8 0.6 %collective-permute-start.9 = (bf16[32,2688]{1,0:T(8,128)(2,1)S(1)}, bf16[32,2688]{1,0:T(8,128)(2,1)S(1)}, u32[]{:S(2)}, u32[]{:S(2)}) collective-permute-start(bf16[32,2688]{1,0:T(8,128)(2,1)S(1)} %get-tuple-element.29), channel_id=1, source_target_pairs={{0,1},{1,0},{2,3},{3,2},{4,5},{5,4},{6,7},{7,6},{8,9},{9,8},{10,11... | collective-permute-start | bytes 516104 | tf_op jit(solution)/shard_map/ppermute | solution.py:315
  19.3 0.1 collective-permute-start.8
  19.4 1.0 %collective-permute-done.9.refs_1_ = bf16[32,2688]{1,0:T(8,128)(2,1)S(1)} collective-permute-done((bf16[32,2688]{1,0:T(8,128)(2,1)S(1)}, bf16[32,2688]{1,0:T(8,128)(2,1)S(1)}, u32[]{:S(2)}, u32[]{:S(2)}) %collective-permute-start.9) | collective-permute-done | bytes 172064 | tf_op jit(solution)/shard_map/ppermute | solution.py:315
  20.4 0.3 merge.10
  20.6 1.2 %collective-permute-start.11 = (bf16[8,2688]{1,0:T(8,128)(2,1)S(1)}, bf16[8,2688]{1,0:T(8,128)(2,1)S(1)}, u32[]{:S(2)}, u32[]{:S(2)}) collective-permute-start(bf16[8,2688]{1,0:T(8,128)(2,1)S(1)} %get-tuple-element.32), channel_id=1, source_target_pairs={{0,2},{1,3},{2,0},{3,1},{4,6},{5,7},{6,4},{7,5},{8,10},{9,11},{10,... | collective-permute-start | bytes 129032 | tf_op jit(solution)/shard_map/ppermute | solution.py:315
  21.8 0.9 %collective-permute-start.13 = (bf16[8,2688]{1,0:T(8,128)(2,1)S(1)}, bf16[8,2688]{1,0:T(8,128)(2,1)S(1)}, u32[]{:S(2)}, u32[]{:S(2)}) collective-permute-start(bf16[8,2688]{1,0:T(8,128)(2,1)S(1)} %get-tuple-element.34), channel_id=1, source_target_pairs={{0,2},{1,3},{2,0},{3,1},{4,6},{5,7},{6,4},{7,5},{8,10},{9,11},{10,... | collective-permute-start | bytes 129032 | tf_op jit(solution)/shard_map/ppermute | solution.py:315
  22.8 1.1 %collective-permute-start.15 = (bf16[8,2688]{1,0:T(8,128)(2,1)S(1)}, bf16[8,2688]{1,0:T(8,128)(2,1)S(1)}, u32[]{:S(2)}, u32[]{:S(2)}) collective-permute-start(bf16[8,2688]{1,0:T(8,128)(2,1)S(1)} %get-tuple-element.36), channel_id=1, source_target_pairs={{0,2},{1,3},{2,0},{3,1},{4,6},{5,7},{6,4},{7,5},{8,10},{9,11},{10,... | collective-permute-start | bytes 129032 | tf_op jit(solution)/shard_map/ppermute | solution.py:315
  23.9 0.9 %collective-permute-start.10 = (bf16[8,2688]{1,0:T(8,128)(2,1)S(1)}, bf16[8,2688]{1,0:T(8,128)(2,1)S(1)}, u32[]{:S(2)}, u32[]{:S(2)}) collective-permute-start(bf16[8,2688]{1,0:T(8,128)(2,1)S(1)} %get-tuple-element.30), channel_id=1, source_target_pairs={{0,2},{1,3},{2,0},{3,1},{4,6},{5,7},{6,4},{7,5},{8,10},{9,11},{10,... | collective-permute-start | bytes 129032 | tf_op jit(solution)/shard_map/ppermute | solution.py:315
  24.8 0.3 merge.9
  25.1 0.1 merge.12
  25.2 2.8 %collective-permute-start.12 = (bf16[8,2688]{1,0:T(8,128)(2,1)S(1)}, bf16[8,2688]{1,0:T(8,128)(2,1)S(1)}, u32[]{:S(2)}, u32[]{:S(2)}) collective-permute-start(bf16[8,2688]{1,0:T(8,128)(2,1)S(1)} %merge.12), channel_id=1, source_target_pairs={{0,12},{1,13},{2,14},{3,15},{4,8},{5,9},{6,10},{7,11},{8,4},{9,5},... | collective-permute-start | bytes 129032 | tf_op jit(solution)/shard_map/ppermute | solution.py:315
  28.0 0.1 merge.13
  28.2 0.4 %collective-permute-start.14 = (bf16[8,2688]{1,0:T(8,128)(2,1)S(1)}, bf16[8,2688]{1,0:T(8,128)(2,1)S(1)}, u32[]{:S(2)}, u32[]{:S(2)}) collective-permute-start(bf16[8,2688]{1,0:T(8,128)(2,1)S(1)} %merge.13), channel_id=1, source_target_pairs={{0,8},{1,9},{2,10},{3,11},{4,12},{5,13},{6,14},{7,15},{8,0},{9,1},... | collective-permute-start | bytes 129032 | tf_op jit(solution)/shard_map/ppermute | solution.py:315
  28.6 0.1 merge.14
  28.8 1.4 %collective-permute-start.16 = (bf16[8,2688]{1,0:T(8,128)(2,1)S(1)}, bf16[8,2688]{1,0:T(8,128)(2,1)S(1)}, u32[]{:S(2)}, u32[]{:S(2)}) collective-permute-start(bf16[8,2688]{1,0:T(8,128)(2,1)S(1)} %merge.14), channel_id=1, source_target_pairs={{0,4},{1,5},{2,6},{3,7},{4,0},{5,1},{6,2},{7,3},{8,12},{9,13},{10,... | collective-permute-start | bytes 129032 | tf_op jit(solution)/shard_map/ppermute | solution.py:315
  30.1 0.1 merge.11.refs_0_
  30.3 0.8 %collective-permute-done.12.refs_1_ = bf16[8,2688]{1,0:T(8,128)(2,1)S(1)} collective-permute-done((bf16[8,2688]{1,0:T(8,128)(2,1)S(1)}, bf16[8,2688]{1,0:T(8,128)(2,1)S(1)}, u32[]{:S(2)}, u32[]{:S(2)}) %collective-permute-start.12) | collective-permute-done | bytes 43040 | tf_op jit(solution)/shard_map/ppermute | solution.py:315
  31.1 2.1 %collective-permute-done.14.refs_2_ = bf16[8,2688]{1,0:T(8,128)(2,1)S(1)} collective-permute-done((bf16[8,2688]{1,0:T(8,128)(2,1)S(1)}, bf16[8,2688]{1,0:T(8,128)(2,1)S(1)}, u32[]{:S(2)}, u32[]{:S(2)}) %collective-permute-start.14) | collective-permute-done | bytes 43040 | tf_op jit(solution)/shard_map/ppermute | solution.py:315
  33.3 0.1 collective-permute-done.16.refs_3_
  33.3 0.9 %merge.15 = bf16[8,2560]{1,0:T(8,128)(2,1)} custom-call(f32[8,2688]{1,0:T(8,128)S(1)} %merge.11.refs_0_, bf16[8,2688]{1,0:T(8,128)(2,1)S(1)} %collective-permute-done.12.refs_1_, bf16[8,2688]{1,0:T(8,128)(2,1)S(1)} %collective-permute-done.14.refs_2_, bf16[8,2688]{1,0:T(8,128)(2,1)S(1)} %collective-permute-done.16.refs_3_), custom_call_target="tpu_custom_call" | custom-call | flops 344064 | bytes 344064 | tf_op jit(solution)/shard_map/merge/pallas_call | solution.py:292
  (13 shorter events, 0.1 us)
Async XLA Ops:
  0.0 7.4 %collective-permute-start.1 = (bf16[8,2560]{1,0:T(8,128)(2,1)}, bf16[8,2560]{1,0:T(8,128)(2,1)S(1)}, u32[]{:S(2)}, u32[]{:S(2)}) collective-permute-start(bf16[8,2560]{1,0:T(8,128)(2,1)} %refs_5_.1), channel_id=1, source_target_pairs={{12,0},{13,1},{14,2},{15,3},{8,4},{9,5},{10,6},{11,7},{4,8},{5,9},... | collective-permute-start | bytes 122888 | tf_op jit(solution)/shard_map/ppermute | solution.py:312
  5.0 4.2 %collective-permute-start = (bf16[8,2560]{1,0:T(8,128)(2,1)}, bf16[8,2560]{1,0:T(8,128)(2,1)S(1)}, u32[]{:S(2)}, u32[]{:S(2)}) collective-permute-start(bf16[8,2560]{1,0:T(8,128)(2,1)} %refs_5_.1), channel_id=1, source_target_pairs={{4,0},{5,1},{6,2},{7,3},{0,4},{1,5},{2,6},{3,7},{12,8},{13,9},{14,... | collective-permute-start | bytes 122888 | tf_op jit(solution)/shard_map/ppermute | solution.py:312
  5.1 5.7 %collective-permute-start.2 = (bf16[8,2560]{1,0:T(8,128)(2,1)}, bf16[8,2560]{1,0:T(8,128)(2,1)S(1)}, u32[]{:S(2)}, u32[]{:S(2)}) collective-permute-start(bf16[8,2560]{1,0:T(8,128)(2,1)} %refs_5_.1), channel_id=1, source_target_pairs={{8,0},{9,1},{10,2},{11,3},{12,4},{13,5},{14,6},{15,7},{0,8},{1,9},... | collective-permute-start | bytes 122888 | tf_op jit(solution)/shard_map/ppermute | solution.py:312
  5.6 8.9 %collective-permute-start.3 = (bf16[8,2560]{1,0:T(8,128)(2,1)}, bf16[8,2560]{1,0:T(8,128)(2,1)S(1)}, u32[]{:S(2)}, u32[]{:S(2)}) collective-permute-start(bf16[8,2560]{1,0:T(8,128)(2,1)} %refs_5_.1), channel_id=1, source_target_pairs={{2,0},{3,1},{0,2},{1,3},{6,4},{7,5},{4,6},{5,7},{10,8},{11,9},{8,1... | collective-permute-start | bytes 122888 | tf_op jit(solution)/shard_map/ppermute | solution.py:312
  7.4 7.2 %collective-permute-start.4 = (bf16[8,2560]{1,0:T(8,128)(2,1)S(1)}, bf16[8,2560]{1,0:T(8,128)(2,1)S(1)}, u32[]{:S(2)}, u32[]{:S(2)}) collective-permute-start(bf16[8,2560]{1,0:T(8,128)(2,1)S(1)} %collective-permute-done.1.refs_1_), channel_id=1, source_target_pairs={{2,0},{3,1},{0,2},{1,3},{6,4},{7,5},{4,6},{5,7},{10,8},{11,9},{8,1... | collective-permute-start | bytes 122888 | tf_op jit(solution)/shard_map/ppermute | solution.py:312
  9.3 5.3 %collective-permute-start.6 = (bf16[8,2560]{1,0:T(8,128)(2,1)S(1)}, bf16[8,2560]{1,0:T(8,128)(2,1)S(1)}, u32[]{:S(2)}, u32[]{:S(2)}) collective-permute-start(bf16[8,2560]{1,0:T(8,128)(2,1)S(1)} %collective-permute-done.refs_6_.refs_3_), channel_id=1, source_target_pairs={{2,0},{3,1},{0,2},{1,3},{6,4},{7,5},{4,6},{5,7},{10,8},{11,9},{8,1... | collective-permute-start | bytes 122888 | tf_op jit(solution)/shard_map/ppermute | solution.py:312
  10.8 4.0 %collective-permute-start.5 = (bf16[8,2560]{1,0:T(8,128)(2,1)S(1)}, bf16[8,2560]{1,0:T(8,128)(2,1)S(1)}, u32[]{:S(2)}, u32[]{:S(2)}) collective-permute-start(bf16[8,2560]{1,0:T(8,128)(2,1)S(1)} %collective-permute-done.2.refs_2_), channel_id=1, source_target_pairs={{2,0},{3,1},{0,2},{1,3},{6,4},{7,5},{4,6},{5,7},{10,8},{11,9},{8,1... | collective-permute-start | bytes 122888 | tf_op jit(solution)/shard_map/ppermute | solution.py:312
  14.8 2.0 %collective-permute-start.7 = (bf16[64,2560]{1,0:T(8,128)(2,1)S(1)}, bf16[64,2560]{1,0:T(8,128)(2,1)S(1)}, u32[]{:S(2)}, u32[]{:S(2)}) collective-permute-start(bf16[64,2560]{1,0:T(8,128)(2,1)S(1)} %merge.8.refs_1_), channel_id=1, source_target_pairs={{1,0},{0,1},{3,2},{2,3},{5,4},{4,5},{7,6},{6,7},{9,8},{8,9},{11,10... | collective-permute-start | bytes 983048 | tf_op jit(solution)/shard_map/ppermute | solution.py:312
  18.8 1.6 %collective-permute-start.9 = (bf16[32,2688]{1,0:T(8,128)(2,1)S(1)}, bf16[32,2688]{1,0:T(8,128)(2,1)S(1)}, u32[]{:S(2)}, u32[]{:S(2)}) collective-permute-start(bf16[32,2688]{1,0:T(8,128)(2,1)S(1)} %get-tuple-element.29), channel_id=1, source_target_pairs={{0,1},{1,0},{2,3},{3,2},{4,5},{5,4},{6,7},{7,6},{8,9},{9,8},{10,11... | collective-permute-start | bytes 516104 | tf_op jit(solution)/shard_map/ppermute | solution.py:315
  19.3 5.5 %collective-permute-start.8 = (bf16[32,2688]{1,0:T(8,128)(2,1)S(1)}, bf16[32,2688]{1,0:T(8,128)(2,1)S(1)}, u32[]{:S(2)}, u32[]{:S(2)}) collective-permute-start(bf16[32,2688]{1,0:T(8,128)(2,1)S(1)} %get-tuple-element.26), channel_id=1, source_target_pairs={{0,1},{1,0},{2,3},{3,2},{4,5},{5,4},{6,7},{7,6},{8,9},{9,8},{10,11... | collective-permute-start | bytes 516104 | tf_op jit(solution)/shard_map/ppermute | solution.py:315
  20.6 4.4 %collective-permute-start.11 = (bf16[8,2688]{1,0:T(8,128)(2,1)S(1)}, bf16[8,2688]{1,0:T(8,128)(2,1)S(1)}, u32[]{:S(2)}, u32[]{:S(2)}) collective-permute-start(bf16[8,2688]{1,0:T(8,128)(2,1)S(1)} %get-tuple-element.32), channel_id=1, source_target_pairs={{0,2},{1,3},{2,0},{3,1},{4,6},{5,7},{6,4},{7,5},{8,10},{9,11},{10,... | collective-permute-start | bytes 129032 | tf_op jit(solution)/shard_map/ppermute | solution.py:315
  21.8 6.2 %collective-permute-start.13 = (bf16[8,2688]{1,0:T(8,128)(2,1)S(1)}, bf16[8,2688]{1,0:T(8,128)(2,1)S(1)}, u32[]{:S(2)}, u32[]{:S(2)}) collective-permute-start(bf16[8,2688]{1,0:T(8,128)(2,1)S(1)} %get-tuple-element.34), channel_id=1, source_target_pairs={{0,2},{1,3},{2,0},{3,1},{4,6},{5,7},{6,4},{7,5},{8,10},{9,11},{10,... | collective-permute-start | bytes 129032 | tf_op jit(solution)/shard_map/ppermute | solution.py:315
  22.8 5.9 %collective-permute-start.15 = (bf16[8,2688]{1,0:T(8,128)(2,1)S(1)}, bf16[8,2688]{1,0:T(8,128)(2,1)S(1)}, u32[]{:S(2)}, u32[]{:S(2)}) collective-permute-start(bf16[8,2688]{1,0:T(8,128)(2,1)S(1)} %get-tuple-element.36), channel_id=1, source_target_pairs={{0,2},{1,3},{2,0},{3,1},{4,6},{5,7},{6,4},{7,5},{8,10},{9,11},{10,... | collective-permute-start | bytes 129032 | tf_op jit(solution)/shard_map/ppermute | solution.py:315
  23.9 6.3 %collective-permute-start.10 = (bf16[8,2688]{1,0:T(8,128)(2,1)S(1)}, bf16[8,2688]{1,0:T(8,128)(2,1)S(1)}, u32[]{:S(2)}, u32[]{:S(2)}) collective-permute-start(bf16[8,2688]{1,0:T(8,128)(2,1)S(1)} %get-tuple-element.30), channel_id=1, source_target_pairs={{0,2},{1,3},{2,0},{3,1},{4,6},{5,7},{6,4},{7,5},{8,10},{9,11},{10,... | collective-permute-start | bytes 129032 | tf_op jit(solution)/shard_map/ppermute | solution.py:315
  25.2 5.9 %collective-permute-start.12 = (bf16[8,2688]{1,0:T(8,128)(2,1)S(1)}, bf16[8,2688]{1,0:T(8,128)(2,1)S(1)}, u32[]{:S(2)}, u32[]{:S(2)}) collective-permute-start(bf16[8,2688]{1,0:T(8,128)(2,1)S(1)} %merge.12), channel_id=1, source_target_pairs={{0,12},{1,13},{2,14},{3,15},{4,8},{5,9},{6,10},{7,11},{8,4},{9,5},... | collective-permute-start | bytes 129032 | tf_op jit(solution)/shard_map/ppermute | solution.py:315
  28.2 5.1 %collective-permute-start.14 = (bf16[8,2688]{1,0:T(8,128)(2,1)S(1)}, bf16[8,2688]{1,0:T(8,128)(2,1)S(1)}, u32[]{:S(2)}, u32[]{:S(2)}) collective-permute-start(bf16[8,2688]{1,0:T(8,128)(2,1)S(1)} %merge.13), channel_id=1, source_target_pairs={{0,8},{1,9},{2,10},{3,11},{4,12},{5,13},{6,14},{7,15},{8,0},{9,1},... | collective-permute-start | bytes 129032 | tf_op jit(solution)/shard_map/ppermute | solution.py:315
  28.8 4.6 %collective-permute-start.16 = (bf16[8,2688]{1,0:T(8,128)(2,1)S(1)}, bf16[8,2688]{1,0:T(8,128)(2,1)S(1)}, u32[]{:S(2)}, u32[]{:S(2)}) collective-permute-start(bf16[8,2688]{1,0:T(8,128)(2,1)S(1)} %merge.14), channel_id=1, source_target_pairs={{0,4},{1,5},{2,6},{3,7},{4,0},{5,1},{6,2},{7,3},{8,12},{9,13},{10,... | collective-permute-start | bytes 129032 | tf_op jit(solution)/shard_map/ppermute | solution.py:315

commit v27 on v25

--- a/solution.py
+++ b/solution.py
@@ -262,6 +262,19 @@
     return call_merge(body, ins, [jax.ShapeDtypeStruct((per, width), kind) for kind in kinds])
 
 
+def merge_half(ins, heads, start, pieces, tok):
+    width = ins[0].shape[1]
+    rows = pieces * tok
+
+    def body(*refs):
+        parts = [lambda cols, r=r: r[start : start + rows, cols].astype(F32) for r in refs[: len(ins)]]
+        for cols, total in merged(parts, heads, False):
+            for j, out in enumerate(refs[len(ins) :]):
+                out[:, cols] = total[j * tok : (j + 1) * tok].astype(out.dtype)
+
+    return call_merge(body, ins, [jax.ShapeDtypeStruct((tok, width), BF16)] * pieces)
+
+
 def finish(ins, heads):
     rows = ins[0].shape[0]
 
@@ -326,6 +339,9 @@
 
     def over_cores(b, kind):
         got = [give(sums[c * b_n + b], 0, 0, c) for c in range(1, c_n)]
+        if b and a_n % 2 == 0 and a_n * tok % 32 == 0:
+            halves = [(h * a_n * tok // 2, a_n // 2) for h in range(2)]
+            return [x for at, n in halves for x in merge_half([sums[b]] + got, heads, at, n, tok)]
         return merge_rows([sums[b]] + got, heads, a_n, [kind] * a_n)
 
     got = [[give(x, 0, b, 0) for x in over_cores(b, BF16)] for b in range(1, b_n)]

time: 33.5 us -> 35.2 us (1.051)
  waiting for transfers between devices: 4.6 us -> 6.12 us
    ppermute x9, waiting for transfers between devices: 3.98 us -> 5.5 us  [give(): return lax.ppermute(x, 'seq', partner_perm(shape, by, True))]
    pallas_call x8 -> x9, Pallas kernels: 2.06 us -> 2.16 us  [call_merge(): pl.pallas_call(body, in_specs=[pl.BlockSpec(memory_space=pltpu.VMEM)] * l...]
  transfers between devices with their start and end apart: 17 -> 17, of which waited for: 6 -> 7; matrix products, arithmetic and copies ran while one was open for 0% -> 0% of each run, Pallas kernels for 16% -> 15%
where the time goes in v27:
time: 35.2 us; the launch traced here: 35.1 us
  starting transfers between devices  21 us (60%)
  Pallas kernels  7.82 us (22%)
  waiting for transfers between devices  6.12 us (17%)
    ppermute x8, starting transfers between devices, fetch(): return lax.ppermute(x, 'seq', partner_perm(shape, by, False))  11.7 us
    ppermute x9, starting transfers between devices, give(): return lax.ppermute(x, 'seq', partner_perm(shape, by, True))  9.35 us
    ppermute x9, waiting for transfers between devices, give(): return lax.ppermute(x, 'seq', partner_perm(shape, by, True))  5.5 us
    pallas_call x2, Pallas kernels, attend(): pl.pallas_call(body, in_specs=[pl.BlockSpec(memory_space=pltpu.VMEM)] * 4...  3.01 us
    pallas_call x1, Pallas kernels, load(): pl.pallas_call(body, in_specs=[in_hbm] * len(held) + [pl.BlockSpec(memory...  2.65 us
    pallas_call x9, Pallas kernels, call_merge(): pl.pallas_call(body, in_specs=[pl.BlockSpec(memory_space=pltpu.VMEM)] * l...  2.16 us
  transfers between devices with their start and end apart: 17, of which 7 were waited for; matrix products, arithmetic and copies ran while one was open for 0% of the time, Pallas kernels for 15%

profile of v27, /device:TPU:0, one launch (start us, length us, event | category | flops | bytes accessed | tf_op | source)
XLA Modules:
  0.0 35.1 jit_solution(17423763543244515806)
XLA Ops:
  0.0 5.0 %collective-permute-start.1 = (bf16[8,2560]{1,0:T(8,128)(2,1)}, bf16[8,2560]{1,0:T(8,128)(2,1)S(1)}, u32[]{:S(2)}, u32[]{:S(2)}) collective-permute-start(bf16[8,2560]{1,0:T(8,128)(2,1)} %refs_5_.1), channel_id=1, source_target_pairs={{12,0},{13,1},{14,2},{15,3},{8,4},{9,5},{10,6},{11,7},{4,8},{5,9},... | collective-permute-start | bytes 122888 | tf_op jit(solution)/shard_map/ppermute | solution.py:323
  5.1 0.6 %collective-permute-start.2 = (bf16[8,2560]{1,0:T(8,128)(2,1)}, bf16[8,2560]{1,0:T(8,128)(2,1)S(1)}, u32[]{:S(2)}, u32[]{:S(2)}) collective-permute-start(bf16[8,2560]{1,0:T(8,128)(2,1)} %refs_5_.1), channel_id=1, source_target_pairs={{8,0},{9,1},{10,2},{11,3},{12,4},{13,5},{14,6},{15,7},{0,8},{1,9},... | collective-permute-start | bytes 122888 | tf_op jit(solution)/shard_map/ppermute | solution.py:323
  5.6 1.8 %collective-permute-start.3 = (bf16[8,2560]{1,0:T(8,128)(2,1)}, bf16[8,2560]{1,0:T(8,128)(2,1)S(1)}, u32[]{:S(2)}, u32[]{:S(2)}) collective-permute-start(bf16[8,2560]{1,0:T(8,128)(2,1)} %refs_5_.1), channel_id=1, source_target_pairs={{2,0},{3,1},{0,2},{1,3},{6,4},{7,5},{4,6},{5,7},{10,8},{11,9},{8,1... | collective-permute-start | bytes 122888 | tf_op jit(solution)/shard_map/ppermute | solution.py:323
  7.4 1.6 %collective-permute-start.4 = (bf16[8,2560]{1,0:T(8,128)(2,1)S(1)}, bf16[8,2560]{1,0:T(8,128)(2,1)S(1)}, u32[]{:S(2)}, u32[]{:S(2)}) collective-permute-start(bf16[8,2560]{1,0:T(8,128)(2,1)S(1)} %collective-permute-done.1.refs_1_), channel_id=1, source_target_pairs={{2,0},{3,1},{0,2},{1,3},{6,4},{7,5},{4,6},{5,7},{10,8},{11,9},{8,1... | collective-permute-start | bytes 122888 | tf_op jit(solution)/shard_map/ppermute | solution.py:323
  9.0 0.3 collective-permute-done.refs_6_.refs_3_
  9.3 1.5 %collective-permute-start.6 = (bf16[8,2560]{1,0:T(8,128)(2,1)S(1)}, bf16[8,2560]{1,0:T(8,128)(2,1)S(1)}, u32[]{:S(2)}, u32[]{:S(2)}) collective-permute-start(bf16[8,2560]{1,0:T(8,128)(2,1)S(1)} %collective-permute-done.refs_6_.refs_3_), channel_id=1, source_target_pairs={{2,0},{3,1},{0,2},{1,3},{6,4},{7,5},{4,6},{5,7},{10,8},{11,9},{8,1... | collective-permute-start | bytes 122888 | tf_op jit(solution)/shard_map/ppermute | solution.py:323
  10.8 1.1 %collective-permute-start.5 = (bf16[8,2560]{1,0:T(8,128)(2,1)S(1)}, bf16[8,2560]{1,0:T(8,128)(2,1)S(1)}, u32[]{:S(2)}, u32[]{:S(2)}) collective-permute-start(bf16[8,2560]{1,0:T(8,128)(2,1)S(1)} %collective-permute-done.2.refs_2_), channel_id=1, source_target_pairs={{2,0},{3,1},{0,2},{1,3},{6,4},{7,5},{4,6},{5,7},{10,8},{11,9},{8,1... | collective-permute-start | bytes 122888 | tf_op jit(solution)/shard_map/ppermute | solution.py:323
  11.9 2.6 %load.1 = (bf16[528,2560]{1,0:T(8,128)(2,1)S(1)}, bf16[528,2560]{1,0:T(8,128)(2,1)S(1)}, f32[528,128]{1,0:T(8,128)S(1)}, bf16[8,2560]{1,0:T(8,128)(2,1)S(1)}) custom-call(bf16[512,2560]{1,0:T(8,128)(2,1)} %refs_0_.1, bf16[512,2560]{1,0:T(8,128)(2,1)} %refs_1_.1, bf16[8,2560]{1,0:T(8,128)(2,1)} %refs_2_.1, bf16[8,2560]{1,0:T(8,128)(2,1)} %refs_3_.1, ...), custom_call_target="tpu_custom_call" | custom-call | bytes 10485760 | tf_op jit(solution)/shard_map/load/pallas_call | solution.py:214
  14.6 0.2 collective-permute-done.5.refs_6_
  14.9 1.5 %attend.2 = (f32[32,2688]{1,0:T(8,128)S(1)}, f32[32,2688]{1,0:T(8,128)S(1)}) custom-call(f32[528,128]{1,0:T(8,128)S(1)} %get-tuple-element.21.refs_0_, bf16[64,2560]{1,0:T(8,128)(2,1)S(1)} %merge.9.refs_1_, bf16[528,2560]{1,0:T(8,128)(2,1)S(1)} %get-tuple-element.23.refs_2_, bf16[528,2560]{1,0:T(8,128)(2,1)S(1)} %get-tuple-element.24.refs_3_), custom_call_target="tpu_custom_call" | custom-call | flops 346030080 | bytes 5406720 | tf_op jit(solution)/shard_map/attend/pallas_call | solution.py:153
  16.5 1.5 %attend.3 = (bf16[32,2688]{1,0:T(8,128)(2,1)S(1)}, bf16[32,2688]{1,0:T(8,128)(2,1)S(1)}) custom-call(f32[528,128]{1,0:T(8,128)S(1)} %get-tuple-element.21.refs_0_, bf16[64,2560]{1,0:T(8,128)(2,1)S(1)} %collective-permute-done.7.refs_1_, bf16[528,2560]{1,0:T(8,128)(2,1)S(1)} %get-tuple-element.23.refs_2_, bf16[528,2560]{1,0:T(8,128)(2,1)S(1)} %get-tuple-element.24.refs_3_, ...), custom_call_target="tpu_custom_call" | custom-call | flops 346030080 | bytes 5406720 | tf_op jit(solution)/shard_map/attend/pallas_call | solution.py:153
  18.0 0.5 %collective-permute-start.9 = (bf16[32,2688]{1,0:T(8,128)(2,1)S(1)}, bf16[32,2688]{1,0:T(8,128)(2,1)S(1)}, u32[]{:S(2)}, u32[]{:S(2)}) collective-permute-start(bf16[32,2688]{1,0:T(8,128)(2,1)S(1)} %get-tuple-element.29), channel_id=1, source_target_pairs={{0,1},{1,0},{2,3},{3,2},{4,5},{5,4},{6,7},{7,6},{8,9},{9,8},{10,11... | collective-permute-start | bytes 516104 | tf_op jit(solution)/shard_map/ppermute | solution.py:326
  18.5 0.1 collective-permute-start.8
  18.6 0.9 %collective-permute-done.9.refs_1_ = bf16[32,2688]{1,0:T(8,128)(2,1)S(1)} collective-permute-done((bf16[32,2688]{1,0:T(8,128)(2,1)S(1)}, bf16[32,2688]{1,0:T(8,128)(2,1)S(1)}, u32[]{:S(2)}, u32[]{:S(2)}) %collective-permute-start.9) | collective-permute-done | bytes 172064 | tf_op jit(solution)/shard_map/ppermute | solution.py:326
  19.5 0.2 merge.14
  19.7 1.2 %collective-permute-start.13 = (bf16[8,2688]{1,0:T(8,128)(2,1)S(1)}, bf16[8,2688]{1,0:T(8,128)(2,1)S(1)}, u32[]{:S(2)}, u32[]{:S(2)}) collective-permute-start(bf16[8,2688]{1,0:T(8,128)(2,1)S(1)} %get-tuple-element.34), channel_id=1, source_target_pairs={{0,2},{1,3},{2,0},{3,1},{4,6},{5,7},{6,4},{7,5},{8,10},{9,11},{10,... | collective-permute-start | bytes 129032 | tf_op jit(solution)/shard_map/ppermute | solution.py:326
  20.9 0.9 %collective-permute-start.15 = (bf16[8,2688]{1,0:T(8,128)(2,1)S(1)}, bf16[8,2688]{1,0:T(8,128)(2,1)S(1)}, u32[]{:S(2)}, u32[]{:S(2)}) collective-permute-start(bf16[8,2688]{1,0:T(8,128)(2,1)S(1)} %get-tuple-element.36), channel_id=1, source_target_pairs={{0,2},{1,3},{2,0},{3,1},{4,6},{5,7},{6,4},{7,5},{8,10},{9,11},{10,... | collective-permute-start | bytes 129032 | tf_op jit(solution)/shard_map/ppermute | solution.py:326
  21.8 0.2 merge.11
  22.0 1.2 %collective-permute-start.11 = (bf16[8,2688]{1,0:T(8,128)(2,1)S(1)}, bf16[8,2688]{1,0:T(8,128)(2,1)S(1)}, u32[]{:S(2)}, u32[]{:S(2)}) collective-permute-start(bf16[8,2688]{1,0:T(8,128)(2,1)S(1)} %get-tuple-element.32), channel_id=1, source_target_pairs={{0,2},{1,3},{2,0},{3,1},{4,6},{5,7},{6,4},{7,5},{8,10},{9,11},{10,... | collective-permute-start | bytes 129032 | tf_op jit(solution)/shard_map/ppermute | solution.py:326
  23.2 0.9 %collective-permute-start.10 = (bf16[8,2688]{1,0:T(8,128)(2,1)S(1)}, bf16[8,2688]{1,0:T(8,128)(2,1)S(1)}, u32[]{:S(2)}, u32[]{:S(2)}) collective-permute-start(bf16[8,2688]{1,0:T(8,128)(2,1)S(1)} %get-tuple-element.30), channel_id=1, source_target_pairs={{0,2},{1,3},{2,0},{3,1},{4,6},{5,7},{6,4},{7,5},{8,10},{9,11},{10,... | collective-permute-start | bytes 129032 | tf_op jit(solution)/shard_map/ppermute | solution.py:326
  24.1 0.3 merge.10
  24.4 0.1 merge.15
  24.6 0.8 %collective-permute-start.14 = (bf16[8,2688]{1,0:T(8,128)(2,1)S(1)}, bf16[8,2688]{1,0:T(8,128)(2,1)S(1)}, u32[]{:S(2)}, u32[]{:S(2)}) collective-permute-start(bf16[8,2688]{1,0:T(8,128)(2,1)S(1)} %merge.15), channel_id=1, source_target_pairs={{0,8},{1,9},{2,10},{3,11},{4,12},{5,13},{6,14},{7,15},{8,0},{9,1},... | collective-permute-start | bytes 129032 | tf_op jit(solution)/shard_map/ppermute | solution.py:326
  25.4 0.1 merge.16
  25.5 2.6 %collective-permute-start.16 = (bf16[8,2688]{1,0:T(8,128)(2,1)S(1)}, bf16[8,2688]{1,0:T(8,128)(2,1)S(1)}, u32[]{:S(2)}, u32[]{:S(2)}) collective-permute-start(bf16[8,2688]{1,0:T(8,128)(2,1)S(1)} %merge.16), channel_id=1, source_target_pairs={{0,4},{1,5},{2,6},{3,7},{4,0},{5,1},{6,2},{7,3},{8,12},{9,13},{10,... | collective-permute-start | bytes 129032 | tf_op jit(solution)/shard_map/ppermute | solution.py:326
  28.1 0.1 merge.13
  28.3 1.2 %collective-permute-start.12 = (bf16[8,2688]{1,0:T(8,128)(2,1)S(1)}, bf16[8,2688]{1,0:T(8,128)(2,1)S(1)}, u32[]{:S(2)}, u32[]{:S(2)}) collective-permute-start(bf16[8,2688]{1,0:T(8,128)(2,1)S(1)} %merge.13), channel_id=1, source_target_pairs={{0,12},{1,13},{2,14},{3,15},{4,8},{5,9},{6,10},{7,11},{8,4},{9,5},... | collective-permute-start | bytes 129032 | tf_op jit(solution)/shard_map/ppermute | solution.py:326
  29.5 0.1 merge.12.refs_0_
  29.6 0.2 collective-permute-done.14.refs_2_
  29.8 0.4 %collective-permute-done.16.refs_3_ = bf16[8,2688]{1,0:T(8,128)(2,1)S(1)} collective-permute-done((bf16[8,2688]{1,0:T(8,128)(2,1)S(1)}, bf16[8,2688]{1,0:T(8,128)(2,1)S(1)}, u32[]{:S(2)}, u32[]{:S(2)}) %collective-permute-start.16) | collective-permute-done | bytes 43040 | tf_op jit(solution)/shard_map/ppermute | solution.py:326
  30.2 4.0 %collective-permute-done.12.refs_1_ = bf16[8,2688]{1,0:T(8,128)(2,1)S(1)} collective-permute-done((bf16[8,2688]{1,0:T(8,128)(2,1)S(1)}, bf16[8,2688]{1,0:T(8,128)(2,1)S(1)}, u32[]{:S(2)}, u32[]{:S(2)}) %collective-permute-start.12) | collective-permute-done | bytes 43040 | tf_op jit(solution)/shard_map/ppermute | solution.py:326
  34.2 0.9 %merge.17 = bf16[8,2560]{1,0:T(8,128)(2,1)} custom-call(f32[8,2688]{1,0:T(8,128)S(1)} %merge.12.refs_0_, bf16[8,2688]{1,0:T(8,128)(2,1)S(1)} %collective-permute-done.12.refs_1_, bf16[8,2688]{1,0:T(8,128)(2,1)S(1)} %collective-permute-done.14.refs_2_, bf16[8,2688]{1,0:T(8,128)(2,1)S(1)} %collective-permute-done.16.refs_3_), custom_call_target="tpu_custom_call" | custom-call | flops 344064 | bytes 344064 | tf_op jit(solution)/shard_map/merge/pallas_call | solution.py:303
  (14 shorter events, 0.2 us)
Async XLA Ops:
  0.0 7.4 %collective-permute-start.1 = (bf16[8,2560]{1,0:T(8,128)(2,1)}, bf16[8,2560]{1,0:T(8,128)(2,1)S(1)}, u32[]{:S(2)}, u32[]{:S(2)}) collective-permute-start(bf16[8,2560]{1,0:T(8,128)(2,1)} %refs_5_.1), channel_id=1, source_target_pairs={{12,0},{13,1},{14,2},{15,3},{8,4},{9,5},{10,6},{11,7},{4,8},{5,9},... | collective-permute-start | bytes 122888 | tf_op jit(solution)/shard_map/ppermute | solution.py:323
  5.0 4.2 %collective-permute-start = (bf16[8,2560]{1,0:T(8,128)(2,1)}, bf16[8,2560]{1,0:T(8,128)(2,1)S(1)}, u32[]{:S(2)}, u32[]{:S(2)}) collective-permute-start(bf16[8,2560]{1,0:T(8,128)(2,1)} %refs_5_.1), channel_id=1, source_target_pairs={{4,0},{5,1},{6,2},{7,3},{0,4},{1,5},{2,6},{3,7},{12,8},{13,9},{14,... | collective-permute-start | bytes 122888 | tf_op jit(solution)/shard_map/ppermute | solution.py:323
  5.1 5.7 %collective-permute-start.2 = (bf16[8,2560]{1,0:T(8,128)(2,1)}, bf16[8,2560]{1,0:T(8,128)(2,1)S(1)}, u32[]{:S(2)}, u32[]{:S(2)}) collective-permute-start(bf16[8,2560]{1,0:T(8,128)(2,1)} %refs_5_.1), channel_id=1, source_target_pairs={{8,0},{9,1},{10,2},{11,3},{12,4},{13,5},{14,6},{15,7},{0,8},{1,9},... | collective-permute-start | bytes 122888 | tf_op jit(solution)/shard_map/ppermute | solution.py:323
  5.6 8.9 %collective-permute-start.3 = (bf16[8,2560]{1,0:T(8,128)(2,1)}, bf16[8,2560]{1,0:T(8,128)(2,1)S(1)}, u32[]{:S(2)}, u32[]{:S(2)}) collective-permute-start(bf16[8,2560]{1,0:T(8,128)(2,1)} %refs_5_.1), channel_id=1, source_target_pairs={{2,0},{3,1},{0,2},{1,3},{6,4},{7,5},{4,6},{5,7},{10,8},{11,9},{8,1... | collective-permute-start | bytes 122888 | tf_op jit(solution)/shard_map/ppermute | solution.py:323
  7.4 7.2 %collective-permute-start.4 = (bf16[8,2560]{1,0:T(8,128)(2,1)S(1)}, bf16[8,2560]{1,0:T(8,128)(2,1)S(1)}, u32[]{:S(2)}, u32[]{:S(2)}) collective-permute-start(bf16[8,2560]{1,0:T(8,128)(2,1)S(1)} %collective-permute-done.1.refs_1_), channel_id=1, source_target_pairs={{2,0},{3,1},{0,2},{1,3},{6,4},{7,5},{4,6},{5,7},{10,8},{11,9},{8,1... | collective-permute-start | bytes 122888 | tf_op jit(solution)/shard_map/ppermute | solution.py:323
  9.3 5.3 %collective-permute-start.6 = (bf16[8,2560]{1,0:T(8,128)(2,1)S(1)}, bf16[8,2560]{1,0:T(8,128)(2,1)S(1)}, u32[]{:S(2)}, u32[]{:S(2)}) collective-permute-start(bf16[8,2560]{1,0:T(8,128)(2,1)S(1)} %collective-permute-done.refs_6_.refs_3_), channel_id=1, source_target_pairs={{2,0},{3,1},{0,2},{1,3},{6,4},{7,5},{4,6},{5,7},{10,8},{11,9},{8,1... | collective-permute-start | bytes 122888 | tf_op jit(solution)/shard_map/ppermute | solution.py:323
  10.8 4.0 %collective-permute-start.5 = (bf16[8,2560]{1,0:T(8,128)(2,1)S(1)}, bf16[8,2560]{1,0:T(8,128)(2,1)S(1)}, u32[]{:S(2)}, u32[]{:S(2)}) collective-permute-start(bf16[8,2560]{1,0:T(8,128)(2,1)S(1)} %collective-permute-done.2.refs_2_), channel_id=1, source_target_pairs={{2,0},{3,1},{0,2},{1,3},{6,4},{7,5},{4,6},{5,7},{10,8},{11,9},{8,1... | collective-permute-start | bytes 122888 | tf_op jit(solution)/shard_map/ppermute | solution.py:323
  14.8 1.7 %collective-permute-start.7 = (bf16[64,2560]{1,0:T(8,128)(2,1)S(1)}, bf16[64,2560]{1,0:T(8,128)(2,1)S(1)}, u32[]{:S(2)}, u32[]{:S(2)}) collective-permute-start(bf16[64,2560]{1,0:T(8,128)(2,1)S(1)} %merge.9.refs_1_), channel_id=1, source_target_pairs={{1,0},{0,1},{3,2},{2,3},{5,4},{4,5},{7,6},{6,7},{9,8},{8,9},{11,10... | collective-permute-start | bytes 983048 | tf_op jit(solution)/shard_map/ppermute | solution.py:323
  18.0 1.5 %collective-permute-start.9 = (bf16[32,2688]{1,0:T(8,128)(2,1)S(1)}, bf16[32,2688]{1,0:T(8,128)(2,1)S(1)}, u32[]{:S(2)}, u32[]{:S(2)}) collective-permute-start(bf16[32,2688]{1,0:T(8,128)(2,1)S(1)} %get-tuple-element.29), channel_id=1, source_target_pairs={{0,1},{1,0},{2,3},{3,2},{4,5},{5,4},{6,7},{7,6},{8,9},{9,8},{10,11... | collective-permute-start | bytes 516104 | tf_op jit(solution)/shard_map/ppermute | solution.py:326
  18.5 5.6 %collective-permute-start.8 = (bf16[32,2688]{1,0:T(8,128)(2,1)S(1)}, bf16[32,2688]{1,0:T(8,128)(2,1)S(1)}, u32[]{:S(2)}, u32[]{:S(2)}) collective-permute-start(bf16[32,2688]{1,0:T(8,128)(2,1)S(1)} %get-tuple-element.26), channel_id=1, source_target_pairs={{0,1},{1,0},{2,3},{3,2},{4,5},{5,4},{6,7},{7,6},{8,9},{9,8},{10,11... | collective-permute-start | bytes 516104 | tf_op jit(solution)/shard_map/ppermute | solution.py:326
  19.7 4.7 %collective-permute-start.13 = (bf16[8,2688]{1,0:T(8,128)(2,1)S(1)}, bf16[8,2688]{1,0:T(8,128)(2,1)S(1)}, u32[]{:S(2)}, u32[]{:S(2)}) collective-permute-start(bf16[8,2688]{1,0:T(8,128)(2,1)S(1)} %get-tuple-element.34), channel_id=1, source_target_pairs={{0,2},{1,3},{2,0},{3,1},{4,6},{5,7},{6,4},{7,5},{8,10},{9,11},{10,... | collective-permute-start | bytes 129032 | tf_op jit(solution)/shard_map/ppermute | solution.py:326
  20.9 4.5 %collective-permute-start.15 = (bf16[8,2688]{1,0:T(8,128)(2,1)S(1)}, bf16[8,2688]{1,0:T(8,128)(2,1)S(1)}, u32[]{:S(2)}, u32[]{:S(2)}) collective-permute-start(bf16[8,2688]{1,0:T(8,128)(2,1)S(1)} %get-tuple-element.36), channel_id=1, source_target_pairs={{0,2},{1,3},{2,0},{3,1},{4,6},{5,7},{6,4},{7,5},{8,10},{9,11},{10,... | collective-permute-start | bytes 129032 | tf_op jit(solution)/shard_map/ppermute | solution.py:326
  22.0 6.1 %collective-permute-start.11 = (bf16[8,2688]{1,0:T(8,128)(2,1)S(1)}, bf16[8,2688]{1,0:T(8,128)(2,1)S(1)}, u32[]{:S(2)}, u32[]{:S(2)}) collective-permute-start(bf16[8,2688]{1,0:T(8,128)(2,1)S(1)} %get-tuple-element.32), channel_id=1, source_target_pairs={{0,2},{1,3},{2,0},{3,1},{4,6},{5,7},{6,4},{7,5},{8,10},{9,11},{10,... | collective-permute-start | bytes 129032 | tf_op jit(solution)/shard_map/ppermute | solution.py:326
  23.2 6.3 %collective-permute-start.10 = (bf16[8,2688]{1,0:T(8,128)(2,1)S(1)}, bf16[8,2688]{1,0:T(8,128)(2,1)S(1)}, u32[]{:S(2)}, u32[]{:S(2)}) collective-permute-start(bf16[8,2688]{1,0:T(8,128)(2,1)S(1)} %get-tuple-element.30), channel_id=1, source_target_pairs={{0,2},{1,3},{2,0},{3,1},{4,6},{5,7},{6,4},{7,5},{8,10},{9,11},{10,... | collective-permute-start | bytes 129032 | tf_op jit(solution)/shard_map/ppermute | solution.py:326
  24.6 5.2 %collective-permute-start.14 = (bf16[8,2688]{1,0:T(8,128)(2,1)S(1)}, bf16[8,2688]{1,0:T(8,128)(2,1)S(1)}, u32[]{:S(2)}, u32[]{:S(2)}) collective-permute-start(bf16[8,2688]{1,0:T(8,128)(2,1)S(1)} %merge.15), channel_id=1, source_target_pairs={{0,8},{1,9},{2,10},{3,11},{4,12},{5,13},{6,14},{7,15},{8,0},{9,1},... | collective-permute-start | bytes 129032 | tf_op jit(solution)/shard_map/ppermute | solution.py:326
  25.5 4.6 %collective-permute-start.16 = (bf16[8,2688]{1,0:T(8,128)(2,1)S(1)}, bf16[8,2688]{1,0:T(8,128)(2,1)S(1)}, u32[]{:S(2)}, u32[]{:S(2)}) collective-permute-start(bf16[8,2688]{1,0:T(8,128)(2,1)S(1)} %merge.16), channel_id=1, source_target_pairs={{0,4},{1,5},{2,6},{3,7},{4,0},{5,1},{6,2},{7,3},{8,12},{9,13},{10,... | collective-permute-start | bytes 129032 | tf_op jit(solution)/shard_map/ppermute | solution.py:326
  28.3 5.9 %collective-permute-start.12 = (bf16[8,2688]{1,0:T(8,128)(2,1)S(1)}, bf16[8,2688]{1,0:T(8,128)(2,1)S(1)}, u32[]{:S(2)}, u32[]{:S(2)}) collective-permute-start(bf16[8,2688]{1,0:T(8,128)(2,1)S(1)} %merge.13), channel_id=1, source_target_pairs={{0,12},{1,13},{2,14},{3,15},{4,8},{5,9},{6,10},{7,11},{8,4},{9,5},... | collective-permute-start | bytes 129032 | tf_op jit(solution)/shard_map/ppermute | solution.py:326
